TPU v7x, 32 devices: a whole 2x2x4 slice. The times are simulated.
32 devices in a mesh: grp: 8 (over y, x, core), blk: 4 (over z).
Axes of the slice: x: 2, y: 2, z: 4, core: 2. Of those that a mesh axis runs over, the one named last changes fastest.
Arguments:
- patches: bfloat16 [4, 3072, 1152], P('blk', 'grp'), may hold values from -6 to 6
- segment_ids: int32 [4, 3072], P('blk'), may hold values from 0 to 3, never falling along the last dimension, each value on 1 to 1024 neighbouring positions
- qkv_weight: bfloat16 [1152, 1728], replicated
- out_weight: bfloat16 [576, 1152], replicated, may hold values from -0.25 to 0.25
- text_embed: bfloat16 [16, 1152], P('blk'), may hold values from -6 to 6
Outputs:
- mixed: bfloat16 [4, 3072, 1152], P('blk', 'grp')
- row_loss: float32 [16], P('blk')
Inputs may be any that keep to these rules, and one draw needn't show every extreme that they name: `segment_ids`: within each group ids never fall, every image has 1 to 1024 rows, and some image has exactly 1024.
All inputs are finite; a program needn't handle non-finite values.
Results may differ from a plain program's by a relative error of at most 0.0025.
The roundings to bfloat16 on the way count: a program that leaves them out, or rounds other values in their place, can miss the bound.
Values may be sent and summed in bfloat16 or wider, within the bound.
No kernel may reach another device: no remote copies, remote signals or barrier semaphores. Data moves between devices by JAX's collectives and lax.ppermute only.
A program may use at most 64 MiB of HBM per device.

v0:
```python
import jax
import jax.numpy as jnp
from jax import lax
from jax.sharding import PartitionSpec as P

HEADS = 8
MAXP = 1024


logit_scale = 30.0
logit_bias = -5.0


def shifted(value, axis, by):
    peers = lax.axis_size(axis)
    pairs = [(i, i + by) for i in range(peers) if 0 <= i + by < peers]
    return lax.ppermute(value, axis, pairs)


def normalize_rows(rows):
    values = rows.astype(jnp.float32)
    center = values - jnp.mean(values, axis=1, keepdims=True)
    spread = jnp.mean(center * center, axis=1, keepdims=True)
    return (center * lax.rsqrt(spread + 1e-06)).astype(jnp.bfloat16)


def unit_rows(matrix):
    return matrix * lax.rsqrt(jnp.sum(matrix * matrix, axis=1, keepdims=True) + 1e-06)


def head_terms(query_head, key_head, value_head, query_ids, key_ids):
    scores = lax.dot_general(
        query_head, key_head, (((1,), (1,)), ((), ())), preferred_element_type=jnp.float32
    )
    scores = scores * query_head.shape[1] ** (-0.5)
    same = query_ids[:, None] == key_ids[None, :]
    scores = jnp.where(same, scores, -1e30)
    highest = jnp.max(scores, axis=1)
    probs = jnp.where(same, jnp.exp(scores - highest[:, None]), 0.0)
    summed = jnp.sum(probs, axis=1)
    weighted = jnp.dot(probs.astype(jnp.bfloat16), value_head, preferred_element_type=jnp.float32)
    return (highest, summed, weighted)


def split_heads(matrix):
    return matrix.reshape(matrix.shape[0], HEADS, -1).transpose(1, 0, 2)


def loss_rows(image_vecs, texts, row_start):
    text_vecs = unit_rows(texts.astype(jnp.float32))
    cosine = jnp.dot(image_vecs, text_vecs.T, precision=lax.Precision.HIGHEST)
    row_index = row_start + jnp.arange(image_vecs.shape[0], dtype=jnp.int32)
    col_index = jnp.arange(texts.shape[0], dtype=jnp.int32)
    labels = jnp.where(row_index[:, None] == col_index[None, :], 1.0, -1.0)
    return jnp.sum(jax.nn.softplus(-labels * (logit_scale * cosine + logit_bias)), axis=1)


def local(patches, segment_ids, qkv_weight, out_weight, text_embed):
    rows = patches[0]
    group_ids = segment_ids[0]
    count = rows.shape[0]
    width = out_weight.shape[0]
    group_size = lax.axis_size("grp")
    image_count = group_size // 2
    own_index = lax.axis_index("grp")
    own_ids = lax.dynamic_slice_in_dim(group_ids, own_index * count, count)
    normed = normalize_rows(rows)
    qkv = jnp.dot(normed, qkv_weight, preferred_element_type=jnp.float32).astype(jnp.bfloat16)
    queries = split_heads(qkv[:, :width])
    keys_values = qkv[:, width:]
    reach_count = min((MAXP + count - 2) // count, group_size - 1)
    near_pieces = [keys_values]
    near_labels = [own_ids]
    for distance in range(1, reach_count + 1):
        for offset in (distance, -distance):
            moved = shifted(keys_values, "grp", offset)
            source = own_index - offset
            inside = jnp.logical_and(source >= 0, source < group_size)
            first_row = jnp.clip(source, 0, group_size - 1) * count
            labels = lax.dynamic_slice_in_dim(group_ids, first_row, count)
            near_pieces.append(moved)
            near_labels.append(jnp.where(inside, labels, -1))
    near_rows = jnp.concatenate(near_pieces, axis=0)
    near_ids = jnp.concatenate(near_labels, axis=0)
    near_keys = split_heads(near_rows[:, :width])
    near_values = split_heads(near_rows[:, width:])

    def near_head(triple):
        highest, summed, weighted = head_terms(triple[0], triple[1], triple[2], own_ids, near_ids)
        return (weighted / summed[:, None]).astype(jnp.bfloat16)

    heads = lax.map(near_head, (queries, near_keys, near_values))
    attended = heads.transpose(1, 0, 2).reshape(count, width)
    mixed = rows.astype(jnp.float32) + jnp.dot(
        attended, out_weight, preferred_element_type=jnp.float32
    )
    mixed = mixed.astype(jnp.bfloat16)
    onehot = (own_ids[:, None] == jnp.arange(image_count, dtype=jnp.int32)[None, :]).astype(
        jnp.bfloat16
    )
    partial_sums = lax.dot_general(
        onehot, mixed, (((0,), (0,)), ((), ())), preferred_element_type=jnp.float32
    )
    pooled = lax.psum(partial_sums.astype(jnp.bfloat16), "grp").astype(jnp.float32)
    image_vecs = unit_rows(pooled)
    row_start = lax.axis_index("blk") * image_count
    row_loss = loss_rows(
        image_vecs, lax.all_gather(text_embed, "blk", axis=0, tiled=True), row_start
    )
    return (mixed[None], row_loss)


def solution(mesh):
    placed = (P("blk", "grp", None), P("blk", None), P(), P(), P("blk", None))
    return jax.shard_map(
        local,
        mesh=mesh,
        in_specs=placed,
        out_specs=(P("blk", "grp", None), P("blk")),
        check_vma=False,
    )
```

profile of v0, /device:TPU:0, one launch (start us, length us, event | category | flops | bytes accessed | tf_op | source)
XLA Modules:
  0.0 177.9 jit_solution(7325091350706163690)
XLA Ops:
  0.6 0.0 copy-start
  0.6 1.5 convert_reduce_fusion
  2.1 1.5 fusion.29
  3.7 0.0 copy-start.4
  3.7 0.0 copy-start.3
  3.7 4.9 %convolution_convert_fusion = bf16[384,1728]{0,1:T(8,128)(2,1)S(1)} fusion(bf16[1152,1728]{0,1:T(8,128)(2,1)} %param.9, bf16[1,384,1152]{2,1,0:T(8,128)(2,1)} %param.7, f32[384]{0:T(512)S(1)} %add_rsqrt_fusion, f32[384]{0:T(512)S(1)} %broadcast_multiply_fusion), kind=kOutput, calls=%fused_computation.21 | convolution fusion | flops 1531256832 | bytes 6196224 | tf_op jit(solution)/shard_map/dot_general | solution.py:68
  8.6 1.4 fusion.53
  10.0 3.3 %collective-permute-start = (bf16[384,1152]{0,1:T(8,128)(2,1)}, bf16[384,1152]{0,1:T(8,128)(2,1)}, u32[]{:S(2)}, u32[]{:S(2)}) collective-permute-start(bf16[384,1152]{0,1:T(8,128)(2,1)} %get-tuple-element.65), channel_id=1, source_target_pairs={{0,4},{4,8},{8,12},{12,16},{16,20},{20,24},{24,28},{1,5},{5,9},{9,... | collective-permute-start | bytes 2654216 | tf_op jit(solution)/shard_map/ppermute | solution.py:17
  13.3 1.3 collective-permute-start.1
  14.6 6.9 %collective-permute-start.2 = (bf16[384,1152]{0,1:T(8,128)(2,1)}, bf16[384,1152]{0,1:T(8,128)(2,1)}, u32[]{:S(2)}, u32[]{:S(2)}) collective-permute-start(bf16[384,1152]{0,1:T(8,128)(2,1)} %get-tuple-element.65), channel_id=1, source_target_pairs={{0,8},{4,12},{8,16},{12,20},{16,24},{20,28},{1,9},{5,13},{9,17},{1... | collective-permute-start | bytes 2654216 | tf_op jit(solution)/shard_map/ppermute | solution.py:17
  21.5 1.3 collective-permute-start.3
  22.7 4.4 %collective-permute-start.4 = (bf16[384,1152]{0,1:T(8,128)(2,1)}, bf16[384,1152]{0,1:T(8,128)(2,1)}, u32[]{:S(2)}, u32[]{:S(2)}) collective-permute-start(bf16[384,1152]{0,1:T(8,128)(2,1)} %get-tuple-element.65), channel_id=1, source_target_pairs={{0,12},{4,16},{8,20},{12,24},{16,28},{1,13},{5,17},{9,21},{13,25},... | collective-permute-start | bytes 2654216 | tf_op jit(solution)/shard_map/ppermute | solution.py:17
  27.1 13.4 %all-gather = bf16[4,4,1152]{2,1,0:T(4,128)(2,1)S(1)} all-gather(bf16[1,4,1152]{2,1,0:T(4,128)(2,1)S(1)} %bitcast.62), channel_id=1, replica_groups=mesh['grp'=8,'blk'=4] {'blk'}, dimensions={0}, use_global_device_ids=true | all-gather | bytes 46080 | tf_op jit(solution)/shard_map/all_gather | solution.py:108
  40.5 0.0 copy-done.3
  40.6 0.1 fusion.50
  40.7 0.1 multiply_reduce_fusion
  40.9 0.4 copy.10
  41.3 0.0 collective-permute-done
  41.3 1.3 collective-permute-start.5
  42.6 2.3 %constant_dynamic-update-slice_fusion.6 = bf16[2688,1152]{0,1:T(8,128)(2,1)} fusion(bf16[2688,1152]{0,1:T(8,128)(2,1)} %get-tuple-element.66, bf16[384,1152]{0,1:T(8,128)(2,1)} %collective-permute-done), kind=kLoop, calls=%fused_computation.49 | loop fusion | bytes 1769472
  44.8 0.0 collective-permute-done.1
  44.8 2.3 %constant_dynamic-update-slice_fusion.5 = bf16[2688,1152]{0,1:T(8,128)(2,1)} fusion(bf16[2688,1152]{0,1:T(8,128)(2,1)} %constant_dynamic-update-slice_fusion.6, bf16[384,1152]{0,1:T(8,128)(2,1)} %collective-permute-done.1), kind=kLoop, calls=%fused_computation.48 | loop fusion | bytes 1769472
  47.1 0.0 collective-permute-done.2
  47.1 2.2 %constant_dynamic-update-slice_fusion.4 = bf16[2688,1152]{0,1:T(8,128)(2,1)} fusion(bf16[2688,1152]{0,1:T(8,128)(2,1)} %constant_dynamic-update-slice_fusion.5, bf16[384,1152]{0,1:T(8,128)(2,1)} %collective-permute-done.2), kind=kLoop, calls=%fused_computation.47 | loop fusion | bytes 1769472
  49.4 28.0 %collective-permute-done.3 = bf16[384,1152]{0,1:T(8,128)(2,1)} collective-permute-done((bf16[384,1152]{0,1:T(8,128)(2,1)}, bf16[384,1152]{0,1:T(8,128)(2,1)}, u32[]{:S(2)}, u32[]{:S(2)}) %collective-permute-start.3) | collective-permute-done | bytes 884768 | tf_op jit(solution)/shard_map/ppermute | solution.py:17
  77.3 2.2 %constant_dynamic-update-slice_fusion.3 = bf16[2688,1152]{0,1:T(8,128)(2,1)} fusion(bf16[2688,1152]{0,1:T(8,128)(2,1)} %constant_dynamic-update-slice_fusion.4, bf16[384,1152]{0,1:T(8,128)(2,1)} %collective-permute-done.3), kind=kLoop, calls=%fused_computation.46 | loop fusion | bytes 1769472
  79.6 0.0 collective-permute-done.4
  79.6 2.2 %constant_dynamic-update-slice_fusion.2 = bf16[2688,1152]{0,1:T(8,128)(2,1)} fusion(bf16[2688,1152]{0,1:T(8,128)(2,1)} %constant_dynamic-update-slice_fusion.3, bf16[384,1152]{0,1:T(8,128)(2,1)} %collective-permute-done.4), kind=kLoop, calls=%fused_computation.45 | loop fusion | bytes 1769472
  81.8 8.8 %collective-permute-done.5 = bf16[384,1152]{0,1:T(8,128)(2,1)S(1)} collective-permute-done((bf16[384,1152]{0,1:T(8,128)(2,1)}, bf16[384,1152]{0,1:T(8,128)(2,1)S(1)}, u32[]{:S(2)}, u32[]{:S(2)}) %collective-permute-start.5) | collective-permute-done | bytes 884768 | tf_op jit(solution)/shard_map/ppermute | solution.py:17
  90.6 1.0 constant_dynamic-update-slice_fusion.1
  91.6 5.9 %fusion.52 = (bf16[2688,576]{0,1:T(8,128)(2,1)}, bf16[2688,576]{0,1:T(8,128)(2,1)}) fusion(bf16[2688,1152]{0,1:T(8,128)(2,1)} %constant_dynamic-update-slice_fusion.1), kind=kLoop, calls=%fused_computation.87 | loop fusion | bytes 12386304 | tf_op jit(solution)/shard_map/slice | solution.py:86
  97.5 6.3 %copy.12 = bf16[2688,8,72]{2,0,1:T(8,128)(2,1)} copy(bf16[2688,8,72]{0,2,1:T(8,128)(2,1)} %bitcast.56) | data formatting | bytes 6193152 | tf_op jit(solution)/shard_map/reshape | solution.py:46
  103.9 6.3 %copy.11 = bf16[2688,8,72]{2,0,1:T(8,128)(2,1)} copy(bf16[2688,8,72]{0,2,1:T(8,128)(2,1)} %bitcast.55) | data formatting | bytes 6193152 | tf_op jit(solution)/shard_map/reshape | solution.py:46
  110.2 46.0 %while.10 = (s32[]{:T(128)}, bf16[8,384,72]{1,2,0:T(8,128)(2,1)}, s32[384]{0:T(512)S(1)}, s32[2688]{0:T(1024)S(1)}, bf16[8,384,72]{2,1,0:T(8,128)(2,1)S(1)}, /*i...) while((s32[]{:T(128)}, bf16[8,384,72]{1,2,0:T(8,128)(2,1)}, s32[384]{0:T(512)S(1)}, ...), condition=%wide.region_5.6_spmd, body=%wide.region_2.5_spmd.sunk | while | flops 309712128 | bytes 13964885 | solution.py:92
  110.2 2.1 %fusion.65 = (f32[384]{0:T(512)S(1)}, f32[384,2688]{1,0:T(8,128)S(1)}) fusion(bf16[8,2688,72]{2,1,0:T(8,128)(2,1)} %get-tuple-element.135, s32[]{:T(128)} %get-tuple-element.122, bf16[8,384,72]{2,1,0:T(8,128)(2,1)S(1)} %get-tuple-element.134, s32[2688]{0:T(1024)S(1)} %get-tuple-element.133, s32[384]{0:T(512)S(1)} %get-tuple-element.132), kind=kOutput, calls=%fused_computation.86.clone.1 | convolution fusion | flops 152764032 | bytes 4932096 | tf_op jit(solution)/shard_map/while/body/eval_jaxpr/dot_general | solution.py:32
  112.3 1.0 fusion.66
  113.3 2.7 %fusion.67 = bf16[8,384,72]{1,2,0:T(8,128)(2,1)} fusion(bf16[8,384,72]{1,2,0:T(8,128)(2,1)} %get-tuple-element.123, s32[]{:T(128)} %get-tuple-element.122, f32[384,2688]{1,0:T(8,128)S(1)} %get-tuple-element.112, f32[384]{0:T(512)S(1)} %get-tuple-element.113, s32[2688]{0:T(1024)S(1)} %get-tuple-element.133, s32[384]{0:T(512)S(1)} %get-tuple-element.132, ...), kind=kOutput, calls=%fused_computation.9.clone.1 | convolution fusion | flops 152819712 | bytes 4888576 | tf_op jit(solution)/shard_map/while/body/eval_jaxpr/dot_general | solution.py:41
  116.0 2.0 %fusion.65 = (f32[384]{0:T(512)S(1)}, f32[384,2688]{1,0:T(8,128)S(1)}) fusion(bf16[8,2688,72]{2,1,0:T(8,128)(2,1)} %get-tuple-element.135, s32[]{:T(128)} %get-tuple-element.122, bf16[8,384,72]{2,1,0:T(8,128)(2,1)S(1)} %get-tuple-element.134, s32[2688]{0:T(1024)S(1)} %get-tuple-element.133, s32[384]{0:T(512)S(1)} %get-tuple-element.132), kind=kOutput, calls=%fused_computation.86.clone.1 | convolution fusion | flops 152764032 | bytes 4932096 | tf_op jit(solution)/shard_map/while/body/eval_jaxpr/dot_general | solution.py:32
  118.0 1.0 fusion.66
  119.0 2.7 %fusion.67 = bf16[8,384,72]{1,2,0:T(8,128)(2,1)} fusion(bf16[8,384,72]{1,2,0:T(8,128)(2,1)} %get-tuple-element.123, s32[]{:T(128)} %get-tuple-element.122, f32[384,2688]{1,0:T(8,128)S(1)} %get-tuple-element.112, f32[384]{0:T(512)S(1)} %get-tuple-element.113, s32[2688]{0:T(1024)S(1)} %get-tuple-element.133, s32[384]{0:T(512)S(1)} %get-tuple-element.132, ...), kind=kOutput, calls=%fused_computation.9.clone.1 | convolution fusion | flops 152819712 | bytes 4888576 | tf_op jit(solution)/shard_map/while/body/eval_jaxpr/dot_general | solution.py:41
  121.8 2.0 %fusion.65 = (f32[384]{0:T(512)S(1)}, f32[384,2688]{1,0:T(8,128)S(1)}) fusion(bf16[8,2688,72]{2,1,0:T(8,128)(2,1)} %get-tuple-element.135, s32[]{:T(128)} %get-tuple-element.122, bf16[8,384,72]{2,1,0:T(8,128)(2,1)S(1)} %get-tuple-element.134, s32[2688]{0:T(1024)S(1)} %get-tuple-element.133, s32[384]{0:T(512)S(1)} %get-tuple-element.132), kind=kOutput, calls=%fused_computation.86.clone.1 | convolution fusion | flops 152764032 | bytes 4932096 | tf_op jit(solution)/shard_map/while/body/eval_jaxpr/dot_general | solution.py:32
  123.8 1.0 fusion.66
  124.8 2.7 %fusion.67 = bf16[8,384,72]{1,2,0:T(8,128)(2,1)} fusion(bf16[8,384,72]{1,2,0:T(8,128)(2,1)} %get-tuple-element.123, s32[]{:T(128)} %get-tuple-element.122, f32[384,2688]{1,0:T(8,128)S(1)} %get-tuple-element.112, f32[384]{0:T(512)S(1)} %get-tuple-element.113, s32[2688]{0:T(1024)S(1)} %get-tuple-element.133, s32[384]{0:T(512)S(1)} %get-tuple-element.132, ...), kind=kOutput, calls=%fused_computation.9.clone.1 | convolution fusion | flops 152819712 | bytes 4888576 | tf_op jit(solution)/shard_map/while/body/eval_jaxpr/dot_general | solution.py:41
  127.5 2.0 %fusion.65 = (f32[384]{0:T(512)S(1)}, f32[384,2688]{1,0:T(8,128)S(1)}) fusion(bf16[8,2688,72]{2,1,0:T(8,128)(2,1)} %get-tuple-element.135, s32[]{:T(128)} %get-tuple-element.122, bf16[8,384,72]{2,1,0:T(8,128)(2,1)S(1)} %get-tuple-element.134, s32[2688]{0:T(1024)S(1)} %get-tuple-element.133, s32[384]{0:T(512)S(1)} %get-tuple-element.132), kind=kOutput, calls=%fused_computation.86.clone.1 | convolution fusion | flops 152764032 | bytes 4932096 | tf_op jit(solution)/shard_map/while/body/eval_jaxpr/dot_general | solution.py:32
  129.5 1.0 fusion.66
  130.5 2.7 %fusion.67 = bf16[8,384,72]{1,2,0:T(8,128)(2,1)} fusion(bf16[8,384,72]{1,2,0:T(8,128)(2,1)} %get-tuple-element.123, s32[]{:T(128)} %get-tuple-element.122, f32[384,2688]{1,0:T(8,128)S(1)} %get-tuple-element.112, f32[384]{0:T(512)S(1)} %get-tuple-element.113, s32[2688]{0:T(1024)S(1)} %get-tuple-element.133, s32[384]{0:T(512)S(1)} %get-tuple-element.132, ...), kind=kOutput, calls=%fused_computation.9.clone.1 | convolution fusion | flops 152819712 | bytes 4888576 | tf_op jit(solution)/shard_map/while/body/eval_jaxpr/dot_general | solution.py:41
  133.2 2.0 %fusion.65 = (f32[384]{0:T(512)S(1)}, f32[384,2688]{1,0:T(8,128)S(1)}) fusion(bf16[8,2688,72]{2,1,0:T(8,128)(2,1)} %get-tuple-element.135, s32[]{:T(128)} %get-tuple-element.122, bf16[8,384,72]{2,1,0:T(8,128)(2,1)S(1)} %get-tuple-element.134, s32[2688]{0:T(1024)S(1)} %get-tuple-element.133, s32[384]{0:T(512)S(1)} %get-tuple-element.132), kind=kOutput, calls=%fused_computation.86.clone.1 | convolution fusion | flops 152764032 | bytes 4932096 | tf_op jit(solution)/shard_map/while/body/eval_jaxpr/dot_general | solution.py:32
  135.3 1.0 fusion.66
  136.2 2.7 %fusion.67 = bf16[8,384,72]{1,2,0:T(8,128)(2,1)} fusion(bf16[8,384,72]{1,2,0:T(8,128)(2,1)} %get-tuple-element.123, s32[]{:T(128)} %get-tuple-element.122, f32[384,2688]{1,0:T(8,128)S(1)} %get-tuple-element.112, f32[384]{0:T(512)S(1)} %get-tuple-element.113, s32[2688]{0:T(1024)S(1)} %get-tuple-element.133, s32[384]{0:T(512)S(1)} %get-tuple-element.132, ...), kind=kOutput, calls=%fused_computation.9.clone.1 | convolution fusion | flops 152819712 | bytes 4888576 | tf_op jit(solution)/shard_map/while/body/eval_jaxpr/dot_general | solution.py:41
  139.0 2.0 %fusion.65 = (f32[384]{0:T(512)S(1)}, f32[384,2688]{1,0:T(8,128)S(1)}) fusion(bf16[8,2688,72]{2,1,0:T(8,128)(2,1)} %get-tuple-element.135, s32[]{:T(128)} %get-tuple-element.122, bf16[8,384,72]{2,1,0:T(8,128)(2,1)S(1)} %get-tuple-element.134, s32[2688]{0:T(1024)S(1)} %get-tuple-element.133, s32[384]{0:T(512)S(1)} %get-tuple-element.132), kind=kOutput, calls=%fused_computation.86.clone.1 | convolution fusion | flops 152764032 | bytes 4932096 | tf_op jit(solution)/shard_map/while/body/eval_jaxpr/dot_general | solution.py:32
  141.0 1.0 fusion.66
  142.0 2.7 %fusion.67 = bf16[8,384,72]{1,2,0:T(8,128)(2,1)} fusion(bf16[8,384,72]{1,2,0:T(8,128)(2,1)} %get-tuple-element.123, s32[]{:T(128)} %get-tuple-element.122, f32[384,2688]{1,0:T(8,128)S(1)} %get-tuple-element.112, f32[384]{0:T(512)S(1)} %get-tuple-element.113, s32[2688]{0:T(1024)S(1)} %get-tuple-element.133, s32[384]{0:T(512)S(1)} %get-tuple-element.132, ...), kind=kOutput, calls=%fused_computation.9.clone.1 | convolution fusion | flops 152819712 | bytes 4888576 | tf_op jit(solution)/shard_map/while/body/eval_jaxpr/dot_general | solution.py:41
  144.7 2.0 %fusion.65 = (f32[384]{0:T(512)S(1)}, f32[384,2688]{1,0:T(8,128)S(1)}) fusion(bf16[8,2688,72]{2,1,0:T(8,128)(2,1)} %get-tuple-element.135, s32[]{:T(128)} %get-tuple-element.122, bf16[8,384,72]{2,1,0:T(8,128)(2,1)S(1)} %get-tuple-element.134, s32[2688]{0:T(1024)S(1)} %get-tuple-element.133, s32[384]{0:T(512)S(1)} %get-tuple-element.132), kind=kOutput, calls=%fused_computation.86.clone.1 | convolution fusion | flops 152764032 | bytes 4932096 | tf_op jit(solution)/shard_map/while/body/eval_jaxpr/dot_general | solution.py:32
  146.8 1.0 fusion.66
  147.7 2.7 %fusion.67 = bf16[8,384,72]{1,2,0:T(8,128)(2,1)} fusion(bf16[8,384,72]{1,2,0:T(8,128)(2,1)} %get-tuple-element.123, s32[]{:T(128)} %get-tuple-element.122, f32[384,2688]{1,0:T(8,128)S(1)} %get-tuple-element.112, f32[384]{0:T(512)S(1)} %get-tuple-element.113, s32[2688]{0:T(1024)S(1)} %get-tuple-element.133, s32[384]{0:T(512)S(1)} %get-tuple-element.132, ...), kind=kOutput, calls=%fused_computation.9.clone.1 | convolution fusion | flops 152819712 | bytes 4888576 | tf_op jit(solution)/shard_map/while/body/eval_jaxpr/dot_general | solution.py:41
  150.5 2.0 %fusion.65 = (f32[384]{0:T(512)S(1)}, f32[384,2688]{1,0:T(8,128)S(1)}) fusion(bf16[8,2688,72]{2,1,0:T(8,128)(2,1)} %get-tuple-element.135, s32[]{:T(128)} %get-tuple-element.122, bf16[8,384,72]{2,1,0:T(8,128)(2,1)S(1)} %get-tuple-element.134, s32[2688]{0:T(1024)S(1)} %get-tuple-element.133, s32[384]{0:T(512)S(1)} %get-tuple-element.132), kind=kOutput, calls=%fused_computation.86.clone.1 | convolution fusion | flops 152764032 | bytes 4932096 | tf_op jit(solution)/shard_map/while/body/eval_jaxpr/dot_general | solution.py:32
  152.5 1.0 fusion.66
  153.5 2.7 %fusion.67 = bf16[8,384,72]{1,2,0:T(8,128)(2,1)} fusion(bf16[8,384,72]{1,2,0:T(8,128)(2,1)} %get-tuple-element.123, s32[]{:T(128)} %get-tuple-element.122, f32[384,2688]{1,0:T(8,128)S(1)} %get-tuple-element.112, f32[384]{0:T(512)S(1)} %get-tuple-element.113, s32[2688]{0:T(1024)S(1)} %get-tuple-element.133, s32[384]{0:T(512)S(1)} %get-tuple-element.132, ...), kind=kOutput, calls=%fused_computation.9.clone.1 | convolution fusion | flops 152819712 | bytes 4888576 | tf_op jit(solution)/shard_map/while/body/eval_jaxpr/dot_general | solution.py:41
  156.2 1.9 %fusion.25 = bf16[384,1152]{1,0:T(8,128)(2,1)S(1)} fusion(bf16[384,576]{0,1:T(8,128)(2,1)} %bitcast.12, bf16[576,1152]{1,0:T(8,128)(2,1)S(1)} %copy-done, bf16[1,384,1152]{2,1,0:T(8,128)(2,1)S(1)} %copy-done.1), kind=kOutput, calls=%fused_computation.20 | convolution fusion | flops 510935040 | bytes 3538944 | tf_op jit(solution)/shard_map/dot_general | solution.py:94
  158.1 0.0 copy-start.2
  158.2 0.4 convolution_convert_fusion.1
  158.5 18.3 %psum.7 = bf16[4,1152]{1,0:T(4,128)(2,1)S(1)} all-reduce(bf16[4,1152]{1,0:T(4,128)(2,1)S(1)} %convolution_convert_fusion.1), channel_id=1, replica_groups=mesh['grp'=8,'blk'=4] {'grp'}, use_global_device_ids=true, to_apply=%region_6.7 | all-reduce | flops 4608 | bytes 18432 | tf_op jit(solution)/shard_map/psum | solution.py:104
  176.8 0.1 fusion.39
  177.0 0.9 fusion.41
  (21 shorter events, 0.1 us)
Async XLA Ops:
  0.6 155.6 %copy-start = (bf16[576,1152]{1,0:T(8,128)(2,1)S(1)}, bf16[576,1152]{1,0:T(8,128)(2,1)}, u32[]{:S(2)}) copy-start(bf16[576,1152]{1,0:T(8,128)(2,1)} %param.10) | copy-start | bytes 3981316
  3.7 23.5 %copy-start.4 = (bf16[4,1152]{1,0:T(4,128)(2,1)S(1)}, bf16[4,1152]{1,0:T(4,128)(2,1)}, u32[]{:S(2)}) copy-start(bf16[4,1152]{1,0:T(4,128)(2,1)} %param.11) | copy-start | bytes 27652
  3.7 36.9 %copy-start.3 = (s32[1,3072]{1,0:T(1,128)S(1)}, s32[1,3072]{1,0:T(1,128)}, u32[]{:S(2)}) copy-start(s32[1,3072]{1,0:T(1,128)} %param.8) | copy-start | bytes 36868
  10.0 31.3 %collective-permute-start = (bf16[384,1152]{0,1:T(8,128)(2,1)}, bf16[384,1152]{0,1:T(8,128)(2,1)}, u32[]{:S(2)}, u32[]{:S(2)}) collective-permute-start(bf16[384,1152]{0,1:T(8,128)(2,1)} %get-tuple-element.65), channel_id=1, source_target_pairs={{0,4},{4,8},{8,12},{12,16},{16,20},{20,24},{24,28},{1,5},{5,9},{9,... | collective-permute-start | bytes 2654216 | tf_op jit(solution)/shard_map/ppermute | solution.py:17
  13.3 31.6 %collective-permute-start.1 = (bf16[384,1152]{0,1:T(8,128)(2,1)}, bf16[384,1152]{0,1:T(8,128)(2,1)}, u32[]{:S(2)}, u32[]{:S(2)}) collective-permute-start(bf16[384,1152]{0,1:T(8,128)(2,1)} %get-tuple-element.65), channel_id=1, source_target_pairs={{4,0},{8,4},{12,8},{16,12},{20,16},{24,20},{28,24},{5,1},{9,5},{13... | collective-permute-start | bytes 2654216 | tf_op jit(solution)/shard_map/ppermute | solution.py:17
  14.6 32.6 %collective-permute-start.2 = (bf16[384,1152]{0,1:T(8,128)(2,1)}, bf16[384,1152]{0,1:T(8,128)(2,1)}, u32[]{:S(2)}, u32[]{:S(2)}) collective-permute-start(bf16[384,1152]{0,1:T(8,128)(2,1)} %get-tuple-element.65), channel_id=1, source_target_pairs={{0,8},{4,12},{8,16},{12,20},{16,24},{20,28},{1,9},{5,13},{9,17},{1... | collective-permute-start | bytes 2654216 | tf_op jit(solution)/shard_map/ppermute | solution.py:17
  21.5 55.9 %collective-permute-start.3 = (bf16[384,1152]{0,1:T(8,128)(2,1)}, bf16[384,1152]{0,1:T(8,128)(2,1)}, u32[]{:S(2)}, u32[]{:S(2)}) collective-permute-start(bf16[384,1152]{0,1:T(8,128)(2,1)} %get-tuple-element.65), channel_id=1, source_target_pairs={{8,0},{12,4},{16,8},{20,12},{24,16},{28,20},{9,1},{13,5},{17,9},{2... | collective-permute-start | bytes 2654216 | tf_op jit(solution)/shard_map/ppermute | solution.py:17
  22.7 56.8 %collective-permute-start.4 = (bf16[384,1152]{0,1:T(8,128)(2,1)}, bf16[384,1152]{0,1:T(8,128)(2,1)}, u32[]{:S(2)}, u32[]{:S(2)}) collective-permute-start(bf16[384,1152]{0,1:T(8,128)(2,1)} %get-tuple-element.65), channel_id=1, source_target_pairs={{0,12},{4,16},{8,20},{12,24},{16,28},{1,13},{5,17},{9,21},{13,25},... | collective-permute-start | bytes 2654216 | tf_op jit(solution)/shard_map/ppermute | solution.py:17
  41.3 49.3 %collective-permute-start.5 = (bf16[384,1152]{0,1:T(8,128)(2,1)}, bf16[384,1152]{0,1:T(8,128)(2,1)S(1)}, u32[]{:S(2)}, u32[]{:S(2)}) collective-permute-start(bf16[384,1152]{0,1:T(8,128)(2,1)} %get-tuple-element.65), channel_id=1, source_target_pairs={{12,0},{16,4},{20,8},{24,12},{28,16},{13,1},{17,5},{21,9},{25,13},... | collective-permute-start | bytes 2654216 | tf_op jit(solution)/shard_map/ppermute | solution.py:17
  110.2 46.0 %copy-start.1 = (bf16[1,384,1152]{2,1,0:T(8,128)(2,1)S(1)}, bf16[1,384,1152]{2,1,0:T(8,128)(2,1)}, u32[]{:S(2)}) copy-start(bf16[1,384,1152]{2,1,0:T(8,128)(2,1)} %param.7) | copy-start | bytes 2654212
  158.1 19.8 %copy-start.2 = (bf16[384,1152]{1,0:T(8,128)(2,1)}, bf16[384,1152]{1,0:T(8,128)(2,1)S(1)}, u32[]{:S(2)}) copy-start(bf16[384,1152]{1,0:T(8,128)(2,1)S(1)} %fusion.25) | copy-start | bytes 2654212
where the time goes:
time: 179 us; the launch traced here: 178 us
  matrix products  46.4 us (26%)
  waiting for transfers between devices  36.7 us (21%)
  local copies, waits for them, and re-layouts  32.8 us (18%)
  blocking collectives  31.7 us (18%)
  starting transfers between devices  18.4 us (10%)
  other arithmetic  11.1 us (6%)
    ppermute x6, waiting for transfers between devices, shifted(): return lax.ppermute(value, axis, pairs)  36.7 us
    dot_general x8, matrix products, head_terms(): jnp.dot(probs.astype(jnp.bfloat16), value_head, preferred_element_type=jn...  21.9 us
    ppermute x6, starting transfers between devices, shifted(): return lax.ppermute(value, axis, pairs)  18.4 us
    psum x1, blocking collectives, local(): lax.psum(partial_sums.astype(jnp.bfloat16), 'grp').astype(jnp.float32)  18.3 us
    dot_general x8, matrix products, head_terms(): lax.dot_general(query_head, key_head, (((1,), (1,)), ((), ())), preferred...  16.4 us
    all_gather x1, blocking collectives, local(): lax.all_gather(text_embed, 'blk', axis=0, tiled=True)  13.4 us
    reshape x3, local copies, waits for them, and re-layouts, split_heads(): return matrix.reshape(matrix.shape[0], HEADS, -1).transpose(1, 0, 2)  13 us
    unnamed x21, local copies, waits for them, and re-layouts  11.3 us
  transfers between devices with their start and end apart: 6, of which 2 were waited for; matrix products, arithmetic and copies ran while one was open for 7% of the time, Pallas kernels for 0%

commit v1 on v0

v1 whole, which is shorter than its diff:
```python
import functools
import math

import jax
import jax.numpy as jnp
from jax import lax
from jax.experimental import pallas as pl
from jax.experimental.pallas import tpu as pltpu
from jax.sharding import PartitionSpec as P

HEADS = 8
MAXP = 1024
LANES = 128
SPARE = 8
HIDDEN = -1e30

logit_scale = 30.0
logit_bias = -5.0

VMEM_LIMIT = 56 * 1024 * 1024


def rounded_up(value, step):
    return (value + step - 1) // step * step


def split_in_two(total, images):
    row = lax.broadcasted_iota(jnp.int32, total.shape, 0)
    main = total.astype(jnp.bfloat16).astype(jnp.float32)
    return jnp.where(row < images, main, total - main)


def image_rows(ids, images):
    row = lax.broadcasted_iota(jnp.int32, (SPARE, ids.shape[1]), 0)
    return (lax.rem(row, images) == ids).astype(jnp.float32).astype(jnp.bfloat16)


def project_kernel(images, piggy, ids_ref, rows_ref, weight_ref, out_ref, weight, turned, sem):
    fetch = pltpu.make_async_copy(weight_ref, weight, sem)
    fetch.start()
    count, depth = rows_ref.shape
    width = weight.shape[1] // 3
    size = width // HEADS
    rows = rows_ref[...]
    values = rows.astype(jnp.float32)
    center = values - jnp.mean(values, axis=1, keepdims=True)
    spread = jnp.mean(center * center, axis=1, keepdims=True)
    normed = (center * lax.rsqrt(spread + 1e-06)).astype(jnp.bfloat16)
    if piggy:
        own = lax.axis_index("grp") * count
        ids = ids_ref[:, pl.ds(pl.multiple_of(own, LANES), count)]
        sums = jnp.dot(image_rows(ids, images), rows, preferred_element_type=jnp.float32)
        sums = split_in_two(sums, images)
    fetch.wait()
    step = 3 * LANES
    for first in range(0, 3 * width, step):
        last = min(first + step, 3 * width)
        part = jnp.dot(normed, weight[:, first:last], preferred_element_type=jnp.float32)
        turned[first:last, :] = part.T
    for head in range(HEADS):
        query, key, value = (
            turned[at * width + head * size : at * width + (head + 1) * size, :] for at in range(3)
        )
        if piggy:
            spare = jnp.concatenate(
                [
                    sums[:, head * LANES : (head + 1) * LANES],
                    sums[:, HEADS * LANES :],
                    jnp.zeros((SPARE, count - depth + (HEADS - 1) * LANES), jnp.float32),
                ],
                axis=1,
            )
        else:
            spare = jnp.zeros((SPARE, count), jnp.float32)
        block = jnp.concatenate([value, key, spare, query], axis=0)
        out_ref[head] = block.astype(jnp.bfloat16)


def attend_kernel(images, piggy, halo, ids_ref, got_ref, *rest):
    if halo:
        left_ref, right_ref, out_ref, keys, values, queries, attended, starts = rest
    else:
        out_ref, keys, values, queries, attended, starts = rest
    count = got_ref.shape[2]
    padded = attended.shape[0]
    size = padded - SPARE
    total_rows = HEADS * count
    length = ids_ref.shape[1]
    window = min(rounded_up(MAXP + LANES - 1, LANES), length)
    tile = 2 * LANES
    bits = max(1, (images - 1).bit_length())
    ids = ids_ref[...]
    for image in range(images):
        starts[image] = jnp.sum((ids < image).astype(jnp.int32))

    row = lax.broadcasted_iota(jnp.int32, (SPARE, length), 0)
    bit = jnp.bitwise_and(lax.shift_right_logical(jnp.broadcast_to(ids, row.shape), row >> 1), 1)
    odd = jnp.bitwise_and(row, 1)
    used = row < 2 * bits
    outside = jnp.logical_or(ids < 0, ids >= images)
    key_side = jnp.where(odd == 1, bit, 1 - bit).astype(jnp.float32)
    key_side = jnp.where(outside, 1.0, key_side)
    key_side = jnp.where(used, key_side * HIDDEN, 0.0)
    query_side = jnp.where(used, jnp.where(odd == 1, 1 - bit, bit), 0).astype(jnp.float32)

    def with_rows(marks, block):
        return jnp.concatenate([marks, block.astype(jnp.float32)[SPARE:]], axis=0).astype(jnp.bfloat16)

    key_at = size - SPARE
    query_at = 2 * size
    for source in range(HEADS):
        here = slice(halo + source * count, halo + (source + 1) * count)
        there = slice(source * count, (source + 1) * count)
        values[:, here] = got_ref[source, 0:padded]
        keys[0:16, here] = with_rows(key_side[:, here], got_ref[source, key_at : key_at + 16])
        keys[16:padded, here] = got_ref[source, key_at + 16 : key_at + padded]
        queries[0:16, there] = with_rows(query_side[:, here], got_ref[source, query_at : query_at + 16])
        queries[16:padded, there] = got_ref[source, query_at + 16 : query_at + padded]
    if halo:
        for ref, here in ((left_ref, slice(0, halo)), (right_ref, slice(length - halo, length))):
            values[:, here] = ref[0:padded]
            keys[0:16, here] = with_rows(key_side[:, here], ref[key_at : key_at + 16])
            keys[16:padded, here] = ref[key_at + 16 : key_at + padded]

    def one_tile(at, _):
        first = pl.multiple_of(at * tile, tile)
        lowest = jnp.int32(0)
        highest = jnp.int32(0)
        for image in range(1, images):
            lowest += (starts[image] <= halo + first).astype(jnp.int32)
            highest += (starts[image] <= halo + first + tile - 1).astype(jnp.int32)
        query = queries[:, pl.ds(first, tile)]
        labels = ids_ref[:, pl.ds(pl.multiple_of(halo + first, LANES), tile)]

        def one_image(image, _):
            begin = jnp.minimum(starts[image] // LANES * LANES, length - window)
            here = pl.ds(pl.multiple_of(begin, LANES), window)
            scores = lax.dot_general(
                keys[:, here], query, (((0,), (0,)), ((), ())), preferred_element_type=jnp.float32
            )
            top = jnp.max(scores, axis=0, keepdims=True)
            probs = jnp.exp2((scores - top) * (size ** (-0.5) * math.log2(math.e)))
            total = jnp.sum(probs, axis=0, keepdims=True)
            weighted = jnp.dot(
                values[:, here], probs.astype(jnp.bfloat16), preferred_element_type=jnp.float32
            )
            result = weighted / total
            place = (slice(None), pl.ds(first, tile))
            attended[place] = jnp.where(labels == image, result, attended[place])
            return 0

        lax.fori_loop(lowest, highest + 1, one_image, 0)
        return 0

    lax.fori_loop(0, total_rows // tile, one_tile, 0)

    odd_head = lax.rem(lax.axis_index("grp"), 2) == 1
    mine = ids[:, halo : halo + total_rows]

    def placed(block, spare):
        even = jnp.concatenate([block[0:size], spare], axis=0)
        odd = jnp.concatenate([spare, block[0:size]], axis=0)
        return jnp.where(odd_head, odd, even)

    if piggy:
        nothing = jnp.zeros((SPARE, total_rows), jnp.float32)
        flat = placed(attended[...], nothing).astype(jnp.bfloat16)
        pooled = lax.dot_general(
            image_rows(mine, images), flat, (((1,), (1,)), ((), ())), preferred_element_type=jnp.float32
        )
        pooled = split_in_two(pooled, images)
        sums = jnp.zeros((SPARE, 2 * LANES), jnp.float32)
        for source in range(HEADS):
            sums += got_ref[source, query_at : query_at + 16].astype(jnp.float32)[0:SPARE, 0 : 2 * LANES]
        sums = split_in_two(sums + pltpu.roll(sums, images, axis=0), images)
        spare = jnp.concatenate(
            [pooled, jnp.zeros((SPARE, LANES - padded), jnp.float32), sums], axis=1
        )
    else:
        spare = jnp.zeros((SPARE, count), jnp.float32)
    for source in range(HEADS):
        block = placed(attended[:, source * count : (source + 1) * count], spare)
        out_ref[source] = block.astype(jnp.bfloat16)


def joined_heads(got_ref, out_weight_ref, flat, weight):
    padded = got_ref.shape[1]
    size = padded - SPARE
    spares = []
    for head in range(HEADS):
        at = head * padded
        from_row = head * size - (SPARE if head % 2 else 0)
        weight[at : at + padded] = out_weight_ref[from_row : from_row + padded]
        edge = 0 if head % 2 else padded - 16
        rest = slice(16, padded) if head % 2 else slice(0, padded - 16)
        mixed_rows = got_ref[head, edge : edge + 16].astype(jnp.float32)
        nothing = jnp.zeros((SPARE, mixed_rows.shape[1]), jnp.float32)
        if head % 2:
            spares.append(mixed_rows[:SPARE])
            block = jnp.concatenate([nothing, mixed_rows[SPARE:]], axis=0)
        else:
            spares.append(mixed_rows[SPARE:])
            block = jnp.concatenate([mixed_rows[:SPARE], nothing], axis=0)
        flat[at + edge : at + edge + 16] = block.astype(jnp.bfloat16)
        flat[at + rest.start : at + rest.stop] = got_ref[head, rest]
    return spares


def mixed_rows_of(rows_ref, flat, weight):
    added = lax.dot_general(
        flat[...], weight[...], (((0,), (0,)), ((), ())), preferred_element_type=jnp.float32
    )
    return (rows_ref[...].astype(jnp.float32) + added).astype(jnp.bfloat16)


def unit_rows(matrix):
    return matrix * lax.rsqrt(jnp.sum(matrix * matrix, axis=1, keepdims=True) + 1e-06)


def losses(cosine, labels):
    logits = -labels * (logit_scale * cosine + logit_bias)
    return jnp.maximum(logits, 0.0) + jnp.log1p(jnp.exp(-jnp.abs(logits)))


def finish_kernel(images, rows_ref, got_ref, out_weight_ref, text_ref, mixed_ref, loss_ref, flat, weight, pooled_heads):
    padded = got_ref.shape[1]
    spares = joined_heads(got_ref, out_weight_ref, flat, weight)
    for head in range(HEADS):
        pooled_heads[:, head * padded : (head + 1) * padded] = spares[head][:, 0:padded]
    pooled = jnp.dot(
        pooled_heads[...].astype(jnp.bfloat16), weight[...], preferred_element_type=jnp.float32
    )
    patch_sums = [spare[:, LANES : 2 * LANES] for spare in spares] + [spares[0][:, 2 * LANES :]]
    pooled = pooled + jnp.concatenate(patch_sums, axis=1)
    pooled = pooled + pltpu.roll(pooled, images, axis=0)
    image_vecs = unit_rows(pooled)
    text_vecs = unit_rows(text_ref[...].astype(jnp.float32))
    cosine = lax.dot_general(
        text_vecs,
        image_vecs,
        (((1,), (1,)), ((), ())),
        precision=lax.Precision.HIGHEST,
        preferred_element_type=jnp.float32,
    )
    text = lax.broadcasted_iota(jnp.int32, cosine.shape, 0)
    image = lax.broadcasted_iota(jnp.int32, cosine.shape, 1)
    terms = losses(cosine, jnp.where(text == image, 1.0, -1.0))
    loss_ref[...] = jnp.sum(terms, axis=0, keepdims=True)[:, 0:images]
    mixed_ref[...] = mixed_rows_of(rows_ref, flat, weight)


def mix_kernel(rows_ref, got_ref, out_weight_ref, mixed_ref, flat, weight):
    joined_heads(got_ref, out_weight_ref, flat, weight)
    mixed_ref[...] = mixed_rows_of(rows_ref, flat, weight)


def in_vmem(count):
    return [pl.BlockSpec(memory_space=pltpu.VMEM)] * count


def call(kernel, out_shape, scratch, in_specs, flops):
    out_specs = jax.tree.map(lambda _: pl.BlockSpec(memory_space=pltpu.VMEM), out_shape)
    return pl.pallas_call(
        kernel,
        out_shape=out_shape,
        in_specs=in_specs,
        out_specs=out_specs,
        scratch_shapes=scratch,
        compiler_params=pltpu.CompilerParams(vmem_limit_bytes=VMEM_LIMIT),
        cost_estimate=pl.CostEstimate(flops=flops, bytes_accessed=8 << 20, transcendentals=0),
    )


def moved(value, axis, pairs):
    return lax.ppermute(value, axis, pairs)


def all_texts(texts):
    peers = lax.axis_size("blk")
    if peers & (peers - 1):
        shifts = range(1, peers)
        others = [moved(texts, "blk", [(i, (i + by) % peers) for i in range(peers)]) for by in shifts]
        return jnp.concatenate([texts] + others, axis=0)
    by = 1
    while by < peers:
        other = moved(texts, "blk", [(i, i ^ by) for i in range(peers)])
        texts = jnp.concatenate([texts, other], axis=0)
        by *= 2
    return texts


def exchanged(blocks, groups):
    return lax.all_to_all(blocks, "grp", 0, 0, axis_index_groups=groups, tiled=True)


def local(patches, segment_ids, qkv_weight, out_weight, text_embed):
    rows = patches[0]
    count, depth = rows.shape
    width = out_weight.shape[0]
    size = width // HEADS
    padded = size + SPARE
    images = text_embed.shape[0]
    group_size = lax.axis_size("grp")
    parts = group_size // HEADS
    piggy = parts == 1 and 2 * images == SPARE and count >= depth - (HEADS - 2) * LANES
    groups = None if parts == 1 else [list(range(p * HEADS, (p + 1) * HEADS)) for p in range(parts)]
    bf16, f32 = jnp.bfloat16, jnp.float32
    shape = jax.ShapeDtypeStruct

    blocks = call(
        functools.partial(project_kernel, images, piggy),
        shape((HEADS, 3 * size + SPARE, count), bf16),
        [
            pltpu.VMEM((depth, 3 * width), bf16),
            pltpu.VMEM((3 * width, count), f32),
            pltpu.SemaphoreType.DMA,
        ],
        in_vmem(2) + [pl.BlockSpec(memory_space=pl.ANY)],
        2 * count * depth * 3 * width,
    )(segment_ids, rows, qkv_weight)
    got = exchanged(blocks, groups)
    texts = all_texts(text_embed)

    length = HEADS * count
    halo = 0
    operands = [segment_ids, got]
    if parts > 1:
        halo = rounded_up(MAXP - 1, LANES)
        part = lax.axis_index("grp") // HEADS
        whole_ids = jnp.concatenate(
            [
                jnp.full((1, halo), -1, jnp.int32),
                segment_ids,
                jnp.full((1, halo), images, jnp.int32),
            ],
            axis=1,
        )
        near_ids = lax.dynamic_slice_in_dim(whole_ids, part * length, length + 2 * halo, axis=1)
        flat = got[:, : 2 * size].transpose(1, 0, 2).reshape(2 * size, length)
        flat = jnp.concatenate([flat, jnp.zeros((16, length), bf16)], axis=0)
        ahead = [(i, i + HEADS) for i in range(group_size - HEADS)]
        back = [(i + HEADS, i) for i in range(group_size - HEADS)]
        left = moved(flat[:, length - halo :], "grp", ahead)
        right = moved(flat[:, :halo], "grp", back)
        operands = [near_ids, got, left, right]
    reach = length + 2 * halo
    answers = call(
        functools.partial(attend_kernel, images, piggy, halo),
        shape((HEADS, padded, count), bf16),
        [
            pltpu.VMEM((padded, reach), bf16),
            pltpu.VMEM((padded, reach), bf16),
            pltpu.VMEM((padded, length), bf16),
            pltpu.VMEM((padded, length), f32),
            pltpu.SMEM((images,), jnp.int32),
        ],
        in_vmem(len(operands)),
        4 * size * length * MAXP,
    )(*operands)
    back_home = exchanged(answers, groups)

    joined = [pltpu.VMEM((HEADS * padded, count), bf16), pltpu.VMEM((HEADS * padded, depth), bf16)]
    flops = 2 * count * depth * width
    if piggy:
        mixed, row_loss = call(
            functools.partial(finish_kernel, images),
            (shape((count, depth), bf16), shape((1, images), f32)),
            joined + [pltpu.VMEM((SPARE, HEADS * padded), f32)],
            in_vmem(4),
            flops,
        )(rows, back_home, out_weight, texts)
        return (mixed[None], row_loss[0])
    mixed = call(mix_kernel, shape((count, depth), bf16), joined, in_vmem(3), flops)(
        rows, back_home, out_weight
    )
    own_ids = lax.dynamic_slice_in_dim(segment_ids[0], lax.axis_index("grp") * count, count)
    onehot = (own_ids[None, :] == jnp.arange(images, dtype=jnp.int32)[:, None]).astype(bf16)
    pooled = lax.psum(jnp.dot(onehot, mixed, preferred_element_type=f32), "grp")
    text_vecs = unit_rows(texts.astype(f32))
    cosine = jnp.dot(unit_rows(pooled), text_vecs.T, precision=lax.Precision.HIGHEST)
    same = jnp.arange(images)[:, None] == jnp.arange(texts.shape[0])[None, :]
    row_loss = jnp.sum(losses(cosine, jnp.where(same, 1.0, -1.0)), axis=1)
    return (mixed[None], row_loss)


def solution(mesh):
    placed = (P("blk", "grp", None), P("blk", None), P(), P(), P("blk", None))
    return jax.shard_map(
        local,
        mesh=mesh,
        in_specs=placed,
        out_specs=(P("blk", "grp", None), P("blk")),
        check_vma=False,
    )
```

time: 179 us -> 72.2 us (0.40)
  matrix products: 46.4 us -> 0 us
  blocking collectives: 31.7 us -> 0 us
  Pallas kernels: 0 us -> 26.2 us
  local copies, waits for them, and re-layouts: 32.8 us -> 8.3 us
  waiting for transfers between devices: 36.7 us -> 23.3 us
  other arithmetic: 11.1 us -> 0.63 us
  starting transfers between devices: 18.4 us -> 13 us
    dot_general x20 -> x0, matrix products: 46.4 us -> none  [the longest x8 21.9 us: head_terms(): jnp.dot(probs.astype(jnp.bfloat16), value_head, preferred_element_type=jn...]
    ppermute x6 -> x2, waiting for transfers between devices: 36.7 us -> 2.27 us  [moved(): return lax.ppermute(value, axis, pairs)]
    pallas_call x0 -> x3, Pallas kernels: none -> 26.2 us  [the longest x1 15.1 us: local(): call(functools.partial(attend_kernel, images, piggy, halo), shape((HEADS,...]
    all_to_all x0 -> x2, waiting for transfers between devices: none -> 21 us  [exchanged(): lax.all_to_all(blocks, 'grp', 0, 0, axis_index_groups=groups, tiled=True)]
    psum x1 -> x0, blocking collectives: 18.3 us -> none  [local(): lax.psum(partial_sums.astype(jnp.bfloat16), 'grp').astype(jnp.float32)]
    ppermute x6 -> x2, starting transfers between devices: 18.4 us -> 4.32 us  [moved(): return lax.ppermute(value, axis, pairs)]
    all_gather x1 -> x0, blocking collectives: 13.4 us -> none  [local(): lax.all_gather(text_embed, 'blk', axis=0, tiled=True)]
    reshape x3 -> x0, local copies, waits for them, and re-layouts: 13 us -> none  [split_heads(): return matrix.reshape(matrix.shape[0], HEADS, -1).transpose(1, 0, 2)]
  transfers between devices with their start and end apart: 6 -> 4, of which waited for: 2 -> 3; matrix products, arithmetic and copies ran while one was open for 7% -> 1% of each run, Pallas kernels for 0% -> 21%
where the time goes in v1:
time: 72.2 us; the launch traced here: 72.1 us
  Pallas kernels  26.2 us (36%)
  waiting for transfers between devices  23.3 us (32%)
  starting transfers between devices  13 us (18%)
  local copies, waits for them, and re-layouts  8.3 us (11%)
    all_to_all x2, waiting for transfers between devices, exchanged(): lax.all_to_all(blocks, 'grp', 0, 0, axis_index_groups=groups, tiled=True)  21 us
    pallas_call x1, Pallas kernels, local(): call(functools.partial(attend_kernel, images, piggy, halo), shape((HEADS,...  15.1 us
    all_to_all x2, starting transfers between devices, exchanged(): lax.all_to_all(blocks, 'grp', 0, 0, axis_index_groups=groups, tiled=True)  8.67 us
    unnamed x7, local copies, waits for them, and re-layouts  8.3 us
    pallas_call x1, Pallas kernels, local(): call(functools.partial(project_kernel, images, piggy), shape((HEADS, 3 *...  6.94 us
    ppermute x2, starting transfers between devices, moved(): return lax.ppermute(value, axis, pairs)  4.32 us
    pallas_call x1, Pallas kernels, local(): call(functools.partial(finish_kernel, images), (shape((count, depth), bf1...  4.14 us
    ppermute x2, waiting for transfers between devices, moved(): return lax.ppermute(value, axis, pairs)  2.27 us
  transfers between devices with their start and end apart: 4, of which 3 were waited for; matrix products, arithmetic and copies ran while one was open for 1% of the time, Pallas kernels for 21%

profile of v1, /device:TPU:0, one launch (start us, length us, event | category | flops | bytes accessed | tf_op | source)
XLA Modules:
  0.0 72.1 jit_solution(13018012262155970023)
XLA Ops:
  0.6 6.4 %copy.7.weight_ref = bf16[1152,1728]{1,0:T(8,128)(2,1)} copy(bf16[1152,1728]{0,1:T(8,128)(2,1)} %param.7) | data formatting | bytes 7962624 | tf_op args[2]
  7.0 6.9 %shard_map.68 = bf16[8,224,384]{2,1,0:T(8,128)(2,1)} custom-call(s32[1,3072]{1,0:T(1,128)} %ids_ref.3, bf16[384,1152]{1,0:T(8,128)(2,1)} %bitcast.3, bf16[1152,1728]{1,0:T(8,128)(2,1)} %copy.7.weight_ref), custom_call_target="tpu_custom_call" | custom-call | flops 1528823808 | bytes 8388608 | tf_op jit(solution)/shard_map/pallas_call | solution.py:310
  14.0 0.0 copy-start.2
  14.0 5.2 %all-to-all-start = ((bf16[8,224,384]{2,1,0:T(8,128)(2,1)}), bf16[8,224,384]{2,1,0:T(8,128)(2,1)S(1)}, u32[]{:S(2)}, u32[]{:S(2)}) async-start(bf16[8,224,384]{2,1,0:T(8,128)(2,1)} %shard_map.68), calls=%async_computation | async-start | bytes 2752512 | tf_op jit(solution)/shard_map/all_to_all | solution.py:293
  19.2 0.0 copy-done.2
  19.2 1.6 %collective-permute-start = (bf16[4,1152]{1,0:T(4,128)(2,1)S(1)}, bf16[4,1152]{1,0:T(4,128)(2,1)S(1)}, u32[]{:S(2)}, u32[]{:S(2)}) collective-permute-start(bf16[4,1152]{1,0:T(4,128)(2,1)S(1)} %copy-done.2), channel_id=1, source_target_pairs={{0,1},{1,0},{2,3},{3,2},{4,5},{5,4},{6,7},{7,6},{8,9},{9,8},{10,11... | collective-permute-start | bytes 27656 | tf_op jit(solution)/shard_map/ppermute | solution.py:275
  20.8 17.3 %all-to-all-done.got_ref = bf16[8,224,384]{2,1,0:T(8,128)(2,1)S(1)} async-done(((bf16[8,224,384]{2,1,0:T(8,128)(2,1)}), bf16[8,224,384]{2,1,0:T(8,128)(2,1)S(1)}, u32[]{:S(2)}, u32[]{:S(2)}) %all-to-all-start) | async-done | bytes 1376288 | tf_op jit(solution)/shard_map/all_to_all | solution.py:293
  38.1 0.0 copy-start.1
  38.1 1.1 %copy-done.1 = bf16[8,224,384]{2,1,0:T(8,128)(2,1)} copy-done((bf16[8,224,384]{2,1,0:T(8,128)(2,1)}, bf16[8,224,384]{2,1,0:T(8,128)(2,1)S(1)}, u32[]{:S(2)}) %copy-start.1) | copy-done | bytes 1376280
  39.2 15.1 %shard_map.69 = bf16[8,80,384]{2,1,0:T(8,128)(2,1)} custom-call(s32[1,3072]{1,0:T(1,128)} %ids_ref.3, bf16[8,224,384]{2,1,0:T(8,128)(2,1)} %copy-done.1), custom_call_target="tpu_custom_call" | custom-call | flops 905969664 | bytes 8388608 | tf_op jit(solution)/shard_map/pallas_call | solution.py:347
  54.3 3.5 %all-to-all-start.1 = ((bf16[8,80,384]{2,1,0:T(8,128)(2,1)}), bf16[8,80,384]{2,1,0:T(8,128)(2,1)S(1)}, u32[]{:S(2)}, u32[]{:S(2)}) async-start(bf16[8,80,384]{2,1,0:T(8,128)(2,1)} %shard_map.69), calls=%async_computation.1 | async-start | bytes 983040 | tf_op jit(solution)/shard_map/all_to_all | solution.py:293
  57.8 0.0 collective-permute-done
  57.9 2.7 %collective-permute-start.1 = (bf16[8,1152]{1,0:T(8,128)(2,1)S(1)}, bf16[8,1152]{1,0:T(8,128)(2,1)S(1)}, u32[]{:S(2)}, u32[]{:S(2)}) collective-permute-start(bf16[8,1152]{1,0:T(8,128)(2,1)S(1)} %pad_maximum_fusion.1), channel_id=1, source_target_pairs={{0,2},{1,3},{2,0},{3,1},{4,6},{5,7},{6,4},{7,5},{8,10},{9,11},{10,... | collective-permute-start | bytes 55304 | tf_op jit(solution)/shard_map/ppermute | solution.py:275
  60.6 2.3 %collective-permute-done.1 = bf16[8,1152]{1,0:T(8,128)(2,1)S(1)} collective-permute-done((bf16[8,1152]{1,0:T(8,128)(2,1)S(1)}, bf16[8,1152]{1,0:T(8,128)(2,1)S(1)}, u32[]{:S(2)}, u32[]{:S(2)}) %collective-permute-start.1) | collective-permute-done | bytes 18464 | tf_op jit(solution)/shard_map/ppermute | solution.py:275
  62.8 0.6 pad_maximum_fusion.text_ref
  63.4 3.7 %all-to-all-done.1.got_ref = bf16[8,80,384]{2,1,0:T(8,128)(2,1)S(1)} async-done(((bf16[8,80,384]{2,1,0:T(8,128)(2,1)}), bf16[8,80,384]{2,1,0:T(8,128)(2,1)S(1)}, u32[]{:S(2)}, u32[]{:S(2)}) %all-to-all-start.1) | async-done | bytes 491552 | tf_op jit(solution)/shard_map/all_to_all | solution.py:293
  67.2 0.0 copy-start
  67.2 0.8 %copy-done = bf16[8,80,384]{2,1,0:T(8,128)(2,1)} copy-done((bf16[8,80,384]{2,1,0:T(8,128)(2,1)}, bf16[8,80,384]{2,1,0:T(8,128)(2,1)S(1)}, u32[]{:S(2)}) %copy-start) | copy-done | bytes 491544
  67.9 4.1 %shard_map.70 = (bf16[384,1152]{1,0:T(8,128)(2,1)}, f32[1,4]{1,0:T(1,128)}) custom-call(bf16[384,1152]{1,0:T(8,128)(2,1)} %bitcast.4, bf16[8,80,384]{2,1,0:T(8,128)(2,1)} %copy-done, bf16[576,1152]{1,0:T(8,128)(2,1)} %out_weight_ref.1, bf16[16,1152]{1,0:T(8,128)(2,1)} %pad_maximum_fusion.text_ref), custom_call_target="tpu_custom_call" | custom-call | flops 509607936 | bytes 8388608 | tf_op jit(solution)/shard_map/pallas_call | solution.py:365
  (1 shorter events, 0.0 us)
Async XLA Ops:
  14.0 5.2 %copy-start.2 = (bf16[4,1152]{1,0:T(4,128)(2,1)S(1)}, bf16[4,1152]{1,0:T(4,128)(2,1)}, u32[]{:S(2)}) copy-start(bf16[4,1152]{1,0:T(4,128)(2,1)} %param.9) | copy-start | bytes 27652
  14.0 24.1 %all-to-all-start = ((bf16[8,224,384]{2,1,0:T(8,128)(2,1)}), bf16[8,224,384]{2,1,0:T(8,128)(2,1)S(1)}, u32[]{:S(2)}, u32[]{:S(2)}) async-start(bf16[8,224,384]{2,1,0:T(8,128)(2,1)} %shard_map.68), calls=%async_computation | async-start | bytes 2752512 | tf_op jit(solution)/shard_map/all_to_all | solution.py:293
  19.2 38.6 %collective-permute-start = (bf16[4,1152]{1,0:T(4,128)(2,1)S(1)}, bf16[4,1152]{1,0:T(4,128)(2,1)S(1)}, u32[]{:S(2)}, u32[]{:S(2)}) collective-permute-start(bf16[4,1152]{1,0:T(4,128)(2,1)S(1)} %copy-done.2), channel_id=1, source_target_pairs={{0,1},{1,0},{2,3},{3,2},{4,5},{5,4},{6,7},{7,6},{8,9},{9,8},{10,11... | collective-permute-start | bytes 27656 | tf_op jit(solution)/shard_map/ppermute | solution.py:275
  38.1 1.1 %copy-start.1 = (bf16[8,224,384]{2,1,0:T(8,128)(2,1)}, bf16[8,224,384]{2,1,0:T(8,128)(2,1)S(1)}, u32[]{:S(2)}) copy-start(bf16[8,224,384]{2,1,0:T(8,128)(2,1)S(1)} %all-to-all-done.got_ref) | copy-start | bytes 4128772
  54.3 12.8 %all-to-all-start.1 = ((bf16[8,80,384]{2,1,0:T(8,128)(2,1)}), bf16[8,80,384]{2,1,0:T(8,128)(2,1)S(1)}, u32[]{:S(2)}, u32[]{:S(2)}) async-start(bf16[8,80,384]{2,1,0:T(8,128)(2,1)} %shard_map.69), calls=%async_computation.1 | async-start | bytes 983040 | tf_op jit(solution)/shard_map/all_to_all | solution.py:293
  57.9 5.0 %collective-permute-start.1 = (bf16[8,1152]{1,0:T(8,128)(2,1)S(1)}, bf16[8,1152]{1,0:T(8,128)(2,1)S(1)}, u32[]{:S(2)}, u32[]{:S(2)}) collective-permute-start(bf16[8,1152]{1,0:T(8,128)(2,1)S(1)} %pad_maximum_fusion.1), channel_id=1, source_target_pairs={{0,2},{1,3},{2,0},{3,1},{4,6},{5,7},{6,4},{7,5},{8,10},{9,11},{10,... | collective-permute-start | bytes 55304 | tf_op jit(solution)/shard_map/ppermute | solution.py:275
  67.2 0.8 %copy-start = (bf16[8,80,384]{2,1,0:T(8,128)(2,1)}, bf16[8,80,384]{2,1,0:T(8,128)(2,1)S(1)}, u32[]{:S(2)}) copy-start(bf16[8,80,384]{2,1,0:T(8,128)(2,1)S(1)} %all-to-all-done.1.got_ref) | copy-start | bytes 1474564

commit v2 on v1

--- a/solution.py
+++ b/solution.py
@@ -17,7 +17,7 @@
 logit_scale = 30.0
 logit_bias = -5.0
 
-VMEM_LIMIT = 56 * 1024 * 1024
+VMEM_LIMIT = 32 * 1024 * 1024
 
 
 def rounded_up(value, step):
@@ -35,12 +35,19 @@
     return (lax.rem(row, images) == ids).astype(jnp.float32).astype(jnp.bfloat16)
 
 
-def project_kernel(images, piggy, ids_ref, rows_ref, weight_ref, out_ref, weight, turned, sem):
-    fetch = pltpu.make_async_copy(weight_ref, weight, sem)
-    fetch.start()
+def project_kernel(images, piggy, ids_ref, rows_ref, weight_ref, out_ref, weight, turned, sems):
     count, depth = rows_ref.shape
-    width = weight.shape[1] // 3
+    width = weight.shape[0] // 3
     size = width // HEADS
+    pieces = sems.shape[0]
+    step = 3 * width // pieces
+    cuts = [slice(piece * step, (piece + 1) * step) for piece in range(pieces)]
+    fetches = [
+        pltpu.make_async_copy(weight_ref.at[cut], weight.at[cut], sems.at[piece])
+        for piece, cut in enumerate(cuts)
+    ]
+    for fetch in fetches:
+        fetch.start()
     rows = rows_ref[...]
     values = rows.astype(jnp.float32)
     center = values - jnp.mean(values, axis=1, keepdims=True)
@@ -51,12 +58,11 @@
         ids = ids_ref[:, pl.ds(pl.multiple_of(own, LANES), count)]
         sums = jnp.dot(image_rows(ids, images), rows, preferred_element_type=jnp.float32)
         sums = split_in_two(sums, images)
-    fetch.wait()
-    step = 3 * LANES
-    for first in range(0, 3 * width, step):
-        last = min(first + step, 3 * width)
-        part = jnp.dot(normed, weight[:, first:last], preferred_element_type=jnp.float32)
-        turned[first:last, :] = part.T
+    for fetch, cut in zip(fetches, cuts):
+        fetch.wait()
+        turned[cut, :] = lax.dot_general(
+            weight[cut, :], normed, (((1,), (1,)), ((), ())), preferred_element_type=jnp.float32
+        )
     for head in range(HEADS):
         query, key, value = (
             turned[at * width + head * size : at * width + (head + 1) * size, :] for at in range(3)
@@ -78,16 +84,16 @@
 
 def attend_kernel(images, piggy, halo, ids_ref, got_ref, *rest):
     if halo:
-        left_ref, right_ref, out_ref, keys, values, queries, attended, starts = rest
-    else:
-        out_ref, keys, values, queries, attended, starts = rest
+        left_ref, right_ref, *rest = rest
+    out_ref, keys, values, queries, attended, scores_a, scores_b, tops_a, tops_b, starts = rest
     count = got_ref.shape[2]
     padded = attended.shape[0]
     size = padded - SPARE
     total_rows = HEADS * count
     length = ids_ref.shape[1]
-    window = min(rounded_up(MAXP + LANES - 1, LANES), length)
-    tile = 2 * LANES
+    window = scores_a.shape[0]
+    tile = scores_a.shape[1]
+    tiles = total_rows // tile
     bits = max(1, (images - 1).bit_length())
     ids = ids_ref[...]
     for image in range(images):
@@ -108,51 +114,80 @@
 
     key_at = size - SPARE
     query_at = 2 * size
+    blank = jnp.zeros((LANES - padded, count), jnp.float32)
+
+    def turned_keys(here, block):
+        marked = jnp.concatenate([key_side[:, here], block.astype(jnp.float32)[SPARE:]], axis=0)
+        filled = jnp.concatenate([marked, jnp.zeros((LANES - padded, block.shape[1]), jnp.float32)], axis=0)
+        return filled.T.astype(jnp.bfloat16)
+
     for source in range(HEADS):
         here = slice(halo + source * count, halo + (source + 1) * count)
         there = slice(source * count, (source + 1) * count)
         values[:, here] = got_ref[source, 0:padded]
-        keys[0:16, here] = with_rows(key_side[:, here], got_ref[source, key_at : key_at + 16])
-        keys[16:padded, here] = got_ref[source, key_at + 16 : key_at + padded]
+        keys[here, :] = turned_keys(here, got_ref[source, key_at : key_at + padded])
         queries[0:16, there] = with_rows(query_side[:, here], got_ref[source, query_at : query_at + 16])
         queries[16:padded, there] = got_ref[source, query_at + 16 : query_at + padded]
+        queries[padded:, there] = blank.astype(jnp.bfloat16)
     if halo:
         for ref, here in ((left_ref, slice(0, halo)), (right_ref, slice(length - halo, length))):
             values[:, here] = ref[0:padded]
-            keys[0:16, here] = with_rows(key_side[:, here], ref[key_at : key_at + 16])
-            keys[16:padded, here] = ref[key_at + 16 : key_at + padded]
-
-    def one_tile(at, _):
+            keys[here, :] = turned_keys(here, ref[key_at : key_at + padded])
+
+    def image_at(position):
+        found = jnp.int32(0)
+        for image in range(1, images):
+            found += (starts[image] <= position).astype(jnp.int32)
+        return found
+
+    def following(state):
+        at, image = state
+        more = image < image_at(halo + at * tile + tile - 1)
+        later = jnp.minimum(at + 1, tiles - 1)
+        first = jnp.maximum(image_at(halo + later * tile), jnp.where(later == at, image, 0))
+        return jnp.where(more, at, later), jnp.where(more, image + 1, first)
+
+    def window_of(image):
+        begin = jnp.minimum(starts[image] // LANES * LANES, length - window)
+        return pl.ds(pl.multiple_of(begin, LANES), window)
+
+    def score(state, scores, tops):
+        at, image = state
+        query = queries[:, pl.ds(pl.multiple_of(at * tile, tile), tile)]
+        found = jnp.dot(keys[window_of(image), :], query, preferred_element_type=jnp.float32)
+        scores[...] = found
+        tops[...] = jnp.max(found, axis=0, keepdims=True)
+
+    def weigh(state, scores, tops):
+        at, image = state
         first = pl.multiple_of(at * tile, tile)
-        lowest = jnp.int32(0)
-        highest = jnp.int32(0)
-        for image in range(1, images):
-            lowest += (starts[image] <= halo + first).astype(jnp.int32)
-            highest += (starts[image] <= halo + first + tile - 1).astype(jnp.int32)
-        query = queries[:, pl.ds(first, tile)]
         labels = ids_ref[:, pl.ds(pl.multiple_of(halo + first, LANES), tile)]
-
-        def one_image(image, _):
-            begin = jnp.minimum(starts[image] // LANES * LANES, length - window)
-            here = pl.ds(pl.multiple_of(begin, LANES), window)
-            scores = lax.dot_general(
-                keys[:, here], query, (((0,), (0,)), ((), ())), preferred_element_type=jnp.float32
-            )
-            top = jnp.max(scores, axis=0, keepdims=True)
-            probs = jnp.exp2((scores - top) * (size ** (-0.5) * math.log2(math.e)))
-            total = jnp.sum(probs, axis=0, keepdims=True)
-            weighted = jnp.dot(
-                values[:, here], probs.astype(jnp.bfloat16), preferred_element_type=jnp.float32
-            )
-            result = weighted / total
-            place = (slice(None), pl.ds(first, tile))
-            attended[place] = jnp.where(labels == image, result, attended[place])
-            return 0
-
-        lax.fori_loop(lowest, highest + 1, one_image, 0)
-        return 0
-
-    lax.fori_loop(0, total_rows // tile, one_tile, 0)
+        probs = jnp.exp2((scores[...] - tops[...]) * (size ** (-0.5) * math.log2(math.e)))
+        total = jnp.sum(probs, axis=0, keepdims=True)
+        weighted = jnp.dot(
+            values[:, window_of(image)], probs.astype(jnp.bfloat16), preferred_element_type=jnp.float32
+        )
+        place = (slice(None), pl.ds(first, tile))
+        attended[place] = jnp.where(labels == image, weighted / total, attended[place])
+
+    pairs = jnp.int32(tiles)
+    for image in range(1, images):
+        offset = starts[image] - halo
+        inside = jnp.logical_and(offset > 0, offset < total_rows)
+        pairs += jnp.logical_and(inside, lax.rem(offset, tile) != 0).astype(jnp.int32)
+
+    def two_pairs(_, state):
+        second = following(state)
+        score(second, scores_b, tops_b)
+        weigh(state, scores_a, tops_a)
+        third = following(second)
+        score(third, scores_a, tops_a)
+        weigh(second, scores_b, tops_b)
+        return third
+
+    begun = (jnp.int32(0), image_at(halo))
+    score(begun, scores_a, tops_a)
+    lax.fori_loop(0, (pairs + 1) // 2, two_pairs, begun)
 
     odd_head = lax.rem(lax.axis_index("grp"), 2) == 1
     mine = ids[:, halo : halo + total_rows]
@@ -311,15 +346,15 @@
         functools.partial(project_kernel, images, piggy),
         shape((HEADS, 3 * size + SPARE, count), bf16),
         [
-            pltpu.VMEM((depth, 3 * width), bf16),
+            pltpu.VMEM((3 * width, depth), bf16),
             pltpu.VMEM((3 * width, count), f32),
-            pltpu.SemaphoreType.DMA,
+            pltpu.SemaphoreType.DMA((4,)),
         ],
         in_vmem(2) + [pl.BlockSpec(memory_space=pl.ANY)],
         2 * count * depth * 3 * width,
-    )(segment_ids, rows, qkv_weight)
+    )(segment_ids, rows, qkv_weight.T)
     got = exchanged(blocks, groups)
-    texts = all_texts(text_embed)
+    got, texts = lax.optimization_barrier((got, all_texts(text_embed)))
 
     length = HEADS * count
     halo = 0
@@ -344,14 +379,20 @@
         right = moved(flat[:, :halo], "grp", back)
         operands = [near_ids, got, left, right]
     reach = length + 2 * halo
+    window = min(rounded_up(MAXP + LANES - 1, LANES), reach)
+    tile = 2 * LANES
     answers = call(
         functools.partial(attend_kernel, images, piggy, halo),
         shape((HEADS, padded, count), bf16),
         [
+            pltpu.VMEM((reach, LANES), bf16),
             pltpu.VMEM((padded, reach), bf16),
-            pltpu.VMEM((padded, reach), bf16),
-            pltpu.VMEM((padded, length), bf16),
+            pltpu.VMEM((LANES, length), bf16),
             pltpu.VMEM((padded, length), f32),
+            pltpu.VMEM((window, tile), f32),
+            pltpu.VMEM((window, tile), f32),
+            pltpu.VMEM((1, tile), f32),
+            pltpu.VMEM((1, tile), f32),
             pltpu.SMEM((images,), jnp.int32),
         ],
         in_vmem(len(operands)),

time: 72.2 us -> 57.5 us (0.80)
  blocking collectives: 0 us -> 11.8 us
  Pallas kernels: 26.2 us -> 17 us
  waiting for transfers between devices: 23.3 us -> 14.6 us
  local copies, waits for them, and re-layouts: 8.3 us -> 4.02 us
  starting transfers between devices: 13 us -> 9.48 us
    all_to_all x0 -> x1, blocking collectives: none -> 11.8 us  [exchanged(): lax.all_to_all(blocks, 'grp', 0, 0, axis_index_groups=groups, tiled=True)]
    all_to_all x2 -> x1, waiting for transfers between devices: 21 us -> 10.4 us  [exchanged(): lax.all_to_all(blocks, 'grp', 0, 0, axis_index_groups=groups, tiled=True)]
    pallas_call x1, Pallas kernels: 15.1 us -> 8.59 us  [local(): call(functools.partial(attend_kernel, images, piggy, halo), shape((HEADS,...]
    unnamed x7 -> x14, local copies, waits for them, and re-layouts: 8.3 us -> 4.02 us
    all_to_all x2 -> x1, starting transfers between devices: 8.67 us -> 5.18 us  [exchanged(): lax.all_to_all(blocks, 'grp', 0, 0, axis_index_groups=groups, tiled=True)]
    ppermute x2, waiting for transfers between devices: 2.27 us -> 4.15 us  [moved(): return lax.ppermute(value, axis, pairs)]
    pallas_call x1, Pallas kernels: 4.14 us -> 2.39 us  [local(): call(functools.partial(finish_kernel, images), (shape((count, depth), bf1...]
    pallas_call x1, Pallas kernels: 6.94 us -> 6.06 us  [local(): call(functools.partial(project_kernel, images, piggy), shape((HEADS, 3 *...]
  transfers between devices with their start and end apart: 4 -> 3, of which waited for: 3 -> 3; matrix products, arithmetic and copies ran while one was open for 1% -> 0% of each run, Pallas kernels for 21% -> 0%
where the time goes in v2:
time: 57.5 us; the launch traced here: 57.6 us
  Pallas kernels  17 us (30%)
  waiting for transfers between devices  14.6 us (25%)
  blocking collectives  11.8 us (21%)
  starting transfers between devices  9.48 us (16%)
  local copies, waits for them, and re-layouts  4.02 us (7%)
  between operations  0.69 us (1%)
    all_to_all x1, blocking collectives, exchanged(): lax.all_to_all(blocks, 'grp', 0, 0, axis_index_groups=groups, tiled=True)  11.8 us
    all_to_all x1, waiting for transfers between devices, exchanged(): lax.all_to_all(blocks, 'grp', 0, 0, axis_index_groups=groups, tiled=True)  10.4 us
    pallas_call x1, Pallas kernels, local(): call(functools.partial(attend_kernel, images, piggy, halo), shape((HEADS,...  8.59 us
    pallas_call x1, Pallas kernels, local(): call(functools.partial(project_kernel, images, piggy), shape((HEADS, 3 *...  6.06 us
    all_to_all x1, starting transfers between devices, exchanged(): lax.all_to_all(blocks, 'grp', 0, 0, axis_index_groups=groups, tiled=True)  5.18 us
    ppermute x2, starting transfers between devices, moved(): return lax.ppermute(value, axis, pairs)  4.3 us
    ppermute x2, waiting for transfers between devices, moved(): return lax.ppermute(value, axis, pairs)  4.15 us
    unnamed x14, local copies, waits for them, and re-layouts  4.02 us
  transfers between devices with their start and end apart: 3, of which 3 were waited for; matrix products, arithmetic and copies ran while one was open for 0% of the time, Pallas kernels for 0%

profile of v2, /device:TPU:0, one launch (start us, length us, event | category | flops | bytes accessed | tf_op | source)
XLA Modules:
  0.0 57.6 jit_solution(4435088417767140220)
XLA Ops:
  0.6 0.0 copy-start
  0.6 2.1 %copy-done = bf16[1152,1728]{0,1:T(8,128)(2,1)S(1)} copy-done((bf16[1152,1728]{0,1:T(8,128)(2,1)S(1)}, bf16[1152,1728]{0,1:T(8,128)(2,1)}, u32[]{:S(2)}) %copy-start) | copy-done | bytes 3981336
  2.8 0.0 copy-start.1
  2.8 1.2 %copy-done.1 = bf16[1,384,1152]{2,1,0:T(8,128)(2,1)S(1)} copy-done((bf16[1,384,1152]{2,1,0:T(8,128)(2,1)S(1)}, bf16[1,384,1152]{2,1,0:T(8,128)(2,1)}, u32[]{:S(2)}) %copy-start.1) | copy-done | bytes 884760
  3.9 0.0 copy-start.4
  3.9 0.7 %copy-done.4 = s32[1,3072]{1,0:T(1,128)S(1)} copy-done((s32[1,3072]{1,0:T(1,128)S(1)}, s32[1,3072]{1,0:T(1,128)}, u32[]{:S(2)}) %copy-start.4) | copy-done | bytes 12312
  4.6 6.1 %shard_map.68 = bf16[8,224,384]{2,1,0:T(8,128)(2,1)} custom-call(s32[1,3072]{1,0:T(1,128)S(1)} %copy-done.4, bf16[384,1152]{1,0:T(8,128)(2,1)S(1)} %bitcast.5, bf16[1728,1152]{1,0:T(8,128)(2,1)S(1)} %bitcast.4), custom_call_target="tpu_custom_call" | custom-call | flops 1528823808 | bytes 8388608 | tf_op jit(solution)/shard_map/pallas_call | solution.py:345
  10.7 0.0 copy-start.6
  10.7 0.0 copy-start.5
  10.7 5.2 %all-to-all-start = ((bf16[8,224,384]{2,1,0:T(8,128)(2,1)}), bf16[8,224,384]{2,1,0:T(8,128)(2,1)S(1)}, u32[]{:S(2)}, u32[]{:S(2)}) async-start(bf16[8,224,384]{2,1,0:T(8,128)(2,1)} %shard_map.68), calls=%async_computation | async-start | bytes 2752512 | tf_op jit(solution)/shard_map/all_to_all | solution.py:328
  15.9 0.0 copy-done.6
  15.9 1.6 %collective-permute-start = (bf16[4,1152]{1,0:T(4,128)(2,1)S(1)}, bf16[4,1152]{1,0:T(4,128)(2,1)S(1)}, u32[]{:S(2)}, u32[]{:S(2)}) collective-permute-start(bf16[4,1152]{1,0:T(4,128)(2,1)S(1)} %copy-done.6), channel_id=1, source_target_pairs={{0,1},{1,0},{2,3},{3,2},{4,5},{5,4},{6,7},{7,6},{8,9},{9,8},{10,11... | collective-permute-start | bytes 27656 | tf_op jit(solution)/shard_map/ppermute | solution.py:310
  17.6 2.1 %collective-permute-done = bf16[4,1152]{1,0:T(4,128)(2,1)S(1)} collective-permute-done((bf16[4,1152]{1,0:T(4,128)(2,1)S(1)}, bf16[4,1152]{1,0:T(4,128)(2,1)S(1)}, u32[]{:S(2)}, u32[]{:S(2)}) %collective-permute-start) | collective-permute-done | bytes 9248 | tf_op jit(solution)/shard_map/ppermute | solution.py:310
  19.7 2.7 %collective-permute-start.1 = (bf16[8,1152]{1,0:T(8,128)(2,1)S(1)}, bf16[8,1152]{1,0:T(8,128)(2,1)S(1)}, u32[]{:S(2)}, u32[]{:S(2)}) collective-permute-start(bf16[8,1152]{1,0:T(8,128)(2,1)S(1)} %pad_maximum_fusion.1), channel_id=1, source_target_pairs={{0,2},{1,3},{2,0},{3,1},{4,6},{5,7},{6,4},{7,5},{8,10},{9,11},{10,... | collective-permute-start | bytes 55304 | tf_op jit(solution)/shard_map/ppermute | solution.py:310
  22.3 2.1 %collective-permute-done.1 = bf16[8,1152]{1,0:T(8,128)(2,1)S(1)} collective-permute-done((bf16[8,1152]{1,0:T(8,128)(2,1)S(1)}, bf16[8,1152]{1,0:T(8,128)(2,1)S(1)}, u32[]{:S(2)}, u32[]{:S(2)}) %collective-permute-start.1) | collective-permute-done | bytes 18464 | tf_op jit(solution)/shard_map/ppermute | solution.py:310
  24.4 0.0 copy-start.2
  24.4 10.4 %all-to-all-done.got_ref = bf16[8,224,384]{2,1,0:T(8,128)(2,1)S(1)} async-done(((bf16[8,224,384]{2,1,0:T(8,128)(2,1)}), bf16[8,224,384]{2,1,0:T(8,128)(2,1)S(1)}, u32[]{:S(2)}, u32[]{:S(2)}) %all-to-all-start) | async-done | bytes 1376288 | tf_op jit(solution)/shard_map/all_to_all | solution.py:328
  34.8 0.0 copy-done.5
  34.8 0.0 copy-start.3
  34.8 8.6 %shard_map.69 = bf16[8,80,384]{2,1,0:T(8,128)(2,1)S(1)} custom-call(s32[1,3072]{1,0:T(1,128)S(1)} %copy-done.5, bf16[8,224,384]{2,1,0:T(8,128)(2,1)S(1)} %all-to-all-done.got_ref), custom_call_target="tpu_custom_call" | custom-call | flops 905969664 | bytes 8388608 | tf_op jit(solution)/shard_map/pallas_call | solution.py:384
  43.4 11.8 %all_to_all.10.got_ref = bf16[8,80,384]{2,1,0:T(8,128)(2,1)S(1)} all-to-all(bf16[8,80,384]{2,1,0:T(8,128)(2,1)S(1)} %shard_map.69), channel_id=1, replica_groups=mesh['grp'=8,'blk'=4] {'grp'}, dimensions={0} | all-to-all | bytes 983040 | tf_op jit(solution)/shard_map/all_to_all | solution.py:328
  55.2 0.0 copy-done.2
  55.2 0.0 copy-done.3
  55.2 2.4 %shard_map.70 = (bf16[384,1152]{1,0:T(8,128)(2,1)}, f32[1,4]{1,0:T(1,128)}) custom-call(bf16[384,1152]{1,0:T(8,128)(2,1)S(1)} %bitcast.6, bf16[8,80,384]{2,1,0:T(8,128)(2,1)S(1)} %all_to_all.10.got_ref, bf16[576,1152]{1,0:T(8,128)(2,1)S(1)} %copy-done.3, bf16[16,1152]{1,0:T(8,128)(2,1)S(1)} %pad_maximum_fusion.text_ref), custom_call_target="tpu_custom_call" | custom-call | flops 509607936 | bytes 8388608 | tf_op jit(solution)/shard_map/pallas_call | solution.py:406
  (2 shorter events, 0.0 us)
Async XLA Ops:
  0.6 2.1 %copy-start = (bf16[1152,1728]{0,1:T(8,128)(2,1)S(1)}, bf16[1152,1728]{0,1:T(8,128)(2,1)}, u32[]{:S(2)}) copy-start(bf16[1152,1728]{0,1:T(8,128)(2,1)} %param.7) | copy-start | bytes 11943940
  2.8 1.2 %copy-start.1 = (bf16[1,384,1152]{2,1,0:T(8,128)(2,1)S(1)}, bf16[1,384,1152]{2,1,0:T(8,128)(2,1)}, u32[]{:S(2)}) copy-start(bf16[1,384,1152]{2,1,0:T(8,128)(2,1)} %param.5) | copy-start | bytes 2654212
  3.9 0.7 %copy-start.4 = (s32[1,3072]{1,0:T(1,128)S(1)}, s32[1,3072]{1,0:T(1,128)}, u32[]{:S(2)}) copy-start(s32[1,3072]{1,0:T(1,128)} %ids_ref.3) | copy-start | bytes 36868
  10.7 5.2 %copy-start.6 = (bf16[4,1152]{1,0:T(4,128)(2,1)S(1)}, bf16[4,1152]{1,0:T(4,128)(2,1)}, u32[]{:S(2)}) copy-start(bf16[4,1152]{1,0:T(4,128)(2,1)} %param.9) | copy-start | bytes 27652
  10.7 24.1 %copy-start.5 = (s32[1,3072]{1,0:T(1,128)S(1)}, s32[1,3072]{1,0:T(1,128)}, u32[]{:S(2)}) copy-start(s32[1,3072]{1,0:T(1,128)} %ids_ref.3) | copy-start | bytes 36868
  10.7 24.1 %all-to-all-start = ((bf16[8,224,384]{2,1,0:T(8,128)(2,1)}), bf16[8,224,384]{2,1,0:T(8,128)(2,1)S(1)}, u32[]{:S(2)}, u32[]{:S(2)}) async-start(bf16[8,224,384]{2,1,0:T(8,128)(2,1)} %shard_map.68), calls=%async_computation | async-start | bytes 2752512 | tf_op jit(solution)/shard_map/all_to_all | solution.py:328
  15.9 3.7 %collective-permute-start = (bf16[4,1152]{1,0:T(4,128)(2,1)S(1)}, bf16[4,1152]{1,0:T(4,128)(2,1)S(1)}, u32[]{:S(2)}, u32[]{:S(2)}) collective-permute-start(bf16[4,1152]{1,0:T(4,128)(2,1)S(1)} %copy-done.6), channel_id=1, source_target_pairs={{0,1},{1,0},{2,3},{3,2},{4,5},{5,4},{6,7},{7,6},{8,9},{9,8},{10,11... | collective-permute-start | bytes 27656 | tf_op jit(solution)/shard_map/ppermute | solution.py:310
  19.7 4.7 %collective-permute-start.1 = (bf16[8,1152]{1,0:T(8,128)(2,1)S(1)}, bf16[8,1152]{1,0:T(8,128)(2,1)S(1)}, u32[]{:S(2)}, u32[]{:S(2)}) collective-permute-start(bf16[8,1152]{1,0:T(8,128)(2,1)S(1)} %pad_maximum_fusion.1), channel_id=1, source_target_pairs={{0,2},{1,3},{2,0},{3,1},{4,6},{5,7},{6,4},{7,5},{8,10},{9,11},{10,... | collective-permute-start | bytes 55304 | tf_op jit(solution)/shard_map/ppermute | solution.py:310
  24.4 30.8 %copy-start.2 = (bf16[1,384,1152]{2,1,0:T(8,128)(2,1)S(1)}, bf16[1,384,1152]{2,1,0:T(8,128)(2,1)}, u32[]{:S(2)}) copy-start(bf16[1,384,1152]{2,1,0:T(8,128)(2,1)} %param.5) | copy-start | bytes 2654212
  34.8 20.4 %copy-start.3 = (bf16[576,1152]{1,0:T(8,128)(2,1)S(1)}, bf16[576,1152]{1,0:T(8,128)(2,1)}, u32[]{:S(2)}) copy-start(bf16[576,1152]{1,0:T(8,128)(2,1)} %out_weight_ref.1) | copy-start | bytes 3981316

commit v3 on v2

--- a/solution.py
+++ b/solution.py
@@ -35,8 +35,13 @@
     return (lax.rem(row, images) == ids).astype(jnp.float32).astype(jnp.bfloat16)
 
 
-def project_kernel(images, piggy, ids_ref, rows_ref, weight_ref, out_ref, weight, turned, sems):
+def project_kernel(images, piggy, ids_ref, rows_ref, weight_ref, out_ref, own_ids, rows_held, weight, turned, id_sem, row_sem, sems):
     count, depth = rows_ref.shape
+    rows_fetch = pltpu.make_async_copy(rows_ref, rows_held, row_sem)
+    rows_fetch.start()
+    own = pl.multiple_of(lax.axis_index("grp") * count, LANES)
+    ids_fetch = pltpu.make_async_copy(ids_ref.at[:, pl.ds(own, count)], own_ids, id_sem)
+    ids_fetch.start()
     width = weight.shape[0] // 3
     size = width // HEADS
     pieces = sems.shape[0]
@@ -48,15 +53,15 @@
     ]
     for fetch in fetches:
         fetch.start()
-    rows = rows_ref[...]
+    rows_fetch.wait()
+    rows = rows_held[...]
     values = rows.astype(jnp.float32)
     center = values - jnp.mean(values, axis=1, keepdims=True)
     spread = jnp.mean(center * center, axis=1, keepdims=True)
     normed = (center * lax.rsqrt(spread + 1e-06)).astype(jnp.bfloat16)
+    ids_fetch.wait()
     if piggy:
-        own = lax.axis_index("grp") * count
-        ids = ids_ref[:, pl.ds(pl.multiple_of(own, LANES), count)]
-        sums = jnp.dot(image_rows(ids, images), rows, preferred_element_type=jnp.float32)
+        sums = jnp.dot(image_rows(own_ids[...], images), rows, preferred_element_type=jnp.float32)
         sums = split_in_two(sums, images)
     for fetch, cut in zip(fetches, cuts):
         fetch.wait()
@@ -293,6 +298,10 @@
     return [pl.BlockSpec(memory_space=pltpu.VMEM)] * count
 
 
+def in_hbm(value):
+    return pltpu.with_memory_space_constraint(value, pltpu.HBM)
+
+
 def call(kernel, out_shape, scratch, in_specs, flops):
     out_specs = jax.tree.map(lambda _: pl.BlockSpec(memory_space=pltpu.VMEM), out_shape)
     return pl.pallas_call(
@@ -346,13 +355,17 @@
         functools.partial(project_kernel, images, piggy),
         shape((HEADS, 3 * size + SPARE, count), bf16),
         [
+            pltpu.VMEM((1, count), jnp.int32),
+            pltpu.VMEM((count, depth), bf16),
             pltpu.VMEM((3 * width, depth), bf16),
             pltpu.VMEM((3 * width, count), f32),
+            pltpu.SemaphoreType.DMA,
+            pltpu.SemaphoreType.DMA,
             pltpu.SemaphoreType.DMA((4,)),
         ],
-        in_vmem(2) + [pl.BlockSpec(memory_space=pl.ANY)],
+        [pl.BlockSpec(memory_space=pltpu.HBM)] * 3,
         2 * count * depth * 3 * width,
-    )(segment_ids, rows, qkv_weight.T)
+    )(in_hbm(segment_ids), in_hbm(rows), in_hbm(qkv_weight.T))
     got = exchanged(blocks, groups)
     got, texts = lax.optimization_barrier((got, all_texts(text_embed)))
 

time: 57.5 us -> 54.3 us (0.944)
  local copies, waits for them, and re-layouts: 4.02 us -> 0.02 us
  Pallas kernels: 17 us -> 17.9 us
    unnamed x14 -> x8, local copies, waits for them, and re-layouts: 4.02 us -> 0.02 us
    pallas_call x1, Pallas kernels: 6.06 us -> 7.06 us  [local(): call(functools.partial(project_kernel, images, piggy), shape((HEADS, 3 *...]
where the time goes in v3:
time: 54.3 us; the launch traced here: 54.5 us
  Pallas kernels  17.9 us (33%)
  waiting for transfers between devices  14.6 us (27%)
  blocking collectives  11.8 us (22%)
  starting transfers between devices  9.48 us (17%)
  between operations  0.68 us (1%)
    all_to_all x1, blocking collectives, exchanged(): lax.all_to_all(blocks, 'grp', 0, 0, axis_index_groups=groups, tiled=True)  11.8 us
    all_to_all x1, waiting for transfers between devices, exchanged(): lax.all_to_all(blocks, 'grp', 0, 0, axis_index_groups=groups, tiled=True)  10.4 us
    pallas_call x1, Pallas kernels, local(): call(functools.partial(attend_kernel, images, piggy, halo), shape((HEADS,...  8.49 us
    pallas_call x1, Pallas kernels, local(): call(functools.partial(project_kernel, images, piggy), shape((HEADS, 3 *...  7.06 us
    all_to_all x1, starting transfers between devices, exchanged(): lax.all_to_all(blocks, 'grp', 0, 0, axis_index_groups=groups, tiled=True)  5.18 us
    ppermute x2, starting transfers between devices, moved(): return lax.ppermute(value, axis, pairs)  4.3 us
    ppermute x2, waiting for transfers between devices, moved(): return lax.ppermute(value, axis, pairs)  4.15 us
    pallas_call x1, Pallas kernels, local(): call(functools.partial(finish_kernel, images), (shape((count, depth), bf1...  2.39 us
  transfers between devices with their start and end apart: 3, of which 3 were waited for; matrix products, arithmetic and copies ran while one was open for 0% of the time, Pallas kernels for 0%

profile of v3, /device:TPU:0, one launch (start us, length us, event | category | flops | bytes accessed | tf_op | source)
XLA Modules:
  0.0 54.5 jit_solution(7425447010249174731)
XLA Ops:
  0.6 7.1 %shard_map.68 = bf16[8,224,384]{2,1,0:T(8,128)(2,1)} custom-call(s32[1,3072]{1,0:T(1,128)} %ids_ref.3, bf16[384,1152]{1,0:T(8,128)(2,1)} %bitcast.4, bf16[1728,1152]{1,0:T(8,128)(2,1)} %bitcast.6), custom_call_target="tpu_custom_call" | custom-call | flops 1528823808 | bytes 8388608 | tf_op jit(solution)/shard_map/pallas_call | solution.py:354
  7.7 0.0 copy-start.3
  7.7 0.0 copy-start.2
  7.7 5.2 %all-to-all-start = ((bf16[8,224,384]{2,1,0:T(8,128)(2,1)}), bf16[8,224,384]{2,1,0:T(8,128)(2,1)S(1)}, u32[]{:S(2)}, u32[]{:S(2)}) async-start(bf16[8,224,384]{2,1,0:T(8,128)(2,1)} %shard_map.68), calls=%async_computation | async-start | bytes 2752512 | tf_op jit(solution)/shard_map/all_to_all | solution.py:337
  12.9 0.0 copy-done.3
  12.9 1.6 %collective-permute-start = (bf16[4,1152]{1,0:T(4,128)(2,1)S(1)}, bf16[4,1152]{1,0:T(4,128)(2,1)S(1)}, u32[]{:S(2)}, u32[]{:S(2)}) collective-permute-start(bf16[4,1152]{1,0:T(4,128)(2,1)S(1)} %copy-done.3), channel_id=1, source_target_pairs={{0,1},{1,0},{2,3},{3,2},{4,5},{5,4},{6,7},{7,6},{8,9},{9,8},{10,11... | collective-permute-start | bytes 27656 | tf_op jit(solution)/shard_map/ppermute | solution.py:319
  14.6 2.1 %collective-permute-done = bf16[4,1152]{1,0:T(4,128)(2,1)S(1)} collective-permute-done((bf16[4,1152]{1,0:T(4,128)(2,1)S(1)}, bf16[4,1152]{1,0:T(4,128)(2,1)S(1)}, u32[]{:S(2)}, u32[]{:S(2)}) %collective-permute-start) | collective-permute-done | bytes 9248 | tf_op jit(solution)/shard_map/ppermute | solution.py:319
  16.7 2.7 %collective-permute-start.1 = (bf16[8,1152]{1,0:T(8,128)(2,1)S(1)}, bf16[8,1152]{1,0:T(8,128)(2,1)S(1)}, u32[]{:S(2)}, u32[]{:S(2)}) collective-permute-start(bf16[8,1152]{1,0:T(8,128)(2,1)S(1)} %pad_maximum_fusion.1), channel_id=1, source_target_pairs={{0,2},{1,3},{2,0},{3,1},{4,6},{5,7},{6,4},{7,5},{8,10},{9,11},{10,... | collective-permute-start | bytes 55304 | tf_op jit(solution)/shard_map/ppermute | solution.py:319
  19.3 2.1 %collective-permute-done.1 = bf16[8,1152]{1,0:T(8,128)(2,1)S(1)} collective-permute-done((bf16[8,1152]{1,0:T(8,128)(2,1)S(1)}, bf16[8,1152]{1,0:T(8,128)(2,1)S(1)}, u32[]{:S(2)}, u32[]{:S(2)}) %collective-permute-start.1) | collective-permute-done | bytes 18464 | tf_op jit(solution)/shard_map/ppermute | solution.py:319
  21.4 0.0 copy-start
  21.4 10.4 %all-to-all-done.got_ref = bf16[8,224,384]{2,1,0:T(8,128)(2,1)S(1)} async-done(((bf16[8,224,384]{2,1,0:T(8,128)(2,1)}), bf16[8,224,384]{2,1,0:T(8,128)(2,1)S(1)}, u32[]{:S(2)}, u32[]{:S(2)}) %all-to-all-start) | async-done | bytes 1376288 | tf_op jit(solution)/shard_map/all_to_all | solution.py:337
  31.8 0.0 copy-done.2
  31.8 0.0 copy-start.1
  31.8 8.5 %shard_map.69 = bf16[8,80,384]{2,1,0:T(8,128)(2,1)S(1)} custom-call(s32[1,3072]{1,0:T(1,128)S(1)} %copy-done.2, bf16[8,224,384]{2,1,0:T(8,128)(2,1)S(1)} %all-to-all-done.got_ref), custom_call_target="tpu_custom_call" | custom-call | flops 905969664 | bytes 8388608 | tf_op jit(solution)/shard_map/pallas_call | solution.py:397
  40.3 11.8 %all_to_all.10.got_ref = bf16[8,80,384]{2,1,0:T(8,128)(2,1)S(1)} all-to-all(bf16[8,80,384]{2,1,0:T(8,128)(2,1)S(1)} %shard_map.69), channel_id=1, replica_groups=mesh['grp'=8,'blk'=4] {'grp'}, dimensions={0} | all-to-all | bytes 983040 | tf_op jit(solution)/shard_map/all_to_all | solution.py:337
  52.1 0.0 copy-done
  52.1 0.0 copy-done.1
  52.1 2.4 %shard_map.70 = (bf16[384,1152]{1,0:T(8,128)(2,1)}, f32[1,4]{1,0:T(1,128)}) custom-call(bf16[384,1152]{1,0:T(8,128)(2,1)S(1)} %bitcast.5, bf16[8,80,384]{2,1,0:T(8,128)(2,1)S(1)} %all_to_all.10.got_ref, bf16[576,1152]{1,0:T(8,128)(2,1)S(1)} %copy-done.1, bf16[16,1152]{1,0:T(8,128)(2,1)S(1)} %pad_maximum_fusion.text_ref), custom_call_target="tpu_custom_call" | custom-call | flops 509607936 | bytes 8388608 | tf_op jit(solution)/shard_map/pallas_call | solution.py:419
  (2 shorter events, 0.0 us)
Async XLA Ops:
  7.7 5.2 %copy-start.3 = (bf16[4,1152]{1,0:T(4,128)(2,1)S(1)}, bf16[4,1152]{1,0:T(4,128)(2,1)}, u32[]{:S(2)}) copy-start(bf16[4,1152]{1,0:T(4,128)(2,1)} %param.9) | copy-start | bytes 27652
  7.7 24.1 %copy-start.2 = (s32[1,3072]{1,0:T(1,128)S(1)}, s32[1,3072]{1,0:T(1,128)}, u32[]{:S(2)}) copy-start(s32[1,3072]{1,0:T(1,128)} %ids_ref.3) | copy-start | bytes 36868
  7.7 24.1 %all-to-all-start = ((bf16[8,224,384]{2,1,0:T(8,128)(2,1)}), bf16[8,224,384]{2,1,0:T(8,128)(2,1)S(1)}, u32[]{:S(2)}, u32[]{:S(2)}) async-start(bf16[8,224,384]{2,1,0:T(8,128)(2,1)} %shard_map.68), calls=%async_computation | async-start | bytes 2752512 | tf_op jit(solution)/shard_map/all_to_all | solution.py:337
  12.9 3.7 %collective-permute-start = (bf16[4,1152]{1,0:T(4,128)(2,1)S(1)}, bf16[4,1152]{1,0:T(4,128)(2,1)S(1)}, u32[]{:S(2)}, u32[]{:S(2)}) collective-permute-start(bf16[4,1152]{1,0:T(4,128)(2,1)S(1)} %copy-done.3), channel_id=1, source_target_pairs={{0,1},{1,0},{2,3},{3,2},{4,5},{5,4},{6,7},{7,6},{8,9},{9,8},{10,11... | collective-permute-start | bytes 27656 | tf_op jit(solution)/shard_map/ppermute | solution.py:319
  16.7 4.7 %collective-permute-start.1 = (bf16[8,1152]{1,0:T(8,128)(2,1)S(1)}, bf16[8,1152]{1,0:T(8,128)(2,1)S(1)}, u32[]{:S(2)}, u32[]{:S(2)}) collective-permute-start(bf16[8,1152]{1,0:T(8,128)(2,1)S(1)} %pad_maximum_fusion.1), channel_id=1, source_target_pairs={{0,2},{1,3},{2,0},{3,1},{4,6},{5,7},{6,4},{7,5},{8,10},{9,11},{10,... | collective-permute-start | bytes 55304 | tf_op jit(solution)/shard_map/ppermute | solution.py:319
  21.4 30.7 %copy-start = (bf16[1,384,1152]{2,1,0:T(8,128)(2,1)S(1)}, bf16[1,384,1152]{2,1,0:T(8,128)(2,1)}, u32[]{:S(2)}) copy-start(bf16[1,384,1152]{2,1,0:T(8,128)(2,1)} %param.5) | copy-start | bytes 2654212
  31.8 20.3 %copy-start.1 = (bf16[576,1152]{1,0:T(8,128)(2,1)S(1)}, bf16[576,1152]{1,0:T(8,128)(2,1)}, u32[]{:S(2)}) copy-start(bf16[576,1152]{1,0:T(8,128)(2,1)} %out_weight_ref.1) | copy-start | bytes 3981316

commit v4 on v3

--- a/solution.py
+++ b/solution.py
@@ -35,22 +35,56 @@
     return (lax.rem(row, images) == ids).astype(jnp.float32).astype(jnp.bfloat16)
 
 
-def project_kernel(images, piggy, ids_ref, rows_ref, weight_ref, out_ref, own_ids, rows_held, weight, turned, id_sem, row_sem, sems):
+def head_blocks(query, key, value, sums, pair):
+    size = query.shape[0] // 2
+    count = query.shape[1]
+    for place in range(2):
+        here = slice(place * size, (place + 1) * size)
+        if sums is None:
+            spare = jnp.zeros((SPARE, count), jnp.float32)
+        else:
+            first = pl.multiple_of((2 * pair + place) * LANES, LANES)
+            parts = [sums[:, pl.ds(first, LANES)], sums[:, HEADS * LANES :]]
+            held = sum(part.shape[1] for part in parts)
+            spare = jnp.concatenate(parts + [jnp.zeros((SPARE, count - held), jnp.float32)], axis=1)
+        block = jnp.concatenate([value[here], key[here], spare, query[here]], axis=0)
+        yield block.astype(jnp.bfloat16)
+
+
+def store_by_core(core, blocks, same_ref, cross_ref):
+    first, second = blocks
+
+    @pl.when(core == 0)
+    def _():
+        same_ref[...] = first
+        cross_ref[...] = second
+
+    @pl.when(core == 1)
+    def _():
+        same_ref[...] = second
+        cross_ref[...] = first
+
+
+def place_in_group():
+    own = lax.rem(lax.axis_index("grp"), HEADS)
+    return lax.div(own, 2), lax.rem(own, 2)
+
+
+def far_kernel(images, piggy, ids_ref, rows_ref, weight_ref, normed_ref, sums_ref, same_ref, cross_ref, own_ids, rows_held, weight, id_sem, row_sem, sems):
     count, depth = rows_ref.shape
+    width = weight_ref.shape[0] // 3
+    wide = weight.shape[1]
     rows_fetch = pltpu.make_async_copy(rows_ref, rows_held, row_sem)
     rows_fetch.start()
     own = pl.multiple_of(lax.axis_index("grp") * count, LANES)
     ids_fetch = pltpu.make_async_copy(ids_ref.at[:, pl.ds(own, count)], own_ids, id_sem)
     ids_fetch.start()
-    width = weight.shape[0] // 3
-    size = width // HEADS
-    pieces = sems.shape[0]
-    step = 3 * width // pieces
-    cuts = [slice(piece * step, (piece + 1) * step) for piece in range(pieces)]
-    fetches = [
-        pltpu.make_async_copy(weight_ref.at[cut], weight.at[cut], sems.at[piece])
-        for piece, cut in enumerate(cuts)
-    ]
+    pair, core = place_in_group()
+    pair = jnp.bitwise_xor(pair, 3)
+    fetches = []
+    for at in range(3):
+        first = pl.multiple_of(at * width + pair * wide, 16)
+        fetches.append(pltpu.make_async_copy(weight_ref.at[pl.ds(first, wide)], weight.at[at], sems.at[at]))
     for fetch in fetches:
         fetch.start()
     rows_fetch.wait()
@@ -59,39 +93,41 @@
     center = values - jnp.mean(values, axis=1, keepdims=True)
     spread = jnp.mean(center * center, axis=1, keepdims=True)
     normed = (center * lax.rsqrt(spread + 1e-06)).astype(jnp.bfloat16)
+    normed_ref[...] = normed.T
     ids_fetch.wait()
     if piggy:
         sums = jnp.dot(image_rows(own_ids[...], images), rows, preferred_element_type=jnp.float32)
-        sums = split_in_two(sums, images)
-    for fetch, cut in zip(fetches, cuts):
+        sums_ref[...] = split_in_two(sums, images)
+    for fetch in fetches:
         fetch.wait()
-        turned[cut, :] = lax.dot_general(
-            weight[cut, :], normed, (((1,), (1,)), ((), ())), preferred_element_type=jnp.float32
-        )
-    for head in range(HEADS):
-        query, key, value = (
-            turned[at * width + head * size : at * width + (head + 1) * size, :] for at in range(3)
-        )
-        if piggy:
-            spare = jnp.concatenate(
-                [
-                    sums[:, head * LANES : (head + 1) * LANES],
-                    sums[:, HEADS * LANES :],
-                    jnp.zeros((SPARE, count - depth + (HEADS - 1) * LANES), jnp.float32),
-                ],
-                axis=1,
+    parts = [
+        jnp.dot(weight[at], normed_ref[...], preferred_element_type=jnp.float32) for at in range(3)
+    ]
+    store_by_core(core, head_blocks(*parts, sums_ref if piggy else None, pair), same_ref, cross_ref)
+
+
+def near_kernel(piggy, normed_ref, sums_ref, weight_ref, *out_refs):
+    width = weight_ref.shape[0] // 3
+    wide = 2 * width // HEADS
+    own, core = place_in_group()
+    for step, move in enumerate((1, 2, 0)):
+        pair = jnp.bitwise_xor(own, move)
+        parts = []
+        for at in range(3):
+            here = pl.ds(pl.multiple_of(at * width + pair * wide, 16), wide)
+            parts.append(
+                jnp.dot(weight_ref[here, :], normed_ref[...], preferred_element_type=jnp.float32)
             )
-        else:
-            spare = jnp.zeros((SPARE, count), jnp.float32)
-        block = jnp.concatenate([value, key, spare, query], axis=0)
-        out_ref[head] = block.astype(jnp.bfloat16)
-
-
-def attend_kernel(images, piggy, halo, ids_ref, got_ref, *rest):
+        blocks = head_blocks(*parts, sums_ref if piggy else None, pair)
+        store_by_core(core, blocks, *out_refs[2 * step : 2 * step + 2])
+
+
+def attend_kernel(images, piggy, halo, ids_ref, *rest):
+    got_refs, rest = rest[:HEADS], rest[HEADS:]
     if halo:
         left_ref, right_ref, *rest = rest
-    out_ref, keys, values, queries, attended, scores_a, scores_b, tops_a, tops_b, starts = rest
-    count = got_ref.shape[2]
+    out_ref, keys, values, queries, attended, scores_a, scores_b, tops_a, tops_b, marks, starts = rest
+    count = got_refs[0].shape[1]
     padded = attended.shape[0]
     size = padded - SPARE
     total_rows = HEADS * count
@@ -111,33 +147,35 @@
     outside = jnp.logical_or(ids < 0, ids >= images)
     key_side = jnp.where(odd == 1, bit, 1 - bit).astype(jnp.float32)
     key_side = jnp.where(outside, 1.0, key_side)
-    key_side = jnp.where(used, key_side * HIDDEN, 0.0)
-    query_side = jnp.where(used, jnp.where(odd == 1, 1 - bit, bit), 0).astype(jnp.float32)
-
-    def with_rows(marks, block):
-        return jnp.concatenate([marks, block.astype(jnp.float32)[SPARE:]], axis=0).astype(jnp.bfloat16)
+    key_marks, query_marks = marks.at[0], marks.at[1]
+    key_marks[...] = jnp.where(used, key_side * HIDDEN, 0.0)
+    query_marks[...] = jnp.where(used, jnp.where(odd == 1, 1 - bit, bit), 0).astype(jnp.float32)
 
     key_at = size - SPARE
     query_at = 2 * size
-    blank = jnp.zeros((LANES - padded, count), jnp.float32)
-
-    def turned_keys(here, block):
-        marked = jnp.concatenate([key_side[:, here], block.astype(jnp.float32)[SPARE:]], axis=0)
-        filled = jnp.concatenate([marked, jnp.zeros((LANES - padded, block.shape[1]), jnp.float32)], axis=0)
-        return filled.T.astype(jnp.bfloat16)
-
-    for source in range(HEADS):
-        here = slice(halo + source * count, halo + (source + 1) * count)
-        there = slice(source * count, (source + 1) * count)
-        values[:, here] = got_ref[source, 0:padded]
-        keys[here, :] = turned_keys(here, got_ref[source, key_at : key_at + padded])
-        queries[0:16, there] = with_rows(query_side[:, here], got_ref[source, query_at : query_at + 16])
-        queries[16:padded, there] = got_ref[source, query_at + 16 : query_at + padded]
-        queries[padded:, there] = blank.astype(jnp.bfloat16)
+    own = lax.rem(lax.axis_index("grp"), HEADS)
+    blank = jnp.zeros((LANES - padded, count), jnp.bfloat16)
+
+    def store_keys(here, ref):
+        block = ref[key_at : key_at + padded].astype(jnp.float32)
+        nothing = jnp.zeros((LANES - padded, block.shape[1]), jnp.float32)
+        full = jnp.concatenate([key_marks[:, here], block[SPARE:], nothing], axis=0)
+        keys[here, :] = full.T.astype(jnp.bfloat16)
+        values[:, here] = ref[0:padded]
+
+    for step, ref in enumerate(got_refs):
+        first = jnp.bitwise_xor(own, step) * count
+        here = pl.ds(pl.multiple_of(halo + first, LANES), count)
+        there = pl.ds(pl.multiple_of(first, LANES), count)
+        store_keys(here, ref)
+        edge = ref[query_at : query_at + 16].astype(jnp.float32)
+        edge = jnp.concatenate([query_marks[:, here], edge[SPARE:]], axis=0)
+        queries[0:16, there] = edge.astype(jnp.bfloat16)
+        queries[16:padded, there] = ref[query_at + 16 : query_at + padded]
+        queries[padded:, there] = blank
     if halo:
-        for ref, here in ((left_ref, slice(0, halo)), (right_ref, slice(length - halo, length))):
-            values[:, here] = ref[0:padded]
-            keys[here, :] = turned_keys(here, ref[key_at : key_at + padded])
+        store_keys(slice(0, halo), left_ref)
+        store_keys(slice(length - halo, length), right_ref)
 
     def image_at(position):
         found = jnp.int32(0)
@@ -210,8 +248,8 @@
         )
         pooled = split_in_two(pooled, images)
         sums = jnp.zeros((SPARE, 2 * LANES), jnp.float32)
-        for source in range(HEADS):
-            sums += got_ref[source, query_at : query_at + 16].astype(jnp.float32)[0:SPARE, 0 : 2 * LANES]
+        for ref in got_refs:
+            sums += ref[query_at : query_at + 16].astype(jnp.float32)[0:SPARE, 0 : 2 * LANES]
         sums = split_in_two(sums + pltpu.roll(sums, images, axis=0), images)
         spare = jnp.concatenate(
             [pooled, jnp.zeros((SPARE, LANES - padded), jnp.float32), sums], axis=1
@@ -351,27 +389,39 @@
     bf16, f32 = jnp.bfloat16, jnp.float32
     shape = jax.ShapeDtypeStruct
 
-    blocks = call(
-        functools.partial(project_kernel, images, piggy),
-        shape((HEADS, 3 * size + SPARE, count), bf16),
+    block = shape((3 * size + SPARE, count), bf16)
+    hbm = pl.BlockSpec(memory_space=pltpu.HBM)
+    turned_weight = qkv_weight.T
+    normed, sums, *sent = call(
+        functools.partial(far_kernel, images, piggy),
+        (shape((depth, count), bf16), shape((SPARE, depth), f32), block, block),
         [
             pltpu.VMEM((1, count), jnp.int32),
             pltpu.VMEM((count, depth), bf16),
-            pltpu.VMEM((3 * width, depth), bf16),
-            pltpu.VMEM((3 * width, count), f32),
+            pltpu.VMEM((3, 2 * size, depth), bf16),
             pltpu.SemaphoreType.DMA,
             pltpu.SemaphoreType.DMA,
-            pltpu.SemaphoreType.DMA((4,)),
+            pltpu.SemaphoreType.DMA((3,)),
         ],
-        [pl.BlockSpec(memory_space=pltpu.HBM)] * 3,
-        2 * count * depth * 3 * width,
-    )(in_hbm(segment_ids), in_hbm(rows), in_hbm(qkv_weight.T))
-    got = exchanged(blocks, groups)
+        [hbm] * 3,
+        2 * count * depth * 6 * size,
+    )(in_hbm(segment_ids), in_hbm(rows), in_hbm(turned_weight))
+    sent += call(
+        functools.partial(near_kernel, piggy),
+        (block,) * 6,
+        [],
+        in_vmem(3),
+        2 * count * depth * 18 * size,
+    )(normed, sums, turned_weight)
+    got = [None] * HEADS
+    for value, by in zip(sent, (6, 7, 2, 3, 4, 5, 0, 1)):
+        pairs = [(i, i ^ by) for i in range(group_size)]
+        got[by] = moved(value, "grp", pairs) if by else value
     got, texts = lax.optimization_barrier((got, all_texts(text_embed)))
 
     length = HEADS * count
     halo = 0
-    operands = [segment_ids, got]
+    operands = [segment_ids, *got]
     if parts > 1:
         halo = rounded_up(MAXP - 1, LANES)
         part = lax.axis_index("grp") // HEADS
@@ -384,13 +434,14 @@
             axis=1,
         )
         near_ids = lax.dynamic_slice_in_dim(whole_ids, part * length, length + 2 * halo, axis=1)
-        flat = got[:, : 2 * size].transpose(1, 0, 2).reshape(2 * size, length)
+        order = jnp.bitwise_xor(lax.axis_index("grp") % HEADS, jnp.arange(HEADS))
+        flat = jnp.stack(got)[order][:, : 2 * size].transpose(1, 0, 2).reshape(2 * size, length)
         flat = jnp.concatenate([flat, jnp.zeros((16, length), bf16)], axis=0)
         ahead = [(i, i + HEADS) for i in range(group_size - HEADS)]
         back = [(i + HEADS, i) for i in range(group_size - HEADS)]
         left = moved(flat[:, length - halo :], "grp", ahead)
         right = moved(flat[:, :halo], "grp", back)
-        operands = [near_ids, got, left, right]
+        operands = [near_ids, *got, left, right]
     reach = length + 2 * halo
     window = min(rounded_up(MAXP + LANES - 1, LANES), reach)
     tile = 2 * LANES
@@ -406,6 +457,7 @@
             pltpu.VMEM((window, tile), f32),
             pltpu.VMEM((1, tile), f32),
             pltpu.VMEM((1, tile), f32),
+            pltpu.VMEM((2, SPARE, reach), f32),
             pltpu.SMEM((images,), jnp.int32),
         ],
         in_vmem(len(operands)),

time: 54.3 us -> 54.2 us (level)
  starting transfers between devices: 9.48 us -> 12.8 us
  Pallas kernels: 17.9 us -> 15.3 us
  waiting for transfers between devices: 14.6 us -> 12.2 us
  blocking collectives: 11.8 us -> 12.9 us
    all_to_all x1 -> x0, waiting for transfers between devices: 10.4 us -> none  [exchanged(): lax.all_to_all(blocks, 'grp', 0, 0, axis_index_groups=groups, tiled=True)]
    ppermute x2 -> x9, starting transfers between devices: 4.3 us -> 12.8 us  [moved(): return lax.ppermute(value, axis, pairs)]
    ppermute x2 -> x9, waiting for transfers between devices: 4.15 us -> 12.2 us  [moved(): return lax.ppermute(value, axis, pairs)]
    all_to_all x1 -> x0, starting transfers between devices: 5.18 us -> none  [exchanged(): lax.all_to_all(blocks, 'grp', 0, 0, axis_index_groups=groups, tiled=True)]
    pallas_call x1 -> x2, Pallas kernels: 7.06 us -> 5.33 us  [the longest x1 2.99 us: local(): call(functools.partial(far_kernel, images, piggy), (shape((depth, count),...]
    all_to_all x1, blocking collectives: 11.8 us -> 12.9 us  [exchanged(): lax.all_to_all(blocks, 'grp', 0, 0, axis_index_groups=groups, tiled=True)]
    pallas_call x1, Pallas kernels: 8.49 us -> 7.61 us  [local(): call(functools.partial(attend_kernel, images, piggy, halo), shape((HEADS,...]
  transfers between devices with their start and end apart: 3 -> 9, of which waited for: 3 -> 4; matrix products, arithmetic and copies ran while one was open for 0% -> 0% of each run, Pallas kernels for 0% -> 10%
where the time goes in v4:
time: 54.2 us; the launch traced here: 54 us
  Pallas kernels  15.3 us (28%)
  blocking collectives  12.9 us (24%)
  starting transfers between devices  12.8 us (24%)
  waiting for transfers between devices  12.2 us (23%)
  between operations  0.72 us (1%)
    all_to_all x1, blocking collectives, exchanged(): lax.all_to_all(blocks, 'grp', 0, 0, axis_index_groups=groups, tiled=True)  12.9 us
    ppermute x9, starting transfers between devices, moved(): return lax.ppermute(value, axis, pairs)  12.8 us
    ppermute x9, waiting for transfers between devices, moved(): return lax.ppermute(value, axis, pairs)  12.2 us
    pallas_call x1, Pallas kernels, local(): call(functools.partial(attend_kernel, images, piggy, halo), shape((HEADS,...  7.61 us
    pallas_call x1, Pallas kernels, local(): call(functools.partial(far_kernel, images, piggy), (shape((depth, count),...  2.99 us
    pallas_call x1, Pallas kernels, local(): call(functools.partial(finish_kernel, images), (shape((count, depth), bf1...  2.4 us
    pallas_call x1, Pallas kernels, local(): call(functools.partial(near_kernel, piggy), (block,) * 6, [], in_vmem(3),...  2.34 us
  transfers between devices with their start and end apart: 9, of which 4 were waited for; matrix products, arithmetic and copies ran while one was open for 0% of the time, Pallas kernels for 10%

profile of v4, /device:TPU:0, one launch (start us, length us, event | category | flops | bytes accessed | tf_op | source)
XLA Modules:
  0.0 54.0 jit_solution(5783404612366532140)
XLA Ops:
  0.6 0.0 copy-start
  0.6 3.1 %collective-permute-start.7 = (bf16[4,1152]{1,0:T(4,128)(2,1)}, bf16[4,1152]{1,0:T(4,128)(2,1)S(1)}, u32[]{:S(2)}, u32[]{:S(2)}) collective-permute-start(bf16[4,1152]{1,0:T(4,128)(2,1)} %param.9), channel_id=1, source_target_pairs={{0,1},{1,0},{2,3},{3,2},{4,5},{5,4},{6,7},{7,6},{8,9},{9,8},{10,11... | collective-permute-start | bytes 27656 | tf_op jit(solution)/shard_map/ppermute | solution.py:357
  3.7 0.0 copy-start.4
  3.7 0.0 copy-start.3
  3.7 3.0 %shard_map.68 = (bf16[1152,384]{1,0:T(8,128)(2,1)S(1)}, f32[8,1152]{1,0:T(8,128)S(1)}, bf16[224,384]{1,0:T(8,128)(2,1)S(1)}, bf16[224,384]{1,0:T(8,128)(2,1)S(1)}) custom-call(s32[1,3072]{1,0:T(1,128)} %ids_ref.3, bf16[384,1152]{1,0:T(8,128)(2,1)} %bitcast.6, bf16[1728,1152]{1,0:T(8,128)(2,1)} %bitcast.4), custom_call_target="tpu_custom_call" | custom-call | flops 382205952 | bytes 8388608 | tf_op jit(solution)/shard_map/pallas_call | solution.py:395
  6.7 0.0 copy-done
  6.7 0.0 copy-start.1
  6.8 0.0 copy-start.2
  6.8 2.3 %shard_map.69 = (bf16[224,384]{1,0:T(8,128)(2,1)S(1)}, bf16[224,384]{1,0:T(8,128)(2,1)S(1)}, bf16[224,384]{1,0:T(8,128)(2,1)S(1)}, bf16[224,384]{1,0:T(8,128)(2,...) custom-call(bf16[1152,384]{1,0:T(8,128)(2,1)S(1)} %get-tuple-element.23.normed_ref, ...), custom_call_target="tpu_custom_call" | custom-call | flops 1146617856 | bytes 8388608 | tf_op jit(solution)/shard_map/pallas_call | solution.py:409
  9.1 0.1 collective-permute-start
  9.2 1.6 %collective-permute-start.1 = (bf16[224,384]{1,0:T(8,128)(2,1)S(1)}, bf16[224,384]{1,0:T(8,128)(2,1)S(1)}, u32[]{:S(2)}, u32[]{:S(2)}) collective-permute-start(bf16[224,384]{1,0:T(8,128)(2,1)S(1)} %get-tuple-element.27), channel_id=1, source_target_pairs={{0,8},{4,12},{8,0},{12,4},{16,24},{20,28},{24,16},{28,20},{1,9},{5... | collective-permute-start | bytes 516104 | tf_op jit(solution)/shard_map/ppermute | solution.py:357
  10.7 0.0 collective-permute-done.7
  10.8 0.0 copy-done.4
  10.8 2.7 %collective-permute-start.8 = (bf16[8,1152]{1,0:T(8,128)(2,1)S(1)}, bf16[8,1152]{1,0:T(8,128)(2,1)S(1)}, u32[]{:S(2)}, u32[]{:S(2)}) collective-permute-start(bf16[8,1152]{1,0:T(8,128)(2,1)S(1)} %pad_maximum_fusion.1), channel_id=1, source_target_pairs={{0,2},{1,3},{2,0},{3,1},{4,6},{5,7},{6,4},{7,5},{8,10},{9,11},{10,... | collective-permute-start | bytes 55304 | tf_op jit(solution)/shard_map/ppermute | solution.py:357
  13.4 0.0 collective-permute-start.2
  13.5 1.5 %collective-permute-start.3 = (bf16[224,384]{1,0:T(8,128)(2,1)S(1)}, bf16[224,384]{1,0:T(8,128)(2,1)S(1)}, u32[]{:S(2)}, u32[]{:S(2)}) collective-permute-start(bf16[224,384]{1,0:T(8,128)(2,1)S(1)} %get-tuple-element.29), channel_id=1, source_target_pairs={{0,16},{4,20},{8,24},{12,28},{16,0},{20,4},{24,8},{28,12},{1,17},{... | collective-permute-start | bytes 516104 | tf_op jit(solution)/shard_map/ppermute | solution.py:357
  15.0 0.5 collective-permute-done.8
  15.5 0.1 collective-permute-start.4
  15.6 0.0 collective-permute-done.rest_1_
  15.6 2.2 %collective-permute-start.5 = (bf16[224,384]{1,0:T(8,128)(2,1)S(1)}, bf16[224,384]{1,0:T(8,128)(2,1)S(1)}, u32[]{:S(2)}, u32[]{:S(2)}) collective-permute-start(bf16[224,384]{1,0:T(8,128)(2,1)S(1)} %get-tuple-element.31), channel_id=1, source_target_pairs={{0,24},{4,28},{8,16},{12,20},{16,8},{20,12},{24,0},{28,4},{1,25},{... | collective-permute-start | bytes 516104 | tf_op jit(solution)/shard_map/ppermute | solution.py:357
  17.9 0.0 collective-permute-done.1.rest_2_
  17.9 1.5 %collective-permute-start.6 = (bf16[224,384]{1,0:T(8,128)(2,1)S(1)}, bf16[224,384]{1,0:T(8,128)(2,1)S(1)}, u32[]{:S(2)}, u32[]{:S(2)}) collective-permute-start(bf16[224,384]{1,0:T(8,128)(2,1)S(1)} %get-tuple-element.32), channel_id=1, source_target_pairs={{0,28},{4,24},{8,20},{12,16},{16,12},{20,8},{24,4},{28,0},{1,29},{... | collective-permute-start | bytes 516104 | tf_op jit(solution)/shard_map/ppermute | solution.py:357
  19.4 0.6 %collective-permute-done.2.rest_3_ = bf16[224,384]{1,0:T(8,128)(2,1)S(1)} collective-permute-done((bf16[224,384]{1,0:T(8,128)(2,1)S(1)}, bf16[224,384]{1,0:T(8,128)(2,1)S(1)}, u32[]{:S(2)}, u32[]{:S(2)}) %collective-permute-start.2) | collective-permute-done | bytes 172064 | tf_op jit(solution)/shard_map/ppermute | solution.py:357
  20.0 6.9 %collective-permute-done.3.rest_4_ = bf16[224,384]{1,0:T(8,128)(2,1)S(1)} collective-permute-done((bf16[224,384]{1,0:T(8,128)(2,1)S(1)}, bf16[224,384]{1,0:T(8,128)(2,1)S(1)}, u32[]{:S(2)}, u32[]{:S(2)}) %collective-permute-start.3) | collective-permute-done | bytes 172064 | tf_op jit(solution)/shard_map/ppermute | solution.py:357
  27.0 4.1 %collective-permute-done.4.rest_5_ = bf16[224,384]{1,0:T(8,128)(2,1)S(1)} collective-permute-done((bf16[224,384]{1,0:T(8,128)(2,1)S(1)}, bf16[224,384]{1,0:T(8,128)(2,1)S(1)}, u32[]{:S(2)}, u32[]{:S(2)}) %collective-permute-start.4) | collective-permute-done | bytes 172064 | tf_op jit(solution)/shard_map/ppermute | solution.py:357
  31.1 0.0 collective-permute-done.5.rest_6_
  31.1 0.0 collective-permute-done.6.rest_7_
  31.1 0.0 copy-done.3
  31.1 7.6 %shard_map.70 = bf16[8,80,384]{2,1,0:T(8,128)(2,1)S(1)} custom-call(s32[1,3072]{1,0:T(1,128)S(1)} %copy-done.3, bf16[224,384]{1,0:T(8,128)(2,1)S(1)} %get-tuple-element.33.rest_0_, bf16[224,384]{1,0:T(8,128)(2,1)S(1)} %collective-permute-done.rest_1_, bf16[224,384]{1,0:T(8,128)(2,1)S(1)} %collective-permute-done.1.rest_2_, ...), custom_call_target="tpu_custom_call" | custom-call | flops 905969664 | bytes 8388608 | tf_op jit(solution)/shard_map/pallas_call | solution.py:448
  38.7 12.9 %all_to_all.5.got_ref = bf16[8,80,384]{2,1,0:T(8,128)(2,1)S(1)} all-to-all(bf16[8,80,384]{2,1,0:T(8,128)(2,1)S(1)} %shard_map.70), channel_id=1, replica_groups=mesh['grp'=8,'blk'=4] {'grp'}, dimensions={0} | all-to-all | bytes 983040 | tf_op jit(solution)/shard_map/all_to_all | solution.py:375
  51.6 0.0 copy-done.1
  51.6 0.0 copy-done.2
  51.6 2.4 %shard_map.71 = (bf16[384,1152]{1,0:T(8,128)(2,1)}, f32[1,4]{1,0:T(1,128)}) custom-call(bf16[384,1152]{1,0:T(8,128)(2,1)S(1)} %bitcast.7, bf16[8,80,384]{2,1,0:T(8,128)(2,1)S(1)} %all_to_all.5.got_ref, bf16[576,1152]{1,0:T(8,128)(2,1)S(1)} %copy-done.2, bf16[16,1152]{1,0:T(8,128)(2,1)S(1)} %pad_maximum_fusion.text_ref), custom_call_target="tpu_custom_call" | custom-call | flops 509607936 | bytes 8388608 | tf_op jit(solution)/shard_map/pallas_call | solution.py:471
  (2 shorter events, 0.0 us)
Async XLA Ops:
  0.6 6.1 %copy-start = (bf16[1152,1728]{0,1:T(8,128)(2,1)S(1)}, bf16[1152,1728]{0,1:T(8,128)(2,1)}, u32[]{:S(2)}) copy-start(bf16[1152,1728]{0,1:T(8,128)(2,1)} %param.7) | copy-start | bytes 11943940
  0.6 10.1 %collective-permute-start.7 = (bf16[4,1152]{1,0:T(4,128)(2,1)}, bf16[4,1152]{1,0:T(4,128)(2,1)S(1)}, u32[]{:S(2)}, u32[]{:S(2)}) collective-permute-start(bf16[4,1152]{1,0:T(4,128)(2,1)} %param.9), channel_id=1, source_target_pairs={{0,1},{1,0},{2,3},{3,2},{4,5},{5,4},{6,7},{7,6},{8,9},{9,8},{10,11... | collective-permute-start | bytes 27656 | tf_op jit(solution)/shard_map/ppermute | solution.py:357
  3.7 7.0 %copy-start.4 = (bf16[4,1152]{1,0:T(4,128)(2,1)S(1)}, bf16[4,1152]{1,0:T(4,128)(2,1)}, u32[]{:S(2)}) copy-start(bf16[4,1152]{1,0:T(4,128)(2,1)} %param.9) | copy-start | bytes 27652
  3.7 27.4 %copy-start.3 = (s32[1,3072]{1,0:T(1,128)S(1)}, s32[1,3072]{1,0:T(1,128)}, u32[]{:S(2)}) copy-start(s32[1,3072]{1,0:T(1,128)} %ids_ref.3) | copy-start | bytes 36868
  6.7 44.9 %copy-start.1 = (bf16[1,384,1152]{2,1,0:T(8,128)(2,1)S(1)}, bf16[1,384,1152]{2,1,0:T(8,128)(2,1)}, u32[]{:S(2)}) copy-start(bf16[1,384,1152]{2,1,0:T(8,128)(2,1)} %param.5) | copy-start | bytes 2654212
  6.8 44.9 %copy-start.2 = (bf16[576,1152]{1,0:T(8,128)(2,1)S(1)}, bf16[576,1152]{1,0:T(8,128)(2,1)}, u32[]{:S(2)}) copy-start(bf16[576,1152]{1,0:T(8,128)(2,1)} %out_weight_ref.1) | copy-start | bytes 3981316
  9.1 6.5 %collective-permute-start = (bf16[224,384]{1,0:T(8,128)(2,1)S(1)}, bf16[224,384]{1,0:T(8,128)(2,1)S(1)}, u32[]{:S(2)}, u32[]{:S(2)}) collective-permute-start(bf16[224,384]{1,0:T(8,128)(2,1)S(1)} %get-tuple-element.26), channel_id=1, source_target_pairs={{0,4},{4,0},{8,12},{12,8},{16,20},{20,16},{24,28},{28,24},{1,5},{5... | collective-permute-start | bytes 516104 | tf_op jit(solution)/shard_map/ppermute | solution.py:357
  9.2 8.7 %collective-permute-start.1 = (bf16[224,384]{1,0:T(8,128)(2,1)S(1)}, bf16[224,384]{1,0:T(8,128)(2,1)S(1)}, u32[]{:S(2)}, u32[]{:S(2)}) collective-permute-start(bf16[224,384]{1,0:T(8,128)(2,1)S(1)} %get-tuple-element.27), channel_id=1, source_target_pairs={{0,8},{4,12},{8,0},{12,4},{16,24},{20,28},{24,16},{28,20},{1,9},{5... | collective-permute-start | bytes 516104 | tf_op jit(solution)/shard_map/ppermute | solution.py:357
  10.8 4.7 %collective-permute-start.8 = (bf16[8,1152]{1,0:T(8,128)(2,1)S(1)}, bf16[8,1152]{1,0:T(8,128)(2,1)S(1)}, u32[]{:S(2)}, u32[]{:S(2)}) collective-permute-start(bf16[8,1152]{1,0:T(8,128)(2,1)S(1)} %pad_maximum_fusion.1), channel_id=1, source_target_pairs={{0,2},{1,3},{2,0},{3,1},{4,6},{5,7},{6,4},{7,5},{8,10},{9,11},{10,... | collective-permute-start | bytes 55304 | tf_op jit(solution)/shard_map/ppermute | solution.py:357
  13.4 6.6 %collective-permute-start.2 = (bf16[224,384]{1,0:T(8,128)(2,1)S(1)}, bf16[224,384]{1,0:T(8,128)(2,1)S(1)}, u32[]{:S(2)}, u32[]{:S(2)}) collective-permute-start(bf16[224,384]{1,0:T(8,128)(2,1)S(1)} %get-tuple-element.28), channel_id=1, source_target_pairs={{0,12},{4,8},{8,4},{12,0},{16,28},{20,24},{24,20},{28,16},{1,13},{... | collective-permute-start | bytes 516104 | tf_op jit(solution)/shard_map/ppermute | solution.py:357
  13.5 13.5 %collective-permute-start.3 = (bf16[224,384]{1,0:T(8,128)(2,1)S(1)}, bf16[224,384]{1,0:T(8,128)(2,1)S(1)}, u32[]{:S(2)}, u32[]{:S(2)}) collective-permute-start(bf16[224,384]{1,0:T(8,128)(2,1)S(1)} %get-tuple-element.29), channel_id=1, source_target_pairs={{0,16},{4,20},{8,24},{12,28},{16,0},{20,4},{24,8},{28,12},{1,17},{... | collective-permute-start | bytes 516104 | tf_op jit(solution)/shard_map/ppermute | solution.py:357
  15.5 15.6 %collective-permute-start.4 = (bf16[224,384]{1,0:T(8,128)(2,1)S(1)}, bf16[224,384]{1,0:T(8,128)(2,1)S(1)}, u32[]{:S(2)}, u32[]{:S(2)}) collective-permute-start(bf16[224,384]{1,0:T(8,128)(2,1)S(1)} %get-tuple-element.30), channel_id=1, source_target_pairs={{0,20},{4,16},{8,28},{12,24},{16,4},{20,0},{24,12},{28,8},{1,21},{... | collective-permute-start | bytes 516104 | tf_op jit(solution)/shard_map/ppermute | solution.py:357
  15.6 15.4 %collective-permute-start.5 = (bf16[224,384]{1,0:T(8,128)(2,1)S(1)}, bf16[224,384]{1,0:T(8,128)(2,1)S(1)}, u32[]{:S(2)}, u32[]{:S(2)}) collective-permute-start(bf16[224,384]{1,0:T(8,128)(2,1)S(1)} %get-tuple-element.31), channel_id=1, source_target_pairs={{0,24},{4,28},{8,16},{12,20},{16,8},{20,12},{24,0},{28,4},{1,25},{... | collective-permute-start | bytes 516104 | tf_op jit(solution)/shard_map/ppermute | solution.py:357
  17.9 13.2 %collective-permute-start.6 = (bf16[224,384]{1,0:T(8,128)(2,1)S(1)}, bf16[224,384]{1,0:T(8,128)(2,1)S(1)}, u32[]{:S(2)}, u32[]{:S(2)}) collective-permute-start(bf16[224,384]{1,0:T(8,128)(2,1)S(1)} %get-tuple-element.32), channel_id=1, source_target_pairs={{0,28},{4,24},{8,20},{12,16},{16,12},{20,8},{24,4},{28,0},{1,29},{... | collective-permute-start | bytes 516104 | tf_op jit(solution)/shard_map/ppermute | solution.py:357

commit v5 on v4

--- a/solution.py
+++ b/solution.py
@@ -13,6 +13,7 @@
 LANES = 128
 SPARE = 8
 HIDDEN = -1e30
+ORDER = (6, 7, 2, 4, 3, 5, 1, 0)
 
 logit_scale = 30.0
 logit_bias = -5.0
@@ -163,8 +164,8 @@
         keys[here, :] = full.T.astype(jnp.bfloat16)
         values[:, here] = ref[0:padded]
 
-    for step, ref in enumerate(got_refs):
-        first = jnp.bitwise_xor(own, step) * count
+    for by, ref in zip(ORDER, got_refs):
+        first = jnp.bitwise_xor(own, by) * count
         here = pl.ds(pl.multiple_of(halo + first, LANES), count)
         there = pl.ds(pl.multiple_of(first, LANES), count)
         store_keys(here, ref)
@@ -413,10 +414,12 @@
         in_vmem(3),
         2 * count * depth * 18 * size,
     )(normed, sums, turned_weight)
-    got = [None] * HEADS
-    for value, by in zip(sent, (6, 7, 2, 3, 4, 5, 0, 1)):
+    sent = dict(zip((6, 7, 2, 3, 4, 5, 0, 1), sent))
+    got = []
+    for by in ORDER:
         pairs = [(i, i ^ by) for i in range(group_size)]
-        got[by] = moved(value, "grp", pairs) if by else value
+        got.append(moved(sent[by], "grp", pairs) if by else sent[by])
+    text_embed, got[0] = lax.optimization_barrier((text_embed, got[0]))
     got, texts = lax.optimization_barrier((got, all_texts(text_embed)))
 
     length = HEADS * count
@@ -435,7 +438,7 @@
         )
         near_ids = lax.dynamic_slice_in_dim(whole_ids, part * length, length + 2 * halo, axis=1)
         order = jnp.bitwise_xor(lax.axis_index("grp") % HEADS, jnp.arange(HEADS))
-        flat = jnp.stack(got)[order][:, : 2 * size].transpose(1, 0, 2).reshape(2 * size, length)
+        flat = jnp.stack([got[ORDER.index(by)] for by in range(HEADS)])[order][:, : 2 * size].transpose(1, 0, 2).reshape(2 * size, length)
         flat = jnp.concatenate([flat, jnp.zeros((16, length), bf16)], axis=0)
         ahead = [(i, i + HEADS) for i in range(group_size - HEADS)]
         back = [(i + HEADS, i) for i in range(group_size - HEADS)]

time: 54.2 us -> 53.8 us (level)
  blocking collectives: 12.9 us -> 12.2 us
  waiting for transfers between devices: 12.2 us -> 11.5 us
    ppermute x9, waiting for transfers between devices: 12.2 us -> 11.5 us  [moved(): return lax.ppermute(value, axis, pairs)]
    all_to_all x1, blocking collectives: 12.9 us -> 12.2 us  [exchanged(): lax.all_to_all(blocks, 'grp', 0, 0, axis_index_groups=groups, tiled=True)]
  transfers between devices with their start and end apart: 9 -> 9, of which waited for: 4 -> 5; matrix products, arithmetic and copies ran while one was open for 0% -> 0% of each run, Pallas kernels for 10% -> 4%
where the time goes in v5:
time: 53.8 us; the launch traced here: 53.1 us
  Pallas kernels  15.5 us (29%)
  starting transfers between devices  13.1 us (24%)
  blocking collectives  12.2 us (23%)
  waiting for transfers between devices  11.5 us (21%)
  between operations  0.7 us (1%)
    ppermute x9, starting transfers between devices, moved(): return lax.ppermute(value, axis, pairs)  13.1 us
    all_to_all x1, blocking collectives, exchanged(): lax.all_to_all(blocks, 'grp', 0, 0, axis_index_groups=groups, tiled=True)  12.2 us
    ppermute x9, waiting for transfers between devices, moved(): return lax.ppermute(value, axis, pairs)  11.5 us
    pallas_call x1, Pallas kernels, local(): call(functools.partial(attend_kernel, images, piggy, halo), shape((HEADS,...  7.64 us
    pallas_call x1, Pallas kernels, local(): call(functools.partial(far_kernel, images, piggy), (shape((depth, count),...  3.12 us
    pallas_call x1, Pallas kernels, local(): call(functools.partial(finish_kernel, images), (shape((count, depth), bf1...  2.4 us
    pallas_call x1, Pallas kernels, local(): call(functools.partial(near_kernel, piggy), (block,) * 6, [], in_vmem(3),...  2.34 us
  transfers between devices with their start and end apart: 9, of which 5 were waited for; matrix products, arithmetic and copies ran while one was open for 0% of the time, Pallas kernels for 4%

profile of v5, /device:TPU:0, one launch (start us, length us, event | category | flops | bytes accessed | tf_op | source)
XLA Modules:
  0.0 53.1 jit_solution(12124290841813243023)
XLA Ops:
  0.6 0.0 copy-start
  0.6 0.0 copy-start.4
  0.7 0.0 copy-start.3
  0.7 3.1 %shard_map.68 = (bf16[1152,384]{1,0:T(8,128)(2,1)S(1)}, f32[8,1152]{1,0:T(8,128)S(1)}, bf16[224,384]{1,0:T(8,128)(2,1)S(1)}, bf16[224,384]{1,0:T(8,128)(2,1)S(1)}) custom-call(s32[1,3072]{1,0:T(1,128)} %ids_ref.3, bf16[384,1152]{1,0:T(8,128)(2,1)} %bitcast.6, bf16[1728,1152]{1,0:T(8,128)(2,1)} %bitcast.4), custom_call_target="tpu_custom_call" | custom-call | flops 382205952 | bytes 8388608 | tf_op jit(solution)/shard_map/pallas_call | solution.py:396
  3.8 4.0 %collective-permute-start = (bf16[224,384]{1,0:T(8,128)(2,1)S(1)}, bf16[224,384]{1,0:T(8,128)(2,1)S(1)}, u32[]{:S(2)}, u32[]{:S(2)}) collective-permute-start(bf16[224,384]{1,0:T(8,128)(2,1)S(1)} %get-tuple-element.25), channel_id=1, source_target_pairs={{0,24},{4,28},{8,16},{12,20},{16,8},{20,12},{24,0},{28,4},{1,25},{... | collective-permute-start | bytes 516104 | tf_op jit(solution)/shard_map/ppermute | solution.py:358
  7.7 4.4 %collective-permute-done.rest_0_ = bf16[224,384]{1,0:T(8,128)(2,1)S(1)} collective-permute-done((bf16[224,384]{1,0:T(8,128)(2,1)S(1)}, bf16[224,384]{1,0:T(8,128)(2,1)S(1)}, u32[]{:S(2)}, u32[]{:S(2)}) %collective-permute-start) | collective-permute-done | bytes 172064 | tf_op jit(solution)/shard_map/ppermute | solution.py:358
  12.1 0.0 copy-done.4
  12.1 1.8 %collective-permute-start.7 = (bf16[4,1152]{1,0:T(4,128)(2,1)S(1)}, bf16[4,1152]{1,0:T(4,128)(2,1)S(1)}, u32[]{:S(2)}, u32[]{:S(2)}) collective-permute-start(bf16[4,1152]{1,0:T(4,128)(2,1)S(1)} %copy-done.4), channel_id=1, source_target_pairs={{0,1},{1,0},{2,3},{3,2},{4,5},{5,4},{6,7},{7,6},{8,9},{9,8},{10,11... | collective-permute-start | bytes 27656 | tf_op jit(solution)/shard_map/ppermute | solution.py:358
  13.9 0.7 %collective-permute-start.1 = (bf16[224,384]{1,0:T(8,128)(2,1)S(1)}, bf16[224,384]{1,0:T(8,128)(2,1)S(1)}, u32[]{:S(2)}, u32[]{:S(2)}) collective-permute-start(bf16[224,384]{1,0:T(8,128)(2,1)S(1)} %get-tuple-element.27), channel_id=1, source_target_pairs={{0,28},{4,24},{8,20},{12,16},{16,12},{20,8},{24,4},{28,0},{1,29},{... | collective-permute-start | bytes 516104 | tf_op jit(solution)/shard_map/ppermute | solution.py:358
  14.6 1.2 %collective-permute-done.7 = bf16[4,1152]{1,0:T(4,128)(2,1)S(1)} collective-permute-done((bf16[4,1152]{1,0:T(4,128)(2,1)S(1)}, bf16[4,1152]{1,0:T(4,128)(2,1)S(1)}, u32[]{:S(2)}, u32[]{:S(2)}) %collective-permute-start.7) | collective-permute-done | bytes 9248 | tf_op jit(solution)/shard_map/ppermute | solution.py:358
  15.8 2.8 %collective-permute-start.8 = (bf16[8,1152]{1,0:T(8,128)(2,1)S(1)}, bf16[8,1152]{1,0:T(8,128)(2,1)S(1)}, u32[]{:S(2)}, u32[]{:S(2)}) collective-permute-start(bf16[8,1152]{1,0:T(8,128)(2,1)S(1)} %pad_maximum_fusion.1), channel_id=1, source_target_pairs={{0,2},{1,3},{2,0},{3,1},{4,6},{5,7},{6,4},{7,5},{8,10},{9,11},{10,... | collective-permute-start | bytes 55304 | tf_op jit(solution)/shard_map/ppermute | solution.py:358
  18.7 0.0 copy-done
  18.7 0.0 copy-start.1
  18.7 0.0 copy-start.2
  18.7 2.3 %shard_map.69 = (bf16[224,384]{1,0:T(8,128)(2,1)S(1)}, bf16[224,384]{1,0:T(8,128)(2,1)S(1)}, bf16[224,384]{1,0:T(8,128)(2,1)S(1)}, bf16[224,384]{1,0:T(8,128)(2,...) custom-call(bf16[1152,384]{1,0:T(8,128)(2,1)S(1)} %get-tuple-element.28.normed_ref, ...), custom_call_target="tpu_custom_call" | custom-call | flops 1146617856 | bytes 8388608 | tf_op jit(solution)/shard_map/pallas_call | solution.py:410
  21.0 1.6 %collective-permute-start.2 = (bf16[224,384]{1,0:T(8,128)(2,1)S(1)}, bf16[224,384]{1,0:T(8,128)(2,1)S(1)}, u32[]{:S(2)}, u32[]{:S(2)}) collective-permute-start(bf16[224,384]{1,0:T(8,128)(2,1)S(1)} %get-tuple-element.30), channel_id=1, source_target_pairs={{0,8},{4,12},{8,0},{12,4},{16,24},{20,28},{24,16},{28,20},{1,9},{5... | collective-permute-start | bytes 516104 | tf_op jit(solution)/shard_map/ppermute | solution.py:358
  22.6 1.5 %collective-permute-start.3 = (bf16[224,384]{1,0:T(8,128)(2,1)S(1)}, bf16[224,384]{1,0:T(8,128)(2,1)S(1)}, u32[]{:S(2)}, u32[]{:S(2)}) collective-permute-start(bf16[224,384]{1,0:T(8,128)(2,1)S(1)} %get-tuple-element.31), channel_id=1, source_target_pairs={{0,16},{4,20},{8,24},{12,28},{16,0},{20,4},{24,8},{28,12},{1,17},{... | collective-permute-start | bytes 516104 | tf_op jit(solution)/shard_map/ppermute | solution.py:358
  24.1 0.0 collective-permute-start.4
  24.1 0.0 collective-permute-done.1.rest_1_
  24.1 0.8 %collective-permute-start.5 = (bf16[224,384]{1,0:T(8,128)(2,1)S(1)}, bf16[224,384]{1,0:T(8,128)(2,1)S(1)}, u32[]{:S(2)}, u32[]{:S(2)}) collective-permute-start(bf16[224,384]{1,0:T(8,128)(2,1)S(1)} %get-tuple-element.33), channel_id=1, source_target_pairs={{0,20},{4,16},{8,28},{12,24},{16,4},{20,0},{24,12},{28,8},{1,21},{... | collective-permute-start | bytes 516104 | tf_op jit(solution)/shard_map/ppermute | solution.py:358
  24.9 0.0 collective-permute-done.8
  24.9 0.0 collective-permute-start.6
  24.9 3.1 %collective-permute-done.2.rest_2_ = bf16[224,384]{1,0:T(8,128)(2,1)S(1)} collective-permute-done((bf16[224,384]{1,0:T(8,128)(2,1)S(1)}, bf16[224,384]{1,0:T(8,128)(2,1)S(1)}, u32[]{:S(2)}, u32[]{:S(2)}) %collective-permute-start.2) | collective-permute-done | bytes 172064 | tf_op jit(solution)/shard_map/ppermute | solution.py:358
  28.0 0.9 %collective-permute-done.3.rest_3_ = bf16[224,384]{1,0:T(8,128)(2,1)S(1)} collective-permute-done((bf16[224,384]{1,0:T(8,128)(2,1)S(1)}, bf16[224,384]{1,0:T(8,128)(2,1)S(1)}, u32[]{:S(2)}, u32[]{:S(2)}) %collective-permute-start.3) | collective-permute-done | bytes 172064 | tf_op jit(solution)/shard_map/ppermute | solution.py:358
  28.9 1.9 %collective-permute-done.4.rest_4_ = bf16[224,384]{1,0:T(8,128)(2,1)S(1)} collective-permute-done((bf16[224,384]{1,0:T(8,128)(2,1)S(1)}, bf16[224,384]{1,0:T(8,128)(2,1)S(1)}, u32[]{:S(2)}, u32[]{:S(2)}) %collective-permute-start.4) | collective-permute-done | bytes 172064 | tf_op jit(solution)/shard_map/ppermute | solution.py:358
  30.8 0.0 collective-permute-done.5.rest_5_
  30.8 0.0 collective-permute-done.6.rest_6_
  30.8 0.0 copy-done.3
  30.8 7.6 %shard_map.70 = bf16[8,80,384]{2,1,0:T(8,128)(2,1)S(1)} custom-call(s32[1,3072]{1,0:T(1,128)S(1)} %copy-done.3, bf16[224,384]{1,0:T(8,128)(2,1)S(1)} %collective-permute-done.rest_0_, bf16[224,384]{1,0:T(8,128)(2,1)S(1)} %collective-permute-done.1.rest_1_, bf16[224,384]{1,0:T(8,128)(2,1)S(1)} %collective-permute-done.2.rest_2_, ...), custom_call_target="tpu_custom_call" | custom-call | flops 905969664 | bytes 8388608 | tf_op jit(solution)/shard_map/pallas_call | solution.py:451
  38.5 12.2 %all_to_all.5.got_ref = bf16[8,80,384]{2,1,0:T(8,128)(2,1)S(1)} all-to-all(bf16[8,80,384]{2,1,0:T(8,128)(2,1)S(1)} %shard_map.70), channel_id=1, replica_groups=mesh['grp'=8,'blk'=4] {'grp'}, dimensions={0} | all-to-all | bytes 983040 | tf_op jit(solution)/shard_map/all_to_all | solution.py:376
  50.7 0.0 copy-done.1
  50.7 0.0 copy-done.2
  50.7 2.4 %shard_map.71 = (bf16[384,1152]{1,0:T(8,128)(2,1)}, f32[1,4]{1,0:T(1,128)}) custom-call(bf16[384,1152]{1,0:T(8,128)(2,1)S(1)} %bitcast.7, bf16[8,80,384]{2,1,0:T(8,128)(2,1)S(1)} %all_to_all.5.got_ref, bf16[576,1152]{1,0:T(8,128)(2,1)S(1)} %copy-done.2, bf16[16,1152]{1,0:T(8,128)(2,1)S(1)} %pad_maximum_fusion.text_ref), custom_call_target="tpu_custom_call" | custom-call | flops 509607936 | bytes 8388608 | tf_op jit(solution)/shard_map/pallas_call | solution.py:474
  (2 shorter events, 0.0 us)
Async XLA Ops:
  0.6 18.0 %copy-start = (bf16[1152,1728]{0,1:T(8,128)(2,1)S(1)}, bf16[1152,1728]{0,1:T(8,128)(2,1)}, u32[]{:S(2)}) copy-start(bf16[1152,1728]{0,1:T(8,128)(2,1)} %param.7) | copy-start | bytes 11943940
  0.6 11.5 %copy-start.4 = (bf16[4,1152]{1,0:T(4,128)(2,1)S(1)}, bf16[4,1152]{1,0:T(4,128)(2,1)}, u32[]{:S(2)}) copy-start(bf16[4,1152]{1,0:T(4,128)(2,1)} %param.9) | copy-start | bytes 27652
  0.7 30.2 %copy-start.3 = (s32[1,3072]{1,0:T(1,128)S(1)}, s32[1,3072]{1,0:T(1,128)}, u32[]{:S(2)}) copy-start(s32[1,3072]{1,0:T(1,128)} %ids_ref.3) | copy-start | bytes 36868
  3.8 8.3 %collective-permute-start = (bf16[224,384]{1,0:T(8,128)(2,1)S(1)}, bf16[224,384]{1,0:T(8,128)(2,1)S(1)}, u32[]{:S(2)}, u32[]{:S(2)}) collective-permute-start(bf16[224,384]{1,0:T(8,128)(2,1)S(1)} %get-tuple-element.25), channel_id=1, source_target_pairs={{0,24},{4,28},{8,16},{12,20},{16,8},{20,12},{24,0},{28,4},{1,25},{... | collective-permute-start | bytes 516104 | tf_op jit(solution)/shard_map/ppermute | solution.py:358
  12.1 3.7 %collective-permute-start.7 = (bf16[4,1152]{1,0:T(4,128)(2,1)S(1)}, bf16[4,1152]{1,0:T(4,128)(2,1)S(1)}, u32[]{:S(2)}, u32[]{:S(2)}) collective-permute-start(bf16[4,1152]{1,0:T(4,128)(2,1)S(1)} %copy-done.4), channel_id=1, source_target_pairs={{0,1},{1,0},{2,3},{3,2},{4,5},{5,4},{6,7},{7,6},{8,9},{9,8},{10,11... | collective-permute-start | bytes 27656 | tf_op jit(solution)/shard_map/ppermute | solution.py:358
  13.9 10.2 %collective-permute-start.1 = (bf16[224,384]{1,0:T(8,128)(2,1)S(1)}, bf16[224,384]{1,0:T(8,128)(2,1)S(1)}, u32[]{:S(2)}, u32[]{:S(2)}) collective-permute-start(bf16[224,384]{1,0:T(8,128)(2,1)S(1)} %get-tuple-element.27), channel_id=1, source_target_pairs={{0,28},{4,24},{8,20},{12,16},{16,12},{20,8},{24,4},{28,0},{1,29},{... | collective-permute-start | bytes 516104 | tf_op jit(solution)/shard_map/ppermute | solution.py:358
  15.8 9.0 %collective-permute-start.8 = (bf16[8,1152]{1,0:T(8,128)(2,1)S(1)}, bf16[8,1152]{1,0:T(8,128)(2,1)S(1)}, u32[]{:S(2)}, u32[]{:S(2)}) collective-permute-start(bf16[8,1152]{1,0:T(8,128)(2,1)S(1)} %pad_maximum_fusion.1), channel_id=1, source_target_pairs={{0,2},{1,3},{2,0},{3,1},{4,6},{5,7},{6,4},{7,5},{8,10},{9,11},{10,... | collective-permute-start | bytes 55304 | tf_op jit(solution)/shard_map/ppermute | solution.py:358
  18.7 32.1 %copy-start.1 = (bf16[1,384,1152]{2,1,0:T(8,128)(2,1)S(1)}, bf16[1,384,1152]{2,1,0:T(8,128)(2,1)}, u32[]{:S(2)}) copy-start(bf16[1,384,1152]{2,1,0:T(8,128)(2,1)} %param.5) | copy-start | bytes 2654212
  18.7 32.1 %copy-start.2 = (bf16[576,1152]{1,0:T(8,128)(2,1)S(1)}, bf16[576,1152]{1,0:T(8,128)(2,1)}, u32[]{:S(2)}) copy-start(bf16[576,1152]{1,0:T(8,128)(2,1)} %out_weight_ref.1) | copy-start | bytes 3981316
  21.0 7.0 %collective-permute-start.2 = (bf16[224,384]{1,0:T(8,128)(2,1)S(1)}, bf16[224,384]{1,0:T(8,128)(2,1)S(1)}, u32[]{:S(2)}, u32[]{:S(2)}) collective-permute-start(bf16[224,384]{1,0:T(8,128)(2,1)S(1)} %get-tuple-element.30), channel_id=1, source_target_pairs={{0,8},{4,12},{8,0},{12,4},{16,24},{20,28},{24,16},{28,20},{1,9},{5... | collective-permute-start | bytes 516104 | tf_op jit(solution)/shard_map/ppermute | solution.py:358
  22.6 6.3 %collective-permute-start.3 = (bf16[224,384]{1,0:T(8,128)(2,1)S(1)}, bf16[224,384]{1,0:T(8,128)(2,1)S(1)}, u32[]{:S(2)}, u32[]{:S(2)}) collective-permute-start(bf16[224,384]{1,0:T(8,128)(2,1)S(1)} %get-tuple-element.31), channel_id=1, source_target_pairs={{0,16},{4,20},{8,24},{12,28},{16,0},{20,4},{24,8},{28,12},{1,17},{... | collective-permute-start | bytes 516104 | tf_op jit(solution)/shard_map/ppermute | solution.py:358
  24.1 6.7 %collective-permute-start.4 = (bf16[224,384]{1,0:T(8,128)(2,1)S(1)}, bf16[224,384]{1,0:T(8,128)(2,1)S(1)}, u32[]{:S(2)}, u32[]{:S(2)}) collective-permute-start(bf16[224,384]{1,0:T(8,128)(2,1)S(1)} %get-tuple-element.32), channel_id=1, source_target_pairs={{0,12},{4,8},{8,4},{12,0},{16,28},{20,24},{24,20},{28,16},{1,13},{... | collective-permute-start | bytes 516104 | tf_op jit(solution)/shard_map/ppermute | solution.py:358
  24.1 6.7 %collective-permute-start.5 = (bf16[224,384]{1,0:T(8,128)(2,1)S(1)}, bf16[224,384]{1,0:T(8,128)(2,1)S(1)}, u32[]{:S(2)}, u32[]{:S(2)}) collective-permute-start(bf16[224,384]{1,0:T(8,128)(2,1)S(1)} %get-tuple-element.33), channel_id=1, source_target_pairs={{0,20},{4,16},{8,28},{12,24},{16,4},{20,0},{24,12},{28,8},{1,21},{... | collective-permute-start | bytes 516104 | tf_op jit(solution)/shard_map/ppermute | solution.py:358
  24.9 6.0 %collective-permute-start.6 = (bf16[224,384]{1,0:T(8,128)(2,1)S(1)}, bf16[224,384]{1,0:T(8,128)(2,1)S(1)}, u32[]{:S(2)}, u32[]{:S(2)}) collective-permute-start(bf16[224,384]{1,0:T(8,128)(2,1)S(1)} %get-tuple-element.34), channel_id=1, source_target_pairs={{0,4},{4,0},{8,12},{12,8},{16,20},{20,16},{24,28},{28,24},{1,5},{5... | collective-permute-start | bytes 516104 | tf_op jit(solution)/shard_map/ppermute | solution.py:358

commit v6 on v5

--- a/solution.py
+++ b/solution.py
@@ -360,16 +360,8 @@
 
 def all_texts(texts):
     peers = lax.axis_size("blk")
-    if peers & (peers - 1):
-        shifts = range(1, peers)
-        others = [moved(texts, "blk", [(i, (i + by) % peers) for i in range(peers)]) for by in shifts]
-        return jnp.concatenate([texts] + others, axis=0)
-    by = 1
-    while by < peers:
-        other = moved(texts, "blk", [(i, i ^ by) for i in range(peers)])
-        texts = jnp.concatenate([texts, other], axis=0)
-        by *= 2
-    return texts
+    shifts = range(1, peers)
+    return [texts] + [moved(texts, "blk", [(i, (i + by) % peers) for i in range(peers)]) for by in shifts]
 
 
 def exchanged(blocks, groups):
@@ -419,8 +411,9 @@
     for by in ORDER:
         pairs = [(i, i ^ by) for i in range(group_size)]
         got.append(moved(sent[by], "grp", pairs) if by else sent[by])
-    text_embed, got[0] = lax.optimization_barrier((text_embed, got[0]))
+    text_embed, got[-1] = lax.optimization_barrier((text_embed, got[-1]))
     got, texts = lax.optimization_barrier((got, all_texts(text_embed)))
+    texts = jnp.concatenate(texts, axis=0)
 
     length = HEADS * count
     halo = 0

time: 53.8 us -> 51 us (0.948)
  blocking collectives: 12.2 us -> 0 us
  waiting for transfers between devices: 11.5 us -> 16.7 us
  starting transfers between devices: 13.1 us -> 17.1 us
  Pallas kernels: 15.5 us -> 16.3 us
    all_to_all x1 -> x0, blocking collectives: 12.2 us -> none  [exchanged(): lax.all_to_all(blocks, 'grp', 0, 0, axis_index_groups=groups, tiled=True)]
    all_to_all x0 -> x1, waiting for transfers between devices: none -> 9.36 us  [exchanged(): lax.all_to_all(blocks, 'grp', 0, 0, axis_index_groups=groups, tiled=True)]
    ppermute x9 -> x10, waiting for transfers between devices: 11.5 us -> 7.36 us  [moved(): return lax.ppermute(value, axis, pairs)]
    all_to_all x0 -> x1, starting transfers between devices: none -> 4.09 us  [exchanged(): lax.all_to_all(blocks, 'grp', 0, 0, axis_index_groups=groups, tiled=True)]
    pallas_call x1, Pallas kernels: 7.64 us -> 8.45 us  [local(): call(functools.partial(attend_kernel, images, piggy, halo), shape((HEADS,...]
    ppermute x9 -> x10, starting transfers between devices: 13.1 us -> 13 us  [moved(): return lax.ppermute(value, axis, pairs)]
  transfers between devices with their start and end apart: 9 -> 11, of which waited for: 5 -> 6; matrix products, arithmetic and copies ran while one was open for 0% -> 0% of each run, Pallas kernels for 4% -> 5%
where the time goes in v6:
time: 51 us; the launch traced here: 50.8 us
  starting transfers between devices  17.1 us (34%)
  waiting for transfers between devices  16.7 us (33%)
  Pallas kernels  16.3 us (32%)
  between operations  0.7 us (1%)
    ppermute x10, starting transfers between devices, moved(): return lax.ppermute(value, axis, pairs)  13 us
    all_to_all x1, waiting for transfers between devices, exchanged(): lax.all_to_all(blocks, 'grp', 0, 0, axis_index_groups=groups, tiled=True)  9.36 us
    pallas_call x1, Pallas kernels, local(): call(functools.partial(attend_kernel, images, piggy, halo), shape((HEADS,...  8.45 us
    ppermute x10, waiting for transfers between devices, moved(): return lax.ppermute(value, axis, pairs)  7.36 us
    all_to_all x1, starting transfers between devices, exchanged(): lax.all_to_all(blocks, 'grp', 0, 0, axis_index_groups=groups, tiled=True)  4.09 us
    pallas_call x1, Pallas kernels, local(): call(functools.partial(far_kernel, images, piggy), (shape((depth, count),...  3.12 us
    pallas_call x1, Pallas kernels, local(): call(functools.partial(finish_kernel, images), (shape((count, depth), bf1...  2.38 us
    pallas_call x1, Pallas kernels, local(): call(functools.partial(near_kernel, piggy), (block,) * 6, [], in_vmem(3),...  2.35 us
  transfers between devices with their start and end apart: 11, of which 6 were waited for; matrix products, arithmetic and copies ran while one was open for 0% of the time, Pallas kernels for 5%

profile of v6, /device:TPU:0, one launch (start us, length us, event | category | flops | bytes accessed | tf_op | source)
XLA Modules:
  0.0 50.8 jit_solution(7092307801988721322)
XLA Ops:
  0.6 0.0 copy-start
  0.6 0.0 copy-start.4
  0.7 0.0 copy-start.3
  0.7 3.1 %shard_map.68 = (bf16[1152,384]{1,0:T(8,128)(2,1)S(1)}, f32[8,1152]{1,0:T(8,128)S(1)}, bf16[224,384]{1,0:T(8,128)(2,1)S(1)}, bf16[224,384]{1,0:T(8,128)(2,1)S(1)}) custom-call(s32[1,3072]{1,0:T(1,128)} %ids_ref.3, bf16[384,1152]{1,0:T(8,128)(2,1)} %bitcast.6, bf16[1728,1152]{1,0:T(8,128)(2,1)} %bitcast.4), custom_call_target="tpu_custom_call" | custom-call | flops 382205952 | bytes 8388608 | tf_op jit(solution)/shard_map/pallas_call | solution.py:388
  3.8 4.0 %collective-permute-start = (bf16[224,384]{1,0:T(8,128)(2,1)S(1)}, bf16[224,384]{1,0:T(8,128)(2,1)S(1)}, u32[]{:S(2)}, u32[]{:S(2)}) collective-permute-start(bf16[224,384]{1,0:T(8,128)(2,1)S(1)} %get-tuple-element.28), channel_id=1, source_target_pairs={{0,24},{4,28},{8,16},{12,20},{16,8},{20,12},{24,0},{28,4},{1,25},{... | collective-permute-start | bytes 516104 | tf_op jit(solution)/shard_map/ppermute | solution.py:358
  7.7 0.0 collective-permute-start.1
  7.8 0.0 copy-done
  7.8 0.0 copy-start.1
  7.8 0.0 copy-start.2
  7.8 2.4 %shard_map.69 = (bf16[224,384]{1,0:T(8,128)(2,1)S(1)}, bf16[224,384]{1,0:T(8,128)(2,1)S(1)}, bf16[224,384]{1,0:T(8,128)(2,1)S(1)}, bf16[224,384]{1,0:T(8,128)(2,...) custom-call(bf16[1152,384]{1,0:T(8,128)(2,1)S(1)} %get-tuple-element.30.normed_ref, ...), custom_call_target="tpu_custom_call" | custom-call | flops 1146617856 | bytes 8388608 | tf_op jit(solution)/shard_map/pallas_call | solution.py:402
  10.1 0.0 copy-done.4
  10.1 3.7 %collective-permute-start.9 = (bf16[4,1152]{1,0:T(4,128)(2,1)S(1)}, bf16[4,1152]{1,0:T(4,128)(2,1)S(1)}, u32[]{:S(2)}, u32[]{:S(2)}) collective-permute-start(bf16[4,1152]{1,0:T(4,128)(2,1)S(1)} %copy-done.4), channel_id=1, source_target_pairs={{0,3},{1,0},{2,1},{3,2},{4,7},{5,4},{6,5},{7,6},{8,11},{9,8},{10,9... | collective-permute-start | bytes 27656 | tf_op jit(solution)/shard_map/ppermute | solution.py:358
  13.8 0.0 collective-permute-start.8
  13.8 1.0 %collective-permute-start.7 = (bf16[4,1152]{1,0:T(4,128)(2,1)S(1)}, bf16[4,1152]{1,0:T(4,128)(2,1)S(1)}, u32[]{:S(2)}, u32[]{:S(2)}) collective-permute-start(bf16[4,1152]{1,0:T(4,128)(2,1)S(1)} %copy-done.4), channel_id=1, source_target_pairs={{0,1},{1,2},{2,3},{3,0},{4,5},{5,6},{6,7},{7,4},{8,9},{9,10},{10,1... | collective-permute-start | bytes 27656 | tf_op jit(solution)/shard_map/ppermute | solution.py:358
  14.8 0.4 collective-permute-done.9
  15.2 1.1 %collective-permute-start.2 = (bf16[224,384]{1,0:T(8,128)(2,1)S(1)}, bf16[224,384]{1,0:T(8,128)(2,1)S(1)}, u32[]{:S(2)}, u32[]{:S(2)}) collective-permute-start(bf16[224,384]{1,0:T(8,128)(2,1)S(1)} %get-tuple-element.32), channel_id=1, source_target_pairs={{0,8},{4,12},{8,0},{12,4},{16,24},{20,28},{24,16},{28,20},{1,9},{5... | collective-permute-start | bytes 516104 | tf_op jit(solution)/shard_map/ppermute | solution.py:358
  16.3 2.1 %collective-permute-done.8 = bf16[4,1152]{1,0:T(4,128)(2,1)S(1)} collective-permute-done((bf16[4,1152]{1,0:T(4,128)(2,1)S(1)}, bf16[4,1152]{1,0:T(4,128)(2,1)S(1)}, u32[]{:S(2)}, u32[]{:S(2)}) %collective-permute-start.8) | collective-permute-done | bytes 9248 | tf_op jit(solution)/shard_map/ppermute | solution.py:358
  18.3 1.1 %collective-permute-start.3 = (bf16[224,384]{1,0:T(8,128)(2,1)S(1)}, bf16[224,384]{1,0:T(8,128)(2,1)S(1)}, u32[]{:S(2)}, u32[]{:S(2)}) collective-permute-start(bf16[224,384]{1,0:T(8,128)(2,1)S(1)} %get-tuple-element.33), channel_id=1, source_target_pairs={{0,16},{4,20},{8,24},{12,28},{16,0},{20,4},{24,8},{28,12},{1,17},{... | collective-permute-start | bytes 516104 | tf_op jit(solution)/shard_map/ppermute | solution.py:358
  19.5 0.0 collective-permute-done.7
  19.5 0.3 collective-permute-start.4
  19.8 0.0 collective-permute-done.rest_0_
  19.8 1.8 %collective-permute-start.5 = (bf16[224,384]{1,0:T(8,128)(2,1)S(1)}, bf16[224,384]{1,0:T(8,128)(2,1)S(1)}, u32[]{:S(2)}, u32[]{:S(2)}) collective-permute-start(bf16[224,384]{1,0:T(8,128)(2,1)S(1)} %get-tuple-element.35), channel_id=1, source_target_pairs={{0,20},{4,16},{8,28},{12,24},{16,4},{20,0},{24,12},{28,8},{1,21},{... | collective-permute-start | bytes 516104 | tf_op jit(solution)/shard_map/ppermute | solution.py:358
  21.6 0.0 collective-permute-done.1.rest_1_
  21.6 0.0 collective-permute-start.6
  21.6 0.0 collective-permute-done.2.rest_2_
  21.6 3.1 %collective-permute-done.3.rest_3_ = bf16[224,384]{1,0:T(8,128)(2,1)S(1)} collective-permute-done((bf16[224,384]{1,0:T(8,128)(2,1)S(1)}, bf16[224,384]{1,0:T(8,128)(2,1)S(1)}, u32[]{:S(2)}, u32[]{:S(2)}) %collective-permute-start.3) | collective-permute-done | bytes 172064 | tf_op jit(solution)/shard_map/ppermute | solution.py:358
  24.7 1.4 %collective-permute-done.4.rest_4_ = bf16[224,384]{1,0:T(8,128)(2,1)S(1)} collective-permute-done((bf16[224,384]{1,0:T(8,128)(2,1)S(1)}, bf16[224,384]{1,0:T(8,128)(2,1)S(1)}, u32[]{:S(2)}, u32[]{:S(2)}) %collective-permute-start.4) | collective-permute-done | bytes 172064 | tf_op jit(solution)/shard_map/ppermute | solution.py:358
  26.1 0.4 collective-permute-done.5.rest_5_
  26.5 0.0 collective-permute-done.6.rest_6_
  26.5 0.0 copy-done.3
  26.5 8.4 %shard_map.70 = bf16[8,80,384]{2,1,0:T(8,128)(2,1)} custom-call(s32[1,3072]{1,0:T(1,128)S(1)} %copy-done.3, bf16[224,384]{1,0:T(8,128)(2,1)S(1)} %collective-permute-done.rest_0_, bf16[224,384]{1,0:T(8,128)(2,1)S(1)} %collective-permute-done.1.rest_1_, bf16[224,384]{1,0:T(8,128)(2,1)S(1)} %collective-permute-done.2.rest_2_, ...), custom_call_target="tpu_custom_call" | custom-call | flops 905969664 | bytes 8388608 | tf_op jit(solution)/shard_map/pallas_call | solution.py:444
  35.0 4.1 %all-to-all-start = ((bf16[8,80,384]{2,1,0:T(8,128)(2,1)}), bf16[8,80,384]{2,1,0:T(8,128)(2,1)S(1)}, u32[]{:S(2)}, u32[]{:S(2)}) async-start(bf16[8,80,384]{2,1,0:T(8,128)(2,1)} %shard_map.70), calls=%async_computation | async-start | bytes 983040 | tf_op jit(solution)/shard_map/all_to_all | solution.py:368
  39.1 9.4 %all-to-all-done.got_ref = bf16[8,80,384]{2,1,0:T(8,128)(2,1)S(1)} async-done(((bf16[8,80,384]{2,1,0:T(8,128)(2,1)}), bf16[8,80,384]{2,1,0:T(8,128)(2,1)S(1)}, u32[]{:S(2)}, u32[]{:S(2)}) %all-to-all-start) | async-done | bytes 491552 | tf_op jit(solution)/shard_map/all_to_all | solution.py:368
  48.5 0.0 copy-done.1
  48.5 0.0 copy-done.2
  48.5 2.4 %shard_map.71 = (bf16[384,1152]{1,0:T(8,128)(2,1)}, f32[1,4]{1,0:T(1,128)}) custom-call(bf16[384,1152]{1,0:T(8,128)(2,1)S(1)} %bitcast.7, bf16[8,80,384]{2,1,0:T(8,128)(2,1)S(1)} %all-to-all-done.got_ref, bf16[576,1152]{1,0:T(8,128)(2,1)S(1)} %copy-done.2, bf16[16,1152]{1,0:T(8,128)(2,1)S(1)} %pad_maximum_fusion.text_ref), custom_call_target="tpu_custom_call" | custom-call | flops 509607936 | bytes 8388608 | tf_op jit(solution)/shard_map/pallas_call | solution.py:467
  (1 shorter events, 0.0 us)
Async XLA Ops:
  0.6 7.1 %copy-start = (bf16[1152,1728]{0,1:T(8,128)(2,1)S(1)}, bf16[1152,1728]{0,1:T(8,128)(2,1)}, u32[]{:S(2)}) copy-start(bf16[1152,1728]{0,1:T(8,128)(2,1)} %param.7) | copy-start | bytes 11943940
  0.6 9.5 %copy-start.4 = (bf16[4,1152]{1,0:T(4,128)(2,1)S(1)}, bf16[4,1152]{1,0:T(4,128)(2,1)}, u32[]{:S(2)}) copy-start(bf16[4,1152]{1,0:T(4,128)(2,1)} %param.9) | copy-start | bytes 27652
  0.7 25.9 %copy-start.3 = (s32[1,3072]{1,0:T(1,128)S(1)}, s32[1,3072]{1,0:T(1,128)}, u32[]{:S(2)}) copy-start(s32[1,3072]{1,0:T(1,128)} %ids_ref.3) | copy-start | bytes 36868
  3.8 16.1 %collective-permute-start = (bf16[224,384]{1,0:T(8,128)(2,1)S(1)}, bf16[224,384]{1,0:T(8,128)(2,1)S(1)}, u32[]{:S(2)}, u32[]{:S(2)}) collective-permute-start(bf16[224,384]{1,0:T(8,128)(2,1)S(1)} %get-tuple-element.28), channel_id=1, source_target_pairs={{0,24},{4,28},{8,16},{12,20},{16,8},{20,12},{24,0},{28,4},{1,25},{... | collective-permute-start | bytes 516104 | tf_op jit(solution)/shard_map/ppermute | solution.py:358
  7.7 13.9 %collective-permute-start.1 = (bf16[224,384]{1,0:T(8,128)(2,1)S(1)}, bf16[224,384]{1,0:T(8,128)(2,1)S(1)}, u32[]{:S(2)}, u32[]{:S(2)}) collective-permute-start(bf16[224,384]{1,0:T(8,128)(2,1)S(1)} %get-tuple-element.29), channel_id=1, source_target_pairs={{0,28},{4,24},{8,20},{12,16},{16,12},{20,8},{24,4},{28,0},{1,29},{... | collective-permute-start | bytes 516104 | tf_op jit(solution)/shard_map/ppermute | solution.py:358
  7.8 40.7 %copy-start.1 = (bf16[1,384,1152]{2,1,0:T(8,128)(2,1)S(1)}, bf16[1,384,1152]{2,1,0:T(8,128)(2,1)}, u32[]{:S(2)}) copy-start(bf16[1,384,1152]{2,1,0:T(8,128)(2,1)} %param.5) | copy-start | bytes 2654212
  7.8 40.7 %copy-start.2 = (bf16[576,1152]{1,0:T(8,128)(2,1)S(1)}, bf16[576,1152]{1,0:T(8,128)(2,1)}, u32[]{:S(2)}) copy-start(bf16[576,1152]{1,0:T(8,128)(2,1)} %out_weight_ref.1) | copy-start | bytes 3981316
  10.1 5.0 %collective-permute-start.9 = (bf16[4,1152]{1,0:T(4,128)(2,1)S(1)}, bf16[4,1152]{1,0:T(4,128)(2,1)S(1)}, u32[]{:S(2)}, u32[]{:S(2)}) collective-permute-start(bf16[4,1152]{1,0:T(4,128)(2,1)S(1)} %copy-done.4), channel_id=1, source_target_pairs={{0,3},{1,0},{2,1},{3,2},{4,7},{5,4},{6,5},{7,6},{8,11},{9,8},{10,9... | collective-permute-start | bytes 27656 | tf_op jit(solution)/shard_map/ppermute | solution.py:358
  13.8 4.6 %collective-permute-start.8 = (bf16[4,1152]{1,0:T(4,128)(2,1)S(1)}, bf16[4,1152]{1,0:T(4,128)(2,1)S(1)}, u32[]{:S(2)}, u32[]{:S(2)}) collective-permute-start(bf16[4,1152]{1,0:T(4,128)(2,1)S(1)} %copy-done.4), channel_id=1, source_target_pairs={{0,2},{1,3},{2,0},{3,1},{4,6},{5,7},{6,4},{7,5},{8,10},{9,11},{10,... | collective-permute-start | bytes 27656 | tf_op jit(solution)/shard_map/ppermute | solution.py:358
  13.8 5.7 %collective-permute-start.7 = (bf16[4,1152]{1,0:T(4,128)(2,1)S(1)}, bf16[4,1152]{1,0:T(4,128)(2,1)S(1)}, u32[]{:S(2)}, u32[]{:S(2)}) collective-permute-start(bf16[4,1152]{1,0:T(4,128)(2,1)S(1)} %copy-done.4), channel_id=1, source_target_pairs={{0,1},{1,2},{2,3},{3,0},{4,5},{5,6},{6,7},{7,4},{8,9},{9,10},{10,1... | collective-permute-start | bytes 27656 | tf_op jit(solution)/shard_map/ppermute | solution.py:358
  15.2 6.4 %collective-permute-start.2 = (bf16[224,384]{1,0:T(8,128)(2,1)S(1)}, bf16[224,384]{1,0:T(8,128)(2,1)S(1)}, u32[]{:S(2)}, u32[]{:S(2)}) collective-permute-start(bf16[224,384]{1,0:T(8,128)(2,1)S(1)} %get-tuple-element.32), channel_id=1, source_target_pairs={{0,8},{4,12},{8,0},{12,4},{16,24},{20,28},{24,16},{28,20},{1,9},{5... | collective-permute-start | bytes 516104 | tf_op jit(solution)/shard_map/ppermute | solution.py:358
  18.3 6.4 %collective-permute-start.3 = (bf16[224,384]{1,0:T(8,128)(2,1)S(1)}, bf16[224,384]{1,0:T(8,128)(2,1)S(1)}, u32[]{:S(2)}, u32[]{:S(2)}) collective-permute-start(bf16[224,384]{1,0:T(8,128)(2,1)S(1)} %get-tuple-element.33), channel_id=1, source_target_pairs={{0,16},{4,20},{8,24},{12,28},{16,0},{20,4},{24,8},{28,12},{1,17},{... | collective-permute-start | bytes 516104 | tf_op jit(solution)/shard_map/ppermute | solution.py:358
  19.5 6.6 %collective-permute-start.4 = (bf16[224,384]{1,0:T(8,128)(2,1)S(1)}, bf16[224,384]{1,0:T(8,128)(2,1)S(1)}, u32[]{:S(2)}, u32[]{:S(2)}) collective-permute-start(bf16[224,384]{1,0:T(8,128)(2,1)S(1)} %get-tuple-element.34), channel_id=1, source_target_pairs={{0,12},{4,8},{8,4},{12,0},{16,28},{20,24},{24,20},{28,16},{1,13},{... | collective-permute-start | bytes 516104 | tf_op jit(solution)/shard_map/ppermute | solution.py:358
  19.8 6.7 %collective-permute-start.5 = (bf16[224,384]{1,0:T(8,128)(2,1)S(1)}, bf16[224,384]{1,0:T(8,128)(2,1)S(1)}, u32[]{:S(2)}, u32[]{:S(2)}) collective-permute-start(bf16[224,384]{1,0:T(8,128)(2,1)S(1)} %get-tuple-element.35), channel_id=1, source_target_pairs={{0,20},{4,16},{8,28},{12,24},{16,4},{20,0},{24,12},{28,8},{1,21},{... | collective-permute-start | bytes 516104 | tf_op jit(solution)/shard_map/ppermute | solution.py:358
  21.6 4.9 %collective-permute-start.6 = (bf16[224,384]{1,0:T(8,128)(2,1)S(1)}, bf16[224,384]{1,0:T(8,128)(2,1)S(1)}, u32[]{:S(2)}, u32[]{:S(2)}) collective-permute-start(bf16[224,384]{1,0:T(8,128)(2,1)S(1)} %get-tuple-element.36), channel_id=1, source_target_pairs={{0,4},{4,0},{8,12},{12,8},{16,20},{20,16},{24,28},{28,24},{1,5},{5... | collective-permute-start | bytes 516104 | tf_op jit(solution)/shard_map/ppermute | solution.py:358
  35.0 13.5 %all-to-all-start = ((bf16[8,80,384]{2,1,0:T(8,128)(2,1)}), bf16[8,80,384]{2,1,0:T(8,128)(2,1)S(1)}, u32[]{:S(2)}, u32[]{:S(2)}) async-start(bf16[8,80,384]{2,1,0:T(8,128)(2,1)} %shard_map.70), calls=%async_computation | async-start | bytes 983040 | tf_op jit(solution)/shard_map/all_to_all | solution.py:368

commit v7 on v6

--- a/solution.py
+++ b/solution.py
@@ -411,9 +411,6 @@
     for by in ORDER:
         pairs = [(i, i ^ by) for i in range(group_size)]
         got.append(moved(sent[by], "grp", pairs) if by else sent[by])
-    text_embed, got[-1] = lax.optimization_barrier((text_embed, got[-1]))
-    got, texts = lax.optimization_barrier((got, all_texts(text_embed)))
-    texts = jnp.concatenate(texts, axis=0)
 
     length = HEADS * count
     halo = 0
@@ -460,6 +457,8 @@
         4 * size * length * MAXP,
     )(*operands)
     back_home = exchanged(answers, groups)
+    text_embed, _ = lax.optimization_barrier((text_embed, answers))
+    texts = jnp.concatenate(all_texts(text_embed), axis=0)
 
     joined = [pltpu.VMEM((HEADS * padded, count), bf16), pltpu.VMEM((HEADS * padded, depth), bf16)]
     flops = 2 * count * depth * width

time: 51 us -> 48.3 us (0.947)
  waiting for transfers between devices: 16.7 us -> 14.9 us
  starting transfers between devices: 17.1 us -> 15.4 us
  Pallas kernels: 16.3 us -> 17.3 us
    all_to_all x1, waiting for transfers between devices: 9.36 us -> 0.79 us  [exchanged(): lax.all_to_all(blocks, 'grp', 0, 0, axis_index_groups=groups, tiled=True)]
    ppermute x10, waiting for transfers between devices: 7.36 us -> 14.1 us  [moved(): return lax.ppermute(value, axis, pairs)]
    ppermute x10, starting transfers between devices: 13 us -> 11.5 us  [moved(): return lax.ppermute(value, axis, pairs)]
    pallas_call x1, Pallas kernels: 8.45 us -> 9.42 us  [local(): call(functools.partial(attend_kernel, images, piggy, halo), shape((HEADS,...]
  transfers between devices with their start and end apart: 11 -> 11, of which waited for: 6 -> 8; matrix products, arithmetic and copies ran while one was open for 0% -> 0% of each run, Pallas kernels for 5% -> 5%
where the time goes in v7:
time: 48.3 us
  Pallas kernels  17.3 us (36%)
  starting transfers between devices  15.4 us (32%)
  waiting for transfers between devices  14.9 us (31%)
  between operations  0.7 us (1%)
    ppermute x10, waiting for transfers between devices, moved(): return lax.ppermute(value, axis, pairs)  14.1 us
    ppermute x10, starting transfers between devices, moved(): return lax.ppermute(value, axis, pairs)  11.5 us
    pallas_call x1, Pallas kernels, local(): call(functools.partial(attend_kernel, images, piggy, halo), shape((HEADS,...  9.42 us
    all_to_all x1, starting transfers between devices, exchanged(): lax.all_to_all(blocks, 'grp', 0, 0, axis_index_groups=groups, tiled=True)  3.91 us
    pallas_call x1, Pallas kernels, local(): call(functools.partial(far_kernel, images, piggy), (shape((depth, count),...  3.12 us
    pallas_call x1, Pallas kernels, local(): call(functools.partial(finish_kernel, images), (shape((count, depth), bf1...  2.38 us
    pallas_call x1, Pallas kernels, local(): call(functools.partial(near_kernel, piggy), (block,) * 6, [], in_vmem(3),...  2.34 us
  transfers between devices with their start and end apart: 11, of which 8 were waited for; matrix products, arithmetic and copies ran while one was open for 0% of the time, Pallas kernels for 5%

profile of v7, /device:TPU:0, one launch (start us, length us, event | category | flops | bytes accessed | tf_op | source)
XLA Modules:
  0.0 48.3 jit_solution(13894297874997280054)
XLA Ops:
  0.6 0.0 copy-start
  0.6 0.0 copy-start.3
  0.6 3.1 %shard_map.68 = (bf16[1152,384]{1,0:T(8,128)(2,1)S(1)}, f32[8,1152]{1,0:T(8,128)S(1)}, bf16[224,384]{1,0:T(8,128)(2,1)S(1)}, bf16[224,384]{1,0:T(8,128)(2,1)S(1)}) custom-call(s32[1,3072]{1,0:T(1,128)} %ids_ref.3, bf16[384,1152]{1,0:T(8,128)(2,1)} %bitcast.6, bf16[1728,1152]{1,0:T(8,128)(2,1)} %bitcast.4), custom_call_target="tpu_custom_call" | custom-call | flops 382205952 | bytes 8388608 | tf_op jit(solution)/shard_map/pallas_call | solution.py:388
  3.8 4.0 %collective-permute-start = (bf16[224,384]{1,0:T(8,128)(2,1)S(1)}, bf16[224,384]{1,0:T(8,128)(2,1)S(1)}, u32[]{:S(2)}, u32[]{:S(2)}) collective-permute-start(bf16[224,384]{1,0:T(8,128)(2,1)S(1)} %get-tuple-element.15), channel_id=1, source_target_pairs={{0,24},{4,28},{8,16},{12,20},{16,8},{20,12},{24,0},{28,4},{1,25},{... | collective-permute-start | bytes 516104 | tf_op jit(solution)/shard_map/ppermute | solution.py:358
  7.7 0.0 collective-permute-start.1
  7.7 0.0 copy-done
  7.7 0.0 copy-start.4
  7.7 0.0 copy-start.1
  7.8 0.0 copy-start.2
  7.8 2.3 %shard_map.69 = (bf16[224,384]{1,0:T(8,128)(2,1)S(1)}, bf16[224,384]{1,0:T(8,128)(2,1)S(1)}, bf16[224,384]{1,0:T(8,128)(2,1)S(1)}, bf16[224,384]{1,0:T(8,128)(2,...) custom-call(bf16[1152,384]{1,0:T(8,128)(2,1)S(1)} %get-tuple-element.17.normed_ref, ...), custom_call_target="tpu_custom_call" | custom-call | flops 1146617856 | bytes 8388608 | tf_op jit(solution)/shard_map/pallas_call | solution.py:402
  10.1 1.2 %collective-permute-start.2 = (bf16[224,384]{1,0:T(8,128)(2,1)S(1)}, bf16[224,384]{1,0:T(8,128)(2,1)S(1)}, u32[]{:S(2)}, u32[]{:S(2)}) collective-permute-start(bf16[224,384]{1,0:T(8,128)(2,1)S(1)} %get-tuple-element.19), channel_id=1, source_target_pairs={{0,8},{4,12},{8,0},{12,4},{16,24},{20,28},{24,16},{28,20},{1,9},{5... | collective-permute-start | bytes 516104 | tf_op jit(solution)/shard_map/ppermute | solution.py:358
  11.3 1.5 %collective-permute-start.3 = (bf16[224,384]{1,0:T(8,128)(2,1)S(1)}, bf16[224,384]{1,0:T(8,128)(2,1)S(1)}, u32[]{:S(2)}, u32[]{:S(2)}) collective-permute-start(bf16[224,384]{1,0:T(8,128)(2,1)S(1)} %get-tuple-element.20), channel_id=1, source_target_pairs={{0,16},{4,20},{8,24},{12,28},{16,0},{20,4},{24,8},{28,12},{1,17},{... | collective-permute-start | bytes 516104 | tf_op jit(solution)/shard_map/ppermute | solution.py:358
  12.8 0.6 %collective-permute-start.4 = (bf16[224,384]{1,0:T(8,128)(2,1)S(1)}, bf16[224,384]{1,0:T(8,128)(2,1)S(1)}, u32[]{:S(2)}, u32[]{:S(2)}) collective-permute-start(bf16[224,384]{1,0:T(8,128)(2,1)S(1)} %get-tuple-element.21), channel_id=1, source_target_pairs={{0,12},{4,8},{8,4},{12,0},{16,28},{20,24},{24,20},{28,16},{1,13},{... | collective-permute-start | bytes 516104 | tf_op jit(solution)/shard_map/ppermute | solution.py:358
  13.4 0.0 collective-permute-done.rest_0_
  13.4 0.6 %collective-permute-start.5 = (bf16[224,384]{1,0:T(8,128)(2,1)S(1)}, bf16[224,384]{1,0:T(8,128)(2,1)S(1)}, u32[]{:S(2)}, u32[]{:S(2)}) collective-permute-start(bf16[224,384]{1,0:T(8,128)(2,1)S(1)} %get-tuple-element.22), channel_id=1, source_target_pairs={{0,20},{4,16},{8,28},{12,24},{16,4},{20,0},{24,12},{28,8},{1,21},{... | collective-permute-start | bytes 516104 | tf_op jit(solution)/shard_map/ppermute | solution.py:358
  14.0 2.2 %collective-permute-done.1.rest_1_ = bf16[224,384]{1,0:T(8,128)(2,1)S(1)} collective-permute-done((bf16[224,384]{1,0:T(8,128)(2,1)S(1)}, bf16[224,384]{1,0:T(8,128)(2,1)S(1)}, u32[]{:S(2)}, u32[]{:S(2)}) %collective-permute-start.1) | collective-permute-done | bytes 172064 | tf_op jit(solution)/shard_map/ppermute | solution.py:358
  16.2 0.0 collective-permute-start.6
  16.2 4.7 %collective-permute-done.2.rest_2_ = bf16[224,384]{1,0:T(8,128)(2,1)S(1)} collective-permute-done((bf16[224,384]{1,0:T(8,128)(2,1)S(1)}, bf16[224,384]{1,0:T(8,128)(2,1)S(1)}, u32[]{:S(2)}, u32[]{:S(2)}) %collective-permute-start.2) | collective-permute-done | bytes 172064 | tf_op jit(solution)/shard_map/ppermute | solution.py:358
  20.9 0.0 collective-permute-done.3.rest_3_
  20.9 1.5 %collective-permute-done.4.rest_4_ = bf16[224,384]{1,0:T(8,128)(2,1)S(1)} collective-permute-done((bf16[224,384]{1,0:T(8,128)(2,1)S(1)}, bf16[224,384]{1,0:T(8,128)(2,1)S(1)}, u32[]{:S(2)}, u32[]{:S(2)}) %collective-permute-start.4) | collective-permute-done | bytes 172064 | tf_op jit(solution)/shard_map/ppermute | solution.py:358
  22.4 0.7 %collective-permute-done.5.rest_5_ = bf16[224,384]{1,0:T(8,128)(2,1)S(1)} collective-permute-done((bf16[224,384]{1,0:T(8,128)(2,1)S(1)}, bf16[224,384]{1,0:T(8,128)(2,1)S(1)}, u32[]{:S(2)}, u32[]{:S(2)}) %collective-permute-start.5) | collective-permute-done | bytes 172064 | tf_op jit(solution)/shard_map/ppermute | solution.py:358
  23.1 0.0 collective-permute-done.6.rest_6_
  23.2 0.0 copy-done.3
  23.2 9.4 %shard_map.70 = bf16[8,80,384]{2,1,0:T(8,128)(2,1)} custom-call(s32[1,3072]{1,0:T(1,128)S(1)} %copy-done.3, bf16[224,384]{1,0:T(8,128)(2,1)S(1)} %collective-permute-done.rest_0_, bf16[224,384]{1,0:T(8,128)(2,1)S(1)} %collective-permute-done.1.rest_1_, bf16[224,384]{1,0:T(8,128)(2,1)S(1)} %collective-permute-done.2.rest_2_, ...), custom_call_target="tpu_custom_call" | custom-call | flops 905969664 | bytes 8388608 | tf_op jit(solution)/shard_map/pallas_call | solution.py:441
  32.6 3.9 %all-to-all-start = ((bf16[8,80,384]{2,1,0:T(8,128)(2,1)}), bf16[8,80,384]{2,1,0:T(8,128)(2,1)S(1)}, u32[]{:S(2)}, u32[]{:S(2)}) async-start(bf16[8,80,384]{2,1,0:T(8,128)(2,1)} %shard_map.70), calls=%async_computation | async-start | bytes 983040 | tf_op jit(solution)/shard_map/all_to_all | solution.py:368
  36.5 0.0 copy-done.4
  36.5 2.7 %collective-permute-start.9 = (bf16[4,1152]{1,0:T(4,128)(2,1)S(1)}, bf16[4,1152]{1,0:T(4,128)(2,1)S(1)}, u32[]{:S(2)}, u32[]{:S(2)}) collective-permute-start(bf16[4,1152]{1,0:T(4,128)(2,1)S(1)} %copy-done.4), channel_id=1, source_target_pairs={{0,3},{1,0},{2,1},{3,2},{4,7},{5,4},{6,5},{7,6},{8,11},{9,8},{10,9... | collective-permute-start | bytes 27656 | tf_op jit(solution)/shard_map/ppermute | solution.py:358
  39.2 0.4 collective-permute-start.8
  39.6 0.6 %collective-permute-start.7 = (bf16[4,1152]{1,0:T(4,128)(2,1)S(1)}, bf16[4,1152]{1,0:T(4,128)(2,1)S(1)}, u32[]{:S(2)}, u32[]{:S(2)}) collective-permute-start(bf16[4,1152]{1,0:T(4,128)(2,1)S(1)} %copy-done.4), channel_id=1, source_target_pairs={{0,1},{1,2},{2,3},{3,0},{4,5},{5,6},{6,7},{7,4},{8,9},{9,10},{10,1... | collective-permute-start | bytes 27656 | tf_op jit(solution)/shard_map/ppermute | solution.py:358
  40.2 0.4 collective-permute-done.9
  40.5 3.2 %collective-permute-done.8 = bf16[4,1152]{1,0:T(4,128)(2,1)S(1)} collective-permute-done((bf16[4,1152]{1,0:T(4,128)(2,1)S(1)}, bf16[4,1152]{1,0:T(4,128)(2,1)S(1)}, u32[]{:S(2)}, u32[]{:S(2)}) %collective-permute-start.8) | collective-permute-done | bytes 9248 | tf_op jit(solution)/shard_map/ppermute | solution.py:358
  43.7 1.3 %collective-permute-done.7 = bf16[4,1152]{1,0:T(4,128)(2,1)S(1)} collective-permute-done((bf16[4,1152]{1,0:T(4,128)(2,1)S(1)}, bf16[4,1152]{1,0:T(4,128)(2,1)S(1)}, u32[]{:S(2)}, u32[]{:S(2)}) %collective-permute-start.7) | collective-permute-done | bytes 9248 | tf_op jit(solution)/shard_map/ppermute | solution.py:358
  45.1 0.8 %all-to-all-done.got_ref = bf16[8,80,384]{2,1,0:T(8,128)(2,1)S(1)} async-done(((bf16[8,80,384]{2,1,0:T(8,128)(2,1)}), bf16[8,80,384]{2,1,0:T(8,128)(2,1)S(1)}, u32[]{:S(2)}, u32[]{:S(2)}) %all-to-all-start) | async-done | bytes 491552 | tf_op jit(solution)/shard_map/all_to_all | solution.py:368
  45.9 0.0 copy-done.1
  45.9 0.0 copy-done.2
  45.9 2.4 %shard_map.71 = (bf16[384,1152]{1,0:T(8,128)(2,1)}, f32[1,4]{1,0:T(1,128)}) custom-call(bf16[384,1152]{1,0:T(8,128)(2,1)S(1)} %bitcast.7, bf16[8,80,384]{2,1,0:T(8,128)(2,1)S(1)} %all-to-all-done.got_ref, bf16[576,1152]{1,0:T(8,128)(2,1)S(1)} %copy-done.2, bf16[16,1152]{1,0:T(8,128)(2,1)S(1)} %pad_maximum_fusion.text_ref), custom_call_target="tpu_custom_call" | custom-call | flops 509607936 | bytes 8388608 | tf_op jit(solution)/shard_map/pallas_call | solution.py:466
  (1 shorter events, 0.0 us)
Async XLA Ops:
  0.6 7.1 %copy-start = (bf16[1152,1728]{0,1:T(8,128)(2,1)S(1)}, bf16[1152,1728]{0,1:T(8,128)(2,1)}, u32[]{:S(2)}) copy-start(bf16[1152,1728]{0,1:T(8,128)(2,1)} %param.7) | copy-start | bytes 11943940
  0.6 22.5 %copy-start.3 = (s32[1,3072]{1,0:T(1,128)S(1)}, s32[1,3072]{1,0:T(1,128)}, u32[]{:S(2)}) copy-start(s32[1,3072]{1,0:T(1,128)} %ids_ref.3) | copy-start | bytes 36868
  3.8 9.6 %collective-permute-start = (bf16[224,384]{1,0:T(8,128)(2,1)S(1)}, bf16[224,384]{1,0:T(8,128)(2,1)S(1)}, u32[]{:S(2)}, u32[]{:S(2)}) collective-permute-start(bf16[224,384]{1,0:T(8,128)(2,1)S(1)} %get-tuple-element.15), channel_id=1, source_target_pairs={{0,24},{4,28},{8,16},{12,20},{16,8},{20,12},{24,0},{28,4},{1,25},{... | collective-permute-start | bytes 516104 | tf_op jit(solution)/shard_map/ppermute | solution.py:358
  7.7 8.5 %collective-permute-start.1 = (bf16[224,384]{1,0:T(8,128)(2,1)S(1)}, bf16[224,384]{1,0:T(8,128)(2,1)S(1)}, u32[]{:S(2)}, u32[]{:S(2)}) collective-permute-start(bf16[224,384]{1,0:T(8,128)(2,1)S(1)} %get-tuple-element.16), channel_id=1, source_target_pairs={{0,28},{4,24},{8,20},{12,16},{16,12},{20,8},{24,4},{28,0},{1,29},{... | collective-permute-start | bytes 516104 | tf_op jit(solution)/shard_map/ppermute | solution.py:358
  7.7 28.7 %copy-start.4 = (bf16[4,1152]{1,0:T(4,128)(2,1)S(1)}, bf16[4,1152]{1,0:T(4,128)(2,1)}, u32[]{:S(2)}) copy-start(bf16[4,1152]{1,0:T(4,128)(2,1)} %param.9) | copy-start | bytes 27652
  7.7 38.1 %copy-start.1 = (bf16[1,384,1152]{2,1,0:T(8,128)(2,1)S(1)}, bf16[1,384,1152]{2,1,0:T(8,128)(2,1)}, u32[]{:S(2)}) copy-start(bf16[1,384,1152]{2,1,0:T(8,128)(2,1)} %param.5) | copy-start | bytes 2654212
  7.8 38.1 %copy-start.2 = (bf16[576,1152]{1,0:T(8,128)(2,1)S(1)}, bf16[576,1152]{1,0:T(8,128)(2,1)}, u32[]{:S(2)}) copy-start(bf16[576,1152]{1,0:T(8,128)(2,1)} %out_weight_ref.1) | copy-start | bytes 3981316
  10.1 10.8 %collective-permute-start.2 = (bf16[224,384]{1,0:T(8,128)(2,1)S(1)}, bf16[224,384]{1,0:T(8,128)(2,1)S(1)}, u32[]{:S(2)}, u32[]{:S(2)}) collective-permute-start(bf16[224,384]{1,0:T(8,128)(2,1)S(1)} %get-tuple-element.19), channel_id=1, source_target_pairs={{0,8},{4,12},{8,0},{12,4},{16,24},{20,28},{24,16},{28,20},{1,9},{5... | collective-permute-start | bytes 516104 | tf_op jit(solution)/shard_map/ppermute | solution.py:358
  11.3 9.6 %collective-permute-start.3 = (bf16[224,384]{1,0:T(8,128)(2,1)S(1)}, bf16[224,384]{1,0:T(8,128)(2,1)S(1)}, u32[]{:S(2)}, u32[]{:S(2)}) collective-permute-start(bf16[224,384]{1,0:T(8,128)(2,1)S(1)} %get-tuple-element.20), channel_id=1, source_target_pairs={{0,16},{4,20},{8,24},{12,28},{16,0},{20,4},{24,8},{28,12},{1,17},{... | collective-permute-start | bytes 516104 | tf_op jit(solution)/shard_map/ppermute | solution.py:358
  12.8 9.6 %collective-permute-start.4 = (bf16[224,384]{1,0:T(8,128)(2,1)S(1)}, bf16[224,384]{1,0:T(8,128)(2,1)S(1)}, u32[]{:S(2)}, u32[]{:S(2)}) collective-permute-start(bf16[224,384]{1,0:T(8,128)(2,1)S(1)} %get-tuple-element.21), channel_id=1, source_target_pairs={{0,12},{4,8},{8,4},{12,0},{16,28},{20,24},{24,20},{28,16},{1,13},{... | collective-permute-start | bytes 516104 | tf_op jit(solution)/shard_map/ppermute | solution.py:358
  13.4 9.8 %collective-permute-start.5 = (bf16[224,384]{1,0:T(8,128)(2,1)S(1)}, bf16[224,384]{1,0:T(8,128)(2,1)S(1)}, u32[]{:S(2)}, u32[]{:S(2)}) collective-permute-start(bf16[224,384]{1,0:T(8,128)(2,1)S(1)} %get-tuple-element.22), channel_id=1, source_target_pairs={{0,20},{4,16},{8,28},{12,24},{16,4},{20,0},{24,12},{28,8},{1,21},{... | collective-permute-start | bytes 516104 | tf_op jit(solution)/shard_map/ppermute | solution.py:358
  16.2 6.9 %collective-permute-start.6 = (bf16[224,384]{1,0:T(8,128)(2,1)S(1)}, bf16[224,384]{1,0:T(8,128)(2,1)S(1)}, u32[]{:S(2)}, u32[]{:S(2)}) collective-permute-start(bf16[224,384]{1,0:T(8,128)(2,1)S(1)} %get-tuple-element.23), channel_id=1, source_target_pairs={{0,4},{4,0},{8,12},{12,8},{16,20},{20,16},{24,28},{28,24},{1,5},{5... | collective-permute-start | bytes 516104 | tf_op jit(solution)/shard_map/ppermute | solution.py:358
  32.6 13.3 %all-to-all-start = ((bf16[8,80,384]{2,1,0:T(8,128)(2,1)}), bf16[8,80,384]{2,1,0:T(8,128)(2,1)S(1)}, u32[]{:S(2)}, u32[]{:S(2)}) async-start(bf16[8,80,384]{2,1,0:T(8,128)(2,1)} %shard_map.70), calls=%async_computation | async-start | bytes 983040 | tf_op jit(solution)/shard_map/all_to_all | solution.py:368
  36.5 4.1 %collective-permute-start.9 = (bf16[4,1152]{1,0:T(4,128)(2,1)S(1)}, bf16[4,1152]{1,0:T(4,128)(2,1)S(1)}, u32[]{:S(2)}, u32[]{:S(2)}) collective-permute-start(bf16[4,1152]{1,0:T(4,128)(2,1)S(1)} %copy-done.4), channel_id=1, source_target_pairs={{0,3},{1,0},{2,1},{3,2},{4,7},{5,4},{6,5},{7,6},{8,11},{9,8},{10,9... | collective-permute-start | bytes 27656 | tf_op jit(solution)/shard_map/ppermute | solution.py:358
  39.2 4.6 %collective-permute-start.8 = (bf16[4,1152]{1,0:T(4,128)(2,1)S(1)}, bf16[4,1152]{1,0:T(4,128)(2,1)S(1)}, u32[]{:S(2)}, u32[]{:S(2)}) collective-permute-start(bf16[4,1152]{1,0:T(4,128)(2,1)S(1)} %copy-done.4), channel_id=1, source_target_pairs={{0,2},{1,3},{2,0},{3,1},{4,6},{5,7},{6,4},{7,5},{8,10},{9,11},{10,... | collective-permute-start | bytes 27656 | tf_op jit(solution)/shard_map/ppermute | solution.py:358
  39.6 5.5 %collective-permute-start.7 = (bf16[4,1152]{1,0:T(4,128)(2,1)S(1)}, bf16[4,1152]{1,0:T(4,128)(2,1)S(1)}, u32[]{:S(2)}, u32[]{:S(2)}) collective-permute-start(bf16[4,1152]{1,0:T(4,128)(2,1)S(1)} %copy-done.4), channel_id=1, source_target_pairs={{0,1},{1,2},{2,3},{3,0},{4,5},{5,6},{6,7},{7,4},{8,9},{9,10},{10,1... | collective-permute-start | bytes 27656 | tf_op jit(solution)/shard_map/ppermute | solution.py:358

commit v8 on v7

--- a/solution.py
+++ b/solution.py
@@ -161,7 +161,7 @@
         block = ref[key_at : key_at + padded].astype(jnp.float32)
         nothing = jnp.zeros((LANES - padded, block.shape[1]), jnp.float32)
         full = jnp.concatenate([key_marks[:, here], block[SPARE:], nothing], axis=0)
-        keys[here, :] = full.T.astype(jnp.bfloat16)
+        keys[here, :] = full.astype(jnp.bfloat16).T
         values[:, here] = ref[0:padded]
 
     for by, ref in zip(ORDER, got_refs):
@@ -207,12 +207,12 @@
         first = pl.multiple_of(at * tile, tile)
         labels = ids_ref[:, pl.ds(pl.multiple_of(halo + first, LANES), tile)]
         probs = jnp.exp2((scores[...] - tops[...]) * (size ** (-0.5) * math.log2(math.e)))
-        total = jnp.sum(probs, axis=0, keepdims=True)
+        share = 1.0 / jnp.sum(probs, axis=0, keepdims=True)
         weighted = jnp.dot(
             values[:, window_of(image)], probs.astype(jnp.bfloat16), preferred_element_type=jnp.float32
         )
         place = (slice(None), pl.ds(first, tile))
-        attended[place] = jnp.where(labels == image, weighted / total, attended[place])
+        attended[place] = jnp.where(labels == image, weighted * share, attended[place])
 
     pairs = jnp.int32(tiles)
     for image in range(1, images):
@@ -231,7 +231,11 @@
 
     begun = (jnp.int32(0), image_at(halo))
     score(begun, scores_a, tops_a)
-    lax.fori_loop(0, (pairs + 1) // 2, two_pairs, begun)
+    last = lax.fori_loop(0, pairs // 2, two_pairs, begun)
+
+    @pl.when(lax.rem(pairs, 2) == 1)
+    def _():
+        weigh(last, scores_a, tops_a)
 
     odd_head = lax.rem(lax.axis_index("grp"), 2) == 1
     mine = ids[:, halo : halo + total_rows]
@@ -285,11 +289,18 @@
     return spares
 
 
-def mixed_rows_of(rows_ref, flat, weight):
-    added = lax.dot_general(
-        flat[...], weight[...], (((0,), (0,)), ((), ())), preferred_element_type=jnp.float32
-    )
-    return (rows_ref[...].astype(jnp.float32) + added).astype(jnp.bfloat16)
+def send_mixed_rows(rows_ref, flat, weight, turned, mixed, mixed_ref, sems):
+    turned[...] = flat[...].T
+    pieces = sems.shape[0]
+    step = rows_ref.shape[0] // pieces
+    copies = []
+    for piece in range(pieces):
+        cut = slice(piece * step, (piece + 1) * step)
+        added = jnp.dot(turned[cut, :], weight[...], preferred_element_type=jnp.float32)
+        mixed[cut, :] = (rows_ref[cut, :].astype(jnp.float32) + added).astype(jnp.bfloat16)
+        copies.append(pltpu.make_async_copy(mixed.at[cut], mixed_ref.at[cut], sems.at[piece]))
+        copies[-1].start()
+    return copies
 
 
 def unit_rows(matrix):
@@ -301,9 +312,10 @@
     return jnp.maximum(logits, 0.0) + jnp.log1p(jnp.exp(-jnp.abs(logits)))
 
 
-def finish_kernel(images, rows_ref, got_ref, out_weight_ref, text_ref, mixed_ref, loss_ref, flat, weight, pooled_heads):
+def finish_kernel(images, rows_ref, got_ref, out_weight_ref, text_ref, mixed_ref, loss_ref, flat, weight, turned, mixed, sems, pooled_heads):
     padded = got_ref.shape[1]
     spares = joined_heads(got_ref, out_weight_ref, flat, weight)
+    copies = send_mixed_rows(rows_ref, flat, weight, turned, mixed, mixed_ref, sems)
     for head in range(HEADS):
         pooled_heads[:, head * padded : (head + 1) * padded] = spares[head][:, 0:padded]
     pooled = jnp.dot(
@@ -325,12 +337,14 @@
     image = lax.broadcasted_iota(jnp.int32, cosine.shape, 1)
     terms = losses(cosine, jnp.where(text == image, 1.0, -1.0))
     loss_ref[...] = jnp.sum(terms, axis=0, keepdims=True)[:, 0:images]
-    mixed_ref[...] = mixed_rows_of(rows_ref, flat, weight)
-
-
-def mix_kernel(rows_ref, got_ref, out_weight_ref, mixed_ref, flat, weight):
+    for copy in copies:
+        copy.wait()
+
+
+def mix_kernel(rows_ref, got_ref, out_weight_ref, mixed_ref, flat, weight, turned, mixed, sems):
     joined_heads(got_ref, out_weight_ref, flat, weight)
-    mixed_ref[...] = mixed_rows_of(rows_ref, flat, weight)
+    for copy in send_mixed_rows(rows_ref, flat, weight, turned, mixed, mixed_ref, sems):
+        copy.wait()
 
 
 def in_vmem(count):
@@ -341,8 +355,9 @@
     return pltpu.with_memory_space_constraint(value, pltpu.HBM)
 
 
-def call(kernel, out_shape, scratch, in_specs, flops):
-    out_specs = jax.tree.map(lambda _: pl.BlockSpec(memory_space=pltpu.VMEM), out_shape)
+def call(kernel, out_shape, scratch, in_specs, flops, out_specs=None):
+    if out_specs is None:
+        out_specs = jax.tree.map(lambda _: pl.BlockSpec(memory_space=pltpu.VMEM), out_shape)
     return pl.pallas_call(
         kernel,
         out_shape=out_shape,
@@ -460,7 +475,13 @@
     text_embed, _ = lax.optimization_barrier((text_embed, answers))
     texts = jnp.concatenate(all_texts(text_embed), axis=0)
 
-    joined = [pltpu.VMEM((HEADS * padded, count), bf16), pltpu.VMEM((HEADS * padded, depth), bf16)]
+    joined = [
+        pltpu.VMEM((HEADS * padded, count), bf16),
+        pltpu.VMEM((HEADS * padded, depth), bf16),
+        pltpu.VMEM((count, HEADS * padded), bf16),
+        pltpu.VMEM((count, depth), bf16),
+        pltpu.SemaphoreType.DMA((3,)),
+    ]
     flops = 2 * count * depth * width
     if piggy:
         mixed, row_loss = call(
@@ -469,9 +490,10 @@
             joined + [pltpu.VMEM((SPARE, HEADS * padded), f32)],
             in_vmem(4),
             flops,
+            (hbm, pl.BlockSpec(memory_space=pltpu.VMEM)),
         )(rows, back_home, out_weight, texts)
         return (mixed[None], row_loss[0])
-    mixed = call(mix_kernel, shape((count, depth), bf16), joined, in_vmem(3), flops)(
+    mixed = call(mix_kernel, shape((count, depth), bf16), joined, in_vmem(3), flops, hbm)(
         rows, back_home, out_weight
     )
     own_ids = lax.dynamic_slice_in_dim(segment_ids[0], lax.axis_index("grp") * count, count)

time: 48.3 us -> 47.5 us (0.983)
  starting transfers between devices: 15.4 us -> 16.8 us
  waiting for transfers between devices: 14.9 us -> 13.6 us
  Pallas kernels: 17.3 us -> 16.2 us
    ppermute x10, starting transfers between devices: 11.5 us -> 12.9 us  [moved(): return lax.ppermute(value, axis, pairs)]
    pallas_call x1, Pallas kernels: 9.42 us -> 8.41 us  [local(): call(functools.partial(attend_kernel, images, piggy, halo), shape((HEADS,...]
    all_to_all x1, waiting for transfers between devices: 0.79 us -> 0.01 us  [exchanged(): lax.all_to_all(blocks, 'grp', 0, 0, axis_index_groups=groups, tiled=True)]
  transfers between devices with their start and end apart: 11 -> 11, of which waited for: 8 -> 7; matrix products, arithmetic and copies ran while one was open for 0% -> 0% of each run, Pallas kernels for 5% -> 5%
where the time goes in v8:
time: 47.5 us; the launch traced here: 47.3 us
  starting transfers between devices  16.8 us (35%)
  Pallas kernels  16.2 us (34%)
  waiting for transfers between devices  13.6 us (29%)
  between operations  0.72 us (2%)
    ppermute x10, waiting for transfers between devices, moved(): return lax.ppermute(value, axis, pairs)  13.6 us
    ppermute x10, starting transfers between devices, moved(): return lax.ppermute(value, axis, pairs)  12.9 us
    pallas_call x1, Pallas kernels, local(): call(functools.partial(attend_kernel, images, piggy, halo), shape((HEADS,...  8.41 us
    all_to_all x1, starting transfers between devices, exchanged(): lax.all_to_all(blocks, 'grp', 0, 0, axis_index_groups=groups, tiled=True)  3.92 us
    pallas_call x1, Pallas kernels, local(): call(functools.partial(far_kernel, images, piggy), (shape((depth, count),...  3.12 us
    pallas_call x1, Pallas kernels, local(): call(functools.partial(near_kernel, piggy), (block,) * 6, [], in_vmem(3),...  2.34 us
    pallas_call x1, Pallas kernels, local(): call(functools.partial(finish_kernel, images), (shape((count, depth), bf1...  2.29 us
  transfers between devices with their start and end apart: 11, of which 7 were waited for; matrix products, arithmetic and copies ran while one was open for 0% of the time, Pallas kernels for 5%

profile of v8, /device:TPU:0, one launch (start us, length us, event | category | flops | bytes accessed | tf_op | source)
XLA Modules:
  0.0 47.3 jit_solution(7272824360667755626)
XLA Ops:
  0.6 0.0 copy-start
  0.6 0.0 copy-start.3
  0.6 3.1 %shard_map.68 = (bf16[1152,384]{1,0:T(8,128)(2,1)S(1)}, f32[8,1152]{1,0:T(8,128)S(1)}, bf16[224,384]{1,0:T(8,128)(2,1)S(1)}, bf16[224,384]{1,0:T(8,128)(2,1)S(1)}) custom-call(s32[1,3072]{1,0:T(1,128)} %ids_ref.3, bf16[384,1152]{1,0:T(8,128)(2,1)} %bitcast.6, bf16[1728,1152]{1,0:T(8,128)(2,1)} %bitcast.4), custom_call_target="tpu_custom_call" | custom-call | flops 382205952 | bytes 8388608 | tf_op jit(solution)/shard_map/pallas_call | solution.py:403
  3.8 4.0 %collective-permute-start = (bf16[224,384]{1,0:T(8,128)(2,1)S(1)}, bf16[224,384]{1,0:T(8,128)(2,1)S(1)}, u32[]{:S(2)}, u32[]{:S(2)}) collective-permute-start(bf16[224,384]{1,0:T(8,128)(2,1)S(1)} %get-tuple-element.15), channel_id=1, source_target_pairs={{0,24},{4,28},{8,16},{12,20},{16,8},{20,12},{24,0},{28,4},{1,25},{... | collective-permute-start | bytes 516104 | tf_op jit(solution)/shard_map/ppermute | solution.py:373
  7.7 0.0 collective-permute-start.1
  7.7 0.0 copy-done
  7.7 0.0 copy-start.4
  7.7 0.0 copy-start.1
  7.8 0.0 copy-start.2
  7.8 2.3 %shard_map.69 = (bf16[224,384]{1,0:T(8,128)(2,1)S(1)}, bf16[224,384]{1,0:T(8,128)(2,1)S(1)}, bf16[224,384]{1,0:T(8,128)(2,1)S(1)}, bf16[224,384]{1,0:T(8,128)(2,...) custom-call(bf16[1152,384]{1,0:T(8,128)(2,1)S(1)} %get-tuple-element.17.normed_ref, ...), custom_call_target="tpu_custom_call" | custom-call | flops 1146617856 | bytes 8388608 | tf_op jit(solution)/shard_map/pallas_call | solution.py:417
  10.1 1.2 %collective-permute-start.2 = (bf16[224,384]{1,0:T(8,128)(2,1)S(1)}, bf16[224,384]{1,0:T(8,128)(2,1)S(1)}, u32[]{:S(2)}, u32[]{:S(2)}) collective-permute-start(bf16[224,384]{1,0:T(8,128)(2,1)S(1)} %get-tuple-element.19), channel_id=1, source_target_pairs={{0,8},{4,12},{8,0},{12,4},{16,24},{20,28},{24,16},{28,20},{1,9},{5... | collective-permute-start | bytes 516104 | tf_op jit(solution)/shard_map/ppermute | solution.py:373
  11.3 1.5 %collective-permute-start.3 = (bf16[224,384]{1,0:T(8,128)(2,1)S(1)}, bf16[224,384]{1,0:T(8,128)(2,1)S(1)}, u32[]{:S(2)}, u32[]{:S(2)}) collective-permute-start(bf16[224,384]{1,0:T(8,128)(2,1)S(1)} %get-tuple-element.20), channel_id=1, source_target_pairs={{0,16},{4,20},{8,24},{12,28},{16,0},{20,4},{24,8},{28,12},{1,17},{... | collective-permute-start | bytes 516104 | tf_op jit(solution)/shard_map/ppermute | solution.py:373
  12.8 0.6 %collective-permute-start.4 = (bf16[224,384]{1,0:T(8,128)(2,1)S(1)}, bf16[224,384]{1,0:T(8,128)(2,1)S(1)}, u32[]{:S(2)}, u32[]{:S(2)}) collective-permute-start(bf16[224,384]{1,0:T(8,128)(2,1)S(1)} %get-tuple-element.21), channel_id=1, source_target_pairs={{0,12},{4,8},{8,4},{12,0},{16,28},{20,24},{24,20},{28,16},{1,13},{... | collective-permute-start | bytes 516104 | tf_op jit(solution)/shard_map/ppermute | solution.py:373
  13.4 0.0 collective-permute-done.rest_0_
  13.4 0.6 %collective-permute-start.5 = (bf16[224,384]{1,0:T(8,128)(2,1)S(1)}, bf16[224,384]{1,0:T(8,128)(2,1)S(1)}, u32[]{:S(2)}, u32[]{:S(2)}) collective-permute-start(bf16[224,384]{1,0:T(8,128)(2,1)S(1)} %get-tuple-element.22), channel_id=1, source_target_pairs={{0,20},{4,16},{8,28},{12,24},{16,4},{20,0},{24,12},{28,8},{1,21},{... | collective-permute-start | bytes 516104 | tf_op jit(solution)/shard_map/ppermute | solution.py:373
  14.0 2.2 %collective-permute-done.1.rest_1_ = bf16[224,384]{1,0:T(8,128)(2,1)S(1)} collective-permute-done((bf16[224,384]{1,0:T(8,128)(2,1)S(1)}, bf16[224,384]{1,0:T(8,128)(2,1)S(1)}, u32[]{:S(2)}, u32[]{:S(2)}) %collective-permute-start.1) | collective-permute-done | bytes 172064 | tf_op jit(solution)/shard_map/ppermute | solution.py:373
  16.2 0.0 collective-permute-start.6
  16.2 4.7 %collective-permute-done.2.rest_2_ = bf16[224,384]{1,0:T(8,128)(2,1)S(1)} collective-permute-done((bf16[224,384]{1,0:T(8,128)(2,1)S(1)}, bf16[224,384]{1,0:T(8,128)(2,1)S(1)}, u32[]{:S(2)}, u32[]{:S(2)}) %collective-permute-start.2) | collective-permute-done | bytes 172064 | tf_op jit(solution)/shard_map/ppermute | solution.py:373
  20.9 0.0 collective-permute-done.3.rest_3_
  20.9 1.5 %collective-permute-done.4.rest_4_ = bf16[224,384]{1,0:T(8,128)(2,1)S(1)} collective-permute-done((bf16[224,384]{1,0:T(8,128)(2,1)S(1)}, bf16[224,384]{1,0:T(8,128)(2,1)S(1)}, u32[]{:S(2)}, u32[]{:S(2)}) %collective-permute-start.4) | collective-permute-done | bytes 172064 | tf_op jit(solution)/shard_map/ppermute | solution.py:373
  22.4 0.7 %collective-permute-done.5.rest_5_ = bf16[224,384]{1,0:T(8,128)(2,1)S(1)} collective-permute-done((bf16[224,384]{1,0:T(8,128)(2,1)S(1)}, bf16[224,384]{1,0:T(8,128)(2,1)S(1)}, u32[]{:S(2)}, u32[]{:S(2)}) %collective-permute-start.5) | collective-permute-done | bytes 172064 | tf_op jit(solution)/shard_map/ppermute | solution.py:373
  23.1 0.0 collective-permute-done.6.rest_6_
  23.2 0.0 copy-done.3
  23.2 8.4 %shard_map.70 = bf16[8,80,384]{2,1,0:T(8,128)(2,1)} custom-call(s32[1,3072]{1,0:T(1,128)S(1)} %copy-done.3, bf16[224,384]{1,0:T(8,128)(2,1)S(1)} %collective-permute-done.rest_0_, bf16[224,384]{1,0:T(8,128)(2,1)S(1)} %collective-permute-done.1.rest_1_, bf16[224,384]{1,0:T(8,128)(2,1)S(1)} %collective-permute-done.2.rest_2_, ...), custom_call_target="tpu_custom_call" | custom-call | flops 905969664 | bytes 8388608 | tf_op jit(solution)/shard_map/pallas_call | solution.py:456
  31.6 3.9 %all-to-all-start = ((bf16[8,80,384]{2,1,0:T(8,128)(2,1)}), bf16[8,80,384]{2,1,0:T(8,128)(2,1)S(1)}, u32[]{:S(2)}, u32[]{:S(2)}) async-start(bf16[8,80,384]{2,1,0:T(8,128)(2,1)} %shard_map.70), calls=%async_computation | async-start | bytes 983040 | tf_op jit(solution)/shard_map/all_to_all | solution.py:383
  35.5 0.0 copy-done.4
  35.5 4.0 %collective-permute-start.9 = (bf16[4,1152]{1,0:T(4,128)(2,1)S(1)}, bf16[4,1152]{1,0:T(4,128)(2,1)S(1)}, u32[]{:S(2)}, u32[]{:S(2)}) collective-permute-start(bf16[4,1152]{1,0:T(4,128)(2,1)S(1)} %copy-done.4), channel_id=1, source_target_pairs={{0,3},{1,0},{2,1},{3,2},{4,7},{5,4},{6,5},{7,6},{8,11},{9,8},{10,9... | collective-permute-start | bytes 27656 | tf_op jit(solution)/shard_map/ppermute | solution.py:373
  39.5 0.0 collective-permute-start.8
  39.5 1.0 %collective-permute-start.7 = (bf16[4,1152]{1,0:T(4,128)(2,1)S(1)}, bf16[4,1152]{1,0:T(4,128)(2,1)S(1)}, u32[]{:S(2)}, u32[]{:S(2)}) collective-permute-start(bf16[4,1152]{1,0:T(4,128)(2,1)S(1)} %copy-done.4), channel_id=1, source_target_pairs={{0,1},{1,2},{2,3},{3,0},{4,5},{5,6},{6,7},{7,4},{8,9},{9,10},{10,1... | collective-permute-start | bytes 27656 | tf_op jit(solution)/shard_map/ppermute | solution.py:373
  40.5 0.4 collective-permute-done.9
  40.9 3.2 %collective-permute-done.8 = bf16[4,1152]{1,0:T(4,128)(2,1)S(1)} collective-permute-done((bf16[4,1152]{1,0:T(4,128)(2,1)S(1)}, bf16[4,1152]{1,0:T(4,128)(2,1)S(1)}, u32[]{:S(2)}, u32[]{:S(2)}) %collective-permute-start.8) | collective-permute-done | bytes 9248 | tf_op jit(solution)/shard_map/ppermute | solution.py:373
  44.1 0.9 %collective-permute-done.7 = bf16[4,1152]{1,0:T(4,128)(2,1)S(1)} collective-permute-done((bf16[4,1152]{1,0:T(4,128)(2,1)S(1)}, bf16[4,1152]{1,0:T(4,128)(2,1)S(1)}, u32[]{:S(2)}, u32[]{:S(2)}) %collective-permute-start.7) | collective-permute-done | bytes 9248 | tf_op jit(solution)/shard_map/ppermute | solution.py:373
  45.0 0.0 all-to-all-done.got_ref
  45.0 0.0 copy-done.1
  45.0 0.0 copy-done.2
  45.0 2.3 %shard_map.71 = (bf16[384,1152]{1,0:T(8,128)(2,1)}, f32[1,4]{1,0:T(1,128)}) custom-call(bf16[384,1152]{1,0:T(8,128)(2,1)S(1)} %bitcast.7, bf16[8,80,384]{2,1,0:T(8,128)(2,1)S(1)} %all-to-all-done.got_ref, bf16[576,1152]{1,0:T(8,128)(2,1)S(1)} %copy-done.2, bf16[16,1152]{1,0:T(8,128)(2,1)S(1)} %pad_maximum_fusion.text_ref), custom_call_target="tpu_custom_call" | custom-call | flops 509607936 | bytes 8388608 | tf_op jit(solution)/shard_map/pallas_call | solution.py:487
  (1 shorter events, 0.0 us)
Async XLA Ops:
  0.6 7.1 %copy-start = (bf16[1152,1728]{0,1:T(8,128)(2,1)S(1)}, bf16[1152,1728]{0,1:T(8,128)(2,1)}, u32[]{:S(2)}) copy-start(bf16[1152,1728]{0,1:T(8,128)(2,1)} %param.7) | copy-start | bytes 11943940
  0.6 22.5 %copy-start.3 = (s32[1,3072]{1,0:T(1,128)S(1)}, s32[1,3072]{1,0:T(1,128)}, u32[]{:S(2)}) copy-start(s32[1,3072]{1,0:T(1,128)} %ids_ref.3) | copy-start | bytes 36868
  3.8 9.6 %collective-permute-start = (bf16[224,384]{1,0:T(8,128)(2,1)S(1)}, bf16[224,384]{1,0:T(8,128)(2,1)S(1)}, u32[]{:S(2)}, u32[]{:S(2)}) collective-permute-start(bf16[224,384]{1,0:T(8,128)(2,1)S(1)} %get-tuple-element.15), channel_id=1, source_target_pairs={{0,24},{4,28},{8,16},{12,20},{16,8},{20,12},{24,0},{28,4},{1,25},{... | collective-permute-start | bytes 516104 | tf_op jit(solution)/shard_map/ppermute | solution.py:373
  7.7 8.5 %collective-permute-start.1 = (bf16[224,384]{1,0:T(8,128)(2,1)S(1)}, bf16[224,384]{1,0:T(8,128)(2,1)S(1)}, u32[]{:S(2)}, u32[]{:S(2)}) collective-permute-start(bf16[224,384]{1,0:T(8,128)(2,1)S(1)} %get-tuple-element.16), channel_id=1, source_target_pairs={{0,28},{4,24},{8,20},{12,16},{16,12},{20,8},{24,4},{28,0},{1,29},{... | collective-permute-start | bytes 516104 | tf_op jit(solution)/shard_map/ppermute | solution.py:373
  7.7 27.7 %copy-start.4 = (bf16[4,1152]{1,0:T(4,128)(2,1)S(1)}, bf16[4,1152]{1,0:T(4,128)(2,1)}, u32[]{:S(2)}) copy-start(bf16[4,1152]{1,0:T(4,128)(2,1)} %param.9) | copy-start | bytes 27652
  7.7 37.3 %copy-start.1 = (bf16[1,384,1152]{2,1,0:T(8,128)(2,1)S(1)}, bf16[1,384,1152]{2,1,0:T(8,128)(2,1)}, u32[]{:S(2)}) copy-start(bf16[1,384,1152]{2,1,0:T(8,128)(2,1)} %param.5) | copy-start | bytes 2654212
  7.8 37.3 %copy-start.2 = (bf16[576,1152]{1,0:T(8,128)(2,1)S(1)}, bf16[576,1152]{1,0:T(8,128)(2,1)}, u32[]{:S(2)}) copy-start(bf16[576,1152]{1,0:T(8,128)(2,1)} %out_weight_ref.1) | copy-start | bytes 3981316
  10.1 10.8 %collective-permute-start.2 = (bf16[224,384]{1,0:T(8,128)(2,1)S(1)}, bf16[224,384]{1,0:T(8,128)(2,1)S(1)}, u32[]{:S(2)}, u32[]{:S(2)}) collective-permute-start(bf16[224,384]{1,0:T(8,128)(2,1)S(1)} %get-tuple-element.19), channel_id=1, source_target_pairs={{0,8},{4,12},{8,0},{12,4},{16,24},{20,28},{24,16},{28,20},{1,9},{5... | collective-permute-start | bytes 516104 | tf_op jit(solution)/shard_map/ppermute | solution.py:373
  11.3 9.6 %collective-permute-start.3 = (bf16[224,384]{1,0:T(8,128)(2,1)S(1)}, bf16[224,384]{1,0:T(8,128)(2,1)S(1)}, u32[]{:S(2)}, u32[]{:S(2)}) collective-permute-start(bf16[224,384]{1,0:T(8,128)(2,1)S(1)} %get-tuple-element.20), channel_id=1, source_target_pairs={{0,16},{4,20},{8,24},{12,28},{16,0},{20,4},{24,8},{28,12},{1,17},{... | collective-permute-start | bytes 516104 | tf_op jit(solution)/shard_map/ppermute | solution.py:373
  12.8 9.6 %collective-permute-start.4 = (bf16[224,384]{1,0:T(8,128)(2,1)S(1)}, bf16[224,384]{1,0:T(8,128)(2,1)S(1)}, u32[]{:S(2)}, u32[]{:S(2)}) collective-permute-start(bf16[224,384]{1,0:T(8,128)(2,1)S(1)} %get-tuple-element.21), channel_id=1, source_target_pairs={{0,12},{4,8},{8,4},{12,0},{16,28},{20,24},{24,20},{28,16},{1,13},{... | collective-permute-start | bytes 516104 | tf_op jit(solution)/shard_map/ppermute | solution.py:373
  13.4 9.8 %collective-permute-start.5 = (bf16[224,384]{1,0:T(8,128)(2,1)S(1)}, bf16[224,384]{1,0:T(8,128)(2,1)S(1)}, u32[]{:S(2)}, u32[]{:S(2)}) collective-permute-start(bf16[224,384]{1,0:T(8,128)(2,1)S(1)} %get-tuple-element.22), channel_id=1, source_target_pairs={{0,20},{4,16},{8,28},{12,24},{16,4},{20,0},{24,12},{28,8},{1,21},{... | collective-permute-start | bytes 516104 | tf_op jit(solution)/shard_map/ppermute | solution.py:373
  16.2 6.9 %collective-permute-start.6 = (bf16[224,384]{1,0:T(8,128)(2,1)S(1)}, bf16[224,384]{1,0:T(8,128)(2,1)S(1)}, u32[]{:S(2)}, u32[]{:S(2)}) collective-permute-start(bf16[224,384]{1,0:T(8,128)(2,1)S(1)} %get-tuple-element.23), channel_id=1, source_target_pairs={{0,4},{4,0},{8,12},{12,8},{16,20},{20,16},{24,28},{28,24},{1,5},{5... | collective-permute-start | bytes 516104 | tf_op jit(solution)/shard_map/ppermute | solution.py:373
  31.6 13.5 %all-to-all-start = ((bf16[8,80,384]{2,1,0:T(8,128)(2,1)}), bf16[8,80,384]{2,1,0:T(8,128)(2,1)S(1)}, u32[]{:S(2)}, u32[]{:S(2)}) async-start(bf16[8,80,384]{2,1,0:T(8,128)(2,1)} %shard_map.70), calls=%async_computation | async-start | bytes 983040 | tf_op jit(solution)/shard_map/all_to_all | solution.py:383
  35.5 5.4 %collective-permute-start.9 = (bf16[4,1152]{1,0:T(4,128)(2,1)S(1)}, bf16[4,1152]{1,0:T(4,128)(2,1)S(1)}, u32[]{:S(2)}, u32[]{:S(2)}) collective-permute-start(bf16[4,1152]{1,0:T(4,128)(2,1)S(1)} %copy-done.4), channel_id=1, source_target_pairs={{0,3},{1,0},{2,1},{3,2},{4,7},{5,4},{6,5},{7,6},{8,11},{9,8},{10,9... | collective-permute-start | bytes 27656 | tf_op jit(solution)/shard_map/ppermute | solution.py:373
  39.5 4.6 %collective-permute-start.8 = (bf16[4,1152]{1,0:T(4,128)(2,1)S(1)}, bf16[4,1152]{1,0:T(4,128)(2,1)S(1)}, u32[]{:S(2)}, u32[]{:S(2)}) collective-permute-start(bf16[4,1152]{1,0:T(4,128)(2,1)S(1)} %copy-done.4), channel_id=1, source_target_pairs={{0,2},{1,3},{2,0},{3,1},{4,6},{5,7},{6,4},{7,5},{8,10},{9,11},{10,... | collective-permute-start | bytes 27656 | tf_op jit(solution)/shard_map/ppermute | solution.py:373
  39.5 5.5 %collective-permute-start.7 = (bf16[4,1152]{1,0:T(4,128)(2,1)S(1)}, bf16[4,1152]{1,0:T(4,128)(2,1)S(1)}, u32[]{:S(2)}, u32[]{:S(2)}) collective-permute-start(bf16[4,1152]{1,0:T(4,128)(2,1)S(1)} %copy-done.4), channel_id=1, source_target_pairs={{0,1},{1,2},{2,3},{3,0},{4,5},{5,6},{6,7},{7,4},{8,9},{9,10},{10,1... | collective-permute-start | bytes 27656 | tf_op jit(solution)/shard_map/ppermute | solution.py:373

commit v9 on v8

--- a/solution.py
+++ b/solution.py
@@ -13,7 +13,12 @@
 LANES = 128
 SPARE = 8
 HIDDEN = -1e30
-ORDER = (6, 7, 2, 4, 3, 5, 1, 0)
+NEAR = (2, 4, 3, 5, 1)
+FAR = (6, 7)
+EARLY = (2, 3, 1, 0)
+LATE = (4, 5, 6, 7)
+FIRST = (1, 2)
+SECOND = (3, 0)
 
 logit_scale = 30.0
 logit_bias = -5.0
@@ -71,7 +76,9 @@
     return lax.div(own, 2), lax.rem(own, 2)
 
 
-def far_kernel(images, piggy, ids_ref, rows_ref, weight_ref, normed_ref, sums_ref, same_ref, cross_ref, own_ids, rows_held, weight, id_sem, row_sem, sems):
+def first_kernel(images, piggy, ids_ref, rows_ref, weight_ref, normed_ref, sums_ref, *rest):
+    out_refs, rest = rest[: 2 * len(FIRST)], rest[2 * len(FIRST) :]
+    own_ids, rows_held, weight, id_sem, row_sem, sems = rest
     count, depth = rows_ref.shape
     width = weight_ref.shape[0] // 3
     wide = weight.shape[1]
@@ -80,14 +87,19 @@
     own = pl.multiple_of(lax.axis_index("grp") * count, LANES)
     ids_fetch = pltpu.make_async_copy(ids_ref.at[:, pl.ds(own, count)], own_ids, id_sem)
     ids_fetch.start()
-    pair, core = place_in_group()
-    pair = jnp.bitwise_xor(pair, 3)
+    own_pair, core = place_in_group()
     fetches = []
-    for at in range(3):
-        first = pl.multiple_of(at * width + pair * wide, 16)
-        fetches.append(pltpu.make_async_copy(weight_ref.at[pl.ds(first, wide)], weight.at[at], sems.at[at]))
-    for fetch in fetches:
-        fetch.start()
+    for step, move in enumerate(FIRST):
+        pair = jnp.bitwise_xor(own_pair, move)
+        for at in range(3):
+            first = pl.multiple_of(at * width + pair * wide, 16)
+            place = 3 * step + at
+            fetches.append(
+                pltpu.make_async_copy(
+                    weight_ref.at[pl.ds(first, wide)], weight.at[place], sems.at[place]
+                )
+            )
+            fetches[-1].start()
     rows_fetch.wait()
     rows = rows_held[...]
     values = rows.astype(jnp.float32)
@@ -99,19 +111,22 @@
     if piggy:
         sums = jnp.dot(image_rows(own_ids[...], images), rows, preferred_element_type=jnp.float32)
         sums_ref[...] = split_in_two(sums, images)
-    for fetch in fetches:
-        fetch.wait()
-    parts = [
-        jnp.dot(weight[at], normed_ref[...], preferred_element_type=jnp.float32) for at in range(3)
-    ]
-    store_by_core(core, head_blocks(*parts, sums_ref if piggy else None, pair), same_ref, cross_ref)
-
-
-def near_kernel(piggy, normed_ref, sums_ref, weight_ref, *out_refs):
+    for step, move in enumerate(FIRST):
+        parts = []
+        for place in range(3 * step, 3 * step + 3):
+            fetches[place].wait()
+            parts.append(
+                jnp.dot(weight[place], normed_ref[...], preferred_element_type=jnp.float32)
+            )
+        blocks = head_blocks(*parts, sums_ref if piggy else None, jnp.bitwise_xor(own_pair, move))
+        store_by_core(core, blocks, *out_refs[2 * step : 2 * step + 2])
+
+
+def second_kernel(piggy, normed_ref, sums_ref, weight_ref, *out_refs):
     width = weight_ref.shape[0] // 3
     wide = 2 * width // HEADS
     own, core = place_in_group()
-    for step, move in enumerate((1, 2, 0)):
+    for step, move in enumerate(SECOND):
         pair = jnp.bitwise_xor(own, move)
         parts = []
         for at in range(3):
@@ -123,77 +138,93 @@
         store_by_core(core, blocks, *out_refs[2 * step : 2 * step + 2])
 
 
-def attend_kernel(images, piggy, halo, ids_ref, *rest):
-    got_refs, rest = rest[:HEADS], rest[HEADS:]
-    if halo:
-        left_ref, right_ref, *rest = rest
-    out_ref, keys, values, queries, attended, scores_a, scores_b, tops_a, tops_b, marks, starts = rest
-    count = got_refs[0].shape[1]
-    padded = attended.shape[0]
-    size = padded - SPARE
-    total_rows = HEADS * count
-    length = ids_ref.shape[1]
-    window = scores_a.shape[0]
-    tile = scores_a.shape[1]
-    tiles = total_rows // tile
+def find_starts(images, ids, starts):
+    for image in range(images + 1):
+        starts[image] = jnp.sum((ids < image).astype(jnp.int32))
+
+
+def write_marks(images, ids, marks):
     bits = max(1, (images - 1).bit_length())
-    ids = ids_ref[...]
-    for image in range(images):
-        starts[image] = jnp.sum((ids < image).astype(jnp.int32))
-
-    row = lax.broadcasted_iota(jnp.int32, (SPARE, length), 0)
+    row = lax.broadcasted_iota(jnp.int32, (SPARE, ids.shape[1]), 0)
     bit = jnp.bitwise_and(lax.shift_right_logical(jnp.broadcast_to(ids, row.shape), row >> 1), 1)
     odd = jnp.bitwise_and(row, 1)
     used = row < 2 * bits
     outside = jnp.logical_or(ids < 0, ids >= images)
     key_side = jnp.where(odd == 1, bit, 1 - bit).astype(jnp.float32)
     key_side = jnp.where(outside, 1.0, key_side)
-    key_marks, query_marks = marks.at[0], marks.at[1]
-    key_marks[...] = jnp.where(used, key_side * HIDDEN, 0.0)
-    query_marks[...] = jnp.where(used, jnp.where(odd == 1, 1 - bit, bit), 0).astype(jnp.float32)
-
-    key_at = size - SPARE
-    query_at = 2 * size
-    own = lax.rem(lax.axis_index("grp"), HEADS)
-    blank = jnp.zeros((LANES - padded, count), jnp.bfloat16)
-
-    def store_keys(here, ref):
-        block = ref[key_at : key_at + padded].astype(jnp.float32)
-        nothing = jnp.zeros((LANES - padded, block.shape[1]), jnp.float32)
-        full = jnp.concatenate([key_marks[:, here], block[SPARE:], nothing], axis=0)
-        keys[here, :] = full.astype(jnp.bfloat16).T
-        values[:, here] = ref[0:padded]
-
-    for by, ref in zip(ORDER, got_refs):
-        first = jnp.bitwise_xor(own, by) * count
-        here = pl.ds(pl.multiple_of(halo + first, LANES), count)
-        there = pl.ds(pl.multiple_of(first, LANES), count)
-        store_keys(here, ref)
-        edge = ref[query_at : query_at + 16].astype(jnp.float32)
-        edge = jnp.concatenate([query_marks[:, here], edge[SPARE:]], axis=0)
-        queries[0:16, there] = edge.astype(jnp.bfloat16)
-        queries[16:padded, there] = ref[query_at + 16 : query_at + padded]
-        queries[padded:, there] = blank
-    if halo:
-        store_keys(slice(0, halo), left_ref)
-        store_keys(slice(length - halo, length), right_ref)
-
-    def image_at(position):
-        found = jnp.int32(0)
-        for image in range(1, images):
-            found += (starts[image] <= position).astype(jnp.int32)
-        return found
+    marks[0] = jnp.where(used, key_side * HIDDEN, 0.0)
+    marks[1] = jnp.where(used, jnp.where(odd == 1, 1 - bit, bit), 0).astype(jnp.float32)
+
+
+def store_keys(marked, block_ref, keys, values, here):
+    padded = values.shape[0]
+    key_at = padded - 2 * SPARE
+    block = block_ref[key_at : key_at + padded].astype(jnp.float32)
+    nothing = jnp.zeros((LANES - padded, block.shape[1]), jnp.float32)
+    full = jnp.concatenate([marked, block[SPARE:], nothing], axis=0)
+    keys[here, :] = full.astype(jnp.bfloat16).T
+    values[:, here] = block_ref[0:padded]
+
+
+def store_queries(marked, block_ref, queries, padded, there):
+    query_at = 2 * (padded - SPARE)
+    edge = block_ref[query_at : query_at + 16].astype(jnp.float32)
+    edge = jnp.concatenate([marked, edge[SPARE:]], axis=0)
+    queries[0:16, there] = edge.astype(jnp.bfloat16)
+    queries[16:padded, there] = block_ref[query_at + 16 : query_at + padded]
+    queries[padded:, there] = jnp.zeros((LANES - padded, block_ref.shape[1]), jnp.bfloat16)
+
+
+def spare_sums(refs, padded):
+    query_at = 2 * (padded - SPARE)
+    parts = [ref[query_at : query_at + 16].astype(jnp.float32)[0:SPARE, 0 : 2 * LANES] for ref in refs]
+    return sum(parts[1:], parts[0])
+
+
+def image_at(images, starts, position):
+    found = jnp.int32(0)
+    for image in range(1, images):
+        found += (starts[image] <= position).astype(jnp.int32)
+    return found
+
+
+def near_images(images, starts, begin, end):
+    first = image_at(images, starts, begin)
+    first += (starts[first] < begin).astype(jnp.int32)
+    last = image_at(images, starts, end - 1)
+    last -= (starts[last + 1] > end).astype(jnp.int32)
+    return first, last
+
+
+def attend_images(images, ids_ref, keys, values, queries, attended, work, starts, bases, low, high, skipped):
+    scores_a, scores_b, tops_a, tops_b = work
+    key_base, query_base = bases
+    window, tile = scores_a.shape
+    size = attended.shape[0] - SPARE
+    held = queries.shape[1]
+    tiles = held // tile
+
+    def bounds(image):
+        first = lax.div(jnp.maximum(starts[image] - query_base, 0), tile)
+        last = lax.div(jnp.minimum(starts[image + 1] - query_base, held) - 1, tile)
+        return jnp.minimum(first, tiles - 1), last
+
+    def after(image):
+        later = image + 1
+        if skipped is not None:
+            jump = jnp.logical_and(later == skipped[0], skipped[0] <= skipped[1])
+            later = jnp.where(jump, skipped[1] + 1, later)
+        return jnp.clip(later, 0, images - 1)
 
     def following(state):
         at, image = state
-        more = image < image_at(halo + at * tile + tile - 1)
-        later = jnp.minimum(at + 1, tiles - 1)
-        first = jnp.maximum(image_at(halo + later * tile), jnp.where(later == at, image, 0))
-        return jnp.where(more, at, later), jnp.where(more, image + 1, first)
+        more = at < bounds(image)[1]
+        later = after(image)
+        return jnp.where(more, at + 1, bounds(later)[0]), jnp.where(more, image, later)
 
     def window_of(image):
-        begin = jnp.minimum(starts[image] // LANES * LANES, length - window)
-        return pl.ds(pl.multiple_of(begin, LANES), window)
+        begin = lax.div(jnp.maximum(starts[image] - key_base, 0), LANES) * LANES
+        return pl.ds(pl.multiple_of(jnp.minimum(begin, keys.shape[0] - window), LANES), window)
 
     def score(state, scores, tops):
         at, image = state
@@ -205,7 +236,7 @@
     def weigh(state, scores, tops):
         at, image = state
         first = pl.multiple_of(at * tile, tile)
-        labels = ids_ref[:, pl.ds(pl.multiple_of(halo + first, LANES), tile)]
+        labels = ids_ref[:, pl.ds(pl.multiple_of(query_base + first, LANES), tile)]
         probs = jnp.exp2((scores[...] - tops[...]) * (size ** (-0.5) * math.log2(math.e)))
         share = 1.0 / jnp.sum(probs, axis=0, keepdims=True)
         weighted = jnp.dot(
@@ -214,11 +245,13 @@
         place = (slice(None), pl.ds(first, tile))
         attended[place] = jnp.where(labels == image, weighted * share, attended[place])
 
-    pairs = jnp.int32(tiles)
-    for image in range(1, images):
-        offset = starts[image] - halo
-        inside = jnp.logical_and(offset > 0, offset < total_rows)
-        pairs += jnp.logical_and(inside, lax.rem(offset, tile) != 0).astype(jnp.int32)
+    pairs = jnp.int32(0)
+    for image in range(images):
+        first, last = bounds(image)
+        wanted = jnp.logical_and(low <= image, image <= high)
+        if skipped is not None:
+            wanted = jnp.logical_and(wanted, jnp.logical_or(image < skipped[0], image > skipped[1]))
+        pairs += jnp.where(wanted, last - first + 1, 0)
 
     def two_pairs(_, state):
         second = following(state)
@@ -229,15 +262,80 @@
         weigh(second, scores_b, tops_b)
         return third
 
-    begun = (jnp.int32(0), image_at(halo))
+    begin = after(low - 1)
+    begun = (bounds(begin)[0], begin)
     score(begun, scores_a, tops_a)
-    last = lax.fori_loop(0, pairs // 2, two_pairs, begun)
+    last_state = lax.fori_loop(0, lax.div(pairs, 2), two_pairs, begun)
 
     @pl.when(lax.rem(pairs, 2) == 1)
     def _():
-        weigh(last, scores_a, tops_a)
-
-    odd_head = lax.rem(lax.axis_index("grp"), 2) == 1
+        weigh(last_state, scores_a, tops_a)
+
+
+def early_kernel(images, halo, ids_ref, *rest):
+    got_refs, rest = rest[: len(EARLY)], rest[len(EARLY) :]
+    keys, values, queries, attended, sums, *work, marks, starts = rest
+    count = got_refs[0].shape[1]
+    padded = attended.shape[0]
+    ids = ids_ref[...]
+    find_starts(images, ids, starts)
+    write_marks(images, ids, marks)
+    own = lax.rem(lax.axis_index("grp"), HEADS)
+    half = lax.div(own, len(EARLY)) * (len(EARLY) * count)
+    for by, ref in zip(EARLY, got_refs):
+        first = jnp.bitwise_xor(own, by) * count
+        marked = pl.ds(pl.multiple_of(halo + first, LANES), count)
+        here = pl.ds(pl.multiple_of(first - half, LANES), count)
+        store_keys(marks[0, :, marked], ref, keys, values, here)
+        store_queries(marks[1, :, marked], ref, queries, padded, here)
+    sums[...] = spare_sums(got_refs, padded)
+    base = halo + half
+    low, high = near_images(images, starts, base, base + len(EARLY) * count)
+    attend_images(
+        images, ids_ref, keys, values, queries, attended, work, starts, (base, base), low, high, None
+    )
+
+
+def late_kernel(images, piggy, halo, ids_ref, *rest):
+    near_keys, near_values, near_queries, near_attended, near_sums, *rest = rest
+    got_refs, rest = rest[: len(LATE)], rest[len(LATE) :]
+    if halo:
+        left_ref, right_ref, *rest = rest
+    out_ref, keys, values, queries, attended, *work, marks, starts = rest
+    count = got_refs[0].shape[1]
+    padded = attended.shape[0]
+    size = padded - SPARE
+    total_rows = HEADS * count
+    length = ids_ref.shape[1]
+    ids = ids_ref[...]
+    find_starts(images, ids, starts)
+    write_marks(images, ids, marks)
+
+    own = lax.rem(lax.axis_index("grp"), HEADS)
+    half = lax.div(own, len(EARLY)) * (len(EARLY) * count)
+    near = pl.ds(pl.multiple_of(half, LANES), len(EARLY) * count)
+    near_here = pl.ds(pl.multiple_of(halo + half, LANES), len(EARLY) * count)
+    keys[near_here, :] = near_keys[...]
+    values[:, near_here] = near_values[...]
+    queries[:, near] = near_queries[...]
+    attended[:, near] = near_attended[...]
+    for by, ref in zip(LATE, got_refs):
+        first = jnp.bitwise_xor(own, by) * count
+        here = pl.ds(pl.multiple_of(halo + first, LANES), count)
+        there = pl.ds(pl.multiple_of(first, LANES), count)
+        store_keys(marks[0, :, here], ref, keys, values, here)
+        store_queries(marks[1, :, here], ref, queries, padded, there)
+    if halo:
+        for ref, here in ((left_ref, slice(0, halo)), (right_ref, slice(length - halo, length))):
+            store_keys(marks[0, :, here], ref, keys, values, here)
+    done = near_images(images, starts, halo + half, halo + half + len(EARLY) * count)
+    low = image_at(images, starts, halo)
+    high = image_at(images, starts, halo + total_rows - 1)
+    attend_images(
+        images, ids_ref, keys, values, queries, attended, work, starts, (0, halo), low, high, done
+    )
+
+    odd_head = lax.rem(own, 2) == 1
     mine = ids[:, halo : halo + total_rows]
 
     def placed(block, spare):
@@ -252,9 +350,7 @@
             image_rows(mine, images), flat, (((1,), (1,)), ((), ())), preferred_element_type=jnp.float32
         )
         pooled = split_in_two(pooled, images)
-        sums = jnp.zeros((SPARE, 2 * LANES), jnp.float32)
-        for ref in got_refs:
-            sums += ref[query_at : query_at + 16].astype(jnp.float32)[0:SPARE, 0 : 2 * LANES]
+        sums = near_sums[...] + spare_sums(got_refs, padded)
         sums = split_in_two(sums + pltpu.roll(sums, images, axis=0), images)
         spare = jnp.concatenate(
             [pooled, jnp.zeros((SPARE, LANES - padded), jnp.float32), sums], axis=1
@@ -401,35 +497,36 @@
     hbm = pl.BlockSpec(memory_space=pltpu.HBM)
     turned_weight = qkv_weight.T
     normed, sums, *sent = call(
-        functools.partial(far_kernel, images, piggy),
-        (shape((depth, count), bf16), shape((SPARE, depth), f32), block, block),
+        functools.partial(first_kernel, images, piggy),
+        (shape((depth, count), bf16), shape((SPARE, depth), f32)) + (block,) * (2 * len(FIRST)),
         [
             pltpu.VMEM((1, count), jnp.int32),
             pltpu.VMEM((count, depth), bf16),
-            pltpu.VMEM((3, 2 * size, depth), bf16),
+            pltpu.VMEM((3 * len(FIRST), 2 * size, depth), bf16),
             pltpu.SemaphoreType.DMA,
             pltpu.SemaphoreType.DMA,
-            pltpu.SemaphoreType.DMA((3,)),
+            pltpu.SemaphoreType.DMA((3 * len(FIRST),)),
         ],
         [hbm] * 3,
-        2 * count * depth * 6 * size,
+        2 * count * depth * 6 * size * len(FIRST),
     )(in_hbm(segment_ids), in_hbm(rows), in_hbm(turned_weight))
     sent += call(
-        functools.partial(near_kernel, piggy),
-        (block,) * 6,
+        functools.partial(second_kernel, piggy),
+        (block,) * (2 * len(SECOND)),
         [],
         in_vmem(3),
-        2 * count * depth * 18 * size,
+        2 * count * depth * 6 * size * len(SECOND),
     )(normed, sums, turned_weight)
-    sent = dict(zip((6, 7, 2, 3, 4, 5, 0, 1), sent))
-    got = []
-    for by in ORDER:
-        pairs = [(i, i ^ by) for i in range(group_size)]
-        got.append(moved(sent[by], "grp", pairs) if by else sent[by])
+    sent = dict(zip([2 * move + cross for move in FIRST + SECOND for cross in range(2)], sent))
+    got = {0: sent[0]}
+    for by in NEAR + FAR:
+        got[by] = moved(sent[by], "grp", [(i, i ^ by) for i in range(group_size)])
+    got.update(zip(NEAR, lax.optimization_barrier(tuple(got[by] for by in NEAR))))
 
     length = HEADS * count
     halo = 0
-    operands = [segment_ids, *got]
+    near_ids = segment_ids
+    halos = []
     if parts > 1:
         halo = rounded_up(MAXP - 1, LANES)
         part = lax.axis_index("grp") // HEADS
@@ -443,31 +540,49 @@
         )
         near_ids = lax.dynamic_slice_in_dim(whole_ids, part * length, length + 2 * halo, axis=1)
         order = jnp.bitwise_xor(lax.axis_index("grp") % HEADS, jnp.arange(HEADS))
-        flat = jnp.stack([got[ORDER.index(by)] for by in range(HEADS)])[order][:, : 2 * size].transpose(1, 0, 2).reshape(2 * size, length)
+        flat = jnp.stack([got[by] for by in range(HEADS)])[order][:, : 2 * size].transpose(1, 0, 2).reshape(2 * size, length)
         flat = jnp.concatenate([flat, jnp.zeros((16, length), bf16)], axis=0)
         ahead = [(i, i + HEADS) for i in range(group_size - HEADS)]
         back = [(i + HEADS, i) for i in range(group_size - HEADS)]
         left = moved(flat[:, length - halo :], "grp", ahead)
         right = moved(flat[:, :halo], "grp", back)
-        operands = [near_ids, *got, left, right]
+        halos = [left, right]
     reach = length + 2 * halo
     window = min(rounded_up(MAXP + LANES - 1, LANES), reach)
     tile = 2 * LANES
+    work = [
+        pltpu.VMEM((window, tile), f32),
+        pltpu.VMEM((window, tile), f32),
+        pltpu.VMEM((1, tile), f32),
+        pltpu.VMEM((1, tile), f32),
+        pltpu.VMEM((2, SPARE, reach), f32),
+        pltpu.SMEM((images + 1,), jnp.int32),
+    ]
+    half = len(EARLY) * count
+    early = call(
+        functools.partial(early_kernel, images, halo),
+        (
+            shape((half, LANES), bf16),
+            shape((padded, half), bf16),
+            shape((LANES, half), bf16),
+            shape((padded, half), f32),
+            shape((SPARE, 2 * LANES), f32),
+        ),
+        work,
+        in_vmem(1 + len(EARLY)),
+        4 * size * half * MAXP,
+    )(near_ids, *[got[by] for by in EARLY])
+    operands = [near_ids, *early, *[got[by] for by in LATE], *halos]
     answers = call(
-        functools.partial(attend_kernel, images, piggy, halo),
+        functools.partial(late_kernel, images, piggy, halo),
         shape((HEADS, padded, count), bf16),
         [
             pltpu.VMEM((reach, LANES), bf16),
             pltpu.VMEM((padded, reach), bf16),
             pltpu.VMEM((LANES, length), bf16),
             pltpu.VMEM((padded, length), f32),
-            pltpu.VMEM((window, tile), f32),
-            pltpu.VMEM((window, tile), f32),
-            pltpu.VMEM((1, tile), f32),
-            pltpu.VMEM((1, tile), f32),
-            pltpu.VMEM((2, SPARE, reach), f32),
-            pltpu.SMEM((images,), jnp.int32),
-        ],
+        ]
+        + work,
         in_vmem(len(operands)),
         4 * size * length * MAXP,
     )(*operands)

time: 47.5 us -> 48.9 us (1.029)
  Pallas kernels: 16.2 us -> 17.8 us
    pallas_call x3 -> x4, Pallas kernels: 13.9 us -> 15.5 us  [the longest x1 5.58 us: local(): call(functools.partial(late_kernel, images, piggy, halo), shape((HEADS, p...]
    ppermute x10, waiting for transfers between devices: 13.6 us -> 12.7 us  [moved(): return lax.ppermute(value, axis, pairs)]
    ppermute x10, starting transfers between devices: 12.9 us -> 13.4 us  [moved(): return lax.ppermute(value, axis, pairs)]
    all_to_all x1, waiting for transfers between devices: 0.01 us -> 0.54 us  [exchanged(): lax.all_to_all(blocks, 'grp', 0, 0, axis_index_groups=groups, tiled=True)]
  transfers between devices with their start and end apart: 11 -> 11, of which waited for: 7 -> 5; matrix products, arithmetic and copies ran while one was open for 0% -> 0% of each run, Pallas kernels for 5% -> 11%
where the time goes in v9:
time: 48.9 us; the launch traced here: 48.7 us
  Pallas kernels  17.8 us (36%)
  starting transfers between devices  16.9 us (35%)
  waiting for transfers between devices  13.2 us (27%)
  between operations  0.74 us (2%)
    ppermute x10, starting transfers between devices, moved(): return lax.ppermute(value, axis, pairs)  13.4 us
    ppermute x10, waiting for transfers between devices, moved(): return lax.ppermute(value, axis, pairs)  12.7 us
    pallas_call x1, Pallas kernels, local(): call(functools.partial(late_kernel, images, piggy, halo), shape((HEADS, p...  5.58 us
    pallas_call x1, Pallas kernels, local(): call(functools.partial(first_kernel, images, piggy), (shape((depth, count...  4.59 us
    pallas_call x1, Pallas kernels, local(): call(functools.partial(early_kernel, images, halo), (shape((half, LANES),...  3.8 us
    all_to_all x1, starting transfers between devices, exchanged(): lax.all_to_all(blocks, 'grp', 0, 0, axis_index_groups=groups, tiled=True)  3.48 us
    pallas_call x1, Pallas kernels, local(): call(functools.partial(finish_kernel, images), (shape((count, depth), bf1...  2.29 us
    pallas_call x1, Pallas kernels, local(): call(functools.partial(second_kernel, piggy), (block,) * (2 * len(SECOND)...  1.56 us
  transfers between devices with their start and end apart: 11, of which 5 were waited for; matrix products, arithmetic and copies ran while one was open for 0% of the time, Pallas kernels for 11%

profile of v9, /device:TPU:0, one launch (start us, length us, event | category | flops | bytes accessed | tf_op | source)
XLA Modules:
  0.0 48.7 jit_solution(11509469717611507276)
XLA Ops:
  0.6 0.0 copy-start
  0.6 0.0 copy-start.3
  0.6 4.6 %shard_map.68 = (bf16[1152,384]{1,0:T(8,128)(2,1)S(1)}, f32[8,1152]{1,0:T(8,128)S(1)}, bf16[224,384]{1,0:T(8,128)(2,1)S(1)}, bf16[224,384]{1,0:T(8,128)(2,1)S(1)...) custom-call(s32[1,3072]{1,0:T(1,128)} %ids_ref.5, bf16[384,1152]{1,0:T(8,128)(2,1)} %bitcast.6, ...), custom_call_target="tpu_custom_call" | custom-call | flops 764411904 | bytes 8388608 | tf_op jit(solution)/shard_map/pallas_call | solution.py:499
  5.2 3.0 %collective-permute-start = (bf16[224,384]{1,0:T(8,128)(2,1)S(1)}, bf16[224,384]{1,0:T(8,128)(2,1)S(1)}, u32[]{:S(2)}, u32[]{:S(2)}) collective-permute-start(bf16[224,384]{1,0:T(8,128)(2,1)S(1)} %get-tuple-element.25), channel_id=1, source_target_pairs={{0,8},{4,12},{8,0},{12,4},{16,24},{20,28},{24,16},{28,20},{1,9},{5... | collective-permute-start | bytes 516104 | tf_op jit(solution)/shard_map/ppermute | solution.py:469
  8.3 1.5 %collective-permute-start.1 = (bf16[224,384]{1,0:T(8,128)(2,1)S(1)}, bf16[224,384]{1,0:T(8,128)(2,1)S(1)}, u32[]{:S(2)}, u32[]{:S(2)}) collective-permute-start(bf16[224,384]{1,0:T(8,128)(2,1)S(1)} %get-tuple-element.26), channel_id=1, source_target_pairs={{0,16},{4,20},{8,24},{12,28},{16,0},{20,4},{24,8},{28,12},{1,17},{... | collective-permute-start | bytes 516104 | tf_op jit(solution)/shard_map/ppermute | solution.py:469
  9.8 0.0 collective-permute-start.2
  9.8 0.3 collective-permute-start.3
  10.1 0.0 copy-done
  10.1 1.6 %shard_map.69 = (bf16[224,384]{1,0:T(8,128)(2,1)S(1)}, bf16[224,384]{1,0:T(8,128)(2,1)S(1)}, bf16[224,384]{1,0:T(8,128)(2,1)S(1)}, bf16[224,384]{1,0:T(8,128)(2,1)S(1)}) custom-call(bf16[1152,384]{1,0:T(8,128)(2,1)S(1)} %get-tuple-element.29.normed_ref, f32[8,1152]{1,0:T(8,128)S(1)} %get-tuple-element.30.sums_ref, bf16[1728,1152]{1,0:T(8,128)(2,1)S(1)} %bitcast.5), custom_call_target="tpu_custom_call" | custom-call | flops 764411904 | bytes 8388608 | tf_op jit(solution)/shard_map/pallas_call | solution.py:513
  11.7 0.0 copy-start.4
  11.7 0.0 copy-start.1
  11.7 0.0 copy-start.2
  11.7 0.4 collective-permute-start.4
  12.1 0.8 %collective-permute-done.rest_0_ = bf16[224,384]{1,0:T(8,128)(2,1)S(1)} collective-permute-done((bf16[224,384]{1,0:T(8,128)(2,1)S(1)}, bf16[224,384]{1,0:T(8,128)(2,1)S(1)}, u32[]{:S(2)}, u32[]{:S(2)}) %collective-permute-start) | collective-permute-done | bytes 172064 | tf_op jit(solution)/shard_map/ppermute | solution.py:469
  12.9 3.6 %collective-permute-start.5 = (bf16[224,384]{1,0:T(8,128)(2,1)S(1)}, bf16[224,384]{1,0:T(8,128)(2,1)S(1)}, u32[]{:S(2)}, u32[]{:S(2)}) collective-permute-start(bf16[224,384]{1,0:T(8,128)(2,1)S(1)} %get-tuple-element.43), channel_id=1, source_target_pairs={{0,24},{4,28},{8,16},{12,20},{16,8},{20,12},{24,0},{28,4},{1,25},{... | collective-permute-start | bytes 516104 | tf_op jit(solution)/shard_map/ppermute | solution.py:469
  16.5 0.0 collective-permute-done.1.rest_5_
  16.5 0.0 collective-permute-start.6
  16.5 0.0 collective-permute-done.2.rest_1_
  16.5 7.7 %collective-permute-done.3.rest_6_ = bf16[224,384]{1,0:T(8,128)(2,1)S(1)} collective-permute-done((bf16[224,384]{1,0:T(8,128)(2,1)S(1)}, bf16[224,384]{1,0:T(8,128)(2,1)S(1)}, u32[]{:S(2)}, u32[]{:S(2)}) %collective-permute-start.3) | collective-permute-done | bytes 172064 | tf_op jit(solution)/shard_map/ppermute | solution.py:469
  24.2 0.0 collective-permute-done.4.rest_2_
  24.2 0.0 copy-done.3
  24.2 3.8 %shard_map.70 = (bf16[1536,128]{1,0:T(8,128)(2,1)S(1)}, bf16[80,1536]{1,0:T(8,128)(2,1)S(1)}, bf16[128,1536]{1,0:T(8,128)(2,1)S(1)}, f32[80,1536]{1,0:T(8,128)S(1)}, f32[8,256]{1,0:T(8,128)S(1)}) custom-call(s32[1,3072]{1,0:T(1,128)S(1)} %copy-done.3, bf16[224,384]{1,0:T(8,128)(2,1)S(1)} %collective-permute-done.rest_0_, ...), custom_call_target="tpu_custom_call" | custom-call | flops 452984832 | bytes 8388608 | tf_op jit(solution)/shard_map/pallas_call | solution.py:562
  28.0 0.0 collective-permute-done.5.rest_7_
  28.0 0.0 collective-permute-done.6.rest_8_
  28.0 5.6 %shard_map.71 = bf16[8,80,384]{2,1,0:T(8,128)(2,1)} custom-call(s32[1,3072]{1,0:T(1,128)S(1)} %copy-done.3, bf16[1536,128]{1,0:T(8,128)(2,1)S(1)} %get-tuple-element.36.rest_0_, bf16[80,1536]{1,0:T(8,128)(2,1)S(1)} %get-tuple-element.37.rest_1_, bf16[128,1536]{1,0:T(8,128)(2,1)S(1)} %get-tuple-element.38.rest_2_, f32[80,1536]{1,0:T(8,128)S(1)} %get-tuple-element.39.rest_3_, ...), custom_call_target="tpu_custom_call" | custom-call | flops 905969664 | bytes 8388608 | tf_op jit(solution)/shard_map/pallas_call | solution.py:576
  33.6 3.5 %all-to-all-start = ((bf16[8,80,384]{2,1,0:T(8,128)(2,1)}), bf16[8,80,384]{2,1,0:T(8,128)(2,1)S(1)}, u32[]{:S(2)}, u32[]{:S(2)}) async-start(bf16[8,80,384]{2,1,0:T(8,128)(2,1)} %shard_map.71), calls=%async_computation | async-start | bytes 983040 | tf_op jit(solution)/shard_map/all_to_all | solution.py:479
  37.1 0.0 copy-done.4
  37.1 3.3 %collective-permute-start.9 = (bf16[4,1152]{1,0:T(4,128)(2,1)S(1)}, bf16[4,1152]{1,0:T(4,128)(2,1)S(1)}, u32[]{:S(2)}, u32[]{:S(2)}) collective-permute-start(bf16[4,1152]{1,0:T(4,128)(2,1)S(1)} %copy-done.4), channel_id=1, source_target_pairs={{0,3},{1,0},{2,1},{3,2},{4,7},{5,4},{6,5},{7,6},{8,11},{9,8},{10,9... | collective-permute-start | bytes 27656 | tf_op jit(solution)/shard_map/ppermute | solution.py:469
  40.4 0.0 collective-permute-start.8
  40.4 1.3 %collective-permute-start.7 = (bf16[4,1152]{1,0:T(4,128)(2,1)S(1)}, bf16[4,1152]{1,0:T(4,128)(2,1)S(1)}, u32[]{:S(2)}, u32[]{:S(2)}) collective-permute-start(bf16[4,1152]{1,0:T(4,128)(2,1)S(1)} %copy-done.4), channel_id=1, source_target_pairs={{0,1},{1,2},{2,3},{3,0},{4,5},{5,6},{6,7},{7,4},{8,9},{9,10},{10,1... | collective-permute-start | bytes 27656 | tf_op jit(solution)/shard_map/ppermute | solution.py:469
  41.7 0.0 collective-permute-done.9
  41.8 3.2 %collective-permute-done.8 = bf16[4,1152]{1,0:T(4,128)(2,1)S(1)} collective-permute-done((bf16[4,1152]{1,0:T(4,128)(2,1)S(1)}, bf16[4,1152]{1,0:T(4,128)(2,1)S(1)}, u32[]{:S(2)}, u32[]{:S(2)}) %collective-permute-start.8) | collective-permute-done | bytes 9248 | tf_op jit(solution)/shard_map/ppermute | solution.py:469
  45.0 0.9 %collective-permute-done.7 = bf16[4,1152]{1,0:T(4,128)(2,1)S(1)} collective-permute-done((bf16[4,1152]{1,0:T(4,128)(2,1)S(1)}, bf16[4,1152]{1,0:T(4,128)(2,1)S(1)}, u32[]{:S(2)}, u32[]{:S(2)}) %collective-permute-start.7) | collective-permute-done | bytes 9248 | tf_op jit(solution)/shard_map/ppermute | solution.py:469
  45.9 0.5 %all-to-all-done.got_ref = bf16[8,80,384]{2,1,0:T(8,128)(2,1)S(1)} async-done(((bf16[8,80,384]{2,1,0:T(8,128)(2,1)}), bf16[8,80,384]{2,1,0:T(8,128)(2,1)S(1)}, u32[]{:S(2)}, u32[]{:S(2)}) %all-to-all-start) | async-done | bytes 491552 | tf_op jit(solution)/shard_map/all_to_all | solution.py:479
  46.4 0.0 copy-done.1
  46.4 0.0 copy-done.2
  46.4 2.3 %shard_map.72 = (bf16[384,1152]{1,0:T(8,128)(2,1)}, f32[1,4]{1,0:T(1,128)}) custom-call(bf16[384,1152]{1,0:T(8,128)(2,1)S(1)} %bitcast.7, bf16[8,80,384]{2,1,0:T(8,128)(2,1)S(1)} %all-to-all-done.got_ref, bf16[576,1152]{1,0:T(8,128)(2,1)S(1)} %copy-done.2, bf16[16,1152]{1,0:T(8,128)(2,1)S(1)} %pad_maximum_fusion.text_ref), custom_call_target="tpu_custom_call" | custom-call | flops 509607936 | bytes 8388608 | tf_op jit(solution)/shard_map/pallas_call | solution.py:602
  (1 shorter events, 0.0 us)
Async XLA Ops:
  0.6 9.5 %copy-start = (bf16[1152,1728]{0,1:T(8,128)(2,1)S(1)}, bf16[1152,1728]{0,1:T(8,128)(2,1)}, u32[]{:S(2)}) copy-start(bf16[1152,1728]{0,1:T(8,128)(2,1)} %param.7) | copy-start | bytes 11943940
  0.6 23.6 %copy-start.3 = (s32[1,3072]{1,0:T(1,128)S(1)}, s32[1,3072]{1,0:T(1,128)}, u32[]{:S(2)}) copy-start(s32[1,3072]{1,0:T(1,128)} %ids_ref.5) | copy-start | bytes 36868
  5.2 7.7 %collective-permute-start = (bf16[224,384]{1,0:T(8,128)(2,1)S(1)}, bf16[224,384]{1,0:T(8,128)(2,1)S(1)}, u32[]{:S(2)}, u32[]{:S(2)}) collective-permute-start(bf16[224,384]{1,0:T(8,128)(2,1)S(1)} %get-tuple-element.25), channel_id=1, source_target_pairs={{0,8},{4,12},{8,0},{12,4},{16,24},{20,28},{24,16},{28,20},{1,9},{5... | collective-permute-start | bytes 516104 | tf_op jit(solution)/shard_map/ppermute | solution.py:469
  8.3 8.2 %collective-permute-start.1 = (bf16[224,384]{1,0:T(8,128)(2,1)S(1)}, bf16[224,384]{1,0:T(8,128)(2,1)S(1)}, u32[]{:S(2)}, u32[]{:S(2)}) collective-permute-start(bf16[224,384]{1,0:T(8,128)(2,1)S(1)} %get-tuple-element.26), channel_id=1, source_target_pairs={{0,16},{4,20},{8,24},{12,28},{16,0},{20,4},{24,8},{28,12},{1,17},{... | collective-permute-start | bytes 516104 | tf_op jit(solution)/shard_map/ppermute | solution.py:469
  9.8 6.7 %collective-permute-start.2 = (bf16[224,384]{1,0:T(8,128)(2,1)S(1)}, bf16[224,384]{1,0:T(8,128)(2,1)S(1)}, u32[]{:S(2)}, u32[]{:S(2)}) collective-permute-start(bf16[224,384]{1,0:T(8,128)(2,1)S(1)} %get-tuple-element.27), channel_id=1, source_target_pairs={{0,12},{4,8},{8,4},{12,0},{16,28},{20,24},{24,20},{28,16},{1,13},{... | collective-permute-start | bytes 516104 | tf_op jit(solution)/shard_map/ppermute | solution.py:469
  9.8 14.4 %collective-permute-start.3 = (bf16[224,384]{1,0:T(8,128)(2,1)S(1)}, bf16[224,384]{1,0:T(8,128)(2,1)S(1)}, u32[]{:S(2)}, u32[]{:S(2)}) collective-permute-start(bf16[224,384]{1,0:T(8,128)(2,1)S(1)} %get-tuple-element.28), channel_id=1, source_target_pairs={{0,20},{4,16},{8,28},{12,24},{16,4},{20,0},{24,12},{28,8},{1,21},{... | collective-permute-start | bytes 516104 | tf_op jit(solution)/shard_map/ppermute | solution.py:469
  11.7 25.5 %copy-start.4 = (bf16[4,1152]{1,0:T(4,128)(2,1)S(1)}, bf16[4,1152]{1,0:T(4,128)(2,1)}, u32[]{:S(2)}) copy-start(bf16[4,1152]{1,0:T(4,128)(2,1)} %param.9) | copy-start | bytes 27652
  11.7 34.8 %copy-start.1 = (bf16[1,384,1152]{2,1,0:T(8,128)(2,1)S(1)}, bf16[1,384,1152]{2,1,0:T(8,128)(2,1)}, u32[]{:S(2)}) copy-start(bf16[1,384,1152]{2,1,0:T(8,128)(2,1)} %param.5) | copy-start | bytes 2654212
  11.7 34.8 %copy-start.2 = (bf16[576,1152]{1,0:T(8,128)(2,1)S(1)}, bf16[576,1152]{1,0:T(8,128)(2,1)}, u32[]{:S(2)}) copy-start(bf16[576,1152]{1,0:T(8,128)(2,1)} %out_weight_ref.1) | copy-start | bytes 3981316
  11.7 12.5 %collective-permute-start.4 = (bf16[224,384]{1,0:T(8,128)(2,1)S(1)}, bf16[224,384]{1,0:T(8,128)(2,1)S(1)}, u32[]{:S(2)}, u32[]{:S(2)}) collective-permute-start(bf16[224,384]{1,0:T(8,128)(2,1)S(1)} %get-tuple-element.31), channel_id=1, source_target_pairs={{0,4},{4,0},{8,12},{12,8},{16,20},{20,16},{24,28},{28,24},{1,5},{5... | collective-permute-start | bytes 516104 | tf_op jit(solution)/shard_map/ppermute | solution.py:469
  12.9 15.1 %collective-permute-start.5 = (bf16[224,384]{1,0:T(8,128)(2,1)S(1)}, bf16[224,384]{1,0:T(8,128)(2,1)S(1)}, u32[]{:S(2)}, u32[]{:S(2)}) collective-permute-start(bf16[224,384]{1,0:T(8,128)(2,1)S(1)} %get-tuple-element.43), channel_id=1, source_target_pairs={{0,24},{4,28},{8,16},{12,20},{16,8},{20,12},{24,0},{28,4},{1,25},{... | collective-permute-start | bytes 516104 | tf_op jit(solution)/shard_map/ppermute | solution.py:469
  16.5 11.5 %collective-permute-start.6 = (bf16[224,384]{1,0:T(8,128)(2,1)S(1)}, bf16[224,384]{1,0:T(8,128)(2,1)S(1)}, u32[]{:S(2)}, u32[]{:S(2)}) collective-permute-start(bf16[224,384]{1,0:T(8,128)(2,1)S(1)} %get-tuple-element.44), channel_id=1, source_target_pairs={{0,28},{4,24},{8,20},{12,16},{16,12},{20,8},{24,4},{28,0},{1,29},{... | collective-permute-start | bytes 516104 | tf_op jit(solution)/shard_map/ppermute | solution.py:469
  33.6 12.8 %all-to-all-start = ((bf16[8,80,384]{2,1,0:T(8,128)(2,1)}), bf16[8,80,384]{2,1,0:T(8,128)(2,1)S(1)}, u32[]{:S(2)}, u32[]{:S(2)}) async-start(bf16[8,80,384]{2,1,0:T(8,128)(2,1)} %shard_map.71), calls=%async_computation | async-start | bytes 983040 | tf_op jit(solution)/shard_map/all_to_all | solution.py:479
  37.1 4.7 %collective-permute-start.9 = (bf16[4,1152]{1,0:T(4,128)(2,1)S(1)}, bf16[4,1152]{1,0:T(4,128)(2,1)S(1)}, u32[]{:S(2)}, u32[]{:S(2)}) collective-permute-start(bf16[4,1152]{1,0:T(4,128)(2,1)S(1)} %copy-done.4), channel_id=1, source_target_pairs={{0,3},{1,0},{2,1},{3,2},{4,7},{5,4},{6,5},{7,6},{8,11},{9,8},{10,9... | collective-permute-start | bytes 27656 | tf_op jit(solution)/shard_map/ppermute | solution.py:469
  40.4 4.6 %collective-permute-start.8 = (bf16[4,1152]{1,0:T(4,128)(2,1)S(1)}, bf16[4,1152]{1,0:T(4,128)(2,1)S(1)}, u32[]{:S(2)}, u32[]{:S(2)}) collective-permute-start(bf16[4,1152]{1,0:T(4,128)(2,1)S(1)} %copy-done.4), channel_id=1, source_target_pairs={{0,2},{1,3},{2,0},{3,1},{4,6},{5,7},{6,4},{7,5},{8,10},{9,11},{10,... | collective-permute-start | bytes 27656 | tf_op jit(solution)/shard_map/ppermute | solution.py:469
  40.4 5.5 %collective-permute-start.7 = (bf16[4,1152]{1,0:T(4,128)(2,1)S(1)}, bf16[4,1152]{1,0:T(4,128)(2,1)S(1)}, u32[]{:S(2)}, u32[]{:S(2)}) collective-permute-start(bf16[4,1152]{1,0:T(4,128)(2,1)S(1)} %copy-done.4), channel_id=1, source_target_pairs={{0,1},{1,2},{2,3},{3,0},{4,5},{5,6},{6,7},{7,4},{8,9},{9,10},{10,1... | collective-permute-start | bytes 27656 | tf_op jit(solution)/shard_map/ppermute | solution.py:469

commit v10 on v8

--- a/solution.py
+++ b/solution.py
@@ -12,8 +12,14 @@
 MAXP = 1024
 LANES = 128
 SPARE = 8
+SIZE = 72
+PADDED = SIZE + SPARE
+KEY_AT = SIZE - SPARE
+QUERY_AT = 2 * SIZE
 HIDDEN = -1e30
 ORDER = (6, 7, 2, 4, 3, 5, 1, 0)
+EARLY = (6, 7, 1, 0)
+LATE = (2, 4, 3, 5)
 
 logit_scale = 30.0
 logit_bias = -5.0
@@ -123,77 +129,61 @@
         store_by_core(core, blocks, *out_refs[2 * step : 2 * step + 2])
 
 
-def attend_kernel(images, piggy, halo, ids_ref, *rest):
-    got_refs, rest = rest[:HEADS], rest[HEADS:]
-    if halo:
-        left_ref, right_ref, *rest = rest
-    out_ref, keys, values, queries, attended, scores_a, scores_b, tops_a, tops_b, marks, starts = rest
-    count = got_refs[0].shape[1]
-    padded = attended.shape[0]
-    size = padded - SPARE
-    total_rows = HEADS * count
-    length = ids_ref.shape[1]
-    window = scores_a.shape[0]
-    tile = scores_a.shape[1]
-    tiles = total_rows // tile
+def find_starts(images, ids, starts):
+    for image in range(images + 1):
+        starts[image] = jnp.sum((ids < image).astype(jnp.int32))
+
+
+def write_marks(images, ids, marks):
     bits = max(1, (images - 1).bit_length())
-    ids = ids_ref[...]
-    for image in range(images):
-        starts[image] = jnp.sum((ids < image).astype(jnp.int32))
-
-    row = lax.broadcasted_iota(jnp.int32, (SPARE, length), 0)
+    row = lax.broadcasted_iota(jnp.int32, (SPARE, ids.shape[1]), 0)
     bit = jnp.bitwise_and(lax.shift_right_logical(jnp.broadcast_to(ids, row.shape), row >> 1), 1)
     odd = jnp.bitwise_and(row, 1)
     used = row < 2 * bits
     outside = jnp.logical_or(ids < 0, ids >= images)
     key_side = jnp.where(odd == 1, bit, 1 - bit).astype(jnp.float32)
     key_side = jnp.where(outside, 1.0, key_side)
-    key_marks, query_marks = marks.at[0], marks.at[1]
-    key_marks[...] = jnp.where(used, key_side * HIDDEN, 0.0)
-    query_marks[...] = jnp.where(used, jnp.where(odd == 1, 1 - bit, bit), 0).astype(jnp.float32)
-
-    key_at = size - SPARE
-    query_at = 2 * size
-    own = lax.rem(lax.axis_index("grp"), HEADS)
-    blank = jnp.zeros((LANES - padded, count), jnp.bfloat16)
-
-    def store_keys(here, ref):
-        block = ref[key_at : key_at + padded].astype(jnp.float32)
-        nothing = jnp.zeros((LANES - padded, block.shape[1]), jnp.float32)
-        full = jnp.concatenate([key_marks[:, here], block[SPARE:], nothing], axis=0)
-        keys[here, :] = full.astype(jnp.bfloat16).T
-        values[:, here] = ref[0:padded]
-
-    for by, ref in zip(ORDER, got_refs):
-        first = jnp.bitwise_xor(own, by) * count
-        here = pl.ds(pl.multiple_of(halo + first, LANES), count)
-        there = pl.ds(pl.multiple_of(first, LANES), count)
-        store_keys(here, ref)
-        edge = ref[query_at : query_at + 16].astype(jnp.float32)
-        edge = jnp.concatenate([query_marks[:, here], edge[SPARE:]], axis=0)
-        queries[0:16, there] = edge.astype(jnp.bfloat16)
-        queries[16:padded, there] = ref[query_at + 16 : query_at + padded]
-        queries[padded:, there] = blank
-    if halo:
-        store_keys(slice(0, halo), left_ref)
-        store_keys(slice(length - halo, length), right_ref)
-
-    def image_at(position):
-        found = jnp.int32(0)
-        for image in range(1, images):
-            found += (starts[image] <= position).astype(jnp.int32)
-        return found
+    marks[0] = jnp.where(used, key_side * HIDDEN, 0.0)
+    marks[1] = jnp.where(used, jnp.where(odd == 1, 1 - bit, bit), 0).astype(jnp.float32)
+
+
+def spare_sums(refs):
+    parts = [ref[QUERY_AT : QUERY_AT + 16].astype(jnp.float32)[0:SPARE, 0 : 2 * LANES] for ref in refs]
+    return sum(parts[1:], parts[0])
+
+
+def image_at(images, starts, position):
+    found = jnp.int32(0)
+    for image in range(1, images):
+        found += (starts[image] <= position).astype(jnp.int32)
+    return found
+
+
+def attend_images(images, ids_ref, keys, values, queries, attended, work, starts, halo):
+    scores_a, scores_b, tops_a, tops_b = work
+    query_base = halo
+    window, tile = scores_a.shape
+    size = attended.shape[0] - SPARE
+    held = queries.shape[1]
+    tiles = held // tile
+
+    def bounds(image):
+        first = lax.div(jnp.maximum(starts[image] - query_base, 0), tile)
+        last = lax.div(jnp.minimum(starts[image + 1] - query_base, held) - 1, tile)
+        return jnp.minimum(first, tiles - 1), last
+
+    def after(image):
+        return jnp.minimum(image + 1, images - 1)
 
     def following(state):
         at, image = state
-        more = image < image_at(halo + at * tile + tile - 1)
-        later = jnp.minimum(at + 1, tiles - 1)
-        first = jnp.maximum(image_at(halo + later * tile), jnp.where(later == at, image, 0))
-        return jnp.where(more, at, later), jnp.where(more, image + 1, first)
+        more = at < bounds(image)[1]
+        later = after(image)
+        return jnp.where(more, at + 1, bounds(later)[0]), jnp.where(more, image, later)
 
     def window_of(image):
-        begin = jnp.minimum(starts[image] // LANES * LANES, length - window)
-        return pl.ds(pl.multiple_of(begin, LANES), window)
+        begin = lax.div(starts[image], LANES) * LANES
+        return pl.ds(pl.multiple_of(jnp.minimum(begin, keys.shape[0] - window), LANES), window)
 
     def score(state, scores, tops):
         at, image = state
@@ -205,20 +195,22 @@
     def weigh(state, scores, tops):
         at, image = state
         first = pl.multiple_of(at * tile, tile)
-        labels = ids_ref[:, pl.ds(pl.multiple_of(halo + first, LANES), tile)]
+        labels = ids_ref[:, pl.ds(pl.multiple_of(query_base + first, LANES), tile)]
         probs = jnp.exp2((scores[...] - tops[...]) * (size ** (-0.5) * math.log2(math.e)))
-        share = 1.0 / jnp.sum(probs, axis=0, keepdims=True)
         weighted = jnp.dot(
             values[:, window_of(image)], probs.astype(jnp.bfloat16), preferred_element_type=jnp.float32
         )
+        share = 1.0 / weighted[size : size + 1]
         place = (slice(None), pl.ds(first, tile))
         attended[place] = jnp.where(labels == image, weighted * share, attended[place])
 
-    pairs = jnp.int32(tiles)
-    for image in range(1, images):
-        offset = starts[image] - halo
-        inside = jnp.logical_and(offset > 0, offset < total_rows)
-        pairs += jnp.logical_and(inside, lax.rem(offset, tile) != 0).astype(jnp.int32)
+    low = image_at(images, starts, query_base)
+    high = image_at(images, starts, query_base + held - 1)
+    pairs = jnp.int32(0)
+    for image in range(images):
+        first, last = bounds(image)
+        wanted = jnp.logical_and(low <= image, image <= high)
+        pairs += jnp.where(wanted, last - first + 1, 0)
 
     def two_pairs(_, state):
         second = following(state)
@@ -229,15 +221,79 @@
         weigh(second, scores_b, tops_b)
         return third
 
-    begun = (jnp.int32(0), image_at(halo))
+    begun = (jnp.int32(0), low)
     score(begun, scores_a, tops_a)
-    last = lax.fori_loop(0, pairs // 2, two_pairs, begun)
+    last_state = lax.fori_loop(0, lax.div(pairs, 2), two_pairs, begun)
 
     @pl.when(lax.rem(pairs, 2) == 1)
     def _():
-        weigh(last, scores_a, tops_a)
-
-    odd_head = lax.rem(lax.axis_index("grp"), 2) == 1
+        weigh(last_state, scores_a, tops_a)
+
+
+def turned_keys(marked, block_ref):
+    block = block_ref[KEY_AT : KEY_AT + PADDED].astype(jnp.float32)
+    nothing = jnp.zeros((LANES - PADDED, block.shape[1]), jnp.float32)
+    full = jnp.concatenate([marked, block[SPARE:], nothing], axis=0)
+    return full.astype(jnp.bfloat16).T
+
+
+def store_queries(marked, block_ref, queries, there):
+    edge = block_ref[QUERY_AT : QUERY_AT + 16].astype(jnp.float32)
+    edge = jnp.concatenate([marked, edge[SPARE:]], axis=0)
+    queries[0:16, there] = edge.astype(jnp.bfloat16)
+    queries[16:PADDED, there] = block_ref[QUERY_AT + 16 : QUERY_AT + PADDED]
+    queries[PADDED:, there] = jnp.zeros((LANES - PADDED, block_ref.shape[1]), jnp.bfloat16)
+
+
+def store_values(block_ref, values, here):
+    edge = block_ref[PADDED - 16 : PADDED].astype(jnp.float32)
+    ones = jnp.ones((SPARE, edge.shape[1]), jnp.float32)
+    values[0 : PADDED - 16, here] = block_ref[0 : PADDED - 16]
+    values[PADDED - 16 : PADDED, here] = jnp.concatenate([edge[:SPARE], ones], axis=0).astype(jnp.bfloat16)
+
+
+def prepare_kernel(images, halo, ids_ref, *rest):
+    got_refs, (keys, marks) = rest[: len(EARLY)], rest[len(EARLY) :]
+    count = got_refs[0].shape[1]
+    write_marks(images, ids_ref[...], marks)
+    own = lax.rem(lax.axis_index("grp"), HEADS)
+    for step, (by, ref) in enumerate(zip(EARLY, got_refs)):
+        first = jnp.bitwise_xor(own, by) * count
+        here = pl.ds(pl.multiple_of(halo + first, LANES), count)
+        keys[step * count : (step + 1) * count, :] = turned_keys(marks[0, :, here], ref)
+
+
+def attend_kernel(images, piggy, halo, ids_ref, marks, early_keys, *rest):
+    got_refs, rest = rest[:HEADS], rest[HEADS:]
+    if halo:
+        left_ref, right_ref, *rest = rest
+    out_ref, keys, values, queries, attended, *work, starts = rest
+    count = got_refs[0].shape[1]
+    padded = attended.shape[0]
+    size = padded - SPARE
+    total_rows = HEADS * count
+    length = ids_ref.shape[1]
+    ids = ids_ref[...]
+    find_starts(images, ids, starts)
+
+    own = lax.rem(lax.axis_index("grp"), HEADS)
+    for step, (by, ref) in enumerate(zip(EARLY + LATE, got_refs)):
+        first = jnp.bitwise_xor(own, by) * count
+        here = pl.ds(pl.multiple_of(halo + first, LANES), count)
+        there = pl.ds(pl.multiple_of(first, LANES), count)
+        if by in EARLY:
+            keys[here, :] = early_keys[step * count : (step + 1) * count, :]
+        else:
+            keys[here, :] = turned_keys(marks[0, :, here], ref)
+        store_values(ref, values, here)
+        store_queries(marks[1, :, here], ref, queries, there)
+    if halo:
+        for ref, here in ((left_ref, slice(0, halo)), (right_ref, slice(length - halo, length))):
+            keys[here, :] = turned_keys(marks[0, :, here], ref)
+            store_values(ref, values, here)
+    attend_images(images, ids_ref, keys, values, queries, attended, work, starts, halo)
+
+    odd_head = lax.rem(own, 2) == 1
     mine = ids[:, halo : halo + total_rows]
 
     def placed(block, spare):
@@ -252,9 +308,7 @@
             image_rows(mine, images), flat, (((1,), (1,)), ((), ())), preferred_element_type=jnp.float32
         )
         pooled = split_in_two(pooled, images)
-        sums = jnp.zeros((SPARE, 2 * LANES), jnp.float32)
-        for ref in got_refs:
-            sums += ref[query_at : query_at + 16].astype(jnp.float32)[0:SPARE, 0 : 2 * LANES]
+        sums = spare_sums(got_refs)
         sums = split_in_two(sums + pltpu.roll(sums, images, axis=0), images)
         spare = jnp.concatenate(
             [pooled, jnp.zeros((SPARE, LANES - padded), jnp.float32), sums], axis=1
@@ -422,14 +476,14 @@
         2 * count * depth * 18 * size,
     )(normed, sums, turned_weight)
     sent = dict(zip((6, 7, 2, 3, 4, 5, 0, 1), sent))
-    got = []
-    for by in ORDER:
-        pairs = [(i, i ^ by) for i in range(group_size)]
-        got.append(moved(sent[by], "grp", pairs) if by else sent[by])
+    got = {0: sent[0]}
+    for by in ORDER[:-1]:
+        got[by] = moved(sent[by], "grp", [(i, i ^ by) for i in range(group_size)])
 
     length = HEADS * count
     halo = 0
-    operands = [segment_ids, *got]
+    near_ids = segment_ids
+    halos = []
     if parts > 1:
         halo = rounded_up(MAXP - 1, LANES)
         part = lax.axis_index("grp") // HEADS
@@ -443,16 +497,24 @@
         )
         near_ids = lax.dynamic_slice_in_dim(whole_ids, part * length, length + 2 * halo, axis=1)
         order = jnp.bitwise_xor(lax.axis_index("grp") % HEADS, jnp.arange(HEADS))
-        flat = jnp.stack([got[ORDER.index(by)] for by in range(HEADS)])[order][:, : 2 * size].transpose(1, 0, 2).reshape(2 * size, length)
+        flat = jnp.stack([got[by] for by in range(HEADS)])[order][:, : 2 * size].transpose(1, 0, 2).reshape(2 * size, length)
         flat = jnp.concatenate([flat, jnp.zeros((16, length), bf16)], axis=0)
         ahead = [(i, i + HEADS) for i in range(group_size - HEADS)]
         back = [(i + HEADS, i) for i in range(group_size - HEADS)]
         left = moved(flat[:, length - halo :], "grp", ahead)
         right = moved(flat[:, :halo], "grp", back)
-        operands = [near_ids, *got, left, right]
+        halos = [left, right]
     reach = length + 2 * halo
     window = min(rounded_up(MAXP + LANES - 1, LANES), reach)
     tile = 2 * LANES
+    early_keys, marks = call(
+        functools.partial(prepare_kernel, images, halo),
+        (shape((len(EARLY) * count, LANES), bf16), shape((2, SPARE, reach), f32)),
+        [],
+        in_vmem(1 + len(EARLY)),
+        1 << 30,
+    )(near_ids, *[got[by] for by in EARLY])
+    operands = [near_ids, marks, early_keys, *[got[by] for by in EARLY + LATE], *halos]
     answers = call(
         functools.partial(attend_kernel, images, piggy, halo),
         shape((HEADS, padded, count), bf16),
@@ -465,8 +527,7 @@
             pltpu.VMEM((window, tile), f32),
             pltpu.VMEM((1, tile), f32),
             pltpu.VMEM((1, tile), f32),
-            pltpu.VMEM((2, SPARE, reach), f32),
-            pltpu.SMEM((images,), jnp.int32),
+            pltpu.SMEM((images + 1,), jnp.int32),
         ],
         in_vmem(len(operands)),
         4 * size * length * MAXP,

time: 47.5 us -> 47.4 us (level)
  waiting for transfers between devices: 13.6 us -> 11.4 us
  starting transfers between devices: 16.8 us -> 18.1 us
  Pallas kernels: 16.2 us -> 16.8 us
    ppermute x10, waiting for transfers between devices: 13.6 us -> 11.3 us  [moved(): return lax.ppermute(value, axis, pairs)]
    ppermute x10, starting transfers between devices: 12.9 us -> 14.6 us  [moved(): return lax.ppermute(value, axis, pairs)]
where the time goes in v10:
time: 47.4 us; the launch traced here: 47.1 us
  starting transfers between devices  18.1 us (38%)
  Pallas kernels  16.8 us (35%)
  waiting for transfers between devices  11.4 us (24%)
  between operations  0.71 us (1%)
    ppermute x10, starting transfers between devices, moved(): return lax.ppermute(value, axis, pairs)  14.6 us
    ppermute x10, waiting for transfers between devices, moved(): return lax.ppermute(value, axis, pairs)  11.3 us
    pallas_call x1, Pallas kernels, local(): call(functools.partial(attend_kernel, images, piggy, halo), shape((HEADS,...  8.79 us
    all_to_all x1, starting transfers between devices, exchanged(): lax.all_to_all(blocks, 'grp', 0, 0, axis_index_groups=groups, tiled=True)  3.49 us
    pallas_call x1, Pallas kernels, local(): call(functools.partial(far_kernel, images, piggy), (shape((depth, count),...  3.12 us
    pallas_call x1, Pallas kernels, local(): call(functools.partial(near_kernel, piggy), (block,) * 6, [], in_vmem(3),...  2.35 us
    pallas_call x1, Pallas kernels, local(): call(functools.partial(finish_kernel, images), (shape((count, depth), bf1...  2.29 us
  transfers between devices with their start and end apart: 11, of which 7 were waited for; matrix products, arithmetic and copies ran while one was open for 0% of the time, Pallas kernels for 5%

profile of v10, /device:TPU:0, one launch (start us, length us, event | category | flops | bytes accessed | tf_op | source)
XLA Modules:
  0.0 47.1 jit_solution(16686800758436298322)
XLA Ops:
  0.6 0.0 copy-start
  0.6 0.0 copy-start.3
  0.6 3.1 %shard_map.68 = (bf16[1152,384]{1,0:T(8,128)(2,1)S(1)}, f32[8,1152]{1,0:T(8,128)S(1)}, bf16[224,384]{1,0:T(8,128)(2,1)S(1)}, bf16[224,384]{1,0:T(8,128)(2,1)S(1)}) custom-call(s32[1,3072]{1,0:T(1,128)} %ids_ref.5, bf16[384,1152]{1,0:T(8,128)(2,1)} %bitcast.6, bf16[1728,1152]{1,0:T(8,128)(2,1)} %bitcast.4), custom_call_target="tpu_custom_call" | custom-call | flops 382205952 | bytes 8388608 | tf_op jit(solution)/shard_map/pallas_call | solution.py:457
  3.8 4.0 %collective-permute-start = (bf16[224,384]{1,0:T(8,128)(2,1)S(1)}, bf16[224,384]{1,0:T(8,128)(2,1)S(1)}, u32[]{:S(2)}, u32[]{:S(2)}) collective-permute-start(bf16[224,384]{1,0:T(8,128)(2,1)S(1)} %get-tuple-element.17), channel_id=1, source_target_pairs={{0,24},{4,28},{8,16},{12,20},{16,8},{20,12},{24,0},{28,4},{1,25},{... | collective-permute-start | bytes 516104 | tf_op jit(solution)/shard_map/ppermute | solution.py:427
  7.7 0.0 collective-permute-start.1
  7.7 0.0 copy-done
  7.7 2.3 %shard_map.69 = (bf16[224,384]{1,0:T(8,128)(2,1)S(1)}, bf16[224,384]{1,0:T(8,128)(2,1)S(1)}, bf16[224,384]{1,0:T(8,128)(2,1)S(1)}, bf16[224,384]{1,0:T(8,128)(2,...) custom-call(bf16[1152,384]{1,0:T(8,128)(2,1)S(1)} %get-tuple-element.19.normed_ref, ...), custom_call_target="tpu_custom_call" | custom-call | flops 1146617856 | bytes 8388608 | tf_op jit(solution)/shard_map/pallas_call | solution.py:471
  10.1 0.3 collective-permute-start.2
  10.4 1.9 %collective-permute-start.3 = (bf16[224,384]{1,0:T(8,128)(2,1)S(1)}, bf16[224,384]{1,0:T(8,128)(2,1)S(1)}, u32[]{:S(2)}, u32[]{:S(2)}) collective-permute-start(bf16[224,384]{1,0:T(8,128)(2,1)S(1)} %get-tuple-element.25), channel_id=1, source_target_pairs={{0,8},{4,12},{8,0},{12,4},{16,24},{20,28},{24,16},{28,20},{1,9},{5... | collective-permute-start | bytes 516104 | tf_op jit(solution)/shard_map/ppermute | solution.py:427
  12.2 1.5 %collective-permute-start.4 = (bf16[224,384]{1,0:T(8,128)(2,1)S(1)}, bf16[224,384]{1,0:T(8,128)(2,1)S(1)}, u32[]{:S(2)}, u32[]{:S(2)}) collective-permute-start(bf16[224,384]{1,0:T(8,128)(2,1)S(1)} %get-tuple-element.26), channel_id=1, source_target_pairs={{0,16},{4,20},{8,24},{12,28},{16,0},{20,4},{24,8},{28,12},{1,17},{... | collective-permute-start | bytes 516104 | tf_op jit(solution)/shard_map/ppermute | solution.py:427
  13.8 0.0 collective-permute-done.rest_0_
  13.8 0.0 collective-permute-start.5
  13.8 2.4 %collective-permute-done.1.rest_1_ = bf16[224,384]{1,0:T(8,128)(2,1)S(1)} collective-permute-done((bf16[224,384]{1,0:T(8,128)(2,1)S(1)}, bf16[224,384]{1,0:T(8,128)(2,1)S(1)}, u32[]{:S(2)}, u32[]{:S(2)}) %collective-permute-start.1) | collective-permute-done | bytes 172064 | tf_op jit(solution)/shard_map/ppermute | solution.py:427
  16.2 1.9 %collective-permute-start.6 = (bf16[224,384]{1,0:T(8,128)(2,1)S(1)}, bf16[224,384]{1,0:T(8,128)(2,1)S(1)}, u32[]{:S(2)}, u32[]{:S(2)}) collective-permute-start(bf16[224,384]{1,0:T(8,128)(2,1)S(1)} %get-tuple-element.28), channel_id=1, source_target_pairs={{0,20},{4,16},{8,28},{12,24},{16,4},{20,0},{24,12},{28,8},{1,21},{... | collective-permute-start | bytes 516104 | tf_op jit(solution)/shard_map/ppermute | solution.py:427
  18.1 0.0 collective-permute-done.2.rest_2_
  18.1 0.0 copy-done.3
  18.1 0.0 copy-start.4
  18.1 0.0 copy-start.1
  18.1 0.0 copy-start.2
  18.1 0.2 shard_map.70
  18.3 2.5 %collective-permute-done.3.rest_4_ = bf16[224,384]{1,0:T(8,128)(2,1)S(1)} collective-permute-done((bf16[224,384]{1,0:T(8,128)(2,1)S(1)}, bf16[224,384]{1,0:T(8,128)(2,1)S(1)}, u32[]{:S(2)}, u32[]{:S(2)}) %collective-permute-start.3) | collective-permute-done | bytes 172064 | tf_op jit(solution)/shard_map/ppermute | solution.py:427
  20.9 0.0 collective-permute-done.4.rest_5_
  20.9 1.5 %collective-permute-done.5.rest_6_ = bf16[224,384]{1,0:T(8,128)(2,1)S(1)} collective-permute-done((bf16[224,384]{1,0:T(8,128)(2,1)S(1)}, bf16[224,384]{1,0:T(8,128)(2,1)S(1)}, u32[]{:S(2)}, u32[]{:S(2)}) %collective-permute-start.5) | collective-permute-done | bytes 172064 | tf_op jit(solution)/shard_map/ppermute | solution.py:427
  22.4 0.6 %collective-permute-done.6.rest_7_ = bf16[224,384]{1,0:T(8,128)(2,1)S(1)} collective-permute-done((bf16[224,384]{1,0:T(8,128)(2,1)S(1)}, bf16[224,384]{1,0:T(8,128)(2,1)S(1)}, u32[]{:S(2)}, u32[]{:S(2)}) %collective-permute-start.6) | collective-permute-done | bytes 172064 | tf_op jit(solution)/shard_map/ppermute | solution.py:427
  23.1 8.8 %shard_map.71 = bf16[8,80,384]{2,1,0:T(8,128)(2,1)} custom-call(s32[1,3072]{1,0:T(1,128)S(1)} %copy-done.3, f32[2,8,3072]{2,1,0:T(8,128)S(1)} %get-tuple-element.23.marks, bf16[1536,128]{1,0:T(8,128)(2,1)S(1)} %get-tuple-element.24.early_keys, bf16[224,384]{1,0:T(8,128)(2,1)S(1)} %collective-permute-done.rest_0_, ...), custom_call_target="tpu_custom_call" | custom-call | flops 905969664 | bytes 8388608 | tf_op jit(solution)/shard_map/pallas_call | solution.py:518
  31.9 3.5 %all-to-all-start = ((bf16[8,80,384]{2,1,0:T(8,128)(2,1)}), bf16[8,80,384]{2,1,0:T(8,128)(2,1)S(1)}, u32[]{:S(2)}, u32[]{:S(2)}) async-start(bf16[8,80,384]{2,1,0:T(8,128)(2,1)} %shard_map.71), calls=%async_computation | async-start | bytes 983040 | tf_op jit(solution)/shard_map/all_to_all | solution.py:437
  35.4 0.0 copy-done.4
  35.4 3.7 %collective-permute-start.9 = (bf16[4,1152]{1,0:T(4,128)(2,1)S(1)}, bf16[4,1152]{1,0:T(4,128)(2,1)S(1)}, u32[]{:S(2)}, u32[]{:S(2)}) collective-permute-start(bf16[4,1152]{1,0:T(4,128)(2,1)S(1)} %copy-done.4), channel_id=1, source_target_pairs={{0,3},{1,0},{2,1},{3,2},{4,7},{5,4},{6,5},{7,6},{8,11},{9,8},{10,9... | collective-permute-start | bytes 27656 | tf_op jit(solution)/shard_map/ppermute | solution.py:427
  39.1 0.0 collective-permute-start.8
  39.1 1.3 %collective-permute-start.7 = (bf16[4,1152]{1,0:T(4,128)(2,1)S(1)}, bf16[4,1152]{1,0:T(4,128)(2,1)S(1)}, u32[]{:S(2)}, u32[]{:S(2)}) collective-permute-start(bf16[4,1152]{1,0:T(4,128)(2,1)S(1)} %copy-done.4), channel_id=1, source_target_pairs={{0,1},{1,2},{2,3},{3,0},{4,5},{5,6},{6,7},{7,4},{8,9},{9,10},{10,1... | collective-permute-start | bytes 27656 | tf_op jit(solution)/shard_map/ppermute | solution.py:427
  40.5 0.0 collective-permute-done.9
  40.5 3.2 %collective-permute-done.8 = bf16[4,1152]{1,0:T(4,128)(2,1)S(1)} collective-permute-done((bf16[4,1152]{1,0:T(4,128)(2,1)S(1)}, bf16[4,1152]{1,0:T(4,128)(2,1)S(1)}, u32[]{:S(2)}, u32[]{:S(2)}) %collective-permute-start.8) | collective-permute-done | bytes 9248 | tf_op jit(solution)/shard_map/ppermute | solution.py:427
  43.7 0.9 %collective-permute-done.7 = bf16[4,1152]{1,0:T(4,128)(2,1)S(1)} collective-permute-done((bf16[4,1152]{1,0:T(4,128)(2,1)S(1)}, bf16[4,1152]{1,0:T(4,128)(2,1)S(1)}, u32[]{:S(2)}, u32[]{:S(2)}) %collective-permute-start.7) | collective-permute-done | bytes 9248 | tf_op jit(solution)/shard_map/ppermute | solution.py:427
  44.6 0.1 all-to-all-done.got_ref
  44.8 0.0 copy-done.1
  44.8 0.0 copy-done.2
  44.8 2.3 %shard_map.72 = (bf16[384,1152]{1,0:T(8,128)(2,1)}, f32[1,4]{1,0:T(1,128)}) custom-call(bf16[384,1152]{1,0:T(8,128)(2,1)S(1)} %bitcast.7, bf16[8,80,384]{2,1,0:T(8,128)(2,1)S(1)} %all-to-all-done.got_ref, bf16[576,1152]{1,0:T(8,128)(2,1)S(1)} %copy-done.2, bf16[16,1152]{1,0:T(8,128)(2,1)S(1)} %pad_maximum_fusion.text_ref), custom_call_target="tpu_custom_call" | custom-call | flops 509607936 | bytes 8388608 | tf_op jit(solution)/shard_map/pallas_call | solution.py:548
  (1 shorter events, 0.0 us)
Async XLA Ops:
  0.6 7.1 %copy-start = (bf16[1152,1728]{0,1:T(8,128)(2,1)S(1)}, bf16[1152,1728]{0,1:T(8,128)(2,1)}, u32[]{:S(2)}) copy-start(bf16[1152,1728]{0,1:T(8,128)(2,1)} %param.7) | copy-start | bytes 11943940
  0.6 17.5 %copy-start.3 = (s32[1,3072]{1,0:T(1,128)S(1)}, s32[1,3072]{1,0:T(1,128)}, u32[]{:S(2)}) copy-start(s32[1,3072]{1,0:T(1,128)} %ids_ref.5) | copy-start | bytes 36868
  3.8 10.0 %collective-permute-start = (bf16[224,384]{1,0:T(8,128)(2,1)S(1)}, bf16[224,384]{1,0:T(8,128)(2,1)S(1)}, u32[]{:S(2)}, u32[]{:S(2)}) collective-permute-start(bf16[224,384]{1,0:T(8,128)(2,1)S(1)} %get-tuple-element.17), channel_id=1, source_target_pairs={{0,24},{4,28},{8,16},{12,20},{16,8},{20,12},{24,0},{28,4},{1,25},{... | collective-permute-start | bytes 516104 | tf_op jit(solution)/shard_map/ppermute | solution.py:427
  7.7 8.5 %collective-permute-start.1 = (bf16[224,384]{1,0:T(8,128)(2,1)S(1)}, bf16[224,384]{1,0:T(8,128)(2,1)S(1)}, u32[]{:S(2)}, u32[]{:S(2)}) collective-permute-start(bf16[224,384]{1,0:T(8,128)(2,1)S(1)} %get-tuple-element.18), channel_id=1, source_target_pairs={{0,28},{4,24},{8,20},{12,16},{16,12},{20,8},{24,4},{28,0},{1,29},{... | collective-permute-start | bytes 516104 | tf_op jit(solution)/shard_map/ppermute | solution.py:427
  10.1 8.0 %collective-permute-start.2 = (bf16[224,384]{1,0:T(8,128)(2,1)S(1)}, bf16[224,384]{1,0:T(8,128)(2,1)S(1)}, u32[]{:S(2)}, u32[]{:S(2)}) collective-permute-start(bf16[224,384]{1,0:T(8,128)(2,1)S(1)} %get-tuple-element.21), channel_id=1, source_target_pairs={{0,4},{4,0},{8,12},{12,8},{16,20},{20,16},{24,28},{28,24},{1,5},{5... | collective-permute-start | bytes 516104 | tf_op jit(solution)/shard_map/ppermute | solution.py:427
  10.4 10.5 %collective-permute-start.3 = (bf16[224,384]{1,0:T(8,128)(2,1)S(1)}, bf16[224,384]{1,0:T(8,128)(2,1)S(1)}, u32[]{:S(2)}, u32[]{:S(2)}) collective-permute-start(bf16[224,384]{1,0:T(8,128)(2,1)S(1)} %get-tuple-element.25), channel_id=1, source_target_pairs={{0,8},{4,12},{8,0},{12,4},{16,24},{20,28},{24,16},{28,20},{1,9},{5... | collective-permute-start | bytes 516104 | tf_op jit(solution)/shard_map/ppermute | solution.py:427
  12.2 8.6 %collective-permute-start.4 = (bf16[224,384]{1,0:T(8,128)(2,1)S(1)}, bf16[224,384]{1,0:T(8,128)(2,1)S(1)}, u32[]{:S(2)}, u32[]{:S(2)}) collective-permute-start(bf16[224,384]{1,0:T(8,128)(2,1)S(1)} %get-tuple-element.26), channel_id=1, source_target_pairs={{0,16},{4,20},{8,24},{12,28},{16,0},{20,4},{24,8},{28,12},{1,17},{... | collective-permute-start | bytes 516104 | tf_op jit(solution)/shard_map/ppermute | solution.py:427
  13.8 8.7 %collective-permute-start.5 = (bf16[224,384]{1,0:T(8,128)(2,1)S(1)}, bf16[224,384]{1,0:T(8,128)(2,1)S(1)}, u32[]{:S(2)}, u32[]{:S(2)}) collective-permute-start(bf16[224,384]{1,0:T(8,128)(2,1)S(1)} %get-tuple-element.27), channel_id=1, source_target_pairs={{0,12},{4,8},{8,4},{12,0},{16,28},{20,24},{24,20},{28,16},{1,13},{... | collective-permute-start | bytes 516104 | tf_op jit(solution)/shard_map/ppermute | solution.py:427
  16.2 6.9 %collective-permute-start.6 = (bf16[224,384]{1,0:T(8,128)(2,1)S(1)}, bf16[224,384]{1,0:T(8,128)(2,1)S(1)}, u32[]{:S(2)}, u32[]{:S(2)}) collective-permute-start(bf16[224,384]{1,0:T(8,128)(2,1)S(1)} %get-tuple-element.28), channel_id=1, source_target_pairs={{0,20},{4,16},{8,28},{12,24},{16,4},{20,0},{24,12},{28,8},{1,21},{... | collective-permute-start | bytes 516104 | tf_op jit(solution)/shard_map/ppermute | solution.py:427
  18.1 17.3 %copy-start.4 = (bf16[4,1152]{1,0:T(4,128)(2,1)S(1)}, bf16[4,1152]{1,0:T(4,128)(2,1)}, u32[]{:S(2)}) copy-start(bf16[4,1152]{1,0:T(4,128)(2,1)} %param.9) | copy-start | bytes 27652
  18.1 26.7 %copy-start.1 = (bf16[1,384,1152]{2,1,0:T(8,128)(2,1)S(1)}, bf16[1,384,1152]{2,1,0:T(8,128)(2,1)}, u32[]{:S(2)}) copy-start(bf16[1,384,1152]{2,1,0:T(8,128)(2,1)} %param.5) | copy-start | bytes 2654212
  18.1 26.7 %copy-start.2 = (bf16[576,1152]{1,0:T(8,128)(2,1)S(1)}, bf16[576,1152]{1,0:T(8,128)(2,1)}, u32[]{:S(2)}) copy-start(bf16[576,1152]{1,0:T(8,128)(2,1)} %out_weight_ref.1) | copy-start | bytes 3981316
  31.9 12.9 %all-to-all-start = ((bf16[8,80,384]{2,1,0:T(8,128)(2,1)}), bf16[8,80,384]{2,1,0:T(8,128)(2,1)S(1)}, u32[]{:S(2)}, u32[]{:S(2)}) async-start(bf16[8,80,384]{2,1,0:T(8,128)(2,1)} %shard_map.71), calls=%async_computation | async-start | bytes 983040 | tf_op jit(solution)/shard_map/all_to_all | solution.py:437
  35.4 5.1 %collective-permute-start.9 = (bf16[4,1152]{1,0:T(4,128)(2,1)S(1)}, bf16[4,1152]{1,0:T(4,128)(2,1)S(1)}, u32[]{:S(2)}, u32[]{:S(2)}) collective-permute-start(bf16[4,1152]{1,0:T(4,128)(2,1)S(1)} %copy-done.4), channel_id=1, source_target_pairs={{0,3},{1,0},{2,1},{3,2},{4,7},{5,4},{6,5},{7,6},{8,11},{9,8},{10,9... | collective-permute-start | bytes 27656 | tf_op jit(solution)/shard_map/ppermute | solution.py:427
  39.1 4.6 %collective-permute-start.8 = (bf16[4,1152]{1,0:T(4,128)(2,1)S(1)}, bf16[4,1152]{1,0:T(4,128)(2,1)S(1)}, u32[]{:S(2)}, u32[]{:S(2)}) collective-permute-start(bf16[4,1152]{1,0:T(4,128)(2,1)S(1)} %copy-done.4), channel_id=1, source_target_pairs={{0,2},{1,3},{2,0},{3,1},{4,6},{5,7},{6,4},{7,5},{8,10},{9,11},{10,... | collective-permute-start | bytes 27656 | tf_op jit(solution)/shard_map/ppermute | solution.py:427
  39.1 5.5 %collective-permute-start.7 = (bf16[4,1152]{1,0:T(4,128)(2,1)S(1)}, bf16[4,1152]{1,0:T(4,128)(2,1)S(1)}, u32[]{:S(2)}, u32[]{:S(2)}) collective-permute-start(bf16[4,1152]{1,0:T(4,128)(2,1)S(1)} %copy-done.4), channel_id=1, source_target_pairs={{0,1},{1,2},{2,3},{3,0},{4,5},{5,6},{6,7},{7,4},{8,9},{9,10},{10,1... | collective-permute-start | bytes 27656 | tf_op jit(solution)/shard_map/ppermute | solution.py:427

commit v11 on v10

--- a/solution.py
+++ b/solution.py
@@ -130,8 +130,10 @@
 
 
 def find_starts(images, ids, starts):
+    image = lax.broadcasted_iota(jnp.int32, (rounded_up(images + 1, SPARE), ids.shape[1]), 0)
+    before = jnp.sum((ids < image).astype(jnp.int32), axis=1, keepdims=True)
     for image in range(images + 1):
-        starts[image] = jnp.sum((ids < image).astype(jnp.int32))
+        starts[image] = before[image, 0]
 
 
 def write_marks(images, ids, marks):
@@ -159,75 +161,45 @@
     return found
 
 
-def attend_images(images, ids_ref, keys, values, queries, attended, work, starts, halo):
+def attend_images(ids_ref, keys, values, queries, attended, work, table, halo):
     scores_a, scores_b, tops_a, tops_b = work
-    query_base = halo
     window, tile = scores_a.shape
     size = attended.shape[0] - SPARE
-    held = queries.shape[1]
-    tiles = held // tile
-
-    def bounds(image):
-        first = lax.div(jnp.maximum(starts[image] - query_base, 0), tile)
-        last = lax.div(jnp.minimum(starts[image + 1] - query_base, held) - 1, tile)
-        return jnp.minimum(first, tiles - 1), last
-
-    def after(image):
-        return jnp.minimum(image + 1, images - 1)
-
-    def following(state):
-        at, image = state
-        more = at < bounds(image)[1]
-        later = after(image)
-        return jnp.where(more, at + 1, bounds(later)[0]), jnp.where(more, image, later)
-
-    def window_of(image):
-        begin = lax.div(starts[image], LANES) * LANES
-        return pl.ds(pl.multiple_of(jnp.minimum(begin, keys.shape[0] - window), LANES), window)
+
+    def state_of(step):
+        at = pl.multiple_of(table[0, step] * tile, tile)
+        return at, table[1, step], pl.ds(pl.multiple_of(table[2, step], LANES), window)
 
     def score(state, scores, tops):
-        at, image = state
-        query = queries[:, pl.ds(pl.multiple_of(at * tile, tile), tile)]
-        found = jnp.dot(keys[window_of(image), :], query, preferred_element_type=jnp.float32)
+        first, _, here = state
+        found = jnp.dot(keys[here, :], queries[:, pl.ds(first, tile)], preferred_element_type=jnp.float32)
         scores[...] = found
         tops[...] = jnp.max(found, axis=0, keepdims=True)
 
     def weigh(state, scores, tops):
-        at, image = state
-        first = pl.multiple_of(at * tile, tile)
-        labels = ids_ref[:, pl.ds(pl.multiple_of(query_base + first, LANES), tile)]
+        first, image, here = state
+        labels = ids_ref[:, pl.ds(pl.multiple_of(halo + first, LANES), tile)]
         probs = jnp.exp2((scores[...] - tops[...]) * (size ** (-0.5) * math.log2(math.e)))
-        weighted = jnp.dot(
-            values[:, window_of(image)], probs.astype(jnp.bfloat16), preferred_element_type=jnp.float32
-        )
+        weighted = jnp.dot(values[:, here], probs.astype(jnp.bfloat16), preferred_element_type=jnp.float32)
         share = 1.0 / weighted[size : size + 1]
         place = (slice(None), pl.ds(first, tile))
         attended[place] = jnp.where(labels == image, weighted * share, attended[place])
 
-    low = image_at(images, starts, query_base)
-    high = image_at(images, starts, query_base + held - 1)
-    pairs = jnp.int32(0)
-    for image in range(images):
-        first, last = bounds(image)
-        wanted = jnp.logical_and(low <= image, image <= high)
-        pairs += jnp.where(wanted, last - first + 1, 0)
-
-    def two_pairs(_, state):
-        second = following(state)
+    def two_pairs(step, _):
+        first, second, third = (state_of(2 * step + more) for more in range(3))
         score(second, scores_b, tops_b)
-        weigh(state, scores_a, tops_a)
-        third = following(second)
+        weigh(first, scores_a, tops_a)
         score(third, scores_a, tops_a)
         weigh(second, scores_b, tops_b)
-        return third
-
-    begun = (jnp.int32(0), low)
-    score(begun, scores_a, tops_a)
-    last_state = lax.fori_loop(0, lax.div(pairs, 2), two_pairs, begun)
+        return 0
+
+    pairs = table[3, 0]
+    score(state_of(0), scores_a, tops_a)
+    lax.fori_loop(0, lax.div(pairs, 2), two_pairs, 0)
 
     @pl.when(lax.rem(pairs, 2) == 1)
     def _():
-        weigh(last_state, scores_a, tops_a)
+        weigh(state_of(pairs - 1), scores_a, tops_a)
 
 
 def turned_keys(marked, block_ref):
@@ -252,29 +224,55 @@
     values[PADDED - 16 : PADDED, here] = jnp.concatenate([edge[:SPARE], ones], axis=0).astype(jnp.bfloat16)
 
 
-def prepare_kernel(images, halo, ids_ref, *rest):
-    got_refs, (keys, marks) = rest[: len(EARLY)], rest[len(EARLY) :]
+def list_pairs(images, held, tile, window, length, halo, starts, table):
+    low = image_at(images, starts, halo)
+    high = image_at(images, starts, halo + held - 1)
+
+    def one_image(image, count):
+        first = lax.div(jnp.maximum(starts[image] - halo, 0), tile)
+        last = lax.div(jnp.minimum(starts[image + 1] - halo, held) - 1, tile)
+        begin = jnp.minimum(lax.div(starts[image], LANES) * LANES, length - window)
+
+        def one_tile(at, count):
+            table[0, count] = at
+            table[1, count] = image
+            table[2, count] = begin
+            return count + 1
+
+        return lax.fori_loop(first, last + 1, one_tile, count)
+
+    pairs = lax.fori_loop(low, high + 1, one_image, jnp.int32(0))
+    for row in range(3):
+        table[row, pairs] = table[row, pairs - 1]
+    table[3, 0] = pairs
+
+
+def prepare_kernel(images, halo, tile, window, ids_ref, *rest):
+    got_refs, (keys, marks, table, starts) = rest[: len(EARLY)], rest[len(EARLY) :]
     count = got_refs[0].shape[1]
+    find_starts(images, ids_ref[...], starts)
     write_marks(images, ids_ref[...], marks)
     own = lax.rem(lax.axis_index("grp"), HEADS)
     for step, (by, ref) in enumerate(zip(EARLY, got_refs)):
         first = jnp.bitwise_xor(own, by) * count
         here = pl.ds(pl.multiple_of(halo + first, LANES), count)
         keys[step * count : (step + 1) * count, :] = turned_keys(marks[0, :, here], ref)
-
-
-def attend_kernel(images, piggy, halo, ids_ref, marks, early_keys, *rest):
+    list_pairs(images, HEADS * count, tile, window, ids_ref.shape[1], halo, starts, table)
+
+
+def attend_kernel(images, piggy, halo, ids_ref, table_ref, marks, early_keys, *rest):
     got_refs, rest = rest[:HEADS], rest[HEADS:]
     if halo:
         left_ref, right_ref, *rest = rest
-    out_ref, keys, values, queries, attended, *work, starts = rest
+    out_ref, keys, values, queries, attended, *work, table, sem = rest
+    fetch = pltpu.make_async_copy(table_ref, table, sem)
+    fetch.start()
     count = got_refs[0].shape[1]
     padded = attended.shape[0]
     size = padded - SPARE
     total_rows = HEADS * count
     length = ids_ref.shape[1]
     ids = ids_ref[...]
-    find_starts(images, ids, starts)
 
     own = lax.rem(lax.axis_index("grp"), HEADS)
     for step, (by, ref) in enumerate(zip(EARLY + LATE, got_refs)):
@@ -291,33 +289,47 @@
         for ref, here in ((left_ref, slice(0, halo)), (right_ref, slice(length - halo, length))):
             keys[here, :] = turned_keys(marks[0, :, here], ref)
             store_values(ref, values, here)
-    attend_images(images, ids_ref, keys, values, queries, attended, work, starts, halo)
+    fetch.wait()
+    attend_images(ids_ref, keys, values, queries, attended, work, table, halo)
 
     odd_head = lax.rem(own, 2) == 1
     mine = ids[:, halo : halo + total_rows]
 
-    def placed(block, spare):
-        even = jnp.concatenate([block[0:size], spare], axis=0)
-        odd = jnp.concatenate([spare, block[0:size]], axis=0)
-        return jnp.where(odd_head, odd, even)
-
+    @pl.when(odd_head)
+    def _():
+        attended[SPARE:padded, :] = attended[0:size, :]
+
+    row = lax.broadcasted_iota(jnp.int32, (padded, count), 0)
+    lowest = jnp.where(odd_head, SPARE, 0)
+    kept = jnp.logical_and(row >= lowest, row < lowest + size)
+    pooled = jnp.zeros((SPARE, padded), jnp.float32)
+    for source in range(HEADS):
+        here = slice(source * count, (source + 1) * count)
+        block = jnp.where(kept, attended[:, here], 0.0).astype(jnp.bfloat16)
+        out_ref[source] = block
+        if piggy:
+            pooled += lax.dot_general(
+                image_rows(mine[:, here], images),
+                block,
+                (((1,), (1,)), ((), ())),
+                preferred_element_type=jnp.float32,
+            )
     if piggy:
-        nothing = jnp.zeros((SPARE, total_rows), jnp.float32)
-        flat = placed(attended[...], nothing).astype(jnp.bfloat16)
-        pooled = lax.dot_general(
-            image_rows(mine, images), flat, (((1,), (1,)), ((), ())), preferred_element_type=jnp.float32
-        )
         pooled = split_in_two(pooled, images)
         sums = spare_sums(got_refs)
         sums = split_in_two(sums + pltpu.roll(sums, images, axis=0), images)
         spare = jnp.concatenate(
             [pooled, jnp.zeros((SPARE, LANES - padded), jnp.float32), sums], axis=1
         )
-    else:
-        spare = jnp.zeros((SPARE, count), jnp.float32)
-    for source in range(HEADS):
-        block = placed(attended[:, source * count : (source + 1) * count], spare)
-        out_ref[source] = block.astype(jnp.bfloat16)
+
+        def store_spare(edge, rows):
+            for source in range(HEADS):
+                block = attended[edge, source * count : (source + 1) * count]
+                parts = [spare, block[SPARE:]] if rows == 0 else [block[:SPARE], spare]
+                out_ref[source, edge] = jnp.concatenate(parts, axis=0).astype(jnp.bfloat16)
+
+        pl.when(odd_head)(lambda: store_spare(slice(0, 16), 0))
+        pl.when(jnp.logical_not(odd_head))(lambda: store_spare(slice(padded - 16, padded), SPARE))
 
 
 def joined_heads(got_ref, out_weight_ref, flat, weight):
@@ -507,14 +519,21 @@
     reach = length + 2 * halo
     window = min(rounded_up(MAXP + LANES - 1, LANES), reach)
     tile = 2 * LANES
-    early_keys, marks = call(
-        functools.partial(prepare_kernel, images, halo),
-        (shape((len(EARLY) * count, LANES), bf16), shape((2, SPARE, reach), f32)),
-        [],
+    vmem = pl.BlockSpec(memory_space=pltpu.VMEM)
+    listed = (4, rounded_up(length // tile + images, LANES))
+    early_keys, marks, table = call(
+        functools.partial(prepare_kernel, images, halo, tile, window),
+        (
+            shape((len(EARLY) * count, LANES), bf16),
+            shape((2, SPARE, reach), f32),
+            shape(listed, jnp.int32),
+        ),
+        [pltpu.SMEM((images + 1,), jnp.int32)],
         in_vmem(1 + len(EARLY)),
         1 << 30,
+        (vmem, vmem, pl.BlockSpec(memory_space=pltpu.SMEM)),
     )(near_ids, *[got[by] for by in EARLY])
-    operands = [near_ids, marks, early_keys, *[got[by] for by in EARLY + LATE], *halos]
+    operands = [marks, early_keys, *[got[by] for by in EARLY + LATE], *halos]
     answers = call(
         functools.partial(attend_kernel, images, piggy, halo),
         shape((HEADS, padded, count), bf16),
@@ -527,11 +546,12 @@
             pltpu.VMEM((window, tile), f32),
             pltpu.VMEM((1, tile), f32),
             pltpu.VMEM((1, tile), f32),
-            pltpu.SMEM((images + 1,), jnp.int32),
+            pltpu.SMEM(listed, jnp.int32),
+            pltpu.SemaphoreType.DMA,
         ],
-        in_vmem(len(operands)),
+        in_vmem(1) + [hbm] + in_vmem(len(operands)),
         4 * size * length * MAXP,
-    )(*operands)
+    )(near_ids, table, *operands)
     back_home = exchanged(answers, groups)
     text_embed, _ = lax.optimization_barrier((text_embed, answers))
     texts = jnp.concatenate(all_texts(text_embed), axis=0)

time: 47.4 us -> 47.8 us (level)
  Pallas kernels: 16.8 us -> 18.3 us
    pallas_call x1, Pallas kernels: 0.22 us -> 1.05 us  [local(): call(functools.partial(prepare_kernel, images, halo, tile, window), (shap...]
    pallas_call x1, Pallas kernels: 8.79 us -> 9.46 us  [local(): call(functools.partial(attend_kernel, images, piggy, halo), shape((HEADS,...]
    ppermute x10, waiting for transfers between devices: 11.3 us -> 10.8 us  [moved(): return lax.ppermute(value, axis, pairs)]
  transfers between devices with their start and end apart: 11 -> 11, of which waited for: 7 -> 8; matrix products, arithmetic and copies ran while one was open for 0% -> 0% of each run, Pallas kernels for 5% -> 7%
where the time goes in v11:
time: 47.8 us
  Pallas kernels  18.3 us (38%)
  starting transfers between devices  17.8 us (37%)
  waiting for transfers between devices  11 us (23%)
  between operations  0.71 us (1%)
    ppermute x10, starting transfers between devices, moved(): return lax.ppermute(value, axis, pairs)  14.2 us
    ppermute x10, waiting for transfers between devices, moved(): return lax.ppermute(value, axis, pairs)  10.8 us
    pallas_call x1, Pallas kernels, local(): call(functools.partial(attend_kernel, images, piggy, halo), shape((HEADS,...  9.46 us
    all_to_all x1, starting transfers between devices, exchanged(): lax.all_to_all(blocks, 'grp', 0, 0, axis_index_groups=groups, tiled=True)  3.53 us
    pallas_call x1, Pallas kernels, local(): call(functools.partial(far_kernel, images, piggy), (shape((depth, count),...  3.12 us
    pallas_call x1, Pallas kernels, local(): call(functools.partial(near_kernel, piggy), (block,) * 6, [], in_vmem(3),...  2.35 us
    pallas_call x1, Pallas kernels, local(): call(functools.partial(finish_kernel, images), (shape((count, depth), bf1...  2.29 us
    pallas_call x1, Pallas kernels, local(): call(functools.partial(prepare_kernel, images, halo, tile, window), (shap...  1.05 us
  transfers between devices with their start and end apart: 11, of which 8 were waited for; matrix products, arithmetic and copies ran while one was open for 0% of the time, Pallas kernels for 7%

profile of v11, /device:TPU:0, one launch (start us, length us, event | category | flops | bytes accessed | tf_op | source)
XLA Modules:
  0.0 47.8 jit_solution(7976260655048554064)
XLA Ops:
  0.6 0.0 copy-start
  0.6 0.0 copy-start.3
  0.6 3.1 %shard_map.68 = (bf16[1152,384]{1,0:T(8,128)(2,1)S(1)}, f32[8,1152]{1,0:T(8,128)S(1)}, bf16[224,384]{1,0:T(8,128)(2,1)S(1)}, bf16[224,384]{1,0:T(8,128)(2,1)S(1)}) custom-call(s32[1,3072]{1,0:T(1,128)} %ids_ref.5, bf16[384,1152]{1,0:T(8,128)(2,1)} %bitcast.6, bf16[1728,1152]{1,0:T(8,128)(2,1)} %bitcast.4), custom_call_target="tpu_custom_call" | custom-call | flops 382205952 | bytes 8388608 | tf_op jit(solution)/shard_map/pallas_call | solution.py:469
  3.8 4.0 %collective-permute-start = (bf16[224,384]{1,0:T(8,128)(2,1)S(1)}, bf16[224,384]{1,0:T(8,128)(2,1)S(1)}, u32[]{:S(2)}, u32[]{:S(2)}) collective-permute-start(bf16[224,384]{1,0:T(8,128)(2,1)S(1)} %get-tuple-element.18), channel_id=1, source_target_pairs={{0,24},{4,28},{8,16},{12,20},{16,8},{20,12},{24,0},{28,4},{1,25},{... | collective-permute-start | bytes 516104 | tf_op jit(solution)/shard_map/ppermute | solution.py:439
  7.7 0.0 collective-permute-start.1
  7.7 0.0 copy-done
  7.7 2.3 %shard_map.69 = (bf16[224,384]{1,0:T(8,128)(2,1)S(1)}, bf16[224,384]{1,0:T(8,128)(2,1)S(1)}, bf16[224,384]{1,0:T(8,128)(2,1)S(1)}, bf16[224,384]{1,0:T(8,128)(2,...) custom-call(bf16[1152,384]{1,0:T(8,128)(2,1)S(1)} %get-tuple-element.20.normed_ref, ...), custom_call_target="tpu_custom_call" | custom-call | flops 1146617856 | bytes 8388608 | tf_op jit(solution)/shard_map/pallas_call | solution.py:483
  10.1 0.3 collective-permute-start.2
  10.4 1.9 %collective-permute-start.3 = (bf16[224,384]{1,0:T(8,128)(2,1)S(1)}, bf16[224,384]{1,0:T(8,128)(2,1)S(1)}, u32[]{:S(2)}, u32[]{:S(2)}) collective-permute-start(bf16[224,384]{1,0:T(8,128)(2,1)S(1)} %get-tuple-element.27), channel_id=1, source_target_pairs={{0,8},{4,12},{8,0},{12,4},{16,24},{20,28},{24,16},{28,20},{1,9},{5... | collective-permute-start | bytes 516104 | tf_op jit(solution)/shard_map/ppermute | solution.py:439
  12.2 1.5 %collective-permute-start.4 = (bf16[224,384]{1,0:T(8,128)(2,1)S(1)}, bf16[224,384]{1,0:T(8,128)(2,1)S(1)}, u32[]{:S(2)}, u32[]{:S(2)}) collective-permute-start(bf16[224,384]{1,0:T(8,128)(2,1)S(1)} %get-tuple-element.28), channel_id=1, source_target_pairs={{0,16},{4,20},{8,24},{12,28},{16,0},{20,4},{24,8},{28,12},{1,17},{... | collective-permute-start | bytes 516104 | tf_op jit(solution)/shard_map/ppermute | solution.py:439
  13.8 0.0 collective-permute-done.rest_0_
  13.8 0.0 collective-permute-start.5
  13.8 2.4 %collective-permute-done.1.rest_1_ = bf16[224,384]{1,0:T(8,128)(2,1)S(1)} collective-permute-done((bf16[224,384]{1,0:T(8,128)(2,1)S(1)}, bf16[224,384]{1,0:T(8,128)(2,1)S(1)}, u32[]{:S(2)}, u32[]{:S(2)}) %collective-permute-start.1) | collective-permute-done | bytes 172064 | tf_op jit(solution)/shard_map/ppermute | solution.py:439
  16.2 1.9 %collective-permute-start.6 = (bf16[224,384]{1,0:T(8,128)(2,1)S(1)}, bf16[224,384]{1,0:T(8,128)(2,1)S(1)}, u32[]{:S(2)}, u32[]{:S(2)}) collective-permute-start(bf16[224,384]{1,0:T(8,128)(2,1)S(1)} %get-tuple-element.30), channel_id=1, source_target_pairs={{0,20},{4,16},{8,28},{12,24},{16,4},{20,0},{24,12},{28,8},{1,21},{... | collective-permute-start | bytes 516104 | tf_op jit(solution)/shard_map/ppermute | solution.py:439
  18.1 0.0 collective-permute-done.2.rest_2_
  18.1 0.0 copy-done.3
  18.1 0.0 copy-start.4
  18.1 0.0 copy-start.1
  18.1 0.0 copy-start.2
  18.1 1.0 %shard_map.70 = (bf16[1536,128]{1,0:T(8,128)(2,1)S(1)}, f32[2,8,3072]{2,1,0:T(8,128)S(1)}, s32[4,128]{1,0:T(4,128)S(1)}) custom-call(s32[1,3072]{1,0:T(1,128)S(1)} %copy-done.3, bf16[224,384]{1,0:T(8,128)(2,1)S(1)} %collective-permute-done.rest_0_, bf16[224,384]{1,0:T(8,128)(2,1)S(1)} %collective-permute-done.1.rest_1_, ...), custom_call_target="tpu_custom_call" | custom-call | flops 1073741824 | bytes 8388608 | tf_op jit(solution)/shard_map/pallas_call | solution.py:524
  19.2 1.7 %collective-permute-done.3.rest_4_ = bf16[224,384]{1,0:T(8,128)(2,1)S(1)} collective-permute-done((bf16[224,384]{1,0:T(8,128)(2,1)S(1)}, bf16[224,384]{1,0:T(8,128)(2,1)S(1)}, u32[]{:S(2)}, u32[]{:S(2)}) %collective-permute-start.3) | collective-permute-done | bytes 172064 | tf_op jit(solution)/shard_map/ppermute | solution.py:439
  20.9 0.0 collective-permute-done.4.rest_5_
  20.9 1.5 %collective-permute-done.5.rest_6_ = bf16[224,384]{1,0:T(8,128)(2,1)S(1)} collective-permute-done((bf16[224,384]{1,0:T(8,128)(2,1)S(1)}, bf16[224,384]{1,0:T(8,128)(2,1)S(1)}, u32[]{:S(2)}, u32[]{:S(2)}) %collective-permute-start.5) | collective-permute-done | bytes 172064 | tf_op jit(solution)/shard_map/ppermute | solution.py:439
  22.4 0.6 %collective-permute-done.6.rest_7_ = bf16[224,384]{1,0:T(8,128)(2,1)S(1)} collective-permute-done((bf16[224,384]{1,0:T(8,128)(2,1)S(1)}, bf16[224,384]{1,0:T(8,128)(2,1)S(1)}, u32[]{:S(2)}, u32[]{:S(2)}) %collective-permute-start.6) | collective-permute-done | bytes 172064 | tf_op jit(solution)/shard_map/ppermute | solution.py:439
  23.1 9.5 %shard_map.71 = bf16[8,80,384]{2,1,0:T(8,128)(2,1)} custom-call(s32[1,3072]{1,0:T(1,128)S(1)} %copy-done.3, s32[4,128]{1,0:T(4,128)S(1)} %get-tuple-element.24.table_ref, f32[2,8,3072]{2,1,0:T(8,128)S(1)} %get-tuple-element.25.marks, bf16[1536,128]{1,0:T(8,128)(2,1)S(1)} %get-tuple-element.26.early_keys, bf16[224,384]{1,0:T(8,128)(2,1)S(1)} %collective-permute-done.rest_0_, ...), custom_call_target="tpu_custom_call" | custom-call | flops 905969664 | bytes 8388608 | tf_op jit(solution)/shard_map/pallas_call | solution.py:537
  32.6 3.5 %all-to-all-start = ((bf16[8,80,384]{2,1,0:T(8,128)(2,1)}), bf16[8,80,384]{2,1,0:T(8,128)(2,1)S(1)}, u32[]{:S(2)}, u32[]{:S(2)}) async-start(bf16[8,80,384]{2,1,0:T(8,128)(2,1)} %shard_map.71), calls=%async_computation | async-start | bytes 983040 | tf_op jit(solution)/shard_map/all_to_all | solution.py:449
  36.1 0.0 copy-done.4
  36.1 3.7 %collective-permute-start.9 = (bf16[4,1152]{1,0:T(4,128)(2,1)S(1)}, bf16[4,1152]{1,0:T(4,128)(2,1)S(1)}, u32[]{:S(2)}, u32[]{:S(2)}) collective-permute-start(bf16[4,1152]{1,0:T(4,128)(2,1)S(1)} %copy-done.4), channel_id=1, source_target_pairs={{0,3},{1,0},{2,1},{3,2},{4,7},{5,4},{6,5},{7,6},{8,11},{9,8},{10,9... | collective-permute-start | bytes 27656 | tf_op jit(solution)/shard_map/ppermute | solution.py:439
  39.8 0.0 collective-permute-start.8
  39.8 1.0 %collective-permute-start.7 = (bf16[4,1152]{1,0:T(4,128)(2,1)S(1)}, bf16[4,1152]{1,0:T(4,128)(2,1)S(1)}, u32[]{:S(2)}, u32[]{:S(2)}) collective-permute-start(bf16[4,1152]{1,0:T(4,128)(2,1)S(1)} %copy-done.4), channel_id=1, source_target_pairs={{0,1},{1,2},{2,3},{3,0},{4,5},{5,6},{6,7},{7,4},{8,9},{9,10},{10,1... | collective-permute-start | bytes 27656 | tf_op jit(solution)/shard_map/ppermute | solution.py:439
  40.8 0.4 collective-permute-done.9
  41.2 3.2 %collective-permute-done.8 = bf16[4,1152]{1,0:T(4,128)(2,1)S(1)} collective-permute-done((bf16[4,1152]{1,0:T(4,128)(2,1)S(1)}, bf16[4,1152]{1,0:T(4,128)(2,1)S(1)}, u32[]{:S(2)}, u32[]{:S(2)}) %collective-permute-start.8) | collective-permute-done | bytes 9248 | tf_op jit(solution)/shard_map/ppermute | solution.py:439
  44.4 0.9 %collective-permute-done.7 = bf16[4,1152]{1,0:T(4,128)(2,1)S(1)} collective-permute-done((bf16[4,1152]{1,0:T(4,128)(2,1)S(1)}, bf16[4,1152]{1,0:T(4,128)(2,1)S(1)}, u32[]{:S(2)}, u32[]{:S(2)}) %collective-permute-start.7) | collective-permute-done | bytes 9248 | tf_op jit(solution)/shard_map/ppermute | solution.py:439
  45.3 0.2 all-to-all-done.got_ref
  45.5 0.0 copy-done.1
  45.5 0.0 copy-done.2
  45.5 2.3 %shard_map.72 = (bf16[384,1152]{1,0:T(8,128)(2,1)}, f32[1,4]{1,0:T(1,128)}) custom-call(bf16[384,1152]{1,0:T(8,128)(2,1)S(1)} %bitcast.7, bf16[8,80,384]{2,1,0:T(8,128)(2,1)S(1)} %all-to-all-done.got_ref, bf16[576,1152]{1,0:T(8,128)(2,1)S(1)} %copy-done.2, bf16[16,1152]{1,0:T(8,128)(2,1)S(1)} %pad_maximum_fusion.text_ref), custom_call_target="tpu_custom_call" | custom-call | flops 509607936 | bytes 8388608 | tf_op jit(solution)/shard_map/pallas_call | solution.py:568
  (1 shorter events, 0.0 us)
Async XLA Ops:
  0.6 7.1 %copy-start = (bf16[1152,1728]{0,1:T(8,128)(2,1)S(1)}, bf16[1152,1728]{0,1:T(8,128)(2,1)}, u32[]{:S(2)}) copy-start(bf16[1152,1728]{0,1:T(8,128)(2,1)} %param.7) | copy-start | bytes 11943940
  0.6 17.5 %copy-start.3 = (s32[1,3072]{1,0:T(1,128)S(1)}, s32[1,3072]{1,0:T(1,128)}, u32[]{:S(2)}) copy-start(s32[1,3072]{1,0:T(1,128)} %ids_ref.5) | copy-start | bytes 36868
  3.8 10.0 %collective-permute-start = (bf16[224,384]{1,0:T(8,128)(2,1)S(1)}, bf16[224,384]{1,0:T(8,128)(2,1)S(1)}, u32[]{:S(2)}, u32[]{:S(2)}) collective-permute-start(bf16[224,384]{1,0:T(8,128)(2,1)S(1)} %get-tuple-element.18), channel_id=1, source_target_pairs={{0,24},{4,28},{8,16},{12,20},{16,8},{20,12},{24,0},{28,4},{1,25},{... | collective-permute-start | bytes 516104 | tf_op jit(solution)/shard_map/ppermute | solution.py:439
  7.7 8.5 %collective-permute-start.1 = (bf16[224,384]{1,0:T(8,128)(2,1)S(1)}, bf16[224,384]{1,0:T(8,128)(2,1)S(1)}, u32[]{:S(2)}, u32[]{:S(2)}) collective-permute-start(bf16[224,384]{1,0:T(8,128)(2,1)S(1)} %get-tuple-element.19), channel_id=1, source_target_pairs={{0,28},{4,24},{8,20},{12,16},{16,12},{20,8},{24,4},{28,0},{1,29},{... | collective-permute-start | bytes 516104 | tf_op jit(solution)/shard_map/ppermute | solution.py:439
  10.1 8.0 %collective-permute-start.2 = (bf16[224,384]{1,0:T(8,128)(2,1)S(1)}, bf16[224,384]{1,0:T(8,128)(2,1)S(1)}, u32[]{:S(2)}, u32[]{:S(2)}) collective-permute-start(bf16[224,384]{1,0:T(8,128)(2,1)S(1)} %get-tuple-element.22), channel_id=1, source_target_pairs={{0,4},{4,0},{8,12},{12,8},{16,20},{20,16},{24,28},{28,24},{1,5},{5... | collective-permute-start | bytes 516104 | tf_op jit(solution)/shard_map/ppermute | solution.py:439
  10.4 10.5 %collective-permute-start.3 = (bf16[224,384]{1,0:T(8,128)(2,1)S(1)}, bf16[224,384]{1,0:T(8,128)(2,1)S(1)}, u32[]{:S(2)}, u32[]{:S(2)}) collective-permute-start(bf16[224,384]{1,0:T(8,128)(2,1)S(1)} %get-tuple-element.27), channel_id=1, source_target_pairs={{0,8},{4,12},{8,0},{12,4},{16,24},{20,28},{24,16},{28,20},{1,9},{5... | collective-permute-start | bytes 516104 | tf_op jit(solution)/shard_map/ppermute | solution.py:439
  12.2 8.6 %collective-permute-start.4 = (bf16[224,384]{1,0:T(8,128)(2,1)S(1)}, bf16[224,384]{1,0:T(8,128)(2,1)S(1)}, u32[]{:S(2)}, u32[]{:S(2)}) collective-permute-start(bf16[224,384]{1,0:T(8,128)(2,1)S(1)} %get-tuple-element.28), channel_id=1, source_target_pairs={{0,16},{4,20},{8,24},{12,28},{16,0},{20,4},{24,8},{28,12},{1,17},{... | collective-permute-start | bytes 516104 | tf_op jit(solution)/shard_map/ppermute | solution.py:439
  13.8 8.7 %collective-permute-start.5 = (bf16[224,384]{1,0:T(8,128)(2,1)S(1)}, bf16[224,384]{1,0:T(8,128)(2,1)S(1)}, u32[]{:S(2)}, u32[]{:S(2)}) collective-permute-start(bf16[224,384]{1,0:T(8,128)(2,1)S(1)} %get-tuple-element.29), channel_id=1, source_target_pairs={{0,12},{4,8},{8,4},{12,0},{16,28},{20,24},{24,20},{28,16},{1,13},{... | collective-permute-start | bytes 516104 | tf_op jit(solution)/shard_map/ppermute | solution.py:439
  16.2 6.9 %collective-permute-start.6 = (bf16[224,384]{1,0:T(8,128)(2,1)S(1)}, bf16[224,384]{1,0:T(8,128)(2,1)S(1)}, u32[]{:S(2)}, u32[]{:S(2)}) collective-permute-start(bf16[224,384]{1,0:T(8,128)(2,1)S(1)} %get-tuple-element.30), channel_id=1, source_target_pairs={{0,20},{4,16},{8,28},{12,24},{16,4},{20,0},{24,12},{28,8},{1,21},{... | collective-permute-start | bytes 516104 | tf_op jit(solution)/shard_map/ppermute | solution.py:439
  18.1 18.0 %copy-start.4 = (bf16[4,1152]{1,0:T(4,128)(2,1)S(1)}, bf16[4,1152]{1,0:T(4,128)(2,1)}, u32[]{:S(2)}) copy-start(bf16[4,1152]{1,0:T(4,128)(2,1)} %param.9) | copy-start | bytes 27652
  18.1 27.4 %copy-start.1 = (bf16[1,384,1152]{2,1,0:T(8,128)(2,1)S(1)}, bf16[1,384,1152]{2,1,0:T(8,128)(2,1)}, u32[]{:S(2)}) copy-start(bf16[1,384,1152]{2,1,0:T(8,128)(2,1)} %param.5) | copy-start | bytes 2654212
  18.1 27.4 %copy-start.2 = (bf16[576,1152]{1,0:T(8,128)(2,1)S(1)}, bf16[576,1152]{1,0:T(8,128)(2,1)}, u32[]{:S(2)}) copy-start(bf16[576,1152]{1,0:T(8,128)(2,1)} %out_weight_ref.1) | copy-start | bytes 3981316
  32.6 12.9 %all-to-all-start = ((bf16[8,80,384]{2,1,0:T(8,128)(2,1)}), bf16[8,80,384]{2,1,0:T(8,128)(2,1)S(1)}, u32[]{:S(2)}, u32[]{:S(2)}) async-start(bf16[8,80,384]{2,1,0:T(8,128)(2,1)} %shard_map.71), calls=%async_computation | async-start | bytes 983040 | tf_op jit(solution)/shard_map/all_to_all | solution.py:449
  36.1 5.1 %collective-permute-start.9 = (bf16[4,1152]{1,0:T(4,128)(2,1)S(1)}, bf16[4,1152]{1,0:T(4,128)(2,1)S(1)}, u32[]{:S(2)}, u32[]{:S(2)}) collective-permute-start(bf16[4,1152]{1,0:T(4,128)(2,1)S(1)} %copy-done.4), channel_id=1, source_target_pairs={{0,3},{1,0},{2,1},{3,2},{4,7},{5,4},{6,5},{7,6},{8,11},{9,8},{10,9... | collective-permute-start | bytes 27656 | tf_op jit(solution)/shard_map/ppermute | solution.py:439
  39.8 4.6 %collective-permute-start.8 = (bf16[4,1152]{1,0:T(4,128)(2,1)S(1)}, bf16[4,1152]{1,0:T(4,128)(2,1)S(1)}, u32[]{:S(2)}, u32[]{:S(2)}) collective-permute-start(bf16[4,1152]{1,0:T(4,128)(2,1)S(1)} %copy-done.4), channel_id=1, source_target_pairs={{0,2},{1,3},{2,0},{3,1},{4,6},{5,7},{6,4},{7,5},{8,10},{9,11},{10,... | collective-permute-start | bytes 27656 | tf_op jit(solution)/shard_map/ppermute | solution.py:439
  39.8 5.5 %collective-permute-start.7 = (bf16[4,1152]{1,0:T(4,128)(2,1)S(1)}, bf16[4,1152]{1,0:T(4,128)(2,1)S(1)}, u32[]{:S(2)}, u32[]{:S(2)}) collective-permute-start(bf16[4,1152]{1,0:T(4,128)(2,1)S(1)} %copy-done.4), channel_id=1, source_target_pairs={{0,1},{1,2},{2,3},{3,0},{4,5},{5,6},{6,7},{7,4},{8,9},{9,10},{10,1... | collective-permute-start | bytes 27656 | tf_op jit(solution)/shard_map/ppermute | solution.py:439

commit v12 on v10

--- a/solution.py
+++ b/solution.py
@@ -129,9 +129,10 @@
         store_by_core(core, blocks, *out_refs[2 * step : 2 * step + 2])
 
 
-def find_starts(images, ids, starts):
-    for image in range(images + 1):
-        starts[image] = jnp.sum((ids < image).astype(jnp.int32))
+def count_before(images, ids):
+    image = lax.broadcasted_iota(jnp.int32, (rounded_up(images + 1, SPARE), ids.shape[1]), 0)
+    before = jnp.sum((ids < image).astype(jnp.int32), axis=1, keepdims=True)
+    return jnp.broadcast_to(before, (before.shape[0], LANES))
 
 
 def write_marks(images, ids, marks):
@@ -197,10 +198,10 @@
         first = pl.multiple_of(at * tile, tile)
         labels = ids_ref[:, pl.ds(pl.multiple_of(query_base + first, LANES), tile)]
         probs = jnp.exp2((scores[...] - tops[...]) * (size ** (-0.5) * math.log2(math.e)))
+        share = 1.0 / jnp.sum(probs, axis=0, keepdims=True)
         weighted = jnp.dot(
             values[:, window_of(image)], probs.astype(jnp.bfloat16), preferred_element_type=jnp.float32
         )
-        share = 1.0 / weighted[size : size + 1]
         place = (slice(None), pl.ds(first, tile))
         attended[place] = jnp.where(labels == image, weighted * share, attended[place])
 
@@ -245,16 +246,10 @@
     queries[PADDED:, there] = jnp.zeros((LANES - PADDED, block_ref.shape[1]), jnp.bfloat16)
 
 
-def store_values(block_ref, values, here):
-    edge = block_ref[PADDED - 16 : PADDED].astype(jnp.float32)
-    ones = jnp.ones((SPARE, edge.shape[1]), jnp.float32)
-    values[0 : PADDED - 16, here] = block_ref[0 : PADDED - 16]
-    values[PADDED - 16 : PADDED, here] = jnp.concatenate([edge[:SPARE], ones], axis=0).astype(jnp.bfloat16)
-
-
 def prepare_kernel(images, halo, ids_ref, *rest):
-    got_refs, (keys, marks) = rest[: len(EARLY)], rest[len(EARLY) :]
+    got_refs, (keys, marks, before) = rest[: len(EARLY)], rest[len(EARLY) :]
     count = got_refs[0].shape[1]
+    before[...] = count_before(images, ids_ref[...])
     write_marks(images, ids_ref[...], marks)
     own = lax.rem(lax.axis_index("grp"), HEADS)
     for step, (by, ref) in enumerate(zip(EARLY, got_refs)):
@@ -263,18 +258,21 @@
         keys[step * count : (step + 1) * count, :] = turned_keys(marks[0, :, here], ref)
 
 
-def attend_kernel(images, piggy, halo, ids_ref, marks, early_keys, *rest):
+def attend_kernel(images, piggy, halo, ids_ref, before_ref, marks, early_keys, *rest):
     got_refs, rest = rest[:HEADS], rest[HEADS:]
     if halo:
         left_ref, right_ref, *rest = rest
-    out_ref, keys, values, queries, attended, *work, starts = rest
+    out_refs, rest = rest[:HEADS], rest[HEADS:]
+    keys, values, queries, attended, *work, starts = rest
     count = got_refs[0].shape[1]
     padded = attended.shape[0]
     size = padded - SPARE
     total_rows = HEADS * count
     length = ids_ref.shape[1]
     ids = ids_ref[...]
-    find_starts(images, ids, starts)
+    before = before_ref[...]
+    for image in range(images + 1):
+        starts[image] = before[image, 0]
 
     own = lax.rem(lax.axis_index("grp"), HEADS)
     for step, (by, ref) in enumerate(zip(EARLY + LATE, got_refs)):
@@ -285,12 +283,12 @@
             keys[here, :] = early_keys[step * count : (step + 1) * count, :]
         else:
             keys[here, :] = turned_keys(marks[0, :, here], ref)
-        store_values(ref, values, here)
+        values[:, here] = ref[0:PADDED]
         store_queries(marks[1, :, here], ref, queries, there)
     if halo:
         for ref, here in ((left_ref, slice(0, halo)), (right_ref, slice(length - halo, length))):
             keys[here, :] = turned_keys(marks[0, :, here], ref)
-            store_values(ref, values, here)
+            values[:, here] = ref[0:PADDED]
     attend_images(images, ids_ref, keys, values, queries, attended, work, starts, halo)
 
     odd_head = lax.rem(own, 2) == 1
@@ -315,31 +313,28 @@
         )
     else:
         spare = jnp.zeros((SPARE, count), jnp.float32)
-    for source in range(HEADS):
-        block = placed(attended[:, source * count : (source + 1) * count], spare)
-        out_ref[source] = block.astype(jnp.bfloat16)
-
-
-def joined_heads(got_ref, out_weight_ref, flat, weight):
-    padded = got_ref.shape[1]
-    size = padded - SPARE
+    for by, out_ref in zip(ORDER, out_refs):
+        there = pl.multiple_of(jnp.bitwise_xor(own, by) * count, LANES)
+        out_ref[...] = placed(attended[:, pl.ds(there, count)], spare).astype(jnp.bfloat16)
+
+
+def joined_heads(got_refs, out_weight_ref, flat, weight):
+    own = lax.rem(lax.axis_index("grp"), HEADS)
     spares = []
-    for head in range(HEADS):
-        at = head * padded
-        from_row = head * size - (SPARE if head % 2 else 0)
-        weight[at : at + padded] = out_weight_ref[from_row : from_row + padded]
-        edge = 0 if head % 2 else padded - 16
-        rest = slice(16, padded) if head % 2 else slice(0, padded - 16)
-        mixed_rows = got_ref[head, edge : edge + 16].astype(jnp.float32)
-        nothing = jnp.zeros((SPARE, mixed_rows.shape[1]), jnp.float32)
-        if head % 2:
-            spares.append(mixed_rows[:SPARE])
-            block = jnp.concatenate([nothing, mixed_rows[SPARE:]], axis=0)
-        else:
-            spares.append(mixed_rows[SPARE:])
-            block = jnp.concatenate([mixed_rows[:SPARE], nothing], axis=0)
-        flat[at + edge : at + edge + 16] = block.astype(jnp.bfloat16)
-        flat[at + rest.start : at + rest.stop] = got_ref[head, rest]
+    for step, (by, got_ref) in enumerate(zip(ORDER, got_refs)):
+        head = jnp.bitwise_xor(own, by)
+        odd = lax.rem(head, 2)
+        first = pl.multiple_of(lax.div(head, 2) * (2 * SIZE) + odd * (SIZE - SPARE), 16)
+        at = step * PADDED
+        weight[at : at + PADDED] = out_weight_ref[pl.ds(first, PADDED), :]
+        top = got_ref[0:16].astype(jnp.float32)
+        bottom = got_ref[PADDED - 16 : PADDED].astype(jnp.float32)
+        spares.append(jnp.where(odd == 1, top[:SPARE], bottom[SPARE:]))
+        top = jnp.concatenate([jnp.where(odd == 1, 0.0, top[:SPARE]), top[SPARE:]], axis=0)
+        bottom = jnp.concatenate([bottom[:SPARE], jnp.where(odd == 1, bottom[SPARE:], 0.0)], axis=0)
+        flat[at : at + 16] = top.astype(jnp.bfloat16)
+        flat[at + 16 : at + PADDED - 16] = got_ref[16 : PADDED - 16]
+        flat[at + PADDED - 16 : at + PADDED] = bottom.astype(jnp.bfloat16)
     return spares
 
 
@@ -366,17 +361,21 @@
     return jnp.maximum(logits, 0.0) + jnp.log1p(jnp.exp(-jnp.abs(logits)))
 
 
-def finish_kernel(images, rows_ref, got_ref, out_weight_ref, text_ref, mixed_ref, loss_ref, flat, weight, turned, mixed, sems, pooled_heads):
-    padded = got_ref.shape[1]
-    spares = joined_heads(got_ref, out_weight_ref, flat, weight)
+def finish_kernel(images, rows_ref, out_weight_ref, text_ref, *rest):
+    got_refs, rest = rest[:HEADS], rest[HEADS:]
+    mixed_ref, loss_ref, flat, weight, turned, mixed, sems, pooled_heads, patch_sums = rest
+    spares = joined_heads(got_refs, out_weight_ref, flat, weight)
     copies = send_mixed_rows(rows_ref, flat, weight, turned, mixed, mixed_ref, sems)
-    for head in range(HEADS):
-        pooled_heads[:, head * padded : (head + 1) * padded] = spares[head][:, 0:padded]
+    own = lax.rem(lax.axis_index("grp"), HEADS)
+    patch_sums[:, HEADS * LANES :] = spares[0][:, 2 * LANES :]
+    for step, (by, spare) in enumerate(zip(ORDER, spares)):
+        pooled_heads[:, step * PADDED : (step + 1) * PADDED] = spare[:, 0:PADDED]
+        head = jnp.bitwise_xor(own, by)
+        patch_sums[:, pl.ds(pl.multiple_of(head * LANES, LANES), LANES)] = spare[:, LANES : 2 * LANES]
     pooled = jnp.dot(
         pooled_heads[...].astype(jnp.bfloat16), weight[...], preferred_element_type=jnp.float32
     )
-    patch_sums = [spare[:, LANES : 2 * LANES] for spare in spares] + [spares[0][:, 2 * LANES :]]
-    pooled = pooled + jnp.concatenate(patch_sums, axis=1)
+    pooled = pooled + patch_sums[...]
     pooled = pooled + pltpu.roll(pooled, images, axis=0)
     image_vecs = unit_rows(pooled)
     text_vecs = unit_rows(text_ref[...].astype(jnp.float32))
@@ -395,8 +394,10 @@
         copy.wait()
 
 
-def mix_kernel(rows_ref, got_ref, out_weight_ref, mixed_ref, flat, weight, turned, mixed, sems):
-    joined_heads(got_ref, out_weight_ref, flat, weight)
+def mix_kernel(rows_ref, out_weight_ref, *rest):
+    got_refs, rest = rest[:HEADS], rest[HEADS:]
+    mixed_ref, flat, weight, turned, mixed, sems = rest
+    joined_heads(got_refs, out_weight_ref, flat, weight)
     for copy in send_mixed_rows(rows_ref, flat, weight, turned, mixed, mixed_ref, sems):
         copy.wait()
 
@@ -433,8 +434,10 @@
     return [texts] + [moved(texts, "blk", [(i, (i + by) % peers) for i in range(peers)]) for by in shifts]
 
 
-def exchanged(blocks, groups):
-    return lax.all_to_all(blocks, "grp", 0, 0, axis_index_groups=groups, tiled=True)
+def traded(blocks):
+    peers = range(lax.axis_size("grp"))
+    trades = {by: moved(blocks[by], "grp", [(i, i ^ by) for i in peers]) for by in ORDER if by}
+    return {**trades, 0: blocks[0]}
 
 
 def local(patches, segment_ids, qkv_weight, out_weight, text_embed):
@@ -447,7 +450,6 @@
     group_size = lax.axis_size("grp")
     parts = group_size // HEADS
     piggy = parts == 1 and 2 * images == SPARE and count >= depth - (HEADS - 2) * LANES
-    groups = None if parts == 1 else [list(range(p * HEADS, (p + 1) * HEADS)) for p in range(parts)]
     bf16, f32 = jnp.bfloat16, jnp.float32
     shape = jax.ShapeDtypeStruct
 
@@ -476,9 +478,7 @@
         2 * count * depth * 18 * size,
     )(normed, sums, turned_weight)
     sent = dict(zip((6, 7, 2, 3, 4, 5, 0, 1), sent))
-    got = {0: sent[0]}
-    for by in ORDER[:-1]:
-        got[by] = moved(sent[by], "grp", [(i, i ^ by) for i in range(group_size)])
+    got = traded(sent)
 
     length = HEADS * count
     halo = 0
@@ -507,17 +507,24 @@
     reach = length + 2 * halo
     window = min(rounded_up(MAXP + LANES - 1, LANES), reach)
     tile = 2 * LANES
-    early_keys, marks = call(
+    early_keys, marks, before = call(
         functools.partial(prepare_kernel, images, halo),
-        (shape((len(EARLY) * count, LANES), bf16), shape((2, SPARE, reach), f32)),
+        (
+            shape((len(EARLY) * count, LANES), bf16),
+            shape((2, SPARE, reach), f32),
+            shape((rounded_up(images + 1, SPARE), LANES), jnp.int32),
+        ),
         [],
         in_vmem(1 + len(EARLY)),
         1 << 30,
     )(near_ids, *[got[by] for by in EARLY])
-    operands = [near_ids, marks, early_keys, *[got[by] for by in EARLY + LATE], *halos]
+    text_embed, marks = lax.optimization_barrier((text_embed, marks))
+    texts, marks = lax.optimization_barrier((all_texts(text_embed), marks))
+    texts = jnp.concatenate(texts, axis=0)
+    operands = [near_ids, before, marks, early_keys, *[got[by] for by in EARLY + LATE], *halos]
     answers = call(
         functools.partial(attend_kernel, images, piggy, halo),
-        shape((HEADS, padded, count), bf16),
+        (shape((padded, count), bf16),) * HEADS,
         [
             pltpu.VMEM((reach, LANES), bf16),
             pltpu.VMEM((padded, reach), bf16),
@@ -532,9 +539,8 @@
         in_vmem(len(operands)),
         4 * size * length * MAXP,
     )(*operands)
-    back_home = exchanged(answers, groups)
-    text_embed, _ = lax.optimization_barrier((text_embed, answers))
-    texts = jnp.concatenate(all_texts(text_embed), axis=0)
+    home = traded(dict(zip(ORDER, answers)))
+    home = [home[by] for by in ORDER]
 
     joined = [
         pltpu.VMEM((HEADS * padded, count), bf16),
@@ -548,14 +554,14 @@
         mixed, row_loss = call(
             functools.partial(finish_kernel, images),
             (shape((count, depth), bf16), shape((1, images), f32)),
-            joined + [pltpu.VMEM((SPARE, HEADS * padded), f32)],
-            in_vmem(4),
+            joined + [pltpu.VMEM((SPARE, HEADS * padded), f32), pltpu.VMEM((SPARE, depth), f32)],
+            in_vmem(3 + HEADS),
             flops,
             (hbm, pl.BlockSpec(memory_space=pltpu.VMEM)),
-        )(rows, back_home, out_weight, texts)
+        )(rows, out_weight, texts, *home)
         return (mixed[None], row_loss[0])
-    mixed = call(mix_kernel, shape((count, depth), bf16), joined, in_vmem(3), flops, hbm)(
-        rows, back_home, out_weight
+    mixed = call(mix_kernel, shape((count, depth), bf16), joined, in_vmem(2 + HEADS), flops, hbm)(
+        rows, out_weight, *home
     )
     own_ids = lax.dynamic_slice_in_dim(segment_ids[0], lax.axis_index("grp") * count, count)
     onehot = (own_ids[None, :] == jnp.arange(images, dtype=jnp.int32)[:, None]).astype(bf16)

time: 47.4 us -> 53.3 us (1.12)
  waiting for transfers between devices: 11.4 us -> 15.4 us
  starting transfers between devices: 18.1 us -> 21.1 us
  Pallas kernels: 16.8 us -> 16 us
    ppermute x10 -> x17, starting transfers between devices: 14.6 us -> 21.1 us  [moved(): return lax.ppermute(value, axis, pairs)]
    ppermute x10 -> x17, waiting for transfers between devices: 11.3 us -> 15.4 us  [moved(): return lax.ppermute(value, axis, pairs)]
    all_to_all x1 -> x0, starting transfers between devices: 3.49 us -> none  [exchanged(): lax.all_to_all(blocks, 'grp', 0, 0, axis_index_groups=groups, tiled=True)]
    pallas_call x1, Pallas kernels: 8.79 us -> 7.9 us  [local(): call(functools.partial(attend_kernel, images, piggy, halo), (shape((padde...]
  transfers between devices with their start and end apart: 11 -> 17, of which waited for: 7 -> 9; matrix products, arithmetic and copies ran while one was open for 0% -> 0% of each run, Pallas kernels for 5% -> 5%
where the time goes in v12:
time: 53.3 us
  starting transfers between devices  21.1 us (40%)
  Pallas kernels  16 us (30%)
  waiting for transfers between devices  15.4 us (29%)
  between operations  0.74 us (1%)
    ppermute x17, starting transfers between devices, moved(): return lax.ppermute(value, axis, pairs)  21.1 us
    ppermute x17, waiting for transfers between devices, moved(): return lax.ppermute(value, axis, pairs)  15.4 us
    pallas_call x1, Pallas kernels, local(): call(functools.partial(attend_kernel, images, piggy, halo), (shape((padde...  7.9 us
    pallas_call x1, Pallas kernels, local(): call(functools.partial(far_kernel, images, piggy), (shape((depth, count),...  3.12 us
    pallas_call x1, Pallas kernels, local(): call(functools.partial(finish_kernel, images), (shape((count, depth), bf1...  2.36 us
    pallas_call x1, Pallas kernels, local(): call(functools.partial(near_kernel, piggy), (block,) * 6, [], in_vmem(3),...  2.35 us
  transfers between devices with their start and end apart: 17, of which 9 were waited for; matrix products, arithmetic and copies ran while one was open for 0% of the time, Pallas kernels for 5%

profile of v12, /device:TPU:0, one launch (start us, length us, event | category | flops | bytes accessed | tf_op | source)
XLA Modules:
  0.0 53.3 jit_solution(3908019332748782130)
XLA Ops:
  0.6 0.0 copy-start
  0.6 0.0 copy-start.3
  0.6 3.1 %shard_map.68 = (bf16[1152,384]{1,0:T(8,128)(2,1)S(1)}, f32[8,1152]{1,0:T(8,128)S(1)}, bf16[224,384]{1,0:T(8,128)(2,1)S(1)}, bf16[224,384]{1,0:T(8,128)(2,1)S(1)}) custom-call(s32[1,3072]{1,0:T(1,128)} %ids_ref.5, bf16[384,1152]{1,0:T(8,128)(2,1)} %bitcast.6, bf16[1728,1152]{1,0:T(8,128)(2,1)} %bitcast.4), custom_call_target="tpu_custom_call" | custom-call | flops 382205952 | bytes 8388608 | tf_op jit(solution)/shard_map/pallas_call | solution.py:459
  3.8 4.0 %collective-permute-start = (bf16[224,384]{1,0:T(8,128)(2,1)S(1)}, bf16[224,384]{1,0:T(8,128)(2,1)S(1)}, u32[]{:S(2)}, u32[]{:S(2)}) collective-permute-start(bf16[224,384]{1,0:T(8,128)(2,1)S(1)} %get-tuple-element.32), channel_id=1, source_target_pairs={{0,24},{4,28},{8,16},{12,20},{16,8},{20,12},{24,0},{28,4},{1,25},{... | collective-permute-start | bytes 516104 | tf_op jit(solution)/shard_map/ppermute | solution.py:428
  7.7 0.0 collective-permute-start.1
  7.7 0.0 copy-done
  7.7 0.0 copy-start.4
  7.7 2.3 %shard_map.69 = (bf16[224,384]{1,0:T(8,128)(2,1)S(1)}, bf16[224,384]{1,0:T(8,128)(2,1)S(1)}, bf16[224,384]{1,0:T(8,128)(2,1)S(1)}, bf16[224,384]{1,0:T(8,128)(2,...) custom-call(bf16[1152,384]{1,0:T(8,128)(2,1)S(1)} %get-tuple-element.34.normed_ref, ...), custom_call_target="tpu_custom_call" | custom-call | flops 1146617856 | bytes 8388608 | tf_op jit(solution)/shard_map/pallas_call | solution.py:473
  10.1 0.0 copy-start.1
  10.1 0.0 copy-start.2
  10.1 0.3 collective-permute-start.2
  10.4 1.9 %collective-permute-start.6 = (bf16[224,384]{1,0:T(8,128)(2,1)S(1)}, bf16[224,384]{1,0:T(8,128)(2,1)S(1)}, u32[]{:S(2)}, u32[]{:S(2)}) collective-permute-start(bf16[224,384]{1,0:T(8,128)(2,1)S(1)} %get-tuple-element.48), channel_id=1, source_target_pairs={{0,8},{4,12},{8,0},{12,4},{16,24},{20,28},{24,16},{28,20},{1,9},{5... | collective-permute-start | bytes 516104 | tf_op jit(solution)/shard_map/ppermute | solution.py:428
  12.3 1.5 %collective-permute-start.7 = (bf16[224,384]{1,0:T(8,128)(2,1)S(1)}, bf16[224,384]{1,0:T(8,128)(2,1)S(1)}, u32[]{:S(2)}, u32[]{:S(2)}) collective-permute-start(bf16[224,384]{1,0:T(8,128)(2,1)S(1)} %get-tuple-element.49), channel_id=1, source_target_pairs={{0,16},{4,20},{8,24},{12,28},{16,0},{20,4},{24,8},{28,12},{1,17},{... | collective-permute-start | bytes 516104 | tf_op jit(solution)/shard_map/ppermute | solution.py:428
  13.8 0.0 collective-permute-done.rest_0_
  13.8 0.0 collective-permute-start.8
  13.8 2.4 %collective-permute-done.1.rest_1_ = bf16[224,384]{1,0:T(8,128)(2,1)S(1)} collective-permute-done((bf16[224,384]{1,0:T(8,128)(2,1)S(1)}, bf16[224,384]{1,0:T(8,128)(2,1)S(1)}, u32[]{:S(2)}, u32[]{:S(2)}) %collective-permute-start.1) | collective-permute-done | bytes 172064 | tf_op jit(solution)/shard_map/ppermute | solution.py:428
  16.2 1.9 %collective-permute-start.9 = (bf16[224,384]{1,0:T(8,128)(2,1)S(1)}, bf16[224,384]{1,0:T(8,128)(2,1)S(1)}, u32[]{:S(2)}, u32[]{:S(2)}) collective-permute-start(bf16[224,384]{1,0:T(8,128)(2,1)S(1)} %get-tuple-element.51), channel_id=1, source_target_pairs={{0,20},{4,16},{8,28},{12,24},{16,4},{20,0},{24,12},{28,8},{1,21},{... | collective-permute-start | bytes 516104 | tf_op jit(solution)/shard_map/ppermute | solution.py:428
  18.1 0.0 collective-permute-done.2.rest_2_
  18.1 0.0 copy-done.3
  18.1 0.2 shard_map.70
  18.3 0.0 copy-done.4
  18.4 3.7 %collective-permute-start.5 = (bf16[4,1152]{1,0:T(4,128)(2,1)S(1)}, bf16[4,1152]{1,0:T(4,128)(2,1)S(1)}, u32[]{:S(2)}, u32[]{:S(2)}) collective-permute-start(bf16[4,1152]{1,0:T(4,128)(2,1)S(1)} %copy-done.4), channel_id=1, source_target_pairs={{0,3},{1,0},{2,1},{3,2},{4,7},{5,4},{6,5},{7,6},{8,11},{9,8},{10,9... | collective-permute-start | bytes 27656 | tf_op jit(solution)/shard_map/ppermute | solution.py:428
  22.0 1.4 %collective-permute-done.5 = bf16[4,1152]{1,0:T(4,128)(2,1)S(1)} collective-permute-done((bf16[4,1152]{1,0:T(4,128)(2,1)S(1)}, bf16[4,1152]{1,0:T(4,128)(2,1)S(1)}, u32[]{:S(2)}, u32[]{:S(2)}) %collective-permute-start.5) | collective-permute-done | bytes 9248 | tf_op jit(solution)/shard_map/ppermute | solution.py:428
  23.4 1.3 %collective-permute-start.4 = (bf16[4,1152]{1,0:T(4,128)(2,1)S(1)}, bf16[4,1152]{1,0:T(4,128)(2,1)S(1)}, u32[]{:S(2)}, u32[]{:S(2)}) collective-permute-start(bf16[4,1152]{1,0:T(4,128)(2,1)S(1)} %copy-done.4), channel_id=1, source_target_pairs={{0,2},{1,3},{2,0},{3,1},{4,6},{5,7},{6,4},{7,5},{8,10},{9,11},{10,... | collective-permute-start | bytes 27656 | tf_op jit(solution)/shard_map/ppermute | solution.py:428
  24.7 3.3 %collective-permute-done.4 = bf16[4,1152]{1,0:T(4,128)(2,1)S(1)} collective-permute-done((bf16[4,1152]{1,0:T(4,128)(2,1)S(1)}, bf16[4,1152]{1,0:T(4,128)(2,1)S(1)}, u32[]{:S(2)}, u32[]{:S(2)}) %collective-permute-start.4) | collective-permute-done | bytes 9248 | tf_op jit(solution)/shard_map/ppermute | solution.py:428
  27.9 1.7 %collective-permute-start.3 = (bf16[4,1152]{1,0:T(4,128)(2,1)S(1)}, bf16[4,1152]{1,0:T(4,128)(2,1)S(1)}, u32[]{:S(2)}, u32[]{:S(2)}) collective-permute-start(bf16[4,1152]{1,0:T(4,128)(2,1)S(1)} %copy-done.4), channel_id=1, source_target_pairs={{0,1},{1,2},{2,3},{3,0},{4,5},{5,6},{6,7},{7,4},{8,9},{9,10},{10,1... | collective-permute-start | bytes 27656 | tf_op jit(solution)/shard_map/ppermute | solution.py:428
  29.7 4.0 %collective-permute-done.3 = bf16[4,1152]{1,0:T(4,128)(2,1)S(1)} collective-permute-done((bf16[4,1152]{1,0:T(4,128)(2,1)S(1)}, bf16[4,1152]{1,0:T(4,128)(2,1)S(1)}, u32[]{:S(2)}, u32[]{:S(2)}) %collective-permute-start.3) | collective-permute-done | bytes 9248 | tf_op jit(solution)/shard_map/ppermute | solution.py:428
  33.7 0.0 collective-permute-done.6.rest_4_
  33.7 0.0 collective-permute-done.7.rest_5_
  33.7 0.0 collective-permute-done.8.rest_6_
  33.7 0.0 collective-permute-done.9.rest_7_
  33.7 7.9 %shard_map.71 = (bf16[80,384]{1,0:T(8,128)(2,1)S(1)}, bf16[80,384]{1,0:T(8,128)(2,1)S(1)}, bf16[80,384]{1,0:T(8,128)(2,1)S(1)}, bf16[80,384]{1,0:T(8,128)(2,1)S(...) custom-call(s32[1,3072]{1,0:T(1,128)S(1)} %copy-done.3, ...), custom_call_target="tpu_custom_call" | custom-call | flops 905969664 | bytes 8388608 | tf_op jit(solution)/shard_map/pallas_call | solution.py:525
  41.6 1.5 %collective-permute-start.10 = (bf16[80,384]{1,0:T(8,128)(2,1)S(1)}, bf16[80,384]{1,0:T(8,128)(2,1)S(1)}, u32[]{:S(2)}, u32[]{:S(2)}) collective-permute-start(bf16[80,384]{1,0:T(8,128)(2,1)S(1)} %get-tuple-element.52), channel_id=1, source_target_pairs={{0,24},{4,28},{8,16},{12,20},{16,8},{20,12},{24,0},{28,4},{1,25},{... | collective-permute-start | bytes 184328 | tf_op jit(solution)/shard_map/ppermute | solution.py:428
  43.1 0.0 collective-permute-start.11
  43.1 0.2 collective-permute-start.12
  43.3 1.8 %collective-permute-start.13 = (bf16[80,384]{1,0:T(8,128)(2,1)S(1)}, bf16[80,384]{1,0:T(8,128)(2,1)S(1)}, u32[]{:S(2)}, u32[]{:S(2)}) collective-permute-start(bf16[80,384]{1,0:T(8,128)(2,1)S(1)} %get-tuple-element.55), channel_id=1, source_target_pairs={{0,16},{4,20},{8,24},{12,28},{16,0},{20,4},{24,8},{28,12},{1,17},{... | collective-permute-start | bytes 184328 | tf_op jit(solution)/shard_map/ppermute | solution.py:428
  45.2 0.9 %collective-permute-start.14 = (bf16[80,384]{1,0:T(8,128)(2,1)S(1)}, bf16[80,384]{1,0:T(8,128)(2,1)S(1)}, u32[]{:S(2)}, u32[]{:S(2)}) collective-permute-start(bf16[80,384]{1,0:T(8,128)(2,1)S(1)} %get-tuple-element.56), channel_id=1, source_target_pairs={{0,12},{4,8},{8,4},{12,0},{16,28},{20,24},{24,20},{28,16},{1,13},{... | collective-permute-start | bytes 184328 | tf_op jit(solution)/shard_map/ppermute | solution.py:428
  46.1 0.7 %collective-permute-done.10.rest_0_ = bf16[80,384]{1,0:T(8,128)(2,1)S(1)} collective-permute-done((bf16[80,384]{1,0:T(8,128)(2,1)S(1)}, bf16[80,384]{1,0:T(8,128)(2,1)S(1)}, u32[]{:S(2)}, u32[]{:S(2)}) %collective-permute-start.10) | collective-permute-done | bytes 61472 | tf_op jit(solution)/shard_map/ppermute | solution.py:428
  46.8 0.5 collective-permute-start.15
  47.3 1.0 %collective-permute-done.11.rest_1_ = bf16[80,384]{1,0:T(8,128)(2,1)S(1)} collective-permute-done((bf16[80,384]{1,0:T(8,128)(2,1)S(1)}, bf16[80,384]{1,0:T(8,128)(2,1)S(1)}, u32[]{:S(2)}, u32[]{:S(2)}) %collective-permute-start.11) | collective-permute-done | bytes 61472 | tf_op jit(solution)/shard_map/ppermute | solution.py:428
  48.3 0.0 collective-permute-start.16
  48.3 0.0 collective-permute-done.12.rest_2_
  48.3 0.6 %collective-permute-done.13.rest_3_ = bf16[80,384]{1,0:T(8,128)(2,1)S(1)} collective-permute-done((bf16[80,384]{1,0:T(8,128)(2,1)S(1)}, bf16[80,384]{1,0:T(8,128)(2,1)S(1)}, u32[]{:S(2)}, u32[]{:S(2)}) %collective-permute-start.13) | collective-permute-done | bytes 61472 | tf_op jit(solution)/shard_map/ppermute | solution.py:428
  48.9 0.4 collective-permute-done.14.rest_4_
  49.3 1.6 %collective-permute-done.15.rest_5_ = bf16[80,384]{1,0:T(8,128)(2,1)S(1)} collective-permute-done((bf16[80,384]{1,0:T(8,128)(2,1)S(1)}, bf16[80,384]{1,0:T(8,128)(2,1)S(1)}, u32[]{:S(2)}, u32[]{:S(2)}) %collective-permute-start.15) | collective-permute-done | bytes 61472 | tf_op jit(solution)/shard_map/ppermute | solution.py:428
  50.9 0.0 collective-permute-done.16.rest_6_
  50.9 0.0 copy-done.1
  50.9 0.0 copy-done.2
  50.9 2.4 %shard_map.72 = (bf16[384,1152]{1,0:T(8,128)(2,1)}, f32[1,4]{1,0:T(1,128)}) custom-call(bf16[384,1152]{1,0:T(8,128)(2,1)S(1)} %bitcast.7, bf16[576,1152]{1,0:T(8,128)(2,1)S(1)} %copy-done.2, bf16[16,1152]{1,0:T(8,128)(2,1)S(1)} %pad_maximum_fusion.text_ref, bf16[80,384]{1,0:T(8,128)(2,1)S(1)} %collective-permute-done.10.rest_0_, ...), custom_call_target="tpu_custom_call" | custom-call | flops 509607936 | bytes 8388608 | tf_op jit(solution)/shard_map/pallas_call | solution.py:554
  (1 shorter events, 0.0 us)
Async XLA Ops:
  0.6 7.1 %copy-start = (bf16[1152,1728]{0,1:T(8,128)(2,1)S(1)}, bf16[1152,1728]{0,1:T(8,128)(2,1)}, u32[]{:S(2)}) copy-start(bf16[1152,1728]{0,1:T(8,128)(2,1)} %param.7) | copy-start | bytes 11943940
  0.6 17.5 %copy-start.3 = (s32[1,3072]{1,0:T(1,128)S(1)}, s32[1,3072]{1,0:T(1,128)}, u32[]{:S(2)}) copy-start(s32[1,3072]{1,0:T(1,128)} %ids_ref.5) | copy-start | bytes 36868
  3.8 10.0 %collective-permute-start = (bf16[224,384]{1,0:T(8,128)(2,1)S(1)}, bf16[224,384]{1,0:T(8,128)(2,1)S(1)}, u32[]{:S(2)}, u32[]{:S(2)}) collective-permute-start(bf16[224,384]{1,0:T(8,128)(2,1)S(1)} %get-tuple-element.32), channel_id=1, source_target_pairs={{0,24},{4,28},{8,16},{12,20},{16,8},{20,12},{24,0},{28,4},{1,25},{... | collective-permute-start | bytes 516104 | tf_op jit(solution)/shard_map/ppermute | solution.py:428
  7.7 8.5 %collective-permute-start.1 = (bf16[224,384]{1,0:T(8,128)(2,1)S(1)}, bf16[224,384]{1,0:T(8,128)(2,1)S(1)}, u32[]{:S(2)}, u32[]{:S(2)}) collective-permute-start(bf16[224,384]{1,0:T(8,128)(2,1)S(1)} %get-tuple-element.33), channel_id=1, source_target_pairs={{0,28},{4,24},{8,20},{12,16},{16,12},{20,8},{24,4},{28,0},{1,29},{... | collective-permute-start | bytes 516104 | tf_op jit(solution)/shard_map/ppermute | solution.py:428
  7.7 10.6 %copy-start.4 = (bf16[4,1152]{1,0:T(4,128)(2,1)S(1)}, bf16[4,1152]{1,0:T(4,128)(2,1)}, u32[]{:S(2)}) copy-start(bf16[4,1152]{1,0:T(4,128)(2,1)} %param.9) | copy-start | bytes 27652
  10.1 40.8 %copy-start.1 = (bf16[1,384,1152]{2,1,0:T(8,128)(2,1)S(1)}, bf16[1,384,1152]{2,1,0:T(8,128)(2,1)}, u32[]{:S(2)}) copy-start(bf16[1,384,1152]{2,1,0:T(8,128)(2,1)} %param.5) | copy-start | bytes 2654212
  10.1 40.8 %copy-start.2 = (bf16[576,1152]{1,0:T(8,128)(2,1)S(1)}, bf16[576,1152]{1,0:T(8,128)(2,1)}, u32[]{:S(2)}) copy-start(bf16[576,1152]{1,0:T(8,128)(2,1)} %out_weight_ref.1) | copy-start | bytes 3981316
  10.1 8.0 %collective-permute-start.2 = (bf16[224,384]{1,0:T(8,128)(2,1)S(1)}, bf16[224,384]{1,0:T(8,128)(2,1)S(1)}, u32[]{:S(2)}, u32[]{:S(2)}) collective-permute-start(bf16[224,384]{1,0:T(8,128)(2,1)S(1)} %get-tuple-element.36), channel_id=1, source_target_pairs={{0,4},{4,0},{8,12},{12,8},{16,20},{20,16},{24,28},{28,24},{1,5},{5... | collective-permute-start | bytes 516104 | tf_op jit(solution)/shard_map/ppermute | solution.py:428
  10.4 23.3 %collective-permute-start.6 = (bf16[224,384]{1,0:T(8,128)(2,1)S(1)}, bf16[224,384]{1,0:T(8,128)(2,1)S(1)}, u32[]{:S(2)}, u32[]{:S(2)}) collective-permute-start(bf16[224,384]{1,0:T(8,128)(2,1)S(1)} %get-tuple-element.48), channel_id=1, source_target_pairs={{0,8},{4,12},{8,0},{12,4},{16,24},{20,28},{24,16},{28,20},{1,9},{5... | collective-permute-start | bytes 516104 | tf_op jit(solution)/shard_map/ppermute | solution.py:428
  12.3 21.4 %collective-permute-start.7 = (bf16[224,384]{1,0:T(8,128)(2,1)S(1)}, bf16[224,384]{1,0:T(8,128)(2,1)S(1)}, u32[]{:S(2)}, u32[]{:S(2)}) collective-permute-start(bf16[224,384]{1,0:T(8,128)(2,1)S(1)} %get-tuple-element.49), channel_id=1, source_target_pairs={{0,16},{4,20},{8,24},{12,28},{16,0},{20,4},{24,8},{28,12},{1,17},{... | collective-permute-start | bytes 516104 | tf_op jit(solution)/shard_map/ppermute | solution.py:428
  13.8 19.9 %collective-permute-start.8 = (bf16[224,384]{1,0:T(8,128)(2,1)S(1)}, bf16[224,384]{1,0:T(8,128)(2,1)S(1)}, u32[]{:S(2)}, u32[]{:S(2)}) collective-permute-start(bf16[224,384]{1,0:T(8,128)(2,1)S(1)} %get-tuple-element.50), channel_id=1, source_target_pairs={{0,12},{4,8},{8,4},{12,0},{16,28},{20,24},{24,20},{28,16},{1,13},{... | collective-permute-start | bytes 516104 | tf_op jit(solution)/shard_map/ppermute | solution.py:428
  16.2 17.5 %collective-permute-start.9 = (bf16[224,384]{1,0:T(8,128)(2,1)S(1)}, bf16[224,384]{1,0:T(8,128)(2,1)S(1)}, u32[]{:S(2)}, u32[]{:S(2)}) collective-permute-start(bf16[224,384]{1,0:T(8,128)(2,1)S(1)} %get-tuple-element.51), channel_id=1, source_target_pairs={{0,20},{4,16},{8,28},{12,24},{16,4},{20,0},{24,12},{28,8},{1,21},{... | collective-permute-start | bytes 516104 | tf_op jit(solution)/shard_map/ppermute | solution.py:428
  18.4 5.0 %collective-permute-start.5 = (bf16[4,1152]{1,0:T(4,128)(2,1)S(1)}, bf16[4,1152]{1,0:T(4,128)(2,1)S(1)}, u32[]{:S(2)}, u32[]{:S(2)}) collective-permute-start(bf16[4,1152]{1,0:T(4,128)(2,1)S(1)} %copy-done.4), channel_id=1, source_target_pairs={{0,3},{1,0},{2,1},{3,2},{4,7},{5,4},{6,5},{7,6},{8,11},{9,8},{10,9... | collective-permute-start | bytes 27656 | tf_op jit(solution)/shard_map/ppermute | solution.py:428
  23.4 4.6 %collective-permute-start.4 = (bf16[4,1152]{1,0:T(4,128)(2,1)S(1)}, bf16[4,1152]{1,0:T(4,128)(2,1)S(1)}, u32[]{:S(2)}, u32[]{:S(2)}) collective-permute-start(bf16[4,1152]{1,0:T(4,128)(2,1)S(1)} %copy-done.4), channel_id=1, source_target_pairs={{0,2},{1,3},{2,0},{3,1},{4,6},{5,7},{6,4},{7,5},{8,10},{9,11},{10,... | collective-permute-start | bytes 27656 | tf_op jit(solution)/shard_map/ppermute | solution.py:428
  27.9 5.7 %collective-permute-start.3 = (bf16[4,1152]{1,0:T(4,128)(2,1)S(1)}, bf16[4,1152]{1,0:T(4,128)(2,1)S(1)}, u32[]{:S(2)}, u32[]{:S(2)}) collective-permute-start(bf16[4,1152]{1,0:T(4,128)(2,1)S(1)} %copy-done.4), channel_id=1, source_target_pairs={{0,1},{1,2},{2,3},{3,0},{4,5},{5,6},{6,7},{7,4},{8,9},{9,10},{10,1... | collective-permute-start | bytes 27656 | tf_op jit(solution)/shard_map/ppermute | solution.py:428
  41.6 5.2 %collective-permute-start.10 = (bf16[80,384]{1,0:T(8,128)(2,1)S(1)}, bf16[80,384]{1,0:T(8,128)(2,1)S(1)}, u32[]{:S(2)}, u32[]{:S(2)}) collective-permute-start(bf16[80,384]{1,0:T(8,128)(2,1)S(1)} %get-tuple-element.52), channel_id=1, source_target_pairs={{0,24},{4,28},{8,16},{12,20},{16,8},{20,12},{24,0},{28,4},{1,25},{... | collective-permute-start | bytes 184328 | tf_op jit(solution)/shard_map/ppermute | solution.py:428
  43.1 5.2 %collective-permute-start.11 = (bf16[80,384]{1,0:T(8,128)(2,1)S(1)}, bf16[80,384]{1,0:T(8,128)(2,1)S(1)}, u32[]{:S(2)}, u32[]{:S(2)}) collective-permute-start(bf16[80,384]{1,0:T(8,128)(2,1)S(1)} %get-tuple-element.53), channel_id=1, source_target_pairs={{0,28},{4,24},{8,20},{12,16},{16,12},{20,8},{24,4},{28,0},{1,29},{... | collective-permute-start | bytes 184328 | tf_op jit(solution)/shard_map/ppermute | solution.py:428
  43.1 5.2 %collective-permute-start.12 = (bf16[80,384]{1,0:T(8,128)(2,1)S(1)}, bf16[80,384]{1,0:T(8,128)(2,1)S(1)}, u32[]{:S(2)}, u32[]{:S(2)}) collective-permute-start(bf16[80,384]{1,0:T(8,128)(2,1)S(1)} %get-tuple-element.54), channel_id=1, source_target_pairs={{0,8},{4,12},{8,0},{12,4},{16,24},{20,28},{24,16},{28,20},{1,9},{5... | collective-permute-start | bytes 184328 | tf_op jit(solution)/shard_map/ppermute | solution.py:428
  43.3 5.6 %collective-permute-start.13 = (bf16[80,384]{1,0:T(8,128)(2,1)S(1)}, bf16[80,384]{1,0:T(8,128)(2,1)S(1)}, u32[]{:S(2)}, u32[]{:S(2)}) collective-permute-start(bf16[80,384]{1,0:T(8,128)(2,1)S(1)} %get-tuple-element.55), channel_id=1, source_target_pairs={{0,16},{4,20},{8,24},{12,28},{16,0},{20,4},{24,8},{28,12},{1,17},{... | collective-permute-start | bytes 184328 | tf_op jit(solution)/shard_map/ppermute | solution.py:428
  45.2 4.1 %collective-permute-start.14 = (bf16[80,384]{1,0:T(8,128)(2,1)S(1)}, bf16[80,384]{1,0:T(8,128)(2,1)S(1)}, u32[]{:S(2)}, u32[]{:S(2)}) collective-permute-start(bf16[80,384]{1,0:T(8,128)(2,1)S(1)} %get-tuple-element.56), channel_id=1, source_target_pairs={{0,12},{4,8},{8,4},{12,0},{16,28},{20,24},{24,20},{28,16},{1,13},{... | collective-permute-start | bytes 184328 | tf_op jit(solution)/shard_map/ppermute | solution.py:428
  46.8 4.1 %collective-permute-start.15 = (bf16[80,384]{1,0:T(8,128)(2,1)S(1)}, bf16[80,384]{1,0:T(8,128)(2,1)S(1)}, u32[]{:S(2)}, u32[]{:S(2)}) collective-permute-start(bf16[80,384]{1,0:T(8,128)(2,1)S(1)} %get-tuple-element.57), channel_id=1, source_target_pairs={{0,20},{4,16},{8,28},{12,24},{16,4},{20,0},{24,12},{28,8},{1,21},{... | collective-permute-start | bytes 184328 | tf_op jit(solution)/shard_map/ppermute | solution.py:428
  48.3 2.7 %collective-permute-start.16 = (bf16[80,384]{1,0:T(8,128)(2,1)S(1)}, bf16[80,384]{1,0:T(8,128)(2,1)S(1)}, u32[]{:S(2)}, u32[]{:S(2)}) collective-permute-start(bf16[80,384]{1,0:T(8,128)(2,1)S(1)} %get-tuple-element.58), channel_id=1, source_target_pairs={{0,4},{4,0},{8,12},{12,8},{16,20},{20,16},{24,28},{28,24},{1,5},{5... | collective-permute-start | bytes 184328 | tf_op jit(solution)/shard_map/ppermute | solution.py:428

commit v13 on v10

--- a/solution.py
+++ b/solution.py
@@ -129,9 +129,10 @@
         store_by_core(core, blocks, *out_refs[2 * step : 2 * step + 2])
 
 
-def find_starts(images, ids, starts):
-    for image in range(images + 1):
-        starts[image] = jnp.sum((ids < image).astype(jnp.int32))
+def count_before(images, ids):
+    image = lax.broadcasted_iota(jnp.int32, (rounded_up(images + 1, SPARE), ids.shape[1]), 0)
+    before = jnp.sum((ids < image).astype(jnp.int32), axis=1, keepdims=True)
+    return jnp.broadcast_to(before, (before.shape[0], LANES))
 
 
 def write_marks(images, ids, marks):
@@ -197,10 +198,10 @@
         first = pl.multiple_of(at * tile, tile)
         labels = ids_ref[:, pl.ds(pl.multiple_of(query_base + first, LANES), tile)]
         probs = jnp.exp2((scores[...] - tops[...]) * (size ** (-0.5) * math.log2(math.e)))
+        share = 1.0 / jnp.sum(probs, axis=0, keepdims=True)
         weighted = jnp.dot(
             values[:, window_of(image)], probs.astype(jnp.bfloat16), preferred_element_type=jnp.float32
         )
-        share = 1.0 / weighted[size : size + 1]
         place = (slice(None), pl.ds(first, tile))
         attended[place] = jnp.where(labels == image, weighted * share, attended[place])
 
@@ -245,16 +246,10 @@
     queries[PADDED:, there] = jnp.zeros((LANES - PADDED, block_ref.shape[1]), jnp.bfloat16)
 
 
-def store_values(block_ref, values, here):
-    edge = block_ref[PADDED - 16 : PADDED].astype(jnp.float32)
-    ones = jnp.ones((SPARE, edge.shape[1]), jnp.float32)
-    values[0 : PADDED - 16, here] = block_ref[0 : PADDED - 16]
-    values[PADDED - 16 : PADDED, here] = jnp.concatenate([edge[:SPARE], ones], axis=0).astype(jnp.bfloat16)
-
-
 def prepare_kernel(images, halo, ids_ref, *rest):
-    got_refs, (keys, marks) = rest[: len(EARLY)], rest[len(EARLY) :]
+    got_refs, (keys, marks, before) = rest[: len(EARLY)], rest[len(EARLY) :]
     count = got_refs[0].shape[1]
+    before[...] = count_before(images, ids_ref[...])
     write_marks(images, ids_ref[...], marks)
     own = lax.rem(lax.axis_index("grp"), HEADS)
     for step, (by, ref) in enumerate(zip(EARLY, got_refs)):
@@ -263,7 +258,7 @@
         keys[step * count : (step + 1) * count, :] = turned_keys(marks[0, :, here], ref)
 
 
-def attend_kernel(images, piggy, halo, ids_ref, marks, early_keys, *rest):
+def attend_kernel(images, piggy, halo, ids_ref, before_ref, marks, early_keys, *rest):
     got_refs, rest = rest[:HEADS], rest[HEADS:]
     if halo:
         left_ref, right_ref, *rest = rest
@@ -274,7 +269,9 @@
     total_rows = HEADS * count
     length = ids_ref.shape[1]
     ids = ids_ref[...]
-    find_starts(images, ids, starts)
+    before = before_ref[...]
+    for image in range(images + 1):
+        starts[image] = before[image, 0]
 
     own = lax.rem(lax.axis_index("grp"), HEADS)
     for step, (by, ref) in enumerate(zip(EARLY + LATE, got_refs)):
@@ -285,12 +282,12 @@
             keys[here, :] = early_keys[step * count : (step + 1) * count, :]
         else:
             keys[here, :] = turned_keys(marks[0, :, here], ref)
-        store_values(ref, values, here)
+        values[:, here] = ref[0:PADDED]
         store_queries(marks[1, :, here], ref, queries, there)
     if halo:
         for ref, here in ((left_ref, slice(0, halo)), (right_ref, slice(length - halo, length))):
             keys[here, :] = turned_keys(marks[0, :, here], ref)
-            store_values(ref, values, here)
+            values[:, here] = ref[0:PADDED]
     attend_images(images, ids_ref, keys, values, queries, attended, work, starts, halo)
 
     odd_head = lax.rem(own, 2) == 1
@@ -429,8 +426,12 @@
 
 def all_texts(texts):
     peers = lax.axis_size("blk")
-    shifts = range(1, peers)
-    return [texts] + [moved(texts, "blk", [(i, (i + by) % peers) for i in range(peers)]) for by in shifts]
+    paired = peers & (peers - 1) == 0
+    others = []
+    for by in range(1, peers):
+        pairs = [(i, i ^ by if paired else (i + by) % peers) for i in range(peers)]
+        others.append(moved(texts, "blk", pairs))
+    return [texts] + others
 
 
 def exchanged(blocks, groups):
@@ -507,14 +508,18 @@
     reach = length + 2 * halo
     window = min(rounded_up(MAXP + LANES - 1, LANES), reach)
     tile = 2 * LANES
-    early_keys, marks = call(
+    early_keys, marks, before = call(
         functools.partial(prepare_kernel, images, halo),
-        (shape((len(EARLY) * count, LANES), bf16), shape((2, SPARE, reach), f32)),
+        (
+            shape((len(EARLY) * count, LANES), bf16),
+            shape((2, SPARE, reach), f32),
+            shape((rounded_up(images + 1, SPARE), LANES), jnp.int32),
+        ),
         [],
         in_vmem(1 + len(EARLY)),
         1 << 30,
     )(near_ids, *[got[by] for by in EARLY])
-    operands = [near_ids, marks, early_keys, *[got[by] for by in EARLY + LATE], *halos]
+    operands = [near_ids, before, marks, early_keys, *[got[by] for by in EARLY + LATE], *halos]
     answers = call(
         functools.partial(attend_kernel, images, piggy, halo),
         shape((HEADS, padded, count), bf16),

time: 47.4 us -> 46.7 us (0.985)
  waiting for transfers between devices: 11.4 us -> 12.1 us
  starting transfers between devices: 18.1 us -> 17.5 us
  Pallas kernels: 16.8 us -> 16.3 us
    all_to_all x1, waiting for transfers between devices: 0.15 us -> 1.03 us  [exchanged(): lax.all_to_all(blocks, 'grp', 0, 0, axis_index_groups=groups, tiled=True)]
    ppermute x10, starting transfers between devices: 14.6 us -> 14 us  [moved(): return lax.ppermute(value, axis, pairs)]
    pallas_call x1, Pallas kernels: 8.79 us -> 8.26 us  [local(): call(functools.partial(attend_kernel, images, piggy, halo), shape((HEADS,...]
  transfers between devices with their start and end apart: 11 -> 11, of which waited for: 7 -> 7; matrix products, arithmetic and copies ran while one was open for 0% -> 0% of each run, Pallas kernels for 5% -> 6%
where the time goes in v13:
time: 46.7 us; the launch traced here: 46.5 us
  starting transfers between devices  17.5 us (37%)
  Pallas kernels  16.3 us (35%)
  waiting for transfers between devices  12.1 us (26%)
  between operations  0.7 us (1%)
    ppermute x10, starting transfers between devices, moved(): return lax.ppermute(value, axis, pairs)  14 us
    ppermute x10, waiting for transfers between devices, moved(): return lax.ppermute(value, axis, pairs)  11 us
    pallas_call x1, Pallas kernels, local(): call(functools.partial(attend_kernel, images, piggy, halo), shape((HEADS,...  8.26 us
    all_to_all x1, starting transfers between devices, exchanged(): lax.all_to_all(blocks, 'grp', 0, 0, axis_index_groups=groups, tiled=True)  3.5 us
    pallas_call x1, Pallas kernels, local(): call(functools.partial(far_kernel, images, piggy), (shape((depth, count),...  3.12 us
    pallas_call x1, Pallas kernels, local(): call(functools.partial(near_kernel, piggy), (block,) * 6, [], in_vmem(3),...  2.35 us
    pallas_call x1, Pallas kernels, local(): call(functools.partial(finish_kernel, images), (shape((count, depth), bf1...  2.29 us
    all_to_all x1, waiting for transfers between devices, exchanged(): lax.all_to_all(blocks, 'grp', 0, 0, axis_index_groups=groups, tiled=True)  1.03 us
  transfers between devices with their start and end apart: 11, of which 7 were waited for; matrix products, arithmetic and copies ran while one was open for 0% of the time, Pallas kernels for 6%

profile of v13, /device:TPU:0, one launch (start us, length us, event | category | flops | bytes accessed | tf_op | source)
XLA Modules:
  0.0 46.5 jit_solution(2066292240946100768)
XLA Ops:
  0.6 0.0 copy-start
  0.6 0.0 copy-start.3
  0.6 3.1 %shard_map.68 = (bf16[1152,384]{1,0:T(8,128)(2,1)S(1)}, f32[8,1152]{1,0:T(8,128)S(1)}, bf16[224,384]{1,0:T(8,128)(2,1)S(1)}, bf16[224,384]{1,0:T(8,128)(2,1)S(1)}) custom-call(s32[1,3072]{1,0:T(1,128)} %ids_ref.5, bf16[384,1152]{1,0:T(8,128)(2,1)} %bitcast.6, bf16[1728,1152]{1,0:T(8,128)(2,1)} %bitcast.4), custom_call_target="tpu_custom_call" | custom-call | flops 382205952 | bytes 8388608 | tf_op jit(solution)/shard_map/pallas_call | solution.py:458
  3.8 4.0 %collective-permute-start = (bf16[224,384]{1,0:T(8,128)(2,1)S(1)}, bf16[224,384]{1,0:T(8,128)(2,1)S(1)}, u32[]{:S(2)}, u32[]{:S(2)}) collective-permute-start(bf16[224,384]{1,0:T(8,128)(2,1)S(1)} %get-tuple-element.18), channel_id=1, source_target_pairs={{0,24},{4,28},{8,16},{12,20},{16,8},{20,12},{24,0},{28,4},{1,25},{... | collective-permute-start | bytes 516104 | tf_op jit(solution)/shard_map/ppermute | solution.py:424
  7.7 0.0 collective-permute-start.1
  7.7 0.0 copy-done
  7.7 2.3 %shard_map.69 = (bf16[224,384]{1,0:T(8,128)(2,1)S(1)}, bf16[224,384]{1,0:T(8,128)(2,1)S(1)}, bf16[224,384]{1,0:T(8,128)(2,1)S(1)}, bf16[224,384]{1,0:T(8,128)(2,...) custom-call(bf16[1152,384]{1,0:T(8,128)(2,1)S(1)} %get-tuple-element.20.normed_ref, ...), custom_call_target="tpu_custom_call" | custom-call | flops 1146617856 | bytes 8388608 | tf_op jit(solution)/shard_map/pallas_call | solution.py:472
  10.1 0.3 collective-permute-start.2
  10.4 1.9 %collective-permute-start.3 = (bf16[224,384]{1,0:T(8,128)(2,1)S(1)}, bf16[224,384]{1,0:T(8,128)(2,1)S(1)}, u32[]{:S(2)}, u32[]{:S(2)}) collective-permute-start(bf16[224,384]{1,0:T(8,128)(2,1)S(1)} %get-tuple-element.27), channel_id=1, source_target_pairs={{0,8},{4,12},{8,0},{12,4},{16,24},{20,28},{24,16},{28,20},{1,9},{5... | collective-permute-start | bytes 516104 | tf_op jit(solution)/shard_map/ppermute | solution.py:424
  12.2 1.5 %collective-permute-start.4 = (bf16[224,384]{1,0:T(8,128)(2,1)S(1)}, bf16[224,384]{1,0:T(8,128)(2,1)S(1)}, u32[]{:S(2)}, u32[]{:S(2)}) collective-permute-start(bf16[224,384]{1,0:T(8,128)(2,1)S(1)} %get-tuple-element.28), channel_id=1, source_target_pairs={{0,16},{4,20},{8,24},{12,28},{16,0},{20,4},{24,8},{28,12},{1,17},{... | collective-permute-start | bytes 516104 | tf_op jit(solution)/shard_map/ppermute | solution.py:424
  13.8 0.0 collective-permute-done.rest_0_
  13.8 0.0 collective-permute-start.5
  13.8 2.4 %collective-permute-done.1.rest_1_ = bf16[224,384]{1,0:T(8,128)(2,1)S(1)} collective-permute-done((bf16[224,384]{1,0:T(8,128)(2,1)S(1)}, bf16[224,384]{1,0:T(8,128)(2,1)S(1)}, u32[]{:S(2)}, u32[]{:S(2)}) %collective-permute-start.1) | collective-permute-done | bytes 172064 | tf_op jit(solution)/shard_map/ppermute | solution.py:424
  16.2 1.9 %collective-permute-start.6 = (bf16[224,384]{1,0:T(8,128)(2,1)S(1)}, bf16[224,384]{1,0:T(8,128)(2,1)S(1)}, u32[]{:S(2)}, u32[]{:S(2)}) collective-permute-start(bf16[224,384]{1,0:T(8,128)(2,1)S(1)} %get-tuple-element.30), channel_id=1, source_target_pairs={{0,20},{4,16},{8,28},{12,24},{16,4},{20,0},{24,12},{28,8},{1,21},{... | collective-permute-start | bytes 516104 | tf_op jit(solution)/shard_map/ppermute | solution.py:424
  18.1 0.0 collective-permute-done.2.rest_2_
  18.1 0.0 copy-done.3
  18.1 0.0 copy-start.4
  18.1 0.0 copy-start.1
  18.1 0.0 copy-start.2
  18.1 0.2 shard_map.70
  18.4 2.5 %collective-permute-done.3.rest_4_ = bf16[224,384]{1,0:T(8,128)(2,1)S(1)} collective-permute-done((bf16[224,384]{1,0:T(8,128)(2,1)S(1)}, bf16[224,384]{1,0:T(8,128)(2,1)S(1)}, u32[]{:S(2)}, u32[]{:S(2)}) %collective-permute-start.3) | collective-permute-done | bytes 172064 | tf_op jit(solution)/shard_map/ppermute | solution.py:424
  20.9 0.0 collective-permute-done.4.rest_5_
  20.9 1.5 %collective-permute-done.5.rest_6_ = bf16[224,384]{1,0:T(8,128)(2,1)S(1)} collective-permute-done((bf16[224,384]{1,0:T(8,128)(2,1)S(1)}, bf16[224,384]{1,0:T(8,128)(2,1)S(1)}, u32[]{:S(2)}, u32[]{:S(2)}) %collective-permute-start.5) | collective-permute-done | bytes 172064 | tf_op jit(solution)/shard_map/ppermute | solution.py:424
  22.4 0.6 %collective-permute-done.6.rest_7_ = bf16[224,384]{1,0:T(8,128)(2,1)S(1)} collective-permute-done((bf16[224,384]{1,0:T(8,128)(2,1)S(1)}, bf16[224,384]{1,0:T(8,128)(2,1)S(1)}, u32[]{:S(2)}, u32[]{:S(2)}) %collective-permute-start.6) | collective-permute-done | bytes 172064 | tf_op jit(solution)/shard_map/ppermute | solution.py:424
  23.1 8.3 %shard_map.71 = bf16[8,80,384]{2,1,0:T(8,128)(2,1)} custom-call(s32[1,3072]{1,0:T(1,128)S(1)} %copy-done.3, s32[8,128]{1,0:T(8,128)S(1)} %get-tuple-element.24.before_ref, f32[2,8,3072]{2,1,0:T(8,128)S(1)} %get-tuple-element.25.marks, bf16[1536,128]{1,0:T(8,128)(2,1)S(1)} %get-tuple-element.26.early_keys, bf16[224,384]{1,0:T(8,128)(2,1)S(1)} %collective-permute-done.rest_0_, ...), custom_call_target="tpu_custom_call" | custom-call | flops 905969664 | bytes 8388608 | tf_op jit(solution)/shard_map/pallas_call | solution.py:523
  31.3 3.5 %all-to-all-start = ((bf16[8,80,384]{2,1,0:T(8,128)(2,1)}), bf16[8,80,384]{2,1,0:T(8,128)(2,1)S(1)}, u32[]{:S(2)}, u32[]{:S(2)}) async-start(bf16[8,80,384]{2,1,0:T(8,128)(2,1)} %shard_map.71), calls=%async_computation | async-start | bytes 983040 | tf_op jit(solution)/shard_map/all_to_all | solution.py:438
  34.8 0.0 copy-done.4
  34.9 3.8 %collective-permute-start.9 = (bf16[4,1152]{1,0:T(4,128)(2,1)S(1)}, bf16[4,1152]{1,0:T(4,128)(2,1)S(1)}, u32[]{:S(2)}, u32[]{:S(2)}) collective-permute-start(bf16[4,1152]{1,0:T(4,128)(2,1)S(1)} %copy-done.4), channel_id=1, source_target_pairs={{0,3},{1,2},{2,1},{3,0},{4,7},{5,6},{6,5},{7,4},{8,11},{9,10},{10,... | collective-permute-start | bytes 27656 | tf_op jit(solution)/shard_map/ppermute | solution.py:424
  38.6 0.0 collective-permute-start.8
  38.6 0.7 %collective-permute-start.7 = (bf16[4,1152]{1,0:T(4,128)(2,1)S(1)}, bf16[4,1152]{1,0:T(4,128)(2,1)S(1)}, u32[]{:S(2)}, u32[]{:S(2)}) collective-permute-start(bf16[4,1152]{1,0:T(4,128)(2,1)S(1)} %copy-done.4), channel_id=1, source_target_pairs={{0,1},{1,0},{2,3},{3,2},{4,5},{5,4},{6,7},{7,6},{8,9},{9,8},{10,11... | collective-permute-start | bytes 27656 | tf_op jit(solution)/shard_map/ppermute | solution.py:424
  39.3 1.1 %collective-permute-done.9 = bf16[4,1152]{1,0:T(4,128)(2,1)S(1)} collective-permute-done((bf16[4,1152]{1,0:T(4,128)(2,1)S(1)}, bf16[4,1152]{1,0:T(4,128)(2,1)S(1)}, u32[]{:S(2)}, u32[]{:S(2)}) %collective-permute-start.9) | collective-permute-done | bytes 9248 | tf_op jit(solution)/shard_map/ppermute | solution.py:424
  40.4 2.8 %collective-permute-done.8 = bf16[4,1152]{1,0:T(4,128)(2,1)S(1)} collective-permute-done((bf16[4,1152]{1,0:T(4,128)(2,1)S(1)}, bf16[4,1152]{1,0:T(4,128)(2,1)S(1)}, u32[]{:S(2)}, u32[]{:S(2)}) %collective-permute-start.8) | collective-permute-done | bytes 9248 | tf_op jit(solution)/shard_map/ppermute | solution.py:424
  43.2 0.0 collective-permute-done.7
  43.2 1.0 %all-to-all-done.got_ref = bf16[8,80,384]{2,1,0:T(8,128)(2,1)S(1)} async-done(((bf16[8,80,384]{2,1,0:T(8,128)(2,1)}), bf16[8,80,384]{2,1,0:T(8,128)(2,1)S(1)}, u32[]{:S(2)}, u32[]{:S(2)}) %all-to-all-start) | async-done | bytes 491552 | tf_op jit(solution)/shard_map/all_to_all | solution.py:438
  44.2 0.0 copy-done.1
  44.2 0.0 copy-done.2
  44.2 2.3 %shard_map.72 = (bf16[384,1152]{1,0:T(8,128)(2,1)}, f32[1,4]{1,0:T(1,128)}) custom-call(bf16[384,1152]{1,0:T(8,128)(2,1)S(1)} %bitcast.7, bf16[8,80,384]{2,1,0:T(8,128)(2,1)S(1)} %all-to-all-done.got_ref, bf16[576,1152]{1,0:T(8,128)(2,1)S(1)} %copy-done.2, bf16[16,1152]{1,0:T(8,128)(2,1)S(1)} %pad_maximum_fusion.text_ref), custom_call_target="tpu_custom_call" | custom-call | flops 509607936 | bytes 8388608 | tf_op jit(solution)/shard_map/pallas_call | solution.py:553
  (1 shorter events, 0.0 us)
Async XLA Ops:
  0.6 7.1 %copy-start = (bf16[1152,1728]{0,1:T(8,128)(2,1)S(1)}, bf16[1152,1728]{0,1:T(8,128)(2,1)}, u32[]{:S(2)}) copy-start(bf16[1152,1728]{0,1:T(8,128)(2,1)} %param.7) | copy-start | bytes 11943940
  0.6 17.5 %copy-start.3 = (s32[1,3072]{1,0:T(1,128)S(1)}, s32[1,3072]{1,0:T(1,128)}, u32[]{:S(2)}) copy-start(s32[1,3072]{1,0:T(1,128)} %ids_ref.5) | copy-start | bytes 36868
  3.8 10.0 %collective-permute-start = (bf16[224,384]{1,0:T(8,128)(2,1)S(1)}, bf16[224,384]{1,0:T(8,128)(2,1)S(1)}, u32[]{:S(2)}, u32[]{:S(2)}) collective-permute-start(bf16[224,384]{1,0:T(8,128)(2,1)S(1)} %get-tuple-element.18), channel_id=1, source_target_pairs={{0,24},{4,28},{8,16},{12,20},{16,8},{20,12},{24,0},{28,4},{1,25},{... | collective-permute-start | bytes 516104 | tf_op jit(solution)/shard_map/ppermute | solution.py:424
  7.7 8.5 %collective-permute-start.1 = (bf16[224,384]{1,0:T(8,128)(2,1)S(1)}, bf16[224,384]{1,0:T(8,128)(2,1)S(1)}, u32[]{:S(2)}, u32[]{:S(2)}) collective-permute-start(bf16[224,384]{1,0:T(8,128)(2,1)S(1)} %get-tuple-element.19), channel_id=1, source_target_pairs={{0,28},{4,24},{8,20},{12,16},{16,12},{20,8},{24,4},{28,0},{1,29},{... | collective-permute-start | bytes 516104 | tf_op jit(solution)/shard_map/ppermute | solution.py:424
  10.1 8.0 %collective-permute-start.2 = (bf16[224,384]{1,0:T(8,128)(2,1)S(1)}, bf16[224,384]{1,0:T(8,128)(2,1)S(1)}, u32[]{:S(2)}, u32[]{:S(2)}) collective-permute-start(bf16[224,384]{1,0:T(8,128)(2,1)S(1)} %get-tuple-element.22), channel_id=1, source_target_pairs={{0,4},{4,0},{8,12},{12,8},{16,20},{20,16},{24,28},{28,24},{1,5},{5... | collective-permute-start | bytes 516104 | tf_op jit(solution)/shard_map/ppermute | solution.py:424
  10.4 10.5 %collective-permute-start.3 = (bf16[224,384]{1,0:T(8,128)(2,1)S(1)}, bf16[224,384]{1,0:T(8,128)(2,1)S(1)}, u32[]{:S(2)}, u32[]{:S(2)}) collective-permute-start(bf16[224,384]{1,0:T(8,128)(2,1)S(1)} %get-tuple-element.27), channel_id=1, source_target_pairs={{0,8},{4,12},{8,0},{12,4},{16,24},{20,28},{24,16},{28,20},{1,9},{5... | collective-permute-start | bytes 516104 | tf_op jit(solution)/shard_map/ppermute | solution.py:424
  12.2 8.6 %collective-permute-start.4 = (bf16[224,384]{1,0:T(8,128)(2,1)S(1)}, bf16[224,384]{1,0:T(8,128)(2,1)S(1)}, u32[]{:S(2)}, u32[]{:S(2)}) collective-permute-start(bf16[224,384]{1,0:T(8,128)(2,1)S(1)} %get-tuple-element.28), channel_id=1, source_target_pairs={{0,16},{4,20},{8,24},{12,28},{16,0},{20,4},{24,8},{28,12},{1,17},{... | collective-permute-start | bytes 516104 | tf_op jit(solution)/shard_map/ppermute | solution.py:424
  13.8 8.7 %collective-permute-start.5 = (bf16[224,384]{1,0:T(8,128)(2,1)S(1)}, bf16[224,384]{1,0:T(8,128)(2,1)S(1)}, u32[]{:S(2)}, u32[]{:S(2)}) collective-permute-start(bf16[224,384]{1,0:T(8,128)(2,1)S(1)} %get-tuple-element.29), channel_id=1, source_target_pairs={{0,12},{4,8},{8,4},{12,0},{16,28},{20,24},{24,20},{28,16},{1,13},{... | collective-permute-start | bytes 516104 | tf_op jit(solution)/shard_map/ppermute | solution.py:424
  16.2 6.9 %collective-permute-start.6 = (bf16[224,384]{1,0:T(8,128)(2,1)S(1)}, bf16[224,384]{1,0:T(8,128)(2,1)S(1)}, u32[]{:S(2)}, u32[]{:S(2)}) collective-permute-start(bf16[224,384]{1,0:T(8,128)(2,1)S(1)} %get-tuple-element.30), channel_id=1, source_target_pairs={{0,20},{4,16},{8,28},{12,24},{16,4},{20,0},{24,12},{28,8},{1,21},{... | collective-permute-start | bytes 516104 | tf_op jit(solution)/shard_map/ppermute | solution.py:424
  18.1 16.8 %copy-start.4 = (bf16[4,1152]{1,0:T(4,128)(2,1)S(1)}, bf16[4,1152]{1,0:T(4,128)(2,1)}, u32[]{:S(2)}) copy-start(bf16[4,1152]{1,0:T(4,128)(2,1)} %param.9) | copy-start | bytes 27652
  18.1 26.1 %copy-start.1 = (bf16[1,384,1152]{2,1,0:T(8,128)(2,1)S(1)}, bf16[1,384,1152]{2,1,0:T(8,128)(2,1)}, u32[]{:S(2)}) copy-start(bf16[1,384,1152]{2,1,0:T(8,128)(2,1)} %param.5) | copy-start | bytes 2654212
  18.1 26.1 %copy-start.2 = (bf16[576,1152]{1,0:T(8,128)(2,1)S(1)}, bf16[576,1152]{1,0:T(8,128)(2,1)}, u32[]{:S(2)}) copy-start(bf16[576,1152]{1,0:T(8,128)(2,1)} %out_weight_ref.1) | copy-start | bytes 3981316
  31.3 12.9 %all-to-all-start = ((bf16[8,80,384]{2,1,0:T(8,128)(2,1)}), bf16[8,80,384]{2,1,0:T(8,128)(2,1)S(1)}, u32[]{:S(2)}, u32[]{:S(2)}) async-start(bf16[8,80,384]{2,1,0:T(8,128)(2,1)} %shard_map.71), calls=%async_computation | async-start | bytes 983040 | tf_op jit(solution)/shard_map/all_to_all | solution.py:438
  34.9 5.5 %collective-permute-start.9 = (bf16[4,1152]{1,0:T(4,128)(2,1)S(1)}, bf16[4,1152]{1,0:T(4,128)(2,1)S(1)}, u32[]{:S(2)}, u32[]{:S(2)}) collective-permute-start(bf16[4,1152]{1,0:T(4,128)(2,1)S(1)} %copy-done.4), channel_id=1, source_target_pairs={{0,3},{1,2},{2,1},{3,0},{4,7},{5,6},{6,5},{7,4},{8,11},{9,10},{10,... | collective-permute-start | bytes 27656 | tf_op jit(solution)/shard_map/ppermute | solution.py:424
  38.6 4.6 %collective-permute-start.8 = (bf16[4,1152]{1,0:T(4,128)(2,1)S(1)}, bf16[4,1152]{1,0:T(4,128)(2,1)S(1)}, u32[]{:S(2)}, u32[]{:S(2)}) collective-permute-start(bf16[4,1152]{1,0:T(4,128)(2,1)S(1)} %copy-done.4), channel_id=1, source_target_pairs={{0,2},{1,3},{2,0},{3,1},{4,6},{5,7},{6,4},{7,5},{8,10},{9,11},{10,... | collective-permute-start | bytes 27656 | tf_op jit(solution)/shard_map/ppermute | solution.py:424
  38.6 4.6 %collective-permute-start.7 = (bf16[4,1152]{1,0:T(4,128)(2,1)S(1)}, bf16[4,1152]{1,0:T(4,128)(2,1)S(1)}, u32[]{:S(2)}, u32[]{:S(2)}) collective-permute-start(bf16[4,1152]{1,0:T(4,128)(2,1)S(1)} %copy-done.4), channel_id=1, source_target_pairs={{0,1},{1,0},{2,3},{3,2},{4,5},{5,4},{6,7},{7,6},{8,9},{9,8},{10,11... | collective-permute-start | bytes 27656 | tf_op jit(solution)/shard_map/ppermute | solution.py:424

commit v14 on v12

--- a/solution.py
+++ b/solution.py
@@ -16,6 +16,7 @@
 PADDED = SIZE + SPARE
 KEY_AT = SIZE - SPARE
 QUERY_AT = 2 * SIZE
+TEXT_ROWS = 16
 HIDDEN = -1e30
 ORDER = (6, 7, 2, 4, 3, 5, 1, 0)
 EARLY = (6, 7, 1, 0)
@@ -260,6 +261,8 @@
 
 def attend_kernel(images, piggy, halo, ids_ref, before_ref, marks, early_keys, *rest):
     got_refs, rest = rest[:HEADS], rest[HEADS:]
+    if piggy:
+        text_ref, *rest = rest
     if halo:
         left_ref, right_ref, *rest = rest
     out_refs, rest = rest[:HEADS], rest[HEADS:]
@@ -311,11 +314,18 @@
         spare = jnp.concatenate(
             [pooled, jnp.zeros((SPARE, LANES - padded), jnp.float32), sums], axis=1
         )
+        texts = text_ref[...].astype(jnp.float32)
+        parts = [texts[:, at : at + count] for at in range(0, texts.shape[1], count)]
+        unused = TEXT_ROWS - images * len(parts)
+        below = jnp.concatenate(parts + [jnp.zeros((unused, count), jnp.float32)] * (unused > 0), axis=0)
+        below = below.astype(jnp.bfloat16)
     else:
         spare = jnp.zeros((SPARE, count), jnp.float32)
     for by, out_ref in zip(ORDER, out_refs):
         there = pl.multiple_of(jnp.bitwise_xor(own, by) * count, LANES)
-        out_ref[...] = placed(attended[:, pl.ds(there, count)], spare).astype(jnp.bfloat16)
+        out_ref[0:padded] = placed(attended[:, pl.ds(there, count)], spare).astype(jnp.bfloat16)
+        if piggy:
+            out_ref[padded:] = below
 
 
 def joined_heads(got_refs, out_weight_ref, flat, weight):
@@ -363,7 +373,7 @@
 
 def finish_kernel(images, rows_ref, out_weight_ref, text_ref, *rest):
     got_refs, rest = rest[:HEADS], rest[HEADS:]
-    mixed_ref, loss_ref, flat, weight, turned, mixed, sems, pooled_heads, patch_sums = rest
+    mixed_ref, loss_ref, flat, weight, turned, mixed, sems, pooled_heads, patch_sums, far_texts = rest
     spares = joined_heads(got_refs, out_weight_ref, flat, weight)
     copies = send_mixed_rows(rows_ref, flat, weight, turned, mixed, mixed_ref, sems)
     own = lax.rem(lax.axis_index("grp"), HEADS)
@@ -372,13 +382,20 @@
         pooled_heads[:, step * PADDED : (step + 1) * PADDED] = spare[:, 0:PADDED]
         head = jnp.bitwise_xor(own, by)
         patch_sums[:, pl.ds(pl.multiple_of(head * LANES, LANES), LANES)] = spare[:, LANES : 2 * LANES]
+        below = got_refs[step][PADDED:].astype(jnp.float32)
+        count = below.shape[1]
+        for part in range(patch_sums.shape[1] // count):
+            here = slice(part * count, (part + 1) * count)
+            far_texts[head, :, here] = below[part * images : (part + 1) * images]
     pooled = jnp.dot(
         pooled_heads[...].astype(jnp.bfloat16), weight[...], preferred_element_type=jnp.float32
     )
     pooled = pooled + patch_sums[...]
     pooled = pooled + pltpu.roll(pooled, images, axis=0)
     image_vecs = unit_rows(pooled)
-    text_vecs = unit_rows(text_ref[...].astype(jnp.float32))
+    others = [far_texts[place] for place in range(lax.axis_size("blk") - 1)]
+    texts = jnp.concatenate([text_ref[...].astype(jnp.float32)] + others, axis=0)
+    text_vecs = unit_rows(texts)
     cosine = lax.dot_general(
         text_vecs,
         image_vecs,
@@ -428,10 +445,23 @@
     return lax.ppermute(value, axis, pairs)
 
 
+def partner(place, by, peers):
+    return place ^ by if peers & (peers - 1) == 0 else (place + by) % peers
+
+
 def all_texts(texts):
     peers = lax.axis_size("blk")
-    shifts = range(1, peers)
-    return [texts] + [moved(texts, "blk", [(i, (i + by) % peers) for i in range(peers)]) for by in shifts]
+    steps = [[(partner(i, by, peers), i) for i in range(peers)] for by in range(1, peers)]
+    return jnp.concatenate([texts] + [moved(texts, "blk", pairs) for pairs in steps], axis=0)
+
+
+def one_text_block(texts):
+    peers = lax.axis_size("blk")
+    pairs = []
+    for place in range(lax.axis_size("grp")):
+        by = place % (peers - 1) + 1
+        pairs += [(place * peers + partner(i, by, peers), place * peers + i) for i in range(peers)]
+    return moved(texts, ("grp", "blk"), pairs)
 
 
 def traded(blocks):
@@ -449,7 +479,14 @@
     images = text_embed.shape[0]
     group_size = lax.axis_size("grp")
     parts = group_size // HEADS
-    piggy = parts == 1 and 2 * images == SPARE and count >= depth - (HEADS - 2) * LANES
+    piggy = (
+        parts == 1
+        and 2 * images == SPARE
+        and count >= depth - (HEADS - 2) * LANES
+        and depth % count == 0
+        and images * (depth // count) <= TEXT_ROWS
+        and 1 < lax.axis_size("blk") <= HEADS + 1
+    )
     bf16, f32 = jnp.bfloat16, jnp.float32
     shape = jax.ShapeDtypeStruct
 
@@ -478,12 +515,16 @@
         2 * count * depth * 18 * size,
     )(normed, sums, turned_weight)
     sent = dict(zip((6, 7, 2, 3, 4, 5, 0, 1), sent))
+    if piggy:
+        late_texts, sent[0] = lax.optimization_barrier((text_embed, sent[0]))
+        halos_and_texts = [one_text_block(late_texts)]
+    else:
+        halos_and_texts = []
     got = traded(sent)
 
     length = HEADS * count
     halo = 0
     near_ids = segment_ids
-    halos = []
     if parts > 1:
         halo = rounded_up(MAXP - 1, LANES)
         part = lax.axis_index("grp") // HEADS
@@ -503,7 +544,7 @@
         back = [(i + HEADS, i) for i in range(group_size - HEADS)]
         left = moved(flat[:, length - halo :], "grp", ahead)
         right = moved(flat[:, :halo], "grp", back)
-        halos = [left, right]
+        halos_and_texts += [left, right]
     reach = length + 2 * halo
     window = min(rounded_up(MAXP + LANES - 1, LANES), reach)
     tile = 2 * LANES
@@ -518,13 +559,10 @@
         in_vmem(1 + len(EARLY)),
         1 << 30,
     )(near_ids, *[got[by] for by in EARLY])
-    text_embed, marks = lax.optimization_barrier((text_embed, marks))
-    texts, marks = lax.optimization_barrier((all_texts(text_embed), marks))
-    texts = jnp.concatenate(texts, axis=0)
-    operands = [near_ids, before, marks, early_keys, *[got[by] for by in EARLY + LATE], *halos]
+    operands = [near_ids, before, marks, early_keys, *[got[by] for by in EARLY + LATE], *halos_and_texts]
     answers = call(
         functools.partial(attend_kernel, images, piggy, halo),
-        (shape((padded, count), bf16),) * HEADS,
+        (shape((padded + TEXT_ROWS * piggy, count), bf16),) * HEADS,
         [
             pltpu.VMEM((reach, LANES), bf16),
             pltpu.VMEM((padded, reach), bf16),
@@ -554,11 +592,16 @@
         mixed, row_loss = call(
             functools.partial(finish_kernel, images),
             (shape((count, depth), bf16), shape((1, images), f32)),
-            joined + [pltpu.VMEM((SPARE, HEADS * padded), f32), pltpu.VMEM((SPARE, depth), f32)],
+            joined
+            + [
+                pltpu.VMEM((SPARE, HEADS * padded), f32),
+                pltpu.VMEM((SPARE, depth), f32),
+                pltpu.VMEM((HEADS, images, depth), f32),
+            ],
             in_vmem(3 + HEADS),
             flops,
             (hbm, pl.BlockSpec(memory_space=pltpu.VMEM)),
-        )(rows, out_weight, texts, *home)
+        )(rows, out_weight, text_embed, *home)
         return (mixed[None], row_loss[0])
     mixed = call(mix_kernel, shape((count, depth), bf16), joined, in_vmem(2 + HEADS), flops, hbm)(
         rows, out_weight, *home
@@ -566,9 +609,9 @@
     own_ids = lax.dynamic_slice_in_dim(segment_ids[0], lax.axis_index("grp") * count, count)
     onehot = (own_ids[None, :] == jnp.arange(images, dtype=jnp.int32)[:, None]).astype(bf16)
     pooled = lax.psum(jnp.dot(onehot, mixed, preferred_element_type=f32), "grp")
-    text_vecs = unit_rows(texts.astype(f32))
+    text_vecs = unit_rows(all_texts(text_embed).astype(f32))
     cosine = jnp.dot(unit_rows(pooled), text_vecs.T, precision=lax.Precision.HIGHEST)
-    same = jnp.arange(images)[:, None] == jnp.arange(texts.shape[0])[None, :]
+    same = jnp.arange(images)[:, None] == jnp.arange(text_vecs.shape[0])[None, :]
     row_loss = jnp.sum(losses(cosine, jnp.where(same, 1.0, -1.0)), axis=1)
     return (mixed[None], row_loss)
 

time: 53.3 us -> 44.3 us (0.83)
  waiting for transfers between devices: 15.4 us -> 9.79 us
  starting transfers between devices: 21.1 us -> 17.6 us
    ppermute x17 -> x15, waiting for transfers between devices: 15.4 us -> 9.79 us  [moved(): return lax.ppermute(value, axis, pairs)]
    ppermute x17 -> x15, starting transfers between devices: 21.1 us -> 17.6 us  [moved(): return lax.ppermute(value, axis, pairs)]
  transfers between devices with their start and end apart: 17 -> 15, of which waited for: 9 -> 9; matrix products, arithmetic and copies ran while one was open for 0% -> 0% of each run, Pallas kernels for 5% -> 6%
where the time goes in v14:
time: 44.3 us; the launch traced here: 44.1 us
  starting transfers between devices  17.6 us (40%)
  Pallas kernels  16 us (36%)
  waiting for transfers between devices  9.79 us (22%)
  between operations  0.72 us (2%)
    ppermute x15, starting transfers between devices, moved(): return lax.ppermute(value, axis, pairs)  17.6 us
    ppermute x15, waiting for transfers between devices, moved(): return lax.ppermute(value, axis, pairs)  9.79 us
    pallas_call x1, Pallas kernels, local(): call(functools.partial(attend_kernel, images, piggy, halo), (shape((padde...  7.86 us
    pallas_call x1, Pallas kernels, local(): call(functools.partial(far_kernel, images, piggy), (shape((depth, count),...  3.12 us
    pallas_call x1, Pallas kernels, local(): call(functools.partial(finish_kernel, images), (shape((count, depth), bf1...  2.41 us
    pallas_call x1, Pallas kernels, local(): call(functools.partial(near_kernel, piggy), (block,) * 6, [], in_vmem(3),...  2.35 us
  transfers between devices with their start and end apart: 15, of which 9 were waited for; matrix products, arithmetic and copies ran while one was open for 0% of the time, Pallas kernels for 6%

profile of v14, /device:TPU:0, one launch (start us, length us, event | category | flops | bytes accessed | tf_op | source)
XLA Modules:
  0.0 44.1 jit_solution(4100100320739365027)
XLA Ops:
  0.6 0.0 copy-start
  0.6 0.0 copy-start.4
  0.7 0.0 copy-start.3
  0.7 3.1 %shard_map.68 = (bf16[1152,384]{1,0:T(8,128)(2,1)S(1)}, f32[8,1152]{1,0:T(8,128)S(1)}, bf16[224,384]{1,0:T(8,128)(2,1)S(1)}, bf16[224,384]{1,0:T(8,128)(2,1)S(1)}) custom-call(s32[1,3072]{1,0:T(1,128)} %ids_ref.5, bf16[384,1152]{1,0:T(8,128)(2,1)} %bitcast.6, bf16[1728,1152]{1,0:T(8,128)(2,1)} %bitcast.4), custom_call_target="tpu_custom_call" | custom-call | flops 382205952 | bytes 8388608 | tf_op jit(solution)/shard_map/pallas_call | solution.py:496
  3.8 4.0 %collective-permute-start = (bf16[224,384]{1,0:T(8,128)(2,1)S(1)}, bf16[224,384]{1,0:T(8,128)(2,1)S(1)}, u32[]{:S(2)}, u32[]{:S(2)}) collective-permute-start(bf16[224,384]{1,0:T(8,128)(2,1)S(1)} %get-tuple-element.27), channel_id=1, source_target_pairs={{0,24},{4,28},{8,16},{12,20},{16,8},{20,12},{24,0},{28,4},{1,25},{... | collective-permute-start | bytes 516104 | tf_op jit(solution)/shard_map/ppermute | solution.py:445
  7.7 0.0 collective-permute-start.1
  7.8 0.0 copy-done
  7.8 2.3 %shard_map.69 = (bf16[224,384]{1,0:T(8,128)(2,1)S(1)}, bf16[224,384]{1,0:T(8,128)(2,1)S(1)}, bf16[224,384]{1,0:T(8,128)(2,1)S(1)}, bf16[224,384]{1,0:T(8,128)(2,...) custom-call(bf16[1152,384]{1,0:T(8,128)(2,1)S(1)} %get-tuple-element.29.normed_ref, ...), custom_call_target="tpu_custom_call" | custom-call | flops 1146617856 | bytes 8388608 | tf_op jit(solution)/shard_map/pallas_call | solution.py:510
  10.1 0.0 copy-start.1
  10.1 0.0 copy-start.2
  10.1 0.3 collective-permute-start.2
  10.4 1.9 %collective-permute-start.3 = (bf16[224,384]{1,0:T(8,128)(2,1)S(1)}, bf16[224,384]{1,0:T(8,128)(2,1)S(1)}, u32[]{:S(2)}, u32[]{:S(2)}) collective-permute-start(bf16[224,384]{1,0:T(8,128)(2,1)S(1)} %get-tuple-element.37), channel_id=1, source_target_pairs={{0,8},{4,12},{8,0},{12,4},{16,24},{20,28},{24,16},{28,20},{1,9},{5... | collective-permute-start | bytes 516104 | tf_op jit(solution)/shard_map/ppermute | solution.py:445
  12.3 1.5 %collective-permute-start.4 = (bf16[224,384]{1,0:T(8,128)(2,1)S(1)}, bf16[224,384]{1,0:T(8,128)(2,1)S(1)}, u32[]{:S(2)}, u32[]{:S(2)}) collective-permute-start(bf16[224,384]{1,0:T(8,128)(2,1)S(1)} %get-tuple-element.38), channel_id=1, source_target_pairs={{0,16},{4,20},{8,24},{12,28},{16,0},{20,4},{24,8},{28,12},{1,17},{... | collective-permute-start | bytes 516104 | tf_op jit(solution)/shard_map/ppermute | solution.py:445
  13.8 0.0 collective-permute-done.rest_0_
  13.8 0.0 collective-permute-start.5
  13.8 2.4 %collective-permute-done.1.rest_1_ = bf16[224,384]{1,0:T(8,128)(2,1)S(1)} collective-permute-done((bf16[224,384]{1,0:T(8,128)(2,1)S(1)}, bf16[224,384]{1,0:T(8,128)(2,1)S(1)}, u32[]{:S(2)}, u32[]{:S(2)}) %collective-permute-start.1) | collective-permute-done | bytes 172064 | tf_op jit(solution)/shard_map/ppermute | solution.py:445
  16.2 1.9 %collective-permute-start.6 = (bf16[224,384]{1,0:T(8,128)(2,1)S(1)}, bf16[224,384]{1,0:T(8,128)(2,1)S(1)}, u32[]{:S(2)}, u32[]{:S(2)}) collective-permute-start(bf16[224,384]{1,0:T(8,128)(2,1)S(1)} %get-tuple-element.40), channel_id=1, source_target_pairs={{0,20},{4,16},{8,28},{12,24},{16,4},{20,0},{24,12},{28,8},{1,21},{... | collective-permute-start | bytes 516104 | tf_op jit(solution)/shard_map/ppermute | solution.py:445
  18.1 0.0 collective-permute-done.2.rest_2_
  18.1 0.0 copy-done.4
  18.1 1.6 %collective-permute-start.7 = (bf16[4,1152]{1,0:T(4,128)(2,1)S(1)}, bf16[4,1152]{1,0:T(4,128)(2,1)S(1)}, u32[]{:S(2)}, u32[]{:S(2)}) collective-permute-start(bf16[4,1152]{1,0:T(4,128)(2,1)S(1)} %copy-done.4), channel_id=1, source_target_pairs={{1,0},{0,1},{3,2},{2,3},{6,4},{7,5},{4,6},{5,7},{11,8},{10,9},{9,1... | collective-permute-start | bytes 27656 | tf_op jit(solution)/shard_map/ppermute | solution.py:445
  19.7 0.0 copy-done.3
  19.7 0.2 shard_map.70
  19.9 1.8 %collective-permute-done.7.rest_8_ = bf16[4,1152]{1,0:T(4,128)(2,1)S(1)} collective-permute-done((bf16[4,1152]{1,0:T(4,128)(2,1)S(1)}, bf16[4,1152]{1,0:T(4,128)(2,1)S(1)}, u32[]{:S(2)}, u32[]{:S(2)}) %collective-permute-start.7) | collective-permute-done | bytes 9248 | tf_op jit(solution)/shard_map/ppermute | solution.py:445
  21.8 0.0 collective-permute-done.3.rest_4_
  21.8 0.0 collective-permute-done.4.rest_5_
  21.8 0.7 %collective-permute-done.5.rest_6_ = bf16[224,384]{1,0:T(8,128)(2,1)S(1)} collective-permute-done((bf16[224,384]{1,0:T(8,128)(2,1)S(1)}, bf16[224,384]{1,0:T(8,128)(2,1)S(1)}, u32[]{:S(2)}, u32[]{:S(2)}) %collective-permute-start.5) | collective-permute-done | bytes 172064 | tf_op jit(solution)/shard_map/ppermute | solution.py:445
  22.4 0.6 %collective-permute-done.6.rest_7_ = bf16[224,384]{1,0:T(8,128)(2,1)S(1)} collective-permute-done((bf16[224,384]{1,0:T(8,128)(2,1)S(1)}, bf16[224,384]{1,0:T(8,128)(2,1)S(1)}, u32[]{:S(2)}, u32[]{:S(2)}) %collective-permute-start.6) | collective-permute-done | bytes 172064 | tf_op jit(solution)/shard_map/ppermute | solution.py:445
  23.1 7.9 %shard_map.71 = (bf16[96,384]{1,0:T(8,128)(2,1)S(1)}, bf16[96,384]{1,0:T(8,128)(2,1)S(1)}, bf16[96,384]{1,0:T(8,128)(2,1)S(1)}, bf16[96,384]{1,0:T(8,128)(2,1)S(...) custom-call(s32[1,3072]{1,0:T(1,128)S(1)} %copy-done.3, ...), custom_call_target="tpu_custom_call" | custom-call | flops 905969664 | bytes 8388608 | tf_op jit(solution)/shard_map/pallas_call | solution.py:563
  31.0 2.3 %collective-permute-start.8 = (bf16[96,384]{1,0:T(8,128)(2,1)S(1)}, bf16[96,384]{1,0:T(8,128)(2,1)S(1)}, u32[]{:S(2)}, u32[]{:S(2)}) collective-permute-start(bf16[96,384]{1,0:T(8,128)(2,1)S(1)} %get-tuple-element.42), channel_id=1, source_target_pairs={{0,24},{4,28},{8,16},{12,20},{16,8},{20,12},{24,0},{28,4},{1,25},{... | collective-permute-start | bytes 221192 | tf_op jit(solution)/shard_map/ppermute | solution.py:445
  33.2 0.2 collective-permute-start.9
  33.4 1.8 %collective-permute-start.10 = (bf16[96,384]{1,0:T(8,128)(2,1)S(1)}, bf16[96,384]{1,0:T(8,128)(2,1)S(1)}, u32[]{:S(2)}, u32[]{:S(2)}) collective-permute-start(bf16[96,384]{1,0:T(8,128)(2,1)S(1)} %get-tuple-element.44), channel_id=1, source_target_pairs={{0,8},{4,12},{8,0},{12,4},{16,24},{20,28},{24,16},{28,20},{1,9},{5... | collective-permute-start | bytes 221192 | tf_op jit(solution)/shard_map/ppermute | solution.py:445
  35.2 1.2 %collective-permute-start.11 = (bf16[96,384]{1,0:T(8,128)(2,1)S(1)}, bf16[96,384]{1,0:T(8,128)(2,1)S(1)}, u32[]{:S(2)}, u32[]{:S(2)}) collective-permute-start(bf16[96,384]{1,0:T(8,128)(2,1)S(1)} %get-tuple-element.45), channel_id=1, source_target_pairs={{0,16},{4,20},{8,24},{12,28},{16,0},{20,4},{24,8},{28,12},{1,17},{... | collective-permute-start | bytes 221192 | tf_op jit(solution)/shard_map/ppermute | solution.py:445
  36.4 0.0 collective-permute-start.12
  36.4 0.0 collective-permute-done.8.rest_0_
  36.4 0.8 %collective-permute-start.13 = (bf16[96,384]{1,0:T(8,128)(2,1)S(1)}, bf16[96,384]{1,0:T(8,128)(2,1)S(1)}, u32[]{:S(2)}, u32[]{:S(2)}) collective-permute-start(bf16[96,384]{1,0:T(8,128)(2,1)S(1)} %get-tuple-element.47), channel_id=1, source_target_pairs={{0,20},{4,16},{8,28},{12,24},{16,4},{20,0},{24,12},{28,8},{1,21},{... | collective-permute-start | bytes 221192 | tf_op jit(solution)/shard_map/ppermute | solution.py:445
  37.2 1.3 %collective-permute-done.9.rest_1_ = bf16[96,384]{1,0:T(8,128)(2,1)S(1)} collective-permute-done((bf16[96,384]{1,0:T(8,128)(2,1)S(1)}, bf16[96,384]{1,0:T(8,128)(2,1)S(1)}, u32[]{:S(2)}, u32[]{:S(2)}) %collective-permute-start.9) | collective-permute-done | bytes 73760 | tf_op jit(solution)/shard_map/ppermute | solution.py:445
  38.5 0.3 collective-permute-start.14
  38.8 1.0 %collective-permute-done.10.rest_2_ = bf16[96,384]{1,0:T(8,128)(2,1)S(1)} collective-permute-done((bf16[96,384]{1,0:T(8,128)(2,1)S(1)}, bf16[96,384]{1,0:T(8,128)(2,1)S(1)}, u32[]{:S(2)}, u32[]{:S(2)}) %collective-permute-start.10) | collective-permute-done | bytes 73760 | tf_op jit(solution)/shard_map/ppermute | solution.py:445
  39.8 0.7 %collective-permute-done.11.rest_3_ = bf16[96,384]{1,0:T(8,128)(2,1)S(1)} collective-permute-done((bf16[96,384]{1,0:T(8,128)(2,1)S(1)}, bf16[96,384]{1,0:T(8,128)(2,1)S(1)}, u32[]{:S(2)}, u32[]{:S(2)}) %collective-permute-start.11) | collective-permute-done | bytes 73760 | tf_op jit(solution)/shard_map/ppermute | solution.py:445
  40.4 1.1 %collective-permute-done.12.rest_4_ = bf16[96,384]{1,0:T(8,128)(2,1)S(1)} collective-permute-done((bf16[96,384]{1,0:T(8,128)(2,1)S(1)}, bf16[96,384]{1,0:T(8,128)(2,1)S(1)}, u32[]{:S(2)}, u32[]{:S(2)}) %collective-permute-start.12) | collective-permute-done | bytes 73760 | tf_op jit(solution)/shard_map/ppermute | solution.py:445
  41.5 0.2 collective-permute-done.13.rest_5_
  41.7 0.0 collective-permute-done.14.rest_6_
  41.7 0.0 copy-done.1
  41.7 0.0 copy-done.2
  41.7 2.4 %shard_map.72 = (bf16[384,1152]{1,0:T(8,128)(2,1)}, f32[1,4]{1,0:T(1,128)}) custom-call(bf16[384,1152]{1,0:T(8,128)(2,1)S(1)} %bitcast.7, bf16[576,1152]{1,0:T(8,128)(2,1)S(1)} %copy-done.2, bf16[4,1152]{1,0:T(4,128)(2,1)S(1)} %copy-done.4, bf16[96,384]{1,0:T(8,128)(2,1)S(1)} %collective-permute-done.8.rest_0_, ...), custom_call_target="tpu_custom_call" | custom-call | flops 509607936 | bytes 8388608 | tf_op jit(solution)/shard_map/pallas_call | solution.py:592
Async XLA Ops:
  0.6 7.1 %copy-start = (bf16[1152,1728]{0,1:T(8,128)(2,1)S(1)}, bf16[1152,1728]{0,1:T(8,128)(2,1)}, u32[]{:S(2)}) copy-start(bf16[1152,1728]{0,1:T(8,128)(2,1)} %param.7) | copy-start | bytes 11943940
  0.6 17.5 %copy-start.4 = (bf16[4,1152]{1,0:T(4,128)(2,1)S(1)}, bf16[4,1152]{1,0:T(4,128)(2,1)}, u32[]{:S(2)}) copy-start(bf16[4,1152]{1,0:T(4,128)(2,1)} %text_ref.1) | copy-start | bytes 27652
  0.7 19.0 %copy-start.3 = (s32[1,3072]{1,0:T(1,128)S(1)}, s32[1,3072]{1,0:T(1,128)}, u32[]{:S(2)}) copy-start(s32[1,3072]{1,0:T(1,128)} %ids_ref.5) | copy-start | bytes 36868
  3.8 10.0 %collective-permute-start = (bf16[224,384]{1,0:T(8,128)(2,1)S(1)}, bf16[224,384]{1,0:T(8,128)(2,1)S(1)}, u32[]{:S(2)}, u32[]{:S(2)}) collective-permute-start(bf16[224,384]{1,0:T(8,128)(2,1)S(1)} %get-tuple-element.27), channel_id=1, source_target_pairs={{0,24},{4,28},{8,16},{12,20},{16,8},{20,12},{24,0},{28,4},{1,25},{... | collective-permute-start | bytes 516104 | tf_op jit(solution)/shard_map/ppermute | solution.py:445
  7.7 8.5 %collective-permute-start.1 = (bf16[224,384]{1,0:T(8,128)(2,1)S(1)}, bf16[224,384]{1,0:T(8,128)(2,1)S(1)}, u32[]{:S(2)}, u32[]{:S(2)}) collective-permute-start(bf16[224,384]{1,0:T(8,128)(2,1)S(1)} %get-tuple-element.28), channel_id=1, source_target_pairs={{0,28},{4,24},{8,20},{12,16},{16,12},{20,8},{24,4},{28,0},{1,29},{... | collective-permute-start | bytes 516104 | tf_op jit(solution)/shard_map/ppermute | solution.py:445
  10.1 31.6 %copy-start.1 = (bf16[1,384,1152]{2,1,0:T(8,128)(2,1)S(1)}, bf16[1,384,1152]{2,1,0:T(8,128)(2,1)}, u32[]{:S(2)}) copy-start(bf16[1,384,1152]{2,1,0:T(8,128)(2,1)} %param.5) | copy-start | bytes 2654212
  10.1 31.6 %copy-start.2 = (bf16[576,1152]{1,0:T(8,128)(2,1)S(1)}, bf16[576,1152]{1,0:T(8,128)(2,1)}, u32[]{:S(2)}) copy-start(bf16[576,1152]{1,0:T(8,128)(2,1)} %out_weight_ref.1) | copy-start | bytes 3981316
  10.1 8.0 %collective-permute-start.2 = (bf16[224,384]{1,0:T(8,128)(2,1)S(1)}, bf16[224,384]{1,0:T(8,128)(2,1)S(1)}, u32[]{:S(2)}, u32[]{:S(2)}) collective-permute-start(bf16[224,384]{1,0:T(8,128)(2,1)S(1)} %get-tuple-element.31), channel_id=1, source_target_pairs={{0,4},{4,0},{8,12},{12,8},{16,20},{20,16},{24,28},{28,24},{1,5},{5... | collective-permute-start | bytes 516104 | tf_op jit(solution)/shard_map/ppermute | solution.py:445
  10.4 11.4 %collective-permute-start.3 = (bf16[224,384]{1,0:T(8,128)(2,1)S(1)}, bf16[224,384]{1,0:T(8,128)(2,1)S(1)}, u32[]{:S(2)}, u32[]{:S(2)}) collective-permute-start(bf16[224,384]{1,0:T(8,128)(2,1)S(1)} %get-tuple-element.37), channel_id=1, source_target_pairs={{0,8},{4,12},{8,0},{12,4},{16,24},{20,28},{24,16},{28,20},{1,9},{5... | collective-permute-start | bytes 516104 | tf_op jit(solution)/shard_map/ppermute | solution.py:445
  12.3 9.5 %collective-permute-start.4 = (bf16[224,384]{1,0:T(8,128)(2,1)S(1)}, bf16[224,384]{1,0:T(8,128)(2,1)S(1)}, u32[]{:S(2)}, u32[]{:S(2)}) collective-permute-start(bf16[224,384]{1,0:T(8,128)(2,1)S(1)} %get-tuple-element.38), channel_id=1, source_target_pairs={{0,16},{4,20},{8,24},{12,28},{16,0},{20,4},{24,8},{28,12},{1,17},{... | collective-permute-start | bytes 516104 | tf_op jit(solution)/shard_map/ppermute | solution.py:445
  13.8 8.6 %collective-permute-start.5 = (bf16[224,384]{1,0:T(8,128)(2,1)S(1)}, bf16[224,384]{1,0:T(8,128)(2,1)S(1)}, u32[]{:S(2)}, u32[]{:S(2)}) collective-permute-start(bf16[224,384]{1,0:T(8,128)(2,1)S(1)} %get-tuple-element.39), channel_id=1, source_target_pairs={{0,12},{4,8},{8,4},{12,0},{16,28},{20,24},{24,20},{28,16},{1,13},{... | collective-permute-start | bytes 516104 | tf_op jit(solution)/shard_map/ppermute | solution.py:445
  16.2 6.9 %collective-permute-start.6 = (bf16[224,384]{1,0:T(8,128)(2,1)S(1)}, bf16[224,384]{1,0:T(8,128)(2,1)S(1)}, u32[]{:S(2)}, u32[]{:S(2)}) collective-permute-start(bf16[224,384]{1,0:T(8,128)(2,1)S(1)} %get-tuple-element.40), channel_id=1, source_target_pairs={{0,20},{4,16},{8,28},{12,24},{16,4},{20,0},{24,12},{28,8},{1,21},{... | collective-permute-start | bytes 516104 | tf_op jit(solution)/shard_map/ppermute | solution.py:445
  18.1 3.7 %collective-permute-start.7 = (bf16[4,1152]{1,0:T(4,128)(2,1)S(1)}, bf16[4,1152]{1,0:T(4,128)(2,1)S(1)}, u32[]{:S(2)}, u32[]{:S(2)}) collective-permute-start(bf16[4,1152]{1,0:T(4,128)(2,1)S(1)} %copy-done.4), channel_id=1, source_target_pairs={{1,0},{0,1},{3,2},{2,3},{6,4},{7,5},{4,6},{5,7},{11,8},{10,9},{9,1... | collective-permute-start | bytes 27656 | tf_op jit(solution)/shard_map/ppermute | solution.py:445
  31.0 5.5 %collective-permute-start.8 = (bf16[96,384]{1,0:T(8,128)(2,1)S(1)}, bf16[96,384]{1,0:T(8,128)(2,1)S(1)}, u32[]{:S(2)}, u32[]{:S(2)}) collective-permute-start(bf16[96,384]{1,0:T(8,128)(2,1)S(1)} %get-tuple-element.42), channel_id=1, source_target_pairs={{0,24},{4,28},{8,16},{12,20},{16,8},{20,12},{24,0},{28,4},{1,25},{... | collective-permute-start | bytes 221192 | tf_op jit(solution)/shard_map/ppermute | solution.py:445
  33.2 5.2 %collective-permute-start.9 = (bf16[96,384]{1,0:T(8,128)(2,1)S(1)}, bf16[96,384]{1,0:T(8,128)(2,1)S(1)}, u32[]{:S(2)}, u32[]{:S(2)}) collective-permute-start(bf16[96,384]{1,0:T(8,128)(2,1)S(1)} %get-tuple-element.43), channel_id=1, source_target_pairs={{0,28},{4,24},{8,20},{12,16},{16,12},{20,8},{24,4},{28,0},{1,29},{... | collective-permute-start | bytes 221192 | tf_op jit(solution)/shard_map/ppermute | solution.py:445
  33.4 6.3 %collective-permute-start.10 = (bf16[96,384]{1,0:T(8,128)(2,1)S(1)}, bf16[96,384]{1,0:T(8,128)(2,1)S(1)}, u32[]{:S(2)}, u32[]{:S(2)}) collective-permute-start(bf16[96,384]{1,0:T(8,128)(2,1)S(1)} %get-tuple-element.44), channel_id=1, source_target_pairs={{0,8},{4,12},{8,0},{12,4},{16,24},{20,28},{24,16},{28,20},{1,9},{5... | collective-permute-start | bytes 221192 | tf_op jit(solution)/shard_map/ppermute | solution.py:445
  35.2 5.2 %collective-permute-start.11 = (bf16[96,384]{1,0:T(8,128)(2,1)S(1)}, bf16[96,384]{1,0:T(8,128)(2,1)S(1)}, u32[]{:S(2)}, u32[]{:S(2)}) collective-permute-start(bf16[96,384]{1,0:T(8,128)(2,1)S(1)} %get-tuple-element.45), channel_id=1, source_target_pairs={{0,16},{4,20},{8,24},{12,28},{16,0},{20,4},{24,8},{28,12},{1,17},{... | collective-permute-start | bytes 221192 | tf_op jit(solution)/shard_map/ppermute | solution.py:445
  36.4 5.1 %collective-permute-start.12 = (bf16[96,384]{1,0:T(8,128)(2,1)S(1)}, bf16[96,384]{1,0:T(8,128)(2,1)S(1)}, u32[]{:S(2)}, u32[]{:S(2)}) collective-permute-start(bf16[96,384]{1,0:T(8,128)(2,1)S(1)} %get-tuple-element.46), channel_id=1, source_target_pairs={{0,12},{4,8},{8,4},{12,0},{16,28},{20,24},{24,20},{28,16},{1,13},{... | collective-permute-start | bytes 221192 | tf_op jit(solution)/shard_map/ppermute | solution.py:445
  36.4 5.3 %collective-permute-start.13 = (bf16[96,384]{1,0:T(8,128)(2,1)S(1)}, bf16[96,384]{1,0:T(8,128)(2,1)S(1)}, u32[]{:S(2)}, u32[]{:S(2)}) collective-permute-start(bf16[96,384]{1,0:T(8,128)(2,1)S(1)} %get-tuple-element.47), channel_id=1, source_target_pairs={{0,20},{4,16},{8,28},{12,24},{16,4},{20,0},{24,12},{28,8},{1,21},{... | collective-permute-start | bytes 221192 | tf_op jit(solution)/shard_map/ppermute | solution.py:445
  38.5 3.2 %collective-permute-start.14 = (bf16[96,384]{1,0:T(8,128)(2,1)S(1)}, bf16[96,384]{1,0:T(8,128)(2,1)S(1)}, u32[]{:S(2)}, u32[]{:S(2)}) collective-permute-start(bf16[96,384]{1,0:T(8,128)(2,1)S(1)} %get-tuple-element.48), channel_id=1, source_target_pairs={{0,4},{4,0},{8,12},{12,8},{16,20},{20,16},{24,28},{28,24},{1,5},{5... | collective-permute-start | bytes 221192 | tf_op jit(solution)/shard_map/ppermute | solution.py:445

commit v15 on v14

--- a/solution.py
+++ b/solution.py
@@ -21,6 +21,7 @@
 ORDER = (6, 7, 2, 4, 3, 5, 1, 0)
 EARLY = (6, 7, 1, 0)
 LATE = (2, 4, 3, 5)
+SECOND = (1, 2, 0)
 
 logit_scale = 30.0
 logit_bias = -5.0
@@ -78,55 +79,67 @@
     return lax.div(own, 2), lax.rem(own, 2)
 
 
-def far_kernel(images, piggy, ids_ref, rows_ref, weight_ref, normed_ref, sums_ref, same_ref, cross_ref, own_ids, rows_held, weight, id_sem, row_sem, sems):
+def project_pair(weight, normed, sums, pair):
+    turned = jnp.dot(weight, normed, preferred_element_type=jnp.float32)
+    wide = turned.shape[0] // 3
+    return head_blocks(turned[:wide], turned[wide : 2 * wide], turned[2 * wide :], sums, pair)
+
+
+def far_kernel(images, piggy, ids_ref, rows_ref, weight_ref, normed_ref, sums_ref, rest_ref, same_ref, cross_ref, own_ids, rows_held, weight, id_sem, row_sems, sems):
     count, depth = rows_ref.shape
     width = weight_ref.shape[0] // 3
-    wide = weight.shape[1]
-    rows_fetch = pltpu.make_async_copy(rows_ref, rows_held, row_sem)
-    rows_fetch.start()
+    wide = weight.shape[0] // 3
+    pieces = row_sems.shape[0]
+    step = count // pieces
+    cuts = [slice(piece * step, (piece + 1) * step) for piece in range(pieces)]
+    row_fetches = [
+        pltpu.make_async_copy(rows_ref.at[cut], rows_held.at[cut], row_sems.at[piece])
+        for piece, cut in enumerate(cuts)
+    ]
+    for fetch in row_fetches:
+        fetch.start()
     own = pl.multiple_of(lax.axis_index("grp") * count, LANES)
     ids_fetch = pltpu.make_async_copy(ids_ref.at[:, pl.ds(own, count)], own_ids, id_sem)
     ids_fetch.start()
     pair, core = place_in_group()
-    pair = jnp.bitwise_xor(pair, 3)
     fetches = []
-    for at in range(3):
-        first = pl.multiple_of(at * width + pair * wide, 16)
-        fetches.append(pltpu.make_async_copy(weight_ref.at[pl.ds(first, wide)], weight.at[at], sems.at[at]))
-    for fetch in fetches:
-        fetch.start()
-    rows_fetch.wait()
-    rows = rows_held[...]
-    values = rows.astype(jnp.float32)
-    center = values - jnp.mean(values, axis=1, keepdims=True)
-    spread = jnp.mean(center * center, axis=1, keepdims=True)
-    normed = (center * lax.rsqrt(spread + 1e-06)).astype(jnp.bfloat16)
-    normed_ref[...] = normed.T
+    for place, move in enumerate((3,) + SECOND):
+        for at in range(3):
+            first = pl.multiple_of(at * width + jnp.bitwise_xor(pair, move) * wide, 16)
+            if place == 0:
+                target = weight.at[at * wide : (at + 1) * wide]
+            else:
+                target = rest_ref.at[place - 1, at * wide : (at + 1) * wide]
+            fetches.append(
+                pltpu.make_async_copy(weight_ref.at[pl.ds(first, wide)], target, sems.at[3 * place + at])
+            )
+            fetches[-1].start()
+    for fetch, cut in zip(row_fetches, cuts):
+        fetch.wait()
+        values = rows_held[cut, :].astype(jnp.float32)
+        center = values - jnp.mean(values, axis=1, keepdims=True)
+        spread = jnp.mean(center * center, axis=1, keepdims=True)
+        normed_ref[:, cut] = (center * lax.rsqrt(spread + 1e-06)).astype(jnp.bfloat16).T
     ids_fetch.wait()
     if piggy:
-        sums = jnp.dot(image_rows(own_ids[...], images), rows, preferred_element_type=jnp.float32)
+        sums = jnp.dot(image_rows(own_ids[...], images), rows_held[...], preferred_element_type=jnp.float32)
         sums_ref[...] = split_in_two(sums, images)
-    for fetch in fetches:
+    for fetch in fetches[:3]:
         fetch.wait()
-    parts = [
-        jnp.dot(weight[at], normed_ref[...], preferred_element_type=jnp.float32) for at in range(3)
-    ]
-    store_by_core(core, head_blocks(*parts, sums_ref if piggy else None, pair), same_ref, cross_ref)
+    blocks = project_pair(
+        weight[...], normed_ref[...], sums_ref if piggy else None, jnp.bitwise_xor(pair, 3)
+    )
+    store_by_core(core, blocks, same_ref, cross_ref)
+    for fetch in fetches[3:]:
+        fetch.wait()
 
 
 def near_kernel(piggy, normed_ref, sums_ref, weight_ref, *out_refs):
-    width = weight_ref.shape[0] // 3
-    wide = 2 * width // HEADS
     own, core = place_in_group()
-    for step, move in enumerate((1, 2, 0)):
-        pair = jnp.bitwise_xor(own, move)
-        parts = []
-        for at in range(3):
-            here = pl.ds(pl.multiple_of(at * width + pair * wide, 16), wide)
-            parts.append(
-                jnp.dot(weight_ref[here, :], normed_ref[...], preferred_element_type=jnp.float32)
-            )
-        blocks = head_blocks(*parts, sums_ref if piggy else None, pair)
+    for step, move in enumerate(SECOND):
+        blocks = project_pair(
+            weight_ref[step], normed_ref[...], sums_ref if piggy else None, jnp.bitwise_xor(own, move)
+        )
         store_by_core(core, blocks, *out_refs[2 * step : 2 * step + 2])
 
 
@@ -247,9 +260,21 @@
     queries[PADDED:, there] = jnp.zeros((LANES - PADDED, block_ref.shape[1]), jnp.bfloat16)
 
 
-def prepare_kernel(images, halo, ids_ref, *rest):
-    got_refs, (keys, marks, before) = rest[: len(EARLY)], rest[len(EARLY) :]
+def prepare_kernel(images, halo, ids_ref, out_weight_ref, *rest):
+    got_refs, (keys, marks, before, weight, sems) = rest[: len(EARLY)], rest[len(EARLY) :]
     count = got_refs[0].shape[1]
+    fetches = []
+    for step, by in enumerate(ORDER):
+        head = jnp.bitwise_xor(lax.rem(lax.axis_index("grp"), HEADS), by)
+        first = lax.div(head, 2) * (2 * SIZE) + lax.rem(head, 2) * (SIZE - SPARE)
+        fetches.append(
+            pltpu.make_async_copy(
+                out_weight_ref.at[pl.ds(pl.multiple_of(first, 16), PADDED)],
+                weight.at[step * PADDED : (step + 1) * PADDED],
+                sems.at[step],
+            )
+        )
+        fetches[-1].start()
     before[...] = count_before(images, ids_ref[...])
     write_marks(images, ids_ref[...], marks)
     own = lax.rem(lax.axis_index("grp"), HEADS)
@@ -257,6 +282,8 @@
         first = jnp.bitwise_xor(own, by) * count
         here = pl.ds(pl.multiple_of(halo + first, LANES), count)
         keys[step * count : (step + 1) * count, :] = turned_keys(marks[0, :, here], ref)
+    for fetch in fetches:
+        fetch.wait()
 
 
 def attend_kernel(images, piggy, halo, ids_ref, before_ref, marks, early_keys, *rest):
@@ -328,15 +355,12 @@
             out_ref[padded:] = below
 
 
-def joined_heads(got_refs, out_weight_ref, flat, weight):
+def joined_heads(got_refs, flat):
     own = lax.rem(lax.axis_index("grp"), HEADS)
     spares = []
     for step, (by, got_ref) in enumerate(zip(ORDER, got_refs)):
-        head = jnp.bitwise_xor(own, by)
-        odd = lax.rem(head, 2)
-        first = pl.multiple_of(lax.div(head, 2) * (2 * SIZE) + odd * (SIZE - SPARE), 16)
+        odd = lax.rem(jnp.bitwise_xor(own, by), 2)
         at = step * PADDED
-        weight[at : at + PADDED] = out_weight_ref[pl.ds(first, PADDED), :]
         top = got_ref[0:16].astype(jnp.float32)
         bottom = got_ref[PADDED - 16 : PADDED].astype(jnp.float32)
         spares.append(jnp.where(odd == 1, top[:SPARE], bottom[SPARE:]))
@@ -348,18 +372,19 @@
     return spares
 
 
-def send_mixed_rows(rows_ref, flat, weight, turned, mixed, mixed_ref, sems):
-    turned[...] = flat[...].T
+def send_mixed_rows(rows_ref, weight_ref, turned, mixed, mixed_ref, sems):
     pieces = sems.shape[0]
-    step = rows_ref.shape[0] // pieces
-    copies = []
+    count = rows_ref.shape[0]
+    step = rows_ref.shape[1] // pieces
+    copies, below = [], []
     for piece in range(pieces):
         cut = slice(piece * step, (piece + 1) * step)
-        added = jnp.dot(turned[cut, :], weight[...], preferred_element_type=jnp.float32)
-        mixed[cut, :] = (rows_ref[cut, :].astype(jnp.float32) + added).astype(jnp.bfloat16)
-        copies.append(pltpu.make_async_copy(mixed.at[cut], mixed_ref.at[cut], sems.at[piece]))
+        added = jnp.dot(turned[...], weight_ref[:, cut], preferred_element_type=jnp.float32)
+        mixed[:, cut] = (rows_ref[:, cut].astype(jnp.float32) + added[:count]).astype(jnp.bfloat16)
+        below.append(added[count:])
+        copies.append(pltpu.make_async_copy(mixed.at[:, cut], mixed_ref.at[:, cut], sems.at[piece]))
         copies[-1].start()
-    return copies
+    return copies, jnp.concatenate(below, axis=1)
 
 
 def unit_rows(matrix):
@@ -371,26 +396,26 @@
     return jnp.maximum(logits, 0.0) + jnp.log1p(jnp.exp(-jnp.abs(logits)))
 
 
-def finish_kernel(images, rows_ref, out_weight_ref, text_ref, *rest):
+def finish_kernel(images, rows_ref, weight_ref, text_ref, *rest):
     got_refs, rest = rest[:HEADS], rest[HEADS:]
-    mixed_ref, loss_ref, flat, weight, turned, mixed, sems, pooled_heads, patch_sums, far_texts = rest
-    spares = joined_heads(got_refs, out_weight_ref, flat, weight)
-    copies = send_mixed_rows(rows_ref, flat, weight, turned, mixed, mixed_ref, sems)
+    mixed_ref, loss_ref, flat, turned, mixed, sems, pooled_heads, patch_sums, far_texts = rest
+    spares = joined_heads(got_refs, flat)
     own = lax.rem(lax.axis_index("grp"), HEADS)
+    count = rows_ref.shape[0]
     patch_sums[:, HEADS * LANES :] = spares[0][:, 2 * LANES :]
     for step, (by, spare) in enumerate(zip(ORDER, spares)):
-        pooled_heads[:, step * PADDED : (step + 1) * PADDED] = spare[:, 0:PADDED]
+        pooled_heads[0:SPARE, step * PADDED : (step + 1) * PADDED] = spare[:, 0:PADDED]
         head = jnp.bitwise_xor(own, by)
         patch_sums[:, pl.ds(pl.multiple_of(head * LANES, LANES), LANES)] = spare[:, LANES : 2 * LANES]
         below = got_refs[step][PADDED:].astype(jnp.float32)
-        count = below.shape[1]
         for part in range(patch_sums.shape[1] // count):
             here = slice(part * count, (part + 1) * count)
             far_texts[head, :, here] = below[part * images : (part + 1) * images]
-    pooled = jnp.dot(
-        pooled_heads[...].astype(jnp.bfloat16), weight[...], preferred_element_type=jnp.float32
-    )
-    pooled = pooled + patch_sums[...]
+    pooled_heads[SPARE:, :] = jnp.zeros_like(pooled_heads[SPARE:, :])
+    turned[0:count, :] = flat[...].T
+    turned[count:, :] = pooled_heads[...].astype(jnp.bfloat16)
+    copies, pooled = send_mixed_rows(rows_ref, weight_ref, turned, mixed, mixed_ref, sems)
+    pooled = pooled[0:SPARE] + patch_sums[...]
     pooled = pooled + pltpu.roll(pooled, images, axis=0)
     image_vecs = unit_rows(pooled)
     others = [far_texts[place] for place in range(lax.axis_size("blk") - 1)]
@@ -411,11 +436,12 @@
         copy.wait()
 
 
-def mix_kernel(rows_ref, out_weight_ref, *rest):
+def mix_kernel(rows_ref, weight_ref, *rest):
     got_refs, rest = rest[:HEADS], rest[HEADS:]
-    mixed_ref, flat, weight, turned, mixed, sems = rest
-    joined_heads(got_refs, out_weight_ref, flat, weight)
-    for copy in send_mixed_rows(rows_ref, flat, weight, turned, mixed, mixed_ref, sems):
+    mixed_ref, flat, turned, mixed, sems = rest
+    joined_heads(got_refs, flat)
+    turned[...] = flat[...].T
+    for copy in send_mixed_rows(rows_ref, weight_ref, turned, mixed, mixed_ref, sems)[0]:
         copy.wait()
 
 
@@ -492,28 +518,33 @@
 
     block = shape((3 * size + SPARE, count), bf16)
     hbm = pl.BlockSpec(memory_space=pltpu.HBM)
-    turned_weight = qkv_weight.T
-    normed, sums, *sent = call(
+    normed, sums, rest, *sent = call(
         functools.partial(far_kernel, images, piggy),
-        (shape((depth, count), bf16), shape((SPARE, depth), f32), block, block),
+        (
+            shape((depth, count), bf16),
+            shape((SPARE, depth), f32),
+            shape((len(SECOND), 6 * size, depth), bf16),
+            block,
+            block,
+        ),
         [
             pltpu.VMEM((1, count), jnp.int32),
             pltpu.VMEM((count, depth), bf16),
-            pltpu.VMEM((3, 2 * size, depth), bf16),
-            pltpu.SemaphoreType.DMA,
+            pltpu.VMEM((6 * size, depth), bf16),
             pltpu.SemaphoreType.DMA,
             pltpu.SemaphoreType.DMA((3,)),
+            pltpu.SemaphoreType.DMA((3 + 3 * len(SECOND),)),
         ],
         [hbm] * 3,
         2 * count * depth * 6 * size,
-    )(in_hbm(segment_ids), in_hbm(rows), in_hbm(turned_weight))
+    )(in_hbm(segment_ids), in_hbm(rows), in_hbm(qkv_weight.T))
     sent += call(
         functools.partial(near_kernel, piggy),
-        (block,) * 6,
+        (block,) * (2 * len(SECOND)),
         [],
         in_vmem(3),
         2 * count * depth * 18 * size,
-    )(normed, sums, turned_weight)
+    )(normed, sums, rest)
     sent = dict(zip((6, 7, 2, 3, 4, 5, 0, 1), sent))
     if piggy:
         late_texts, sent[0] = lax.optimization_barrier((text_embed, sent[0]))
@@ -548,17 +579,18 @@
     reach = length + 2 * halo
     window = min(rounded_up(MAXP + LANES - 1, LANES), reach)
     tile = 2 * LANES
-    early_keys, marks, before = call(
+    early_keys, marks, before, weight = call(
         functools.partial(prepare_kernel, images, halo),
         (
             shape((len(EARLY) * count, LANES), bf16),
             shape((2, SPARE, reach), f32),
             shape((rounded_up(images + 1, SPARE), LANES), jnp.int32),
+            shape((HEADS * padded, depth), bf16),
         ),
-        [],
-        in_vmem(1 + len(EARLY)),
+        [pltpu.SemaphoreType.DMA((HEADS,))],
+        in_vmem(1) + [hbm] + in_vmem(len(EARLY)),
         1 << 30,
-    )(near_ids, *[got[by] for by in EARLY])
+    )(near_ids, in_hbm(out_weight), *[got[by] for by in EARLY])
     operands = [near_ids, before, marks, early_keys, *[got[by] for by in EARLY + LATE], *halos_and_texts]
     answers = call(
         functools.partial(attend_kernel, images, piggy, halo),
@@ -582,8 +614,7 @@
 
     joined = [
         pltpu.VMEM((HEADS * padded, count), bf16),
-        pltpu.VMEM((HEADS * padded, depth), bf16),
-        pltpu.VMEM((count, HEADS * padded), bf16),
+        pltpu.VMEM((count + 2 * SPARE * piggy, HEADS * padded), bf16),
         pltpu.VMEM((count, depth), bf16),
         pltpu.SemaphoreType.DMA((3,)),
     ]
@@ -594,17 +625,17 @@
             (shape((count, depth), bf16), shape((1, images), f32)),
             joined
             + [
-                pltpu.VMEM((SPARE, HEADS * padded), f32),
+                pltpu.VMEM((2 * SPARE, HEADS * padded), f32),
                 pltpu.VMEM((SPARE, depth), f32),
                 pltpu.VMEM((HEADS, images, depth), f32),
             ],
             in_vmem(3 + HEADS),
             flops,
             (hbm, pl.BlockSpec(memory_space=pltpu.VMEM)),
-        )(rows, out_weight, text_embed, *home)
+        )(rows, weight, text_embed, *home)
         return (mixed[None], row_loss[0])
     mixed = call(mix_kernel, shape((count, depth), bf16), joined, in_vmem(2 + HEADS), flops, hbm)(
-        rows, out_weight, *home
+        rows, weight, *home
     )
     own_ids = lax.dynamic_slice_in_dim(segment_ids[0], lax.axis_index("grp") * count, count)
     onehot = (own_ids[None, :] == jnp.arange(images, dtype=jnp.int32)[:, None]).astype(bf16)

time: 44.3 us -> 45.1 us (1.018)
  Pallas kernels: 16 us -> 18.1 us
  waiting for transfers between devices: 9.79 us -> 8.33 us
    ppermute x15, waiting for transfers between devices: 9.79 us -> 8.33 us  [moved(): return lax.ppermute(value, axis, pairs)]
    pallas_call x1, Pallas kernels: 0.24 us -> 1.64 us  [local(): call(functools.partial(prepare_kernel, images, halo), (shape((len(EARLY)...]
    pallas_call x1, Pallas kernels: 3.12 us -> 4.17 us  [local(): call(functools.partial(far_kernel, images, piggy), (shape((depth, count),...]
  transfers between devices with their start and end apart: 15 -> 15, of which waited for: 9 -> 9; matrix products, arithmetic and copies ran while one was open for 0% -> 0% of each run, Pallas kernels for 6% -> 9%
where the time goes in v15:
time: 45.1 us; the launch traced here: 44.9 us
  Pallas kernels  18.1 us (40%)
  starting transfers between devices  17.7 us (39%)
  waiting for transfers between devices  8.33 us (18%)
  between operations  0.69 us (2%)
    ppermute x15, starting transfers between devices, moved(): return lax.ppermute(value, axis, pairs)  17.7 us
    ppermute x15, waiting for transfers between devices, moved(): return lax.ppermute(value, axis, pairs)  8.33 us
    pallas_call x1, Pallas kernels, local(): call(functools.partial(attend_kernel, images, piggy, halo), (shape((padde...  7.51 us
    pallas_call x1, Pallas kernels, local(): call(functools.partial(far_kernel, images, piggy), (shape((depth, count),...  4.17 us
    pallas_call x1, Pallas kernels, local(): call(functools.partial(finish_kernel, images), (shape((count, depth), bf1...  2.52 us
    pallas_call x1, Pallas kernels, local(): call(functools.partial(near_kernel, piggy), (block,) * (2 * len(SECOND)),...  2.31 us
    pallas_call x1, Pallas kernels, local(): call(functools.partial(prepare_kernel, images, halo), (shape((len(EARLY)...  1.64 us
  transfers between devices with their start and end apart: 15, of which 9 were waited for; matrix products, arithmetic and copies ran while one was open for 0% of the time, Pallas kernels for 9%

profile of v15, /device:TPU:0, one launch (start us, length us, event | category | flops | bytes accessed | tf_op | source)
XLA Modules:
  0.0 44.9 jit_solution(8568477108015930329)
XLA Ops:
  0.6 4.2 %shard_map.68 = (bf16[1152,384]{1,0:T(8,128)(2,1)S(1)}, f32[8,1152]{1,0:T(8,128)S(1)}, bf16[3,432,1152]{2,1,0:T(8,128)(2,1)S(1)}, bf16[224,384]{1,0:T(8,128)(2,1)S(1)}, bf16[224,384]{1,0:T(8,128)(2,1)S(1)}) custom-call(s32[1,3072]{1,0:T(1,128)} %ids_ref.5, bf16[384,1152]{1,0:T(8,128)(2,1)} %bitcast.4, bf16[1728,1152]{1,0:T(8,128)(2,1)} %bitcast.6), custom_call_target="tpu_custom_call" | custom-call | flops 382205952 | bytes 8388608 | tf_op jit(solution)/shard_map/pallas_call | solution.py:521
  4.8 0.0 copy-start.2
  4.8 0.0 copy-start.1
  4.8 4.0 %collective-permute-start = (bf16[224,384]{1,0:T(8,128)(2,1)S(1)}, bf16[224,384]{1,0:T(8,128)(2,1)S(1)}, u32[]{:S(2)}, u32[]{:S(2)}) collective-permute-start(bf16[224,384]{1,0:T(8,128)(2,1)S(1)} %get-tuple-element.29), channel_id=1, source_target_pairs={{0,24},{4,28},{8,16},{12,20},{16,8},{20,12},{24,0},{28,4},{1,25},{... | collective-permute-start | bytes 516104 | tf_op jit(solution)/shard_map/ppermute | solution.py:471
  8.8 0.0 collective-permute-start.1
  8.8 2.3 %shard_map.69 = (bf16[224,384]{1,0:T(8,128)(2,1)S(1)}, bf16[224,384]{1,0:T(8,128)(2,1)S(1)}, bf16[224,384]{1,0:T(8,128)(2,1)S(1)}, bf16[224,384]{1,0:T(8,128)(2,...) custom-call(bf16[1152,384]{1,0:T(8,128)(2,1)S(1)} %get-tuple-element.31.normed_ref, ...), custom_call_target="tpu_custom_call" | custom-call | flops 1146617856 | bytes 8388608 | tf_op jit(solution)/shard_map/pallas_call | solution.py:541
  11.1 0.3 collective-permute-start.2
  11.4 1.9 %collective-permute-start.3 = (bf16[224,384]{1,0:T(8,128)(2,1)S(1)}, bf16[224,384]{1,0:T(8,128)(2,1)S(1)}, u32[]{:S(2)}, u32[]{:S(2)}) collective-permute-start(bf16[224,384]{1,0:T(8,128)(2,1)S(1)} %get-tuple-element.41), channel_id=1, source_target_pairs={{0,8},{4,12},{8,0},{12,4},{16,24},{20,28},{24,16},{28,20},{1,9},{5... | collective-permute-start | bytes 516104 | tf_op jit(solution)/shard_map/ppermute | solution.py:471
  13.3 1.5 %collective-permute-start.4 = (bf16[224,384]{1,0:T(8,128)(2,1)S(1)}, bf16[224,384]{1,0:T(8,128)(2,1)S(1)}, u32[]{:S(2)}, u32[]{:S(2)}) collective-permute-start(bf16[224,384]{1,0:T(8,128)(2,1)S(1)} %get-tuple-element.42), channel_id=1, source_target_pairs={{0,16},{4,20},{8,24},{12,28},{16,0},{20,4},{24,8},{28,12},{1,17},{... | collective-permute-start | bytes 516104 | tf_op jit(solution)/shard_map/ppermute | solution.py:471
  14.8 0.0 collective-permute-done.rest_0_
  14.8 0.0 collective-permute-start.5
  14.8 2.5 %collective-permute-done.1.rest_1_ = bf16[224,384]{1,0:T(8,128)(2,1)S(1)} collective-permute-done((bf16[224,384]{1,0:T(8,128)(2,1)S(1)}, bf16[224,384]{1,0:T(8,128)(2,1)S(1)}, u32[]{:S(2)}, u32[]{:S(2)}) %collective-permute-start.1) | collective-permute-done | bytes 172064 | tf_op jit(solution)/shard_map/ppermute | solution.py:471
  17.3 1.9 %collective-permute-start.6 = (bf16[224,384]{1,0:T(8,128)(2,1)S(1)}, bf16[224,384]{1,0:T(8,128)(2,1)S(1)}, u32[]{:S(2)}, u32[]{:S(2)}) collective-permute-start(bf16[224,384]{1,0:T(8,128)(2,1)S(1)} %get-tuple-element.44), channel_id=1, source_target_pairs={{0,20},{4,16},{8,28},{12,24},{16,4},{20,0},{24,12},{28,8},{1,21},{... | collective-permute-start | bytes 516104 | tf_op jit(solution)/shard_map/ppermute | solution.py:471
  19.1 0.0 copy-start
  19.1 0.0 collective-permute-done.2.rest_2_
  19.1 0.0 copy-done.2
  19.1 1.6 %collective-permute-start.7 = (bf16[4,1152]{1,0:T(4,128)(2,1)S(1)}, bf16[4,1152]{1,0:T(4,128)(2,1)S(1)}, u32[]{:S(2)}, u32[]{:S(2)}) collective-permute-start(bf16[4,1152]{1,0:T(4,128)(2,1)S(1)} %copy-done.2), channel_id=1, source_target_pairs={{1,0},{0,1},{3,2},{2,3},{6,4},{7,5},{4,6},{5,7},{11,8},{10,9},{9,1... | collective-permute-start | bytes 27656 | tf_op jit(solution)/shard_map/ppermute | solution.py:471
  20.8 0.0 copy-done.1
  20.8 1.6 %shard_map.70 = (bf16[1536,128]{1,0:T(8,128)(2,1)S(1)}, f32[2,8,3072]{2,1,0:T(8,128)S(1)}, s32[8,128]{1,0:T(8,128)S(1)}, bf16[640,1152]{1,0:T(8,128)(2,1)S(1)}) custom-call(s32[1,3072]{1,0:T(1,128)S(1)} %copy-done.1, bf16[576,1152]{1,0:T(8,128)(2,1)} %out_weight_ref.1, bf16[224,384]{1,0:T(8,128)(2,1)S(1)} %collective-permute-done.rest_0_, ...), custom_call_target="tpu_custom_call" | custom-call | flops 1073741824 | bytes 8388608 | tf_op jit(solution)/shard_map/pallas_call | solution.py:582
  22.4 0.4 collective-permute-done.7.rest_8_
  22.9 0.0 collective-permute-done.3.rest_4_
  22.9 0.0 collective-permute-done.4.rest_5_
  22.9 0.6 %collective-permute-done.5.rest_6_ = bf16[224,384]{1,0:T(8,128)(2,1)S(1)} collective-permute-done((bf16[224,384]{1,0:T(8,128)(2,1)S(1)}, bf16[224,384]{1,0:T(8,128)(2,1)S(1)}, u32[]{:S(2)}, u32[]{:S(2)}) %collective-permute-start.5) | collective-permute-done | bytes 172064 | tf_op jit(solution)/shard_map/ppermute | solution.py:471
  23.5 0.6 %collective-permute-done.6.rest_7_ = bf16[224,384]{1,0:T(8,128)(2,1)S(1)} collective-permute-done((bf16[224,384]{1,0:T(8,128)(2,1)S(1)}, bf16[224,384]{1,0:T(8,128)(2,1)S(1)}, u32[]{:S(2)}, u32[]{:S(2)}) %collective-permute-start.6) | collective-permute-done | bytes 172064 | tf_op jit(solution)/shard_map/ppermute | solution.py:471
  24.1 7.5 %shard_map.71 = (bf16[96,384]{1,0:T(8,128)(2,1)S(1)}, bf16[96,384]{1,0:T(8,128)(2,1)S(1)}, bf16[96,384]{1,0:T(8,128)(2,1)S(1)}, bf16[96,384]{1,0:T(8,128)(2,1)S(...) custom-call(s32[1,3072]{1,0:T(1,128)S(1)} %copy-done.1, ...), custom_call_target="tpu_custom_call" | custom-call | flops 905969664 | bytes 8388608 | tf_op jit(solution)/shard_map/pallas_call | solution.py:595
  31.6 2.3 %collective-permute-start.8 = (bf16[96,384]{1,0:T(8,128)(2,1)S(1)}, bf16[96,384]{1,0:T(8,128)(2,1)S(1)}, u32[]{:S(2)}, u32[]{:S(2)}) collective-permute-start(bf16[96,384]{1,0:T(8,128)(2,1)S(1)} %get-tuple-element.46), channel_id=1, source_target_pairs={{0,24},{4,28},{8,16},{12,20},{16,8},{20,12},{24,0},{28,4},{1,25},{... | collective-permute-start | bytes 221192 | tf_op jit(solution)/shard_map/ppermute | solution.py:471
  33.9 0.2 collective-permute-start.9
  34.1 1.8 %collective-permute-start.10 = (bf16[96,384]{1,0:T(8,128)(2,1)S(1)}, bf16[96,384]{1,0:T(8,128)(2,1)S(1)}, u32[]{:S(2)}, u32[]{:S(2)}) collective-permute-start(bf16[96,384]{1,0:T(8,128)(2,1)S(1)} %get-tuple-element.48), channel_id=1, source_target_pairs={{0,8},{4,12},{8,0},{12,4},{16,24},{20,28},{24,16},{28,20},{1,9},{5... | collective-permute-start | bytes 221192 | tf_op jit(solution)/shard_map/ppermute | solution.py:471
  35.9 1.2 %collective-permute-start.11 = (bf16[96,384]{1,0:T(8,128)(2,1)S(1)}, bf16[96,384]{1,0:T(8,128)(2,1)S(1)}, u32[]{:S(2)}, u32[]{:S(2)}) collective-permute-start(bf16[96,384]{1,0:T(8,128)(2,1)S(1)} %get-tuple-element.49), channel_id=1, source_target_pairs={{0,16},{4,20},{8,24},{12,28},{16,0},{20,4},{24,8},{28,12},{1,17},{... | collective-permute-start | bytes 221192 | tf_op jit(solution)/shard_map/ppermute | solution.py:471
  37.1 0.1 collective-permute-start.12
  37.1 0.0 collective-permute-done.8.rest_0_
  37.1 0.8 %collective-permute-start.13 = (bf16[96,384]{1,0:T(8,128)(2,1)S(1)}, bf16[96,384]{1,0:T(8,128)(2,1)S(1)}, u32[]{:S(2)}, u32[]{:S(2)}) collective-permute-start(bf16[96,384]{1,0:T(8,128)(2,1)S(1)} %get-tuple-element.51), channel_id=1, source_target_pairs={{0,20},{4,16},{8,28},{12,24},{16,4},{20,0},{24,12},{28,8},{1,21},{... | collective-permute-start | bytes 221192 | tf_op jit(solution)/shard_map/ppermute | solution.py:471
  37.9 1.2 %collective-permute-done.9.rest_1_ = bf16[96,384]{1,0:T(8,128)(2,1)S(1)} collective-permute-done((bf16[96,384]{1,0:T(8,128)(2,1)S(1)}, bf16[96,384]{1,0:T(8,128)(2,1)S(1)}, u32[]{:S(2)}, u32[]{:S(2)}) %collective-permute-start.9) | collective-permute-done | bytes 73760 | tf_op jit(solution)/shard_map/ppermute | solution.py:471
  39.1 0.3 collective-permute-start.14
  39.4 1.0 %collective-permute-done.10.rest_2_ = bf16[96,384]{1,0:T(8,128)(2,1)S(1)} collective-permute-done((bf16[96,384]{1,0:T(8,128)(2,1)S(1)}, bf16[96,384]{1,0:T(8,128)(2,1)S(1)}, u32[]{:S(2)}, u32[]{:S(2)}) %collective-permute-start.10) | collective-permute-done | bytes 73760 | tf_op jit(solution)/shard_map/ppermute | solution.py:471
  40.4 0.7 %collective-permute-done.11.rest_3_ = bf16[96,384]{1,0:T(8,128)(2,1)S(1)} collective-permute-done((bf16[96,384]{1,0:T(8,128)(2,1)S(1)}, bf16[96,384]{1,0:T(8,128)(2,1)S(1)}, u32[]{:S(2)}, u32[]{:S(2)}) %collective-permute-start.11) | collective-permute-done | bytes 73760 | tf_op jit(solution)/shard_map/ppermute | solution.py:471
  41.1 1.1 %collective-permute-done.12.rest_4_ = bf16[96,384]{1,0:T(8,128)(2,1)S(1)} collective-permute-done((bf16[96,384]{1,0:T(8,128)(2,1)S(1)}, bf16[96,384]{1,0:T(8,128)(2,1)S(1)}, u32[]{:S(2)}, u32[]{:S(2)}) %collective-permute-start.12) | collective-permute-done | bytes 73760 | tf_op jit(solution)/shard_map/ppermute | solution.py:471
  42.2 0.2 collective-permute-done.13.rest_5_
  42.4 0.0 collective-permute-done.14.rest_6_
  42.4 0.0 copy-done
  42.4 2.5 %shard_map.72 = (bf16[384,1152]{1,0:T(8,128)(2,1)}, f32[1,4]{1,0:T(1,128)}) custom-call(bf16[384,1152]{1,0:T(8,128)(2,1)S(1)} %bitcast.5, bf16[640,1152]{1,0:T(8,128)(2,1)S(1)} %get-tuple-element.37.weight_ref, bf16[4,1152]{1,0:T(4,128)(2,1)S(1)} %copy-done.2, bf16[96,384]{1,0:T(8,128)(2,1)S(1)} %collective-permute-done.8.rest_0_, ...), custom_call_target="tpu_custom_call" | custom-call | flops 509607936 | bytes 8388608 | tf_op jit(solution)/shard_map/pallas_call | solution.py:623
Async XLA Ops:
  4.8 14.3 %copy-start.2 = (bf16[4,1152]{1,0:T(4,128)(2,1)S(1)}, bf16[4,1152]{1,0:T(4,128)(2,1)}, u32[]{:S(2)}) copy-start(bf16[4,1152]{1,0:T(4,128)(2,1)} %text_ref.1) | copy-start | bytes 27652
  4.8 16.0 %copy-start.1 = (s32[1,3072]{1,0:T(1,128)S(1)}, s32[1,3072]{1,0:T(1,128)}, u32[]{:S(2)}) copy-start(s32[1,3072]{1,0:T(1,128)} %ids_ref.5) | copy-start | bytes 36868
  4.8 10.0 %collective-permute-start = (bf16[224,384]{1,0:T(8,128)(2,1)S(1)}, bf16[224,384]{1,0:T(8,128)(2,1)S(1)}, u32[]{:S(2)}, u32[]{:S(2)}) collective-permute-start(bf16[224,384]{1,0:T(8,128)(2,1)S(1)} %get-tuple-element.29), channel_id=1, source_target_pairs={{0,24},{4,28},{8,16},{12,20},{16,8},{20,12},{24,0},{28,4},{1,25},{... | collective-permute-start | bytes 516104 | tf_op jit(solution)/shard_map/ppermute | solution.py:471
  8.8 8.5 %collective-permute-start.1 = (bf16[224,384]{1,0:T(8,128)(2,1)S(1)}, bf16[224,384]{1,0:T(8,128)(2,1)S(1)}, u32[]{:S(2)}, u32[]{:S(2)}) collective-permute-start(bf16[224,384]{1,0:T(8,128)(2,1)S(1)} %get-tuple-element.30), channel_id=1, source_target_pairs={{0,28},{4,24},{8,20},{12,16},{16,12},{20,8},{24,4},{28,0},{1,29},{... | collective-permute-start | bytes 516104 | tf_op jit(solution)/shard_map/ppermute | solution.py:471
  11.1 8.0 %collective-permute-start.2 = (bf16[224,384]{1,0:T(8,128)(2,1)S(1)}, bf16[224,384]{1,0:T(8,128)(2,1)S(1)}, u32[]{:S(2)}, u32[]{:S(2)}) collective-permute-start(bf16[224,384]{1,0:T(8,128)(2,1)S(1)} %get-tuple-element.34), channel_id=1, source_target_pairs={{0,4},{4,0},{8,12},{12,8},{16,20},{20,16},{24,28},{28,24},{1,5},{5... | collective-permute-start | bytes 516104 | tf_op jit(solution)/shard_map/ppermute | solution.py:471
  11.4 11.5 %collective-permute-start.3 = (bf16[224,384]{1,0:T(8,128)(2,1)S(1)}, bf16[224,384]{1,0:T(8,128)(2,1)S(1)}, u32[]{:S(2)}, u32[]{:S(2)}) collective-permute-start(bf16[224,384]{1,0:T(8,128)(2,1)S(1)} %get-tuple-element.41), channel_id=1, source_target_pairs={{0,8},{4,12},{8,0},{12,4},{16,24},{20,28},{24,16},{28,20},{1,9},{5... | collective-permute-start | bytes 516104 | tf_op jit(solution)/shard_map/ppermute | solution.py:471
  13.3 9.6 %collective-permute-start.4 = (bf16[224,384]{1,0:T(8,128)(2,1)S(1)}, bf16[224,384]{1,0:T(8,128)(2,1)S(1)}, u32[]{:S(2)}, u32[]{:S(2)}) collective-permute-start(bf16[224,384]{1,0:T(8,128)(2,1)S(1)} %get-tuple-element.42), channel_id=1, source_target_pairs={{0,16},{4,20},{8,24},{12,28},{16,0},{20,4},{24,8},{28,12},{1,17},{... | collective-permute-start | bytes 516104 | tf_op jit(solution)/shard_map/ppermute | solution.py:471
  14.8 8.7 %collective-permute-start.5 = (bf16[224,384]{1,0:T(8,128)(2,1)S(1)}, bf16[224,384]{1,0:T(8,128)(2,1)S(1)}, u32[]{:S(2)}, u32[]{:S(2)}) collective-permute-start(bf16[224,384]{1,0:T(8,128)(2,1)S(1)} %get-tuple-element.43), channel_id=1, source_target_pairs={{0,12},{4,8},{8,4},{12,0},{16,28},{20,24},{24,20},{28,16},{1,13},{... | collective-permute-start | bytes 516104 | tf_op jit(solution)/shard_map/ppermute | solution.py:471
  17.3 6.9 %collective-permute-start.6 = (bf16[224,384]{1,0:T(8,128)(2,1)S(1)}, bf16[224,384]{1,0:T(8,128)(2,1)S(1)}, u32[]{:S(2)}, u32[]{:S(2)}) collective-permute-start(bf16[224,384]{1,0:T(8,128)(2,1)S(1)} %get-tuple-element.44), channel_id=1, source_target_pairs={{0,20},{4,16},{8,28},{12,24},{16,4},{20,0},{24,12},{28,8},{1,21},{... | collective-permute-start | bytes 516104 | tf_op jit(solution)/shard_map/ppermute | solution.py:471
  19.1 23.3 %copy-start = (bf16[1,384,1152]{2,1,0:T(8,128)(2,1)S(1)}, bf16[1,384,1152]{2,1,0:T(8,128)(2,1)}, u32[]{:S(2)}) copy-start(bf16[1,384,1152]{2,1,0:T(8,128)(2,1)} %param.5) | copy-start | bytes 2654212
  19.1 3.7 %collective-permute-start.7 = (bf16[4,1152]{1,0:T(4,128)(2,1)S(1)}, bf16[4,1152]{1,0:T(4,128)(2,1)S(1)}, u32[]{:S(2)}, u32[]{:S(2)}) collective-permute-start(bf16[4,1152]{1,0:T(4,128)(2,1)S(1)} %copy-done.2), channel_id=1, source_target_pairs={{1,0},{0,1},{3,2},{2,3},{6,4},{7,5},{4,6},{5,7},{11,8},{10,9},{9,1... | collective-permute-start | bytes 27656 | tf_op jit(solution)/shard_map/ppermute | solution.py:471
  31.6 5.5 %collective-permute-start.8 = (bf16[96,384]{1,0:T(8,128)(2,1)S(1)}, bf16[96,384]{1,0:T(8,128)(2,1)S(1)}, u32[]{:S(2)}, u32[]{:S(2)}) collective-permute-start(bf16[96,384]{1,0:T(8,128)(2,1)S(1)} %get-tuple-element.46), channel_id=1, source_target_pairs={{0,24},{4,28},{8,16},{12,20},{16,8},{20,12},{24,0},{28,4},{1,25},{... | collective-permute-start | bytes 221192 | tf_op jit(solution)/shard_map/ppermute | solution.py:471
  33.9 5.2 %collective-permute-start.9 = (bf16[96,384]{1,0:T(8,128)(2,1)S(1)}, bf16[96,384]{1,0:T(8,128)(2,1)S(1)}, u32[]{:S(2)}, u32[]{:S(2)}) collective-permute-start(bf16[96,384]{1,0:T(8,128)(2,1)S(1)} %get-tuple-element.47), channel_id=1, source_target_pairs={{0,28},{4,24},{8,20},{12,16},{16,12},{20,8},{24,4},{28,0},{1,29},{... | collective-permute-start | bytes 221192 | tf_op jit(solution)/shard_map/ppermute | solution.py:471
  34.1 6.3 %collective-permute-start.10 = (bf16[96,384]{1,0:T(8,128)(2,1)S(1)}, bf16[96,384]{1,0:T(8,128)(2,1)S(1)}, u32[]{:S(2)}, u32[]{:S(2)}) collective-permute-start(bf16[96,384]{1,0:T(8,128)(2,1)S(1)} %get-tuple-element.48), channel_id=1, source_target_pairs={{0,8},{4,12},{8,0},{12,4},{16,24},{20,28},{24,16},{28,20},{1,9},{5... | collective-permute-start | bytes 221192 | tf_op jit(solution)/shard_map/ppermute | solution.py:471
  35.9 5.2 %collective-permute-start.11 = (bf16[96,384]{1,0:T(8,128)(2,1)S(1)}, bf16[96,384]{1,0:T(8,128)(2,1)S(1)}, u32[]{:S(2)}, u32[]{:S(2)}) collective-permute-start(bf16[96,384]{1,0:T(8,128)(2,1)S(1)} %get-tuple-element.49), channel_id=1, source_target_pairs={{0,16},{4,20},{8,24},{12,28},{16,0},{20,4},{24,8},{28,12},{1,17},{... | collective-permute-start | bytes 221192 | tf_op jit(solution)/shard_map/ppermute | solution.py:471
  37.1 5.1 %collective-permute-start.12 = (bf16[96,384]{1,0:T(8,128)(2,1)S(1)}, bf16[96,384]{1,0:T(8,128)(2,1)S(1)}, u32[]{:S(2)}, u32[]{:S(2)}) collective-permute-start(bf16[96,384]{1,0:T(8,128)(2,1)S(1)} %get-tuple-element.50), channel_id=1, source_target_pairs={{0,12},{4,8},{8,4},{12,0},{16,28},{20,24},{24,20},{28,16},{1,13},{... | collective-permute-start | bytes 221192 | tf_op jit(solution)/shard_map/ppermute | solution.py:471
  37.1 5.2 %collective-permute-start.13 = (bf16[96,384]{1,0:T(8,128)(2,1)S(1)}, bf16[96,384]{1,0:T(8,128)(2,1)S(1)}, u32[]{:S(2)}, u32[]{:S(2)}) collective-permute-start(bf16[96,384]{1,0:T(8,128)(2,1)S(1)} %get-tuple-element.51), channel_id=1, source_target_pairs={{0,20},{4,16},{8,28},{12,24},{16,4},{20,0},{24,12},{28,8},{1,21},{... | collective-permute-start | bytes 221192 | tf_op jit(solution)/shard_map/ppermute | solution.py:471
  39.1 3.2 %collective-permute-start.14 = (bf16[96,384]{1,0:T(8,128)(2,1)S(1)}, bf16[96,384]{1,0:T(8,128)(2,1)S(1)}, u32[]{:S(2)}, u32[]{:S(2)}) collective-permute-start(bf16[96,384]{1,0:T(8,128)(2,1)S(1)} %get-tuple-element.52), channel_id=1, source_target_pairs={{0,4},{4,0},{8,12},{12,8},{16,20},{20,16},{24,28},{28,24},{1,5},{5... | collective-permute-start | bytes 221192 | tf_op jit(solution)/shard_map/ppermute | solution.py:471

commit v16 on v14

--- a/solution.py
+++ b/solution.py
@@ -78,12 +78,19 @@
     return lax.div(own, 2), lax.rem(own, 2)
 
 
-def far_kernel(images, piggy, ids_ref, rows_ref, weight_ref, normed_ref, sums_ref, same_ref, cross_ref, own_ids, rows_held, weight, id_sem, row_sem, sems):
+def far_kernel(images, piggy, ids_ref, rows_ref, weight_ref, normed_ref, sums_ref, same_ref, cross_ref, own_ids, rows_held, weight, id_sem, row_sems, sems):
     count, depth = rows_ref.shape
     width = weight_ref.shape[0] // 3
-    wide = weight.shape[1]
-    rows_fetch = pltpu.make_async_copy(rows_ref, rows_held, row_sem)
-    rows_fetch.start()
+    wide = weight.shape[0] // 3
+    pieces = row_sems.shape[0]
+    step = count // pieces
+    cuts = [slice(piece * step, (piece + 1) * step) for piece in range(pieces)]
+    row_fetches = [
+        pltpu.make_async_copy(rows_ref.at[cut], rows_held.at[cut], row_sems.at[piece])
+        for piece, cut in enumerate(cuts)
+    ]
+    for fetch in row_fetches:
+        fetch.start()
     own = pl.multiple_of(lax.axis_index("grp") * count, LANES)
     ids_fetch = pltpu.make_async_copy(ids_ref.at[:, pl.ds(own, count)], own_ids, id_sem)
     ids_fetch.start()
@@ -92,25 +99,23 @@
     fetches = []
     for at in range(3):
         first = pl.multiple_of(at * width + pair * wide, 16)
-        fetches.append(pltpu.make_async_copy(weight_ref.at[pl.ds(first, wide)], weight.at[at], sems.at[at]))
+        fetches.append(pltpu.make_async_copy(weight_ref.at[pl.ds(first, wide)], weight.at[at * wide : (at + 1) * wide], sems.at[at]))
     for fetch in fetches:
         fetch.start()
-    rows_fetch.wait()
-    rows = rows_held[...]
-    values = rows.astype(jnp.float32)
-    center = values - jnp.mean(values, axis=1, keepdims=True)
-    spread = jnp.mean(center * center, axis=1, keepdims=True)
-    normed = (center * lax.rsqrt(spread + 1e-06)).astype(jnp.bfloat16)
-    normed_ref[...] = normed.T
+    for fetch, cut in zip(row_fetches, cuts):
+        fetch.wait()
+        values = rows_held[cut, :].astype(jnp.float32)
+        center = values - jnp.mean(values, axis=1, keepdims=True)
+        spread = jnp.mean(center * center, axis=1, keepdims=True)
+        normed_ref[:, cut] = (center * lax.rsqrt(spread + 1e-06)).astype(jnp.bfloat16).T
     ids_fetch.wait()
     if piggy:
-        sums = jnp.dot(image_rows(own_ids[...], images), rows, preferred_element_type=jnp.float32)
+        sums = jnp.dot(image_rows(own_ids[...], images), rows_held[...], preferred_element_type=jnp.float32)
         sums_ref[...] = split_in_two(sums, images)
     for fetch in fetches:
         fetch.wait()
-    parts = [
-        jnp.dot(weight[at], normed_ref[...], preferred_element_type=jnp.float32) for at in range(3)
-    ]
+    turned = jnp.dot(weight[...], normed_ref[...], preferred_element_type=jnp.float32)
+    parts = [turned[at * wide : (at + 1) * wide] for at in range(3)]
     store_by_core(core, head_blocks(*parts, sums_ref if piggy else None, pair), same_ref, cross_ref)
 
 
@@ -247,9 +252,21 @@
     queries[PADDED:, there] = jnp.zeros((LANES - PADDED, block_ref.shape[1]), jnp.bfloat16)
 
 
-def prepare_kernel(images, halo, ids_ref, *rest):
-    got_refs, (keys, marks, before) = rest[: len(EARLY)], rest[len(EARLY) :]
+def prepare_kernel(images, halo, ids_ref, out_weight_ref, *rest):
+    got_refs, (keys, marks, before, weight, sems) = rest[: len(EARLY)], rest[len(EARLY) :]
     count = got_refs[0].shape[1]
+    fetches = []
+    for step, by in enumerate(ORDER):
+        head = jnp.bitwise_xor(lax.rem(lax.axis_index("grp"), HEADS), by)
+        first = lax.div(head, 2) * (2 * SIZE) + lax.rem(head, 2) * (SIZE - SPARE)
+        fetches.append(
+            pltpu.make_async_copy(
+                out_weight_ref.at[pl.ds(pl.multiple_of(first, 16), PADDED)],
+                weight.at[step * PADDED : (step + 1) * PADDED],
+                sems.at[step],
+            )
+        )
+        fetches[-1].start()
     before[...] = count_before(images, ids_ref[...])
     write_marks(images, ids_ref[...], marks)
     own = lax.rem(lax.axis_index("grp"), HEADS)
@@ -257,6 +274,8 @@
         first = jnp.bitwise_xor(own, by) * count
         here = pl.ds(pl.multiple_of(halo + first, LANES), count)
         keys[step * count : (step + 1) * count, :] = turned_keys(marks[0, :, here], ref)
+    for fetch in fetches:
+        fetch.wait()
 
 
 def attend_kernel(images, piggy, halo, ids_ref, before_ref, marks, early_keys, *rest):
@@ -328,15 +347,12 @@
             out_ref[padded:] = below
 
 
-def joined_heads(got_refs, out_weight_ref, flat, weight):
+def joined_heads(got_refs, flat):
     own = lax.rem(lax.axis_index("grp"), HEADS)
     spares = []
     for step, (by, got_ref) in enumerate(zip(ORDER, got_refs)):
-        head = jnp.bitwise_xor(own, by)
-        odd = lax.rem(head, 2)
-        first = pl.multiple_of(lax.div(head, 2) * (2 * SIZE) + odd * (SIZE - SPARE), 16)
+        odd = lax.rem(jnp.bitwise_xor(own, by), 2)
         at = step * PADDED
-        weight[at : at + PADDED] = out_weight_ref[pl.ds(first, PADDED), :]
         top = got_ref[0:16].astype(jnp.float32)
         bottom = got_ref[PADDED - 16 : PADDED].astype(jnp.float32)
         spares.append(jnp.where(odd == 1, top[:SPARE], bottom[SPARE:]))
@@ -348,14 +364,14 @@
     return spares
 
 
-def send_mixed_rows(rows_ref, flat, weight, turned, mixed, mixed_ref, sems):
+def send_mixed_rows(rows_ref, weight_ref, flat, turned, mixed, mixed_ref, sems):
     turned[...] = flat[...].T
     pieces = sems.shape[0]
     step = rows_ref.shape[0] // pieces
     copies = []
     for piece in range(pieces):
         cut = slice(piece * step, (piece + 1) * step)
-        added = jnp.dot(turned[cut, :], weight[...], preferred_element_type=jnp.float32)
+        added = jnp.dot(turned[cut, :], weight_ref[...], preferred_element_type=jnp.float32)
         mixed[cut, :] = (rows_ref[cut, :].astype(jnp.float32) + added).astype(jnp.bfloat16)
         copies.append(pltpu.make_async_copy(mixed.at[cut], mixed_ref.at[cut], sems.at[piece]))
         copies[-1].start()
@@ -371,11 +387,11 @@
     return jnp.maximum(logits, 0.0) + jnp.log1p(jnp.exp(-jnp.abs(logits)))
 
 
-def finish_kernel(images, rows_ref, out_weight_ref, text_ref, *rest):
+def finish_kernel(images, rows_ref, weight_ref, text_ref, *rest):
     got_refs, rest = rest[:HEADS], rest[HEADS:]
-    mixed_ref, loss_ref, flat, weight, turned, mixed, sems, pooled_heads, patch_sums, far_texts = rest
-    spares = joined_heads(got_refs, out_weight_ref, flat, weight)
-    copies = send_mixed_rows(rows_ref, flat, weight, turned, mixed, mixed_ref, sems)
+    mixed_ref, loss_ref, flat, turned, mixed, sems, pooled_heads, patch_sums, far_texts = rest
+    spares = joined_heads(got_refs, flat)
+    copies = send_mixed_rows(rows_ref, weight_ref, flat, turned, mixed, mixed_ref, sems)
     own = lax.rem(lax.axis_index("grp"), HEADS)
     patch_sums[:, HEADS * LANES :] = spares[0][:, 2 * LANES :]
     for step, (by, spare) in enumerate(zip(ORDER, spares)):
@@ -388,7 +404,7 @@
             here = slice(part * count, (part + 1) * count)
             far_texts[head, :, here] = below[part * images : (part + 1) * images]
     pooled = jnp.dot(
-        pooled_heads[...].astype(jnp.bfloat16), weight[...], preferred_element_type=jnp.float32
+        pooled_heads[...].astype(jnp.bfloat16), weight_ref[...], preferred_element_type=jnp.float32
     )
     pooled = pooled + patch_sums[...]
     pooled = pooled + pltpu.roll(pooled, images, axis=0)
@@ -411,11 +427,11 @@
         copy.wait()
 
 
-def mix_kernel(rows_ref, out_weight_ref, *rest):
+def mix_kernel(rows_ref, weight_ref, *rest):
     got_refs, rest = rest[:HEADS], rest[HEADS:]
-    mixed_ref, flat, weight, turned, mixed, sems = rest
-    joined_heads(got_refs, out_weight_ref, flat, weight)
-    for copy in send_mixed_rows(rows_ref, flat, weight, turned, mixed, mixed_ref, sems):
+    mixed_ref, flat, turned, mixed, sems = rest
+    joined_heads(got_refs, flat)
+    for copy in send_mixed_rows(rows_ref, weight_ref, flat, turned, mixed, mixed_ref, sems):
         copy.wait()
 
 
@@ -499,9 +515,9 @@
         [
             pltpu.VMEM((1, count), jnp.int32),
             pltpu.VMEM((count, depth), bf16),
-            pltpu.VMEM((3, 2 * size, depth), bf16),
+            pltpu.VMEM((6 * size, depth), bf16),
             pltpu.SemaphoreType.DMA,
-            pltpu.SemaphoreType.DMA,
+            pltpu.SemaphoreType.DMA((3,)),
             pltpu.SemaphoreType.DMA((3,)),
         ],
         [hbm] * 3,
@@ -548,17 +564,18 @@
     reach = length + 2 * halo
     window = min(rounded_up(MAXP + LANES - 1, LANES), reach)
     tile = 2 * LANES
-    early_keys, marks, before = call(
+    early_keys, marks, before, weight = call(
         functools.partial(prepare_kernel, images, halo),
         (
             shape((len(EARLY) * count, LANES), bf16),
             shape((2, SPARE, reach), f32),
             shape((rounded_up(images + 1, SPARE), LANES), jnp.int32),
+            shape((HEADS * padded, depth), bf16),
         ),
-        [],
-        in_vmem(1 + len(EARLY)),
+        [pltpu.SemaphoreType.DMA((HEADS,))],
+        in_vmem(1) + [hbm] + in_vmem(len(EARLY)),
         1 << 30,
-    )(near_ids, *[got[by] for by in EARLY])
+    )(near_ids, in_hbm(out_weight), *[got[by] for by in EARLY])
     operands = [near_ids, before, marks, early_keys, *[got[by] for by in EARLY + LATE], *halos_and_texts]
     answers = call(
         functools.partial(attend_kernel, images, piggy, halo),
@@ -582,7 +599,6 @@
 
     joined = [
         pltpu.VMEM((HEADS * padded, count), bf16),
-        pltpu.VMEM((HEADS * padded, depth), bf16),
         pltpu.VMEM((count, HEADS * padded), bf16),
         pltpu.VMEM((count, depth), bf16),
         pltpu.SemaphoreType.DMA((3,)),
@@ -601,10 +617,10 @@
             in_vmem(3 + HEADS),
             flops,
             (hbm, pl.BlockSpec(memory_space=pltpu.VMEM)),
-        )(rows, out_weight, text_embed, *home)
+        )(rows, weight, text_embed, *home)
         return (mixed[None], row_loss[0])
     mixed = call(mix_kernel, shape((count, depth), bf16), joined, in_vmem(2 + HEADS), flops, hbm)(
-        rows, out_weight, *home
+        rows, weight, *home
     )
     own_ids = lax.dynamic_slice_in_dim(segment_ids[0], lax.axis_index("grp") * count, count)
     onehot = (own_ids[None, :] == jnp.arange(images, dtype=jnp.int32)[:, None]).astype(bf16)

time: 44.3 us -> 44.3 us (level)
  Pallas kernels: 16 us -> 17.6 us
  waiting for transfers between devices: 9.79 us -> 8.45 us
    pallas_call x1, Pallas kernels: 0.24 us -> 1.64 us  [local(): call(functools.partial(prepare_kernel, images, halo), (shape((len(EARLY)...]
    ppermute x15, waiting for transfers between devices: 9.79 us -> 8.45 us  [moved(): return lax.ppermute(value, axis, pairs)]
  transfers between devices with their start and end apart: 15 -> 15, of which waited for: 9 -> 9; matrix products, arithmetic and copies ran while one was open for 0% -> 0% of each run, Pallas kernels for 6% -> 9%
where the time goes in v16:
time: 44.3 us
  Pallas kernels  17.6 us (40%)
  starting transfers between devices  17.6 us (40%)
  waiting for transfers between devices  8.45 us (19%)
  between operations  0.69 us (2%)
    ppermute x15, starting transfers between devices, moved(): return lax.ppermute(value, axis, pairs)  17.6 us
    ppermute x15, waiting for transfers between devices, moved(): return lax.ppermute(value, axis, pairs)  8.45 us
    pallas_call x1, Pallas kernels, local(): call(functools.partial(attend_kernel, images, piggy, halo), (shape((padde...  7.88 us
    pallas_call x1, Pallas kernels, local(): call(functools.partial(far_kernel, images, piggy), (shape((depth, count),...  3.3 us
    pallas_call x1, Pallas kernels, local(): call(functools.partial(finish_kernel, images), (shape((count, depth), bf1...  2.4 us
    pallas_call x1, Pallas kernels, local(): call(functools.partial(near_kernel, piggy), (block,) * 6, [], in_vmem(3),...  2.35 us
    pallas_call x1, Pallas kernels, local(): call(functools.partial(prepare_kernel, images, halo), (shape((len(EARLY)...  1.64 us
  transfers between devices with their start and end apart: 15, of which 9 were waited for; matrix products, arithmetic and copies ran while one was open for 0% of the time, Pallas kernels for 9%

profile of v16, /device:TPU:0, one launch (start us, length us, event | category | flops | bytes accessed | tf_op | source)
XLA Modules:
  0.0 44.3 jit_solution(15010994973389671598)
XLA Ops:
  0.6 0.0 copy-start
  0.6 3.3 %shard_map.68 = (bf16[1152,384]{1,0:T(8,128)(2,1)S(1)}, f32[8,1152]{1,0:T(8,128)S(1)}, bf16[224,384]{1,0:T(8,128)(2,1)S(1)}, bf16[224,384]{1,0:T(8,128)(2,1)S(1)}) custom-call(s32[1,3072]{1,0:T(1,128)} %ids_ref.5, bf16[384,1152]{1,0:T(8,128)(2,1)} %bitcast.6, bf16[1728,1152]{1,0:T(8,128)(2,1)} %bitcast.4), custom_call_target="tpu_custom_call" | custom-call | flops 382205952 | bytes 8388608 | tf_op jit(solution)/shard_map/pallas_call | solution.py:512
  3.9 4.0 %collective-permute-start = (bf16[224,384]{1,0:T(8,128)(2,1)S(1)}, bf16[224,384]{1,0:T(8,128)(2,1)S(1)}, u32[]{:S(2)}, u32[]{:S(2)}) collective-permute-start(bf16[224,384]{1,0:T(8,128)(2,1)S(1)} %get-tuple-element.28), channel_id=1, source_target_pairs={{0,24},{4,28},{8,16},{12,20},{16,8},{20,12},{24,0},{28,4},{1,25},{... | collective-permute-start | bytes 516104 | tf_op jit(solution)/shard_map/ppermute | solution.py:461
  7.9 0.0 collective-permute-start.1
  7.9 0.0 copy-done
  7.9 0.0 copy-start.3
  7.9 0.0 copy-start.2
  7.9 2.4 %shard_map.69 = (bf16[224,384]{1,0:T(8,128)(2,1)S(1)}, bf16[224,384]{1,0:T(8,128)(2,1)S(1)}, bf16[224,384]{1,0:T(8,128)(2,1)S(1)}, bf16[224,384]{1,0:T(8,128)(2,...) custom-call(bf16[1152,384]{1,0:T(8,128)(2,1)S(1)} %get-tuple-element.30.normed_ref, ...), custom_call_target="tpu_custom_call" | custom-call | flops 1146617856 | bytes 8388608 | tf_op jit(solution)/shard_map/pallas_call | solution.py:526
  10.3 0.3 collective-permute-start.2
  10.5 1.9 %collective-permute-start.3 = (bf16[224,384]{1,0:T(8,128)(2,1)S(1)}, bf16[224,384]{1,0:T(8,128)(2,1)S(1)}, u32[]{:S(2)}, u32[]{:S(2)}) collective-permute-start(bf16[224,384]{1,0:T(8,128)(2,1)S(1)} %get-tuple-element.39), channel_id=1, source_target_pairs={{0,8},{4,12},{8,0},{12,4},{16,24},{20,28},{24,16},{28,20},{1,9},{5... | collective-permute-start | bytes 516104 | tf_op jit(solution)/shard_map/ppermute | solution.py:461
  12.4 1.5 %collective-permute-start.4 = (bf16[224,384]{1,0:T(8,128)(2,1)S(1)}, bf16[224,384]{1,0:T(8,128)(2,1)S(1)}, u32[]{:S(2)}, u32[]{:S(2)}) collective-permute-start(bf16[224,384]{1,0:T(8,128)(2,1)S(1)} %get-tuple-element.40), channel_id=1, source_target_pairs={{0,16},{4,20},{8,24},{12,28},{16,0},{20,4},{24,8},{28,12},{1,17},{... | collective-permute-start | bytes 516104 | tf_op jit(solution)/shard_map/ppermute | solution.py:461
  13.9 0.0 collective-permute-done.rest_0_
  13.9 0.0 collective-permute-start.5
  13.9 2.4 %collective-permute-done.1.rest_1_ = bf16[224,384]{1,0:T(8,128)(2,1)S(1)} collective-permute-done((bf16[224,384]{1,0:T(8,128)(2,1)S(1)}, bf16[224,384]{1,0:T(8,128)(2,1)S(1)}, u32[]{:S(2)}, u32[]{:S(2)}) %collective-permute-start.1) | collective-permute-done | bytes 172064 | tf_op jit(solution)/shard_map/ppermute | solution.py:461
  16.4 1.9 %collective-permute-start.6 = (bf16[224,384]{1,0:T(8,128)(2,1)S(1)}, bf16[224,384]{1,0:T(8,128)(2,1)S(1)}, u32[]{:S(2)}, u32[]{:S(2)}) collective-permute-start(bf16[224,384]{1,0:T(8,128)(2,1)S(1)} %get-tuple-element.42), channel_id=1, source_target_pairs={{0,20},{4,16},{8,28},{12,24},{16,4},{20,0},{24,12},{28,8},{1,21},{... | collective-permute-start | bytes 516104 | tf_op jit(solution)/shard_map/ppermute | solution.py:461
  18.3 0.0 collective-permute-done.2.rest_2_
  18.3 0.0 copy-done.3
  18.3 1.6 %collective-permute-start.7 = (bf16[4,1152]{1,0:T(4,128)(2,1)S(1)}, bf16[4,1152]{1,0:T(4,128)(2,1)S(1)}, u32[]{:S(2)}, u32[]{:S(2)}) collective-permute-start(bf16[4,1152]{1,0:T(4,128)(2,1)S(1)} %copy-done.3), channel_id=1, source_target_pairs={{1,0},{0,1},{3,2},{2,3},{6,4},{7,5},{4,6},{5,7},{11,8},{10,9},{9,1... | collective-permute-start | bytes 27656 | tf_op jit(solution)/shard_map/ppermute | solution.py:461
  19.8 0.0 copy-done.2
  19.8 1.6 %shard_map.70 = (bf16[1536,128]{1,0:T(8,128)(2,1)S(1)}, f32[2,8,3072]{2,1,0:T(8,128)S(1)}, s32[8,128]{1,0:T(8,128)S(1)}, bf16[640,1152]{1,0:T(8,128)(2,1)S(1)}) custom-call(s32[1,3072]{1,0:T(1,128)S(1)} %copy-done.2, bf16[576,1152]{1,0:T(8,128)(2,1)} %out_weight_ref.1, bf16[224,384]{1,0:T(8,128)(2,1)S(1)} %collective-permute-done.rest_0_, ...), custom_call_target="tpu_custom_call" | custom-call | flops 1073741824 | bytes 8388608 | tf_op jit(solution)/shard_map/pallas_call | solution.py:567
  21.5 0.4 collective-permute-done.7.rest_8_
  21.9 0.0 collective-permute-done.3.rest_4_
  21.9 0.0 collective-permute-done.4.rest_5_
  21.9 0.7 %collective-permute-done.5.rest_6_ = bf16[224,384]{1,0:T(8,128)(2,1)S(1)} collective-permute-done((bf16[224,384]{1,0:T(8,128)(2,1)S(1)}, bf16[224,384]{1,0:T(8,128)(2,1)S(1)}, u32[]{:S(2)}, u32[]{:S(2)}) %collective-permute-start.5) | collective-permute-done | bytes 172064 | tf_op jit(solution)/shard_map/ppermute | solution.py:461
  22.6 0.6 %collective-permute-done.6.rest_7_ = bf16[224,384]{1,0:T(8,128)(2,1)S(1)} collective-permute-done((bf16[224,384]{1,0:T(8,128)(2,1)S(1)}, bf16[224,384]{1,0:T(8,128)(2,1)S(1)}, u32[]{:S(2)}, u32[]{:S(2)}) %collective-permute-start.6) | collective-permute-done | bytes 172064 | tf_op jit(solution)/shard_map/ppermute | solution.py:461
  23.3 0.0 copy-start.1
  23.3 7.9 %shard_map.71 = (bf16[96,384]{1,0:T(8,128)(2,1)S(1)}, bf16[96,384]{1,0:T(8,128)(2,1)S(1)}, bf16[96,384]{1,0:T(8,128)(2,1)S(1)}, bf16[96,384]{1,0:T(8,128)(2,1)S(...) custom-call(s32[1,3072]{1,0:T(1,128)S(1)} %copy-done.2, ...), custom_call_target="tpu_custom_call" | custom-call | flops 905969664 | bytes 8388608 | tf_op jit(solution)/shard_map/pallas_call | solution.py:580
  31.1 2.3 %collective-permute-start.8 = (bf16[96,384]{1,0:T(8,128)(2,1)S(1)}, bf16[96,384]{1,0:T(8,128)(2,1)S(1)}, u32[]{:S(2)}, u32[]{:S(2)}) collective-permute-start(bf16[96,384]{1,0:T(8,128)(2,1)S(1)} %get-tuple-element.44), channel_id=1, source_target_pairs={{0,24},{4,28},{8,16},{12,20},{16,8},{20,12},{24,0},{28,4},{1,25},{... | collective-permute-start | bytes 221192 | tf_op jit(solution)/shard_map/ppermute | solution.py:461
  33.4 0.2 collective-permute-start.9
  33.6 1.8 %collective-permute-start.10 = (bf16[96,384]{1,0:T(8,128)(2,1)S(1)}, bf16[96,384]{1,0:T(8,128)(2,1)S(1)}, u32[]{:S(2)}, u32[]{:S(2)}) collective-permute-start(bf16[96,384]{1,0:T(8,128)(2,1)S(1)} %get-tuple-element.46), channel_id=1, source_target_pairs={{0,8},{4,12},{8,0},{12,4},{16,24},{20,28},{24,16},{28,20},{1,9},{5... | collective-permute-start | bytes 221192 | tf_op jit(solution)/shard_map/ppermute | solution.py:461
  35.4 1.2 %collective-permute-start.11 = (bf16[96,384]{1,0:T(8,128)(2,1)S(1)}, bf16[96,384]{1,0:T(8,128)(2,1)S(1)}, u32[]{:S(2)}, u32[]{:S(2)}) collective-permute-start(bf16[96,384]{1,0:T(8,128)(2,1)S(1)} %get-tuple-element.47), channel_id=1, source_target_pairs={{0,16},{4,20},{8,24},{12,28},{16,0},{20,4},{24,8},{28,12},{1,17},{... | collective-permute-start | bytes 221192 | tf_op jit(solution)/shard_map/ppermute | solution.py:461
  36.6 0.0 collective-permute-start.12
  36.6 0.0 collective-permute-done.8.rest_0_
  36.6 0.8 %collective-permute-start.13 = (bf16[96,384]{1,0:T(8,128)(2,1)S(1)}, bf16[96,384]{1,0:T(8,128)(2,1)S(1)}, u32[]{:S(2)}, u32[]{:S(2)}) collective-permute-start(bf16[96,384]{1,0:T(8,128)(2,1)S(1)} %get-tuple-element.49), channel_id=1, source_target_pairs={{0,20},{4,16},{8,28},{12,24},{16,4},{20,0},{24,12},{28,8},{1,21},{... | collective-permute-start | bytes 221192 | tf_op jit(solution)/shard_map/ppermute | solution.py:461
  37.4 1.3 %collective-permute-done.9.rest_1_ = bf16[96,384]{1,0:T(8,128)(2,1)S(1)} collective-permute-done((bf16[96,384]{1,0:T(8,128)(2,1)S(1)}, bf16[96,384]{1,0:T(8,128)(2,1)S(1)}, u32[]{:S(2)}, u32[]{:S(2)}) %collective-permute-start.9) | collective-permute-done | bytes 73760 | tf_op jit(solution)/shard_map/ppermute | solution.py:461
  38.7 0.3 collective-permute-start.14
  38.9 1.0 %collective-permute-done.10.rest_2_ = bf16[96,384]{1,0:T(8,128)(2,1)S(1)} collective-permute-done((bf16[96,384]{1,0:T(8,128)(2,1)S(1)}, bf16[96,384]{1,0:T(8,128)(2,1)S(1)}, u32[]{:S(2)}, u32[]{:S(2)}) %collective-permute-start.10) | collective-permute-done | bytes 73760 | tf_op jit(solution)/shard_map/ppermute | solution.py:461
  40.0 0.7 %collective-permute-done.11.rest_3_ = bf16[96,384]{1,0:T(8,128)(2,1)S(1)} collective-permute-done((bf16[96,384]{1,0:T(8,128)(2,1)S(1)}, bf16[96,384]{1,0:T(8,128)(2,1)S(1)}, u32[]{:S(2)}, u32[]{:S(2)}) %collective-permute-start.11) | collective-permute-done | bytes 73760 | tf_op jit(solution)/shard_map/ppermute | solution.py:461
  40.6 1.1 %collective-permute-done.12.rest_4_ = bf16[96,384]{1,0:T(8,128)(2,1)S(1)} collective-permute-done((bf16[96,384]{1,0:T(8,128)(2,1)S(1)}, bf16[96,384]{1,0:T(8,128)(2,1)S(1)}, u32[]{:S(2)}, u32[]{:S(2)}) %collective-permute-start.12) | collective-permute-done | bytes 73760 | tf_op jit(solution)/shard_map/ppermute | solution.py:461
  41.7 0.2 collective-permute-done.13.rest_5_
  41.9 0.0 collective-permute-done.14.rest_6_
  41.9 0.0 copy-done.1
  41.9 2.4 %shard_map.72 = (bf16[384,1152]{1,0:T(8,128)(2,1)}, f32[1,4]{1,0:T(1,128)}) custom-call(bf16[384,1152]{1,0:T(8,128)(2,1)S(1)} %bitcast.7, bf16[640,1152]{1,0:T(8,128)(2,1)S(1)} %get-tuple-element.35.weight_ref, bf16[4,1152]{1,0:T(4,128)(2,1)S(1)} %copy-done.3, bf16[96,384]{1,0:T(8,128)(2,1)S(1)} %collective-permute-done.8.rest_0_, ...), custom_call_target="tpu_custom_call" | custom-call | flops 509607936 | bytes 8388608 | tf_op jit(solution)/shard_map/pallas_call | solution.py:608
Async XLA Ops:
  0.6 7.3 %copy-start = (bf16[1152,1728]{0,1:T(8,128)(2,1)S(1)}, bf16[1152,1728]{0,1:T(8,128)(2,1)}, u32[]{:S(2)}) copy-start(bf16[1152,1728]{0,1:T(8,128)(2,1)} %param.7) | copy-start | bytes 11943940
  3.9 10.0 %collective-permute-start = (bf16[224,384]{1,0:T(8,128)(2,1)S(1)}, bf16[224,384]{1,0:T(8,128)(2,1)S(1)}, u32[]{:S(2)}, u32[]{:S(2)}) collective-permute-start(bf16[224,384]{1,0:T(8,128)(2,1)S(1)} %get-tuple-element.28), channel_id=1, source_target_pairs={{0,24},{4,28},{8,16},{12,20},{16,8},{20,12},{24,0},{28,4},{1,25},{... | collective-permute-start | bytes 516104 | tf_op jit(solution)/shard_map/ppermute | solution.py:461
  7.9 8.5 %collective-permute-start.1 = (bf16[224,384]{1,0:T(8,128)(2,1)S(1)}, bf16[224,384]{1,0:T(8,128)(2,1)S(1)}, u32[]{:S(2)}, u32[]{:S(2)}) collective-permute-start(bf16[224,384]{1,0:T(8,128)(2,1)S(1)} %get-tuple-element.29), channel_id=1, source_target_pairs={{0,28},{4,24},{8,20},{12,16},{16,12},{20,8},{24,4},{28,0},{1,29},{... | collective-permute-start | bytes 516104 | tf_op jit(solution)/shard_map/ppermute | solution.py:461
  7.9 10.3 %copy-start.3 = (bf16[4,1152]{1,0:T(4,128)(2,1)S(1)}, bf16[4,1152]{1,0:T(4,128)(2,1)}, u32[]{:S(2)}) copy-start(bf16[4,1152]{1,0:T(4,128)(2,1)} %text_ref.1) | copy-start | bytes 27652
  7.9 11.9 %copy-start.2 = (s32[1,3072]{1,0:T(1,128)S(1)}, s32[1,3072]{1,0:T(1,128)}, u32[]{:S(2)}) copy-start(s32[1,3072]{1,0:T(1,128)} %ids_ref.5) | copy-start | bytes 36868
  10.3 8.0 %collective-permute-start.2 = (bf16[224,384]{1,0:T(8,128)(2,1)S(1)}, bf16[224,384]{1,0:T(8,128)(2,1)S(1)}, u32[]{:S(2)}, u32[]{:S(2)}) collective-permute-start(bf16[224,384]{1,0:T(8,128)(2,1)S(1)} %get-tuple-element.32), channel_id=1, source_target_pairs={{0,4},{4,0},{8,12},{12,8},{16,20},{20,16},{24,28},{28,24},{1,5},{5... | collective-permute-start | bytes 516104 | tf_op jit(solution)/shard_map/ppermute | solution.py:461
  10.5 11.4 %collective-permute-start.3 = (bf16[224,384]{1,0:T(8,128)(2,1)S(1)}, bf16[224,384]{1,0:T(8,128)(2,1)S(1)}, u32[]{:S(2)}, u32[]{:S(2)}) collective-permute-start(bf16[224,384]{1,0:T(8,128)(2,1)S(1)} %get-tuple-element.39), channel_id=1, source_target_pairs={{0,8},{4,12},{8,0},{12,4},{16,24},{20,28},{24,16},{28,20},{1,9},{5... | collective-permute-start | bytes 516104 | tf_op jit(solution)/shard_map/ppermute | solution.py:461
  12.4 9.5 %collective-permute-start.4 = (bf16[224,384]{1,0:T(8,128)(2,1)S(1)}, bf16[224,384]{1,0:T(8,128)(2,1)S(1)}, u32[]{:S(2)}, u32[]{:S(2)}) collective-permute-start(bf16[224,384]{1,0:T(8,128)(2,1)S(1)} %get-tuple-element.40), channel_id=1, source_target_pairs={{0,16},{4,20},{8,24},{12,28},{16,0},{20,4},{24,8},{28,12},{1,17},{... | collective-permute-start | bytes 516104 | tf_op jit(solution)/shard_map/ppermute | solution.py:461
  13.9 8.7 %collective-permute-start.5 = (bf16[224,384]{1,0:T(8,128)(2,1)S(1)}, bf16[224,384]{1,0:T(8,128)(2,1)S(1)}, u32[]{:S(2)}, u32[]{:S(2)}) collective-permute-start(bf16[224,384]{1,0:T(8,128)(2,1)S(1)} %get-tuple-element.41), channel_id=1, source_target_pairs={{0,12},{4,8},{8,4},{12,0},{16,28},{20,24},{24,20},{28,16},{1,13},{... | collective-permute-start | bytes 516104 | tf_op jit(solution)/shard_map/ppermute | solution.py:461
  16.4 6.9 %collective-permute-start.6 = (bf16[224,384]{1,0:T(8,128)(2,1)S(1)}, bf16[224,384]{1,0:T(8,128)(2,1)S(1)}, u32[]{:S(2)}, u32[]{:S(2)}) collective-permute-start(bf16[224,384]{1,0:T(8,128)(2,1)S(1)} %get-tuple-element.42), channel_id=1, source_target_pairs={{0,20},{4,16},{8,28},{12,24},{16,4},{20,0},{24,12},{28,8},{1,21},{... | collective-permute-start | bytes 516104 | tf_op jit(solution)/shard_map/ppermute | solution.py:461
  18.3 3.7 %collective-permute-start.7 = (bf16[4,1152]{1,0:T(4,128)(2,1)S(1)}, bf16[4,1152]{1,0:T(4,128)(2,1)S(1)}, u32[]{:S(2)}, u32[]{:S(2)}) collective-permute-start(bf16[4,1152]{1,0:T(4,128)(2,1)S(1)} %copy-done.3), channel_id=1, source_target_pairs={{1,0},{0,1},{3,2},{2,3},{6,4},{7,5},{4,6},{5,7},{11,8},{10,9},{9,1... | collective-permute-start | bytes 27656 | tf_op jit(solution)/shard_map/ppermute | solution.py:461
  23.3 18.7 %copy-start.1 = (bf16[1,384,1152]{2,1,0:T(8,128)(2,1)S(1)}, bf16[1,384,1152]{2,1,0:T(8,128)(2,1)}, u32[]{:S(2)}) copy-start(bf16[1,384,1152]{2,1,0:T(8,128)(2,1)} %param.5) | copy-start | bytes 2654212
  31.1 5.5 %collective-permute-start.8 = (bf16[96,384]{1,0:T(8,128)(2,1)S(1)}, bf16[96,384]{1,0:T(8,128)(2,1)S(1)}, u32[]{:S(2)}, u32[]{:S(2)}) collective-permute-start(bf16[96,384]{1,0:T(8,128)(2,1)S(1)} %get-tuple-element.44), channel_id=1, source_target_pairs={{0,24},{4,28},{8,16},{12,20},{16,8},{20,12},{24,0},{28,4},{1,25},{... | collective-permute-start | bytes 221192 | tf_op jit(solution)/shard_map/ppermute | solution.py:461
  33.4 5.3 %collective-permute-start.9 = (bf16[96,384]{1,0:T(8,128)(2,1)S(1)}, bf16[96,384]{1,0:T(8,128)(2,1)S(1)}, u32[]{:S(2)}, u32[]{:S(2)}) collective-permute-start(bf16[96,384]{1,0:T(8,128)(2,1)S(1)} %get-tuple-element.45), channel_id=1, source_target_pairs={{0,28},{4,24},{8,20},{12,16},{16,12},{20,8},{24,4},{28,0},{1,29},{... | collective-permute-start | bytes 221192 | tf_op jit(solution)/shard_map/ppermute | solution.py:461
  33.6 6.3 %collective-permute-start.10 = (bf16[96,384]{1,0:T(8,128)(2,1)S(1)}, bf16[96,384]{1,0:T(8,128)(2,1)S(1)}, u32[]{:S(2)}, u32[]{:S(2)}) collective-permute-start(bf16[96,384]{1,0:T(8,128)(2,1)S(1)} %get-tuple-element.46), channel_id=1, source_target_pairs={{0,8},{4,12},{8,0},{12,4},{16,24},{20,28},{24,16},{28,20},{1,9},{5... | collective-permute-start | bytes 221192 | tf_op jit(solution)/shard_map/ppermute | solution.py:461
  35.4 5.2 %collective-permute-start.11 = (bf16[96,384]{1,0:T(8,128)(2,1)S(1)}, bf16[96,384]{1,0:T(8,128)(2,1)S(1)}, u32[]{:S(2)}, u32[]{:S(2)}) collective-permute-start(bf16[96,384]{1,0:T(8,128)(2,1)S(1)} %get-tuple-element.47), channel_id=1, source_target_pairs={{0,16},{4,20},{8,24},{12,28},{16,0},{20,4},{24,8},{28,12},{1,17},{... | collective-permute-start | bytes 221192 | tf_op jit(solution)/shard_map/ppermute | solution.py:461
  36.6 5.1 %collective-permute-start.12 = (bf16[96,384]{1,0:T(8,128)(2,1)S(1)}, bf16[96,384]{1,0:T(8,128)(2,1)S(1)}, u32[]{:S(2)}, u32[]{:S(2)}) collective-permute-start(bf16[96,384]{1,0:T(8,128)(2,1)S(1)} %get-tuple-element.48), channel_id=1, source_target_pairs={{0,12},{4,8},{8,4},{12,0},{16,28},{20,24},{24,20},{28,16},{1,13},{... | collective-permute-start | bytes 221192 | tf_op jit(solution)/shard_map/ppermute | solution.py:461
  36.6 5.3 %collective-permute-start.13 = (bf16[96,384]{1,0:T(8,128)(2,1)S(1)}, bf16[96,384]{1,0:T(8,128)(2,1)S(1)}, u32[]{:S(2)}, u32[]{:S(2)}) collective-permute-start(bf16[96,384]{1,0:T(8,128)(2,1)S(1)} %get-tuple-element.49), channel_id=1, source_target_pairs={{0,20},{4,16},{8,28},{12,24},{16,4},{20,0},{24,12},{28,8},{1,21},{... | collective-permute-start | bytes 221192 | tf_op jit(solution)/shard_map/ppermute | solution.py:461
  38.7 3.2 %collective-permute-start.14 = (bf16[96,384]{1,0:T(8,128)(2,1)S(1)}, bf16[96,384]{1,0:T(8,128)(2,1)S(1)}, u32[]{:S(2)}, u32[]{:S(2)}) collective-permute-start(bf16[96,384]{1,0:T(8,128)(2,1)S(1)} %get-tuple-element.50), channel_id=1, source_target_pairs={{0,4},{4,0},{8,12},{12,8},{16,20},{20,16},{24,28},{28,24},{1,5},{5... | collective-permute-start | bytes 221192 | tf_op jit(solution)/shard_map/ppermute | solution.py:461

commit v17 on v16

--- a/solution.py
+++ b/solution.py
@@ -78,19 +78,12 @@
     return lax.div(own, 2), lax.rem(own, 2)
 
 
-def far_kernel(images, piggy, ids_ref, rows_ref, weight_ref, normed_ref, sums_ref, same_ref, cross_ref, own_ids, rows_held, weight, id_sem, row_sems, sems):
+def far_kernel(images, piggy, ids_ref, rows_ref, weight_ref, normed_ref, sums_ref, same_ref, cross_ref, own_ids, rows_held, weight, id_sem, row_sem, sems):
     count, depth = rows_ref.shape
     width = weight_ref.shape[0] // 3
-    wide = weight.shape[0] // 3
-    pieces = row_sems.shape[0]
-    step = count // pieces
-    cuts = [slice(piece * step, (piece + 1) * step) for piece in range(pieces)]
-    row_fetches = [
-        pltpu.make_async_copy(rows_ref.at[cut], rows_held.at[cut], row_sems.at[piece])
-        for piece, cut in enumerate(cuts)
-    ]
-    for fetch in row_fetches:
-        fetch.start()
+    wide = weight.shape[1]
+    rows_fetch = pltpu.make_async_copy(rows_ref, rows_held, row_sem)
+    rows_fetch.start()
     own = pl.multiple_of(lax.axis_index("grp") * count, LANES)
     ids_fetch = pltpu.make_async_copy(ids_ref.at[:, pl.ds(own, count)], own_ids, id_sem)
     ids_fetch.start()
@@ -99,23 +92,25 @@
     fetches = []
     for at in range(3):
         first = pl.multiple_of(at * width + pair * wide, 16)
-        fetches.append(pltpu.make_async_copy(weight_ref.at[pl.ds(first, wide)], weight.at[at * wide : (at + 1) * wide], sems.at[at]))
+        fetches.append(pltpu.make_async_copy(weight_ref.at[pl.ds(first, wide)], weight.at[at], sems.at[at]))
     for fetch in fetches:
         fetch.start()
-    for fetch, cut in zip(row_fetches, cuts):
-        fetch.wait()
-        values = rows_held[cut, :].astype(jnp.float32)
-        center = values - jnp.mean(values, axis=1, keepdims=True)
-        spread = jnp.mean(center * center, axis=1, keepdims=True)
-        normed_ref[:, cut] = (center * lax.rsqrt(spread + 1e-06)).astype(jnp.bfloat16).T
     ids_fetch.wait()
+    rows_fetch.wait()
+    rows = rows_held[...]
     if piggy:
-        sums = jnp.dot(image_rows(own_ids[...], images), rows_held[...], preferred_element_type=jnp.float32)
+        sums = jnp.dot(image_rows(own_ids[...], images), rows, preferred_element_type=jnp.float32)
         sums_ref[...] = split_in_two(sums, images)
+    values = rows.astype(jnp.float32)
+    center = values - jnp.mean(values, axis=1, keepdims=True)
+    spread = jnp.mean(center * center, axis=1, keepdims=True)
+    normed = (center * lax.rsqrt(spread + 1e-06)).astype(jnp.bfloat16)
+    normed_ref[...] = normed.T
     for fetch in fetches:
         fetch.wait()
-    turned = jnp.dot(weight[...], normed_ref[...], preferred_element_type=jnp.float32)
-    parts = [turned[at * wide : (at + 1) * wide] for at in range(3)]
+    parts = [
+        jnp.dot(weight[at], normed_ref[...], preferred_element_type=jnp.float32) for at in range(3)
+    ]
     store_by_core(core, head_blocks(*parts, sums_ref if piggy else None, pair), same_ref, cross_ref)
 
 
@@ -228,13 +223,17 @@
         weigh(second, scores_b, tops_b)
         return third
 
+    def four_pairs(step, state):
+        return two_pairs(step, two_pairs(step, state))
+
     begun = (jnp.int32(0), low)
     score(begun, scores_a, tops_a)
-    last_state = lax.fori_loop(0, lax.div(pairs, 2), two_pairs, begun)
+    reached = lax.fori_loop(0, lax.div(pairs, 4), four_pairs, begun)
+    reached = lax.fori_loop(0, lax.div(lax.rem(pairs, 4), 2), two_pairs, reached)
 
     @pl.when(lax.rem(pairs, 2) == 1)
     def _():
-        weigh(last_state, scores_a, tops_a)
+        weigh(reached, scores_a, tops_a)
 
 
 def turned_keys(marked, block_ref):
@@ -364,13 +363,15 @@
     return spares
 
 
-def send_mixed_rows(rows_ref, weight_ref, flat, turned, mixed, mixed_ref, sems):
+def send_mixed_rows(rows_ref, weight_ref, flat, turned, mixed, mixed_ref, sems, meanwhile=None):
     turned[...] = flat[...].T
     pieces = sems.shape[0]
     step = rows_ref.shape[0] // pieces
-    copies = []
+    copies, value = [], None
     for piece in range(pieces):
         cut = slice(piece * step, (piece + 1) * step)
+        if meanwhile is not None:
+            value = meanwhile[piece](value)
         added = jnp.dot(turned[cut, :], weight_ref[...], preferred_element_type=jnp.float32)
         mixed[cut, :] = (rows_ref[cut, :].astype(jnp.float32) + added).astype(jnp.bfloat16)
         copies.append(pltpu.make_async_copy(mixed.at[cut], mixed_ref.at[cut], sems.at[piece]))
@@ -389,9 +390,8 @@
 
 def finish_kernel(images, rows_ref, weight_ref, text_ref, *rest):
     got_refs, rest = rest[:HEADS], rest[HEADS:]
-    mixed_ref, loss_ref, flat, turned, mixed, sems, pooled_heads, patch_sums, far_texts = rest
+    mixed_ref, loss_ref, flat, turned, mixed, sems, pooled_heads, patch_sums, far_texts, loss, loss_sem = rest
     spares = joined_heads(got_refs, flat)
-    copies = send_mixed_rows(rows_ref, weight_ref, flat, turned, mixed, mixed_ref, sems)
     own = lax.rem(lax.axis_index("grp"), HEADS)
     patch_sums[:, HEADS * LANES :] = spares[0][:, 2 * LANES :]
     for step, (by, spare) in enumerate(zip(ORDER, spares)):
@@ -403,27 +403,37 @@
         for part in range(patch_sums.shape[1] // count):
             here = slice(part * count, (part + 1) * count)
             far_texts[head, :, here] = below[part * images : (part + 1) * images]
-    pooled = jnp.dot(
-        pooled_heads[...].astype(jnp.bfloat16), weight_ref[...], preferred_element_type=jnp.float32
-    )
-    pooled = pooled + patch_sums[...]
-    pooled = pooled + pltpu.roll(pooled, images, axis=0)
-    image_vecs = unit_rows(pooled)
-    others = [far_texts[place] for place in range(lax.axis_size("blk") - 1)]
-    texts = jnp.concatenate([text_ref[...].astype(jnp.float32)] + others, axis=0)
-    text_vecs = unit_rows(texts)
-    cosine = lax.dot_general(
-        text_vecs,
-        image_vecs,
-        (((1,), (1,)), ((), ())),
-        precision=lax.Precision.HIGHEST,
-        preferred_element_type=jnp.float32,
-    )
-    text = lax.broadcasted_iota(jnp.int32, cosine.shape, 0)
-    image = lax.broadcasted_iota(jnp.int32, cosine.shape, 1)
-    terms = losses(cosine, jnp.where(text == image, 1.0, -1.0))
-    loss_ref[...] = jnp.sum(terms, axis=0, keepdims=True)[:, 0:images]
-    for copy in copies:
+
+    def find_images(_):
+        pooled = jnp.dot(
+            pooled_heads[...].astype(jnp.bfloat16), weight_ref[...], preferred_element_type=jnp.float32
+        )
+        pooled = pooled + patch_sums[...]
+        others = [far_texts[place] for place in range(lax.axis_size("blk") - 1)]
+        texts = jnp.concatenate([text_ref[...].astype(jnp.float32)] + others, axis=0)
+        return pooled + pltpu.roll(pooled, images, axis=0), unit_rows(texts)
+
+    def find_cosines(vectors):
+        pooled, text_vecs = vectors
+        return lax.dot_general(
+            text_vecs,
+            unit_rows(pooled),
+            (((1,), (1,)), ((), ())),
+            precision=lax.Precision.HIGHEST,
+            preferred_element_type=jnp.float32,
+        )
+
+    def find_losses(cosine):
+        text = lax.broadcasted_iota(jnp.int32, cosine.shape, 0)
+        image = lax.broadcasted_iota(jnp.int32, cosine.shape, 1)
+        terms = losses(cosine, jnp.where(text == image, 1.0, -1.0))
+        loss[...] = jnp.sum(terms, axis=0, keepdims=True)[:, 0:images]
+        loss_copy.start()
+
+    loss_copy = pltpu.make_async_copy(loss, loss_ref, loss_sem)
+    meanwhile = (find_images, find_cosines, find_losses)
+    copies = send_mixed_rows(rows_ref, weight_ref, flat, turned, mixed, mixed_ref, sems, meanwhile)
+    for copy in copies + [loss_copy]:
         copy.wait()
 
 
@@ -515,9 +525,9 @@
         [
             pltpu.VMEM((1, count), jnp.int32),
             pltpu.VMEM((count, depth), bf16),
-            pltpu.VMEM((6 * size, depth), bf16),
+            pltpu.VMEM((3, 2 * size, depth), bf16),
             pltpu.SemaphoreType.DMA,
-            pltpu.SemaphoreType.DMA((3,)),
+            pltpu.SemaphoreType.DMA,
             pltpu.SemaphoreType.DMA((3,)),
         ],
         [hbm] * 3,
@@ -613,10 +623,12 @@
                 pltpu.VMEM((SPARE, HEADS * padded), f32),
                 pltpu.VMEM((SPARE, depth), f32),
                 pltpu.VMEM((HEADS, images, depth), f32),
+                pltpu.VMEM((1, images), f32),
+                pltpu.SemaphoreType.DMA,
             ],
             in_vmem(3 + HEADS),
             flops,
-            (hbm, pl.BlockSpec(memory_space=pltpu.VMEM)),
+            (hbm, hbm),
         )(rows, weight, text_embed, *home)
         return (mixed[None], row_loss[0])
     mixed = call(mix_kernel, shape((count, depth), bf16), joined, in_vmem(2 + HEADS), flops, hbm)(

time: 44.3 us -> 42 us (0.948)
  Pallas kernels: 17.6 us -> 15.1 us
    pallas_call x1, Pallas kernels: 7.88 us -> 6.14 us  [local(): call(functools.partial(attend_kernel, images, piggy, halo), (shape((padde...]
    pallas_call x1, Pallas kernels: 3.3 us -> 2.83 us  [local(): call(functools.partial(far_kernel, images, piggy), (shape((depth, count),...]
  transfers between devices with their start and end apart: 15 -> 15, of which waited for: 9 -> 9; matrix products, arithmetic and copies ran while one was open for 0% -> 0% of each run, Pallas kernels for 9% -> 10%
where the time goes in v17:
time: 42 us; the launch traced here: 41.8 us
  starting transfers between devices  17.7 us (42%)
  Pallas kernels  15.1 us (36%)
  waiting for transfers between devices  8.38 us (20%)
  between operations  0.69 us (2%)
    ppermute x15, starting transfers between devices, moved(): return lax.ppermute(value, axis, pairs)  17.7 us
    ppermute x15, waiting for transfers between devices, moved(): return lax.ppermute(value, axis, pairs)  8.38 us
    pallas_call x1, Pallas kernels, local(): call(functools.partial(attend_kernel, images, piggy, halo), (shape((padde...  6.14 us
    pallas_call x1, Pallas kernels, local(): call(functools.partial(far_kernel, images, piggy), (shape((depth, count),...  2.83 us
    pallas_call x1, Pallas kernels, local(): call(functools.partial(near_kernel, piggy), (block,) * 6, [], in_vmem(3),...  2.34 us
    pallas_call x1, Pallas kernels, local(): call(functools.partial(finish_kernel, images), (shape((count, depth), bf1...  2.14 us
    pallas_call x1, Pallas kernels, local(): call(functools.partial(prepare_kernel, images, halo), (shape((len(EARLY)...  1.64 us
  transfers between devices with their start and end apart: 15, of which 9 were waited for; matrix products, arithmetic and copies ran while one was open for 0% of the time, Pallas kernels for 10%

profile of v17, /device:TPU:0, one launch (start us, length us, event | category | flops | bytes accessed | tf_op | source)
XLA Modules:
  0.0 41.8 jit_solution(3993746216312032703)
XLA Ops:
  0.6 0.0 copy-start
  0.6 2.8 %shard_map.68 = (bf16[1152,384]{1,0:T(8,128)(2,1)S(1)}, f32[8,1152]{1,0:T(8,128)S(1)}, bf16[224,384]{1,0:T(8,128)(2,1)S(1)}, bf16[224,384]{1,0:T(8,128)(2,1)S(1)}) custom-call(s32[1,3072]{1,0:T(1,128)} %ids_ref.5, bf16[384,1152]{1,0:T(8,128)(2,1)} %bitcast.6, bf16[1728,1152]{1,0:T(8,128)(2,1)} %bitcast.4), custom_call_target="tpu_custom_call" | custom-call | flops 382205952 | bytes 8388608 | tf_op jit(solution)/shard_map/pallas_call | solution.py:522
  3.5 4.0 %collective-permute-start = (bf16[224,384]{1,0:T(8,128)(2,1)S(1)}, bf16[224,384]{1,0:T(8,128)(2,1)S(1)}, u32[]{:S(2)}, u32[]{:S(2)}) collective-permute-start(bf16[224,384]{1,0:T(8,128)(2,1)S(1)} %get-tuple-element.28), channel_id=1, source_target_pairs={{0,24},{4,28},{8,16},{12,20},{16,8},{20,12},{24,0},{28,4},{1,25},{... | collective-permute-start | bytes 516104 | tf_op jit(solution)/shard_map/ppermute | solution.py:471
  7.4 0.0 collective-permute-start.1
  7.4 0.0 copy-done
  7.4 0.0 copy-start.3
  7.4 0.0 copy-start.2
  7.4 2.3 %shard_map.69 = (bf16[224,384]{1,0:T(8,128)(2,1)S(1)}, bf16[224,384]{1,0:T(8,128)(2,1)S(1)}, bf16[224,384]{1,0:T(8,128)(2,1)S(1)}, bf16[224,384]{1,0:T(8,128)(2,...) custom-call(bf16[1152,384]{1,0:T(8,128)(2,1)S(1)} %get-tuple-element.30.normed_ref, ...), custom_call_target="tpu_custom_call" | custom-call | flops 1146617856 | bytes 8388608 | tf_op jit(solution)/shard_map/pallas_call | solution.py:536
  9.8 0.3 collective-permute-start.2
  10.1 1.9 %collective-permute-start.3 = (bf16[224,384]{1,0:T(8,128)(2,1)S(1)}, bf16[224,384]{1,0:T(8,128)(2,1)S(1)}, u32[]{:S(2)}, u32[]{:S(2)}) collective-permute-start(bf16[224,384]{1,0:T(8,128)(2,1)S(1)} %get-tuple-element.39), channel_id=1, source_target_pairs={{0,8},{4,12},{8,0},{12,4},{16,24},{20,28},{24,16},{28,20},{1,9},{5... | collective-permute-start | bytes 516104 | tf_op jit(solution)/shard_map/ppermute | solution.py:471
  11.9 1.5 %collective-permute-start.4 = (bf16[224,384]{1,0:T(8,128)(2,1)S(1)}, bf16[224,384]{1,0:T(8,128)(2,1)S(1)}, u32[]{:S(2)}, u32[]{:S(2)}) collective-permute-start(bf16[224,384]{1,0:T(8,128)(2,1)S(1)} %get-tuple-element.40), channel_id=1, source_target_pairs={{0,16},{4,20},{8,24},{12,28},{16,0},{20,4},{24,8},{28,12},{1,17},{... | collective-permute-start | bytes 516104 | tf_op jit(solution)/shard_map/ppermute | solution.py:471
  13.5 0.0 collective-permute-done.rest_0_
  13.5 0.0 collective-permute-start.5
  13.5 2.4 %collective-permute-done.1.rest_1_ = bf16[224,384]{1,0:T(8,128)(2,1)S(1)} collective-permute-done((bf16[224,384]{1,0:T(8,128)(2,1)S(1)}, bf16[224,384]{1,0:T(8,128)(2,1)S(1)}, u32[]{:S(2)}, u32[]{:S(2)}) %collective-permute-start.1) | collective-permute-done | bytes 172064 | tf_op jit(solution)/shard_map/ppermute | solution.py:471
  15.9 1.9 %collective-permute-start.6 = (bf16[224,384]{1,0:T(8,128)(2,1)S(1)}, bf16[224,384]{1,0:T(8,128)(2,1)S(1)}, u32[]{:S(2)}, u32[]{:S(2)}) collective-permute-start(bf16[224,384]{1,0:T(8,128)(2,1)S(1)} %get-tuple-element.42), channel_id=1, source_target_pairs={{0,20},{4,16},{8,28},{12,24},{16,4},{20,0},{24,12},{28,8},{1,21},{... | collective-permute-start | bytes 516104 | tf_op jit(solution)/shard_map/ppermute | solution.py:471
  17.8 0.0 collective-permute-done.2.rest_2_
  17.8 0.0 copy-done.3
  17.8 1.6 %collective-permute-start.7 = (bf16[4,1152]{1,0:T(4,128)(2,1)S(1)}, bf16[4,1152]{1,0:T(4,128)(2,1)S(1)}, u32[]{:S(2)}, u32[]{:S(2)}) collective-permute-start(bf16[4,1152]{1,0:T(4,128)(2,1)S(1)} %copy-done.3), channel_id=1, source_target_pairs={{1,0},{0,1},{3,2},{2,3},{6,4},{7,5},{4,6},{5,7},{11,8},{10,9},{9,1... | collective-permute-start | bytes 27656 | tf_op jit(solution)/shard_map/ppermute | solution.py:471
  19.4 0.0 copy-done.2
  19.4 1.6 %shard_map.70 = (bf16[1536,128]{1,0:T(8,128)(2,1)S(1)}, f32[2,8,3072]{2,1,0:T(8,128)S(1)}, s32[8,128]{1,0:T(8,128)S(1)}, bf16[640,1152]{1,0:T(8,128)(2,1)S(1)}) custom-call(s32[1,3072]{1,0:T(1,128)S(1)} %copy-done.2, bf16[576,1152]{1,0:T(8,128)(2,1)} %out_weight_ref.1, bf16[224,384]{1,0:T(8,128)(2,1)S(1)} %collective-permute-done.rest_0_, ...), custom_call_target="tpu_custom_call" | custom-call | flops 1073741824 | bytes 8388608 | tf_op jit(solution)/shard_map/pallas_call | solution.py:577
  21.0 0.4 %collective-permute-done.7.rest_8_ = bf16[4,1152]{1,0:T(4,128)(2,1)S(1)} collective-permute-done((bf16[4,1152]{1,0:T(4,128)(2,1)S(1)}, bf16[4,1152]{1,0:T(4,128)(2,1)S(1)}, u32[]{:S(2)}, u32[]{:S(2)}) %collective-permute-start.7) | collective-permute-done | bytes 9248 | tf_op jit(solution)/shard_map/ppermute | solution.py:471
  21.5 0.0 collective-permute-done.3.rest_4_
  21.5 0.0 collective-permute-done.4.rest_5_
  21.5 0.7 %collective-permute-done.5.rest_6_ = bf16[224,384]{1,0:T(8,128)(2,1)S(1)} collective-permute-done((bf16[224,384]{1,0:T(8,128)(2,1)S(1)}, bf16[224,384]{1,0:T(8,128)(2,1)S(1)}, u32[]{:S(2)}, u32[]{:S(2)}) %collective-permute-start.5) | collective-permute-done | bytes 172064 | tf_op jit(solution)/shard_map/ppermute | solution.py:471
  22.1 0.6 %collective-permute-done.6.rest_7_ = bf16[224,384]{1,0:T(8,128)(2,1)S(1)} collective-permute-done((bf16[224,384]{1,0:T(8,128)(2,1)S(1)}, bf16[224,384]{1,0:T(8,128)(2,1)S(1)}, u32[]{:S(2)}, u32[]{:S(2)}) %collective-permute-start.6) | collective-permute-done | bytes 172064 | tf_op jit(solution)/shard_map/ppermute | solution.py:471
  22.8 0.0 copy-start.1
  22.8 6.1 %shard_map.71 = (bf16[96,384]{1,0:T(8,128)(2,1)S(1)}, bf16[96,384]{1,0:T(8,128)(2,1)S(1)}, bf16[96,384]{1,0:T(8,128)(2,1)S(1)}, bf16[96,384]{1,0:T(8,128)(2,1)S(...) custom-call(s32[1,3072]{1,0:T(1,128)S(1)} %copy-done.2, ...), custom_call_target="tpu_custom_call" | custom-call | flops 905969664 | bytes 8388608 | tf_op jit(solution)/shard_map/pallas_call | solution.py:590
  28.9 2.3 %collective-permute-start.8 = (bf16[96,384]{1,0:T(8,128)(2,1)S(1)}, bf16[96,384]{1,0:T(8,128)(2,1)S(1)}, u32[]{:S(2)}, u32[]{:S(2)}) collective-permute-start(bf16[96,384]{1,0:T(8,128)(2,1)S(1)} %get-tuple-element.44), channel_id=1, source_target_pairs={{0,24},{4,28},{8,16},{12,20},{16,8},{20,12},{24,0},{28,4},{1,25},{... | collective-permute-start | bytes 221192 | tf_op jit(solution)/shard_map/ppermute | solution.py:471
  31.2 0.2 collective-permute-start.9
  31.4 1.8 %collective-permute-start.10 = (bf16[96,384]{1,0:T(8,128)(2,1)S(1)}, bf16[96,384]{1,0:T(8,128)(2,1)S(1)}, u32[]{:S(2)}, u32[]{:S(2)}) collective-permute-start(bf16[96,384]{1,0:T(8,128)(2,1)S(1)} %get-tuple-element.46), channel_id=1, source_target_pairs={{0,8},{4,12},{8,0},{12,4},{16,24},{20,28},{24,16},{28,20},{1,9},{5... | collective-permute-start | bytes 221192 | tf_op jit(solution)/shard_map/ppermute | solution.py:471
  33.2 1.2 %collective-permute-start.11 = (bf16[96,384]{1,0:T(8,128)(2,1)S(1)}, bf16[96,384]{1,0:T(8,128)(2,1)S(1)}, u32[]{:S(2)}, u32[]{:S(2)}) collective-permute-start(bf16[96,384]{1,0:T(8,128)(2,1)S(1)} %get-tuple-element.47), channel_id=1, source_target_pairs={{0,16},{4,20},{8,24},{12,28},{16,0},{20,4},{24,8},{28,12},{1,17},{... | collective-permute-start | bytes 221192 | tf_op jit(solution)/shard_map/ppermute | solution.py:471
  34.4 0.1 collective-permute-start.12
  34.4 0.0 collective-permute-done.8.rest_0_
  34.4 0.8 %collective-permute-start.13 = (bf16[96,384]{1,0:T(8,128)(2,1)S(1)}, bf16[96,384]{1,0:T(8,128)(2,1)S(1)}, u32[]{:S(2)}, u32[]{:S(2)}) collective-permute-start(bf16[96,384]{1,0:T(8,128)(2,1)S(1)} %get-tuple-element.49), channel_id=1, source_target_pairs={{0,20},{4,16},{8,28},{12,24},{16,4},{20,0},{24,12},{28,8},{1,21},{... | collective-permute-start | bytes 221192 | tf_op jit(solution)/shard_map/ppermute | solution.py:471
  35.2 1.2 %collective-permute-done.9.rest_1_ = bf16[96,384]{1,0:T(8,128)(2,1)S(1)} collective-permute-done((bf16[96,384]{1,0:T(8,128)(2,1)S(1)}, bf16[96,384]{1,0:T(8,128)(2,1)S(1)}, u32[]{:S(2)}, u32[]{:S(2)}) %collective-permute-start.9) | collective-permute-done | bytes 73760 | tf_op jit(solution)/shard_map/ppermute | solution.py:471
  36.4 0.3 collective-permute-start.14
  36.8 1.0 %collective-permute-done.10.rest_2_ = bf16[96,384]{1,0:T(8,128)(2,1)S(1)} collective-permute-done((bf16[96,384]{1,0:T(8,128)(2,1)S(1)}, bf16[96,384]{1,0:T(8,128)(2,1)S(1)}, u32[]{:S(2)}, u32[]{:S(2)}) %collective-permute-start.10) | collective-permute-done | bytes 73760 | tf_op jit(solution)/shard_map/ppermute | solution.py:471
  37.8 0.7 %collective-permute-done.11.rest_3_ = bf16[96,384]{1,0:T(8,128)(2,1)S(1)} collective-permute-done((bf16[96,384]{1,0:T(8,128)(2,1)S(1)}, bf16[96,384]{1,0:T(8,128)(2,1)S(1)}, u32[]{:S(2)}, u32[]{:S(2)}) %collective-permute-start.11) | collective-permute-done | bytes 73760 | tf_op jit(solution)/shard_map/ppermute | solution.py:471
  38.4 1.1 %collective-permute-done.12.rest_4_ = bf16[96,384]{1,0:T(8,128)(2,1)S(1)} collective-permute-done((bf16[96,384]{1,0:T(8,128)(2,1)S(1)}, bf16[96,384]{1,0:T(8,128)(2,1)S(1)}, u32[]{:S(2)}, u32[]{:S(2)}) %collective-permute-start.12) | collective-permute-done | bytes 73760 | tf_op jit(solution)/shard_map/ppermute | solution.py:471
  39.5 0.2 collective-permute-done.13.rest_5_
  39.7 0.0 collective-permute-done.14.rest_6_
  39.7 0.0 copy-done.1
  39.7 2.1 %shard_map.72 = (bf16[384,1152]{1,0:T(8,128)(2,1)}, f32[1,4]{1,0:T(1,128)}) custom-call(bf16[384,1152]{1,0:T(8,128)(2,1)S(1)} %bitcast.7, bf16[640,1152]{1,0:T(8,128)(2,1)S(1)} %get-tuple-element.35.weight_ref, bf16[4,1152]{1,0:T(4,128)(2,1)S(1)} %copy-done.3, bf16[96,384]{1,0:T(8,128)(2,1)S(1)} %collective-permute-done.8.rest_0_, ...), custom_call_target="tpu_custom_call" | custom-call | flops 509607936 | bytes 8388608 | tf_op jit(solution)/shard_map/pallas_call | solution.py:618
Async XLA Ops:
  0.6 6.8 %copy-start = (bf16[1152,1728]{0,1:T(8,128)(2,1)S(1)}, bf16[1152,1728]{0,1:T(8,128)(2,1)}, u32[]{:S(2)}) copy-start(bf16[1152,1728]{0,1:T(8,128)(2,1)} %param.7) | copy-start | bytes 11943940
  3.5 10.0 %collective-permute-start = (bf16[224,384]{1,0:T(8,128)(2,1)S(1)}, bf16[224,384]{1,0:T(8,128)(2,1)S(1)}, u32[]{:S(2)}, u32[]{:S(2)}) collective-permute-start(bf16[224,384]{1,0:T(8,128)(2,1)S(1)} %get-tuple-element.28), channel_id=1, source_target_pairs={{0,24},{4,28},{8,16},{12,20},{16,8},{20,12},{24,0},{28,4},{1,25},{... | collective-permute-start | bytes 516104 | tf_op jit(solution)/shard_map/ppermute | solution.py:471
  7.4 8.5 %collective-permute-start.1 = (bf16[224,384]{1,0:T(8,128)(2,1)S(1)}, bf16[224,384]{1,0:T(8,128)(2,1)S(1)}, u32[]{:S(2)}, u32[]{:S(2)}) collective-permute-start(bf16[224,384]{1,0:T(8,128)(2,1)S(1)} %get-tuple-element.29), channel_id=1, source_target_pairs={{0,28},{4,24},{8,20},{12,16},{16,12},{20,8},{24,4},{28,0},{1,29},{... | collective-permute-start | bytes 516104 | tf_op jit(solution)/shard_map/ppermute | solution.py:471
  7.4 10.4 %copy-start.3 = (bf16[4,1152]{1,0:T(4,128)(2,1)S(1)}, bf16[4,1152]{1,0:T(4,128)(2,1)}, u32[]{:S(2)}) copy-start(bf16[4,1152]{1,0:T(4,128)(2,1)} %text_ref.1) | copy-start | bytes 27652
  7.4 11.9 %copy-start.2 = (s32[1,3072]{1,0:T(1,128)S(1)}, s32[1,3072]{1,0:T(1,128)}, u32[]{:S(2)}) copy-start(s32[1,3072]{1,0:T(1,128)} %ids_ref.5) | copy-start | bytes 36868
  9.8 8.0 %collective-permute-start.2 = (bf16[224,384]{1,0:T(8,128)(2,1)S(1)}, bf16[224,384]{1,0:T(8,128)(2,1)S(1)}, u32[]{:S(2)}, u32[]{:S(2)}) collective-permute-start(bf16[224,384]{1,0:T(8,128)(2,1)S(1)} %get-tuple-element.32), channel_id=1, source_target_pairs={{0,4},{4,0},{8,12},{12,8},{16,20},{20,16},{24,28},{28,24},{1,5},{5... | collective-permute-start | bytes 516104 | tf_op jit(solution)/shard_map/ppermute | solution.py:471
  10.1 11.4 %collective-permute-start.3 = (bf16[224,384]{1,0:T(8,128)(2,1)S(1)}, bf16[224,384]{1,0:T(8,128)(2,1)S(1)}, u32[]{:S(2)}, u32[]{:S(2)}) collective-permute-start(bf16[224,384]{1,0:T(8,128)(2,1)S(1)} %get-tuple-element.39), channel_id=1, source_target_pairs={{0,8},{4,12},{8,0},{12,4},{16,24},{20,28},{24,16},{28,20},{1,9},{5... | collective-permute-start | bytes 516104 | tf_op jit(solution)/shard_map/ppermute | solution.py:471
  11.9 9.5 %collective-permute-start.4 = (bf16[224,384]{1,0:T(8,128)(2,1)S(1)}, bf16[224,384]{1,0:T(8,128)(2,1)S(1)}, u32[]{:S(2)}, u32[]{:S(2)}) collective-permute-start(bf16[224,384]{1,0:T(8,128)(2,1)S(1)} %get-tuple-element.40), channel_id=1, source_target_pairs={{0,16},{4,20},{8,24},{12,28},{16,0},{20,4},{24,8},{28,12},{1,17},{... | collective-permute-start | bytes 516104 | tf_op jit(solution)/shard_map/ppermute | solution.py:471
  13.5 8.7 %collective-permute-start.5 = (bf16[224,384]{1,0:T(8,128)(2,1)S(1)}, bf16[224,384]{1,0:T(8,128)(2,1)S(1)}, u32[]{:S(2)}, u32[]{:S(2)}) collective-permute-start(bf16[224,384]{1,0:T(8,128)(2,1)S(1)} %get-tuple-element.41), channel_id=1, source_target_pairs={{0,12},{4,8},{8,4},{12,0},{16,28},{20,24},{24,20},{28,16},{1,13},{... | collective-permute-start | bytes 516104 | tf_op jit(solution)/shard_map/ppermute | solution.py:471
  15.9 6.9 %collective-permute-start.6 = (bf16[224,384]{1,0:T(8,128)(2,1)S(1)}, bf16[224,384]{1,0:T(8,128)(2,1)S(1)}, u32[]{:S(2)}, u32[]{:S(2)}) collective-permute-start(bf16[224,384]{1,0:T(8,128)(2,1)S(1)} %get-tuple-element.42), channel_id=1, source_target_pairs={{0,20},{4,16},{8,28},{12,24},{16,4},{20,0},{24,12},{28,8},{1,21},{... | collective-permute-start | bytes 516104 | tf_op jit(solution)/shard_map/ppermute | solution.py:471
  17.8 3.7 %collective-permute-start.7 = (bf16[4,1152]{1,0:T(4,128)(2,1)S(1)}, bf16[4,1152]{1,0:T(4,128)(2,1)S(1)}, u32[]{:S(2)}, u32[]{:S(2)}) collective-permute-start(bf16[4,1152]{1,0:T(4,128)(2,1)S(1)} %copy-done.3), channel_id=1, source_target_pairs={{1,0},{0,1},{3,2},{2,3},{6,4},{7,5},{4,6},{5,7},{11,8},{10,9},{9,1... | collective-permute-start | bytes 27656 | tf_op jit(solution)/shard_map/ppermute | solution.py:471
  22.8 16.9 %copy-start.1 = (bf16[1,384,1152]{2,1,0:T(8,128)(2,1)S(1)}, bf16[1,384,1152]{2,1,0:T(8,128)(2,1)}, u32[]{:S(2)}) copy-start(bf16[1,384,1152]{2,1,0:T(8,128)(2,1)} %param.5) | copy-start | bytes 2654212
  28.9 5.5 %collective-permute-start.8 = (bf16[96,384]{1,0:T(8,128)(2,1)S(1)}, bf16[96,384]{1,0:T(8,128)(2,1)S(1)}, u32[]{:S(2)}, u32[]{:S(2)}) collective-permute-start(bf16[96,384]{1,0:T(8,128)(2,1)S(1)} %get-tuple-element.44), channel_id=1, source_target_pairs={{0,24},{4,28},{8,16},{12,20},{16,8},{20,12},{24,0},{28,4},{1,25},{... | collective-permute-start | bytes 221192 | tf_op jit(solution)/shard_map/ppermute | solution.py:471
  31.2 5.2 %collective-permute-start.9 = (bf16[96,384]{1,0:T(8,128)(2,1)S(1)}, bf16[96,384]{1,0:T(8,128)(2,1)S(1)}, u32[]{:S(2)}, u32[]{:S(2)}) collective-permute-start(bf16[96,384]{1,0:T(8,128)(2,1)S(1)} %get-tuple-element.45), channel_id=1, source_target_pairs={{0,28},{4,24},{8,20},{12,16},{16,12},{20,8},{24,4},{28,0},{1,29},{... | collective-permute-start | bytes 221192 | tf_op jit(solution)/shard_map/ppermute | solution.py:471
  31.4 6.3 %collective-permute-start.10 = (bf16[96,384]{1,0:T(8,128)(2,1)S(1)}, bf16[96,384]{1,0:T(8,128)(2,1)S(1)}, u32[]{:S(2)}, u32[]{:S(2)}) collective-permute-start(bf16[96,384]{1,0:T(8,128)(2,1)S(1)} %get-tuple-element.46), channel_id=1, source_target_pairs={{0,8},{4,12},{8,0},{12,4},{16,24},{20,28},{24,16},{28,20},{1,9},{5... | collective-permute-start | bytes 221192 | tf_op jit(solution)/shard_map/ppermute | solution.py:471
  33.2 5.2 %collective-permute-start.11 = (bf16[96,384]{1,0:T(8,128)(2,1)S(1)}, bf16[96,384]{1,0:T(8,128)(2,1)S(1)}, u32[]{:S(2)}, u32[]{:S(2)}) collective-permute-start(bf16[96,384]{1,0:T(8,128)(2,1)S(1)} %get-tuple-element.47), channel_id=1, source_target_pairs={{0,16},{4,20},{8,24},{12,28},{16,0},{20,4},{24,8},{28,12},{1,17},{... | collective-permute-start | bytes 221192 | tf_op jit(solution)/shard_map/ppermute | solution.py:471
  34.4 5.1 %collective-permute-start.12 = (bf16[96,384]{1,0:T(8,128)(2,1)S(1)}, bf16[96,384]{1,0:T(8,128)(2,1)S(1)}, u32[]{:S(2)}, u32[]{:S(2)}) collective-permute-start(bf16[96,384]{1,0:T(8,128)(2,1)S(1)} %get-tuple-element.48), channel_id=1, source_target_pairs={{0,12},{4,8},{8,4},{12,0},{16,28},{20,24},{24,20},{28,16},{1,13},{... | collective-permute-start | bytes 221192 | tf_op jit(solution)/shard_map/ppermute | solution.py:471
  34.4 5.2 %collective-permute-start.13 = (bf16[96,384]{1,0:T(8,128)(2,1)S(1)}, bf16[96,384]{1,0:T(8,128)(2,1)S(1)}, u32[]{:S(2)}, u32[]{:S(2)}) collective-permute-start(bf16[96,384]{1,0:T(8,128)(2,1)S(1)} %get-tuple-element.49), channel_id=1, source_target_pairs={{0,20},{4,16},{8,28},{12,24},{16,4},{20,0},{24,12},{28,8},{1,21},{... | collective-permute-start | bytes 221192 | tf_op jit(solution)/shard_map/ppermute | solution.py:471
  36.4 3.2 %collective-permute-start.14 = (bf16[96,384]{1,0:T(8,128)(2,1)S(1)}, bf16[96,384]{1,0:T(8,128)(2,1)S(1)}, u32[]{:S(2)}, u32[]{:S(2)}) collective-permute-start(bf16[96,384]{1,0:T(8,128)(2,1)S(1)} %get-tuple-element.50), channel_id=1, source_target_pairs={{0,4},{4,0},{8,12},{12,8},{16,20},{20,16},{24,28},{28,24},{1,5},{5... | collective-permute-start | bytes 221192 | tf_op jit(solution)/shard_map/ppermute | solution.py:471

commit v18 on v17

--- a/solution.py
+++ b/solution.py
@@ -17,6 +17,7 @@
 KEY_AT = SIZE - SPARE
 QUERY_AT = 2 * SIZE
 TEXT_ROWS = 16
+RUN = 16
 HIDDEN = -1e30
 ORDER = (6, 7, 2, 4, 3, 5, 1, 0)
 EARLY = (6, 7, 1, 0)
@@ -55,22 +56,13 @@
             parts = [sums[:, pl.ds(first, LANES)], sums[:, HEADS * LANES :]]
             held = sum(part.shape[1] for part in parts)
             spare = jnp.concatenate(parts + [jnp.zeros((SPARE, count - held), jnp.float32)], axis=1)
-        block = jnp.concatenate([value[here], key[here], spare, query[here]], axis=0)
-        yield block.astype(jnp.bfloat16)
+        yield jnp.concatenate([value[here], key[here], spare, query[here]], axis=0)
 
 
 def store_by_core(core, blocks, same_ref, cross_ref):
     first, second = blocks
-
-    @pl.when(core == 0)
-    def _():
-        same_ref[...] = first
-        cross_ref[...] = second
-
-    @pl.when(core == 1)
-    def _():
-        same_ref[...] = second
-        cross_ref[...] = first
+    same_ref[...] = jnp.where(core == 0, first, second).astype(jnp.bfloat16)
+    cross_ref[...] = jnp.where(core == 0, second, first).astype(jnp.bfloat16)
 
 
 def place_in_group():
@@ -162,26 +154,27 @@
 
 
 def attend_images(images, ids_ref, keys, values, queries, attended, work, starts, halo):
-    scores_a, scores_b, tops_a, tops_b = work
+    work = list(zip(work[0::2], work[1::2]))
     query_base = halo
-    window, tile = scores_a.shape
+    window, tile = work[0][0].shape
     size = attended.shape[0] - SPARE
     held = queries.shape[1]
     tiles = held // tile
+
+    low = image_at(images, starts, query_base)
+    high = image_at(images, starts, query_base + held - 1)
 
     def bounds(image):
         first = lax.div(jnp.maximum(starts[image] - query_base, 0), tile)
         last = lax.div(jnp.minimum(starts[image + 1] - query_base, held) - 1, tile)
         return jnp.minimum(first, tiles - 1), last
 
-    def after(image):
-        return jnp.minimum(image + 1, images - 1)
-
     def following(state):
         at, image = state
         more = at < bounds(image)[1]
-        later = after(image)
-        return jnp.where(more, at + 1, bounds(later)[0]), jnp.where(more, image, later)
+        later = jnp.minimum(image + 1, high)
+        first = jnp.where(image == high, at, bounds(later)[0])
+        return jnp.where(more, at + 1, first), jnp.where(more, image, later)
 
     def window_of(image):
         begin = lax.div(starts[image], LANES) * LANES
@@ -206,34 +199,29 @@
         place = (slice(None), pl.ds(first, tile))
         attended[place] = jnp.where(labels == image, weighted * share, attended[place])
 
-    low = image_at(images, starts, query_base)
-    high = image_at(images, starts, query_base + held - 1)
     pairs = jnp.int32(0)
     for image in range(images):
         first, last = bounds(image)
         wanted = jnp.logical_and(low <= image, image <= high)
         pairs += jnp.where(wanted, last - first + 1, 0)
 
-    def two_pairs(_, state):
-        second = following(state)
-        score(second, scores_b, tops_b)
-        weigh(state, scores_a, tops_a)
-        third = following(second)
-        score(third, scores_a, tops_a)
-        weigh(second, scores_b, tops_b)
-        return third
-
-    def four_pairs(step, state):
-        return two_pairs(step, two_pairs(step, state))
-
-    begun = (jnp.int32(0), low)
-    score(begun, scores_a, tops_a)
-    reached = lax.fori_loop(0, lax.div(pairs, 4), four_pairs, begun)
-    reached = lax.fori_loop(0, lax.div(lax.rem(pairs, 4), 2), two_pairs, reached)
-
-    @pl.when(lax.rem(pairs, 2) == 1)
-    def _():
-        weigh(reached, scores_a, tops_a)
+    def run(state, steps, ends):
+        for step in range(steps):
+            later = following(state)
+            if step < steps - 1 or not ends:
+                score(later, *work[(step + 1) % len(work)])
+            weigh(state, *work[step % len(work)])
+            state = later
+        return state
+
+    state = (jnp.int32(0), low)
+    score(state, *work[0])
+    limit = tiles + images - 1
+    if limit <= RUN:
+        run(state, limit, True)
+    else:
+        step = len(work) * max(1, RUN // (2 * len(work)))
+        lax.fori_loop(0, lax.div(pairs + step - 1, step), lambda _, state: run(state, step, False), state)
 
 
 def turned_keys(marked, block_ref):
@@ -595,12 +583,9 @@
             pltpu.VMEM((padded, reach), bf16),
             pltpu.VMEM((LANES, length), bf16),
             pltpu.VMEM((padded, length), f32),
-            pltpu.VMEM((window, tile), f32),
-            pltpu.VMEM((window, tile), f32),
-            pltpu.VMEM((1, tile), f32),
-            pltpu.VMEM((1, tile), f32),
-            pltpu.SMEM((images + 1,), jnp.int32),
-        ],
+        ]
+        + [pltpu.VMEM((window, tile), f32), pltpu.VMEM((1, tile), f32)] * 3
+        + [pltpu.SMEM((images + 1,), jnp.int32)],
         in_vmem(len(operands)),
         4 * size * length * MAXP,
     )(*operands)

time: 42 us -> 43.5 us (1.036)
  Pallas kernels: 15.1 us -> 16.2 us
    pallas_call x1, Pallas kernels: 6.14 us -> 7.67 us  [local(): call(functools.partial(attend_kernel, images, piggy, halo), (shape((padde...]
  transfers between devices with their start and end apart: 15 -> 15, of which waited for: 9 -> 9; matrix products, arithmetic and copies ran while one was open for 0% -> 0% of each run, Pallas kernels for 10% -> 8%
where the time goes in v18:
time: 43.5 us; the launch traced here: 43.3 us
  starting transfers between devices  17.6 us (40%)
  Pallas kernels  16.2 us (37%)
  waiting for transfers between devices  8.79 us (20%)
  between operations  0.69 us (2%)
    ppermute x15, starting transfers between devices, moved(): return lax.ppermute(value, axis, pairs)  17.6 us
    ppermute x15, waiting for transfers between devices, moved(): return lax.ppermute(value, axis, pairs)  8.79 us
    pallas_call x1, Pallas kernels, local(): call(functools.partial(attend_kernel, images, piggy, halo), (shape((padde...  7.67 us
    pallas_call x1, Pallas kernels, local(): call(functools.partial(far_kernel, images, piggy), (shape((depth, count),...  2.8 us
    pallas_call x1, Pallas kernels, local(): call(functools.partial(finish_kernel, images), (shape((count, depth), bf1...  2.14 us
    pallas_call x1, Pallas kernels, local(): call(functools.partial(near_kernel, piggy), (block,) * 6, [], in_vmem(3),...  1.95 us
    pallas_call x1, Pallas kernels, local(): call(functools.partial(prepare_kernel, images, halo), (shape((len(EARLY)...  1.64 us
  transfers between devices with their start and end apart: 15, of which 9 were waited for; matrix products, arithmetic and copies ran while one was open for 0% of the time, Pallas kernels for 8%

profile of v18, /device:TPU:0, one launch (start us, length us, event | category | flops | bytes accessed | tf_op | source)
XLA Modules:
  0.0 43.3 jit_solution(17502489744036985607)
XLA Ops:
  0.6 0.0 copy-start
  0.6 2.8 %shard_map.68 = (bf16[1152,384]{1,0:T(8,128)(2,1)S(1)}, f32[8,1152]{1,0:T(8,128)S(1)}, bf16[224,384]{1,0:T(8,128)(2,1)S(1)}, bf16[224,384]{1,0:T(8,128)(2,1)S(1)}) custom-call(s32[1,3072]{1,0:T(1,128)} %ids_ref.5, bf16[384,1152]{1,0:T(8,128)(2,1)} %bitcast.6, bf16[1728,1152]{1,0:T(8,128)(2,1)} %bitcast.4), custom_call_target="tpu_custom_call" | custom-call | flops 382205952 | bytes 8388608 | tf_op jit(solution)/shard_map/pallas_call | solution.py:510
  3.4 4.0 %collective-permute-start = (bf16[224,384]{1,0:T(8,128)(2,1)S(1)}, bf16[224,384]{1,0:T(8,128)(2,1)S(1)}, u32[]{:S(2)}, u32[]{:S(2)}) collective-permute-start(bf16[224,384]{1,0:T(8,128)(2,1)S(1)} %get-tuple-element.28), channel_id=1, source_target_pairs={{0,24},{4,28},{8,16},{12,20},{16,8},{20,12},{24,0},{28,4},{1,25},{... | collective-permute-start | bytes 516104 | tf_op jit(solution)/shard_map/ppermute | solution.py:459
  7.4 0.0 collective-permute-start.1
  7.4 0.0 copy-done
  7.4 0.0 copy-start.3
  7.4 0.0 copy-start.2
  7.4 1.9 %shard_map.69 = (bf16[224,384]{1,0:T(8,128)(2,1)S(1)}, bf16[224,384]{1,0:T(8,128)(2,1)S(1)}, bf16[224,384]{1,0:T(8,128)(2,1)S(1)}, bf16[224,384]{1,0:T(8,128)(2,...) custom-call(bf16[1152,384]{1,0:T(8,128)(2,1)S(1)} %get-tuple-element.30.normed_ref, ...), custom_call_target="tpu_custom_call" | custom-call | flops 1146617856 | bytes 8388608 | tf_op jit(solution)/shard_map/pallas_call | solution.py:524
  9.4 0.2 collective-permute-start.2
  9.6 1.9 %collective-permute-start.3 = (bf16[224,384]{1,0:T(8,128)(2,1)S(1)}, bf16[224,384]{1,0:T(8,128)(2,1)S(1)}, u32[]{:S(2)}, u32[]{:S(2)}) collective-permute-start(bf16[224,384]{1,0:T(8,128)(2,1)S(1)} %get-tuple-element.39), channel_id=1, source_target_pairs={{0,8},{4,12},{8,0},{12,4},{16,24},{20,28},{24,16},{28,20},{1,9},{5... | collective-permute-start | bytes 516104 | tf_op jit(solution)/shard_map/ppermute | solution.py:459
  11.5 1.5 %collective-permute-start.4 = (bf16[224,384]{1,0:T(8,128)(2,1)S(1)}, bf16[224,384]{1,0:T(8,128)(2,1)S(1)}, u32[]{:S(2)}, u32[]{:S(2)}) collective-permute-start(bf16[224,384]{1,0:T(8,128)(2,1)S(1)} %get-tuple-element.40), channel_id=1, source_target_pairs={{0,16},{4,20},{8,24},{12,28},{16,0},{20,4},{24,8},{28,12},{1,17},{... | collective-permute-start | bytes 516104 | tf_op jit(solution)/shard_map/ppermute | solution.py:459
  13.0 0.0 collective-permute-done.rest_0_
  13.0 0.0 collective-permute-start.5
  13.0 2.9 %collective-permute-done.1.rest_1_ = bf16[224,384]{1,0:T(8,128)(2,1)S(1)} collective-permute-done((bf16[224,384]{1,0:T(8,128)(2,1)S(1)}, bf16[224,384]{1,0:T(8,128)(2,1)S(1)}, u32[]{:S(2)}, u32[]{:S(2)}) %collective-permute-start.1) | collective-permute-done | bytes 172064 | tf_op jit(solution)/shard_map/ppermute | solution.py:459
  15.9 1.9 %collective-permute-start.6 = (bf16[224,384]{1,0:T(8,128)(2,1)S(1)}, bf16[224,384]{1,0:T(8,128)(2,1)S(1)}, u32[]{:S(2)}, u32[]{:S(2)}) collective-permute-start(bf16[224,384]{1,0:T(8,128)(2,1)S(1)} %get-tuple-element.42), channel_id=1, source_target_pairs={{0,20},{4,16},{8,28},{12,24},{16,4},{20,0},{24,12},{28,8},{1,21},{... | collective-permute-start | bytes 516104 | tf_op jit(solution)/shard_map/ppermute | solution.py:459
  17.8 0.0 collective-permute-done.2.rest_2_
  17.8 0.0 copy-done.3
  17.8 1.6 %collective-permute-start.7 = (bf16[4,1152]{1,0:T(4,128)(2,1)S(1)}, bf16[4,1152]{1,0:T(4,128)(2,1)S(1)}, u32[]{:S(2)}, u32[]{:S(2)}) collective-permute-start(bf16[4,1152]{1,0:T(4,128)(2,1)S(1)} %copy-done.3), channel_id=1, source_target_pairs={{1,0},{0,1},{3,2},{2,3},{6,4},{7,5},{4,6},{5,7},{11,8},{10,9},{9,1... | collective-permute-start | bytes 27656 | tf_op jit(solution)/shard_map/ppermute | solution.py:459
  19.3 0.0 copy-done.2
  19.3 1.6 %shard_map.70 = (bf16[1536,128]{1,0:T(8,128)(2,1)S(1)}, f32[2,8,3072]{2,1,0:T(8,128)S(1)}, s32[8,128]{1,0:T(8,128)S(1)}, bf16[640,1152]{1,0:T(8,128)(2,1)S(1)}) custom-call(s32[1,3072]{1,0:T(1,128)S(1)} %copy-done.2, bf16[576,1152]{1,0:T(8,128)(2,1)} %out_weight_ref.1, bf16[224,384]{1,0:T(8,128)(2,1)S(1)} %collective-permute-done.rest_0_, ...), custom_call_target="tpu_custom_call" | custom-call | flops 1073741824 | bytes 8388608 | tf_op jit(solution)/shard_map/pallas_call | solution.py:565
  21.0 0.4 %collective-permute-done.7.rest_8_ = bf16[4,1152]{1,0:T(4,128)(2,1)S(1)} collective-permute-done((bf16[4,1152]{1,0:T(4,128)(2,1)S(1)}, bf16[4,1152]{1,0:T(4,128)(2,1)S(1)}, u32[]{:S(2)}, u32[]{:S(2)}) %collective-permute-start.7) | collective-permute-done | bytes 9248 | tf_op jit(solution)/shard_map/ppermute | solution.py:459
  21.4 0.0 collective-permute-done.3.rest_4_
  21.4 0.0 collective-permute-done.4.rest_5_
  21.4 0.7 %collective-permute-done.5.rest_6_ = bf16[224,384]{1,0:T(8,128)(2,1)S(1)} collective-permute-done((bf16[224,384]{1,0:T(8,128)(2,1)S(1)}, bf16[224,384]{1,0:T(8,128)(2,1)S(1)}, u32[]{:S(2)}, u32[]{:S(2)}) %collective-permute-start.5) | collective-permute-done | bytes 172064 | tf_op jit(solution)/shard_map/ppermute | solution.py:459
  22.1 0.6 %collective-permute-done.6.rest_7_ = bf16[224,384]{1,0:T(8,128)(2,1)S(1)} collective-permute-done((bf16[224,384]{1,0:T(8,128)(2,1)S(1)}, bf16[224,384]{1,0:T(8,128)(2,1)S(1)}, u32[]{:S(2)}, u32[]{:S(2)}) %collective-permute-start.6) | collective-permute-done | bytes 172064 | tf_op jit(solution)/shard_map/ppermute | solution.py:459
  22.7 0.0 copy-start.1
  22.7 7.7 %shard_map.71 = (bf16[96,384]{1,0:T(8,128)(2,1)S(1)}, bf16[96,384]{1,0:T(8,128)(2,1)S(1)}, bf16[96,384]{1,0:T(8,128)(2,1)S(1)}, bf16[96,384]{1,0:T(8,128)(2,1)S(...) custom-call(s32[1,3072]{1,0:T(1,128)S(1)} %copy-done.2, ...), custom_call_target="tpu_custom_call" | custom-call | flops 905969664 | bytes 8388608 | tf_op jit(solution)/shard_map/pallas_call | solution.py:578
  30.4 2.3 %collective-permute-start.8 = (bf16[96,384]{1,0:T(8,128)(2,1)S(1)}, bf16[96,384]{1,0:T(8,128)(2,1)S(1)}, u32[]{:S(2)}, u32[]{:S(2)}) collective-permute-start(bf16[96,384]{1,0:T(8,128)(2,1)S(1)} %get-tuple-element.44), channel_id=1, source_target_pairs={{0,24},{4,28},{8,16},{12,20},{16,8},{20,12},{24,0},{28,4},{1,25},{... | collective-permute-start | bytes 221192 | tf_op jit(solution)/shard_map/ppermute | solution.py:459
  32.7 0.2 collective-permute-start.9
  32.9 1.8 %collective-permute-start.10 = (bf16[96,384]{1,0:T(8,128)(2,1)S(1)}, bf16[96,384]{1,0:T(8,128)(2,1)S(1)}, u32[]{:S(2)}, u32[]{:S(2)}) collective-permute-start(bf16[96,384]{1,0:T(8,128)(2,1)S(1)} %get-tuple-element.46), channel_id=1, source_target_pairs={{0,8},{4,12},{8,0},{12,4},{16,24},{20,28},{24,16},{28,20},{1,9},{5... | collective-permute-start | bytes 221192 | tf_op jit(solution)/shard_map/ppermute | solution.py:459
  34.7 1.2 %collective-permute-start.11 = (bf16[96,384]{1,0:T(8,128)(2,1)S(1)}, bf16[96,384]{1,0:T(8,128)(2,1)S(1)}, u32[]{:S(2)}, u32[]{:S(2)}) collective-permute-start(bf16[96,384]{1,0:T(8,128)(2,1)S(1)} %get-tuple-element.47), channel_id=1, source_target_pairs={{0,16},{4,20},{8,24},{12,28},{16,0},{20,4},{24,8},{28,12},{1,17},{... | collective-permute-start | bytes 221192 | tf_op jit(solution)/shard_map/ppermute | solution.py:459
  35.9 0.0 collective-permute-start.12
  35.9 0.0 collective-permute-done.8.rest_0_
  35.9 0.8 %collective-permute-start.13 = (bf16[96,384]{1,0:T(8,128)(2,1)S(1)}, bf16[96,384]{1,0:T(8,128)(2,1)S(1)}, u32[]{:S(2)}, u32[]{:S(2)}) collective-permute-start(bf16[96,384]{1,0:T(8,128)(2,1)S(1)} %get-tuple-element.49), channel_id=1, source_target_pairs={{0,20},{4,16},{8,28},{12,24},{16,4},{20,0},{24,12},{28,8},{1,21},{... | collective-permute-start | bytes 221192 | tf_op jit(solution)/shard_map/ppermute | solution.py:459
  36.7 1.2 %collective-permute-done.9.rest_1_ = bf16[96,384]{1,0:T(8,128)(2,1)S(1)} collective-permute-done((bf16[96,384]{1,0:T(8,128)(2,1)S(1)}, bf16[96,384]{1,0:T(8,128)(2,1)S(1)}, u32[]{:S(2)}, u32[]{:S(2)}) %collective-permute-start.9) | collective-permute-done | bytes 73760 | tf_op jit(solution)/shard_map/ppermute | solution.py:459
  37.9 0.3 collective-permute-start.14
  38.2 1.0 %collective-permute-done.10.rest_2_ = bf16[96,384]{1,0:T(8,128)(2,1)S(1)} collective-permute-done((bf16[96,384]{1,0:T(8,128)(2,1)S(1)}, bf16[96,384]{1,0:T(8,128)(2,1)S(1)}, u32[]{:S(2)}, u32[]{:S(2)}) %collective-permute-start.10) | collective-permute-done | bytes 73760 | tf_op jit(solution)/shard_map/ppermute | solution.py:459
  39.3 0.7 %collective-permute-done.11.rest_3_ = bf16[96,384]{1,0:T(8,128)(2,1)S(1)} collective-permute-done((bf16[96,384]{1,0:T(8,128)(2,1)S(1)}, bf16[96,384]{1,0:T(8,128)(2,1)S(1)}, u32[]{:S(2)}, u32[]{:S(2)}) %collective-permute-start.11) | collective-permute-done | bytes 73760 | tf_op jit(solution)/shard_map/ppermute | solution.py:459
  39.9 1.1 %collective-permute-done.12.rest_4_ = bf16[96,384]{1,0:T(8,128)(2,1)S(1)} collective-permute-done((bf16[96,384]{1,0:T(8,128)(2,1)S(1)}, bf16[96,384]{1,0:T(8,128)(2,1)S(1)}, u32[]{:S(2)}, u32[]{:S(2)}) %collective-permute-start.12) | collective-permute-done | bytes 73760 | tf_op jit(solution)/shard_map/ppermute | solution.py:459
  41.0 0.2 collective-permute-done.13.rest_5_
  41.2 0.0 collective-permute-done.14.rest_6_
  41.2 0.0 copy-done.1
  41.2 2.1 %shard_map.72 = (bf16[384,1152]{1,0:T(8,128)(2,1)}, f32[1,4]{1,0:T(1,128)}) custom-call(bf16[384,1152]{1,0:T(8,128)(2,1)S(1)} %bitcast.7, bf16[640,1152]{1,0:T(8,128)(2,1)S(1)} %get-tuple-element.35.weight_ref, bf16[4,1152]{1,0:T(4,128)(2,1)S(1)} %copy-done.3, bf16[96,384]{1,0:T(8,128)(2,1)S(1)} %collective-permute-done.8.rest_0_, ...), custom_call_target="tpu_custom_call" | custom-call | flops 509607936 | bytes 8388608 | tf_op jit(solution)/shard_map/pallas_call | solution.py:603
Async XLA Ops:
  0.6 6.8 %copy-start = (bf16[1152,1728]{0,1:T(8,128)(2,1)S(1)}, bf16[1152,1728]{0,1:T(8,128)(2,1)}, u32[]{:S(2)}) copy-start(bf16[1152,1728]{0,1:T(8,128)(2,1)} %param.7) | copy-start | bytes 11943940
  3.4 9.6 %collective-permute-start = (bf16[224,384]{1,0:T(8,128)(2,1)S(1)}, bf16[224,384]{1,0:T(8,128)(2,1)S(1)}, u32[]{:S(2)}, u32[]{:S(2)}) collective-permute-start(bf16[224,384]{1,0:T(8,128)(2,1)S(1)} %get-tuple-element.28), channel_id=1, source_target_pairs={{0,24},{4,28},{8,16},{12,20},{16,8},{20,12},{24,0},{28,4},{1,25},{... | collective-permute-start | bytes 516104 | tf_op jit(solution)/shard_map/ppermute | solution.py:459
  7.4 8.5 %collective-permute-start.1 = (bf16[224,384]{1,0:T(8,128)(2,1)S(1)}, bf16[224,384]{1,0:T(8,128)(2,1)S(1)}, u32[]{:S(2)}, u32[]{:S(2)}) collective-permute-start(bf16[224,384]{1,0:T(8,128)(2,1)S(1)} %get-tuple-element.29), channel_id=1, source_target_pairs={{0,28},{4,24},{8,20},{12,16},{16,12},{20,8},{24,4},{28,0},{1,29},{... | collective-permute-start | bytes 516104 | tf_op jit(solution)/shard_map/ppermute | solution.py:459
  7.4 10.4 %copy-start.3 = (bf16[4,1152]{1,0:T(4,128)(2,1)S(1)}, bf16[4,1152]{1,0:T(4,128)(2,1)}, u32[]{:S(2)}) copy-start(bf16[4,1152]{1,0:T(4,128)(2,1)} %text_ref.1) | copy-start | bytes 27652
  7.4 11.9 %copy-start.2 = (s32[1,3072]{1,0:T(1,128)S(1)}, s32[1,3072]{1,0:T(1,128)}, u32[]{:S(2)}) copy-start(s32[1,3072]{1,0:T(1,128)} %ids_ref.5) | copy-start | bytes 36868
  9.4 8.4 %collective-permute-start.2 = (bf16[224,384]{1,0:T(8,128)(2,1)S(1)}, bf16[224,384]{1,0:T(8,128)(2,1)S(1)}, u32[]{:S(2)}, u32[]{:S(2)}) collective-permute-start(bf16[224,384]{1,0:T(8,128)(2,1)S(1)} %get-tuple-element.32), channel_id=1, source_target_pairs={{0,4},{4,0},{8,12},{12,8},{16,20},{20,16},{24,28},{28,24},{1,5},{5... | collective-permute-start | bytes 516104 | tf_op jit(solution)/shard_map/ppermute | solution.py:459
  9.6 11.8 %collective-permute-start.3 = (bf16[224,384]{1,0:T(8,128)(2,1)S(1)}, bf16[224,384]{1,0:T(8,128)(2,1)S(1)}, u32[]{:S(2)}, u32[]{:S(2)}) collective-permute-start(bf16[224,384]{1,0:T(8,128)(2,1)S(1)} %get-tuple-element.39), channel_id=1, source_target_pairs={{0,8},{4,12},{8,0},{12,4},{16,24},{20,28},{24,16},{28,20},{1,9},{5... | collective-permute-start | bytes 516104 | tf_op jit(solution)/shard_map/ppermute | solution.py:459
  11.5 9.9 %collective-permute-start.4 = (bf16[224,384]{1,0:T(8,128)(2,1)S(1)}, bf16[224,384]{1,0:T(8,128)(2,1)S(1)}, u32[]{:S(2)}, u32[]{:S(2)}) collective-permute-start(bf16[224,384]{1,0:T(8,128)(2,1)S(1)} %get-tuple-element.40), channel_id=1, source_target_pairs={{0,16},{4,20},{8,24},{12,28},{16,0},{20,4},{24,8},{28,12},{1,17},{... | collective-permute-start | bytes 516104 | tf_op jit(solution)/shard_map/ppermute | solution.py:459
  13.0 9.1 %collective-permute-start.5 = (bf16[224,384]{1,0:T(8,128)(2,1)S(1)}, bf16[224,384]{1,0:T(8,128)(2,1)S(1)}, u32[]{:S(2)}, u32[]{:S(2)}) collective-permute-start(bf16[224,384]{1,0:T(8,128)(2,1)S(1)} %get-tuple-element.41), channel_id=1, source_target_pairs={{0,12},{4,8},{8,4},{12,0},{16,28},{20,24},{24,20},{28,16},{1,13},{... | collective-permute-start | bytes 516104 | tf_op jit(solution)/shard_map/ppermute | solution.py:459
  15.9 6.9 %collective-permute-start.6 = (bf16[224,384]{1,0:T(8,128)(2,1)S(1)}, bf16[224,384]{1,0:T(8,128)(2,1)S(1)}, u32[]{:S(2)}, u32[]{:S(2)}) collective-permute-start(bf16[224,384]{1,0:T(8,128)(2,1)S(1)} %get-tuple-element.42), channel_id=1, source_target_pairs={{0,20},{4,16},{8,28},{12,24},{16,4},{20,0},{24,12},{28,8},{1,21},{... | collective-permute-start | bytes 516104 | tf_op jit(solution)/shard_map/ppermute | solution.py:459
  17.8 3.7 %collective-permute-start.7 = (bf16[4,1152]{1,0:T(4,128)(2,1)S(1)}, bf16[4,1152]{1,0:T(4,128)(2,1)S(1)}, u32[]{:S(2)}, u32[]{:S(2)}) collective-permute-start(bf16[4,1152]{1,0:T(4,128)(2,1)S(1)} %copy-done.3), channel_id=1, source_target_pairs={{1,0},{0,1},{3,2},{2,3},{6,4},{7,5},{4,6},{5,7},{11,8},{10,9},{9,1... | collective-permute-start | bytes 27656 | tf_op jit(solution)/shard_map/ppermute | solution.py:459
  22.7 18.4 %copy-start.1 = (bf16[1,384,1152]{2,1,0:T(8,128)(2,1)S(1)}, bf16[1,384,1152]{2,1,0:T(8,128)(2,1)}, u32[]{:S(2)}) copy-start(bf16[1,384,1152]{2,1,0:T(8,128)(2,1)} %param.5) | copy-start | bytes 2654212
  30.4 5.5 %collective-permute-start.8 = (bf16[96,384]{1,0:T(8,128)(2,1)S(1)}, bf16[96,384]{1,0:T(8,128)(2,1)S(1)}, u32[]{:S(2)}, u32[]{:S(2)}) collective-permute-start(bf16[96,384]{1,0:T(8,128)(2,1)S(1)} %get-tuple-element.44), channel_id=1, source_target_pairs={{0,24},{4,28},{8,16},{12,20},{16,8},{20,12},{24,0},{28,4},{1,25},{... | collective-permute-start | bytes 221192 | tf_op jit(solution)/shard_map/ppermute | solution.py:459
  32.7 5.2 %collective-permute-start.9 = (bf16[96,384]{1,0:T(8,128)(2,1)S(1)}, bf16[96,384]{1,0:T(8,128)(2,1)S(1)}, u32[]{:S(2)}, u32[]{:S(2)}) collective-permute-start(bf16[96,384]{1,0:T(8,128)(2,1)S(1)} %get-tuple-element.45), channel_id=1, source_target_pairs={{0,28},{4,24},{8,20},{12,16},{16,12},{20,8},{24,4},{28,0},{1,29},{... | collective-permute-start | bytes 221192 | tf_op jit(solution)/shard_map/ppermute | solution.py:459
  32.9 6.3 %collective-permute-start.10 = (bf16[96,384]{1,0:T(8,128)(2,1)S(1)}, bf16[96,384]{1,0:T(8,128)(2,1)S(1)}, u32[]{:S(2)}, u32[]{:S(2)}) collective-permute-start(bf16[96,384]{1,0:T(8,128)(2,1)S(1)} %get-tuple-element.46), channel_id=1, source_target_pairs={{0,8},{4,12},{8,0},{12,4},{16,24},{20,28},{24,16},{28,20},{1,9},{5... | collective-permute-start | bytes 221192 | tf_op jit(solution)/shard_map/ppermute | solution.py:459
  34.7 5.2 %collective-permute-start.11 = (bf16[96,384]{1,0:T(8,128)(2,1)S(1)}, bf16[96,384]{1,0:T(8,128)(2,1)S(1)}, u32[]{:S(2)}, u32[]{:S(2)}) collective-permute-start(bf16[96,384]{1,0:T(8,128)(2,1)S(1)} %get-tuple-element.47), channel_id=1, source_target_pairs={{0,16},{4,20},{8,24},{12,28},{16,0},{20,4},{24,8},{28,12},{1,17},{... | collective-permute-start | bytes 221192 | tf_op jit(solution)/shard_map/ppermute | solution.py:459
  35.9 5.1 %collective-permute-start.12 = (bf16[96,384]{1,0:T(8,128)(2,1)S(1)}, bf16[96,384]{1,0:T(8,128)(2,1)S(1)}, u32[]{:S(2)}, u32[]{:S(2)}) collective-permute-start(bf16[96,384]{1,0:T(8,128)(2,1)S(1)} %get-tuple-element.48), channel_id=1, source_target_pairs={{0,12},{4,8},{8,4},{12,0},{16,28},{20,24},{24,20},{28,16},{1,13},{... | collective-permute-start | bytes 221192 | tf_op jit(solution)/shard_map/ppermute | solution.py:459
  35.9 5.2 %collective-permute-start.13 = (bf16[96,384]{1,0:T(8,128)(2,1)S(1)}, bf16[96,384]{1,0:T(8,128)(2,1)S(1)}, u32[]{:S(2)}, u32[]{:S(2)}) collective-permute-start(bf16[96,384]{1,0:T(8,128)(2,1)S(1)} %get-tuple-element.49), channel_id=1, source_target_pairs={{0,20},{4,16},{8,28},{12,24},{16,4},{20,0},{24,12},{28,8},{1,21},{... | collective-permute-start | bytes 221192 | tf_op jit(solution)/shard_map/ppermute | solution.py:459
  37.9 3.2 %collective-permute-start.14 = (bf16[96,384]{1,0:T(8,128)(2,1)S(1)}, bf16[96,384]{1,0:T(8,128)(2,1)S(1)}, u32[]{:S(2)}, u32[]{:S(2)}) collective-permute-start(bf16[96,384]{1,0:T(8,128)(2,1)S(1)} %get-tuple-element.50), channel_id=1, source_target_pairs={{0,4},{4,0},{8,12},{12,8},{16,20},{20,16},{24,28},{28,24},{1,5},{5... | collective-permute-start | bytes 221192 | tf_op jit(solution)/shard_map/ppermute | solution.py:459

commit v19 on v18

--- a/solution.py
+++ b/solution.py
@@ -17,7 +17,7 @@
 KEY_AT = SIZE - SPARE
 QUERY_AT = 2 * SIZE
 TEXT_ROWS = 16
-RUN = 16
+RUN = 5
 HIDDEN = -1e30
 ORDER = (6, 7, 2, 4, 3, 5, 1, 0)
 EARLY = (6, 7, 1, 0)
@@ -205,23 +205,17 @@
         wanted = jnp.logical_and(low <= image, image <= high)
         pairs += jnp.where(wanted, last - first + 1, 0)
 
-    def run(state, steps, ends):
-        for step in range(steps):
+    def run(_, state):
+        for step in range(len(work)):
             later = following(state)
-            if step < steps - 1 or not ends:
-                score(later, *work[(step + 1) % len(work)])
-            weigh(state, *work[step % len(work)])
+            score(later, *work[(step + 1) % len(work)])
+            weigh(state, *work[step])
             state = later
         return state
 
-    state = (jnp.int32(0), low)
-    score(state, *work[0])
-    limit = tiles + images - 1
-    if limit <= RUN:
-        run(state, limit, True)
-    else:
-        step = len(work) * max(1, RUN // (2 * len(work)))
-        lax.fori_loop(0, lax.div(pairs + step - 1, step), lambda _, state: run(state, step, False), state)
+    begun = (jnp.int32(0), low)
+    score(begun, *work[0])
+    lax.fori_loop(0, lax.div(pairs + len(work) - 1, len(work)), run, begun)
 
 
 def turned_keys(marked, block_ref):
@@ -584,7 +578,7 @@
             pltpu.VMEM((LANES, length), bf16),
             pltpu.VMEM((padded, length), f32),
         ]
-        + [pltpu.VMEM((window, tile), f32), pltpu.VMEM((1, tile), f32)] * 3
+        + [pltpu.VMEM((window, tile), f32), pltpu.VMEM((1, tile), f32)] * RUN
         + [pltpu.SMEM((images + 1,), jnp.int32)],
         in_vmem(len(operands)),
         4 * size * length * MAXP,

time: 43.5 us -> 43.1 us (level)
  no operation moved by 1% of the time
where the time goes in v19:
time: 43.1 us; the launch traced here: 42.9 us
  starting transfers between devices  17.6 us (41%)
  Pallas kernels  15.8 us (37%)
  waiting for transfers between devices  8.74 us (20%)
  between operations  0.69 us (2%)
    ppermute x15, starting transfers between devices, moved(): return lax.ppermute(value, axis, pairs)  17.6 us
    ppermute x15, waiting for transfers between devices, moved(): return lax.ppermute(value, axis, pairs)  8.74 us
    pallas_call x1, Pallas kernels, local(): call(functools.partial(attend_kernel, images, piggy, halo), (shape((padde...  7.26 us
    pallas_call x1, Pallas kernels, local(): call(functools.partial(far_kernel, images, piggy), (shape((depth, count),...  2.8 us
    pallas_call x1, Pallas kernels, local(): call(functools.partial(finish_kernel, images), (shape((count, depth), bf1...  2.13 us
    pallas_call x1, Pallas kernels, local(): call(functools.partial(near_kernel, piggy), (block,) * 6, [], in_vmem(3),...  1.95 us
    pallas_call x1, Pallas kernels, local(): call(functools.partial(prepare_kernel, images, halo), (shape((len(EARLY)...  1.64 us
  transfers between devices with their start and end apart: 15, of which 9 were waited for; matrix products, arithmetic and copies ran while one was open for 0% of the time, Pallas kernels for 8%

profile of v19, /device:TPU:0, one launch (start us, length us, event | category | flops | bytes accessed | tf_op | source)
XLA Modules:
  0.0 42.9 jit_solution(16286897022801700617)
XLA Ops:
  0.6 0.0 copy-start
  0.6 2.8 %shard_map.68 = (bf16[1152,384]{1,0:T(8,128)(2,1)S(1)}, f32[8,1152]{1,0:T(8,128)S(1)}, bf16[224,384]{1,0:T(8,128)(2,1)S(1)}, bf16[224,384]{1,0:T(8,128)(2,1)S(1)}) custom-call(s32[1,3072]{1,0:T(1,128)} %ids_ref.5, bf16[384,1152]{1,0:T(8,128)(2,1)} %bitcast.6, bf16[1728,1152]{1,0:T(8,128)(2,1)} %bitcast.4), custom_call_target="tpu_custom_call" | custom-call | flops 382205952 | bytes 8388608 | tf_op jit(solution)/shard_map/pallas_call | solution.py:504
  3.4 4.0 %collective-permute-start = (bf16[224,384]{1,0:T(8,128)(2,1)S(1)}, bf16[224,384]{1,0:T(8,128)(2,1)S(1)}, u32[]{:S(2)}, u32[]{:S(2)}) collective-permute-start(bf16[224,384]{1,0:T(8,128)(2,1)S(1)} %get-tuple-element.28), channel_id=1, source_target_pairs={{0,24},{4,28},{8,16},{12,20},{16,8},{20,12},{24,0},{28,4},{1,25},{... | collective-permute-start | bytes 516104 | tf_op jit(solution)/shard_map/ppermute | solution.py:453
  7.4 0.0 collective-permute-start.1
  7.4 0.0 copy-done
  7.4 0.0 copy-start.3
  7.4 0.0 copy-start.2
  7.4 1.9 %shard_map.69 = (bf16[224,384]{1,0:T(8,128)(2,1)S(1)}, bf16[224,384]{1,0:T(8,128)(2,1)S(1)}, bf16[224,384]{1,0:T(8,128)(2,1)S(1)}, bf16[224,384]{1,0:T(8,128)(2,...) custom-call(bf16[1152,384]{1,0:T(8,128)(2,1)S(1)} %get-tuple-element.30.normed_ref, ...), custom_call_target="tpu_custom_call" | custom-call | flops 1146617856 | bytes 8388608 | tf_op jit(solution)/shard_map/pallas_call | solution.py:518
  9.4 0.2 collective-permute-start.2
  9.6 1.9 %collective-permute-start.3 = (bf16[224,384]{1,0:T(8,128)(2,1)S(1)}, bf16[224,384]{1,0:T(8,128)(2,1)S(1)}, u32[]{:S(2)}, u32[]{:S(2)}) collective-permute-start(bf16[224,384]{1,0:T(8,128)(2,1)S(1)} %get-tuple-element.39), channel_id=1, source_target_pairs={{0,8},{4,12},{8,0},{12,4},{16,24},{20,28},{24,16},{28,20},{1,9},{5... | collective-permute-start | bytes 516104 | tf_op jit(solution)/shard_map/ppermute | solution.py:453
  11.5 1.5 %collective-permute-start.4 = (bf16[224,384]{1,0:T(8,128)(2,1)S(1)}, bf16[224,384]{1,0:T(8,128)(2,1)S(1)}, u32[]{:S(2)}, u32[]{:S(2)}) collective-permute-start(bf16[224,384]{1,0:T(8,128)(2,1)S(1)} %get-tuple-element.40), channel_id=1, source_target_pairs={{0,16},{4,20},{8,24},{12,28},{16,0},{20,4},{24,8},{28,12},{1,17},{... | collective-permute-start | bytes 516104 | tf_op jit(solution)/shard_map/ppermute | solution.py:453
  13.0 0.0 collective-permute-done.rest_0_
  13.0 0.0 collective-permute-start.5
  13.0 2.9 %collective-permute-done.1.rest_1_ = bf16[224,384]{1,0:T(8,128)(2,1)S(1)} collective-permute-done((bf16[224,384]{1,0:T(8,128)(2,1)S(1)}, bf16[224,384]{1,0:T(8,128)(2,1)S(1)}, u32[]{:S(2)}, u32[]{:S(2)}) %collective-permute-start.1) | collective-permute-done | bytes 172064 | tf_op jit(solution)/shard_map/ppermute | solution.py:453
  15.9 1.9 %collective-permute-start.6 = (bf16[224,384]{1,0:T(8,128)(2,1)S(1)}, bf16[224,384]{1,0:T(8,128)(2,1)S(1)}, u32[]{:S(2)}, u32[]{:S(2)}) collective-permute-start(bf16[224,384]{1,0:T(8,128)(2,1)S(1)} %get-tuple-element.42), channel_id=1, source_target_pairs={{0,20},{4,16},{8,28},{12,24},{16,4},{20,0},{24,12},{28,8},{1,21},{... | collective-permute-start | bytes 516104 | tf_op jit(solution)/shard_map/ppermute | solution.py:453
  17.8 0.0 collective-permute-done.2.rest_2_
  17.8 0.0 copy-done.3
  17.8 1.6 %collective-permute-start.7 = (bf16[4,1152]{1,0:T(4,128)(2,1)S(1)}, bf16[4,1152]{1,0:T(4,128)(2,1)S(1)}, u32[]{:S(2)}, u32[]{:S(2)}) collective-permute-start(bf16[4,1152]{1,0:T(4,128)(2,1)S(1)} %copy-done.3), channel_id=1, source_target_pairs={{1,0},{0,1},{3,2},{2,3},{6,4},{7,5},{4,6},{5,7},{11,8},{10,9},{9,1... | collective-permute-start | bytes 27656 | tf_op jit(solution)/shard_map/ppermute | solution.py:453
  19.3 0.0 copy-done.2
  19.3 1.6 %shard_map.70 = (bf16[1536,128]{1,0:T(8,128)(2,1)S(1)}, f32[2,8,3072]{2,1,0:T(8,128)S(1)}, s32[8,128]{1,0:T(8,128)S(1)}, bf16[640,1152]{1,0:T(8,128)(2,1)S(1)}) custom-call(s32[1,3072]{1,0:T(1,128)S(1)} %copy-done.2, bf16[576,1152]{1,0:T(8,128)(2,1)} %out_weight_ref.1, bf16[224,384]{1,0:T(8,128)(2,1)S(1)} %collective-permute-done.rest_0_, ...), custom_call_target="tpu_custom_call" | custom-call | flops 1073741824 | bytes 8388608 | tf_op jit(solution)/shard_map/pallas_call | solution.py:559
  21.0 0.4 %collective-permute-done.7.rest_8_ = bf16[4,1152]{1,0:T(4,128)(2,1)S(1)} collective-permute-done((bf16[4,1152]{1,0:T(4,128)(2,1)S(1)}, bf16[4,1152]{1,0:T(4,128)(2,1)S(1)}, u32[]{:S(2)}, u32[]{:S(2)}) %collective-permute-start.7) | collective-permute-done | bytes 9248 | tf_op jit(solution)/shard_map/ppermute | solution.py:453
  21.4 0.0 collective-permute-done.3.rest_4_
  21.4 0.0 collective-permute-done.4.rest_5_
  21.4 0.7 %collective-permute-done.5.rest_6_ = bf16[224,384]{1,0:T(8,128)(2,1)S(1)} collective-permute-done((bf16[224,384]{1,0:T(8,128)(2,1)S(1)}, bf16[224,384]{1,0:T(8,128)(2,1)S(1)}, u32[]{:S(2)}, u32[]{:S(2)}) %collective-permute-start.5) | collective-permute-done | bytes 172064 | tf_op jit(solution)/shard_map/ppermute | solution.py:453
  22.1 0.6 %collective-permute-done.6.rest_7_ = bf16[224,384]{1,0:T(8,128)(2,1)S(1)} collective-permute-done((bf16[224,384]{1,0:T(8,128)(2,1)S(1)}, bf16[224,384]{1,0:T(8,128)(2,1)S(1)}, u32[]{:S(2)}, u32[]{:S(2)}) %collective-permute-start.6) | collective-permute-done | bytes 172064 | tf_op jit(solution)/shard_map/ppermute | solution.py:453
  22.7 0.0 copy-start.1
  22.7 7.3 %shard_map.71 = (bf16[96,384]{1,0:T(8,128)(2,1)S(1)}, bf16[96,384]{1,0:T(8,128)(2,1)S(1)}, bf16[96,384]{1,0:T(8,128)(2,1)S(1)}, bf16[96,384]{1,0:T(8,128)(2,1)S(...) custom-call(s32[1,3072]{1,0:T(1,128)S(1)} %copy-done.2, ...), custom_call_target="tpu_custom_call" | custom-call | flops 905969664 | bytes 8388608 | tf_op jit(solution)/shard_map/pallas_call | solution.py:572
  30.0 2.3 %collective-permute-start.8 = (bf16[96,384]{1,0:T(8,128)(2,1)S(1)}, bf16[96,384]{1,0:T(8,128)(2,1)S(1)}, u32[]{:S(2)}, u32[]{:S(2)}) collective-permute-start(bf16[96,384]{1,0:T(8,128)(2,1)S(1)} %get-tuple-element.44), channel_id=1, source_target_pairs={{0,24},{4,28},{8,16},{12,20},{16,8},{20,12},{24,0},{28,4},{1,25},{... | collective-permute-start | bytes 221192 | tf_op jit(solution)/shard_map/ppermute | solution.py:453
  32.3 0.2 collective-permute-start.9
  32.5 1.8 %collective-permute-start.10 = (bf16[96,384]{1,0:T(8,128)(2,1)S(1)}, bf16[96,384]{1,0:T(8,128)(2,1)S(1)}, u32[]{:S(2)}, u32[]{:S(2)}) collective-permute-start(bf16[96,384]{1,0:T(8,128)(2,1)S(1)} %get-tuple-element.46), channel_id=1, source_target_pairs={{0,8},{4,12},{8,0},{12,4},{16,24},{20,28},{24,16},{28,20},{1,9},{5... | collective-permute-start | bytes 221192 | tf_op jit(solution)/shard_map/ppermute | solution.py:453
  34.3 1.2 %collective-permute-start.11 = (bf16[96,384]{1,0:T(8,128)(2,1)S(1)}, bf16[96,384]{1,0:T(8,128)(2,1)S(1)}, u32[]{:S(2)}, u32[]{:S(2)}) collective-permute-start(bf16[96,384]{1,0:T(8,128)(2,1)S(1)} %get-tuple-element.47), channel_id=1, source_target_pairs={{0,16},{4,20},{8,24},{12,28},{16,0},{20,4},{24,8},{28,12},{1,17},{... | collective-permute-start | bytes 221192 | tf_op jit(solution)/shard_map/ppermute | solution.py:453
  35.4 0.0 collective-permute-start.12
  35.5 0.0 collective-permute-done.8.rest_0_
  35.5 0.8 %collective-permute-start.13 = (bf16[96,384]{1,0:T(8,128)(2,1)S(1)}, bf16[96,384]{1,0:T(8,128)(2,1)S(1)}, u32[]{:S(2)}, u32[]{:S(2)}) collective-permute-start(bf16[96,384]{1,0:T(8,128)(2,1)S(1)} %get-tuple-element.49), channel_id=1, source_target_pairs={{0,20},{4,16},{8,28},{12,24},{16,4},{20,0},{24,12},{28,8},{1,21},{... | collective-permute-start | bytes 221192 | tf_op jit(solution)/shard_map/ppermute | solution.py:453
  36.3 1.2 %collective-permute-done.9.rest_1_ = bf16[96,384]{1,0:T(8,128)(2,1)S(1)} collective-permute-done((bf16[96,384]{1,0:T(8,128)(2,1)S(1)}, bf16[96,384]{1,0:T(8,128)(2,1)S(1)}, u32[]{:S(2)}, u32[]{:S(2)}) %collective-permute-start.9) | collective-permute-done | bytes 73760 | tf_op jit(solution)/shard_map/ppermute | solution.py:453
  37.5 0.3 collective-permute-start.14
  37.8 1.0 %collective-permute-done.10.rest_2_ = bf16[96,384]{1,0:T(8,128)(2,1)S(1)} collective-permute-done((bf16[96,384]{1,0:T(8,128)(2,1)S(1)}, bf16[96,384]{1,0:T(8,128)(2,1)S(1)}, u32[]{:S(2)}, u32[]{:S(2)}) %collective-permute-start.10) | collective-permute-done | bytes 73760 | tf_op jit(solution)/shard_map/ppermute | solution.py:453
  38.8 0.7 %collective-permute-done.11.rest_3_ = bf16[96,384]{1,0:T(8,128)(2,1)S(1)} collective-permute-done((bf16[96,384]{1,0:T(8,128)(2,1)S(1)}, bf16[96,384]{1,0:T(8,128)(2,1)S(1)}, u32[]{:S(2)}, u32[]{:S(2)}) %collective-permute-start.11) | collective-permute-done | bytes 73760 | tf_op jit(solution)/shard_map/ppermute | solution.py:453
  39.5 1.1 %collective-permute-done.12.rest_4_ = bf16[96,384]{1,0:T(8,128)(2,1)S(1)} collective-permute-done((bf16[96,384]{1,0:T(8,128)(2,1)S(1)}, bf16[96,384]{1,0:T(8,128)(2,1)S(1)}, u32[]{:S(2)}, u32[]{:S(2)}) %collective-permute-start.12) | collective-permute-done | bytes 73760 | tf_op jit(solution)/shard_map/ppermute | solution.py:453
  40.6 0.2 collective-permute-done.13.rest_5_
  40.7 0.0 collective-permute-done.14.rest_6_
  40.7 0.0 copy-done.1
  40.7 2.1 %shard_map.72 = (bf16[384,1152]{1,0:T(8,128)(2,1)}, f32[1,4]{1,0:T(1,128)}) custom-call(bf16[384,1152]{1,0:T(8,128)(2,1)S(1)} %bitcast.7, bf16[640,1152]{1,0:T(8,128)(2,1)S(1)} %get-tuple-element.35.weight_ref, bf16[4,1152]{1,0:T(4,128)(2,1)S(1)} %copy-done.3, bf16[96,384]{1,0:T(8,128)(2,1)S(1)} %collective-permute-done.8.rest_0_, ...), custom_call_target="tpu_custom_call" | custom-call | flops 509607936 | bytes 8388608 | tf_op jit(solution)/shard_map/pallas_call | solution.py:597
Async XLA Ops:
  0.6 6.8 %copy-start = (bf16[1152,1728]{0,1:T(8,128)(2,1)S(1)}, bf16[1152,1728]{0,1:T(8,128)(2,1)}, u32[]{:S(2)}) copy-start(bf16[1152,1728]{0,1:T(8,128)(2,1)} %param.7) | copy-start | bytes 11943940
  3.4 9.6 %collective-permute-start = (bf16[224,384]{1,0:T(8,128)(2,1)S(1)}, bf16[224,384]{1,0:T(8,128)(2,1)S(1)}, u32[]{:S(2)}, u32[]{:S(2)}) collective-permute-start(bf16[224,384]{1,0:T(8,128)(2,1)S(1)} %get-tuple-element.28), channel_id=1, source_target_pairs={{0,24},{4,28},{8,16},{12,20},{16,8},{20,12},{24,0},{28,4},{1,25},{... | collective-permute-start | bytes 516104 | tf_op jit(solution)/shard_map/ppermute | solution.py:453
  7.4 8.5 %collective-permute-start.1 = (bf16[224,384]{1,0:T(8,128)(2,1)S(1)}, bf16[224,384]{1,0:T(8,128)(2,1)S(1)}, u32[]{:S(2)}, u32[]{:S(2)}) collective-permute-start(bf16[224,384]{1,0:T(8,128)(2,1)S(1)} %get-tuple-element.29), channel_id=1, source_target_pairs={{0,28},{4,24},{8,20},{12,16},{16,12},{20,8},{24,4},{28,0},{1,29},{... | collective-permute-start | bytes 516104 | tf_op jit(solution)/shard_map/ppermute | solution.py:453
  7.4 10.4 %copy-start.3 = (bf16[4,1152]{1,0:T(4,128)(2,1)S(1)}, bf16[4,1152]{1,0:T(4,128)(2,1)}, u32[]{:S(2)}) copy-start(bf16[4,1152]{1,0:T(4,128)(2,1)} %text_ref.1) | copy-start | bytes 27652
  7.4 11.9 %copy-start.2 = (s32[1,3072]{1,0:T(1,128)S(1)}, s32[1,3072]{1,0:T(1,128)}, u32[]{:S(2)}) copy-start(s32[1,3072]{1,0:T(1,128)} %ids_ref.5) | copy-start | bytes 36868
  9.4 8.4 %collective-permute-start.2 = (bf16[224,384]{1,0:T(8,128)(2,1)S(1)}, bf16[224,384]{1,0:T(8,128)(2,1)S(1)}, u32[]{:S(2)}, u32[]{:S(2)}) collective-permute-start(bf16[224,384]{1,0:T(8,128)(2,1)S(1)} %get-tuple-element.32), channel_id=1, source_target_pairs={{0,4},{4,0},{8,12},{12,8},{16,20},{20,16},{24,28},{28,24},{1,5},{5... | collective-permute-start | bytes 516104 | tf_op jit(solution)/shard_map/ppermute | solution.py:453
  9.6 11.8 %collective-permute-start.3 = (bf16[224,384]{1,0:T(8,128)(2,1)S(1)}, bf16[224,384]{1,0:T(8,128)(2,1)S(1)}, u32[]{:S(2)}, u32[]{:S(2)}) collective-permute-start(bf16[224,384]{1,0:T(8,128)(2,1)S(1)} %get-tuple-element.39), channel_id=1, source_target_pairs={{0,8},{4,12},{8,0},{12,4},{16,24},{20,28},{24,16},{28,20},{1,9},{5... | collective-permute-start | bytes 516104 | tf_op jit(solution)/shard_map/ppermute | solution.py:453
  11.5 9.9 %collective-permute-start.4 = (bf16[224,384]{1,0:T(8,128)(2,1)S(1)}, bf16[224,384]{1,0:T(8,128)(2,1)S(1)}, u32[]{:S(2)}, u32[]{:S(2)}) collective-permute-start(bf16[224,384]{1,0:T(8,128)(2,1)S(1)} %get-tuple-element.40), channel_id=1, source_target_pairs={{0,16},{4,20},{8,24},{12,28},{16,0},{20,4},{24,8},{28,12},{1,17},{... | collective-permute-start | bytes 516104 | tf_op jit(solution)/shard_map/ppermute | solution.py:453
  13.0 9.1 %collective-permute-start.5 = (bf16[224,384]{1,0:T(8,128)(2,1)S(1)}, bf16[224,384]{1,0:T(8,128)(2,1)S(1)}, u32[]{:S(2)}, u32[]{:S(2)}) collective-permute-start(bf16[224,384]{1,0:T(8,128)(2,1)S(1)} %get-tuple-element.41), channel_id=1, source_target_pairs={{0,12},{4,8},{8,4},{12,0},{16,28},{20,24},{24,20},{28,16},{1,13},{... | collective-permute-start | bytes 516104 | tf_op jit(solution)/shard_map/ppermute | solution.py:453
  15.9 6.9 %collective-permute-start.6 = (bf16[224,384]{1,0:T(8,128)(2,1)S(1)}, bf16[224,384]{1,0:T(8,128)(2,1)S(1)}, u32[]{:S(2)}, u32[]{:S(2)}) collective-permute-start(bf16[224,384]{1,0:T(8,128)(2,1)S(1)} %get-tuple-element.42), channel_id=1, source_target_pairs={{0,20},{4,16},{8,28},{12,24},{16,4},{20,0},{24,12},{28,8},{1,21},{... | collective-permute-start | bytes 516104 | tf_op jit(solution)/shard_map/ppermute | solution.py:453
  17.8 3.7 %collective-permute-start.7 = (bf16[4,1152]{1,0:T(4,128)(2,1)S(1)}, bf16[4,1152]{1,0:T(4,128)(2,1)S(1)}, u32[]{:S(2)}, u32[]{:S(2)}) collective-permute-start(bf16[4,1152]{1,0:T(4,128)(2,1)S(1)} %copy-done.3), channel_id=1, source_target_pairs={{1,0},{0,1},{3,2},{2,3},{6,4},{7,5},{4,6},{5,7},{11,8},{10,9},{9,1... | collective-permute-start | bytes 27656 | tf_op jit(solution)/shard_map/ppermute | solution.py:453
  22.7 18.0 %copy-start.1 = (bf16[1,384,1152]{2,1,0:T(8,128)(2,1)S(1)}, bf16[1,384,1152]{2,1,0:T(8,128)(2,1)}, u32[]{:S(2)}) copy-start(bf16[1,384,1152]{2,1,0:T(8,128)(2,1)} %param.5) | copy-start | bytes 2654212
  30.0 5.5 %collective-permute-start.8 = (bf16[96,384]{1,0:T(8,128)(2,1)S(1)}, bf16[96,384]{1,0:T(8,128)(2,1)S(1)}, u32[]{:S(2)}, u32[]{:S(2)}) collective-permute-start(bf16[96,384]{1,0:T(8,128)(2,1)S(1)} %get-tuple-element.44), channel_id=1, source_target_pairs={{0,24},{4,28},{8,16},{12,20},{16,8},{20,12},{24,0},{28,4},{1,25},{... | collective-permute-start | bytes 221192 | tf_op jit(solution)/shard_map/ppermute | solution.py:453
  32.3 5.2 %collective-permute-start.9 = (bf16[96,384]{1,0:T(8,128)(2,1)S(1)}, bf16[96,384]{1,0:T(8,128)(2,1)S(1)}, u32[]{:S(2)}, u32[]{:S(2)}) collective-permute-start(bf16[96,384]{1,0:T(8,128)(2,1)S(1)} %get-tuple-element.45), channel_id=1, source_target_pairs={{0,28},{4,24},{8,20},{12,16},{16,12},{20,8},{24,4},{28,0},{1,29},{... | collective-permute-start | bytes 221192 | tf_op jit(solution)/shard_map/ppermute | solution.py:453
  32.5 6.3 %collective-permute-start.10 = (bf16[96,384]{1,0:T(8,128)(2,1)S(1)}, bf16[96,384]{1,0:T(8,128)(2,1)S(1)}, u32[]{:S(2)}, u32[]{:S(2)}) collective-permute-start(bf16[96,384]{1,0:T(8,128)(2,1)S(1)} %get-tuple-element.46), channel_id=1, source_target_pairs={{0,8},{4,12},{8,0},{12,4},{16,24},{20,28},{24,16},{28,20},{1,9},{5... | collective-permute-start | bytes 221192 | tf_op jit(solution)/shard_map/ppermute | solution.py:453
  34.3 5.2 %collective-permute-start.11 = (bf16[96,384]{1,0:T(8,128)(2,1)S(1)}, bf16[96,384]{1,0:T(8,128)(2,1)S(1)}, u32[]{:S(2)}, u32[]{:S(2)}) collective-permute-start(bf16[96,384]{1,0:T(8,128)(2,1)S(1)} %get-tuple-element.47), channel_id=1, source_target_pairs={{0,16},{4,20},{8,24},{12,28},{16,0},{20,4},{24,8},{28,12},{1,17},{... | collective-permute-start | bytes 221192 | tf_op jit(solution)/shard_map/ppermute | solution.py:453
  35.4 5.1 %collective-permute-start.12 = (bf16[96,384]{1,0:T(8,128)(2,1)S(1)}, bf16[96,384]{1,0:T(8,128)(2,1)S(1)}, u32[]{:S(2)}, u32[]{:S(2)}) collective-permute-start(bf16[96,384]{1,0:T(8,128)(2,1)S(1)} %get-tuple-element.48), channel_id=1, source_target_pairs={{0,12},{4,8},{8,4},{12,0},{16,28},{20,24},{24,20},{28,16},{1,13},{... | collective-permute-start | bytes 221192 | tf_op jit(solution)/shard_map/ppermute | solution.py:453
  35.5 5.2 %collective-permute-start.13 = (bf16[96,384]{1,0:T(8,128)(2,1)S(1)}, bf16[96,384]{1,0:T(8,128)(2,1)S(1)}, u32[]{:S(2)}, u32[]{:S(2)}) collective-permute-start(bf16[96,384]{1,0:T(8,128)(2,1)S(1)} %get-tuple-element.49), channel_id=1, source_target_pairs={{0,20},{4,16},{8,28},{12,24},{16,4},{20,0},{24,12},{28,8},{1,21},{... | collective-permute-start | bytes 221192 | tf_op jit(solution)/shard_map/ppermute | solution.py:453
  37.5 3.2 %collective-permute-start.14 = (bf16[96,384]{1,0:T(8,128)(2,1)S(1)}, bf16[96,384]{1,0:T(8,128)(2,1)S(1)}, u32[]{:S(2)}, u32[]{:S(2)}) collective-permute-start(bf16[96,384]{1,0:T(8,128)(2,1)S(1)} %get-tuple-element.50), channel_id=1, source_target_pairs={{0,4},{4,0},{8,12},{12,8},{16,20},{20,16},{24,28},{28,24},{1,5},{5... | collective-permute-start | bytes 221192 | tf_op jit(solution)/shard_map/ppermute | solution.py:453

commit v20 on v19

--- a/solution.py
+++ b/solution.py
@@ -17,7 +17,7 @@
 KEY_AT = SIZE - SPARE
 QUERY_AT = 2 * SIZE
 TEXT_ROWS = 16
-RUN = 5
+RUN = 8
 HIDDEN = -1e30
 ORDER = (6, 7, 2, 4, 3, 5, 1, 0)
 EARLY = (6, 7, 1, 0)
@@ -206,16 +206,16 @@
         pairs += jnp.where(wanted, last - first + 1, 0)
 
     def run(_, state):
-        for step in range(len(work)):
+        for step in range(RUN):
             later = following(state)
-            score(later, *work[(step + 1) % len(work)])
-            weigh(state, *work[step])
+            score(later, *work[(step + 1) % 2])
+            weigh(state, *work[step % 2])
             state = later
         return state
 
     begun = (jnp.int32(0), low)
     score(begun, *work[0])
-    lax.fori_loop(0, lax.div(pairs + len(work) - 1, len(work)), run, begun)
+    lax.fori_loop(0, lax.div(pairs + RUN - 1, RUN), run, begun)
 
 
 def turned_keys(marked, block_ref):
@@ -578,7 +578,7 @@
             pltpu.VMEM((LANES, length), bf16),
             pltpu.VMEM((padded, length), f32),
         ]
-        + [pltpu.VMEM((window, tile), f32), pltpu.VMEM((1, tile), f32)] * RUN
+        + [pltpu.VMEM((window, tile), f32), pltpu.VMEM((1, tile), f32)] * 2
         + [pltpu.SMEM((images + 1,), jnp.int32)],
         in_vmem(len(operands)),
         4 * size * length * MAXP,

time: 43.1 us -> 43.3 us (level)
  no operation moved by 1% of the time
where the time goes in v20:
time: 43.3 us; the launch traced here: 43.2 us
  starting transfers between devices  17.6 us (41%)
  Pallas kernels  16.1 us (37%)
  waiting for transfers between devices  8.8 us (20%)
  between operations  0.69 us (2%)
    ppermute x15, starting transfers between devices, moved(): return lax.ppermute(value, axis, pairs)  17.6 us
    ppermute x15, waiting for transfers between devices, moved(): return lax.ppermute(value, axis, pairs)  8.8 us
    pallas_call x1, Pallas kernels, local(): call(functools.partial(attend_kernel, images, piggy, halo), (shape((padde...  7.54 us
    pallas_call x1, Pallas kernels, local(): call(functools.partial(far_kernel, images, piggy), (shape((depth, count),...  2.8 us
    pallas_call x1, Pallas kernels, local(): call(functools.partial(finish_kernel, images), (shape((count, depth), bf1...  2.13 us
    pallas_call x1, Pallas kernels, local(): call(functools.partial(near_kernel, piggy), (block,) * 6, [], in_vmem(3),...  1.95 us
    pallas_call x1, Pallas kernels, local(): call(functools.partial(prepare_kernel, images, halo), (shape((len(EARLY)...  1.64 us
  transfers between devices with their start and end apart: 15, of which 9 were waited for; matrix products, arithmetic and copies ran while one was open for 0% of the time, Pallas kernels for 8%

profile of v20, /device:TPU:0, one launch (start us, length us, event | category | flops | bytes accessed | tf_op | source)
XLA Modules:
  0.0 43.2 jit_solution(9165571208025831351)
XLA Ops:
  0.6 0.0 copy-start
  0.6 2.8 %shard_map.68 = (bf16[1152,384]{1,0:T(8,128)(2,1)S(1)}, f32[8,1152]{1,0:T(8,128)S(1)}, bf16[224,384]{1,0:T(8,128)(2,1)S(1)}, bf16[224,384]{1,0:T(8,128)(2,1)S(1)}) custom-call(s32[1,3072]{1,0:T(1,128)} %ids_ref.5, bf16[384,1152]{1,0:T(8,128)(2,1)} %bitcast.6, bf16[1728,1152]{1,0:T(8,128)(2,1)} %bitcast.4), custom_call_target="tpu_custom_call" | custom-call | flops 382205952 | bytes 8388608 | tf_op jit(solution)/shard_map/pallas_call | solution.py:504
  3.4 4.0 %collective-permute-start = (bf16[224,384]{1,0:T(8,128)(2,1)S(1)}, bf16[224,384]{1,0:T(8,128)(2,1)S(1)}, u32[]{:S(2)}, u32[]{:S(2)}) collective-permute-start(bf16[224,384]{1,0:T(8,128)(2,1)S(1)} %get-tuple-element.28), channel_id=1, source_target_pairs={{0,24},{4,28},{8,16},{12,20},{16,8},{20,12},{24,0},{28,4},{1,25},{... | collective-permute-start | bytes 516104 | tf_op jit(solution)/shard_map/ppermute | solution.py:453
  7.4 0.0 collective-permute-start.1
  7.4 0.0 copy-done
  7.4 0.0 copy-start.3
  7.4 0.0 copy-start.2
  7.4 1.9 %shard_map.69 = (bf16[224,384]{1,0:T(8,128)(2,1)S(1)}, bf16[224,384]{1,0:T(8,128)(2,1)S(1)}, bf16[224,384]{1,0:T(8,128)(2,1)S(1)}, bf16[224,384]{1,0:T(8,128)(2,...) custom-call(bf16[1152,384]{1,0:T(8,128)(2,1)S(1)} %get-tuple-element.30.normed_ref, ...), custom_call_target="tpu_custom_call" | custom-call | flops 1146617856 | bytes 8388608 | tf_op jit(solution)/shard_map/pallas_call | solution.py:518
  9.4 0.2 collective-permute-start.2
  9.6 1.9 %collective-permute-start.3 = (bf16[224,384]{1,0:T(8,128)(2,1)S(1)}, bf16[224,384]{1,0:T(8,128)(2,1)S(1)}, u32[]{:S(2)}, u32[]{:S(2)}) collective-permute-start(bf16[224,384]{1,0:T(8,128)(2,1)S(1)} %get-tuple-element.39), channel_id=1, source_target_pairs={{0,8},{4,12},{8,0},{12,4},{16,24},{20,28},{24,16},{28,20},{1,9},{5... | collective-permute-start | bytes 516104 | tf_op jit(solution)/shard_map/ppermute | solution.py:453
  11.5 1.5 %collective-permute-start.4 = (bf16[224,384]{1,0:T(8,128)(2,1)S(1)}, bf16[224,384]{1,0:T(8,128)(2,1)S(1)}, u32[]{:S(2)}, u32[]{:S(2)}) collective-permute-start(bf16[224,384]{1,0:T(8,128)(2,1)S(1)} %get-tuple-element.40), channel_id=1, source_target_pairs={{0,16},{4,20},{8,24},{12,28},{16,0},{20,4},{24,8},{28,12},{1,17},{... | collective-permute-start | bytes 516104 | tf_op jit(solution)/shard_map/ppermute | solution.py:453
  13.0 0.0 collective-permute-done.rest_0_
  13.0 0.0 collective-permute-start.5
  13.0 2.9 %collective-permute-done.1.rest_1_ = bf16[224,384]{1,0:T(8,128)(2,1)S(1)} collective-permute-done((bf16[224,384]{1,0:T(8,128)(2,1)S(1)}, bf16[224,384]{1,0:T(8,128)(2,1)S(1)}, u32[]{:S(2)}, u32[]{:S(2)}) %collective-permute-start.1) | collective-permute-done | bytes 172064 | tf_op jit(solution)/shard_map/ppermute | solution.py:453
  15.9 1.9 %collective-permute-start.6 = (bf16[224,384]{1,0:T(8,128)(2,1)S(1)}, bf16[224,384]{1,0:T(8,128)(2,1)S(1)}, u32[]{:S(2)}, u32[]{:S(2)}) collective-permute-start(bf16[224,384]{1,0:T(8,128)(2,1)S(1)} %get-tuple-element.42), channel_id=1, source_target_pairs={{0,20},{4,16},{8,28},{12,24},{16,4},{20,0},{24,12},{28,8},{1,21},{... | collective-permute-start | bytes 516104 | tf_op jit(solution)/shard_map/ppermute | solution.py:453
  17.8 0.0 collective-permute-done.2.rest_2_
  17.8 0.0 copy-done.3
  17.8 1.6 %collective-permute-start.7 = (bf16[4,1152]{1,0:T(4,128)(2,1)S(1)}, bf16[4,1152]{1,0:T(4,128)(2,1)S(1)}, u32[]{:S(2)}, u32[]{:S(2)}) collective-permute-start(bf16[4,1152]{1,0:T(4,128)(2,1)S(1)} %copy-done.3), channel_id=1, source_target_pairs={{1,0},{0,1},{3,2},{2,3},{6,4},{7,5},{4,6},{5,7},{11,8},{10,9},{9,1... | collective-permute-start | bytes 27656 | tf_op jit(solution)/shard_map/ppermute | solution.py:453
  19.3 0.0 copy-done.2
  19.3 1.6 %shard_map.70 = (bf16[1536,128]{1,0:T(8,128)(2,1)S(1)}, f32[2,8,3072]{2,1,0:T(8,128)S(1)}, s32[8,128]{1,0:T(8,128)S(1)}, bf16[640,1152]{1,0:T(8,128)(2,1)S(1)}) custom-call(s32[1,3072]{1,0:T(1,128)S(1)} %copy-done.2, bf16[576,1152]{1,0:T(8,128)(2,1)} %out_weight_ref.1, bf16[224,384]{1,0:T(8,128)(2,1)S(1)} %collective-permute-done.rest_0_, ...), custom_call_target="tpu_custom_call" | custom-call | flops 1073741824 | bytes 8388608 | tf_op jit(solution)/shard_map/pallas_call | solution.py:559
  21.0 0.4 %collective-permute-done.7.rest_8_ = bf16[4,1152]{1,0:T(4,128)(2,1)S(1)} collective-permute-done((bf16[4,1152]{1,0:T(4,128)(2,1)S(1)}, bf16[4,1152]{1,0:T(4,128)(2,1)S(1)}, u32[]{:S(2)}, u32[]{:S(2)}) %collective-permute-start.7) | collective-permute-done | bytes 9248 | tf_op jit(solution)/shard_map/ppermute | solution.py:453
  21.4 0.0 collective-permute-done.3.rest_4_
  21.4 0.0 collective-permute-done.4.rest_5_
  21.4 0.7 %collective-permute-done.5.rest_6_ = bf16[224,384]{1,0:T(8,128)(2,1)S(1)} collective-permute-done((bf16[224,384]{1,0:T(8,128)(2,1)S(1)}, bf16[224,384]{1,0:T(8,128)(2,1)S(1)}, u32[]{:S(2)}, u32[]{:S(2)}) %collective-permute-start.5) | collective-permute-done | bytes 172064 | tf_op jit(solution)/shard_map/ppermute | solution.py:453
  22.1 0.6 %collective-permute-done.6.rest_7_ = bf16[224,384]{1,0:T(8,128)(2,1)S(1)} collective-permute-done((bf16[224,384]{1,0:T(8,128)(2,1)S(1)}, bf16[224,384]{1,0:T(8,128)(2,1)S(1)}, u32[]{:S(2)}, u32[]{:S(2)}) %collective-permute-start.6) | collective-permute-done | bytes 172064 | tf_op jit(solution)/shard_map/ppermute | solution.py:453
  22.7 0.0 copy-start.1
  22.7 7.5 %shard_map.71 = (bf16[96,384]{1,0:T(8,128)(2,1)S(1)}, bf16[96,384]{1,0:T(8,128)(2,1)S(1)}, bf16[96,384]{1,0:T(8,128)(2,1)S(1)}, bf16[96,384]{1,0:T(8,128)(2,1)S(...) custom-call(s32[1,3072]{1,0:T(1,128)S(1)} %copy-done.2, ...), custom_call_target="tpu_custom_call" | custom-call | flops 905969664 | bytes 8388608 | tf_op jit(solution)/shard_map/pallas_call | solution.py:572
  30.3 2.3 %collective-permute-start.8 = (bf16[96,384]{1,0:T(8,128)(2,1)S(1)}, bf16[96,384]{1,0:T(8,128)(2,1)S(1)}, u32[]{:S(2)}, u32[]{:S(2)}) collective-permute-start(bf16[96,384]{1,0:T(8,128)(2,1)S(1)} %get-tuple-element.44), channel_id=1, source_target_pairs={{0,24},{4,28},{8,16},{12,20},{16,8},{20,12},{24,0},{28,4},{1,25},{... | collective-permute-start | bytes 221192 | tf_op jit(solution)/shard_map/ppermute | solution.py:453
  32.6 0.2 collective-permute-start.9
  32.8 1.8 %collective-permute-start.10 = (bf16[96,384]{1,0:T(8,128)(2,1)S(1)}, bf16[96,384]{1,0:T(8,128)(2,1)S(1)}, u32[]{:S(2)}, u32[]{:S(2)}) collective-permute-start(bf16[96,384]{1,0:T(8,128)(2,1)S(1)} %get-tuple-element.46), channel_id=1, source_target_pairs={{0,8},{4,12},{8,0},{12,4},{16,24},{20,28},{24,16},{28,20},{1,9},{5... | collective-permute-start | bytes 221192 | tf_op jit(solution)/shard_map/ppermute | solution.py:453
  34.6 1.1 %collective-permute-start.11 = (bf16[96,384]{1,0:T(8,128)(2,1)S(1)}, bf16[96,384]{1,0:T(8,128)(2,1)S(1)}, u32[]{:S(2)}, u32[]{:S(2)}) collective-permute-start(bf16[96,384]{1,0:T(8,128)(2,1)S(1)} %get-tuple-element.47), channel_id=1, source_target_pairs={{0,16},{4,20},{8,24},{12,28},{16,0},{20,4},{24,8},{28,12},{1,17},{... | collective-permute-start | bytes 221192 | tf_op jit(solution)/shard_map/ppermute | solution.py:453
  35.7 0.1 collective-permute-start.12
  35.8 0.0 collective-permute-done.8.rest_0_
  35.8 0.8 %collective-permute-start.13 = (bf16[96,384]{1,0:T(8,128)(2,1)S(1)}, bf16[96,384]{1,0:T(8,128)(2,1)S(1)}, u32[]{:S(2)}, u32[]{:S(2)}) collective-permute-start(bf16[96,384]{1,0:T(8,128)(2,1)S(1)} %get-tuple-element.49), channel_id=1, source_target_pairs={{0,20},{4,16},{8,28},{12,24},{16,4},{20,0},{24,12},{28,8},{1,21},{... | collective-permute-start | bytes 221192 | tf_op jit(solution)/shard_map/ppermute | solution.py:453
  36.6 1.2 %collective-permute-done.9.rest_1_ = bf16[96,384]{1,0:T(8,128)(2,1)S(1)} collective-permute-done((bf16[96,384]{1,0:T(8,128)(2,1)S(1)}, bf16[96,384]{1,0:T(8,128)(2,1)S(1)}, u32[]{:S(2)}, u32[]{:S(2)}) %collective-permute-start.9) | collective-permute-done | bytes 73760 | tf_op jit(solution)/shard_map/ppermute | solution.py:453
  37.8 0.3 collective-permute-start.14
  38.1 1.0 %collective-permute-done.10.rest_2_ = bf16[96,384]{1,0:T(8,128)(2,1)S(1)} collective-permute-done((bf16[96,384]{1,0:T(8,128)(2,1)S(1)}, bf16[96,384]{1,0:T(8,128)(2,1)S(1)}, u32[]{:S(2)}, u32[]{:S(2)}) %collective-permute-start.10) | collective-permute-done | bytes 73760 | tf_op jit(solution)/shard_map/ppermute | solution.py:453
  39.1 0.7 %collective-permute-done.11.rest_3_ = bf16[96,384]{1,0:T(8,128)(2,1)S(1)} collective-permute-done((bf16[96,384]{1,0:T(8,128)(2,1)S(1)}, bf16[96,384]{1,0:T(8,128)(2,1)S(1)}, u32[]{:S(2)}, u32[]{:S(2)}) %collective-permute-start.11) | collective-permute-done | bytes 73760 | tf_op jit(solution)/shard_map/ppermute | solution.py:453
  39.8 1.1 %collective-permute-done.12.rest_4_ = bf16[96,384]{1,0:T(8,128)(2,1)S(1)} collective-permute-done((bf16[96,384]{1,0:T(8,128)(2,1)S(1)}, bf16[96,384]{1,0:T(8,128)(2,1)S(1)}, u32[]{:S(2)}, u32[]{:S(2)}) %collective-permute-start.12) | collective-permute-done | bytes 73760 | tf_op jit(solution)/shard_map/ppermute | solution.py:453
  40.9 0.2 collective-permute-done.13.rest_5_
  41.0 0.0 collective-permute-done.14.rest_6_
  41.0 0.0 copy-done.1
  41.0 2.1 %shard_map.72 = (bf16[384,1152]{1,0:T(8,128)(2,1)}, f32[1,4]{1,0:T(1,128)}) custom-call(bf16[384,1152]{1,0:T(8,128)(2,1)S(1)} %bitcast.7, bf16[640,1152]{1,0:T(8,128)(2,1)S(1)} %get-tuple-element.35.weight_ref, bf16[4,1152]{1,0:T(4,128)(2,1)S(1)} %copy-done.3, bf16[96,384]{1,0:T(8,128)(2,1)S(1)} %collective-permute-done.8.rest_0_, ...), custom_call_target="tpu_custom_call" | custom-call | flops 509607936 | bytes 8388608 | tf_op jit(solution)/shard_map/pallas_call | solution.py:597
Async XLA Ops:
  0.6 6.8 %copy-start = (bf16[1152,1728]{0,1:T(8,128)(2,1)S(1)}, bf16[1152,1728]{0,1:T(8,128)(2,1)}, u32[]{:S(2)}) copy-start(bf16[1152,1728]{0,1:T(8,128)(2,1)} %param.7) | copy-start | bytes 11943940
  3.4 9.6 %collective-permute-start = (bf16[224,384]{1,0:T(8,128)(2,1)S(1)}, bf16[224,384]{1,0:T(8,128)(2,1)S(1)}, u32[]{:S(2)}, u32[]{:S(2)}) collective-permute-start(bf16[224,384]{1,0:T(8,128)(2,1)S(1)} %get-tuple-element.28), channel_id=1, source_target_pairs={{0,24},{4,28},{8,16},{12,20},{16,8},{20,12},{24,0},{28,4},{1,25},{... | collective-permute-start | bytes 516104 | tf_op jit(solution)/shard_map/ppermute | solution.py:453
  7.4 8.5 %collective-permute-start.1 = (bf16[224,384]{1,0:T(8,128)(2,1)S(1)}, bf16[224,384]{1,0:T(8,128)(2,1)S(1)}, u32[]{:S(2)}, u32[]{:S(2)}) collective-permute-start(bf16[224,384]{1,0:T(8,128)(2,1)S(1)} %get-tuple-element.29), channel_id=1, source_target_pairs={{0,28},{4,24},{8,20},{12,16},{16,12},{20,8},{24,4},{28,0},{1,29},{... | collective-permute-start | bytes 516104 | tf_op jit(solution)/shard_map/ppermute | solution.py:453
  7.4 10.4 %copy-start.3 = (bf16[4,1152]{1,0:T(4,128)(2,1)S(1)}, bf16[4,1152]{1,0:T(4,128)(2,1)}, u32[]{:S(2)}) copy-start(bf16[4,1152]{1,0:T(4,128)(2,1)} %text_ref.1) | copy-start | bytes 27652
  7.4 11.9 %copy-start.2 = (s32[1,3072]{1,0:T(1,128)S(1)}, s32[1,3072]{1,0:T(1,128)}, u32[]{:S(2)}) copy-start(s32[1,3072]{1,0:T(1,128)} %ids_ref.5) | copy-start | bytes 36868
  9.4 8.4 %collective-permute-start.2 = (bf16[224,384]{1,0:T(8,128)(2,1)S(1)}, bf16[224,384]{1,0:T(8,128)(2,1)S(1)}, u32[]{:S(2)}, u32[]{:S(2)}) collective-permute-start(bf16[224,384]{1,0:T(8,128)(2,1)S(1)} %get-tuple-element.32), channel_id=1, source_target_pairs={{0,4},{4,0},{8,12},{12,8},{16,20},{20,16},{24,28},{28,24},{1,5},{5... | collective-permute-start | bytes 516104 | tf_op jit(solution)/shard_map/ppermute | solution.py:453
  9.6 11.8 %collective-permute-start.3 = (bf16[224,384]{1,0:T(8,128)(2,1)S(1)}, bf16[224,384]{1,0:T(8,128)(2,1)S(1)}, u32[]{:S(2)}, u32[]{:S(2)}) collective-permute-start(bf16[224,384]{1,0:T(8,128)(2,1)S(1)} %get-tuple-element.39), channel_id=1, source_target_pairs={{0,8},{4,12},{8,0},{12,4},{16,24},{20,28},{24,16},{28,20},{1,9},{5... | collective-permute-start | bytes 516104 | tf_op jit(solution)/shard_map/ppermute | solution.py:453
  11.5 9.9 %collective-permute-start.4 = (bf16[224,384]{1,0:T(8,128)(2,1)S(1)}, bf16[224,384]{1,0:T(8,128)(2,1)S(1)}, u32[]{:S(2)}, u32[]{:S(2)}) collective-permute-start(bf16[224,384]{1,0:T(8,128)(2,1)S(1)} %get-tuple-element.40), channel_id=1, source_target_pairs={{0,16},{4,20},{8,24},{12,28},{16,0},{20,4},{24,8},{28,12},{1,17},{... | collective-permute-start | bytes 516104 | tf_op jit(solution)/shard_map/ppermute | solution.py:453
  13.0 9.1 %collective-permute-start.5 = (bf16[224,384]{1,0:T(8,128)(2,1)S(1)}, bf16[224,384]{1,0:T(8,128)(2,1)S(1)}, u32[]{:S(2)}, u32[]{:S(2)}) collective-permute-start(bf16[224,384]{1,0:T(8,128)(2,1)S(1)} %get-tuple-element.41), channel_id=1, source_target_pairs={{0,12},{4,8},{8,4},{12,0},{16,28},{20,24},{24,20},{28,16},{1,13},{... | collective-permute-start | bytes 516104 | tf_op jit(solution)/shard_map/ppermute | solution.py:453
  15.9 6.9 %collective-permute-start.6 = (bf16[224,384]{1,0:T(8,128)(2,1)S(1)}, bf16[224,384]{1,0:T(8,128)(2,1)S(1)}, u32[]{:S(2)}, u32[]{:S(2)}) collective-permute-start(bf16[224,384]{1,0:T(8,128)(2,1)S(1)} %get-tuple-element.42), channel_id=1, source_target_pairs={{0,20},{4,16},{8,28},{12,24},{16,4},{20,0},{24,12},{28,8},{1,21},{... | collective-permute-start | bytes 516104 | tf_op jit(solution)/shard_map/ppermute | solution.py:453
  17.8 3.7 %collective-permute-start.7 = (bf16[4,1152]{1,0:T(4,128)(2,1)S(1)}, bf16[4,1152]{1,0:T(4,128)(2,1)S(1)}, u32[]{:S(2)}, u32[]{:S(2)}) collective-permute-start(bf16[4,1152]{1,0:T(4,128)(2,1)S(1)} %copy-done.3), channel_id=1, source_target_pairs={{1,0},{0,1},{3,2},{2,3},{6,4},{7,5},{4,6},{5,7},{11,8},{10,9},{9,1... | collective-permute-start | bytes 27656 | tf_op jit(solution)/shard_map/ppermute | solution.py:453
  22.7 18.3 %copy-start.1 = (bf16[1,384,1152]{2,1,0:T(8,128)(2,1)S(1)}, bf16[1,384,1152]{2,1,0:T(8,128)(2,1)}, u32[]{:S(2)}) copy-start(bf16[1,384,1152]{2,1,0:T(8,128)(2,1)} %param.5) | copy-start | bytes 2654212
  30.3 5.5 %collective-permute-start.8 = (bf16[96,384]{1,0:T(8,128)(2,1)S(1)}, bf16[96,384]{1,0:T(8,128)(2,1)S(1)}, u32[]{:S(2)}, u32[]{:S(2)}) collective-permute-start(bf16[96,384]{1,0:T(8,128)(2,1)S(1)} %get-tuple-element.44), channel_id=1, source_target_pairs={{0,24},{4,28},{8,16},{12,20},{16,8},{20,12},{24,0},{28,4},{1,25},{... | collective-permute-start | bytes 221192 | tf_op jit(solution)/shard_map/ppermute | solution.py:453
  32.6 5.2 %collective-permute-start.9 = (bf16[96,384]{1,0:T(8,128)(2,1)S(1)}, bf16[96,384]{1,0:T(8,128)(2,1)S(1)}, u32[]{:S(2)}, u32[]{:S(2)}) collective-permute-start(bf16[96,384]{1,0:T(8,128)(2,1)S(1)} %get-tuple-element.45), channel_id=1, source_target_pairs={{0,28},{4,24},{8,20},{12,16},{16,12},{20,8},{24,4},{28,0},{1,29},{... | collective-permute-start | bytes 221192 | tf_op jit(solution)/shard_map/ppermute | solution.py:453
  32.8 6.3 %collective-permute-start.10 = (bf16[96,384]{1,0:T(8,128)(2,1)S(1)}, bf16[96,384]{1,0:T(8,128)(2,1)S(1)}, u32[]{:S(2)}, u32[]{:S(2)}) collective-permute-start(bf16[96,384]{1,0:T(8,128)(2,1)S(1)} %get-tuple-element.46), channel_id=1, source_target_pairs={{0,8},{4,12},{8,0},{12,4},{16,24},{20,28},{24,16},{28,20},{1,9},{5... | collective-permute-start | bytes 221192 | tf_op jit(solution)/shard_map/ppermute | solution.py:453
  34.6 5.2 %collective-permute-start.11 = (bf16[96,384]{1,0:T(8,128)(2,1)S(1)}, bf16[96,384]{1,0:T(8,128)(2,1)S(1)}, u32[]{:S(2)}, u32[]{:S(2)}) collective-permute-start(bf16[96,384]{1,0:T(8,128)(2,1)S(1)} %get-tuple-element.47), channel_id=1, source_target_pairs={{0,16},{4,20},{8,24},{12,28},{16,0},{20,4},{24,8},{28,12},{1,17},{... | collective-permute-start | bytes 221192 | tf_op jit(solution)/shard_map/ppermute | solution.py:453
  35.7 5.1 %collective-permute-start.12 = (bf16[96,384]{1,0:T(8,128)(2,1)S(1)}, bf16[96,384]{1,0:T(8,128)(2,1)S(1)}, u32[]{:S(2)}, u32[]{:S(2)}) collective-permute-start(bf16[96,384]{1,0:T(8,128)(2,1)S(1)} %get-tuple-element.48), channel_id=1, source_target_pairs={{0,12},{4,8},{8,4},{12,0},{16,28},{20,24},{24,20},{28,16},{1,13},{... | collective-permute-start | bytes 221192 | tf_op jit(solution)/shard_map/ppermute | solution.py:453
  35.8 5.2 %collective-permute-start.13 = (bf16[96,384]{1,0:T(8,128)(2,1)S(1)}, bf16[96,384]{1,0:T(8,128)(2,1)S(1)}, u32[]{:S(2)}, u32[]{:S(2)}) collective-permute-start(bf16[96,384]{1,0:T(8,128)(2,1)S(1)} %get-tuple-element.49), channel_id=1, source_target_pairs={{0,20},{4,16},{8,28},{12,24},{16,4},{20,0},{24,12},{28,8},{1,21},{... | collective-permute-start | bytes 221192 | tf_op jit(solution)/shard_map/ppermute | solution.py:453
  37.8 3.2 %collective-permute-start.14 = (bf16[96,384]{1,0:T(8,128)(2,1)S(1)}, bf16[96,384]{1,0:T(8,128)(2,1)S(1)}, u32[]{:S(2)}, u32[]{:S(2)}) collective-permute-start(bf16[96,384]{1,0:T(8,128)(2,1)S(1)} %get-tuple-element.50), channel_id=1, source_target_pairs={{0,4},{4,0},{8,12},{12,8},{16,20},{20,16},{24,28},{28,24},{1,5},{5... | collective-permute-start | bytes 221192 | tf_op jit(solution)/shard_map/ppermute | solution.py:453

commit v21 on v20

--- a/solution.py
+++ b/solution.py
@@ -17,7 +17,7 @@
 KEY_AT = SIZE - SPARE
 QUERY_AT = 2 * SIZE
 TEXT_ROWS = 16
-RUN = 8
+RUN = 4
 HIDDEN = -1e30
 ORDER = (6, 7, 2, 4, 3, 5, 1, 0)
 EARLY = (6, 7, 1, 0)

time: 43.3 us -> 43.6 us (level)
  no operation moved by 1% of the time
where the time goes in v21:
time: 43.6 us; the launch traced here: 43.5 us
  starting transfers between devices  17.6 us (40%)
  Pallas kernels  16.4 us (38%)
  waiting for transfers between devices  8.79 us (20%)
  between operations  0.69 us (2%)
    ppermute x15, starting transfers between devices, moved(): return lax.ppermute(value, axis, pairs)  17.6 us
    ppermute x15, waiting for transfers between devices, moved(): return lax.ppermute(value, axis, pairs)  8.79 us
    pallas_call x1, Pallas kernels, local(): call(functools.partial(attend_kernel, images, piggy, halo), (shape((padde...  7.85 us
    pallas_call x1, Pallas kernels, local(): call(functools.partial(far_kernel, images, piggy), (shape((depth, count),...  2.8 us
    pallas_call x1, Pallas kernels, local(): call(functools.partial(finish_kernel, images), (shape((count, depth), bf1...  2.13 us
    pallas_call x1, Pallas kernels, local(): call(functools.partial(near_kernel, piggy), (block,) * 6, [], in_vmem(3),...  1.95 us
    pallas_call x1, Pallas kernels, local(): call(functools.partial(prepare_kernel, images, halo), (shape((len(EARLY)...  1.64 us
  transfers between devices with their start and end apart: 15, of which 9 were waited for; matrix products, arithmetic and copies ran while one was open for 0% of the time, Pallas kernels for 8%

profile of v21, /device:TPU:0, one launch (start us, length us, event | category | flops | bytes accessed | tf_op | source)
XLA Modules:
  0.0 43.5 jit_solution(11644917118586343985)
XLA Ops:
  0.6 0.0 copy-start
  0.6 2.8 %shard_map.68 = (bf16[1152,384]{1,0:T(8,128)(2,1)S(1)}, f32[8,1152]{1,0:T(8,128)S(1)}, bf16[224,384]{1,0:T(8,128)(2,1)S(1)}, bf16[224,384]{1,0:T(8,128)(2,1)S(1)}) custom-call(s32[1,3072]{1,0:T(1,128)} %ids_ref.5, bf16[384,1152]{1,0:T(8,128)(2,1)} %bitcast.6, bf16[1728,1152]{1,0:T(8,128)(2,1)} %bitcast.4), custom_call_target="tpu_custom_call" | custom-call | flops 382205952 | bytes 8388608 | tf_op jit(solution)/shard_map/pallas_call | solution.py:504
  3.4 4.0 %collective-permute-start = (bf16[224,384]{1,0:T(8,128)(2,1)S(1)}, bf16[224,384]{1,0:T(8,128)(2,1)S(1)}, u32[]{:S(2)}, u32[]{:S(2)}) collective-permute-start(bf16[224,384]{1,0:T(8,128)(2,1)S(1)} %get-tuple-element.28), channel_id=1, source_target_pairs={{0,24},{4,28},{8,16},{12,20},{16,8},{20,12},{24,0},{28,4},{1,25},{... | collective-permute-start | bytes 516104 | tf_op jit(solution)/shard_map/ppermute | solution.py:453
  7.4 0.0 collective-permute-start.1
  7.4 0.0 copy-done
  7.4 0.0 copy-start.3
  7.4 0.0 copy-start.2
  7.4 1.9 %shard_map.69 = (bf16[224,384]{1,0:T(8,128)(2,1)S(1)}, bf16[224,384]{1,0:T(8,128)(2,1)S(1)}, bf16[224,384]{1,0:T(8,128)(2,1)S(1)}, bf16[224,384]{1,0:T(8,128)(2,...) custom-call(bf16[1152,384]{1,0:T(8,128)(2,1)S(1)} %get-tuple-element.30.normed_ref, ...), custom_call_target="tpu_custom_call" | custom-call | flops 1146617856 | bytes 8388608 | tf_op jit(solution)/shard_map/pallas_call | solution.py:518
  9.4 0.2 collective-permute-start.2
  9.6 1.9 %collective-permute-start.3 = (bf16[224,384]{1,0:T(8,128)(2,1)S(1)}, bf16[224,384]{1,0:T(8,128)(2,1)S(1)}, u32[]{:S(2)}, u32[]{:S(2)}) collective-permute-start(bf16[224,384]{1,0:T(8,128)(2,1)S(1)} %get-tuple-element.39), channel_id=1, source_target_pairs={{0,8},{4,12},{8,0},{12,4},{16,24},{20,28},{24,16},{28,20},{1,9},{5... | collective-permute-start | bytes 516104 | tf_op jit(solution)/shard_map/ppermute | solution.py:453
  11.5 1.5 %collective-permute-start.4 = (bf16[224,384]{1,0:T(8,128)(2,1)S(1)}, bf16[224,384]{1,0:T(8,128)(2,1)S(1)}, u32[]{:S(2)}, u32[]{:S(2)}) collective-permute-start(bf16[224,384]{1,0:T(8,128)(2,1)S(1)} %get-tuple-element.40), channel_id=1, source_target_pairs={{0,16},{4,20},{8,24},{12,28},{16,0},{20,4},{24,8},{28,12},{1,17},{... | collective-permute-start | bytes 516104 | tf_op jit(solution)/shard_map/ppermute | solution.py:453
  13.0 0.0 collective-permute-done.rest_0_
  13.0 0.0 collective-permute-start.5
  13.0 2.9 %collective-permute-done.1.rest_1_ = bf16[224,384]{1,0:T(8,128)(2,1)S(1)} collective-permute-done((bf16[224,384]{1,0:T(8,128)(2,1)S(1)}, bf16[224,384]{1,0:T(8,128)(2,1)S(1)}, u32[]{:S(2)}, u32[]{:S(2)}) %collective-permute-start.1) | collective-permute-done | bytes 172064 | tf_op jit(solution)/shard_map/ppermute | solution.py:453
  15.9 1.9 %collective-permute-start.6 = (bf16[224,384]{1,0:T(8,128)(2,1)S(1)}, bf16[224,384]{1,0:T(8,128)(2,1)S(1)}, u32[]{:S(2)}, u32[]{:S(2)}) collective-permute-start(bf16[224,384]{1,0:T(8,128)(2,1)S(1)} %get-tuple-element.42), channel_id=1, source_target_pairs={{0,20},{4,16},{8,28},{12,24},{16,4},{20,0},{24,12},{28,8},{1,21},{... | collective-permute-start | bytes 516104 | tf_op jit(solution)/shard_map/ppermute | solution.py:453
  17.8 0.0 collective-permute-done.2.rest_2_
  17.8 0.0 copy-done.3
  17.8 1.6 %collective-permute-start.7 = (bf16[4,1152]{1,0:T(4,128)(2,1)S(1)}, bf16[4,1152]{1,0:T(4,128)(2,1)S(1)}, u32[]{:S(2)}, u32[]{:S(2)}) collective-permute-start(bf16[4,1152]{1,0:T(4,128)(2,1)S(1)} %copy-done.3), channel_id=1, source_target_pairs={{1,0},{0,1},{3,2},{2,3},{6,4},{7,5},{4,6},{5,7},{11,8},{10,9},{9,1... | collective-permute-start | bytes 27656 | tf_op jit(solution)/shard_map/ppermute | solution.py:453
  19.3 0.0 copy-done.2
  19.3 1.6 %shard_map.70 = (bf16[1536,128]{1,0:T(8,128)(2,1)S(1)}, f32[2,8,3072]{2,1,0:T(8,128)S(1)}, s32[8,128]{1,0:T(8,128)S(1)}, bf16[640,1152]{1,0:T(8,128)(2,1)S(1)}) custom-call(s32[1,3072]{1,0:T(1,128)S(1)} %copy-done.2, bf16[576,1152]{1,0:T(8,128)(2,1)} %out_weight_ref.1, bf16[224,384]{1,0:T(8,128)(2,1)S(1)} %collective-permute-done.rest_0_, ...), custom_call_target="tpu_custom_call" | custom-call | flops 1073741824 | bytes 8388608 | tf_op jit(solution)/shard_map/pallas_call | solution.py:559
  21.0 0.4 %collective-permute-done.7.rest_8_ = bf16[4,1152]{1,0:T(4,128)(2,1)S(1)} collective-permute-done((bf16[4,1152]{1,0:T(4,128)(2,1)S(1)}, bf16[4,1152]{1,0:T(4,128)(2,1)S(1)}, u32[]{:S(2)}, u32[]{:S(2)}) %collective-permute-start.7) | collective-permute-done | bytes 9248 | tf_op jit(solution)/shard_map/ppermute | solution.py:453
  21.4 0.0 collective-permute-done.3.rest_4_
  21.4 0.0 collective-permute-done.4.rest_5_
  21.4 0.7 %collective-permute-done.5.rest_6_ = bf16[224,384]{1,0:T(8,128)(2,1)S(1)} collective-permute-done((bf16[224,384]{1,0:T(8,128)(2,1)S(1)}, bf16[224,384]{1,0:T(8,128)(2,1)S(1)}, u32[]{:S(2)}, u32[]{:S(2)}) %collective-permute-start.5) | collective-permute-done | bytes 172064 | tf_op jit(solution)/shard_map/ppermute | solution.py:453
  22.1 0.6 %collective-permute-done.6.rest_7_ = bf16[224,384]{1,0:T(8,128)(2,1)S(1)} collective-permute-done((bf16[224,384]{1,0:T(8,128)(2,1)S(1)}, bf16[224,384]{1,0:T(8,128)(2,1)S(1)}, u32[]{:S(2)}, u32[]{:S(2)}) %collective-permute-start.6) | collective-permute-done | bytes 172064 | tf_op jit(solution)/shard_map/ppermute | solution.py:453
  22.7 0.0 copy-start.1
  22.7 7.9 %shard_map.71 = (bf16[96,384]{1,0:T(8,128)(2,1)S(1)}, bf16[96,384]{1,0:T(8,128)(2,1)S(1)}, bf16[96,384]{1,0:T(8,128)(2,1)S(1)}, bf16[96,384]{1,0:T(8,128)(2,1)S(...) custom-call(s32[1,3072]{1,0:T(1,128)S(1)} %copy-done.2, ...), custom_call_target="tpu_custom_call" | custom-call | flops 905969664 | bytes 8388608 | tf_op jit(solution)/shard_map/pallas_call | solution.py:572
  30.6 2.3 %collective-permute-start.8 = (bf16[96,384]{1,0:T(8,128)(2,1)S(1)}, bf16[96,384]{1,0:T(8,128)(2,1)S(1)}, u32[]{:S(2)}, u32[]{:S(2)}) collective-permute-start(bf16[96,384]{1,0:T(8,128)(2,1)S(1)} %get-tuple-element.44), channel_id=1, source_target_pairs={{0,24},{4,28},{8,16},{12,20},{16,8},{20,12},{24,0},{28,4},{1,25},{... | collective-permute-start | bytes 221192 | tf_op jit(solution)/shard_map/ppermute | solution.py:453
  32.9 0.2 collective-permute-start.9
  33.1 1.8 %collective-permute-start.10 = (bf16[96,384]{1,0:T(8,128)(2,1)S(1)}, bf16[96,384]{1,0:T(8,128)(2,1)S(1)}, u32[]{:S(2)}, u32[]{:S(2)}) collective-permute-start(bf16[96,384]{1,0:T(8,128)(2,1)S(1)} %get-tuple-element.46), channel_id=1, source_target_pairs={{0,8},{4,12},{8,0},{12,4},{16,24},{20,28},{24,16},{28,20},{1,9},{5... | collective-permute-start | bytes 221192 | tf_op jit(solution)/shard_map/ppermute | solution.py:453
  34.9 1.1 %collective-permute-start.11 = (bf16[96,384]{1,0:T(8,128)(2,1)S(1)}, bf16[96,384]{1,0:T(8,128)(2,1)S(1)}, u32[]{:S(2)}, u32[]{:S(2)}) collective-permute-start(bf16[96,384]{1,0:T(8,128)(2,1)S(1)} %get-tuple-element.47), channel_id=1, source_target_pairs={{0,16},{4,20},{8,24},{12,28},{16,0},{20,4},{24,8},{28,12},{1,17},{... | collective-permute-start | bytes 221192 | tf_op jit(solution)/shard_map/ppermute | solution.py:453
  36.0 0.1 collective-permute-start.12
  36.1 0.0 collective-permute-done.8.rest_0_
  36.1 0.8 %collective-permute-start.13 = (bf16[96,384]{1,0:T(8,128)(2,1)S(1)}, bf16[96,384]{1,0:T(8,128)(2,1)S(1)}, u32[]{:S(2)}, u32[]{:S(2)}) collective-permute-start(bf16[96,384]{1,0:T(8,128)(2,1)S(1)} %get-tuple-element.49), channel_id=1, source_target_pairs={{0,20},{4,16},{8,28},{12,24},{16,4},{20,0},{24,12},{28,8},{1,21},{... | collective-permute-start | bytes 221192 | tf_op jit(solution)/shard_map/ppermute | solution.py:453
  36.9 1.2 %collective-permute-done.9.rest_1_ = bf16[96,384]{1,0:T(8,128)(2,1)S(1)} collective-permute-done((bf16[96,384]{1,0:T(8,128)(2,1)S(1)}, bf16[96,384]{1,0:T(8,128)(2,1)S(1)}, u32[]{:S(2)}, u32[]{:S(2)}) %collective-permute-start.9) | collective-permute-done | bytes 73760 | tf_op jit(solution)/shard_map/ppermute | solution.py:453
  38.1 0.3 collective-permute-start.14
  38.4 1.0 %collective-permute-done.10.rest_2_ = bf16[96,384]{1,0:T(8,128)(2,1)S(1)} collective-permute-done((bf16[96,384]{1,0:T(8,128)(2,1)S(1)}, bf16[96,384]{1,0:T(8,128)(2,1)S(1)}, u32[]{:S(2)}, u32[]{:S(2)}) %collective-permute-start.10) | collective-permute-done | bytes 73760 | tf_op jit(solution)/shard_map/ppermute | solution.py:453
  39.4 0.7 %collective-permute-done.11.rest_3_ = bf16[96,384]{1,0:T(8,128)(2,1)S(1)} collective-permute-done((bf16[96,384]{1,0:T(8,128)(2,1)S(1)}, bf16[96,384]{1,0:T(8,128)(2,1)S(1)}, u32[]{:S(2)}, u32[]{:S(2)}) %collective-permute-start.11) | collective-permute-done | bytes 73760 | tf_op jit(solution)/shard_map/ppermute | solution.py:453
  40.1 1.1 %collective-permute-done.12.rest_4_ = bf16[96,384]{1,0:T(8,128)(2,1)S(1)} collective-permute-done((bf16[96,384]{1,0:T(8,128)(2,1)S(1)}, bf16[96,384]{1,0:T(8,128)(2,1)S(1)}, u32[]{:S(2)}, u32[]{:S(2)}) %collective-permute-start.12) | collective-permute-done | bytes 73760 | tf_op jit(solution)/shard_map/ppermute | solution.py:453
  41.2 0.2 collective-permute-done.13.rest_5_
  41.3 0.0 collective-permute-done.14.rest_6_
  41.4 0.0 copy-done.1
  41.4 2.1 %shard_map.72 = (bf16[384,1152]{1,0:T(8,128)(2,1)}, f32[1,4]{1,0:T(1,128)}) custom-call(bf16[384,1152]{1,0:T(8,128)(2,1)S(1)} %bitcast.7, bf16[640,1152]{1,0:T(8,128)(2,1)S(1)} %get-tuple-element.35.weight_ref, bf16[4,1152]{1,0:T(4,128)(2,1)S(1)} %copy-done.3, bf16[96,384]{1,0:T(8,128)(2,1)S(1)} %collective-permute-done.8.rest_0_, ...), custom_call_target="tpu_custom_call" | custom-call | flops 509607936 | bytes 8388608 | tf_op jit(solution)/shard_map/pallas_call | solution.py:597
Async XLA Ops:
  0.6 6.8 %copy-start = (bf16[1152,1728]{0,1:T(8,128)(2,1)S(1)}, bf16[1152,1728]{0,1:T(8,128)(2,1)}, u32[]{:S(2)}) copy-start(bf16[1152,1728]{0,1:T(8,128)(2,1)} %param.7) | copy-start | bytes 11943940
  3.4 9.6 %collective-permute-start = (bf16[224,384]{1,0:T(8,128)(2,1)S(1)}, bf16[224,384]{1,0:T(8,128)(2,1)S(1)}, u32[]{:S(2)}, u32[]{:S(2)}) collective-permute-start(bf16[224,384]{1,0:T(8,128)(2,1)S(1)} %get-tuple-element.28), channel_id=1, source_target_pairs={{0,24},{4,28},{8,16},{12,20},{16,8},{20,12},{24,0},{28,4},{1,25},{... | collective-permute-start | bytes 516104 | tf_op jit(solution)/shard_map/ppermute | solution.py:453
  7.4 8.5 %collective-permute-start.1 = (bf16[224,384]{1,0:T(8,128)(2,1)S(1)}, bf16[224,384]{1,0:T(8,128)(2,1)S(1)}, u32[]{:S(2)}, u32[]{:S(2)}) collective-permute-start(bf16[224,384]{1,0:T(8,128)(2,1)S(1)} %get-tuple-element.29), channel_id=1, source_target_pairs={{0,28},{4,24},{8,20},{12,16},{16,12},{20,8},{24,4},{28,0},{1,29},{... | collective-permute-start | bytes 516104 | tf_op jit(solution)/shard_map/ppermute | solution.py:453
  7.4 10.4 %copy-start.3 = (bf16[4,1152]{1,0:T(4,128)(2,1)S(1)}, bf16[4,1152]{1,0:T(4,128)(2,1)}, u32[]{:S(2)}) copy-start(bf16[4,1152]{1,0:T(4,128)(2,1)} %text_ref.1) | copy-start | bytes 27652
  7.4 11.9 %copy-start.2 = (s32[1,3072]{1,0:T(1,128)S(1)}, s32[1,3072]{1,0:T(1,128)}, u32[]{:S(2)}) copy-start(s32[1,3072]{1,0:T(1,128)} %ids_ref.5) | copy-start | bytes 36868
  9.4 8.4 %collective-permute-start.2 = (bf16[224,384]{1,0:T(8,128)(2,1)S(1)}, bf16[224,384]{1,0:T(8,128)(2,1)S(1)}, u32[]{:S(2)}, u32[]{:S(2)}) collective-permute-start(bf16[224,384]{1,0:T(8,128)(2,1)S(1)} %get-tuple-element.32), channel_id=1, source_target_pairs={{0,4},{4,0},{8,12},{12,8},{16,20},{20,16},{24,28},{28,24},{1,5},{5... | collective-permute-start | bytes 516104 | tf_op jit(solution)/shard_map/ppermute | solution.py:453
  9.6 11.8 %collective-permute-start.3 = (bf16[224,384]{1,0:T(8,128)(2,1)S(1)}, bf16[224,384]{1,0:T(8,128)(2,1)S(1)}, u32[]{:S(2)}, u32[]{:S(2)}) collective-permute-start(bf16[224,384]{1,0:T(8,128)(2,1)S(1)} %get-tuple-element.39), channel_id=1, source_target_pairs={{0,8},{4,12},{8,0},{12,4},{16,24},{20,28},{24,16},{28,20},{1,9},{5... | collective-permute-start | bytes 516104 | tf_op jit(solution)/shard_map/ppermute | solution.py:453
  11.5 9.9 %collective-permute-start.4 = (bf16[224,384]{1,0:T(8,128)(2,1)S(1)}, bf16[224,384]{1,0:T(8,128)(2,1)S(1)}, u32[]{:S(2)}, u32[]{:S(2)}) collective-permute-start(bf16[224,384]{1,0:T(8,128)(2,1)S(1)} %get-tuple-element.40), channel_id=1, source_target_pairs={{0,16},{4,20},{8,24},{12,28},{16,0},{20,4},{24,8},{28,12},{1,17},{... | collective-permute-start | bytes 516104 | tf_op jit(solution)/shard_map/ppermute | solution.py:453
  13.0 9.1 %collective-permute-start.5 = (bf16[224,384]{1,0:T(8,128)(2,1)S(1)}, bf16[224,384]{1,0:T(8,128)(2,1)S(1)}, u32[]{:S(2)}, u32[]{:S(2)}) collective-permute-start(bf16[224,384]{1,0:T(8,128)(2,1)S(1)} %get-tuple-element.41), channel_id=1, source_target_pairs={{0,12},{4,8},{8,4},{12,0},{16,28},{20,24},{24,20},{28,16},{1,13},{... | collective-permute-start | bytes 516104 | tf_op jit(solution)/shard_map/ppermute | solution.py:453
  15.9 6.9 %collective-permute-start.6 = (bf16[224,384]{1,0:T(8,128)(2,1)S(1)}, bf16[224,384]{1,0:T(8,128)(2,1)S(1)}, u32[]{:S(2)}, u32[]{:S(2)}) collective-permute-start(bf16[224,384]{1,0:T(8,128)(2,1)S(1)} %get-tuple-element.42), channel_id=1, source_target_pairs={{0,20},{4,16},{8,28},{12,24},{16,4},{20,0},{24,12},{28,8},{1,21},{... | collective-permute-start | bytes 516104 | tf_op jit(solution)/shard_map/ppermute | solution.py:453
  17.8 3.7 %collective-permute-start.7 = (bf16[4,1152]{1,0:T(4,128)(2,1)S(1)}, bf16[4,1152]{1,0:T(4,128)(2,1)S(1)}, u32[]{:S(2)}, u32[]{:S(2)}) collective-permute-start(bf16[4,1152]{1,0:T(4,128)(2,1)S(1)} %copy-done.3), channel_id=1, source_target_pairs={{1,0},{0,1},{3,2},{2,3},{6,4},{7,5},{4,6},{5,7},{11,8},{10,9},{9,1... | collective-permute-start | bytes 27656 | tf_op jit(solution)/shard_map/ppermute | solution.py:453
  22.7 18.6 %copy-start.1 = (bf16[1,384,1152]{2,1,0:T(8,128)(2,1)S(1)}, bf16[1,384,1152]{2,1,0:T(8,128)(2,1)}, u32[]{:S(2)}) copy-start(bf16[1,384,1152]{2,1,0:T(8,128)(2,1)} %param.5) | copy-start | bytes 2654212
  30.6 5.5 %collective-permute-start.8 = (bf16[96,384]{1,0:T(8,128)(2,1)S(1)}, bf16[96,384]{1,0:T(8,128)(2,1)S(1)}, u32[]{:S(2)}, u32[]{:S(2)}) collective-permute-start(bf16[96,384]{1,0:T(8,128)(2,1)S(1)} %get-tuple-element.44), channel_id=1, source_target_pairs={{0,24},{4,28},{8,16},{12,20},{16,8},{20,12},{24,0},{28,4},{1,25},{... | collective-permute-start | bytes 221192 | tf_op jit(solution)/shard_map/ppermute | solution.py:453
  32.9 5.2 %collective-permute-start.9 = (bf16[96,384]{1,0:T(8,128)(2,1)S(1)}, bf16[96,384]{1,0:T(8,128)(2,1)S(1)}, u32[]{:S(2)}, u32[]{:S(2)}) collective-permute-start(bf16[96,384]{1,0:T(8,128)(2,1)S(1)} %get-tuple-element.45), channel_id=1, source_target_pairs={{0,28},{4,24},{8,20},{12,16},{16,12},{20,8},{24,4},{28,0},{1,29},{... | collective-permute-start | bytes 221192 | tf_op jit(solution)/shard_map/ppermute | solution.py:453
  33.1 6.3 %collective-permute-start.10 = (bf16[96,384]{1,0:T(8,128)(2,1)S(1)}, bf16[96,384]{1,0:T(8,128)(2,1)S(1)}, u32[]{:S(2)}, u32[]{:S(2)}) collective-permute-start(bf16[96,384]{1,0:T(8,128)(2,1)S(1)} %get-tuple-element.46), channel_id=1, source_target_pairs={{0,8},{4,12},{8,0},{12,4},{16,24},{20,28},{24,16},{28,20},{1,9},{5... | collective-permute-start | bytes 221192 | tf_op jit(solution)/shard_map/ppermute | solution.py:453
  34.9 5.2 %collective-permute-start.11 = (bf16[96,384]{1,0:T(8,128)(2,1)S(1)}, bf16[96,384]{1,0:T(8,128)(2,1)S(1)}, u32[]{:S(2)}, u32[]{:S(2)}) collective-permute-start(bf16[96,384]{1,0:T(8,128)(2,1)S(1)} %get-tuple-element.47), channel_id=1, source_target_pairs={{0,16},{4,20},{8,24},{12,28},{16,0},{20,4},{24,8},{28,12},{1,17},{... | collective-permute-start | bytes 221192 | tf_op jit(solution)/shard_map/ppermute | solution.py:453
  36.0 5.1 %collective-permute-start.12 = (bf16[96,384]{1,0:T(8,128)(2,1)S(1)}, bf16[96,384]{1,0:T(8,128)(2,1)S(1)}, u32[]{:S(2)}, u32[]{:S(2)}) collective-permute-start(bf16[96,384]{1,0:T(8,128)(2,1)S(1)} %get-tuple-element.48), channel_id=1, source_target_pairs={{0,12},{4,8},{8,4},{12,0},{16,28},{20,24},{24,20},{28,16},{1,13},{... | collective-permute-start | bytes 221192 | tf_op jit(solution)/shard_map/ppermute | solution.py:453
  36.1 5.2 %collective-permute-start.13 = (bf16[96,384]{1,0:T(8,128)(2,1)S(1)}, bf16[96,384]{1,0:T(8,128)(2,1)S(1)}, u32[]{:S(2)}, u32[]{:S(2)}) collective-permute-start(bf16[96,384]{1,0:T(8,128)(2,1)S(1)} %get-tuple-element.49), channel_id=1, source_target_pairs={{0,20},{4,16},{8,28},{12,24},{16,4},{20,0},{24,12},{28,8},{1,21},{... | collective-permute-start | bytes 221192 | tf_op jit(solution)/shard_map/ppermute | solution.py:453
  38.1 3.2 %collective-permute-start.14 = (bf16[96,384]{1,0:T(8,128)(2,1)S(1)}, bf16[96,384]{1,0:T(8,128)(2,1)S(1)}, u32[]{:S(2)}, u32[]{:S(2)}) collective-permute-start(bf16[96,384]{1,0:T(8,128)(2,1)S(1)} %get-tuple-element.50), channel_id=1, source_target_pairs={{0,4},{4,0},{8,12},{12,8},{16,20},{20,16},{24,28},{28,24},{1,5},{5... | collective-permute-start | bytes 221192 | tf_op jit(solution)/shard_map/ppermute | solution.py:453

commit v22 on v17

--- a/solution.py
+++ b/solution.py
@@ -55,22 +55,13 @@
             parts = [sums[:, pl.ds(first, LANES)], sums[:, HEADS * LANES :]]
             held = sum(part.shape[1] for part in parts)
             spare = jnp.concatenate(parts + [jnp.zeros((SPARE, count - held), jnp.float32)], axis=1)
-        block = jnp.concatenate([value[here], key[here], spare, query[here]], axis=0)
-        yield block.astype(jnp.bfloat16)
+        yield jnp.concatenate([value[here], key[here], spare, query[here]], axis=0)
 
 
 def store_by_core(core, blocks, same_ref, cross_ref):
     first, second = blocks
-
-    @pl.when(core == 0)
-    def _():
-        same_ref[...] = first
-        cross_ref[...] = second
-
-    @pl.when(core == 1)
-    def _():
-        same_ref[...] = second
-        cross_ref[...] = first
+    same_ref[...] = jnp.where(core == 0, first, second).astype(jnp.bfloat16)
+    cross_ref[...] = jnp.where(core == 0, second, first).astype(jnp.bfloat16)
 
 
 def place_in_group():
@@ -168,10 +159,11 @@
     size = attended.shape[0] - SPARE
     held = queries.shape[1]
     tiles = held // tile
+    shift = tile.bit_length() - 1
 
     def bounds(image):
-        first = lax.div(jnp.maximum(starts[image] - query_base, 0), tile)
-        last = lax.div(jnp.minimum(starts[image + 1] - query_base, held) - 1, tile)
+        first = jnp.maximum(starts[image] - query_base, 0) >> shift
+        last = (jnp.minimum(starts[image + 1] - query_base, held) - 1) >> shift
         return jnp.minimum(first, tiles - 1), last
 
     def after(image):
@@ -184,7 +176,7 @@
         return jnp.where(more, at + 1, bounds(later)[0]), jnp.where(more, image, later)
 
     def window_of(image):
-        begin = lax.div(starts[image], LANES) * LANES
+        begin = jnp.bitwise_and(starts[image], -LANES)
         return pl.ds(pl.multiple_of(jnp.minimum(begin, keys.shape[0] - window), LANES), window)
 
     def score(state, scores, tops):

time: 42 us -> 42.1 us (level)
  Pallas kernels: 15.1 us -> 14.6 us
  transfers between devices with their start and end apart: 15 -> 15, of which waited for: 9 -> 9; matrix products, arithmetic and copies ran while one was open for 0% -> 0% of each run, Pallas kernels for 10% -> 9%
where the time goes in v22:
time: 42.1 us; the launch traced here: 41.7 us
  starting transfers between devices  17.6 us (42%)
  Pallas kernels  14.6 us (35%)
  waiting for transfers between devices  8.76 us (21%)
  between operations  0.69 us (2%)
    ppermute x15, starting transfers between devices, moved(): return lax.ppermute(value, axis, pairs)  17.6 us
    ppermute x15, waiting for transfers between devices, moved(): return lax.ppermute(value, axis, pairs)  8.76 us
    pallas_call x1, Pallas kernels, local(): call(functools.partial(attend_kernel, images, piggy, halo), (shape((padde...  6.12 us
    pallas_call x1, Pallas kernels, local(): call(functools.partial(far_kernel, images, piggy), (shape((depth, count),...  2.8 us
    pallas_call x1, Pallas kernels, local(): call(functools.partial(finish_kernel, images), (shape((count, depth), bf1...  2.13 us
    pallas_call x1, Pallas kernels, local(): call(functools.partial(near_kernel, piggy), (block,) * 6, [], in_vmem(3),...  1.95 us
    pallas_call x1, Pallas kernels, local(): call(functools.partial(prepare_kernel, images, halo), (shape((len(EARLY)...  1.64 us
  transfers between devices with their start and end apart: 15, of which 9 were waited for; matrix products, arithmetic and copies ran while one was open for 0% of the time, Pallas kernels for 9%

profile of v22, /device:TPU:0, one launch (start us, length us, event | category | flops | bytes accessed | tf_op | source)
XLA Modules:
  0.0 41.7 jit_solution(2454266183576971541)
XLA Ops:
  0.6 0.0 copy-start
  0.6 2.8 %shard_map.68 = (bf16[1152,384]{1,0:T(8,128)(2,1)S(1)}, f32[8,1152]{1,0:T(8,128)S(1)}, bf16[224,384]{1,0:T(8,128)(2,1)S(1)}, bf16[224,384]{1,0:T(8,128)(2,1)S(1)}) custom-call(s32[1,3072]{1,0:T(1,128)} %ids_ref.5, bf16[384,1152]{1,0:T(8,128)(2,1)} %bitcast.6, bf16[1728,1152]{1,0:T(8,128)(2,1)} %bitcast.4), custom_call_target="tpu_custom_call" | custom-call | flops 382205952 | bytes 8388608 | tf_op jit(solution)/shard_map/pallas_call | solution.py:514
  3.4 4.0 %collective-permute-start = (bf16[224,384]{1,0:T(8,128)(2,1)S(1)}, bf16[224,384]{1,0:T(8,128)(2,1)S(1)}, u32[]{:S(2)}, u32[]{:S(2)}) collective-permute-start(bf16[224,384]{1,0:T(8,128)(2,1)S(1)} %get-tuple-element.28), channel_id=1, source_target_pairs={{0,24},{4,28},{8,16},{12,20},{16,8},{20,12},{24,0},{28,4},{1,25},{... | collective-permute-start | bytes 516104 | tf_op jit(solution)/shard_map/ppermute | solution.py:463
  7.4 0.0 collective-permute-start.1
  7.4 0.0 copy-done
  7.4 0.0 copy-start.3
  7.4 0.0 copy-start.2
  7.4 1.9 %shard_map.69 = (bf16[224,384]{1,0:T(8,128)(2,1)S(1)}, bf16[224,384]{1,0:T(8,128)(2,1)S(1)}, bf16[224,384]{1,0:T(8,128)(2,1)S(1)}, bf16[224,384]{1,0:T(8,128)(2,...) custom-call(bf16[1152,384]{1,0:T(8,128)(2,1)S(1)} %get-tuple-element.30.normed_ref, ...), custom_call_target="tpu_custom_call" | custom-call | flops 1146617856 | bytes 8388608 | tf_op jit(solution)/shard_map/pallas_call | solution.py:528
  9.4 0.2 collective-permute-start.2
  9.6 1.9 %collective-permute-start.3 = (bf16[224,384]{1,0:T(8,128)(2,1)S(1)}, bf16[224,384]{1,0:T(8,128)(2,1)S(1)}, u32[]{:S(2)}, u32[]{:S(2)}) collective-permute-start(bf16[224,384]{1,0:T(8,128)(2,1)S(1)} %get-tuple-element.39), channel_id=1, source_target_pairs={{0,8},{4,12},{8,0},{12,4},{16,24},{20,28},{24,16},{28,20},{1,9},{5... | collective-permute-start | bytes 516104 | tf_op jit(solution)/shard_map/ppermute | solution.py:463
  11.5 1.5 %collective-permute-start.4 = (bf16[224,384]{1,0:T(8,128)(2,1)S(1)}, bf16[224,384]{1,0:T(8,128)(2,1)S(1)}, u32[]{:S(2)}, u32[]{:S(2)}) collective-permute-start(bf16[224,384]{1,0:T(8,128)(2,1)S(1)} %get-tuple-element.40), channel_id=1, source_target_pairs={{0,16},{4,20},{8,24},{12,28},{16,0},{20,4},{24,8},{28,12},{1,17},{... | collective-permute-start | bytes 516104 | tf_op jit(solution)/shard_map/ppermute | solution.py:463
  13.0 0.0 collective-permute-done.rest_0_
  13.0 0.0 collective-permute-start.5
  13.0 2.9 %collective-permute-done.1.rest_1_ = bf16[224,384]{1,0:T(8,128)(2,1)S(1)} collective-permute-done((bf16[224,384]{1,0:T(8,128)(2,1)S(1)}, bf16[224,384]{1,0:T(8,128)(2,1)S(1)}, u32[]{:S(2)}, u32[]{:S(2)}) %collective-permute-start.1) | collective-permute-done | bytes 172064 | tf_op jit(solution)/shard_map/ppermute | solution.py:463
  15.9 1.9 %collective-permute-start.6 = (bf16[224,384]{1,0:T(8,128)(2,1)S(1)}, bf16[224,384]{1,0:T(8,128)(2,1)S(1)}, u32[]{:S(2)}, u32[]{:S(2)}) collective-permute-start(bf16[224,384]{1,0:T(8,128)(2,1)S(1)} %get-tuple-element.42), channel_id=1, source_target_pairs={{0,20},{4,16},{8,28},{12,24},{16,4},{20,0},{24,12},{28,8},{1,21},{... | collective-permute-start | bytes 516104 | tf_op jit(solution)/shard_map/ppermute | solution.py:463
  17.8 0.0 collective-permute-done.2.rest_2_
  17.8 0.0 copy-done.3
  17.8 1.6 %collective-permute-start.7 = (bf16[4,1152]{1,0:T(4,128)(2,1)S(1)}, bf16[4,1152]{1,0:T(4,128)(2,1)S(1)}, u32[]{:S(2)}, u32[]{:S(2)}) collective-permute-start(bf16[4,1152]{1,0:T(4,128)(2,1)S(1)} %copy-done.3), channel_id=1, source_target_pairs={{1,0},{0,1},{3,2},{2,3},{6,4},{7,5},{4,6},{5,7},{11,8},{10,9},{9,1... | collective-permute-start | bytes 27656 | tf_op jit(solution)/shard_map/ppermute | solution.py:463
  19.3 0.0 copy-done.2
  19.3 1.6 %shard_map.70 = (bf16[1536,128]{1,0:T(8,128)(2,1)S(1)}, f32[2,8,3072]{2,1,0:T(8,128)S(1)}, s32[8,128]{1,0:T(8,128)S(1)}, bf16[640,1152]{1,0:T(8,128)(2,1)S(1)}) custom-call(s32[1,3072]{1,0:T(1,128)S(1)} %copy-done.2, bf16[576,1152]{1,0:T(8,128)(2,1)} %out_weight_ref.1, bf16[224,384]{1,0:T(8,128)(2,1)S(1)} %collective-permute-done.rest_0_, ...), custom_call_target="tpu_custom_call" | custom-call | flops 1073741824 | bytes 8388608 | tf_op jit(solution)/shard_map/pallas_call | solution.py:569
  21.0 0.4 %collective-permute-done.7.rest_8_ = bf16[4,1152]{1,0:T(4,128)(2,1)S(1)} collective-permute-done((bf16[4,1152]{1,0:T(4,128)(2,1)S(1)}, bf16[4,1152]{1,0:T(4,128)(2,1)S(1)}, u32[]{:S(2)}, u32[]{:S(2)}) %collective-permute-start.7) | collective-permute-done | bytes 9248 | tf_op jit(solution)/shard_map/ppermute | solution.py:463
  21.4 0.0 collective-permute-done.3.rest_4_
  21.4 0.0 collective-permute-done.4.rest_5_
  21.4 0.7 %collective-permute-done.5.rest_6_ = bf16[224,384]{1,0:T(8,128)(2,1)S(1)} collective-permute-done((bf16[224,384]{1,0:T(8,128)(2,1)S(1)}, bf16[224,384]{1,0:T(8,128)(2,1)S(1)}, u32[]{:S(2)}, u32[]{:S(2)}) %collective-permute-start.5) | collective-permute-done | bytes 172064 | tf_op jit(solution)/shard_map/ppermute | solution.py:463
  22.1 0.6 %collective-permute-done.6.rest_7_ = bf16[224,384]{1,0:T(8,128)(2,1)S(1)} collective-permute-done((bf16[224,384]{1,0:T(8,128)(2,1)S(1)}, bf16[224,384]{1,0:T(8,128)(2,1)S(1)}, u32[]{:S(2)}, u32[]{:S(2)}) %collective-permute-start.6) | collective-permute-done | bytes 172064 | tf_op jit(solution)/shard_map/ppermute | solution.py:463
  22.7 0.0 copy-start.1
  22.7 6.1 %shard_map.71 = (bf16[96,384]{1,0:T(8,128)(2,1)S(1)}, bf16[96,384]{1,0:T(8,128)(2,1)S(1)}, bf16[96,384]{1,0:T(8,128)(2,1)S(1)}, bf16[96,384]{1,0:T(8,128)(2,1)S(...) custom-call(s32[1,3072]{1,0:T(1,128)S(1)} %copy-done.2, ...), custom_call_target="tpu_custom_call" | custom-call | flops 905969664 | bytes 8388608 | tf_op jit(solution)/shard_map/pallas_call | solution.py:582
  28.9 2.3 %collective-permute-start.8 = (bf16[96,384]{1,0:T(8,128)(2,1)S(1)}, bf16[96,384]{1,0:T(8,128)(2,1)S(1)}, u32[]{:S(2)}, u32[]{:S(2)}) collective-permute-start(bf16[96,384]{1,0:T(8,128)(2,1)S(1)} %get-tuple-element.44), channel_id=1, source_target_pairs={{0,24},{4,28},{8,16},{12,20},{16,8},{20,12},{24,0},{28,4},{1,25},{... | collective-permute-start | bytes 221192 | tf_op jit(solution)/shard_map/ppermute | solution.py:463
  31.1 0.2 collective-permute-start.9
  31.4 1.8 %collective-permute-start.10 = (bf16[96,384]{1,0:T(8,128)(2,1)S(1)}, bf16[96,384]{1,0:T(8,128)(2,1)S(1)}, u32[]{:S(2)}, u32[]{:S(2)}) collective-permute-start(bf16[96,384]{1,0:T(8,128)(2,1)S(1)} %get-tuple-element.46), channel_id=1, source_target_pairs={{0,8},{4,12},{8,0},{12,4},{16,24},{20,28},{24,16},{28,20},{1,9},{5... | collective-permute-start | bytes 221192 | tf_op jit(solution)/shard_map/ppermute | solution.py:463
  33.2 1.2 %collective-permute-start.11 = (bf16[96,384]{1,0:T(8,128)(2,1)S(1)}, bf16[96,384]{1,0:T(8,128)(2,1)S(1)}, u32[]{:S(2)}, u32[]{:S(2)}) collective-permute-start(bf16[96,384]{1,0:T(8,128)(2,1)S(1)} %get-tuple-element.47), channel_id=1, source_target_pairs={{0,16},{4,20},{8,24},{12,28},{16,0},{20,4},{24,8},{28,12},{1,17},{... | collective-permute-start | bytes 221192 | tf_op jit(solution)/shard_map/ppermute | solution.py:463
  34.3 0.0 collective-permute-start.12
  34.4 0.0 collective-permute-done.8.rest_0_
  34.4 0.8 %collective-permute-start.13 = (bf16[96,384]{1,0:T(8,128)(2,1)S(1)}, bf16[96,384]{1,0:T(8,128)(2,1)S(1)}, u32[]{:S(2)}, u32[]{:S(2)}) collective-permute-start(bf16[96,384]{1,0:T(8,128)(2,1)S(1)} %get-tuple-element.49), channel_id=1, source_target_pairs={{0,20},{4,16},{8,28},{12,24},{16,4},{20,0},{24,12},{28,8},{1,21},{... | collective-permute-start | bytes 221192 | tf_op jit(solution)/shard_map/ppermute | solution.py:463
  35.1 1.2 %collective-permute-done.9.rest_1_ = bf16[96,384]{1,0:T(8,128)(2,1)S(1)} collective-permute-done((bf16[96,384]{1,0:T(8,128)(2,1)S(1)}, bf16[96,384]{1,0:T(8,128)(2,1)S(1)}, u32[]{:S(2)}, u32[]{:S(2)}) %collective-permute-start.9) | collective-permute-done | bytes 73760 | tf_op jit(solution)/shard_map/ppermute | solution.py:463
  36.4 0.3 collective-permute-start.14
  36.7 1.0 %collective-permute-done.10.rest_2_ = bf16[96,384]{1,0:T(8,128)(2,1)S(1)} collective-permute-done((bf16[96,384]{1,0:T(8,128)(2,1)S(1)}, bf16[96,384]{1,0:T(8,128)(2,1)S(1)}, u32[]{:S(2)}, u32[]{:S(2)}) %collective-permute-start.10) | collective-permute-done | bytes 73760 | tf_op jit(solution)/shard_map/ppermute | solution.py:463
  37.7 0.7 %collective-permute-done.11.rest_3_ = bf16[96,384]{1,0:T(8,128)(2,1)S(1)} collective-permute-done((bf16[96,384]{1,0:T(8,128)(2,1)S(1)}, bf16[96,384]{1,0:T(8,128)(2,1)S(1)}, u32[]{:S(2)}, u32[]{:S(2)}) %collective-permute-start.11) | collective-permute-done | bytes 73760 | tf_op jit(solution)/shard_map/ppermute | solution.py:463
  38.4 1.1 %collective-permute-done.12.rest_4_ = bf16[96,384]{1,0:T(8,128)(2,1)S(1)} collective-permute-done((bf16[96,384]{1,0:T(8,128)(2,1)S(1)}, bf16[96,384]{1,0:T(8,128)(2,1)S(1)}, u32[]{:S(2)}, u32[]{:S(2)}) %collective-permute-start.12) | collective-permute-done | bytes 73760 | tf_op jit(solution)/shard_map/ppermute | solution.py:463
  39.4 0.2 collective-permute-done.13.rest_5_
  39.6 0.0 collective-permute-done.14.rest_6_
  39.6 0.0 copy-done.1
  39.6 2.1 %shard_map.72 = (bf16[384,1152]{1,0:T(8,128)(2,1)}, f32[1,4]{1,0:T(1,128)}) custom-call(bf16[384,1152]{1,0:T(8,128)(2,1)S(1)} %bitcast.7, bf16[640,1152]{1,0:T(8,128)(2,1)S(1)} %get-tuple-element.35.weight_ref, bf16[4,1152]{1,0:T(4,128)(2,1)S(1)} %copy-done.3, bf16[96,384]{1,0:T(8,128)(2,1)S(1)} %collective-permute-done.8.rest_0_, ...), custom_call_target="tpu_custom_call" | custom-call | flops 509607936 | bytes 8388608 | tf_op jit(solution)/shard_map/pallas_call | solution.py:610
Async XLA Ops:
  0.6 6.8 %copy-start = (bf16[1152,1728]{0,1:T(8,128)(2,1)S(1)}, bf16[1152,1728]{0,1:T(8,128)(2,1)}, u32[]{:S(2)}) copy-start(bf16[1152,1728]{0,1:T(8,128)(2,1)} %param.7) | copy-start | bytes 11943940
  3.4 9.6 %collective-permute-start = (bf16[224,384]{1,0:T(8,128)(2,1)S(1)}, bf16[224,384]{1,0:T(8,128)(2,1)S(1)}, u32[]{:S(2)}, u32[]{:S(2)}) collective-permute-start(bf16[224,384]{1,0:T(8,128)(2,1)S(1)} %get-tuple-element.28), channel_id=1, source_target_pairs={{0,24},{4,28},{8,16},{12,20},{16,8},{20,12},{24,0},{28,4},{1,25},{... | collective-permute-start | bytes 516104 | tf_op jit(solution)/shard_map/ppermute | solution.py:463
  7.4 8.5 %collective-permute-start.1 = (bf16[224,384]{1,0:T(8,128)(2,1)S(1)}, bf16[224,384]{1,0:T(8,128)(2,1)S(1)}, u32[]{:S(2)}, u32[]{:S(2)}) collective-permute-start(bf16[224,384]{1,0:T(8,128)(2,1)S(1)} %get-tuple-element.29), channel_id=1, source_target_pairs={{0,28},{4,24},{8,20},{12,16},{16,12},{20,8},{24,4},{28,0},{1,29},{... | collective-permute-start | bytes 516104 | tf_op jit(solution)/shard_map/ppermute | solution.py:463
  7.4 10.4 %copy-start.3 = (bf16[4,1152]{1,0:T(4,128)(2,1)S(1)}, bf16[4,1152]{1,0:T(4,128)(2,1)}, u32[]{:S(2)}) copy-start(bf16[4,1152]{1,0:T(4,128)(2,1)} %text_ref.1) | copy-start | bytes 27652
  7.4 11.9 %copy-start.2 = (s32[1,3072]{1,0:T(1,128)S(1)}, s32[1,3072]{1,0:T(1,128)}, u32[]{:S(2)}) copy-start(s32[1,3072]{1,0:T(1,128)} %ids_ref.5) | copy-start | bytes 36868
  9.4 8.4 %collective-permute-start.2 = (bf16[224,384]{1,0:T(8,128)(2,1)S(1)}, bf16[224,384]{1,0:T(8,128)(2,1)S(1)}, u32[]{:S(2)}, u32[]{:S(2)}) collective-permute-start(bf16[224,384]{1,0:T(8,128)(2,1)S(1)} %get-tuple-element.32), channel_id=1, source_target_pairs={{0,4},{4,0},{8,12},{12,8},{16,20},{20,16},{24,28},{28,24},{1,5},{5... | collective-permute-start | bytes 516104 | tf_op jit(solution)/shard_map/ppermute | solution.py:463
  9.6 11.8 %collective-permute-start.3 = (bf16[224,384]{1,0:T(8,128)(2,1)S(1)}, bf16[224,384]{1,0:T(8,128)(2,1)S(1)}, u32[]{:S(2)}, u32[]{:S(2)}) collective-permute-start(bf16[224,384]{1,0:T(8,128)(2,1)S(1)} %get-tuple-element.39), channel_id=1, source_target_pairs={{0,8},{4,12},{8,0},{12,4},{16,24},{20,28},{24,16},{28,20},{1,9},{5... | collective-permute-start | bytes 516104 | tf_op jit(solution)/shard_map/ppermute | solution.py:463
  11.5 9.9 %collective-permute-start.4 = (bf16[224,384]{1,0:T(8,128)(2,1)S(1)}, bf16[224,384]{1,0:T(8,128)(2,1)S(1)}, u32[]{:S(2)}, u32[]{:S(2)}) collective-permute-start(bf16[224,384]{1,0:T(8,128)(2,1)S(1)} %get-tuple-element.40), channel_id=1, source_target_pairs={{0,16},{4,20},{8,24},{12,28},{16,0},{20,4},{24,8},{28,12},{1,17},{... | collective-permute-start | bytes 516104 | tf_op jit(solution)/shard_map/ppermute | solution.py:463
  13.0 9.1 %collective-permute-start.5 = (bf16[224,384]{1,0:T(8,128)(2,1)S(1)}, bf16[224,384]{1,0:T(8,128)(2,1)S(1)}, u32[]{:S(2)}, u32[]{:S(2)}) collective-permute-start(bf16[224,384]{1,0:T(8,128)(2,1)S(1)} %get-tuple-element.41), channel_id=1, source_target_pairs={{0,12},{4,8},{8,4},{12,0},{16,28},{20,24},{24,20},{28,16},{1,13},{... | collective-permute-start | bytes 516104 | tf_op jit(solution)/shard_map/ppermute | solution.py:463
  15.9 6.9 %collective-permute-start.6 = (bf16[224,384]{1,0:T(8,128)(2,1)S(1)}, bf16[224,384]{1,0:T(8,128)(2,1)S(1)}, u32[]{:S(2)}, u32[]{:S(2)}) collective-permute-start(bf16[224,384]{1,0:T(8,128)(2,1)S(1)} %get-tuple-element.42), channel_id=1, source_target_pairs={{0,20},{4,16},{8,28},{12,24},{16,4},{20,0},{24,12},{28,8},{1,21},{... | collective-permute-start | bytes 516104 | tf_op jit(solution)/shard_map/ppermute | solution.py:463
  17.8 3.7 %collective-permute-start.7 = (bf16[4,1152]{1,0:T(4,128)(2,1)S(1)}, bf16[4,1152]{1,0:T(4,128)(2,1)S(1)}, u32[]{:S(2)}, u32[]{:S(2)}) collective-permute-start(bf16[4,1152]{1,0:T(4,128)(2,1)S(1)} %copy-done.3), channel_id=1, source_target_pairs={{1,0},{0,1},{3,2},{2,3},{6,4},{7,5},{4,6},{5,7},{11,8},{10,9},{9,1... | collective-permute-start | bytes 27656 | tf_op jit(solution)/shard_map/ppermute | solution.py:463
  22.7 16.9 %copy-start.1 = (bf16[1,384,1152]{2,1,0:T(8,128)(2,1)S(1)}, bf16[1,384,1152]{2,1,0:T(8,128)(2,1)}, u32[]{:S(2)}) copy-start(bf16[1,384,1152]{2,1,0:T(8,128)(2,1)} %param.5) | copy-start | bytes 2654212
  28.9 5.5 %collective-permute-start.8 = (bf16[96,384]{1,0:T(8,128)(2,1)S(1)}, bf16[96,384]{1,0:T(8,128)(2,1)S(1)}, u32[]{:S(2)}, u32[]{:S(2)}) collective-permute-start(bf16[96,384]{1,0:T(8,128)(2,1)S(1)} %get-tuple-element.44), channel_id=1, source_target_pairs={{0,24},{4,28},{8,16},{12,20},{16,8},{20,12},{24,0},{28,4},{1,25},{... | collective-permute-start | bytes 221192 | tf_op jit(solution)/shard_map/ppermute | solution.py:463
  31.1 5.2 %collective-permute-start.9 = (bf16[96,384]{1,0:T(8,128)(2,1)S(1)}, bf16[96,384]{1,0:T(8,128)(2,1)S(1)}, u32[]{:S(2)}, u32[]{:S(2)}) collective-permute-start(bf16[96,384]{1,0:T(8,128)(2,1)S(1)} %get-tuple-element.45), channel_id=1, source_target_pairs={{0,28},{4,24},{8,20},{12,16},{16,12},{20,8},{24,4},{28,0},{1,29},{... | collective-permute-start | bytes 221192 | tf_op jit(solution)/shard_map/ppermute | solution.py:463
  31.4 6.3 %collective-permute-start.10 = (bf16[96,384]{1,0:T(8,128)(2,1)S(1)}, bf16[96,384]{1,0:T(8,128)(2,1)S(1)}, u32[]{:S(2)}, u32[]{:S(2)}) collective-permute-start(bf16[96,384]{1,0:T(8,128)(2,1)S(1)} %get-tuple-element.46), channel_id=1, source_target_pairs={{0,8},{4,12},{8,0},{12,4},{16,24},{20,28},{24,16},{28,20},{1,9},{5... | collective-permute-start | bytes 221192 | tf_op jit(solution)/shard_map/ppermute | solution.py:463
  33.2 5.2 %collective-permute-start.11 = (bf16[96,384]{1,0:T(8,128)(2,1)S(1)}, bf16[96,384]{1,0:T(8,128)(2,1)S(1)}, u32[]{:S(2)}, u32[]{:S(2)}) collective-permute-start(bf16[96,384]{1,0:T(8,128)(2,1)S(1)} %get-tuple-element.47), channel_id=1, source_target_pairs={{0,16},{4,20},{8,24},{12,28},{16,0},{20,4},{24,8},{28,12},{1,17},{... | collective-permute-start | bytes 221192 | tf_op jit(solution)/shard_map/ppermute | solution.py:463
  34.3 5.1 %collective-permute-start.12 = (bf16[96,384]{1,0:T(8,128)(2,1)S(1)}, bf16[96,384]{1,0:T(8,128)(2,1)S(1)}, u32[]{:S(2)}, u32[]{:S(2)}) collective-permute-start(bf16[96,384]{1,0:T(8,128)(2,1)S(1)} %get-tuple-element.48), channel_id=1, source_target_pairs={{0,12},{4,8},{8,4},{12,0},{16,28},{20,24},{24,20},{28,16},{1,13},{... | collective-permute-start | bytes 221192 | tf_op jit(solution)/shard_map/ppermute | solution.py:463
  34.4 5.2 %collective-permute-start.13 = (bf16[96,384]{1,0:T(8,128)(2,1)S(1)}, bf16[96,384]{1,0:T(8,128)(2,1)S(1)}, u32[]{:S(2)}, u32[]{:S(2)}) collective-permute-start(bf16[96,384]{1,0:T(8,128)(2,1)S(1)} %get-tuple-element.49), channel_id=1, source_target_pairs={{0,20},{4,16},{8,28},{12,24},{16,4},{20,0},{24,12},{28,8},{1,21},{... | collective-permute-start | bytes 221192 | tf_op jit(solution)/shard_map/ppermute | solution.py:463
  36.4 3.2 %collective-permute-start.14 = (bf16[96,384]{1,0:T(8,128)(2,1)S(1)}, bf16[96,384]{1,0:T(8,128)(2,1)S(1)}, u32[]{:S(2)}, u32[]{:S(2)}) collective-permute-start(bf16[96,384]{1,0:T(8,128)(2,1)S(1)} %get-tuple-element.50), channel_id=1, source_target_pairs={{0,4},{4,0},{8,12},{12,8},{16,20},{20,16},{24,28},{28,24},{1,5},{5... | collective-permute-start | bytes 221192 | tf_op jit(solution)/shard_map/ppermute | solution.py:463

commit v23 on v22

--- a/solution.py
+++ b/solution.py
@@ -152,80 +152,79 @@
     return found
 
 
-def attend_images(images, ids_ref, keys, values, queries, attended, work, starts, halo):
-    scores_a, scores_b, tops_a, tops_b = work
-    query_base = halo
-    window, tile = scores_a.shape
-    size = attended.shape[0] - SPARE
-    held = queries.shape[1]
+def list_pairs(images, held, tile, last_begin, base, starts, table):
     tiles = held // tile
     shift = tile.bit_length() - 1
+    low = image_at(images, starts, base)
+    high = image_at(images, starts, base + held - 1)
 
     def bounds(image):
-        first = jnp.maximum(starts[image] - query_base, 0) >> shift
-        last = (jnp.minimum(starts[image + 1] - query_base, held) - 1) >> shift
+        first = jnp.maximum(starts[image] - base, 0) >> shift
+        last = (jnp.minimum(starts[image + 1] - base, held) - 1) >> shift
         return jnp.minimum(first, tiles - 1), last
 
-    def after(image):
-        return jnp.minimum(image + 1, images - 1)
-
-    def following(state):
-        at, image = state
-        more = at < bounds(image)[1]
-        later = after(image)
-        return jnp.where(more, at + 1, bounds(later)[0]), jnp.where(more, image, later)
-
-    def window_of(image):
-        begin = jnp.bitwise_and(starts[image], -LANES)
-        return pl.ds(pl.multiple_of(jnp.minimum(begin, keys.shape[0] - window), LANES), window)
-
-    def score(state, scores, tops):
-        at, image = state
-        query = queries[:, pl.ds(pl.multiple_of(at * tile, tile), tile)]
-        found = jnp.dot(keys[window_of(image), :], query, preferred_element_type=jnp.float32)
-        scores[...] = found
-        tops[...] = jnp.max(found, axis=0, keepdims=True)
-
-    def weigh(state, scores, tops):
-        at, image = state
-        first = pl.multiple_of(at * tile, tile)
-        labels = ids_ref[:, pl.ds(pl.multiple_of(query_base + first, LANES), tile)]
-        probs = jnp.exp2((scores[...] - tops[...]) * (size ** (-0.5) * math.log2(math.e)))
-        share = 1.0 / jnp.sum(probs, axis=0, keepdims=True)
-        weighted = jnp.dot(
-            values[:, window_of(image)], probs.astype(jnp.bfloat16), preferred_element_type=jnp.float32
-        )
-        place = (slice(None), pl.ds(first, tile))
-        attended[place] = jnp.where(labels == image, weighted * share, attended[place])
-
-    low = image_at(images, starts, query_base)
-    high = image_at(images, starts, query_base + held - 1)
     pairs = jnp.int32(0)
     for image in range(images):
         first, last = bounds(image)
         wanted = jnp.logical_and(low <= image, image <= high)
         pairs += jnp.where(wanted, last - first + 1, 0)
-
-    def two_pairs(_, state):
-        second = following(state)
-        score(second, scores_b, tops_b)
+    at, image = jnp.int32(0), low
+    for step in range(tiles + images):
+        table[0, step] = at
+        table[1, step] = image
+        table[2, step] = jnp.minimum(jnp.bitwise_and(starts[image], -LANES), last_begin)
+        more = at < bounds(image)[1]
+        later = jnp.minimum(image + 1, images - 1)
+        at, image = jnp.where(more, at + 1, bounds(later)[0]), jnp.where(more, image, later)
+    return pairs
+
+
+def attend_images(pairs, table, ids_ref, keys, values, queries, attended, work, query_base):
+    scores_a, scores_b, tops_a, tops_b = work
+    window, tile = scores_a.shape
+    size = attended.shape[0] - SPARE
+
+    def window_of(state):
+        return pl.ds(pl.multiple_of(table[2, state], LANES), window)
+
+    def score(state, scores, tops):
+        query = queries[:, pl.ds(pl.multiple_of(table[0, state] * tile, tile), tile)]
+        found = jnp.dot(keys[window_of(state), :], query, preferred_element_type=jnp.float32)
+        scores[...] = found
+        tops[...] = jnp.max(found, axis=0, keepdims=True)
+
+    def weigh(state, scores, tops):
+        first = pl.multiple_of(table[0, state] * tile, tile)
+        labels = ids_ref[:, pl.ds(pl.multiple_of(query_base + first, LANES), tile)]
+        probs = jnp.exp2((scores[...] - tops[...]) * (size ** (-0.5) * math.log2(math.e)))
+        share = 1.0 / jnp.sum(probs, axis=0, keepdims=True)
+        weighted = jnp.dot(
+            values[:, window_of(state)], probs.astype(jnp.bfloat16), preferred_element_type=jnp.float32
+        )
+        place = (slice(None), pl.ds(first, tile))
+        attended[place] = jnp.where(labels == table[1, state], weighted * share, attended[place])
+
+    def two_pairs(state):
+        score(state + 1, scores_b, tops_b)
         weigh(state, scores_a, tops_a)
-        third = following(second)
-        score(third, scores_a, tops_a)
-        weigh(second, scores_b, tops_b)
-        return third
-
-    def four_pairs(step, state):
-        return two_pairs(step, two_pairs(step, state))
-
-    begun = (jnp.int32(0), low)
-    score(begun, scores_a, tops_a)
-    reached = lax.fori_loop(0, lax.div(pairs, 4), four_pairs, begun)
-    reached = lax.fori_loop(0, lax.div(lax.rem(pairs, 4), 2), two_pairs, reached)
-
-    @pl.when(lax.rem(pairs, 2) == 1)
+        score(state + 2, scores_a, tops_a)
+        weigh(state + 1, scores_b, tops_b)
+
+    def four_pairs(step, _):
+        two_pairs(4 * step)
+        two_pairs(4 * step + 2)
+        return 0
+
+    score(0, scores_a, tops_a)
+    lax.fori_loop(0, pairs >> 2, four_pairs, 0)
+
+    @pl.when(jnp.bitwise_and(pairs, 2) == 2)
     def _():
-        weigh(reached, scores_a, tops_a)
+        two_pairs(jnp.bitwise_and(pairs, -4))
+
+    @pl.when(jnp.bitwise_and(pairs, 1) == 1)
+    def _():
+        weigh(pairs - 1, scores_a, tops_a)
 
 
 def turned_keys(marked, block_ref):
@@ -276,7 +275,7 @@
     if halo:
         left_ref, right_ref, *rest = rest
     out_refs, rest = rest[:HEADS], rest[HEADS:]
-    keys, values, queries, attended, *work, starts = rest
+    keys, values, queries, attended, *work, starts, table = rest
     count = got_refs[0].shape[1]
     padded = attended.shape[0]
     size = padded - SPARE
@@ -286,6 +285,8 @@
     before = before_ref[...]
     for image in range(images + 1):
         starts[image] = before[image, 0]
+    window, tile = work[0].shape
+    pairs = list_pairs(images, total_rows, tile, length - window, halo, starts, table)
 
     own = lax.rem(lax.axis_index("grp"), HEADS)
     for step, (by, ref) in enumerate(zip(EARLY + LATE, got_refs)):
@@ -302,7 +303,7 @@
         for ref, here in ((left_ref, slice(0, halo)), (right_ref, slice(length - halo, length))):
             keys[here, :] = turned_keys(marks[0, :, here], ref)
             values[:, here] = ref[0:PADDED]
-    attend_images(images, ids_ref, keys, values, queries, attended, work, starts, halo)
+    attend_images(pairs, table, ids_ref, keys, values, queries, attended, work, halo)
 
     odd_head = lax.rem(own, 2) == 1
     mine = ids[:, halo : halo + total_rows]
@@ -592,6 +593,7 @@
             pltpu.VMEM((1, tile), f32),
             pltpu.VMEM((1, tile), f32),
             pltpu.SMEM((images + 1,), jnp.int32),
+            pltpu.SMEM((3, length // tile + images), jnp.int32),
         ],
         in_vmem(len(operands)),
         4 * size * length * MAXP,

time: 42.1 us -> 41.8 us (level)
  no operation moved by 1% of the time
where the time goes in v23:
time: 41.8 us; the launch traced here: 41.7 us
  starting transfers between devices  17.6 us (42%)
  Pallas kernels  14.6 us (35%)
  waiting for transfers between devices  8.76 us (21%)
  between operations  0.69 us (2%)
    ppermute x15, starting transfers between devices, moved(): return lax.ppermute(value, axis, pairs)  17.6 us
    ppermute x15, waiting for transfers between devices, moved(): return lax.ppermute(value, axis, pairs)  8.76 us
    pallas_call x1, Pallas kernels, local(): call(functools.partial(attend_kernel, images, piggy, halo), (shape((padde...  6.06 us
    pallas_call x1, Pallas kernels, local(): call(functools.partial(far_kernel, images, piggy), (shape((depth, count),...  2.8 us
    pallas_call x1, Pallas kernels, local(): call(functools.partial(finish_kernel, images), (shape((count, depth), bf1...  2.13 us
    pallas_call x1, Pallas kernels, local(): call(functools.partial(near_kernel, piggy), (block,) * 6, [], in_vmem(3),...  1.95 us
    pallas_call x1, Pallas kernels, local(): call(functools.partial(prepare_kernel, images, halo), (shape((len(EARLY)...  1.64 us
  transfers between devices with their start and end apart: 15, of which 9 were waited for; matrix products, arithmetic and copies ran while one was open for 0% of the time, Pallas kernels for 9%

profile of v23, /device:TPU:0, one launch (start us, length us, event | category | flops | bytes accessed | tf_op | source)
XLA Modules:
  0.0 41.7 jit_solution(2519167039501472079)
XLA Ops:
  0.6 0.0 copy-start
  0.6 2.8 %shard_map.68 = (bf16[1152,384]{1,0:T(8,128)(2,1)S(1)}, f32[8,1152]{1,0:T(8,128)S(1)}, bf16[224,384]{1,0:T(8,128)(2,1)S(1)}, bf16[224,384]{1,0:T(8,128)(2,1)S(1)}) custom-call(s32[1,3072]{1,0:T(1,128)} %ids_ref.5, bf16[384,1152]{1,0:T(8,128)(2,1)} %bitcast.6, bf16[1728,1152]{1,0:T(8,128)(2,1)} %bitcast.4), custom_call_target="tpu_custom_call" | custom-call | flops 382205952 | bytes 8388608 | tf_op jit(solution)/shard_map/pallas_call | solution.py:515
  3.4 4.0 %collective-permute-start = (bf16[224,384]{1,0:T(8,128)(2,1)S(1)}, bf16[224,384]{1,0:T(8,128)(2,1)S(1)}, u32[]{:S(2)}, u32[]{:S(2)}) collective-permute-start(bf16[224,384]{1,0:T(8,128)(2,1)S(1)} %get-tuple-element.28), channel_id=1, source_target_pairs={{0,24},{4,28},{8,16},{12,20},{16,8},{20,12},{24,0},{28,4},{1,25},{... | collective-permute-start | bytes 516104 | tf_op jit(solution)/shard_map/ppermute | solution.py:464
  7.4 0.0 collective-permute-start.1
  7.4 0.0 copy-done
  7.4 0.0 copy-start.3
  7.4 0.0 copy-start.2
  7.4 1.9 %shard_map.69 = (bf16[224,384]{1,0:T(8,128)(2,1)S(1)}, bf16[224,384]{1,0:T(8,128)(2,1)S(1)}, bf16[224,384]{1,0:T(8,128)(2,1)S(1)}, bf16[224,384]{1,0:T(8,128)(2,...) custom-call(bf16[1152,384]{1,0:T(8,128)(2,1)S(1)} %get-tuple-element.30.normed_ref, ...), custom_call_target="tpu_custom_call" | custom-call | flops 1146617856 | bytes 8388608 | tf_op jit(solution)/shard_map/pallas_call | solution.py:529
  9.4 0.2 collective-permute-start.2
  9.6 1.9 %collective-permute-start.3 = (bf16[224,384]{1,0:T(8,128)(2,1)S(1)}, bf16[224,384]{1,0:T(8,128)(2,1)S(1)}, u32[]{:S(2)}, u32[]{:S(2)}) collective-permute-start(bf16[224,384]{1,0:T(8,128)(2,1)S(1)} %get-tuple-element.39), channel_id=1, source_target_pairs={{0,8},{4,12},{8,0},{12,4},{16,24},{20,28},{24,16},{28,20},{1,9},{5... | collective-permute-start | bytes 516104 | tf_op jit(solution)/shard_map/ppermute | solution.py:464
  11.5 1.5 %collective-permute-start.4 = (bf16[224,384]{1,0:T(8,128)(2,1)S(1)}, bf16[224,384]{1,0:T(8,128)(2,1)S(1)}, u32[]{:S(2)}, u32[]{:S(2)}) collective-permute-start(bf16[224,384]{1,0:T(8,128)(2,1)S(1)} %get-tuple-element.40), channel_id=1, source_target_pairs={{0,16},{4,20},{8,24},{12,28},{16,0},{20,4},{24,8},{28,12},{1,17},{... | collective-permute-start | bytes 516104 | tf_op jit(solution)/shard_map/ppermute | solution.py:464
  13.0 0.0 collective-permute-done.rest_0_
  13.0 0.0 collective-permute-start.5
  13.0 2.9 %collective-permute-done.1.rest_1_ = bf16[224,384]{1,0:T(8,128)(2,1)S(1)} collective-permute-done((bf16[224,384]{1,0:T(8,128)(2,1)S(1)}, bf16[224,384]{1,0:T(8,128)(2,1)S(1)}, u32[]{:S(2)}, u32[]{:S(2)}) %collective-permute-start.1) | collective-permute-done | bytes 172064 | tf_op jit(solution)/shard_map/ppermute | solution.py:464
  15.9 1.9 %collective-permute-start.6 = (bf16[224,384]{1,0:T(8,128)(2,1)S(1)}, bf16[224,384]{1,0:T(8,128)(2,1)S(1)}, u32[]{:S(2)}, u32[]{:S(2)}) collective-permute-start(bf16[224,384]{1,0:T(8,128)(2,1)S(1)} %get-tuple-element.42), channel_id=1, source_target_pairs={{0,20},{4,16},{8,28},{12,24},{16,4},{20,0},{24,12},{28,8},{1,21},{... | collective-permute-start | bytes 516104 | tf_op jit(solution)/shard_map/ppermute | solution.py:464
  17.8 0.0 collective-permute-done.2.rest_2_
  17.8 0.0 copy-done.3
  17.8 1.6 %collective-permute-start.7 = (bf16[4,1152]{1,0:T(4,128)(2,1)S(1)}, bf16[4,1152]{1,0:T(4,128)(2,1)S(1)}, u32[]{:S(2)}, u32[]{:S(2)}) collective-permute-start(bf16[4,1152]{1,0:T(4,128)(2,1)S(1)} %copy-done.3), channel_id=1, source_target_pairs={{1,0},{0,1},{3,2},{2,3},{6,4},{7,5},{4,6},{5,7},{11,8},{10,9},{9,1... | collective-permute-start | bytes 27656 | tf_op jit(solution)/shard_map/ppermute | solution.py:464
  19.3 0.0 copy-done.2
  19.3 1.6 %shard_map.70 = (bf16[1536,128]{1,0:T(8,128)(2,1)S(1)}, f32[2,8,3072]{2,1,0:T(8,128)S(1)}, s32[8,128]{1,0:T(8,128)S(1)}, bf16[640,1152]{1,0:T(8,128)(2,1)S(1)}) custom-call(s32[1,3072]{1,0:T(1,128)S(1)} %copy-done.2, bf16[576,1152]{1,0:T(8,128)(2,1)} %out_weight_ref.1, bf16[224,384]{1,0:T(8,128)(2,1)S(1)} %collective-permute-done.rest_0_, ...), custom_call_target="tpu_custom_call" | custom-call | flops 1073741824 | bytes 8388608 | tf_op jit(solution)/shard_map/pallas_call | solution.py:570
  21.0 0.4 %collective-permute-done.7.rest_8_ = bf16[4,1152]{1,0:T(4,128)(2,1)S(1)} collective-permute-done((bf16[4,1152]{1,0:T(4,128)(2,1)S(1)}, bf16[4,1152]{1,0:T(4,128)(2,1)S(1)}, u32[]{:S(2)}, u32[]{:S(2)}) %collective-permute-start.7) | collective-permute-done | bytes 9248 | tf_op jit(solution)/shard_map/ppermute | solution.py:464
  21.4 0.0 collective-permute-done.3.rest_4_
  21.4 0.0 collective-permute-done.4.rest_5_
  21.4 0.7 %collective-permute-done.5.rest_6_ = bf16[224,384]{1,0:T(8,128)(2,1)S(1)} collective-permute-done((bf16[224,384]{1,0:T(8,128)(2,1)S(1)}, bf16[224,384]{1,0:T(8,128)(2,1)S(1)}, u32[]{:S(2)}, u32[]{:S(2)}) %collective-permute-start.5) | collective-permute-done | bytes 172064 | tf_op jit(solution)/shard_map/ppermute | solution.py:464
  22.1 0.6 %collective-permute-done.6.rest_7_ = bf16[224,384]{1,0:T(8,128)(2,1)S(1)} collective-permute-done((bf16[224,384]{1,0:T(8,128)(2,1)S(1)}, bf16[224,384]{1,0:T(8,128)(2,1)S(1)}, u32[]{:S(2)}, u32[]{:S(2)}) %collective-permute-start.6) | collective-permute-done | bytes 172064 | tf_op jit(solution)/shard_map/ppermute | solution.py:464
  22.7 0.0 copy-start.1
  22.7 6.1 %shard_map.71 = (bf16[96,384]{1,0:T(8,128)(2,1)S(1)}, bf16[96,384]{1,0:T(8,128)(2,1)S(1)}, bf16[96,384]{1,0:T(8,128)(2,1)S(1)}, bf16[96,384]{1,0:T(8,128)(2,1)S(...) custom-call(s32[1,3072]{1,0:T(1,128)S(1)} %copy-done.2, ...), custom_call_target="tpu_custom_call" | custom-call | flops 905969664 | bytes 8388608 | tf_op jit(solution)/shard_map/pallas_call | solution.py:583
  28.8 2.3 %collective-permute-start.8 = (bf16[96,384]{1,0:T(8,128)(2,1)S(1)}, bf16[96,384]{1,0:T(8,128)(2,1)S(1)}, u32[]{:S(2)}, u32[]{:S(2)}) collective-permute-start(bf16[96,384]{1,0:T(8,128)(2,1)S(1)} %get-tuple-element.44), channel_id=1, source_target_pairs={{0,24},{4,28},{8,16},{12,20},{16,8},{20,12},{24,0},{28,4},{1,25},{... | collective-permute-start | bytes 221192 | tf_op jit(solution)/shard_map/ppermute | solution.py:464
  31.1 0.2 collective-permute-start.9
  31.3 1.8 %collective-permute-start.10 = (bf16[96,384]{1,0:T(8,128)(2,1)S(1)}, bf16[96,384]{1,0:T(8,128)(2,1)S(1)}, u32[]{:S(2)}, u32[]{:S(2)}) collective-permute-start(bf16[96,384]{1,0:T(8,128)(2,1)S(1)} %get-tuple-element.46), channel_id=1, source_target_pairs={{0,8},{4,12},{8,0},{12,4},{16,24},{20,28},{24,16},{28,20},{1,9},{5... | collective-permute-start | bytes 221192 | tf_op jit(solution)/shard_map/ppermute | solution.py:464
  33.1 1.1 %collective-permute-start.11 = (bf16[96,384]{1,0:T(8,128)(2,1)S(1)}, bf16[96,384]{1,0:T(8,128)(2,1)S(1)}, u32[]{:S(2)}, u32[]{:S(2)}) collective-permute-start(bf16[96,384]{1,0:T(8,128)(2,1)S(1)} %get-tuple-element.47), channel_id=1, source_target_pairs={{0,16},{4,20},{8,24},{12,28},{16,0},{20,4},{24,8},{28,12},{1,17},{... | collective-permute-start | bytes 221192 | tf_op jit(solution)/shard_map/ppermute | solution.py:464
  34.2 0.0 collective-permute-start.12
  34.3 0.0 collective-permute-done.8.rest_0_
  34.3 0.8 %collective-permute-start.13 = (bf16[96,384]{1,0:T(8,128)(2,1)S(1)}, bf16[96,384]{1,0:T(8,128)(2,1)S(1)}, u32[]{:S(2)}, u32[]{:S(2)}) collective-permute-start(bf16[96,384]{1,0:T(8,128)(2,1)S(1)} %get-tuple-element.49), channel_id=1, source_target_pairs={{0,20},{4,16},{8,28},{12,24},{16,4},{20,0},{24,12},{28,8},{1,21},{... | collective-permute-start | bytes 221192 | tf_op jit(solution)/shard_map/ppermute | solution.py:464
  35.1 1.2 %collective-permute-done.9.rest_1_ = bf16[96,384]{1,0:T(8,128)(2,1)S(1)} collective-permute-done((bf16[96,384]{1,0:T(8,128)(2,1)S(1)}, bf16[96,384]{1,0:T(8,128)(2,1)S(1)}, u32[]{:S(2)}, u32[]{:S(2)}) %collective-permute-start.9) | collective-permute-done | bytes 73760 | tf_op jit(solution)/shard_map/ppermute | solution.py:464
  36.3 0.3 collective-permute-start.14
  36.6 1.0 %collective-permute-done.10.rest_2_ = bf16[96,384]{1,0:T(8,128)(2,1)S(1)} collective-permute-done((bf16[96,384]{1,0:T(8,128)(2,1)S(1)}, bf16[96,384]{1,0:T(8,128)(2,1)S(1)}, u32[]{:S(2)}, u32[]{:S(2)}) %collective-permute-start.10) | collective-permute-done | bytes 73760 | tf_op jit(solution)/shard_map/ppermute | solution.py:464
  37.6 0.7 %collective-permute-done.11.rest_3_ = bf16[96,384]{1,0:T(8,128)(2,1)S(1)} collective-permute-done((bf16[96,384]{1,0:T(8,128)(2,1)S(1)}, bf16[96,384]{1,0:T(8,128)(2,1)S(1)}, u32[]{:S(2)}, u32[]{:S(2)}) %collective-permute-start.11) | collective-permute-done | bytes 73760 | tf_op jit(solution)/shard_map/ppermute | solution.py:464
  38.3 1.1 %collective-permute-done.12.rest_4_ = bf16[96,384]{1,0:T(8,128)(2,1)S(1)} collective-permute-done((bf16[96,384]{1,0:T(8,128)(2,1)S(1)}, bf16[96,384]{1,0:T(8,128)(2,1)S(1)}, u32[]{:S(2)}, u32[]{:S(2)}) %collective-permute-start.12) | collective-permute-done | bytes 73760 | tf_op jit(solution)/shard_map/ppermute | solution.py:464
  39.4 0.2 collective-permute-done.13.rest_5_
  39.5 0.0 collective-permute-done.14.rest_6_
  39.5 0.0 copy-done.1
  39.5 2.1 %shard_map.72 = (bf16[384,1152]{1,0:T(8,128)(2,1)}, f32[1,4]{1,0:T(1,128)}) custom-call(bf16[384,1152]{1,0:T(8,128)(2,1)S(1)} %bitcast.7, bf16[640,1152]{1,0:T(8,128)(2,1)S(1)} %get-tuple-element.35.weight_ref, bf16[4,1152]{1,0:T(4,128)(2,1)S(1)} %copy-done.3, bf16[96,384]{1,0:T(8,128)(2,1)S(1)} %collective-permute-done.8.rest_0_, ...), custom_call_target="tpu_custom_call" | custom-call | flops 509607936 | bytes 8388608 | tf_op jit(solution)/shard_map/pallas_call | solution.py:612
Async XLA Ops:
  0.6 6.8 %copy-start = (bf16[1152,1728]{0,1:T(8,128)(2,1)S(1)}, bf16[1152,1728]{0,1:T(8,128)(2,1)}, u32[]{:S(2)}) copy-start(bf16[1152,1728]{0,1:T(8,128)(2,1)} %param.7) | copy-start | bytes 11943940
  3.4 9.6 %collective-permute-start = (bf16[224,384]{1,0:T(8,128)(2,1)S(1)}, bf16[224,384]{1,0:T(8,128)(2,1)S(1)}, u32[]{:S(2)}, u32[]{:S(2)}) collective-permute-start(bf16[224,384]{1,0:T(8,128)(2,1)S(1)} %get-tuple-element.28), channel_id=1, source_target_pairs={{0,24},{4,28},{8,16},{12,20},{16,8},{20,12},{24,0},{28,4},{1,25},{... | collective-permute-start | bytes 516104 | tf_op jit(solution)/shard_map/ppermute | solution.py:464
  7.4 8.5 %collective-permute-start.1 = (bf16[224,384]{1,0:T(8,128)(2,1)S(1)}, bf16[224,384]{1,0:T(8,128)(2,1)S(1)}, u32[]{:S(2)}, u32[]{:S(2)}) collective-permute-start(bf16[224,384]{1,0:T(8,128)(2,1)S(1)} %get-tuple-element.29), channel_id=1, source_target_pairs={{0,28},{4,24},{8,20},{12,16},{16,12},{20,8},{24,4},{28,0},{1,29},{... | collective-permute-start | bytes 516104 | tf_op jit(solution)/shard_map/ppermute | solution.py:464
  7.4 10.4 %copy-start.3 = (bf16[4,1152]{1,0:T(4,128)(2,1)S(1)}, bf16[4,1152]{1,0:T(4,128)(2,1)}, u32[]{:S(2)}) copy-start(bf16[4,1152]{1,0:T(4,128)(2,1)} %text_ref.1) | copy-start | bytes 27652
  7.4 11.9 %copy-start.2 = (s32[1,3072]{1,0:T(1,128)S(1)}, s32[1,3072]{1,0:T(1,128)}, u32[]{:S(2)}) copy-start(s32[1,3072]{1,0:T(1,128)} %ids_ref.5) | copy-start | bytes 36868
  9.4 8.4 %collective-permute-start.2 = (bf16[224,384]{1,0:T(8,128)(2,1)S(1)}, bf16[224,384]{1,0:T(8,128)(2,1)S(1)}, u32[]{:S(2)}, u32[]{:S(2)}) collective-permute-start(bf16[224,384]{1,0:T(8,128)(2,1)S(1)} %get-tuple-element.32), channel_id=1, source_target_pairs={{0,4},{4,0},{8,12},{12,8},{16,20},{20,16},{24,28},{28,24},{1,5},{5... | collective-permute-start | bytes 516104 | tf_op jit(solution)/shard_map/ppermute | solution.py:464
  9.6 11.8 %collective-permute-start.3 = (bf16[224,384]{1,0:T(8,128)(2,1)S(1)}, bf16[224,384]{1,0:T(8,128)(2,1)S(1)}, u32[]{:S(2)}, u32[]{:S(2)}) collective-permute-start(bf16[224,384]{1,0:T(8,128)(2,1)S(1)} %get-tuple-element.39), channel_id=1, source_target_pairs={{0,8},{4,12},{8,0},{12,4},{16,24},{20,28},{24,16},{28,20},{1,9},{5... | collective-permute-start | bytes 516104 | tf_op jit(solution)/shard_map/ppermute | solution.py:464
  11.5 9.9 %collective-permute-start.4 = (bf16[224,384]{1,0:T(8,128)(2,1)S(1)}, bf16[224,384]{1,0:T(8,128)(2,1)S(1)}, u32[]{:S(2)}, u32[]{:S(2)}) collective-permute-start(bf16[224,384]{1,0:T(8,128)(2,1)S(1)} %get-tuple-element.40), channel_id=1, source_target_pairs={{0,16},{4,20},{8,24},{12,28},{16,0},{20,4},{24,8},{28,12},{1,17},{... | collective-permute-start | bytes 516104 | tf_op jit(solution)/shard_map/ppermute | solution.py:464
  13.0 9.1 %collective-permute-start.5 = (bf16[224,384]{1,0:T(8,128)(2,1)S(1)}, bf16[224,384]{1,0:T(8,128)(2,1)S(1)}, u32[]{:S(2)}, u32[]{:S(2)}) collective-permute-start(bf16[224,384]{1,0:T(8,128)(2,1)S(1)} %get-tuple-element.41), channel_id=1, source_target_pairs={{0,12},{4,8},{8,4},{12,0},{16,28},{20,24},{24,20},{28,16},{1,13},{... | collective-permute-start | bytes 516104 | tf_op jit(solution)/shard_map/ppermute | solution.py:464
  15.9 6.9 %collective-permute-start.6 = (bf16[224,384]{1,0:T(8,128)(2,1)S(1)}, bf16[224,384]{1,0:T(8,128)(2,1)S(1)}, u32[]{:S(2)}, u32[]{:S(2)}) collective-permute-start(bf16[224,384]{1,0:T(8,128)(2,1)S(1)} %get-tuple-element.42), channel_id=1, source_target_pairs={{0,20},{4,16},{8,28},{12,24},{16,4},{20,0},{24,12},{28,8},{1,21},{... | collective-permute-start | bytes 516104 | tf_op jit(solution)/shard_map/ppermute | solution.py:464
  17.8 3.7 %collective-permute-start.7 = (bf16[4,1152]{1,0:T(4,128)(2,1)S(1)}, bf16[4,1152]{1,0:T(4,128)(2,1)S(1)}, u32[]{:S(2)}, u32[]{:S(2)}) collective-permute-start(bf16[4,1152]{1,0:T(4,128)(2,1)S(1)} %copy-done.3), channel_id=1, source_target_pairs={{1,0},{0,1},{3,2},{2,3},{6,4},{7,5},{4,6},{5,7},{11,8},{10,9},{9,1... | collective-permute-start | bytes 27656 | tf_op jit(solution)/shard_map/ppermute | solution.py:464
  22.7 16.8 %copy-start.1 = (bf16[1,384,1152]{2,1,0:T(8,128)(2,1)S(1)}, bf16[1,384,1152]{2,1,0:T(8,128)(2,1)}, u32[]{:S(2)}) copy-start(bf16[1,384,1152]{2,1,0:T(8,128)(2,1)} %param.5) | copy-start | bytes 2654212
  28.8 5.5 %collective-permute-start.8 = (bf16[96,384]{1,0:T(8,128)(2,1)S(1)}, bf16[96,384]{1,0:T(8,128)(2,1)S(1)}, u32[]{:S(2)}, u32[]{:S(2)}) collective-permute-start(bf16[96,384]{1,0:T(8,128)(2,1)S(1)} %get-tuple-element.44), channel_id=1, source_target_pairs={{0,24},{4,28},{8,16},{12,20},{16,8},{20,12},{24,0},{28,4},{1,25},{... | collective-permute-start | bytes 221192 | tf_op jit(solution)/shard_map/ppermute | solution.py:464
  31.1 5.2 %collective-permute-start.9 = (bf16[96,384]{1,0:T(8,128)(2,1)S(1)}, bf16[96,384]{1,0:T(8,128)(2,1)S(1)}, u32[]{:S(2)}, u32[]{:S(2)}) collective-permute-start(bf16[96,384]{1,0:T(8,128)(2,1)S(1)} %get-tuple-element.45), channel_id=1, source_target_pairs={{0,28},{4,24},{8,20},{12,16},{16,12},{20,8},{24,4},{28,0},{1,29},{... | collective-permute-start | bytes 221192 | tf_op jit(solution)/shard_map/ppermute | solution.py:464
  31.3 6.3 %collective-permute-start.10 = (bf16[96,384]{1,0:T(8,128)(2,1)S(1)}, bf16[96,384]{1,0:T(8,128)(2,1)S(1)}, u32[]{:S(2)}, u32[]{:S(2)}) collective-permute-start(bf16[96,384]{1,0:T(8,128)(2,1)S(1)} %get-tuple-element.46), channel_id=1, source_target_pairs={{0,8},{4,12},{8,0},{12,4},{16,24},{20,28},{24,16},{28,20},{1,9},{5... | collective-permute-start | bytes 221192 | tf_op jit(solution)/shard_map/ppermute | solution.py:464
  33.1 5.2 %collective-permute-start.11 = (bf16[96,384]{1,0:T(8,128)(2,1)S(1)}, bf16[96,384]{1,0:T(8,128)(2,1)S(1)}, u32[]{:S(2)}, u32[]{:S(2)}) collective-permute-start(bf16[96,384]{1,0:T(8,128)(2,1)S(1)} %get-tuple-element.47), channel_id=1, source_target_pairs={{0,16},{4,20},{8,24},{12,28},{16,0},{20,4},{24,8},{28,12},{1,17},{... | collective-permute-start | bytes 221192 | tf_op jit(solution)/shard_map/ppermute | solution.py:464
  34.2 5.1 %collective-permute-start.12 = (bf16[96,384]{1,0:T(8,128)(2,1)S(1)}, bf16[96,384]{1,0:T(8,128)(2,1)S(1)}, u32[]{:S(2)}, u32[]{:S(2)}) collective-permute-start(bf16[96,384]{1,0:T(8,128)(2,1)S(1)} %get-tuple-element.48), channel_id=1, source_target_pairs={{0,12},{4,8},{8,4},{12,0},{16,28},{20,24},{24,20},{28,16},{1,13},{... | collective-permute-start | bytes 221192 | tf_op jit(solution)/shard_map/ppermute | solution.py:464
  34.3 5.2 %collective-permute-start.13 = (bf16[96,384]{1,0:T(8,128)(2,1)S(1)}, bf16[96,384]{1,0:T(8,128)(2,1)S(1)}, u32[]{:S(2)}, u32[]{:S(2)}) collective-permute-start(bf16[96,384]{1,0:T(8,128)(2,1)S(1)} %get-tuple-element.49), channel_id=1, source_target_pairs={{0,20},{4,16},{8,28},{12,24},{16,4},{20,0},{24,12},{28,8},{1,21},{... | collective-permute-start | bytes 221192 | tf_op jit(solution)/shard_map/ppermute | solution.py:464
  36.3 3.2 %collective-permute-start.14 = (bf16[96,384]{1,0:T(8,128)(2,1)S(1)}, bf16[96,384]{1,0:T(8,128)(2,1)S(1)}, u32[]{:S(2)}, u32[]{:S(2)}) collective-permute-start(bf16[96,384]{1,0:T(8,128)(2,1)S(1)} %get-tuple-element.50), channel_id=1, source_target_pairs={{0,4},{4,0},{8,12},{12,8},{16,20},{20,16},{24,28},{28,24},{1,5},{5... | collective-permute-start | bytes 221192 | tf_op jit(solution)/shard_map/ppermute | solution.py:464

commit v24 on v23

--- a/solution.py
+++ b/solution.py
@@ -17,6 +17,7 @@
 KEY_AT = SIZE - SPARE
 QUERY_AT = 2 * SIZE
 TEXT_ROWS = 16
+RUN = 5
 HIDDEN = -1e30
 ORDER = (6, 7, 2, 4, 3, 5, 1, 0)
 EARLY = (6, 7, 1, 0)
@@ -69,12 +70,17 @@
     return lax.div(own, 2), lax.rem(own, 2)
 
 
-def far_kernel(images, piggy, ids_ref, rows_ref, weight_ref, normed_ref, sums_ref, same_ref, cross_ref, own_ids, rows_held, weight, id_sem, row_sem, sems):
+def far_kernel(images, piggy, ids_ref, rows_ref, weight_ref, normed_ref, sums_ref, same_ref, cross_ref, own_ids, rows_held, weight, id_sem, row_sems, sems):
     count, depth = rows_ref.shape
     width = weight_ref.shape[0] // 3
     wide = weight.shape[1]
-    rows_fetch = pltpu.make_async_copy(rows_ref, rows_held, row_sem)
-    rows_fetch.start()
+    pieces = row_sems.shape[0]
+    step = count // pieces
+    row_fetches = []
+    for piece in range(pieces):
+        cut = slice(piece * step, (piece + 1) * step)
+        row_fetches.append(pltpu.make_async_copy(rows_ref.at[cut], rows_held.at[cut], row_sems.at[piece]))
+        row_fetches[-1].start()
     own = pl.multiple_of(lax.axis_index("grp") * count, LANES)
     ids_fetch = pltpu.make_async_copy(ids_ref.at[:, pl.ds(own, count)], own_ids, id_sem)
     ids_fetch.start()
@@ -87,7 +93,8 @@
     for fetch in fetches:
         fetch.start()
     ids_fetch.wait()
-    rows_fetch.wait()
+    for fetch in row_fetches:
+        fetch.wait()
     rows = rows_held[...]
     if piggy:
         sums = jnp.dot(image_rows(own_ids[...], images), rows, preferred_element_type=jnp.float32)
@@ -169,7 +176,7 @@
         wanted = jnp.logical_and(low <= image, image <= high)
         pairs += jnp.where(wanted, last - first + 1, 0)
     at, image = jnp.int32(0), low
-    for step in range(tiles + images):
+    for step in range(table.shape[1]):
         table[0, step] = at
         table[1, step] = image
         table[2, step] = jnp.minimum(jnp.bitwise_and(starts[image], -LANES), last_begin)
@@ -180,8 +187,8 @@
 
 
 def attend_images(pairs, table, ids_ref, keys, values, queries, attended, work, query_base):
-    scores_a, scores_b, tops_a, tops_b = work
-    window, tile = scores_a.shape
+    work = list(zip(work[0::2], work[1::2]))
+    window, tile = work[0][0].shape
     size = attended.shape[0] - SPARE
 
     def window_of(state):
@@ -204,27 +211,15 @@
         place = (slice(None), pl.ds(first, tile))
         attended[place] = jnp.where(labels == table[1, state], weighted * share, attended[place])
 
-    def two_pairs(state):
-        score(state + 1, scores_b, tops_b)
-        weigh(state, scores_a, tops_a)
-        score(state + 2, scores_a, tops_a)
-        weigh(state + 1, scores_b, tops_b)
-
-    def four_pairs(step, _):
-        two_pairs(4 * step)
-        two_pairs(4 * step + 2)
+    def run(step, _):
+        for place in range(RUN):
+            state = step * RUN + place
+            score(state + 1, *work[(place + 1) % RUN])
+            weigh(state, *work[place])
         return 0
 
-    score(0, scores_a, tops_a)
-    lax.fori_loop(0, pairs >> 2, four_pairs, 0)
-
-    @pl.when(jnp.bitwise_and(pairs, 2) == 2)
-    def _():
-        two_pairs(jnp.bitwise_and(pairs, -4))
-
-    @pl.when(jnp.bitwise_and(pairs, 1) == 1)
-    def _():
-        weigh(pairs - 1, scores_a, tops_a)
+    score(0, *work[0])
+    lax.fori_loop(0, lax.div(pairs + RUN - 1, RUN), run, 0)
 
 
 def turned_keys(marked, block_ref):
@@ -520,7 +515,7 @@
             pltpu.VMEM((count, depth), bf16),
             pltpu.VMEM((3, 2 * size, depth), bf16),
             pltpu.SemaphoreType.DMA,
-            pltpu.SemaphoreType.DMA,
+            pltpu.SemaphoreType.DMA((3,)),
             pltpu.SemaphoreType.DMA((3,)),
         ],
         [hbm] * 3,
@@ -588,12 +583,11 @@
             pltpu.VMEM((padded, reach), bf16),
             pltpu.VMEM((LANES, length), bf16),
             pltpu.VMEM((padded, length), f32),
-            pltpu.VMEM((window, tile), f32),
-            pltpu.VMEM((window, tile), f32),
-            pltpu.VMEM((1, tile), f32),
-            pltpu.VMEM((1, tile), f32),
+        ]
+        + [pltpu.VMEM((window, tile), f32), pltpu.VMEM((1, tile), f32)] * RUN
+        + [
             pltpu.SMEM((images + 1,), jnp.int32),
-            pltpu.SMEM((3, length // tile + images), jnp.int32),
+            pltpu.SMEM((3, rounded_up(length // tile + images, RUN) + 1), jnp.int32),
         ],
         in_vmem(len(operands)),
         4 * size * length * MAXP,

time: 41.8 us -> 43.2 us (1.033)
  Pallas kernels: 14.6 us -> 16 us
    pallas_call x1, Pallas kernels: 6.06 us -> 7.44 us  [local(): call(functools.partial(attend_kernel, images, piggy, halo), (shape((padde...]
  transfers between devices with their start and end apart: 15 -> 15, of which waited for: 9 -> 9; matrix products, arithmetic and copies ran while one was open for 0% -> 0% of each run, Pallas kernels for 9% -> 8%
where the time goes in v24:
time: 43.2 us; the launch traced here: 43 us
  starting transfers between devices  17.6 us (41%)
  Pallas kernels  16 us (37%)
  waiting for transfers between devices  8.76 us (20%)
  between operations  0.69 us (2%)
    ppermute x15, starting transfers between devices, moved(): return lax.ppermute(value, axis, pairs)  17.6 us
    ppermute x15, waiting for transfers between devices, moved(): return lax.ppermute(value, axis, pairs)  8.76 us
    pallas_call x1, Pallas kernels, local(): call(functools.partial(attend_kernel, images, piggy, halo), (shape((padde...  7.44 us
    pallas_call x1, Pallas kernels, local(): call(functools.partial(far_kernel, images, piggy), (shape((depth, count),...  2.79 us
    pallas_call x1, Pallas kernels, local(): call(functools.partial(finish_kernel, images), (shape((count, depth), bf1...  2.14 us
    pallas_call x1, Pallas kernels, local(): call(functools.partial(near_kernel, piggy), (block,) * 6, [], in_vmem(3),...  1.95 us
    pallas_call x1, Pallas kernels, local(): call(functools.partial(prepare_kernel, images, halo), (shape((len(EARLY)...  1.64 us
  transfers between devices with their start and end apart: 15, of which 9 were waited for; matrix products, arithmetic and copies ran while one was open for 0% of the time, Pallas kernels for 8%

profile of v24, /device:TPU:0, one launch (start us, length us, event | category | flops | bytes accessed | tf_op | source)
XLA Modules:
  0.0 43.0 jit_solution(14996659132250638896)
XLA Ops:
  0.6 0.0 copy-start
  0.6 2.8 %shard_map.68 = (bf16[1152,384]{1,0:T(8,128)(2,1)S(1)}, f32[8,1152]{1,0:T(8,128)S(1)}, bf16[224,384]{1,0:T(8,128)(2,1)S(1)}, bf16[224,384]{1,0:T(8,128)(2,1)S(1)}) custom-call(s32[1,3072]{1,0:T(1,128)} %ids_ref.5, bf16[384,1152]{1,0:T(8,128)(2,1)} %bitcast.6, bf16[1728,1152]{1,0:T(8,128)(2,1)} %bitcast.4), custom_call_target="tpu_custom_call" | custom-call | flops 382205952 | bytes 8388608 | tf_op jit(solution)/shard_map/pallas_call | solution.py:510
  3.4 4.0 %collective-permute-start = (bf16[224,384]{1,0:T(8,128)(2,1)S(1)}, bf16[224,384]{1,0:T(8,128)(2,1)S(1)}, u32[]{:S(2)}, u32[]{:S(2)}) collective-permute-start(bf16[224,384]{1,0:T(8,128)(2,1)S(1)} %get-tuple-element.28), channel_id=1, source_target_pairs={{0,24},{4,28},{8,16},{12,20},{16,8},{20,12},{24,0},{28,4},{1,25},{... | collective-permute-start | bytes 516104 | tf_op jit(solution)/shard_map/ppermute | solution.py:459
  7.4 0.0 collective-permute-start.1
  7.4 0.0 copy-done
  7.4 0.0 copy-start.3
  7.4 0.0 copy-start.2
  7.4 1.9 %shard_map.69 = (bf16[224,384]{1,0:T(8,128)(2,1)S(1)}, bf16[224,384]{1,0:T(8,128)(2,1)S(1)}, bf16[224,384]{1,0:T(8,128)(2,1)S(1)}, bf16[224,384]{1,0:T(8,128)(2,...) custom-call(bf16[1152,384]{1,0:T(8,128)(2,1)S(1)} %get-tuple-element.30.normed_ref, ...), custom_call_target="tpu_custom_call" | custom-call | flops 1146617856 | bytes 8388608 | tf_op jit(solution)/shard_map/pallas_call | solution.py:524
  9.4 0.2 collective-permute-start.2
  9.6 1.9 %collective-permute-start.3 = (bf16[224,384]{1,0:T(8,128)(2,1)S(1)}, bf16[224,384]{1,0:T(8,128)(2,1)S(1)}, u32[]{:S(2)}, u32[]{:S(2)}) collective-permute-start(bf16[224,384]{1,0:T(8,128)(2,1)S(1)} %get-tuple-element.39), channel_id=1, source_target_pairs={{0,8},{4,12},{8,0},{12,4},{16,24},{20,28},{24,16},{28,20},{1,9},{5... | collective-permute-start | bytes 516104 | tf_op jit(solution)/shard_map/ppermute | solution.py:459
  11.5 1.5 %collective-permute-start.4 = (bf16[224,384]{1,0:T(8,128)(2,1)S(1)}, bf16[224,384]{1,0:T(8,128)(2,1)S(1)}, u32[]{:S(2)}, u32[]{:S(2)}) collective-permute-start(bf16[224,384]{1,0:T(8,128)(2,1)S(1)} %get-tuple-element.40), channel_id=1, source_target_pairs={{0,16},{4,20},{8,24},{12,28},{16,0},{20,4},{24,8},{28,12},{1,17},{... | collective-permute-start | bytes 516104 | tf_op jit(solution)/shard_map/ppermute | solution.py:459
  13.0 0.0 collective-permute-done.rest_0_
  13.0 0.0 collective-permute-start.5
  13.0 2.9 %collective-permute-done.1.rest_1_ = bf16[224,384]{1,0:T(8,128)(2,1)S(1)} collective-permute-done((bf16[224,384]{1,0:T(8,128)(2,1)S(1)}, bf16[224,384]{1,0:T(8,128)(2,1)S(1)}, u32[]{:S(2)}, u32[]{:S(2)}) %collective-permute-start.1) | collective-permute-done | bytes 172064 | tf_op jit(solution)/shard_map/ppermute | solution.py:459
  15.9 1.9 %collective-permute-start.6 = (bf16[224,384]{1,0:T(8,128)(2,1)S(1)}, bf16[224,384]{1,0:T(8,128)(2,1)S(1)}, u32[]{:S(2)}, u32[]{:S(2)}) collective-permute-start(bf16[224,384]{1,0:T(8,128)(2,1)S(1)} %get-tuple-element.42), channel_id=1, source_target_pairs={{0,20},{4,16},{8,28},{12,24},{16,4},{20,0},{24,12},{28,8},{1,21},{... | collective-permute-start | bytes 516104 | tf_op jit(solution)/shard_map/ppermute | solution.py:459
  17.7 0.0 collective-permute-done.2.rest_2_
  17.7 0.0 copy-done.3
  17.7 1.6 %collective-permute-start.7 = (bf16[4,1152]{1,0:T(4,128)(2,1)S(1)}, bf16[4,1152]{1,0:T(4,128)(2,1)S(1)}, u32[]{:S(2)}, u32[]{:S(2)}) collective-permute-start(bf16[4,1152]{1,0:T(4,128)(2,1)S(1)} %copy-done.3), channel_id=1, source_target_pairs={{1,0},{0,1},{3,2},{2,3},{6,4},{7,5},{4,6},{5,7},{11,8},{10,9},{9,1... | collective-permute-start | bytes 27656 | tf_op jit(solution)/shard_map/ppermute | solution.py:459
  19.3 0.0 copy-done.2
  19.3 1.6 %shard_map.70 = (bf16[1536,128]{1,0:T(8,128)(2,1)S(1)}, f32[2,8,3072]{2,1,0:T(8,128)S(1)}, s32[8,128]{1,0:T(8,128)S(1)}, bf16[640,1152]{1,0:T(8,128)(2,1)S(1)}) custom-call(s32[1,3072]{1,0:T(1,128)S(1)} %copy-done.2, bf16[576,1152]{1,0:T(8,128)(2,1)} %out_weight_ref.1, bf16[224,384]{1,0:T(8,128)(2,1)S(1)} %collective-permute-done.rest_0_, ...), custom_call_target="tpu_custom_call" | custom-call | flops 1073741824 | bytes 8388608 | tf_op jit(solution)/shard_map/pallas_call | solution.py:565
  21.0 0.4 collective-permute-done.7.rest_8_
  21.4 0.0 collective-permute-done.3.rest_4_
  21.4 0.0 collective-permute-done.4.rest_5_
  21.4 0.7 %collective-permute-done.5.rest_6_ = bf16[224,384]{1,0:T(8,128)(2,1)S(1)} collective-permute-done((bf16[224,384]{1,0:T(8,128)(2,1)S(1)}, bf16[224,384]{1,0:T(8,128)(2,1)S(1)}, u32[]{:S(2)}, u32[]{:S(2)}) %collective-permute-start.5) | collective-permute-done | bytes 172064 | tf_op jit(solution)/shard_map/ppermute | solution.py:459
  22.1 0.6 %collective-permute-done.6.rest_7_ = bf16[224,384]{1,0:T(8,128)(2,1)S(1)} collective-permute-done((bf16[224,384]{1,0:T(8,128)(2,1)S(1)}, bf16[224,384]{1,0:T(8,128)(2,1)S(1)}, u32[]{:S(2)}, u32[]{:S(2)}) %collective-permute-start.6) | collective-permute-done | bytes 172064 | tf_op jit(solution)/shard_map/ppermute | solution.py:459
  22.7 0.0 copy-start.1
  22.7 7.4 %shard_map.71 = (bf16[96,384]{1,0:T(8,128)(2,1)S(1)}, bf16[96,384]{1,0:T(8,128)(2,1)S(1)}, bf16[96,384]{1,0:T(8,128)(2,1)S(1)}, bf16[96,384]{1,0:T(8,128)(2,1)S(...) custom-call(s32[1,3072]{1,0:T(1,128)S(1)} %copy-done.2, ...), custom_call_target="tpu_custom_call" | custom-call | flops 905969664 | bytes 8388608 | tf_op jit(solution)/shard_map/pallas_call | solution.py:578
  30.2 2.3 %collective-permute-start.8 = (bf16[96,384]{1,0:T(8,128)(2,1)S(1)}, bf16[96,384]{1,0:T(8,128)(2,1)S(1)}, u32[]{:S(2)}, u32[]{:S(2)}) collective-permute-start(bf16[96,384]{1,0:T(8,128)(2,1)S(1)} %get-tuple-element.44), channel_id=1, source_target_pairs={{0,24},{4,28},{8,16},{12,20},{16,8},{20,12},{24,0},{28,4},{1,25},{... | collective-permute-start | bytes 221192 | tf_op jit(solution)/shard_map/ppermute | solution.py:459
  32.5 0.2 collective-permute-start.9
  32.7 1.8 %collective-permute-start.10 = (bf16[96,384]{1,0:T(8,128)(2,1)S(1)}, bf16[96,384]{1,0:T(8,128)(2,1)S(1)}, u32[]{:S(2)}, u32[]{:S(2)}) collective-permute-start(bf16[96,384]{1,0:T(8,128)(2,1)S(1)} %get-tuple-element.46), channel_id=1, source_target_pairs={{0,8},{4,12},{8,0},{12,4},{16,24},{20,28},{24,16},{28,20},{1,9},{5... | collective-permute-start | bytes 221192 | tf_op jit(solution)/shard_map/ppermute | solution.py:459
  34.5 1.2 %collective-permute-start.11 = (bf16[96,384]{1,0:T(8,128)(2,1)S(1)}, bf16[96,384]{1,0:T(8,128)(2,1)S(1)}, u32[]{:S(2)}, u32[]{:S(2)}) collective-permute-start(bf16[96,384]{1,0:T(8,128)(2,1)S(1)} %get-tuple-element.47), channel_id=1, source_target_pairs={{0,16},{4,20},{8,24},{12,28},{16,0},{20,4},{24,8},{28,12},{1,17},{... | collective-permute-start | bytes 221192 | tf_op jit(solution)/shard_map/ppermute | solution.py:459
  35.6 0.0 collective-permute-start.12
  35.7 0.0 collective-permute-done.8.rest_0_
  35.7 0.8 %collective-permute-start.13 = (bf16[96,384]{1,0:T(8,128)(2,1)S(1)}, bf16[96,384]{1,0:T(8,128)(2,1)S(1)}, u32[]{:S(2)}, u32[]{:S(2)}) collective-permute-start(bf16[96,384]{1,0:T(8,128)(2,1)S(1)} %get-tuple-element.49), channel_id=1, source_target_pairs={{0,20},{4,16},{8,28},{12,24},{16,4},{20,0},{24,12},{28,8},{1,21},{... | collective-permute-start | bytes 221192 | tf_op jit(solution)/shard_map/ppermute | solution.py:459
  36.5 1.2 %collective-permute-done.9.rest_1_ = bf16[96,384]{1,0:T(8,128)(2,1)S(1)} collective-permute-done((bf16[96,384]{1,0:T(8,128)(2,1)S(1)}, bf16[96,384]{1,0:T(8,128)(2,1)S(1)}, u32[]{:S(2)}, u32[]{:S(2)}) %collective-permute-start.9) | collective-permute-done | bytes 73760 | tf_op jit(solution)/shard_map/ppermute | solution.py:459
  37.7 0.3 collective-permute-start.14
  38.0 1.0 %collective-permute-done.10.rest_2_ = bf16[96,384]{1,0:T(8,128)(2,1)S(1)} collective-permute-done((bf16[96,384]{1,0:T(8,128)(2,1)S(1)}, bf16[96,384]{1,0:T(8,128)(2,1)S(1)}, u32[]{:S(2)}, u32[]{:S(2)}) %collective-permute-start.10) | collective-permute-done | bytes 73760 | tf_op jit(solution)/shard_map/ppermute | solution.py:459
  39.0 0.7 %collective-permute-done.11.rest_3_ = bf16[96,384]{1,0:T(8,128)(2,1)S(1)} collective-permute-done((bf16[96,384]{1,0:T(8,128)(2,1)S(1)}, bf16[96,384]{1,0:T(8,128)(2,1)S(1)}, u32[]{:S(2)}, u32[]{:S(2)}) %collective-permute-start.11) | collective-permute-done | bytes 73760 | tf_op jit(solution)/shard_map/ppermute | solution.py:459
  39.7 1.1 %collective-permute-done.12.rest_4_ = bf16[96,384]{1,0:T(8,128)(2,1)S(1)} collective-permute-done((bf16[96,384]{1,0:T(8,128)(2,1)S(1)}, bf16[96,384]{1,0:T(8,128)(2,1)S(1)}, u32[]{:S(2)}, u32[]{:S(2)}) %collective-permute-start.12) | collective-permute-done | bytes 73760 | tf_op jit(solution)/shard_map/ppermute | solution.py:459
  40.7 0.2 collective-permute-done.13.rest_5_
  40.9 0.0 collective-permute-done.14.rest_6_
  40.9 0.0 copy-done.1
  40.9 2.1 %shard_map.72 = (bf16[384,1152]{1,0:T(8,128)(2,1)}, f32[1,4]{1,0:T(1,128)}) custom-call(bf16[384,1152]{1,0:T(8,128)(2,1)S(1)} %bitcast.7, bf16[640,1152]{1,0:T(8,128)(2,1)S(1)} %get-tuple-element.35.weight_ref, bf16[4,1152]{1,0:T(4,128)(2,1)S(1)} %copy-done.3, bf16[96,384]{1,0:T(8,128)(2,1)S(1)} %collective-permute-done.8.rest_0_, ...), custom_call_target="tpu_custom_call" | custom-call | flops 509607936 | bytes 8388608 | tf_op jit(solution)/shard_map/pallas_call | solution.py:606
Async XLA Ops:
  0.6 6.8 %copy-start = (bf16[1152,1728]{0,1:T(8,128)(2,1)S(1)}, bf16[1152,1728]{0,1:T(8,128)(2,1)}, u32[]{:S(2)}) copy-start(bf16[1152,1728]{0,1:T(8,128)(2,1)} %param.7) | copy-start | bytes 11943940
  3.4 9.6 %collective-permute-start = (bf16[224,384]{1,0:T(8,128)(2,1)S(1)}, bf16[224,384]{1,0:T(8,128)(2,1)S(1)}, u32[]{:S(2)}, u32[]{:S(2)}) collective-permute-start(bf16[224,384]{1,0:T(8,128)(2,1)S(1)} %get-tuple-element.28), channel_id=1, source_target_pairs={{0,24},{4,28},{8,16},{12,20},{16,8},{20,12},{24,0},{28,4},{1,25},{... | collective-permute-start | bytes 516104 | tf_op jit(solution)/shard_map/ppermute | solution.py:459
  7.4 8.5 %collective-permute-start.1 = (bf16[224,384]{1,0:T(8,128)(2,1)S(1)}, bf16[224,384]{1,0:T(8,128)(2,1)S(1)}, u32[]{:S(2)}, u32[]{:S(2)}) collective-permute-start(bf16[224,384]{1,0:T(8,128)(2,1)S(1)} %get-tuple-element.29), channel_id=1, source_target_pairs={{0,28},{4,24},{8,20},{12,16},{16,12},{20,8},{24,4},{28,0},{1,29},{... | collective-permute-start | bytes 516104 | tf_op jit(solution)/shard_map/ppermute | solution.py:459
  7.4 10.3 %copy-start.3 = (bf16[4,1152]{1,0:T(4,128)(2,1)S(1)}, bf16[4,1152]{1,0:T(4,128)(2,1)}, u32[]{:S(2)}) copy-start(bf16[4,1152]{1,0:T(4,128)(2,1)} %text_ref.1) | copy-start | bytes 27652
  7.4 11.9 %copy-start.2 = (s32[1,3072]{1,0:T(1,128)S(1)}, s32[1,3072]{1,0:T(1,128)}, u32[]{:S(2)}) copy-start(s32[1,3072]{1,0:T(1,128)} %ids_ref.5) | copy-start | bytes 36868
  9.4 8.4 %collective-permute-start.2 = (bf16[224,384]{1,0:T(8,128)(2,1)S(1)}, bf16[224,384]{1,0:T(8,128)(2,1)S(1)}, u32[]{:S(2)}, u32[]{:S(2)}) collective-permute-start(bf16[224,384]{1,0:T(8,128)(2,1)S(1)} %get-tuple-element.32), channel_id=1, source_target_pairs={{0,4},{4,0},{8,12},{12,8},{16,20},{20,16},{24,28},{28,24},{1,5},{5... | collective-permute-start | bytes 516104 | tf_op jit(solution)/shard_map/ppermute | solution.py:459
  9.6 11.8 %collective-permute-start.3 = (bf16[224,384]{1,0:T(8,128)(2,1)S(1)}, bf16[224,384]{1,0:T(8,128)(2,1)S(1)}, u32[]{:S(2)}, u32[]{:S(2)}) collective-permute-start(bf16[224,384]{1,0:T(8,128)(2,1)S(1)} %get-tuple-element.39), channel_id=1, source_target_pairs={{0,8},{4,12},{8,0},{12,4},{16,24},{20,28},{24,16},{28,20},{1,9},{5... | collective-permute-start | bytes 516104 | tf_op jit(solution)/shard_map/ppermute | solution.py:459
  11.5 9.9 %collective-permute-start.4 = (bf16[224,384]{1,0:T(8,128)(2,1)S(1)}, bf16[224,384]{1,0:T(8,128)(2,1)S(1)}, u32[]{:S(2)}, u32[]{:S(2)}) collective-permute-start(bf16[224,384]{1,0:T(8,128)(2,1)S(1)} %get-tuple-element.40), channel_id=1, source_target_pairs={{0,16},{4,20},{8,24},{12,28},{16,0},{20,4},{24,8},{28,12},{1,17},{... | collective-permute-start | bytes 516104 | tf_op jit(solution)/shard_map/ppermute | solution.py:459
  13.0 9.1 %collective-permute-start.5 = (bf16[224,384]{1,0:T(8,128)(2,1)S(1)}, bf16[224,384]{1,0:T(8,128)(2,1)S(1)}, u32[]{:S(2)}, u32[]{:S(2)}) collective-permute-start(bf16[224,384]{1,0:T(8,128)(2,1)S(1)} %get-tuple-element.41), channel_id=1, source_target_pairs={{0,12},{4,8},{8,4},{12,0},{16,28},{20,24},{24,20},{28,16},{1,13},{... | collective-permute-start | bytes 516104 | tf_op jit(solution)/shard_map/ppermute | solution.py:459
  15.9 6.8 %collective-permute-start.6 = (bf16[224,384]{1,0:T(8,128)(2,1)S(1)}, bf16[224,384]{1,0:T(8,128)(2,1)S(1)}, u32[]{:S(2)}, u32[]{:S(2)}) collective-permute-start(bf16[224,384]{1,0:T(8,128)(2,1)S(1)} %get-tuple-element.42), channel_id=1, source_target_pairs={{0,20},{4,16},{8,28},{12,24},{16,4},{20,0},{24,12},{28,8},{1,21},{... | collective-permute-start | bytes 516104 | tf_op jit(solution)/shard_map/ppermute | solution.py:459
  17.7 3.7 %collective-permute-start.7 = (bf16[4,1152]{1,0:T(4,128)(2,1)S(1)}, bf16[4,1152]{1,0:T(4,128)(2,1)S(1)}, u32[]{:S(2)}, u32[]{:S(2)}) collective-permute-start(bf16[4,1152]{1,0:T(4,128)(2,1)S(1)} %copy-done.3), channel_id=1, source_target_pairs={{1,0},{0,1},{3,2},{2,3},{6,4},{7,5},{4,6},{5,7},{11,8},{10,9},{9,1... | collective-permute-start | bytes 27656 | tf_op jit(solution)/shard_map/ppermute | solution.py:459
  22.7 18.2 %copy-start.1 = (bf16[1,384,1152]{2,1,0:T(8,128)(2,1)S(1)}, bf16[1,384,1152]{2,1,0:T(8,128)(2,1)}, u32[]{:S(2)}) copy-start(bf16[1,384,1152]{2,1,0:T(8,128)(2,1)} %param.5) | copy-start | bytes 2654212
  30.2 5.5 %collective-permute-start.8 = (bf16[96,384]{1,0:T(8,128)(2,1)S(1)}, bf16[96,384]{1,0:T(8,128)(2,1)S(1)}, u32[]{:S(2)}, u32[]{:S(2)}) collective-permute-start(bf16[96,384]{1,0:T(8,128)(2,1)S(1)} %get-tuple-element.44), channel_id=1, source_target_pairs={{0,24},{4,28},{8,16},{12,20},{16,8},{20,12},{24,0},{28,4},{1,25},{... | collective-permute-start | bytes 221192 | tf_op jit(solution)/shard_map/ppermute | solution.py:459
  32.5 5.2 %collective-permute-start.9 = (bf16[96,384]{1,0:T(8,128)(2,1)S(1)}, bf16[96,384]{1,0:T(8,128)(2,1)S(1)}, u32[]{:S(2)}, u32[]{:S(2)}) collective-permute-start(bf16[96,384]{1,0:T(8,128)(2,1)S(1)} %get-tuple-element.45), channel_id=1, source_target_pairs={{0,28},{4,24},{8,20},{12,16},{16,12},{20,8},{24,4},{28,0},{1,29},{... | collective-permute-start | bytes 221192 | tf_op jit(solution)/shard_map/ppermute | solution.py:459
  32.7 6.3 %collective-permute-start.10 = (bf16[96,384]{1,0:T(8,128)(2,1)S(1)}, bf16[96,384]{1,0:T(8,128)(2,1)S(1)}, u32[]{:S(2)}, u32[]{:S(2)}) collective-permute-start(bf16[96,384]{1,0:T(8,128)(2,1)S(1)} %get-tuple-element.46), channel_id=1, source_target_pairs={{0,8},{4,12},{8,0},{12,4},{16,24},{20,28},{24,16},{28,20},{1,9},{5... | collective-permute-start | bytes 221192 | tf_op jit(solution)/shard_map/ppermute | solution.py:459
  34.5 5.2 %collective-permute-start.11 = (bf16[96,384]{1,0:T(8,128)(2,1)S(1)}, bf16[96,384]{1,0:T(8,128)(2,1)S(1)}, u32[]{:S(2)}, u32[]{:S(2)}) collective-permute-start(bf16[96,384]{1,0:T(8,128)(2,1)S(1)} %get-tuple-element.47), channel_id=1, source_target_pairs={{0,16},{4,20},{8,24},{12,28},{16,0},{20,4},{24,8},{28,12},{1,17},{... | collective-permute-start | bytes 221192 | tf_op jit(solution)/shard_map/ppermute | solution.py:459
  35.6 5.1 %collective-permute-start.12 = (bf16[96,384]{1,0:T(8,128)(2,1)S(1)}, bf16[96,384]{1,0:T(8,128)(2,1)S(1)}, u32[]{:S(2)}, u32[]{:S(2)}) collective-permute-start(bf16[96,384]{1,0:T(8,128)(2,1)S(1)} %get-tuple-element.48), channel_id=1, source_target_pairs={{0,12},{4,8},{8,4},{12,0},{16,28},{20,24},{24,20},{28,16},{1,13},{... | collective-permute-start | bytes 221192 | tf_op jit(solution)/shard_map/ppermute | solution.py:459
  35.7 5.2 %collective-permute-start.13 = (bf16[96,384]{1,0:T(8,128)(2,1)S(1)}, bf16[96,384]{1,0:T(8,128)(2,1)S(1)}, u32[]{:S(2)}, u32[]{:S(2)}) collective-permute-start(bf16[96,384]{1,0:T(8,128)(2,1)S(1)} %get-tuple-element.49), channel_id=1, source_target_pairs={{0,20},{4,16},{8,28},{12,24},{16,4},{20,0},{24,12},{28,8},{1,21},{... | collective-permute-start | bytes 221192 | tf_op jit(solution)/shard_map/ppermute | solution.py:459
  37.7 3.2 %collective-permute-start.14 = (bf16[96,384]{1,0:T(8,128)(2,1)S(1)}, bf16[96,384]{1,0:T(8,128)(2,1)S(1)}, u32[]{:S(2)}, u32[]{:S(2)}) collective-permute-start(bf16[96,384]{1,0:T(8,128)(2,1)S(1)} %get-tuple-element.50), channel_id=1, source_target_pairs={{0,4},{4,0},{8,12},{12,8},{16,20},{20,16},{24,28},{28,24},{1,5},{5... | collective-permute-start | bytes 221192 | tf_op jit(solution)/shard_map/ppermute | solution.py:459

commit v25 on v24

--- a/solution.py
+++ b/solution.py
@@ -187,7 +187,7 @@
 
 
 def attend_images(pairs, table, ids_ref, keys, values, queries, attended, work, query_base):
-    work = list(zip(work[0::2], work[1::2]))
+    work = list(zip(work[:RUN], work[RUN:]))
     window, tile = work[0][0].shape
     size = attended.shape[0] - SPARE
 
@@ -584,7 +584,8 @@
             pltpu.VMEM((LANES, length), bf16),
             pltpu.VMEM((padded, length), f32),
         ]
-        + [pltpu.VMEM((window, tile), f32), pltpu.VMEM((1, tile), f32)] * RUN
+        + [pltpu.VMEM((window, tile), f32)] * RUN
+        + [pltpu.VMEM((1, tile), f32)] * RUN
         + [
             pltpu.SMEM((images + 1,), jnp.int32),
             pltpu.SMEM((3, rounded_up(length // tile + images, RUN) + 1), jnp.int32),

time: 43.2 us -> 43.2 us (level)
  no operation moved by 1% of the time
where the time goes in v25:
time: 43.2 us; the launch traced here: 43.1 us
  starting transfers between devices  17.6 us (41%)
  Pallas kernels  16 us (37%)
  waiting for transfers between devices  8.75 us (20%)
  between operations  0.69 us (2%)
    ppermute x15, starting transfers between devices, moved(): return lax.ppermute(value, axis, pairs)  17.6 us
    ppermute x15, waiting for transfers between devices, moved(): return lax.ppermute(value, axis, pairs)  8.75 us
    pallas_call x1, Pallas kernels, local(): call(functools.partial(attend_kernel, images, piggy, halo), (shape((padde...  7.47 us
    pallas_call x1, Pallas kernels, local(): call(functools.partial(far_kernel, images, piggy), (shape((depth, count),...  2.79 us
    pallas_call x1, Pallas kernels, local(): call(functools.partial(finish_kernel, images), (shape((count, depth), bf1...  2.14 us
    pallas_call x1, Pallas kernels, local(): call(functools.partial(near_kernel, piggy), (block,) * 6, [], in_vmem(3),...  1.95 us
    pallas_call x1, Pallas kernels, local(): call(functools.partial(prepare_kernel, images, halo), (shape((len(EARLY)...  1.64 us
  transfers between devices with their start and end apart: 15, of which 9 were waited for; matrix products, arithmetic and copies ran while one was open for 0% of the time, Pallas kernels for 8%

profile of v25, /device:TPU:0, one launch (start us, length us, event | category | flops | bytes accessed | tf_op | source)
XLA Modules:
  0.0 43.1 jit_solution(14996659132250638896)
XLA Ops:
  0.6 0.0 copy-start
  0.6 2.8 %shard_map.68 = (bf16[1152,384]{1,0:T(8,128)(2,1)S(1)}, f32[8,1152]{1,0:T(8,128)S(1)}, bf16[224,384]{1,0:T(8,128)(2,1)S(1)}, bf16[224,384]{1,0:T(8,128)(2,1)S(1)}) custom-call(s32[1,3072]{1,0:T(1,128)} %ids_ref.5, bf16[384,1152]{1,0:T(8,128)(2,1)} %bitcast.6, bf16[1728,1152]{1,0:T(8,128)(2,1)} %bitcast.4), custom_call_target="tpu_custom_call" | custom-call | flops 382205952 | bytes 8388608 | tf_op jit(solution)/shard_map/pallas_call | solution.py:510
  3.4 4.0 %collective-permute-start = (bf16[224,384]{1,0:T(8,128)(2,1)S(1)}, bf16[224,384]{1,0:T(8,128)(2,1)S(1)}, u32[]{:S(2)}, u32[]{:S(2)}) collective-permute-start(bf16[224,384]{1,0:T(8,128)(2,1)S(1)} %get-tuple-element.28), channel_id=1, source_target_pairs={{0,24},{4,28},{8,16},{12,20},{16,8},{20,12},{24,0},{28,4},{1,25},{... | collective-permute-start | bytes 516104 | tf_op jit(solution)/shard_map/ppermute | solution.py:459
  7.4 0.0 collective-permute-start.1
  7.4 0.0 copy-done
  7.4 0.0 copy-start.3
  7.4 0.0 copy-start.2
  7.4 1.9 %shard_map.69 = (bf16[224,384]{1,0:T(8,128)(2,1)S(1)}, bf16[224,384]{1,0:T(8,128)(2,1)S(1)}, bf16[224,384]{1,0:T(8,128)(2,1)S(1)}, bf16[224,384]{1,0:T(8,128)(2,...) custom-call(bf16[1152,384]{1,0:T(8,128)(2,1)S(1)} %get-tuple-element.30.normed_ref, ...), custom_call_target="tpu_custom_call" | custom-call | flops 1146617856 | bytes 8388608 | tf_op jit(solution)/shard_map/pallas_call | solution.py:524
  9.4 0.2 collective-permute-start.2
  9.6 1.9 %collective-permute-start.3 = (bf16[224,384]{1,0:T(8,128)(2,1)S(1)}, bf16[224,384]{1,0:T(8,128)(2,1)S(1)}, u32[]{:S(2)}, u32[]{:S(2)}) collective-permute-start(bf16[224,384]{1,0:T(8,128)(2,1)S(1)} %get-tuple-element.39), channel_id=1, source_target_pairs={{0,8},{4,12},{8,0},{12,4},{16,24},{20,28},{24,16},{28,20},{1,9},{5... | collective-permute-start | bytes 516104 | tf_op jit(solution)/shard_map/ppermute | solution.py:459
  11.5 1.5 %collective-permute-start.4 = (bf16[224,384]{1,0:T(8,128)(2,1)S(1)}, bf16[224,384]{1,0:T(8,128)(2,1)S(1)}, u32[]{:S(2)}, u32[]{:S(2)}) collective-permute-start(bf16[224,384]{1,0:T(8,128)(2,1)S(1)} %get-tuple-element.40), channel_id=1, source_target_pairs={{0,16},{4,20},{8,24},{12,28},{16,0},{20,4},{24,8},{28,12},{1,17},{... | collective-permute-start | bytes 516104 | tf_op jit(solution)/shard_map/ppermute | solution.py:459
  13.0 0.0 collective-permute-done.rest_0_
  13.0 0.0 collective-permute-start.5
  13.0 2.9 %collective-permute-done.1.rest_1_ = bf16[224,384]{1,0:T(8,128)(2,1)S(1)} collective-permute-done((bf16[224,384]{1,0:T(8,128)(2,1)S(1)}, bf16[224,384]{1,0:T(8,128)(2,1)S(1)}, u32[]{:S(2)}, u32[]{:S(2)}) %collective-permute-start.1) | collective-permute-done | bytes 172064 | tf_op jit(solution)/shard_map/ppermute | solution.py:459
  15.9 1.9 %collective-permute-start.6 = (bf16[224,384]{1,0:T(8,128)(2,1)S(1)}, bf16[224,384]{1,0:T(8,128)(2,1)S(1)}, u32[]{:S(2)}, u32[]{:S(2)}) collective-permute-start(bf16[224,384]{1,0:T(8,128)(2,1)S(1)} %get-tuple-element.42), channel_id=1, source_target_pairs={{0,20},{4,16},{8,28},{12,24},{16,4},{20,0},{24,12},{28,8},{1,21},{... | collective-permute-start | bytes 516104 | tf_op jit(solution)/shard_map/ppermute | solution.py:459
  17.7 0.0 collective-permute-done.2.rest_2_
  17.7 0.0 copy-done.3
  17.7 1.6 %collective-permute-start.7 = (bf16[4,1152]{1,0:T(4,128)(2,1)S(1)}, bf16[4,1152]{1,0:T(4,128)(2,1)S(1)}, u32[]{:S(2)}, u32[]{:S(2)}) collective-permute-start(bf16[4,1152]{1,0:T(4,128)(2,1)S(1)} %copy-done.3), channel_id=1, source_target_pairs={{1,0},{0,1},{3,2},{2,3},{6,4},{7,5},{4,6},{5,7},{11,8},{10,9},{9,1... | collective-permute-start | bytes 27656 | tf_op jit(solution)/shard_map/ppermute | solution.py:459
  19.3 0.0 copy-done.2
  19.3 1.6 %shard_map.70 = (bf16[1536,128]{1,0:T(8,128)(2,1)S(1)}, f32[2,8,3072]{2,1,0:T(8,128)S(1)}, s32[8,128]{1,0:T(8,128)S(1)}, bf16[640,1152]{1,0:T(8,128)(2,1)S(1)}) custom-call(s32[1,3072]{1,0:T(1,128)S(1)} %copy-done.2, bf16[576,1152]{1,0:T(8,128)(2,1)} %out_weight_ref.1, bf16[224,384]{1,0:T(8,128)(2,1)S(1)} %collective-permute-done.rest_0_, ...), custom_call_target="tpu_custom_call" | custom-call | flops 1073741824 | bytes 8388608 | tf_op jit(solution)/shard_map/pallas_call | solution.py:565
  21.0 0.4 collective-permute-done.7.rest_8_
  21.4 0.0 collective-permute-done.3.rest_4_
  21.4 0.0 collective-permute-done.4.rest_5_
  21.4 0.7 %collective-permute-done.5.rest_6_ = bf16[224,384]{1,0:T(8,128)(2,1)S(1)} collective-permute-done((bf16[224,384]{1,0:T(8,128)(2,1)S(1)}, bf16[224,384]{1,0:T(8,128)(2,1)S(1)}, u32[]{:S(2)}, u32[]{:S(2)}) %collective-permute-start.5) | collective-permute-done | bytes 172064 | tf_op jit(solution)/shard_map/ppermute | solution.py:459
  22.1 0.6 %collective-permute-done.6.rest_7_ = bf16[224,384]{1,0:T(8,128)(2,1)S(1)} collective-permute-done((bf16[224,384]{1,0:T(8,128)(2,1)S(1)}, bf16[224,384]{1,0:T(8,128)(2,1)S(1)}, u32[]{:S(2)}, u32[]{:S(2)}) %collective-permute-start.6) | collective-permute-done | bytes 172064 | tf_op jit(solution)/shard_map/ppermute | solution.py:459
  22.7 0.0 copy-start.1
  22.7 7.5 %shard_map.71 = (bf16[96,384]{1,0:T(8,128)(2,1)S(1)}, bf16[96,384]{1,0:T(8,128)(2,1)S(1)}, bf16[96,384]{1,0:T(8,128)(2,1)S(1)}, bf16[96,384]{1,0:T(8,128)(2,1)S(...) custom-call(s32[1,3072]{1,0:T(1,128)S(1)} %copy-done.2, ...), custom_call_target="tpu_custom_call" | custom-call | flops 905969664 | bytes 8388608 | tf_op jit(solution)/shard_map/pallas_call | solution.py:578
  30.2 2.3 %collective-permute-start.8 = (bf16[96,384]{1,0:T(8,128)(2,1)S(1)}, bf16[96,384]{1,0:T(8,128)(2,1)S(1)}, u32[]{:S(2)}, u32[]{:S(2)}) collective-permute-start(bf16[96,384]{1,0:T(8,128)(2,1)S(1)} %get-tuple-element.44), channel_id=1, source_target_pairs={{0,24},{4,28},{8,16},{12,20},{16,8},{20,12},{24,0},{28,4},{1,25},{... | collective-permute-start | bytes 221192 | tf_op jit(solution)/shard_map/ppermute | solution.py:459
  32.5 0.2 collective-permute-start.9
  32.7 1.8 %collective-permute-start.10 = (bf16[96,384]{1,0:T(8,128)(2,1)S(1)}, bf16[96,384]{1,0:T(8,128)(2,1)S(1)}, u32[]{:S(2)}, u32[]{:S(2)}) collective-permute-start(bf16[96,384]{1,0:T(8,128)(2,1)S(1)} %get-tuple-element.46), channel_id=1, source_target_pairs={{0,8},{4,12},{8,0},{12,4},{16,24},{20,28},{24,16},{28,20},{1,9},{5... | collective-permute-start | bytes 221192 | tf_op jit(solution)/shard_map/ppermute | solution.py:459
  34.5 1.2 %collective-permute-start.11 = (bf16[96,384]{1,0:T(8,128)(2,1)S(1)}, bf16[96,384]{1,0:T(8,128)(2,1)S(1)}, u32[]{:S(2)}, u32[]{:S(2)}) collective-permute-start(bf16[96,384]{1,0:T(8,128)(2,1)S(1)} %get-tuple-element.47), channel_id=1, source_target_pairs={{0,16},{4,20},{8,24},{12,28},{16,0},{20,4},{24,8},{28,12},{1,17},{... | collective-permute-start | bytes 221192 | tf_op jit(solution)/shard_map/ppermute | solution.py:459
  35.7 0.0 collective-permute-start.12
  35.7 0.0 collective-permute-done.8.rest_0_
  35.7 0.8 %collective-permute-start.13 = (bf16[96,384]{1,0:T(8,128)(2,1)S(1)}, bf16[96,384]{1,0:T(8,128)(2,1)S(1)}, u32[]{:S(2)}, u32[]{:S(2)}) collective-permute-start(bf16[96,384]{1,0:T(8,128)(2,1)S(1)} %get-tuple-element.49), channel_id=1, source_target_pairs={{0,20},{4,16},{8,28},{12,24},{16,4},{20,0},{24,12},{28,8},{1,21},{... | collective-permute-start | bytes 221192 | tf_op jit(solution)/shard_map/ppermute | solution.py:459
  36.5 1.2 %collective-permute-done.9.rest_1_ = bf16[96,384]{1,0:T(8,128)(2,1)S(1)} collective-permute-done((bf16[96,384]{1,0:T(8,128)(2,1)S(1)}, bf16[96,384]{1,0:T(8,128)(2,1)S(1)}, u32[]{:S(2)}, u32[]{:S(2)}) %collective-permute-start.9) | collective-permute-done | bytes 73760 | tf_op jit(solution)/shard_map/ppermute | solution.py:459
  37.7 0.3 collective-permute-start.14
  38.0 1.0 %collective-permute-done.10.rest_2_ = bf16[96,384]{1,0:T(8,128)(2,1)S(1)} collective-permute-done((bf16[96,384]{1,0:T(8,128)(2,1)S(1)}, bf16[96,384]{1,0:T(8,128)(2,1)S(1)}, u32[]{:S(2)}, u32[]{:S(2)}) %collective-permute-start.10) | collective-permute-done | bytes 73760 | tf_op jit(solution)/shard_map/ppermute | solution.py:459
  39.0 0.7 %collective-permute-done.11.rest_3_ = bf16[96,384]{1,0:T(8,128)(2,1)S(1)} collective-permute-done((bf16[96,384]{1,0:T(8,128)(2,1)S(1)}, bf16[96,384]{1,0:T(8,128)(2,1)S(1)}, u32[]{:S(2)}, u32[]{:S(2)}) %collective-permute-start.11) | collective-permute-done | bytes 73760 | tf_op jit(solution)/shard_map/ppermute | solution.py:459
  39.7 1.1 %collective-permute-done.12.rest_4_ = bf16[96,384]{1,0:T(8,128)(2,1)S(1)} collective-permute-done((bf16[96,384]{1,0:T(8,128)(2,1)S(1)}, bf16[96,384]{1,0:T(8,128)(2,1)S(1)}, u32[]{:S(2)}, u32[]{:S(2)}) %collective-permute-start.12) | collective-permute-done | bytes 73760 | tf_op jit(solution)/shard_map/ppermute | solution.py:459
  40.8 0.2 collective-permute-done.13.rest_5_
  40.9 0.0 collective-permute-done.14.rest_6_
  40.9 0.0 copy-done.1
  40.9 2.1 %shard_map.72 = (bf16[384,1152]{1,0:T(8,128)(2,1)}, f32[1,4]{1,0:T(1,128)}) custom-call(bf16[384,1152]{1,0:T(8,128)(2,1)S(1)} %bitcast.7, bf16[640,1152]{1,0:T(8,128)(2,1)S(1)} %get-tuple-element.35.weight_ref, bf16[4,1152]{1,0:T(4,128)(2,1)S(1)} %copy-done.3, bf16[96,384]{1,0:T(8,128)(2,1)S(1)} %collective-permute-done.8.rest_0_, ...), custom_call_target="tpu_custom_call" | custom-call | flops 509607936 | bytes 8388608 | tf_op jit(solution)/shard_map/pallas_call | solution.py:607
Async XLA Ops:
  0.6 6.8 %copy-start = (bf16[1152,1728]{0,1:T(8,128)(2,1)S(1)}, bf16[1152,1728]{0,1:T(8,128)(2,1)}, u32[]{:S(2)}) copy-start(bf16[1152,1728]{0,1:T(8,128)(2,1)} %param.7) | copy-start | bytes 11943940
  3.4 9.6 %collective-permute-start = (bf16[224,384]{1,0:T(8,128)(2,1)S(1)}, bf16[224,384]{1,0:T(8,128)(2,1)S(1)}, u32[]{:S(2)}, u32[]{:S(2)}) collective-permute-start(bf16[224,384]{1,0:T(8,128)(2,1)S(1)} %get-tuple-element.28), channel_id=1, source_target_pairs={{0,24},{4,28},{8,16},{12,20},{16,8},{20,12},{24,0},{28,4},{1,25},{... | collective-permute-start | bytes 516104 | tf_op jit(solution)/shard_map/ppermute | solution.py:459
  7.4 8.5 %collective-permute-start.1 = (bf16[224,384]{1,0:T(8,128)(2,1)S(1)}, bf16[224,384]{1,0:T(8,128)(2,1)S(1)}, u32[]{:S(2)}, u32[]{:S(2)}) collective-permute-start(bf16[224,384]{1,0:T(8,128)(2,1)S(1)} %get-tuple-element.29), channel_id=1, source_target_pairs={{0,28},{4,24},{8,20},{12,16},{16,12},{20,8},{24,4},{28,0},{1,29},{... | collective-permute-start | bytes 516104 | tf_op jit(solution)/shard_map/ppermute | solution.py:459
  7.4 10.3 %copy-start.3 = (bf16[4,1152]{1,0:T(4,128)(2,1)S(1)}, bf16[4,1152]{1,0:T(4,128)(2,1)}, u32[]{:S(2)}) copy-start(bf16[4,1152]{1,0:T(4,128)(2,1)} %text_ref.1) | copy-start | bytes 27652
  7.4 11.9 %copy-start.2 = (s32[1,3072]{1,0:T(1,128)S(1)}, s32[1,3072]{1,0:T(1,128)}, u32[]{:S(2)}) copy-start(s32[1,3072]{1,0:T(1,128)} %ids_ref.5) | copy-start | bytes 36868
  9.4 8.4 %collective-permute-start.2 = (bf16[224,384]{1,0:T(8,128)(2,1)S(1)}, bf16[224,384]{1,0:T(8,128)(2,1)S(1)}, u32[]{:S(2)}, u32[]{:S(2)}) collective-permute-start(bf16[224,384]{1,0:T(8,128)(2,1)S(1)} %get-tuple-element.32), channel_id=1, source_target_pairs={{0,4},{4,0},{8,12},{12,8},{16,20},{20,16},{24,28},{28,24},{1,5},{5... | collective-permute-start | bytes 516104 | tf_op jit(solution)/shard_map/ppermute | solution.py:459
  9.6 11.8 %collective-permute-start.3 = (bf16[224,384]{1,0:T(8,128)(2,1)S(1)}, bf16[224,384]{1,0:T(8,128)(2,1)S(1)}, u32[]{:S(2)}, u32[]{:S(2)}) collective-permute-start(bf16[224,384]{1,0:T(8,128)(2,1)S(1)} %get-tuple-element.39), channel_id=1, source_target_pairs={{0,8},{4,12},{8,0},{12,4},{16,24},{20,28},{24,16},{28,20},{1,9},{5... | collective-permute-start | bytes 516104 | tf_op jit(solution)/shard_map/ppermute | solution.py:459
  11.5 9.9 %collective-permute-start.4 = (bf16[224,384]{1,0:T(8,128)(2,1)S(1)}, bf16[224,384]{1,0:T(8,128)(2,1)S(1)}, u32[]{:S(2)}, u32[]{:S(2)}) collective-permute-start(bf16[224,384]{1,0:T(8,128)(2,1)S(1)} %get-tuple-element.40), channel_id=1, source_target_pairs={{0,16},{4,20},{8,24},{12,28},{16,0},{20,4},{24,8},{28,12},{1,17},{... | collective-permute-start | bytes 516104 | tf_op jit(solution)/shard_map/ppermute | solution.py:459
  13.0 9.1 %collective-permute-start.5 = (bf16[224,384]{1,0:T(8,128)(2,1)S(1)}, bf16[224,384]{1,0:T(8,128)(2,1)S(1)}, u32[]{:S(2)}, u32[]{:S(2)}) collective-permute-start(bf16[224,384]{1,0:T(8,128)(2,1)S(1)} %get-tuple-element.41), channel_id=1, source_target_pairs={{0,12},{4,8},{8,4},{12,0},{16,28},{20,24},{24,20},{28,16},{1,13},{... | collective-permute-start | bytes 516104 | tf_op jit(solution)/shard_map/ppermute | solution.py:459
  15.9 6.8 %collective-permute-start.6 = (bf16[224,384]{1,0:T(8,128)(2,1)S(1)}, bf16[224,384]{1,0:T(8,128)(2,1)S(1)}, u32[]{:S(2)}, u32[]{:S(2)}) collective-permute-start(bf16[224,384]{1,0:T(8,128)(2,1)S(1)} %get-tuple-element.42), channel_id=1, source_target_pairs={{0,20},{4,16},{8,28},{12,24},{16,4},{20,0},{24,12},{28,8},{1,21},{... | collective-permute-start | bytes 516104 | tf_op jit(solution)/shard_map/ppermute | solution.py:459
  17.7 3.7 %collective-permute-start.7 = (bf16[4,1152]{1,0:T(4,128)(2,1)S(1)}, bf16[4,1152]{1,0:T(4,128)(2,1)S(1)}, u32[]{:S(2)}, u32[]{:S(2)}) collective-permute-start(bf16[4,1152]{1,0:T(4,128)(2,1)S(1)} %copy-done.3), channel_id=1, source_target_pairs={{1,0},{0,1},{3,2},{2,3},{6,4},{7,5},{4,6},{5,7},{11,8},{10,9},{9,1... | collective-permute-start | bytes 27656 | tf_op jit(solution)/shard_map/ppermute | solution.py:459
  22.7 18.2 %copy-start.1 = (bf16[1,384,1152]{2,1,0:T(8,128)(2,1)S(1)}, bf16[1,384,1152]{2,1,0:T(8,128)(2,1)}, u32[]{:S(2)}) copy-start(bf16[1,384,1152]{2,1,0:T(8,128)(2,1)} %param.5) | copy-start | bytes 2654212
  30.2 5.5 %collective-permute-start.8 = (bf16[96,384]{1,0:T(8,128)(2,1)S(1)}, bf16[96,384]{1,0:T(8,128)(2,1)S(1)}, u32[]{:S(2)}, u32[]{:S(2)}) collective-permute-start(bf16[96,384]{1,0:T(8,128)(2,1)S(1)} %get-tuple-element.44), channel_id=1, source_target_pairs={{0,24},{4,28},{8,16},{12,20},{16,8},{20,12},{24,0},{28,4},{1,25},{... | collective-permute-start | bytes 221192 | tf_op jit(solution)/shard_map/ppermute | solution.py:459
  32.5 5.2 %collective-permute-start.9 = (bf16[96,384]{1,0:T(8,128)(2,1)S(1)}, bf16[96,384]{1,0:T(8,128)(2,1)S(1)}, u32[]{:S(2)}, u32[]{:S(2)}) collective-permute-start(bf16[96,384]{1,0:T(8,128)(2,1)S(1)} %get-tuple-element.45), channel_id=1, source_target_pairs={{0,28},{4,24},{8,20},{12,16},{16,12},{20,8},{24,4},{28,0},{1,29},{... | collective-permute-start | bytes 221192 | tf_op jit(solution)/shard_map/ppermute | solution.py:459
  32.7 6.3 %collective-permute-start.10 = (bf16[96,384]{1,0:T(8,128)(2,1)S(1)}, bf16[96,384]{1,0:T(8,128)(2,1)S(1)}, u32[]{:S(2)}, u32[]{:S(2)}) collective-permute-start(bf16[96,384]{1,0:T(8,128)(2,1)S(1)} %get-tuple-element.46), channel_id=1, source_target_pairs={{0,8},{4,12},{8,0},{12,4},{16,24},{20,28},{24,16},{28,20},{1,9},{5... | collective-permute-start | bytes 221192 | tf_op jit(solution)/shard_map/ppermute | solution.py:459
  34.5 5.2 %collective-permute-start.11 = (bf16[96,384]{1,0:T(8,128)(2,1)S(1)}, bf16[96,384]{1,0:T(8,128)(2,1)S(1)}, u32[]{:S(2)}, u32[]{:S(2)}) collective-permute-start(bf16[96,384]{1,0:T(8,128)(2,1)S(1)} %get-tuple-element.47), channel_id=1, source_target_pairs={{0,16},{4,20},{8,24},{12,28},{16,0},{20,4},{24,8},{28,12},{1,17},{... | collective-permute-start | bytes 221192 | tf_op jit(solution)/shard_map/ppermute | solution.py:459
  35.7 5.1 %collective-permute-start.12 = (bf16[96,384]{1,0:T(8,128)(2,1)S(1)}, bf16[96,384]{1,0:T(8,128)(2,1)S(1)}, u32[]{:S(2)}, u32[]{:S(2)}) collective-permute-start(bf16[96,384]{1,0:T(8,128)(2,1)S(1)} %get-tuple-element.48), channel_id=1, source_target_pairs={{0,12},{4,8},{8,4},{12,0},{16,28},{20,24},{24,20},{28,16},{1,13},{... | collective-permute-start | bytes 221192 | tf_op jit(solution)/shard_map/ppermute | solution.py:459
  35.7 5.2 %collective-permute-start.13 = (bf16[96,384]{1,0:T(8,128)(2,1)S(1)}, bf16[96,384]{1,0:T(8,128)(2,1)S(1)}, u32[]{:S(2)}, u32[]{:S(2)}) collective-permute-start(bf16[96,384]{1,0:T(8,128)(2,1)S(1)} %get-tuple-element.49), channel_id=1, source_target_pairs={{0,20},{4,16},{8,28},{12,24},{16,4},{20,0},{24,12},{28,8},{1,21},{... | collective-permute-start | bytes 221192 | tf_op jit(solution)/shard_map/ppermute | solution.py:459
  37.7 3.2 %collective-permute-start.14 = (bf16[96,384]{1,0:T(8,128)(2,1)S(1)}, bf16[96,384]{1,0:T(8,128)(2,1)S(1)}, u32[]{:S(2)}, u32[]{:S(2)}) collective-permute-start(bf16[96,384]{1,0:T(8,128)(2,1)S(1)} %get-tuple-element.50), channel_id=1, source_target_pairs={{0,4},{4,0},{8,12},{12,8},{16,20},{20,16},{24,28},{28,24},{1,5},{5... | collective-permute-start | bytes 221192 | tf_op jit(solution)/shard_map/ppermute | solution.py:459

commit v26 on v25

--- a/solution.py
+++ b/solution.py
@@ -17,7 +17,7 @@
 KEY_AT = SIZE - SPARE
 QUERY_AT = 2 * SIZE
 TEXT_ROWS = 16
-RUN = 5
+RUN = 3
 HIDDEN = -1e30
 ORDER = (6, 7, 2, 4, 3, 5, 1, 0)
 EARLY = (6, 7, 1, 0)

time: 43.2 us -> 43.5 us (level)
  no operation moved by 1% of the time
where the time goes in v26:
time: 43.5 us; the launch traced here: 43.3 us
  starting transfers between devices  17.6 us (40%)
  Pallas kernels  16.3 us (37%)
  waiting for transfers between devices  8.75 us (20%)
  between operations  0.69 us (2%)
    ppermute x15, starting transfers between devices, moved(): return lax.ppermute(value, axis, pairs)  17.6 us
    ppermute x15, waiting for transfers between devices, moved(): return lax.ppermute(value, axis, pairs)  8.75 us
    pallas_call x1, Pallas kernels, local(): call(functools.partial(attend_kernel, images, piggy, halo), (shape((padde...  7.75 us
    pallas_call x1, Pallas kernels, local(): call(functools.partial(far_kernel, images, piggy), (shape((depth, count),...  2.79 us
    pallas_call x1, Pallas kernels, local(): call(functools.partial(finish_kernel, images), (shape((count, depth), bf1...  2.12 us
    pallas_call x1, Pallas kernels, local(): call(functools.partial(near_kernel, piggy), (block,) * 6, [], in_vmem(3),...  1.95 us
    pallas_call x1, Pallas kernels, local(): call(functools.partial(prepare_kernel, images, halo), (shape((len(EARLY)...  1.64 us
  transfers between devices with their start and end apart: 15, of which 9 were waited for; matrix products, arithmetic and copies ran while one was open for 0% of the time, Pallas kernels for 8%

profile of v26, /device:TPU:0, one launch (start us, length us, event | category | flops | bytes accessed | tf_op | source)
XLA Modules:
  0.0 43.3 jit_solution(16433340297067760045)
XLA Ops:
  0.6 0.0 copy-start
  0.6 2.8 %shard_map.68 = (bf16[1152,384]{1,0:T(8,128)(2,1)S(1)}, f32[8,1152]{1,0:T(8,128)S(1)}, bf16[224,384]{1,0:T(8,128)(2,1)S(1)}, bf16[224,384]{1,0:T(8,128)(2,1)S(1)}) custom-call(s32[1,3072]{1,0:T(1,128)} %ids_ref.5, bf16[384,1152]{1,0:T(8,128)(2,1)} %bitcast.6, bf16[1728,1152]{1,0:T(8,128)(2,1)} %bitcast.4), custom_call_target="tpu_custom_call" | custom-call | flops 382205952 | bytes 8388608 | tf_op jit(solution)/shard_map/pallas_call | solution.py:510
  3.4 4.0 %collective-permute-start = (bf16[224,384]{1,0:T(8,128)(2,1)S(1)}, bf16[224,384]{1,0:T(8,128)(2,1)S(1)}, u32[]{:S(2)}, u32[]{:S(2)}) collective-permute-start(bf16[224,384]{1,0:T(8,128)(2,1)S(1)} %get-tuple-element.28), channel_id=1, source_target_pairs={{0,24},{4,28},{8,16},{12,20},{16,8},{20,12},{24,0},{28,4},{1,25},{... | collective-permute-start | bytes 516104 | tf_op jit(solution)/shard_map/ppermute | solution.py:459
  7.4 0.0 collective-permute-start.1
  7.4 0.0 copy-done
  7.4 0.0 copy-start.3
  7.4 0.0 copy-start.2
  7.4 1.9 %shard_map.69 = (bf16[224,384]{1,0:T(8,128)(2,1)S(1)}, bf16[224,384]{1,0:T(8,128)(2,1)S(1)}, bf16[224,384]{1,0:T(8,128)(2,1)S(1)}, bf16[224,384]{1,0:T(8,128)(2,...) custom-call(bf16[1152,384]{1,0:T(8,128)(2,1)S(1)} %get-tuple-element.30.normed_ref, ...), custom_call_target="tpu_custom_call" | custom-call | flops 1146617856 | bytes 8388608 | tf_op jit(solution)/shard_map/pallas_call | solution.py:524
  9.4 0.2 collective-permute-start.2
  9.6 1.9 %collective-permute-start.3 = (bf16[224,384]{1,0:T(8,128)(2,1)S(1)}, bf16[224,384]{1,0:T(8,128)(2,1)S(1)}, u32[]{:S(2)}, u32[]{:S(2)}) collective-permute-start(bf16[224,384]{1,0:T(8,128)(2,1)S(1)} %get-tuple-element.39), channel_id=1, source_target_pairs={{0,8},{4,12},{8,0},{12,4},{16,24},{20,28},{24,16},{28,20},{1,9},{5... | collective-permute-start | bytes 516104 | tf_op jit(solution)/shard_map/ppermute | solution.py:459
  11.5 1.5 %collective-permute-start.4 = (bf16[224,384]{1,0:T(8,128)(2,1)S(1)}, bf16[224,384]{1,0:T(8,128)(2,1)S(1)}, u32[]{:S(2)}, u32[]{:S(2)}) collective-permute-start(bf16[224,384]{1,0:T(8,128)(2,1)S(1)} %get-tuple-element.40), channel_id=1, source_target_pairs={{0,16},{4,20},{8,24},{12,28},{16,0},{20,4},{24,8},{28,12},{1,17},{... | collective-permute-start | bytes 516104 | tf_op jit(solution)/shard_map/ppermute | solution.py:459
  13.0 0.0 collective-permute-done.rest_0_
  13.0 0.0 collective-permute-start.5
  13.0 2.9 %collective-permute-done.1.rest_1_ = bf16[224,384]{1,0:T(8,128)(2,1)S(1)} collective-permute-done((bf16[224,384]{1,0:T(8,128)(2,1)S(1)}, bf16[224,384]{1,0:T(8,128)(2,1)S(1)}, u32[]{:S(2)}, u32[]{:S(2)}) %collective-permute-start.1) | collective-permute-done | bytes 172064 | tf_op jit(solution)/shard_map/ppermute | solution.py:459
  15.9 1.9 %collective-permute-start.6 = (bf16[224,384]{1,0:T(8,128)(2,1)S(1)}, bf16[224,384]{1,0:T(8,128)(2,1)S(1)}, u32[]{:S(2)}, u32[]{:S(2)}) collective-permute-start(bf16[224,384]{1,0:T(8,128)(2,1)S(1)} %get-tuple-element.42), channel_id=1, source_target_pairs={{0,20},{4,16},{8,28},{12,24},{16,4},{20,0},{24,12},{28,8},{1,21},{... | collective-permute-start | bytes 516104 | tf_op jit(solution)/shard_map/ppermute | solution.py:459
  17.7 0.0 collective-permute-done.2.rest_2_
  17.7 0.0 copy-done.3
  17.7 1.6 %collective-permute-start.7 = (bf16[4,1152]{1,0:T(4,128)(2,1)S(1)}, bf16[4,1152]{1,0:T(4,128)(2,1)S(1)}, u32[]{:S(2)}, u32[]{:S(2)}) collective-permute-start(bf16[4,1152]{1,0:T(4,128)(2,1)S(1)} %copy-done.3), channel_id=1, source_target_pairs={{1,0},{0,1},{3,2},{2,3},{6,4},{7,5},{4,6},{5,7},{11,8},{10,9},{9,1... | collective-permute-start | bytes 27656 | tf_op jit(solution)/shard_map/ppermute | solution.py:459
  19.3 0.0 copy-done.2
  19.3 1.6 %shard_map.70 = (bf16[1536,128]{1,0:T(8,128)(2,1)S(1)}, f32[2,8,3072]{2,1,0:T(8,128)S(1)}, s32[8,128]{1,0:T(8,128)S(1)}, bf16[640,1152]{1,0:T(8,128)(2,1)S(1)}) custom-call(s32[1,3072]{1,0:T(1,128)S(1)} %copy-done.2, bf16[576,1152]{1,0:T(8,128)(2,1)} %out_weight_ref.1, bf16[224,384]{1,0:T(8,128)(2,1)S(1)} %collective-permute-done.rest_0_, ...), custom_call_target="tpu_custom_call" | custom-call | flops 1073741824 | bytes 8388608 | tf_op jit(solution)/shard_map/pallas_call | solution.py:565
  21.0 0.4 collective-permute-done.7.rest_8_
  21.4 0.0 collective-permute-done.3.rest_4_
  21.4 0.0 collective-permute-done.4.rest_5_
  21.4 0.7 %collective-permute-done.5.rest_6_ = bf16[224,384]{1,0:T(8,128)(2,1)S(1)} collective-permute-done((bf16[224,384]{1,0:T(8,128)(2,1)S(1)}, bf16[224,384]{1,0:T(8,128)(2,1)S(1)}, u32[]{:S(2)}, u32[]{:S(2)}) %collective-permute-start.5) | collective-permute-done | bytes 172064 | tf_op jit(solution)/shard_map/ppermute | solution.py:459
  22.1 0.6 %collective-permute-done.6.rest_7_ = bf16[224,384]{1,0:T(8,128)(2,1)S(1)} collective-permute-done((bf16[224,384]{1,0:T(8,128)(2,1)S(1)}, bf16[224,384]{1,0:T(8,128)(2,1)S(1)}, u32[]{:S(2)}, u32[]{:S(2)}) %collective-permute-start.6) | collective-permute-done | bytes 172064 | tf_op jit(solution)/shard_map/ppermute | solution.py:459
  22.7 0.0 copy-start.1
  22.7 7.7 %shard_map.71 = (bf16[96,384]{1,0:T(8,128)(2,1)S(1)}, bf16[96,384]{1,0:T(8,128)(2,1)S(1)}, bf16[96,384]{1,0:T(8,128)(2,1)S(1)}, bf16[96,384]{1,0:T(8,128)(2,1)S(...) custom-call(s32[1,3072]{1,0:T(1,128)S(1)} %copy-done.2, ...), custom_call_target="tpu_custom_call" | custom-call | flops 905969664 | bytes 8388608 | tf_op jit(solution)/shard_map/pallas_call | solution.py:578
  30.5 2.3 %collective-permute-start.8 = (bf16[96,384]{1,0:T(8,128)(2,1)S(1)}, bf16[96,384]{1,0:T(8,128)(2,1)S(1)}, u32[]{:S(2)}, u32[]{:S(2)}) collective-permute-start(bf16[96,384]{1,0:T(8,128)(2,1)S(1)} %get-tuple-element.44), channel_id=1, source_target_pairs={{0,24},{4,28},{8,16},{12,20},{16,8},{20,12},{24,0},{28,4},{1,25},{... | collective-permute-start | bytes 221192 | tf_op jit(solution)/shard_map/ppermute | solution.py:459
  32.8 0.2 collective-permute-start.9
  33.0 1.8 %collective-permute-start.10 = (bf16[96,384]{1,0:T(8,128)(2,1)S(1)}, bf16[96,384]{1,0:T(8,128)(2,1)S(1)}, u32[]{:S(2)}, u32[]{:S(2)}) collective-permute-start(bf16[96,384]{1,0:T(8,128)(2,1)S(1)} %get-tuple-element.46), channel_id=1, source_target_pairs={{0,8},{4,12},{8,0},{12,4},{16,24},{20,28},{24,16},{28,20},{1,9},{5... | collective-permute-start | bytes 221192 | tf_op jit(solution)/shard_map/ppermute | solution.py:459
  34.8 1.2 %collective-permute-start.11 = (bf16[96,384]{1,0:T(8,128)(2,1)S(1)}, bf16[96,384]{1,0:T(8,128)(2,1)S(1)}, u32[]{:S(2)}, u32[]{:S(2)}) collective-permute-start(bf16[96,384]{1,0:T(8,128)(2,1)S(1)} %get-tuple-element.47), channel_id=1, source_target_pairs={{0,16},{4,20},{8,24},{12,28},{16,0},{20,4},{24,8},{28,12},{1,17},{... | collective-permute-start | bytes 221192 | tf_op jit(solution)/shard_map/ppermute | solution.py:459
  35.9 0.0 collective-permute-start.12
  36.0 0.0 collective-permute-done.8.rest_0_
  36.0 0.8 %collective-permute-start.13 = (bf16[96,384]{1,0:T(8,128)(2,1)S(1)}, bf16[96,384]{1,0:T(8,128)(2,1)S(1)}, u32[]{:S(2)}, u32[]{:S(2)}) collective-permute-start(bf16[96,384]{1,0:T(8,128)(2,1)S(1)} %get-tuple-element.49), channel_id=1, source_target_pairs={{0,20},{4,16},{8,28},{12,24},{16,4},{20,0},{24,12},{28,8},{1,21},{... | collective-permute-start | bytes 221192 | tf_op jit(solution)/shard_map/ppermute | solution.py:459
  36.8 1.2 %collective-permute-done.9.rest_1_ = bf16[96,384]{1,0:T(8,128)(2,1)S(1)} collective-permute-done((bf16[96,384]{1,0:T(8,128)(2,1)S(1)}, bf16[96,384]{1,0:T(8,128)(2,1)S(1)}, u32[]{:S(2)}, u32[]{:S(2)}) %collective-permute-start.9) | collective-permute-done | bytes 73760 | tf_op jit(solution)/shard_map/ppermute | solution.py:459
  38.0 0.3 collective-permute-start.14
  38.3 1.0 %collective-permute-done.10.rest_2_ = bf16[96,384]{1,0:T(8,128)(2,1)S(1)} collective-permute-done((bf16[96,384]{1,0:T(8,128)(2,1)S(1)}, bf16[96,384]{1,0:T(8,128)(2,1)S(1)}, u32[]{:S(2)}, u32[]{:S(2)}) %collective-permute-start.10) | collective-permute-done | bytes 73760 | tf_op jit(solution)/shard_map/ppermute | solution.py:459
  39.3 0.7 %collective-permute-done.11.rest_3_ = bf16[96,384]{1,0:T(8,128)(2,1)S(1)} collective-permute-done((bf16[96,384]{1,0:T(8,128)(2,1)S(1)}, bf16[96,384]{1,0:T(8,128)(2,1)S(1)}, u32[]{:S(2)}, u32[]{:S(2)}) %collective-permute-start.11) | collective-permute-done | bytes 73760 | tf_op jit(solution)/shard_map/ppermute | solution.py:459
  40.0 1.1 %collective-permute-done.12.rest_4_ = bf16[96,384]{1,0:T(8,128)(2,1)S(1)} collective-permute-done((bf16[96,384]{1,0:T(8,128)(2,1)S(1)}, bf16[96,384]{1,0:T(8,128)(2,1)S(1)}, u32[]{:S(2)}, u32[]{:S(2)}) %collective-permute-start.12) | collective-permute-done | bytes 73760 | tf_op jit(solution)/shard_map/ppermute | solution.py:459
  41.1 0.2 collective-permute-done.13.rest_5_
  41.2 0.0 collective-permute-done.14.rest_6_
  41.2 0.0 copy-done.1
  41.2 2.1 %shard_map.72 = (bf16[384,1152]{1,0:T(8,128)(2,1)}, f32[1,4]{1,0:T(1,128)}) custom-call(bf16[384,1152]{1,0:T(8,128)(2,1)S(1)} %bitcast.7, bf16[640,1152]{1,0:T(8,128)(2,1)S(1)} %get-tuple-element.35.weight_ref, bf16[4,1152]{1,0:T(4,128)(2,1)S(1)} %copy-done.3, bf16[96,384]{1,0:T(8,128)(2,1)S(1)} %collective-permute-done.8.rest_0_, ...), custom_call_target="tpu_custom_call" | custom-call | flops 509607936 | bytes 8388608 | tf_op jit(solution)/shard_map/pallas_call | solution.py:607
Async XLA Ops:
  0.6 6.8 %copy-start = (bf16[1152,1728]{0,1:T(8,128)(2,1)S(1)}, bf16[1152,1728]{0,1:T(8,128)(2,1)}, u32[]{:S(2)}) copy-start(bf16[1152,1728]{0,1:T(8,128)(2,1)} %param.7) | copy-start | bytes 11943940
  3.4 9.6 %collective-permute-start = (bf16[224,384]{1,0:T(8,128)(2,1)S(1)}, bf16[224,384]{1,0:T(8,128)(2,1)S(1)}, u32[]{:S(2)}, u32[]{:S(2)}) collective-permute-start(bf16[224,384]{1,0:T(8,128)(2,1)S(1)} %get-tuple-element.28), channel_id=1, source_target_pairs={{0,24},{4,28},{8,16},{12,20},{16,8},{20,12},{24,0},{28,4},{1,25},{... | collective-permute-start | bytes 516104 | tf_op jit(solution)/shard_map/ppermute | solution.py:459
  7.4 8.5 %collective-permute-start.1 = (bf16[224,384]{1,0:T(8,128)(2,1)S(1)}, bf16[224,384]{1,0:T(8,128)(2,1)S(1)}, u32[]{:S(2)}, u32[]{:S(2)}) collective-permute-start(bf16[224,384]{1,0:T(8,128)(2,1)S(1)} %get-tuple-element.29), channel_id=1, source_target_pairs={{0,28},{4,24},{8,20},{12,16},{16,12},{20,8},{24,4},{28,0},{1,29},{... | collective-permute-start | bytes 516104 | tf_op jit(solution)/shard_map/ppermute | solution.py:459
  7.4 10.3 %copy-start.3 = (bf16[4,1152]{1,0:T(4,128)(2,1)S(1)}, bf16[4,1152]{1,0:T(4,128)(2,1)}, u32[]{:S(2)}) copy-start(bf16[4,1152]{1,0:T(4,128)(2,1)} %text_ref.1) | copy-start | bytes 27652
  7.4 11.9 %copy-start.2 = (s32[1,3072]{1,0:T(1,128)S(1)}, s32[1,3072]{1,0:T(1,128)}, u32[]{:S(2)}) copy-start(s32[1,3072]{1,0:T(1,128)} %ids_ref.5) | copy-start | bytes 36868
  9.4 8.4 %collective-permute-start.2 = (bf16[224,384]{1,0:T(8,128)(2,1)S(1)}, bf16[224,384]{1,0:T(8,128)(2,1)S(1)}, u32[]{:S(2)}, u32[]{:S(2)}) collective-permute-start(bf16[224,384]{1,0:T(8,128)(2,1)S(1)} %get-tuple-element.32), channel_id=1, source_target_pairs={{0,4},{4,0},{8,12},{12,8},{16,20},{20,16},{24,28},{28,24},{1,5},{5... | collective-permute-start | bytes 516104 | tf_op jit(solution)/shard_map/ppermute | solution.py:459
  9.6 11.8 %collective-permute-start.3 = (bf16[224,384]{1,0:T(8,128)(2,1)S(1)}, bf16[224,384]{1,0:T(8,128)(2,1)S(1)}, u32[]{:S(2)}, u32[]{:S(2)}) collective-permute-start(bf16[224,384]{1,0:T(8,128)(2,1)S(1)} %get-tuple-element.39), channel_id=1, source_target_pairs={{0,8},{4,12},{8,0},{12,4},{16,24},{20,28},{24,16},{28,20},{1,9},{5... | collective-permute-start | bytes 516104 | tf_op jit(solution)/shard_map/ppermute | solution.py:459
  11.5 9.9 %collective-permute-start.4 = (bf16[224,384]{1,0:T(8,128)(2,1)S(1)}, bf16[224,384]{1,0:T(8,128)(2,1)S(1)}, u32[]{:S(2)}, u32[]{:S(2)}) collective-permute-start(bf16[224,384]{1,0:T(8,128)(2,1)S(1)} %get-tuple-element.40), channel_id=1, source_target_pairs={{0,16},{4,20},{8,24},{12,28},{16,0},{20,4},{24,8},{28,12},{1,17},{... | collective-permute-start | bytes 516104 | tf_op jit(solution)/shard_map/ppermute | solution.py:459
  13.0 9.1 %collective-permute-start.5 = (bf16[224,384]{1,0:T(8,128)(2,1)S(1)}, bf16[224,384]{1,0:T(8,128)(2,1)S(1)}, u32[]{:S(2)}, u32[]{:S(2)}) collective-permute-start(bf16[224,384]{1,0:T(8,128)(2,1)S(1)} %get-tuple-element.41), channel_id=1, source_target_pairs={{0,12},{4,8},{8,4},{12,0},{16,28},{20,24},{24,20},{28,16},{1,13},{... | collective-permute-start | bytes 516104 | tf_op jit(solution)/shard_map/ppermute | solution.py:459
  15.9 6.8 %collective-permute-start.6 = (bf16[224,384]{1,0:T(8,128)(2,1)S(1)}, bf16[224,384]{1,0:T(8,128)(2,1)S(1)}, u32[]{:S(2)}, u32[]{:S(2)}) collective-permute-start(bf16[224,384]{1,0:T(8,128)(2,1)S(1)} %get-tuple-element.42), channel_id=1, source_target_pairs={{0,20},{4,16},{8,28},{12,24},{16,4},{20,0},{24,12},{28,8},{1,21},{... | collective-permute-start | bytes 516104 | tf_op jit(solution)/shard_map/ppermute | solution.py:459
  17.7 3.7 %collective-permute-start.7 = (bf16[4,1152]{1,0:T(4,128)(2,1)S(1)}, bf16[4,1152]{1,0:T(4,128)(2,1)S(1)}, u32[]{:S(2)}, u32[]{:S(2)}) collective-permute-start(bf16[4,1152]{1,0:T(4,128)(2,1)S(1)} %copy-done.3), channel_id=1, source_target_pairs={{1,0},{0,1},{3,2},{2,3},{6,4},{7,5},{4,6},{5,7},{11,8},{10,9},{9,1... | collective-permute-start | bytes 27656 | tf_op jit(solution)/shard_map/ppermute | solution.py:459
  22.7 18.5 %copy-start.1 = (bf16[1,384,1152]{2,1,0:T(8,128)(2,1)S(1)}, bf16[1,384,1152]{2,1,0:T(8,128)(2,1)}, u32[]{:S(2)}) copy-start(bf16[1,384,1152]{2,1,0:T(8,128)(2,1)} %param.5) | copy-start | bytes 2654212
  30.5 5.5 %collective-permute-start.8 = (bf16[96,384]{1,0:T(8,128)(2,1)S(1)}, bf16[96,384]{1,0:T(8,128)(2,1)S(1)}, u32[]{:S(2)}, u32[]{:S(2)}) collective-permute-start(bf16[96,384]{1,0:T(8,128)(2,1)S(1)} %get-tuple-element.44), channel_id=1, source_target_pairs={{0,24},{4,28},{8,16},{12,20},{16,8},{20,12},{24,0},{28,4},{1,25},{... | collective-permute-start | bytes 221192 | tf_op jit(solution)/shard_map/ppermute | solution.py:459
  32.8 5.2 %collective-permute-start.9 = (bf16[96,384]{1,0:T(8,128)(2,1)S(1)}, bf16[96,384]{1,0:T(8,128)(2,1)S(1)}, u32[]{:S(2)}, u32[]{:S(2)}) collective-permute-start(bf16[96,384]{1,0:T(8,128)(2,1)S(1)} %get-tuple-element.45), channel_id=1, source_target_pairs={{0,28},{4,24},{8,20},{12,16},{16,12},{20,8},{24,4},{28,0},{1,29},{... | collective-permute-start | bytes 221192 | tf_op jit(solution)/shard_map/ppermute | solution.py:459
  33.0 6.3 %collective-permute-start.10 = (bf16[96,384]{1,0:T(8,128)(2,1)S(1)}, bf16[96,384]{1,0:T(8,128)(2,1)S(1)}, u32[]{:S(2)}, u32[]{:S(2)}) collective-permute-start(bf16[96,384]{1,0:T(8,128)(2,1)S(1)} %get-tuple-element.46), channel_id=1, source_target_pairs={{0,8},{4,12},{8,0},{12,4},{16,24},{20,28},{24,16},{28,20},{1,9},{5... | collective-permute-start | bytes 221192 | tf_op jit(solution)/shard_map/ppermute | solution.py:459
  34.8 5.2 %collective-permute-start.11 = (bf16[96,384]{1,0:T(8,128)(2,1)S(1)}, bf16[96,384]{1,0:T(8,128)(2,1)S(1)}, u32[]{:S(2)}, u32[]{:S(2)}) collective-permute-start(bf16[96,384]{1,0:T(8,128)(2,1)S(1)} %get-tuple-element.47), channel_id=1, source_target_pairs={{0,16},{4,20},{8,24},{12,28},{16,0},{20,4},{24,8},{28,12},{1,17},{... | collective-permute-start | bytes 221192 | tf_op jit(solution)/shard_map/ppermute | solution.py:459
  35.9 5.1 %collective-permute-start.12 = (bf16[96,384]{1,0:T(8,128)(2,1)S(1)}, bf16[96,384]{1,0:T(8,128)(2,1)S(1)}, u32[]{:S(2)}, u32[]{:S(2)}) collective-permute-start(bf16[96,384]{1,0:T(8,128)(2,1)S(1)} %get-tuple-element.48), channel_id=1, source_target_pairs={{0,12},{4,8},{8,4},{12,0},{16,28},{20,24},{24,20},{28,16},{1,13},{... | collective-permute-start | bytes 221192 | tf_op jit(solution)/shard_map/ppermute | solution.py:459
  36.0 5.2 %collective-permute-start.13 = (bf16[96,384]{1,0:T(8,128)(2,1)S(1)}, bf16[96,384]{1,0:T(8,128)(2,1)S(1)}, u32[]{:S(2)}, u32[]{:S(2)}) collective-permute-start(bf16[96,384]{1,0:T(8,128)(2,1)S(1)} %get-tuple-element.49), channel_id=1, source_target_pairs={{0,20},{4,16},{8,28},{12,24},{16,4},{20,0},{24,12},{28,8},{1,21},{... | collective-permute-start | bytes 221192 | tf_op jit(solution)/shard_map/ppermute | solution.py:459
  38.0 3.2 %collective-permute-start.14 = (bf16[96,384]{1,0:T(8,128)(2,1)S(1)}, bf16[96,384]{1,0:T(8,128)(2,1)S(1)}, u32[]{:S(2)}, u32[]{:S(2)}) collective-permute-start(bf16[96,384]{1,0:T(8,128)(2,1)S(1)} %get-tuple-element.50), channel_id=1, source_target_pairs={{0,4},{4,0},{8,12},{12,8},{16,20},{20,16},{24,28},{28,24},{1,5},{5... | collective-permute-start | bytes 221192 | tf_op jit(solution)/shard_map/ppermute | solution.py:459

commit v27 on v24

--- a/solution.py
+++ b/solution.py
@@ -17,7 +17,7 @@
 KEY_AT = SIZE - SPARE
 QUERY_AT = 2 * SIZE
 TEXT_ROWS = 16
-RUN = 5
+RUN = 8
 HIDDEN = -1e30
 ORDER = (6, 7, 2, 4, 3, 5, 1, 0)
 EARLY = (6, 7, 1, 0)
@@ -187,7 +187,7 @@
 
 
 def attend_images(pairs, table, ids_ref, keys, values, queries, attended, work, query_base):
-    work = list(zip(work[0::2], work[1::2]))
+    work = list(zip(work[:2], work[2:]))
     window, tile = work[0][0].shape
     size = attended.shape[0] - SPARE
 
@@ -214,8 +214,8 @@
     def run(step, _):
         for place in range(RUN):
             state = step * RUN + place
-            score(state + 1, *work[(place + 1) % RUN])
-            weigh(state, *work[place])
+            score(state + 1, *work[(place + 1) % 2])
+            weigh(state, *work[place % 2])
         return 0
 
     score(0, *work[0])
@@ -584,7 +584,8 @@
             pltpu.VMEM((LANES, length), bf16),
             pltpu.VMEM((padded, length), f32),
         ]
-        + [pltpu.VMEM((window, tile), f32), pltpu.VMEM((1, tile), f32)] * RUN
+        + [pltpu.VMEM((window, tile), f32)] * 2
+        + [pltpu.VMEM((1, tile), f32)] * 2
         + [
             pltpu.SMEM((images + 1,), jnp.int32),
             pltpu.SMEM((3, rounded_up(length // tile + images, RUN) + 1), jnp.int32),

time: 43.2 us -> 43.2 us (level)
  no operation moved by 1% of the time
where the time goes in v27:
time: 43.2 us; the launch traced here: 43 us
  starting transfers between devices  17.6 us (41%)
  Pallas kernels  15.9 us (37%)
  waiting for transfers between devices  8.77 us (20%)
  between operations  0.69 us (2%)
    ppermute x15, starting transfers between devices, moved(): return lax.ppermute(value, axis, pairs)  17.6 us
    ppermute x15, waiting for transfers between devices, moved(): return lax.ppermute(value, axis, pairs)  8.77 us
    pallas_call x1, Pallas kernels, local(): call(functools.partial(attend_kernel, images, piggy, halo), (shape((padde...  7.4 us
    pallas_call x1, Pallas kernels, local(): call(functools.partial(far_kernel, images, piggy), (shape((depth, count),...  2.79 us
    pallas_call x1, Pallas kernels, local(): call(functools.partial(finish_kernel, images), (shape((count, depth), bf1...  2.13 us
    pallas_call x1, Pallas kernels, local(): call(functools.partial(near_kernel, piggy), (block,) * 6, [], in_vmem(3),...  1.95 us
    pallas_call x1, Pallas kernels, local(): call(functools.partial(prepare_kernel, images, halo), (shape((len(EARLY)...  1.64 us
  transfers between devices with their start and end apart: 15, of which 9 were waited for; matrix products, arithmetic and copies ran while one was open for 0% of the time, Pallas kernels for 8%

profile of v27, /device:TPU:0, one launch (start us, length us, event | category | flops | bytes accessed | tf_op | source)
XLA Modules:
  0.0 43.0 jit_solution(13543832980562117009)
XLA Ops:
  0.6 0.0 copy-start
  0.6 2.8 %shard_map.68 = (bf16[1152,384]{1,0:T(8,128)(2,1)S(1)}, f32[8,1152]{1,0:T(8,128)S(1)}, bf16[224,384]{1,0:T(8,128)(2,1)S(1)}, bf16[224,384]{1,0:T(8,128)(2,1)S(1)}) custom-call(s32[1,3072]{1,0:T(1,128)} %ids_ref.5, bf16[384,1152]{1,0:T(8,128)(2,1)} %bitcast.6, bf16[1728,1152]{1,0:T(8,128)(2,1)} %bitcast.4), custom_call_target="tpu_custom_call" | custom-call | flops 382205952 | bytes 8388608 | tf_op jit(solution)/shard_map/pallas_call | solution.py:510
  3.4 4.0 %collective-permute-start = (bf16[224,384]{1,0:T(8,128)(2,1)S(1)}, bf16[224,384]{1,0:T(8,128)(2,1)S(1)}, u32[]{:S(2)}, u32[]{:S(2)}) collective-permute-start(bf16[224,384]{1,0:T(8,128)(2,1)S(1)} %get-tuple-element.28), channel_id=1, source_target_pairs={{0,24},{4,28},{8,16},{12,20},{16,8},{20,12},{24,0},{28,4},{1,25},{... | collective-permute-start | bytes 516104 | tf_op jit(solution)/shard_map/ppermute | solution.py:459
  7.4 0.0 collective-permute-start.1
  7.4 0.0 copy-done
  7.4 0.0 copy-start.3
  7.4 0.0 copy-start.2
  7.4 1.9 %shard_map.69 = (bf16[224,384]{1,0:T(8,128)(2,1)S(1)}, bf16[224,384]{1,0:T(8,128)(2,1)S(1)}, bf16[224,384]{1,0:T(8,128)(2,1)S(1)}, bf16[224,384]{1,0:T(8,128)(2,...) custom-call(bf16[1152,384]{1,0:T(8,128)(2,1)S(1)} %get-tuple-element.30.normed_ref, ...), custom_call_target="tpu_custom_call" | custom-call | flops 1146617856 | bytes 8388608 | tf_op jit(solution)/shard_map/pallas_call | solution.py:524
  9.4 0.2 collective-permute-start.2
  9.6 1.9 %collective-permute-start.3 = (bf16[224,384]{1,0:T(8,128)(2,1)S(1)}, bf16[224,384]{1,0:T(8,128)(2,1)S(1)}, u32[]{:S(2)}, u32[]{:S(2)}) collective-permute-start(bf16[224,384]{1,0:T(8,128)(2,1)S(1)} %get-tuple-element.39), channel_id=1, source_target_pairs={{0,8},{4,12},{8,0},{12,4},{16,24},{20,28},{24,16},{28,20},{1,9},{5... | collective-permute-start | bytes 516104 | tf_op jit(solution)/shard_map/ppermute | solution.py:459
  11.5 1.5 %collective-permute-start.4 = (bf16[224,384]{1,0:T(8,128)(2,1)S(1)}, bf16[224,384]{1,0:T(8,128)(2,1)S(1)}, u32[]{:S(2)}, u32[]{:S(2)}) collective-permute-start(bf16[224,384]{1,0:T(8,128)(2,1)S(1)} %get-tuple-element.40), channel_id=1, source_target_pairs={{0,16},{4,20},{8,24},{12,28},{16,0},{20,4},{24,8},{28,12},{1,17},{... | collective-permute-start | bytes 516104 | tf_op jit(solution)/shard_map/ppermute | solution.py:459
  13.0 0.0 collective-permute-done.rest_0_
  13.0 0.0 collective-permute-start.5
  13.0 2.9 %collective-permute-done.1.rest_1_ = bf16[224,384]{1,0:T(8,128)(2,1)S(1)} collective-permute-done((bf16[224,384]{1,0:T(8,128)(2,1)S(1)}, bf16[224,384]{1,0:T(8,128)(2,1)S(1)}, u32[]{:S(2)}, u32[]{:S(2)}) %collective-permute-start.1) | collective-permute-done | bytes 172064 | tf_op jit(solution)/shard_map/ppermute | solution.py:459
  15.9 1.9 %collective-permute-start.6 = (bf16[224,384]{1,0:T(8,128)(2,1)S(1)}, bf16[224,384]{1,0:T(8,128)(2,1)S(1)}, u32[]{:S(2)}, u32[]{:S(2)}) collective-permute-start(bf16[224,384]{1,0:T(8,128)(2,1)S(1)} %get-tuple-element.42), channel_id=1, source_target_pairs={{0,20},{4,16},{8,28},{12,24},{16,4},{20,0},{24,12},{28,8},{1,21},{... | collective-permute-start | bytes 516104 | tf_op jit(solution)/shard_map/ppermute | solution.py:459
  17.7 0.0 collective-permute-done.2.rest_2_
  17.7 0.0 copy-done.3
  17.7 1.6 %collective-permute-start.7 = (bf16[4,1152]{1,0:T(4,128)(2,1)S(1)}, bf16[4,1152]{1,0:T(4,128)(2,1)S(1)}, u32[]{:S(2)}, u32[]{:S(2)}) collective-permute-start(bf16[4,1152]{1,0:T(4,128)(2,1)S(1)} %copy-done.3), channel_id=1, source_target_pairs={{1,0},{0,1},{3,2},{2,3},{6,4},{7,5},{4,6},{5,7},{11,8},{10,9},{9,1... | collective-permute-start | bytes 27656 | tf_op jit(solution)/shard_map/ppermute | solution.py:459
  19.3 0.0 copy-done.2
  19.3 1.6 %shard_map.70 = (bf16[1536,128]{1,0:T(8,128)(2,1)S(1)}, f32[2,8,3072]{2,1,0:T(8,128)S(1)}, s32[8,128]{1,0:T(8,128)S(1)}, bf16[640,1152]{1,0:T(8,128)(2,1)S(1)}) custom-call(s32[1,3072]{1,0:T(1,128)S(1)} %copy-done.2, bf16[576,1152]{1,0:T(8,128)(2,1)} %out_weight_ref.1, bf16[224,384]{1,0:T(8,128)(2,1)S(1)} %collective-permute-done.rest_0_, ...), custom_call_target="tpu_custom_call" | custom-call | flops 1073741824 | bytes 8388608 | tf_op jit(solution)/shard_map/pallas_call | solution.py:565
  21.0 0.4 collective-permute-done.7.rest_8_
  21.4 0.0 collective-permute-done.3.rest_4_
  21.4 0.0 collective-permute-done.4.rest_5_
  21.4 0.7 %collective-permute-done.5.rest_6_ = bf16[224,384]{1,0:T(8,128)(2,1)S(1)} collective-permute-done((bf16[224,384]{1,0:T(8,128)(2,1)S(1)}, bf16[224,384]{1,0:T(8,128)(2,1)S(1)}, u32[]{:S(2)}, u32[]{:S(2)}) %collective-permute-start.5) | collective-permute-done | bytes 172064 | tf_op jit(solution)/shard_map/ppermute | solution.py:459
  22.1 0.6 %collective-permute-done.6.rest_7_ = bf16[224,384]{1,0:T(8,128)(2,1)S(1)} collective-permute-done((bf16[224,384]{1,0:T(8,128)(2,1)S(1)}, bf16[224,384]{1,0:T(8,128)(2,1)S(1)}, u32[]{:S(2)}, u32[]{:S(2)}) %collective-permute-start.6) | collective-permute-done | bytes 172064 | tf_op jit(solution)/shard_map/ppermute | solution.py:459
  22.7 0.0 copy-start.1
  22.7 7.4 %shard_map.71 = (bf16[96,384]{1,0:T(8,128)(2,1)S(1)}, bf16[96,384]{1,0:T(8,128)(2,1)S(1)}, bf16[96,384]{1,0:T(8,128)(2,1)S(1)}, bf16[96,384]{1,0:T(8,128)(2,1)S(...) custom-call(s32[1,3072]{1,0:T(1,128)S(1)} %copy-done.2, ...), custom_call_target="tpu_custom_call" | custom-call | flops 905969664 | bytes 8388608 | tf_op jit(solution)/shard_map/pallas_call | solution.py:578
  30.1 2.3 %collective-permute-start.8 = (bf16[96,384]{1,0:T(8,128)(2,1)S(1)}, bf16[96,384]{1,0:T(8,128)(2,1)S(1)}, u32[]{:S(2)}, u32[]{:S(2)}) collective-permute-start(bf16[96,384]{1,0:T(8,128)(2,1)S(1)} %get-tuple-element.44), channel_id=1, source_target_pairs={{0,24},{4,28},{8,16},{12,20},{16,8},{20,12},{24,0},{28,4},{1,25},{... | collective-permute-start | bytes 221192 | tf_op jit(solution)/shard_map/ppermute | solution.py:459
  32.4 0.2 collective-permute-start.9
  32.6 1.8 %collective-permute-start.10 = (bf16[96,384]{1,0:T(8,128)(2,1)S(1)}, bf16[96,384]{1,0:T(8,128)(2,1)S(1)}, u32[]{:S(2)}, u32[]{:S(2)}) collective-permute-start(bf16[96,384]{1,0:T(8,128)(2,1)S(1)} %get-tuple-element.46), channel_id=1, source_target_pairs={{0,8},{4,12},{8,0},{12,4},{16,24},{20,28},{24,16},{28,20},{1,9},{5... | collective-permute-start | bytes 221192 | tf_op jit(solution)/shard_map/ppermute | solution.py:459
  34.4 1.2 %collective-permute-start.11 = (bf16[96,384]{1,0:T(8,128)(2,1)S(1)}, bf16[96,384]{1,0:T(8,128)(2,1)S(1)}, u32[]{:S(2)}, u32[]{:S(2)}) collective-permute-start(bf16[96,384]{1,0:T(8,128)(2,1)S(1)} %get-tuple-element.47), channel_id=1, source_target_pairs={{0,16},{4,20},{8,24},{12,28},{16,0},{20,4},{24,8},{28,12},{1,17},{... | collective-permute-start | bytes 221192 | tf_op jit(solution)/shard_map/ppermute | solution.py:459
  35.6 0.0 collective-permute-start.12
  35.6 0.0 collective-permute-done.8.rest_0_
  35.6 0.8 %collective-permute-start.13 = (bf16[96,384]{1,0:T(8,128)(2,1)S(1)}, bf16[96,384]{1,0:T(8,128)(2,1)S(1)}, u32[]{:S(2)}, u32[]{:S(2)}) collective-permute-start(bf16[96,384]{1,0:T(8,128)(2,1)S(1)} %get-tuple-element.49), channel_id=1, source_target_pairs={{0,20},{4,16},{8,28},{12,24},{16,4},{20,0},{24,12},{28,8},{1,21},{... | collective-permute-start | bytes 221192 | tf_op jit(solution)/shard_map/ppermute | solution.py:459
  36.4 1.2 %collective-permute-done.9.rest_1_ = bf16[96,384]{1,0:T(8,128)(2,1)S(1)} collective-permute-done((bf16[96,384]{1,0:T(8,128)(2,1)S(1)}, bf16[96,384]{1,0:T(8,128)(2,1)S(1)}, u32[]{:S(2)}, u32[]{:S(2)}) %collective-permute-start.9) | collective-permute-done | bytes 73760 | tf_op jit(solution)/shard_map/ppermute | solution.py:459
  37.6 0.3 collective-permute-start.14
  38.0 1.0 %collective-permute-done.10.rest_2_ = bf16[96,384]{1,0:T(8,128)(2,1)S(1)} collective-permute-done((bf16[96,384]{1,0:T(8,128)(2,1)S(1)}, bf16[96,384]{1,0:T(8,128)(2,1)S(1)}, u32[]{:S(2)}, u32[]{:S(2)}) %collective-permute-start.10) | collective-permute-done | bytes 73760 | tf_op jit(solution)/shard_map/ppermute | solution.py:459
  39.0 0.7 %collective-permute-done.11.rest_3_ = bf16[96,384]{1,0:T(8,128)(2,1)S(1)} collective-permute-done((bf16[96,384]{1,0:T(8,128)(2,1)S(1)}, bf16[96,384]{1,0:T(8,128)(2,1)S(1)}, u32[]{:S(2)}, u32[]{:S(2)}) %collective-permute-start.11) | collective-permute-done | bytes 73760 | tf_op jit(solution)/shard_map/ppermute | solution.py:459
  39.6 1.1 %collective-permute-done.12.rest_4_ = bf16[96,384]{1,0:T(8,128)(2,1)S(1)} collective-permute-done((bf16[96,384]{1,0:T(8,128)(2,1)S(1)}, bf16[96,384]{1,0:T(8,128)(2,1)S(1)}, u32[]{:S(2)}, u32[]{:S(2)}) %collective-permute-start.12) | collective-permute-done | bytes 73760 | tf_op jit(solution)/shard_map/ppermute | solution.py:459
  40.7 0.2 collective-permute-done.13.rest_5_
  40.9 0.0 collective-permute-done.14.rest_6_
  40.9 0.0 copy-done.1
  40.9 2.1 %shard_map.72 = (bf16[384,1152]{1,0:T(8,128)(2,1)}, f32[1,4]{1,0:T(1,128)}) custom-call(bf16[384,1152]{1,0:T(8,128)(2,1)S(1)} %bitcast.7, bf16[640,1152]{1,0:T(8,128)(2,1)S(1)} %get-tuple-element.35.weight_ref, bf16[4,1152]{1,0:T(4,128)(2,1)S(1)} %copy-done.3, bf16[96,384]{1,0:T(8,128)(2,1)S(1)} %collective-permute-done.8.rest_0_, ...), custom_call_target="tpu_custom_call" | custom-call | flops 509607936 | bytes 8388608 | tf_op jit(solution)/shard_map/pallas_call | solution.py:607
Async XLA Ops:
  0.6 6.8 %copy-start = (bf16[1152,1728]{0,1:T(8,128)(2,1)S(1)}, bf16[1152,1728]{0,1:T(8,128)(2,1)}, u32[]{:S(2)}) copy-start(bf16[1152,1728]{0,1:T(8,128)(2,1)} %param.7) | copy-start | bytes 11943940
  3.4 9.6 %collective-permute-start = (bf16[224,384]{1,0:T(8,128)(2,1)S(1)}, bf16[224,384]{1,0:T(8,128)(2,1)S(1)}, u32[]{:S(2)}, u32[]{:S(2)}) collective-permute-start(bf16[224,384]{1,0:T(8,128)(2,1)S(1)} %get-tuple-element.28), channel_id=1, source_target_pairs={{0,24},{4,28},{8,16},{12,20},{16,8},{20,12},{24,0},{28,4},{1,25},{... | collective-permute-start | bytes 516104 | tf_op jit(solution)/shard_map/ppermute | solution.py:459
  7.4 8.5 %collective-permute-start.1 = (bf16[224,384]{1,0:T(8,128)(2,1)S(1)}, bf16[224,384]{1,0:T(8,128)(2,1)S(1)}, u32[]{:S(2)}, u32[]{:S(2)}) collective-permute-start(bf16[224,384]{1,0:T(8,128)(2,1)S(1)} %get-tuple-element.29), channel_id=1, source_target_pairs={{0,28},{4,24},{8,20},{12,16},{16,12},{20,8},{24,4},{28,0},{1,29},{... | collective-permute-start | bytes 516104 | tf_op jit(solution)/shard_map/ppermute | solution.py:459
  7.4 10.3 %copy-start.3 = (bf16[4,1152]{1,0:T(4,128)(2,1)S(1)}, bf16[4,1152]{1,0:T(4,128)(2,1)}, u32[]{:S(2)}) copy-start(bf16[4,1152]{1,0:T(4,128)(2,1)} %text_ref.1) | copy-start | bytes 27652
  7.4 11.9 %copy-start.2 = (s32[1,3072]{1,0:T(1,128)S(1)}, s32[1,3072]{1,0:T(1,128)}, u32[]{:S(2)}) copy-start(s32[1,3072]{1,0:T(1,128)} %ids_ref.5) | copy-start | bytes 36868
  9.4 8.4 %collective-permute-start.2 = (bf16[224,384]{1,0:T(8,128)(2,1)S(1)}, bf16[224,384]{1,0:T(8,128)(2,1)S(1)}, u32[]{:S(2)}, u32[]{:S(2)}) collective-permute-start(bf16[224,384]{1,0:T(8,128)(2,1)S(1)} %get-tuple-element.32), channel_id=1, source_target_pairs={{0,4},{4,0},{8,12},{12,8},{16,20},{20,16},{24,28},{28,24},{1,5},{5... | collective-permute-start | bytes 516104 | tf_op jit(solution)/shard_map/ppermute | solution.py:459
  9.6 11.8 %collective-permute-start.3 = (bf16[224,384]{1,0:T(8,128)(2,1)S(1)}, bf16[224,384]{1,0:T(8,128)(2,1)S(1)}, u32[]{:S(2)}, u32[]{:S(2)}) collective-permute-start(bf16[224,384]{1,0:T(8,128)(2,1)S(1)} %get-tuple-element.39), channel_id=1, source_target_pairs={{0,8},{4,12},{8,0},{12,4},{16,24},{20,28},{24,16},{28,20},{1,9},{5... | collective-permute-start | bytes 516104 | tf_op jit(solution)/shard_map/ppermute | solution.py:459
  11.5 9.9 %collective-permute-start.4 = (bf16[224,384]{1,0:T(8,128)(2,1)S(1)}, bf16[224,384]{1,0:T(8,128)(2,1)S(1)}, u32[]{:S(2)}, u32[]{:S(2)}) collective-permute-start(bf16[224,384]{1,0:T(8,128)(2,1)S(1)} %get-tuple-element.40), channel_id=1, source_target_pairs={{0,16},{4,20},{8,24},{12,28},{16,0},{20,4},{24,8},{28,12},{1,17},{... | collective-permute-start | bytes 516104 | tf_op jit(solution)/shard_map/ppermute | solution.py:459
  13.0 9.1 %collective-permute-start.5 = (bf16[224,384]{1,0:T(8,128)(2,1)S(1)}, bf16[224,384]{1,0:T(8,128)(2,1)S(1)}, u32[]{:S(2)}, u32[]{:S(2)}) collective-permute-start(bf16[224,384]{1,0:T(8,128)(2,1)S(1)} %get-tuple-element.41), channel_id=1, source_target_pairs={{0,12},{4,8},{8,4},{12,0},{16,28},{20,24},{24,20},{28,16},{1,13},{... | collective-permute-start | bytes 516104 | tf_op jit(solution)/shard_map/ppermute | solution.py:459
  15.9 6.8 %collective-permute-start.6 = (bf16[224,384]{1,0:T(8,128)(2,1)S(1)}, bf16[224,384]{1,0:T(8,128)(2,1)S(1)}, u32[]{:S(2)}, u32[]{:S(2)}) collective-permute-start(bf16[224,384]{1,0:T(8,128)(2,1)S(1)} %get-tuple-element.42), channel_id=1, source_target_pairs={{0,20},{4,16},{8,28},{12,24},{16,4},{20,0},{24,12},{28,8},{1,21},{... | collective-permute-start | bytes 516104 | tf_op jit(solution)/shard_map/ppermute | solution.py:459
  17.7 3.7 %collective-permute-start.7 = (bf16[4,1152]{1,0:T(4,128)(2,1)S(1)}, bf16[4,1152]{1,0:T(4,128)(2,1)S(1)}, u32[]{:S(2)}, u32[]{:S(2)}) collective-permute-start(bf16[4,1152]{1,0:T(4,128)(2,1)S(1)} %copy-done.3), channel_id=1, source_target_pairs={{1,0},{0,1},{3,2},{2,3},{6,4},{7,5},{4,6},{5,7},{11,8},{10,9},{9,1... | collective-permute-start | bytes 27656 | tf_op jit(solution)/shard_map/ppermute | solution.py:459
  22.7 18.2 %copy-start.1 = (bf16[1,384,1152]{2,1,0:T(8,128)(2,1)S(1)}, bf16[1,384,1152]{2,1,0:T(8,128)(2,1)}, u32[]{:S(2)}) copy-start(bf16[1,384,1152]{2,1,0:T(8,128)(2,1)} %param.5) | copy-start | bytes 2654212
  30.1 5.5 %collective-permute-start.8 = (bf16[96,384]{1,0:T(8,128)(2,1)S(1)}, bf16[96,384]{1,0:T(8,128)(2,1)S(1)}, u32[]{:S(2)}, u32[]{:S(2)}) collective-permute-start(bf16[96,384]{1,0:T(8,128)(2,1)S(1)} %get-tuple-element.44), channel_id=1, source_target_pairs={{0,24},{4,28},{8,16},{12,20},{16,8},{20,12},{24,0},{28,4},{1,25},{... | collective-permute-start | bytes 221192 | tf_op jit(solution)/shard_map/ppermute | solution.py:459
  32.4 5.2 %collective-permute-start.9 = (bf16[96,384]{1,0:T(8,128)(2,1)S(1)}, bf16[96,384]{1,0:T(8,128)(2,1)S(1)}, u32[]{:S(2)}, u32[]{:S(2)}) collective-permute-start(bf16[96,384]{1,0:T(8,128)(2,1)S(1)} %get-tuple-element.45), channel_id=1, source_target_pairs={{0,28},{4,24},{8,20},{12,16},{16,12},{20,8},{24,4},{28,0},{1,29},{... | collective-permute-start | bytes 221192 | tf_op jit(solution)/shard_map/ppermute | solution.py:459
  32.6 6.3 %collective-permute-start.10 = (bf16[96,384]{1,0:T(8,128)(2,1)S(1)}, bf16[96,384]{1,0:T(8,128)(2,1)S(1)}, u32[]{:S(2)}, u32[]{:S(2)}) collective-permute-start(bf16[96,384]{1,0:T(8,128)(2,1)S(1)} %get-tuple-element.46), channel_id=1, source_target_pairs={{0,8},{4,12},{8,0},{12,4},{16,24},{20,28},{24,16},{28,20},{1,9},{5... | collective-permute-start | bytes 221192 | tf_op jit(solution)/shard_map/ppermute | solution.py:459
  34.4 5.2 %collective-permute-start.11 = (bf16[96,384]{1,0:T(8,128)(2,1)S(1)}, bf16[96,384]{1,0:T(8,128)(2,1)S(1)}, u32[]{:S(2)}, u32[]{:S(2)}) collective-permute-start(bf16[96,384]{1,0:T(8,128)(2,1)S(1)} %get-tuple-element.47), channel_id=1, source_target_pairs={{0,16},{4,20},{8,24},{12,28},{16,0},{20,4},{24,8},{28,12},{1,17},{... | collective-permute-start | bytes 221192 | tf_op jit(solution)/shard_map/ppermute | solution.py:459
  35.6 5.1 %collective-permute-start.12 = (bf16[96,384]{1,0:T(8,128)(2,1)S(1)}, bf16[96,384]{1,0:T(8,128)(2,1)S(1)}, u32[]{:S(2)}, u32[]{:S(2)}) collective-permute-start(bf16[96,384]{1,0:T(8,128)(2,1)S(1)} %get-tuple-element.48), channel_id=1, source_target_pairs={{0,12},{4,8},{8,4},{12,0},{16,28},{20,24},{24,20},{28,16},{1,13},{... | collective-permute-start | bytes 221192 | tf_op jit(solution)/shard_map/ppermute | solution.py:459
  35.6 5.3 %collective-permute-start.13 = (bf16[96,384]{1,0:T(8,128)(2,1)S(1)}, bf16[96,384]{1,0:T(8,128)(2,1)S(1)}, u32[]{:S(2)}, u32[]{:S(2)}) collective-permute-start(bf16[96,384]{1,0:T(8,128)(2,1)S(1)} %get-tuple-element.49), channel_id=1, source_target_pairs={{0,20},{4,16},{8,28},{12,24},{16,4},{20,0},{24,12},{28,8},{1,21},{... | collective-permute-start | bytes 221192 | tf_op jit(solution)/shard_map/ppermute | solution.py:459
  37.6 3.2 %collective-permute-start.14 = (bf16[96,384]{1,0:T(8,128)(2,1)S(1)}, bf16[96,384]{1,0:T(8,128)(2,1)S(1)}, u32[]{:S(2)}, u32[]{:S(2)}) collective-permute-start(bf16[96,384]{1,0:T(8,128)(2,1)S(1)} %get-tuple-element.50), channel_id=1, source_target_pairs={{0,4},{4,0},{8,12},{12,8},{16,20},{20,16},{24,28},{28,24},{1,5},{5... | collective-permute-start | bytes 221192 | tf_op jit(solution)/shard_map/ppermute | solution.py:459

commit v28 on v23

--- a/solution.py
+++ b/solution.py
@@ -41,6 +41,12 @@
 def image_rows(ids, images):
     row = lax.broadcasted_iota(jnp.int32, (SPARE, ids.shape[1]), 0)
     return (lax.rem(row, images) == ids).astype(jnp.float32).astype(jnp.bfloat16)
+
+
+def turned_product(weight, normed):
+    return lax.dot_general(
+        weight, normed, (((1,), (1,)), ((), ())), preferred_element_type=jnp.float32
+    )
 
 
 def head_blocks(query, key, value, sums, pair):
@@ -96,11 +102,11 @@
     center = values - jnp.mean(values, axis=1, keepdims=True)
     spread = jnp.mean(center * center, axis=1, keepdims=True)
     normed = (center * lax.rsqrt(spread + 1e-06)).astype(jnp.bfloat16)
-    normed_ref[...] = normed.T
+    normed_ref[...] = normed
     for fetch in fetches:
         fetch.wait()
     parts = [
-        jnp.dot(weight[at], normed_ref[...], preferred_element_type=jnp.float32) for at in range(3)
+        turned_product(weight[at], normed_ref[...]) for at in range(3)
     ]
     store_by_core(core, head_blocks(*parts, sums_ref if piggy else None, pair), same_ref, cross_ref)
 
@@ -115,7 +121,7 @@
         for at in range(3):
             here = pl.ds(pl.multiple_of(at * width + pair * wide, 16), wide)
             parts.append(
-                jnp.dot(weight_ref[here, :], normed_ref[...], preferred_element_type=jnp.float32)
+                turned_product(weight_ref[here, :], normed_ref[...])
             )
         blocks = head_blocks(*parts, sums_ref if piggy else None, pair)
         store_by_core(core, blocks, *out_refs[2 * step : 2 * step + 2])
@@ -210,17 +216,19 @@
         score(state + 2, scores_a, tops_a)
         weigh(state + 1, scores_b, tops_b)
 
-    def four_pairs(step, _):
-        two_pairs(4 * step)
-        two_pairs(4 * step + 2)
+    def six_pairs(step, _):
+        for place in range(0, 6, 2):
+            two_pairs(6 * step + place)
         return 0
 
+    def left_over(step, _):
+        two_pairs(6 * whole + 2 * step)
+        return 0
+
     score(0, scores_a, tops_a)
-    lax.fori_loop(0, pairs >> 2, four_pairs, 0)
-
-    @pl.when(jnp.bitwise_and(pairs, 2) == 2)
-    def _():
-        two_pairs(jnp.bitwise_and(pairs, -4))
+    whole = lax.div(pairs, 6)
+    lax.fori_loop(0, whole, six_pairs, 0)
+    lax.fori_loop(0, (pairs - 6 * whole) >> 1, left_over, 0)
 
     @pl.when(jnp.bitwise_and(pairs, 1) == 1)
     def _():
@@ -514,7 +522,7 @@
     turned_weight = qkv_weight.T
     normed, sums, *sent = call(
         functools.partial(far_kernel, images, piggy),
-        (shape((depth, count), bf16), shape((SPARE, depth), f32), block, block),
+        (shape((count, depth), bf16), shape((SPARE, depth), f32), block, block),
         [
             pltpu.VMEM((1, count), jnp.int32),
             pltpu.VMEM((count, depth), bf16),

time: 41.8 us -> 42.1 us (level)
  Pallas kernels: 14.6 us -> 15.4 us
  waiting for transfers between devices: 8.76 us -> 8.26 us
    pallas_call x1, Pallas kernels: 1.95 us -> 2.5 us  [local(): call(functools.partial(near_kernel, piggy), (block,) * 6, [], in_vmem(3),...]
    ppermute x15, waiting for transfers between devices: 8.76 us -> 8.26 us  [moved(): return lax.ppermute(value, axis, pairs)]
  transfers between devices with their start and end apart: 15 -> 15, of which waited for: 9 -> 9; matrix products, arithmetic and copies ran while one was open for 0% -> 0% of each run, Pallas kernels for 9% -> 10%
where the time goes in v28:
time: 42.1 us; the launch traced here: 42 us
  starting transfers between devices  17.6 us (42%)
  Pallas kernels  15.4 us (37%)
  waiting for transfers between devices  8.26 us (20%)
  between operations  0.69 us (2%)
    ppermute x15, starting transfers between devices, moved(): return lax.ppermute(value, axis, pairs)  17.6 us
    ppermute x15, waiting for transfers between devices, moved(): return lax.ppermute(value, axis, pairs)  8.26 us
    pallas_call x1, Pallas kernels, local(): call(functools.partial(attend_kernel, images, piggy, halo), (shape((padde...  6.3 us
    pallas_call x1, Pallas kernels, local(): call(functools.partial(far_kernel, images, piggy), (shape((count, depth),...  2.82 us
    pallas_call x1, Pallas kernels, local(): call(functools.partial(near_kernel, piggy), (block,) * 6, [], in_vmem(3),...  2.5 us
    pallas_call x1, Pallas kernels, local(): call(functools.partial(finish_kernel, images), (shape((count, depth), bf1...  2.13 us
    pallas_call x1, Pallas kernels, local(): call(functools.partial(prepare_kernel, images, halo), (shape((len(EARLY)...  1.64 us
  transfers between devices with their start and end apart: 15, of which 9 were waited for; matrix products, arithmetic and copies ran while one was open for 0% of the time, Pallas kernels for 10%

profile of v28, /device:TPU:0, one launch (start us, length us, event | category | flops | bytes accessed | tf_op | source)
XLA Modules:
  0.0 42.0 jit_solution(7548075097608941871)
XLA Ops:
  0.6 0.0 copy-start
  0.6 2.8 %shard_map.68 = (bf16[384,1152]{1,0:T(8,128)(2,1)S(1)}, f32[8,1152]{1,0:T(8,128)S(1)}, bf16[224,384]{1,0:T(8,128)(2,1)S(1)}, bf16[224,384]{1,0:T(8,128)(2,1)S(1)}) custom-call(s32[1,3072]{1,0:T(1,128)} %ids_ref.5, bf16[384,1152]{1,0:T(8,128)(2,1)} %bitcast.6, bf16[1728,1152]{1,0:T(8,128)(2,1)} %bitcast.4), custom_call_target="tpu_custom_call" | custom-call | flops 382205952 | bytes 8388608 | tf_op jit(solution)/shard_map/pallas_call | solution.py:523
  3.5 4.0 %collective-permute-start = (bf16[224,384]{1,0:T(8,128)(2,1)S(1)}, bf16[224,384]{1,0:T(8,128)(2,1)S(1)}, u32[]{:S(2)}, u32[]{:S(2)}) collective-permute-start(bf16[224,384]{1,0:T(8,128)(2,1)S(1)} %get-tuple-element.28), channel_id=1, source_target_pairs={{0,24},{4,28},{8,16},{12,20},{16,8},{20,12},{24,0},{28,4},{1,25},{... | collective-permute-start | bytes 516104 | tf_op jit(solution)/shard_map/ppermute | solution.py:472
  7.4 0.0 collective-permute-start.1
  7.4 0.0 copy-done
  7.4 0.0 copy-start.3
  7.4 0.0 copy-start.2
  7.4 2.5 %shard_map.69 = (bf16[224,384]{1,0:T(8,128)(2,1)S(1)}, bf16[224,384]{1,0:T(8,128)(2,1)S(1)}, bf16[224,384]{1,0:T(8,128)(2,1)S(1)}, bf16[224,384]{1,0:T(8,128)(2,...) custom-call(bf16[384,1152]{1,0:T(8,128)(2,1)S(1)} %get-tuple-element.30.normed_ref, ...), custom_call_target="tpu_custom_call" | custom-call | flops 1146617856 | bytes 8388608 | tf_op jit(solution)/shard_map/pallas_call | solution.py:537
  10.0 0.2 collective-permute-start.2
  10.2 1.9 %collective-permute-start.3 = (bf16[224,384]{1,0:T(8,128)(2,1)S(1)}, bf16[224,384]{1,0:T(8,128)(2,1)S(1)}, u32[]{:S(2)}, u32[]{:S(2)}) collective-permute-start(bf16[224,384]{1,0:T(8,128)(2,1)S(1)} %get-tuple-element.39), channel_id=1, source_target_pairs={{0,8},{4,12},{8,0},{12,4},{16,24},{20,28},{24,16},{28,20},{1,9},{5... | collective-permute-start | bytes 516104 | tf_op jit(solution)/shard_map/ppermute | solution.py:472
  12.1 1.5 %collective-permute-start.4 = (bf16[224,384]{1,0:T(8,128)(2,1)S(1)}, bf16[224,384]{1,0:T(8,128)(2,1)S(1)}, u32[]{:S(2)}, u32[]{:S(2)}) collective-permute-start(bf16[224,384]{1,0:T(8,128)(2,1)S(1)} %get-tuple-element.40), channel_id=1, source_target_pairs={{0,16},{4,20},{8,24},{12,28},{16,0},{20,4},{24,8},{28,12},{1,17},{... | collective-permute-start | bytes 516104 | tf_op jit(solution)/shard_map/ppermute | solution.py:472
  13.6 0.0 collective-permute-done.rest_0_
  13.6 0.0 collective-permute-start.5
  13.6 2.3 %collective-permute-done.1.rest_1_ = bf16[224,384]{1,0:T(8,128)(2,1)S(1)} collective-permute-done((bf16[224,384]{1,0:T(8,128)(2,1)S(1)}, bf16[224,384]{1,0:T(8,128)(2,1)S(1)}, u32[]{:S(2)}, u32[]{:S(2)}) %collective-permute-start.1) | collective-permute-done | bytes 172064 | tf_op jit(solution)/shard_map/ppermute | solution.py:472
  15.9 1.9 %collective-permute-start.6 = (bf16[224,384]{1,0:T(8,128)(2,1)S(1)}, bf16[224,384]{1,0:T(8,128)(2,1)S(1)}, u32[]{:S(2)}, u32[]{:S(2)}) collective-permute-start(bf16[224,384]{1,0:T(8,128)(2,1)S(1)} %get-tuple-element.42), channel_id=1, source_target_pairs={{0,20},{4,16},{8,28},{12,24},{16,4},{20,0},{24,12},{28,8},{1,21},{... | collective-permute-start | bytes 516104 | tf_op jit(solution)/shard_map/ppermute | solution.py:472
  17.8 0.0 collective-permute-done.2.rest_2_
  17.8 0.0 copy-done.3
  17.8 1.6 %collective-permute-start.7 = (bf16[4,1152]{1,0:T(4,128)(2,1)S(1)}, bf16[4,1152]{1,0:T(4,128)(2,1)S(1)}, u32[]{:S(2)}, u32[]{:S(2)}) collective-permute-start(bf16[4,1152]{1,0:T(4,128)(2,1)S(1)} %copy-done.3), channel_id=1, source_target_pairs={{1,0},{0,1},{3,2},{2,3},{6,4},{7,5},{4,6},{5,7},{11,8},{10,9},{9,1... | collective-permute-start | bytes 27656 | tf_op jit(solution)/shard_map/ppermute | solution.py:472
  19.4 0.0 copy-done.2
  19.4 1.6 %shard_map.70 = (bf16[1536,128]{1,0:T(8,128)(2,1)S(1)}, f32[2,8,3072]{2,1,0:T(8,128)S(1)}, s32[8,128]{1,0:T(8,128)S(1)}, bf16[640,1152]{1,0:T(8,128)(2,1)S(1)}) custom-call(s32[1,3072]{1,0:T(1,128)S(1)} %copy-done.2, bf16[576,1152]{1,0:T(8,128)(2,1)} %out_weight_ref.1, bf16[224,384]{1,0:T(8,128)(2,1)S(1)} %collective-permute-done.rest_0_, ...), custom_call_target="tpu_custom_call" | custom-call | flops 1073741824 | bytes 8388608 | tf_op jit(solution)/shard_map/pallas_call | solution.py:578
  21.0 0.4 %collective-permute-done.7.rest_8_ = bf16[4,1152]{1,0:T(4,128)(2,1)S(1)} collective-permute-done((bf16[4,1152]{1,0:T(4,128)(2,1)S(1)}, bf16[4,1152]{1,0:T(4,128)(2,1)S(1)}, u32[]{:S(2)}, u32[]{:S(2)}) %collective-permute-start.7) | collective-permute-done | bytes 9248 | tf_op jit(solution)/shard_map/ppermute | solution.py:472
  21.4 0.0 collective-permute-done.3.rest_4_
  21.4 0.0 collective-permute-done.4.rest_5_
  21.4 0.7 %collective-permute-done.5.rest_6_ = bf16[224,384]{1,0:T(8,128)(2,1)S(1)} collective-permute-done((bf16[224,384]{1,0:T(8,128)(2,1)S(1)}, bf16[224,384]{1,0:T(8,128)(2,1)S(1)}, u32[]{:S(2)}, u32[]{:S(2)}) %collective-permute-start.5) | collective-permute-done | bytes 172064 | tf_op jit(solution)/shard_map/ppermute | solution.py:472
  22.1 0.6 %collective-permute-done.6.rest_7_ = bf16[224,384]{1,0:T(8,128)(2,1)S(1)} collective-permute-done((bf16[224,384]{1,0:T(8,128)(2,1)S(1)}, bf16[224,384]{1,0:T(8,128)(2,1)S(1)}, u32[]{:S(2)}, u32[]{:S(2)}) %collective-permute-start.6) | collective-permute-done | bytes 172064 | tf_op jit(solution)/shard_map/ppermute | solution.py:472
  22.8 0.0 copy-start.1
  22.8 6.3 %shard_map.71 = (bf16[96,384]{1,0:T(8,128)(2,1)S(1)}, bf16[96,384]{1,0:T(8,128)(2,1)S(1)}, bf16[96,384]{1,0:T(8,128)(2,1)S(1)}, bf16[96,384]{1,0:T(8,128)(2,1)S(...) custom-call(s32[1,3072]{1,0:T(1,128)S(1)} %copy-done.2, ...), custom_call_target="tpu_custom_call" | custom-call | flops 905969664 | bytes 8388608 | tf_op jit(solution)/shard_map/pallas_call | solution.py:591
  29.1 2.3 %collective-permute-start.8 = (bf16[96,384]{1,0:T(8,128)(2,1)S(1)}, bf16[96,384]{1,0:T(8,128)(2,1)S(1)}, u32[]{:S(2)}, u32[]{:S(2)}) collective-permute-start(bf16[96,384]{1,0:T(8,128)(2,1)S(1)} %get-tuple-element.44), channel_id=1, source_target_pairs={{0,24},{4,28},{8,16},{12,20},{16,8},{20,12},{24,0},{28,4},{1,25},{... | collective-permute-start | bytes 221192 | tf_op jit(solution)/shard_map/ppermute | solution.py:472
  31.4 0.2 collective-permute-start.9
  31.6 1.8 %collective-permute-start.10 = (bf16[96,384]{1,0:T(8,128)(2,1)S(1)}, bf16[96,384]{1,0:T(8,128)(2,1)S(1)}, u32[]{:S(2)}, u32[]{:S(2)}) collective-permute-start(bf16[96,384]{1,0:T(8,128)(2,1)S(1)} %get-tuple-element.46), channel_id=1, source_target_pairs={{0,8},{4,12},{8,0},{12,4},{16,24},{20,28},{24,16},{28,20},{1,9},{5... | collective-permute-start | bytes 221192 | tf_op jit(solution)/shard_map/ppermute | solution.py:472
  33.3 1.2 %collective-permute-start.11 = (bf16[96,384]{1,0:T(8,128)(2,1)S(1)}, bf16[96,384]{1,0:T(8,128)(2,1)S(1)}, u32[]{:S(2)}, u32[]{:S(2)}) collective-permute-start(bf16[96,384]{1,0:T(8,128)(2,1)S(1)} %get-tuple-element.47), channel_id=1, source_target_pairs={{0,16},{4,20},{8,24},{12,28},{16,0},{20,4},{24,8},{28,12},{1,17},{... | collective-permute-start | bytes 221192 | tf_op jit(solution)/shard_map/ppermute | solution.py:472
  34.5 0.0 collective-permute-start.12
  34.5 0.0 collective-permute-done.8.rest_0_
  34.5 0.8 %collective-permute-start.13 = (bf16[96,384]{1,0:T(8,128)(2,1)S(1)}, bf16[96,384]{1,0:T(8,128)(2,1)S(1)}, u32[]{:S(2)}, u32[]{:S(2)}) collective-permute-start(bf16[96,384]{1,0:T(8,128)(2,1)S(1)} %get-tuple-element.49), channel_id=1, source_target_pairs={{0,20},{4,16},{8,28},{12,24},{16,4},{20,0},{24,12},{28,8},{1,21},{... | collective-permute-start | bytes 221192 | tf_op jit(solution)/shard_map/ppermute | solution.py:472
  35.3 1.3 %collective-permute-done.9.rest_1_ = bf16[96,384]{1,0:T(8,128)(2,1)S(1)} collective-permute-done((bf16[96,384]{1,0:T(8,128)(2,1)S(1)}, bf16[96,384]{1,0:T(8,128)(2,1)S(1)}, u32[]{:S(2)}, u32[]{:S(2)}) %collective-permute-start.9) | collective-permute-done | bytes 73760 | tf_op jit(solution)/shard_map/ppermute | solution.py:472
  36.6 0.3 collective-permute-start.14
  36.9 1.0 %collective-permute-done.10.rest_2_ = bf16[96,384]{1,0:T(8,128)(2,1)S(1)} collective-permute-done((bf16[96,384]{1,0:T(8,128)(2,1)S(1)}, bf16[96,384]{1,0:T(8,128)(2,1)S(1)}, u32[]{:S(2)}, u32[]{:S(2)}) %collective-permute-start.10) | collective-permute-done | bytes 73760 | tf_op jit(solution)/shard_map/ppermute | solution.py:472
  37.9 0.7 %collective-permute-done.11.rest_3_ = bf16[96,384]{1,0:T(8,128)(2,1)S(1)} collective-permute-done((bf16[96,384]{1,0:T(8,128)(2,1)S(1)}, bf16[96,384]{1,0:T(8,128)(2,1)S(1)}, u32[]{:S(2)}, u32[]{:S(2)}) %collective-permute-start.11) | collective-permute-done | bytes 73760 | tf_op jit(solution)/shard_map/ppermute | solution.py:472
  38.6 1.1 %collective-permute-done.12.rest_4_ = bf16[96,384]{1,0:T(8,128)(2,1)S(1)} collective-permute-done((bf16[96,384]{1,0:T(8,128)(2,1)S(1)}, bf16[96,384]{1,0:T(8,128)(2,1)S(1)}, u32[]{:S(2)}, u32[]{:S(2)}) %collective-permute-start.12) | collective-permute-done | bytes 73760 | tf_op jit(solution)/shard_map/ppermute | solution.py:472
  39.6 0.2 collective-permute-done.13.rest_5_
  39.8 0.0 collective-permute-done.14.rest_6_
  39.8 0.0 copy-done.1
  39.8 2.1 %shard_map.72 = (bf16[384,1152]{1,0:T(8,128)(2,1)}, f32[1,4]{1,0:T(1,128)}) custom-call(bf16[384,1152]{1,0:T(8,128)(2,1)S(1)} %bitcast.7, bf16[640,1152]{1,0:T(8,128)(2,1)S(1)} %get-tuple-element.35.weight_ref, bf16[4,1152]{1,0:T(4,128)(2,1)S(1)} %copy-done.3, bf16[96,384]{1,0:T(8,128)(2,1)S(1)} %collective-permute-done.8.rest_0_, ...), custom_call_target="tpu_custom_call" | custom-call | flops 509607936 | bytes 8388608 | tf_op jit(solution)/shard_map/pallas_call | solution.py:620
Async XLA Ops:
  0.6 6.8 %copy-start = (bf16[1152,1728]{0,1:T(8,128)(2,1)S(1)}, bf16[1152,1728]{0,1:T(8,128)(2,1)}, u32[]{:S(2)}) copy-start(bf16[1152,1728]{0,1:T(8,128)(2,1)} %param.7) | copy-start | bytes 11943940
  3.5 10.1 %collective-permute-start = (bf16[224,384]{1,0:T(8,128)(2,1)S(1)}, bf16[224,384]{1,0:T(8,128)(2,1)S(1)}, u32[]{:S(2)}, u32[]{:S(2)}) collective-permute-start(bf16[224,384]{1,0:T(8,128)(2,1)S(1)} %get-tuple-element.28), channel_id=1, source_target_pairs={{0,24},{4,28},{8,16},{12,20},{16,8},{20,12},{24,0},{28,4},{1,25},{... | collective-permute-start | bytes 516104 | tf_op jit(solution)/shard_map/ppermute | solution.py:472
  7.4 8.5 %collective-permute-start.1 = (bf16[224,384]{1,0:T(8,128)(2,1)S(1)}, bf16[224,384]{1,0:T(8,128)(2,1)S(1)}, u32[]{:S(2)}, u32[]{:S(2)}) collective-permute-start(bf16[224,384]{1,0:T(8,128)(2,1)S(1)} %get-tuple-element.29), channel_id=1, source_target_pairs={{0,28},{4,24},{8,20},{12,16},{16,12},{20,8},{24,4},{28,0},{1,29},{... | collective-permute-start | bytes 516104 | tf_op jit(solution)/shard_map/ppermute | solution.py:472
  7.4 10.3 %copy-start.3 = (bf16[4,1152]{1,0:T(4,128)(2,1)S(1)}, bf16[4,1152]{1,0:T(4,128)(2,1)}, u32[]{:S(2)}) copy-start(bf16[4,1152]{1,0:T(4,128)(2,1)} %text_ref.1) | copy-start | bytes 27652
  7.4 11.9 %copy-start.2 = (s32[1,3072]{1,0:T(1,128)S(1)}, s32[1,3072]{1,0:T(1,128)}, u32[]{:S(2)}) copy-start(s32[1,3072]{1,0:T(1,128)} %ids_ref.5) | copy-start | bytes 36868
  10.0 7.8 %collective-permute-start.2 = (bf16[224,384]{1,0:T(8,128)(2,1)S(1)}, bf16[224,384]{1,0:T(8,128)(2,1)S(1)}, u32[]{:S(2)}, u32[]{:S(2)}) collective-permute-start(bf16[224,384]{1,0:T(8,128)(2,1)S(1)} %get-tuple-element.32), channel_id=1, source_target_pairs={{0,4},{4,0},{8,12},{12,8},{16,20},{20,16},{24,28},{28,24},{1,5},{5... | collective-permute-start | bytes 516104 | tf_op jit(solution)/shard_map/ppermute | solution.py:472
  10.2 11.2 %collective-permute-start.3 = (bf16[224,384]{1,0:T(8,128)(2,1)S(1)}, bf16[224,384]{1,0:T(8,128)(2,1)S(1)}, u32[]{:S(2)}, u32[]{:S(2)}) collective-permute-start(bf16[224,384]{1,0:T(8,128)(2,1)S(1)} %get-tuple-element.39), channel_id=1, source_target_pairs={{0,8},{4,12},{8,0},{12,4},{16,24},{20,28},{24,16},{28,20},{1,9},{5... | collective-permute-start | bytes 516104 | tf_op jit(solution)/shard_map/ppermute | solution.py:472
  12.1 9.4 %collective-permute-start.4 = (bf16[224,384]{1,0:T(8,128)(2,1)S(1)}, bf16[224,384]{1,0:T(8,128)(2,1)S(1)}, u32[]{:S(2)}, u32[]{:S(2)}) collective-permute-start(bf16[224,384]{1,0:T(8,128)(2,1)S(1)} %get-tuple-element.40), channel_id=1, source_target_pairs={{0,16},{4,20},{8,24},{12,28},{16,0},{20,4},{24,8},{28,12},{1,17},{... | collective-permute-start | bytes 516104 | tf_op jit(solution)/shard_map/ppermute | solution.py:472
  13.6 8.5 %collective-permute-start.5 = (bf16[224,384]{1,0:T(8,128)(2,1)S(1)}, bf16[224,384]{1,0:T(8,128)(2,1)S(1)}, u32[]{:S(2)}, u32[]{:S(2)}) collective-permute-start(bf16[224,384]{1,0:T(8,128)(2,1)S(1)} %get-tuple-element.41), channel_id=1, source_target_pairs={{0,12},{4,8},{8,4},{12,0},{16,28},{20,24},{24,20},{28,16},{1,13},{... | collective-permute-start | bytes 516104 | tf_op jit(solution)/shard_map/ppermute | solution.py:472
  15.9 6.9 %collective-permute-start.6 = (bf16[224,384]{1,0:T(8,128)(2,1)S(1)}, bf16[224,384]{1,0:T(8,128)(2,1)S(1)}, u32[]{:S(2)}, u32[]{:S(2)}) collective-permute-start(bf16[224,384]{1,0:T(8,128)(2,1)S(1)} %get-tuple-element.42), channel_id=1, source_target_pairs={{0,20},{4,16},{8,28},{12,24},{16,4},{20,0},{24,12},{28,8},{1,21},{... | collective-permute-start | bytes 516104 | tf_op jit(solution)/shard_map/ppermute | solution.py:472
  17.8 3.7 %collective-permute-start.7 = (bf16[4,1152]{1,0:T(4,128)(2,1)S(1)}, bf16[4,1152]{1,0:T(4,128)(2,1)S(1)}, u32[]{:S(2)}, u32[]{:S(2)}) collective-permute-start(bf16[4,1152]{1,0:T(4,128)(2,1)S(1)} %copy-done.3), channel_id=1, source_target_pairs={{1,0},{0,1},{3,2},{2,3},{6,4},{7,5},{4,6},{5,7},{11,8},{10,9},{9,1... | collective-permute-start | bytes 27656 | tf_op jit(solution)/shard_map/ppermute | solution.py:472
  22.8 17.1 %copy-start.1 = (bf16[1,384,1152]{2,1,0:T(8,128)(2,1)S(1)}, bf16[1,384,1152]{2,1,0:T(8,128)(2,1)}, u32[]{:S(2)}) copy-start(bf16[1,384,1152]{2,1,0:T(8,128)(2,1)} %param.5) | copy-start | bytes 2654212
  29.1 5.4 %collective-permute-start.8 = (bf16[96,384]{1,0:T(8,128)(2,1)S(1)}, bf16[96,384]{1,0:T(8,128)(2,1)S(1)}, u32[]{:S(2)}, u32[]{:S(2)}) collective-permute-start(bf16[96,384]{1,0:T(8,128)(2,1)S(1)} %get-tuple-element.44), channel_id=1, source_target_pairs={{0,24},{4,28},{8,16},{12,20},{16,8},{20,12},{24,0},{28,4},{1,25},{... | collective-permute-start | bytes 221192 | tf_op jit(solution)/shard_map/ppermute | solution.py:472
  31.4 5.2 %collective-permute-start.9 = (bf16[96,384]{1,0:T(8,128)(2,1)S(1)}, bf16[96,384]{1,0:T(8,128)(2,1)S(1)}, u32[]{:S(2)}, u32[]{:S(2)}) collective-permute-start(bf16[96,384]{1,0:T(8,128)(2,1)S(1)} %get-tuple-element.45), channel_id=1, source_target_pairs={{0,28},{4,24},{8,20},{12,16},{16,12},{20,8},{24,4},{28,0},{1,29},{... | collective-permute-start | bytes 221192 | tf_op jit(solution)/shard_map/ppermute | solution.py:472
  31.6 6.3 %collective-permute-start.10 = (bf16[96,384]{1,0:T(8,128)(2,1)S(1)}, bf16[96,384]{1,0:T(8,128)(2,1)S(1)}, u32[]{:S(2)}, u32[]{:S(2)}) collective-permute-start(bf16[96,384]{1,0:T(8,128)(2,1)S(1)} %get-tuple-element.46), channel_id=1, source_target_pairs={{0,8},{4,12},{8,0},{12,4},{16,24},{20,28},{24,16},{28,20},{1,9},{5... | collective-permute-start | bytes 221192 | tf_op jit(solution)/shard_map/ppermute | solution.py:472
  33.3 5.2 %collective-permute-start.11 = (bf16[96,384]{1,0:T(8,128)(2,1)S(1)}, bf16[96,384]{1,0:T(8,128)(2,1)S(1)}, u32[]{:S(2)}, u32[]{:S(2)}) collective-permute-start(bf16[96,384]{1,0:T(8,128)(2,1)S(1)} %get-tuple-element.47), channel_id=1, source_target_pairs={{0,16},{4,20},{8,24},{12,28},{16,0},{20,4},{24,8},{28,12},{1,17},{... | collective-permute-start | bytes 221192 | tf_op jit(solution)/shard_map/ppermute | solution.py:472
  34.5 5.1 %collective-permute-start.12 = (bf16[96,384]{1,0:T(8,128)(2,1)S(1)}, bf16[96,384]{1,0:T(8,128)(2,1)S(1)}, u32[]{:S(2)}, u32[]{:S(2)}) collective-permute-start(bf16[96,384]{1,0:T(8,128)(2,1)S(1)} %get-tuple-element.48), channel_id=1, source_target_pairs={{0,12},{4,8},{8,4},{12,0},{16,28},{20,24},{24,20},{28,16},{1,13},{... | collective-permute-start | bytes 221192 | tf_op jit(solution)/shard_map/ppermute | solution.py:472
  34.5 5.3 %collective-permute-start.13 = (bf16[96,384]{1,0:T(8,128)(2,1)S(1)}, bf16[96,384]{1,0:T(8,128)(2,1)S(1)}, u32[]{:S(2)}, u32[]{:S(2)}) collective-permute-start(bf16[96,384]{1,0:T(8,128)(2,1)S(1)} %get-tuple-element.49), channel_id=1, source_target_pairs={{0,20},{4,16},{8,28},{12,24},{16,4},{20,0},{24,12},{28,8},{1,21},{... | collective-permute-start | bytes 221192 | tf_op jit(solution)/shard_map/ppermute | solution.py:472
  36.6 3.2 %collective-permute-start.14 = (bf16[96,384]{1,0:T(8,128)(2,1)S(1)}, bf16[96,384]{1,0:T(8,128)(2,1)S(1)}, u32[]{:S(2)}, u32[]{:S(2)}) collective-permute-start(bf16[96,384]{1,0:T(8,128)(2,1)S(1)} %get-tuple-element.50), channel_id=1, source_target_pairs={{0,4},{4,0},{8,12},{12,8},{16,20},{20,16},{24,28},{28,24},{1,5},{5... | collective-permute-start | bytes 221192 | tf_op jit(solution)/shard_map/ppermute | solution.py:472

commit v29 on v28

--- a/solution.py
+++ b/solution.py
@@ -18,7 +18,7 @@
 QUERY_AT = 2 * SIZE
 TEXT_ROWS = 16
 HIDDEN = -1e30
-ORDER = (6, 7, 2, 4, 3, 5, 1, 0)
+ORDER = (6, 7, 1, 2, 4, 3, 5, 0)
 EARLY = (6, 7, 1, 0)
 LATE = (2, 4, 3, 5)
 
@@ -41,12 +41,6 @@
 def image_rows(ids, images):
     row = lax.broadcasted_iota(jnp.int32, (SPARE, ids.shape[1]), 0)
     return (lax.rem(row, images) == ids).astype(jnp.float32).astype(jnp.bfloat16)
-
-
-def turned_product(weight, normed):
-    return lax.dot_general(
-        weight, normed, (((1,), (1,)), ((), ())), preferred_element_type=jnp.float32
-    )
 
 
 def head_blocks(query, key, value, sums, pair):
@@ -102,11 +96,11 @@
     center = values - jnp.mean(values, axis=1, keepdims=True)
     spread = jnp.mean(center * center, axis=1, keepdims=True)
     normed = (center * lax.rsqrt(spread + 1e-06)).astype(jnp.bfloat16)
-    normed_ref[...] = normed
+    normed_ref[...] = normed.T
     for fetch in fetches:
         fetch.wait()
     parts = [
-        turned_product(weight[at], normed_ref[...]) for at in range(3)
+        jnp.dot(weight[at], normed_ref[...], preferred_element_type=jnp.float32) for at in range(3)
     ]
     store_by_core(core, head_blocks(*parts, sums_ref if piggy else None, pair), same_ref, cross_ref)
 
@@ -121,7 +115,7 @@
         for at in range(3):
             here = pl.ds(pl.multiple_of(at * width + pair * wide, 16), wide)
             parts.append(
-                turned_product(weight_ref[here, :], normed_ref[...])
+                jnp.dot(weight_ref[here, :], normed_ref[...], preferred_element_type=jnp.float32)
             )
         blocks = head_blocks(*parts, sums_ref if piggy else None, pair)
         store_by_core(core, blocks, *out_refs[2 * step : 2 * step + 2])
@@ -522,7 +516,7 @@
     turned_weight = qkv_weight.T
     normed, sums, *sent = call(
         functools.partial(far_kernel, images, piggy),
-        (shape((count, depth), bf16), shape((SPARE, depth), f32), block, block),
+        (shape((depth, count), bf16), shape((SPARE, depth), f32), block, block),
         [
             pltpu.VMEM((1, count), jnp.int32),
             pltpu.VMEM((count, depth), bf16),

time: 42.1 us -> 42.6 us (1.012)
  Pallas kernels: 15.4 us -> 14.5 us
  waiting for transfers between devices: 8.26 us -> 8.95 us
    ppermute x15, waiting for transfers between devices: 8.26 us -> 8.95 us  [moved(): return lax.ppermute(value, axis, pairs)]
    pallas_call x1, Pallas kernels: 2.5 us -> 1.95 us  [local(): call(functools.partial(near_kernel, piggy), (block,) * 6, [], in_vmem(3),...]
  transfers between devices with their start and end apart: 15 -> 15, of which waited for: 9 -> 9; matrix products, arithmetic and copies ran while one was open for 0% -> 0% of each run, Pallas kernels for 10% -> 9%
where the time goes in v29:
time: 42.6 us; the launch traced here: 42.1 us
  starting transfers between devices  18 us (42%)
  Pallas kernels  14.5 us (34%)
  waiting for transfers between devices  8.95 us (21%)
  between operations  0.69 us (2%)
    ppermute x15, starting transfers between devices, moved(): return lax.ppermute(value, axis, pairs)  18 us
    ppermute x15, waiting for transfers between devices, moved(): return lax.ppermute(value, axis, pairs)  8.95 us
    pallas_call x1, Pallas kernels, local(): call(functools.partial(attend_kernel, images, piggy, halo), (shape((padde...  5.95 us
    pallas_call x1, Pallas kernels, local(): call(functools.partial(far_kernel, images, piggy), (shape((depth, count),...  2.8 us
    pallas_call x1, Pallas kernels, local(): call(functools.partial(finish_kernel, images), (shape((count, depth), bf1...  2.13 us
    pallas_call x1, Pallas kernels, local(): call(functools.partial(near_kernel, piggy), (block,) * 6, [], in_vmem(3),...  1.95 us
    pallas_call x1, Pallas kernels, local(): call(functools.partial(prepare_kernel, images, halo), (shape((len(EARLY)...  1.64 us
  transfers between devices with their start and end apart: 15, of which 9 were waited for; matrix products, arithmetic and copies ran while one was open for 0% of the time, Pallas kernels for 9%

profile of v29, /device:TPU:0, one launch (start us, length us, event | category | flops | bytes accessed | tf_op | source)
XLA Modules:
  0.0 42.1 jit_solution(1407766363397944604)
XLA Ops:
  0.6 0.0 copy-start
  0.6 2.8 %shard_map.68 = (bf16[1152,384]{1,0:T(8,128)(2,1)S(1)}, f32[8,1152]{1,0:T(8,128)S(1)}, bf16[224,384]{1,0:T(8,128)(2,1)S(1)}, bf16[224,384]{1,0:T(8,128)(2,1)S(1)}) custom-call(s32[1,3072]{1,0:T(1,128)} %ids_ref.5, bf16[384,1152]{1,0:T(8,128)(2,1)} %bitcast.6, bf16[1728,1152]{1,0:T(8,128)(2,1)} %bitcast.4), custom_call_target="tpu_custom_call" | custom-call | flops 382205952 | bytes 8388608 | tf_op jit(solution)/shard_map/pallas_call | solution.py:517
  3.4 4.0 %collective-permute-start = (bf16[224,384]{1,0:T(8,128)(2,1)S(1)}, bf16[224,384]{1,0:T(8,128)(2,1)S(1)}, u32[]{:S(2)}, u32[]{:S(2)}) collective-permute-start(bf16[224,384]{1,0:T(8,128)(2,1)S(1)} %get-tuple-element.28), channel_id=1, source_target_pairs={{0,24},{4,28},{8,16},{12,20},{16,8},{20,12},{24,0},{28,4},{1,25},{... | collective-permute-start | bytes 516104 | tf_op jit(solution)/shard_map/ppermute | solution.py:466
  7.4 0.0 collective-permute-start.1
  7.4 0.0 copy-done
  7.4 0.0 copy-start.3
  7.4 0.0 copy-start.2
  7.4 1.9 %shard_map.69 = (bf16[224,384]{1,0:T(8,128)(2,1)S(1)}, bf16[224,384]{1,0:T(8,128)(2,1)S(1)}, bf16[224,384]{1,0:T(8,128)(2,1)S(1)}, bf16[224,384]{1,0:T(8,128)(2,...) custom-call(bf16[1152,384]{1,0:T(8,128)(2,1)S(1)} %get-tuple-element.30.normed_ref, ...), custom_call_target="tpu_custom_call" | custom-call | flops 1146617856 | bytes 8388608 | tf_op jit(solution)/shard_map/pallas_call | solution.py:531
  9.4 0.2 collective-permute-start.2
  9.6 1.9 %collective-permute-start.3 = (bf16[224,384]{1,0:T(8,128)(2,1)S(1)}, bf16[224,384]{1,0:T(8,128)(2,1)S(1)}, u32[]{:S(2)}, u32[]{:S(2)}) collective-permute-start(bf16[224,384]{1,0:T(8,128)(2,1)S(1)} %get-tuple-element.39), channel_id=1, source_target_pairs={{0,8},{4,12},{8,0},{12,4},{16,24},{20,28},{24,16},{28,20},{1,9},{5... | collective-permute-start | bytes 516104 | tf_op jit(solution)/shard_map/ppermute | solution.py:466
  11.5 1.5 %collective-permute-start.4 = (bf16[224,384]{1,0:T(8,128)(2,1)S(1)}, bf16[224,384]{1,0:T(8,128)(2,1)S(1)}, u32[]{:S(2)}, u32[]{:S(2)}) collective-permute-start(bf16[224,384]{1,0:T(8,128)(2,1)S(1)} %get-tuple-element.40), channel_id=1, source_target_pairs={{0,16},{4,20},{8,24},{12,28},{16,0},{20,4},{24,8},{28,12},{1,17},{... | collective-permute-start | bytes 516104 | tf_op jit(solution)/shard_map/ppermute | solution.py:466
  13.0 0.0 collective-permute-done.rest_0_
  13.0 0.0 collective-permute-start.5
  13.0 2.9 %collective-permute-done.1.rest_1_ = bf16[224,384]{1,0:T(8,128)(2,1)S(1)} collective-permute-done((bf16[224,384]{1,0:T(8,128)(2,1)S(1)}, bf16[224,384]{1,0:T(8,128)(2,1)S(1)}, u32[]{:S(2)}, u32[]{:S(2)}) %collective-permute-start.1) | collective-permute-done | bytes 172064 | tf_op jit(solution)/shard_map/ppermute | solution.py:466
  15.9 1.9 %collective-permute-start.6 = (bf16[224,384]{1,0:T(8,128)(2,1)S(1)}, bf16[224,384]{1,0:T(8,128)(2,1)S(1)}, u32[]{:S(2)}, u32[]{:S(2)}) collective-permute-start(bf16[224,384]{1,0:T(8,128)(2,1)S(1)} %get-tuple-element.42), channel_id=1, source_target_pairs={{0,20},{4,16},{8,28},{12,24},{16,4},{20,0},{24,12},{28,8},{1,21},{... | collective-permute-start | bytes 516104 | tf_op jit(solution)/shard_map/ppermute | solution.py:466
  17.8 0.0 collective-permute-done.2.rest_2_
  17.8 0.0 copy-done.3
  17.8 1.6 %collective-permute-start.7 = (bf16[4,1152]{1,0:T(4,128)(2,1)S(1)}, bf16[4,1152]{1,0:T(4,128)(2,1)S(1)}, u32[]{:S(2)}, u32[]{:S(2)}) collective-permute-start(bf16[4,1152]{1,0:T(4,128)(2,1)S(1)} %copy-done.3), channel_id=1, source_target_pairs={{1,0},{0,1},{3,2},{2,3},{6,4},{7,5},{4,6},{5,7},{11,8},{10,9},{9,1... | collective-permute-start | bytes 27656 | tf_op jit(solution)/shard_map/ppermute | solution.py:466
  19.3 0.0 copy-done.2
  19.3 1.6 %shard_map.70 = (bf16[1536,128]{1,0:T(8,128)(2,1)S(1)}, f32[2,8,3072]{2,1,0:T(8,128)S(1)}, s32[8,128]{1,0:T(8,128)S(1)}, bf16[640,1152]{1,0:T(8,128)(2,1)S(1)}) custom-call(s32[1,3072]{1,0:T(1,128)S(1)} %copy-done.2, bf16[576,1152]{1,0:T(8,128)(2,1)} %out_weight_ref.1, bf16[224,384]{1,0:T(8,128)(2,1)S(1)} %collective-permute-done.rest_0_, ...), custom_call_target="tpu_custom_call" | custom-call | flops 1073741824 | bytes 8388608 | tf_op jit(solution)/shard_map/pallas_call | solution.py:572
  21.0 0.4 %collective-permute-done.7.rest_8_ = bf16[4,1152]{1,0:T(4,128)(2,1)S(1)} collective-permute-done((bf16[4,1152]{1,0:T(4,128)(2,1)S(1)}, bf16[4,1152]{1,0:T(4,128)(2,1)S(1)}, u32[]{:S(2)}, u32[]{:S(2)}) %collective-permute-start.7) | collective-permute-done | bytes 9248 | tf_op jit(solution)/shard_map/ppermute | solution.py:466
  21.4 0.0 collective-permute-done.3.rest_4_
  21.4 0.0 collective-permute-done.4.rest_5_
  21.4 0.7 %collective-permute-done.5.rest_6_ = bf16[224,384]{1,0:T(8,128)(2,1)S(1)} collective-permute-done((bf16[224,384]{1,0:T(8,128)(2,1)S(1)}, bf16[224,384]{1,0:T(8,128)(2,1)S(1)}, u32[]{:S(2)}, u32[]{:S(2)}) %collective-permute-start.5) | collective-permute-done | bytes 172064 | tf_op jit(solution)/shard_map/ppermute | solution.py:466
  22.1 0.6 %collective-permute-done.6.rest_7_ = bf16[224,384]{1,0:T(8,128)(2,1)S(1)} collective-permute-done((bf16[224,384]{1,0:T(8,128)(2,1)S(1)}, bf16[224,384]{1,0:T(8,128)(2,1)S(1)}, u32[]{:S(2)}, u32[]{:S(2)}) %collective-permute-start.6) | collective-permute-done | bytes 172064 | tf_op jit(solution)/shard_map/ppermute | solution.py:466
  22.7 0.0 copy-start.1
  22.7 6.0 %shard_map.71 = (bf16[96,384]{1,0:T(8,128)(2,1)S(1)}, bf16[96,384]{1,0:T(8,128)(2,1)S(1)}, bf16[96,384]{1,0:T(8,128)(2,1)S(1)}, bf16[96,384]{1,0:T(8,128)(2,1)S(...) custom-call(s32[1,3072]{1,0:T(1,128)S(1)} %copy-done.2, ...), custom_call_target="tpu_custom_call" | custom-call | flops 905969664 | bytes 8388608 | tf_op jit(solution)/shard_map/pallas_call | solution.py:585
  28.7 2.3 %collective-permute-start.8 = (bf16[96,384]{1,0:T(8,128)(2,1)S(1)}, bf16[96,384]{1,0:T(8,128)(2,1)S(1)}, u32[]{:S(2)}, u32[]{:S(2)}) collective-permute-start(bf16[96,384]{1,0:T(8,128)(2,1)S(1)} %get-tuple-element.44), channel_id=1, source_target_pairs={{0,24},{4,28},{8,16},{12,20},{16,8},{20,12},{24,0},{28,4},{1,25},{... | collective-permute-start | bytes 221192 | tf_op jit(solution)/shard_map/ppermute | solution.py:466
  31.0 0.2 collective-permute-start.9
  31.2 0.6 %collective-permute-start.10 = (bf16[96,384]{1,0:T(8,128)(2,1)S(1)}, bf16[96,384]{1,0:T(8,128)(2,1)S(1)}, u32[]{:S(2)}, u32[]{:S(2)}) collective-permute-start(bf16[96,384]{1,0:T(8,128)(2,1)S(1)} %get-tuple-element.46), channel_id=1, source_target_pairs={{0,4},{4,0},{8,12},{12,8},{16,20},{20,16},{24,28},{28,24},{1,5},{5... | collective-permute-start | bytes 221192 | tf_op jit(solution)/shard_map/ppermute | solution.py:466
  31.8 2.0 %collective-permute-start.11 = (bf16[96,384]{1,0:T(8,128)(2,1)S(1)}, bf16[96,384]{1,0:T(8,128)(2,1)S(1)}, u32[]{:S(2)}, u32[]{:S(2)}) collective-permute-start(bf16[96,384]{1,0:T(8,128)(2,1)S(1)} %get-tuple-element.47), channel_id=1, source_target_pairs={{0,8},{4,12},{8,0},{12,4},{16,24},{20,28},{24,16},{28,20},{1,9},{5... | collective-permute-start | bytes 221192 | tf_op jit(solution)/shard_map/ppermute | solution.py:466
  33.8 0.7 %collective-permute-start.12 = (bf16[96,384]{1,0:T(8,128)(2,1)S(1)}, bf16[96,384]{1,0:T(8,128)(2,1)S(1)}, u32[]{:S(2)}, u32[]{:S(2)}) collective-permute-start(bf16[96,384]{1,0:T(8,128)(2,1)S(1)} %get-tuple-element.48), channel_id=1, source_target_pairs={{0,16},{4,20},{8,24},{12,28},{16,0},{20,4},{24,8},{28,12},{1,17},{... | collective-permute-start | bytes 221192 | tf_op jit(solution)/shard_map/ppermute | solution.py:466
  34.6 0.0 collective-permute-done.8.rest_0_
  34.6 0.0 collective-permute-start.13
  34.6 1.6 %collective-permute-done.9.rest_1_ = bf16[96,384]{1,0:T(8,128)(2,1)S(1)} collective-permute-done((bf16[96,384]{1,0:T(8,128)(2,1)S(1)}, bf16[96,384]{1,0:T(8,128)(2,1)S(1)}, u32[]{:S(2)}, u32[]{:S(2)}) %collective-permute-start.9) | collective-permute-done | bytes 73760 | tf_op jit(solution)/shard_map/ppermute | solution.py:466
  36.2 1.1 %collective-permute-start.14 = (bf16[96,384]{1,0:T(8,128)(2,1)S(1)}, bf16[96,384]{1,0:T(8,128)(2,1)S(1)}, u32[]{:S(2)}, u32[]{:S(2)}) collective-permute-start(bf16[96,384]{1,0:T(8,128)(2,1)S(1)} %get-tuple-element.50), channel_id=1, source_target_pairs={{0,20},{4,16},{8,28},{12,24},{16,4},{20,0},{24,12},{28,8},{1,21},{... | collective-permute-start | bytes 221192 | tf_op jit(solution)/shard_map/ppermute | solution.py:466
  37.2 0.0 collective-permute-done.10.rest_2_
  37.2 0.3 collective-permute-done.11.rest_3_
  37.5 0.7 %collective-permute-done.12.rest_4_ = bf16[96,384]{1,0:T(8,128)(2,1)S(1)} collective-permute-done((bf16[96,384]{1,0:T(8,128)(2,1)S(1)}, bf16[96,384]{1,0:T(8,128)(2,1)S(1)}, u32[]{:S(2)}, u32[]{:S(2)}) %collective-permute-start.12) | collective-permute-done | bytes 73760 | tf_op jit(solution)/shard_map/ppermute | solution.py:466
  38.2 0.5 %collective-permute-done.13.rest_5_ = bf16[96,384]{1,0:T(8,128)(2,1)S(1)} collective-permute-done((bf16[96,384]{1,0:T(8,128)(2,1)S(1)}, bf16[96,384]{1,0:T(8,128)(2,1)S(1)}, u32[]{:S(2)}, u32[]{:S(2)}) %collective-permute-start.13) | collective-permute-done | bytes 73760 | tf_op jit(solution)/shard_map/ppermute | solution.py:466
  38.6 1.3 %collective-permute-done.14.rest_6_ = bf16[96,384]{1,0:T(8,128)(2,1)S(1)} collective-permute-done((bf16[96,384]{1,0:T(8,128)(2,1)S(1)}, bf16[96,384]{1,0:T(8,128)(2,1)S(1)}, u32[]{:S(2)}, u32[]{:S(2)}) %collective-permute-start.14) | collective-permute-done | bytes 73760 | tf_op jit(solution)/shard_map/ppermute | solution.py:466
  40.0 0.0 copy-done.1
  40.0 2.1 %shard_map.72 = (bf16[384,1152]{1,0:T(8,128)(2,1)}, f32[1,4]{1,0:T(1,128)}) custom-call(bf16[384,1152]{1,0:T(8,128)(2,1)S(1)} %bitcast.7, bf16[640,1152]{1,0:T(8,128)(2,1)S(1)} %get-tuple-element.35.weight_ref, bf16[4,1152]{1,0:T(4,128)(2,1)S(1)} %copy-done.3, bf16[96,384]{1,0:T(8,128)(2,1)S(1)} %collective-permute-done.8.rest_0_, ...), custom_call_target="tpu_custom_call" | custom-call | flops 509607936 | bytes 8388608 | tf_op jit(solution)/shard_map/pallas_call | solution.py:614
Async XLA Ops:
  0.6 6.8 %copy-start = (bf16[1152,1728]{0,1:T(8,128)(2,1)S(1)}, bf16[1152,1728]{0,1:T(8,128)(2,1)}, u32[]{:S(2)}) copy-start(bf16[1152,1728]{0,1:T(8,128)(2,1)} %param.7) | copy-start | bytes 11943940
  3.4 9.6 %collective-permute-start = (bf16[224,384]{1,0:T(8,128)(2,1)S(1)}, bf16[224,384]{1,0:T(8,128)(2,1)S(1)}, u32[]{:S(2)}, u32[]{:S(2)}) collective-permute-start(bf16[224,384]{1,0:T(8,128)(2,1)S(1)} %get-tuple-element.28), channel_id=1, source_target_pairs={{0,24},{4,28},{8,16},{12,20},{16,8},{20,12},{24,0},{28,4},{1,25},{... | collective-permute-start | bytes 516104 | tf_op jit(solution)/shard_map/ppermute | solution.py:466
  7.4 8.5 %collective-permute-start.1 = (bf16[224,384]{1,0:T(8,128)(2,1)S(1)}, bf16[224,384]{1,0:T(8,128)(2,1)S(1)}, u32[]{:S(2)}, u32[]{:S(2)}) collective-permute-start(bf16[224,384]{1,0:T(8,128)(2,1)S(1)} %get-tuple-element.29), channel_id=1, source_target_pairs={{0,28},{4,24},{8,20},{12,16},{16,12},{20,8},{24,4},{28,0},{1,29},{... | collective-permute-start | bytes 516104 | tf_op jit(solution)/shard_map/ppermute | solution.py:466
  7.4 10.4 %copy-start.3 = (bf16[4,1152]{1,0:T(4,128)(2,1)S(1)}, bf16[4,1152]{1,0:T(4,128)(2,1)}, u32[]{:S(2)}) copy-start(bf16[4,1152]{1,0:T(4,128)(2,1)} %text_ref.1) | copy-start | bytes 27652
  7.4 11.9 %copy-start.2 = (s32[1,3072]{1,0:T(1,128)S(1)}, s32[1,3072]{1,0:T(1,128)}, u32[]{:S(2)}) copy-start(s32[1,3072]{1,0:T(1,128)} %ids_ref.5) | copy-start | bytes 36868
  9.4 8.4 %collective-permute-start.2 = (bf16[224,384]{1,0:T(8,128)(2,1)S(1)}, bf16[224,384]{1,0:T(8,128)(2,1)S(1)}, u32[]{:S(2)}, u32[]{:S(2)}) collective-permute-start(bf16[224,384]{1,0:T(8,128)(2,1)S(1)} %get-tuple-element.32), channel_id=1, source_target_pairs={{0,4},{4,0},{8,12},{12,8},{16,20},{20,16},{24,28},{28,24},{1,5},{5... | collective-permute-start | bytes 516104 | tf_op jit(solution)/shard_map/ppermute | solution.py:466
  9.6 11.8 %collective-permute-start.3 = (bf16[224,384]{1,0:T(8,128)(2,1)S(1)}, bf16[224,384]{1,0:T(8,128)(2,1)S(1)}, u32[]{:S(2)}, u32[]{:S(2)}) collective-permute-start(bf16[224,384]{1,0:T(8,128)(2,1)S(1)} %get-tuple-element.39), channel_id=1, source_target_pairs={{0,8},{4,12},{8,0},{12,4},{16,24},{20,28},{24,16},{28,20},{1,9},{5... | collective-permute-start | bytes 516104 | tf_op jit(solution)/shard_map/ppermute | solution.py:466
  11.5 9.9 %collective-permute-start.4 = (bf16[224,384]{1,0:T(8,128)(2,1)S(1)}, bf16[224,384]{1,0:T(8,128)(2,1)S(1)}, u32[]{:S(2)}, u32[]{:S(2)}) collective-permute-start(bf16[224,384]{1,0:T(8,128)(2,1)S(1)} %get-tuple-element.40), channel_id=1, source_target_pairs={{0,16},{4,20},{8,24},{12,28},{16,0},{20,4},{24,8},{28,12},{1,17},{... | collective-permute-start | bytes 516104 | tf_op jit(solution)/shard_map/ppermute | solution.py:466
  13.0 9.1 %collective-permute-start.5 = (bf16[224,384]{1,0:T(8,128)(2,1)S(1)}, bf16[224,384]{1,0:T(8,128)(2,1)S(1)}, u32[]{:S(2)}, u32[]{:S(2)}) collective-permute-start(bf16[224,384]{1,0:T(8,128)(2,1)S(1)} %get-tuple-element.41), channel_id=1, source_target_pairs={{0,12},{4,8},{8,4},{12,0},{16,28},{20,24},{24,20},{28,16},{1,13},{... | collective-permute-start | bytes 516104 | tf_op jit(solution)/shard_map/ppermute | solution.py:466
  15.9 6.9 %collective-permute-start.6 = (bf16[224,384]{1,0:T(8,128)(2,1)S(1)}, bf16[224,384]{1,0:T(8,128)(2,1)S(1)}, u32[]{:S(2)}, u32[]{:S(2)}) collective-permute-start(bf16[224,384]{1,0:T(8,128)(2,1)S(1)} %get-tuple-element.42), channel_id=1, source_target_pairs={{0,20},{4,16},{8,28},{12,24},{16,4},{20,0},{24,12},{28,8},{1,21},{... | collective-permute-start | bytes 516104 | tf_op jit(solution)/shard_map/ppermute | solution.py:466
  17.8 3.7 %collective-permute-start.7 = (bf16[4,1152]{1,0:T(4,128)(2,1)S(1)}, bf16[4,1152]{1,0:T(4,128)(2,1)S(1)}, u32[]{:S(2)}, u32[]{:S(2)}) collective-permute-start(bf16[4,1152]{1,0:T(4,128)(2,1)S(1)} %copy-done.3), channel_id=1, source_target_pairs={{1,0},{0,1},{3,2},{2,3},{6,4},{7,5},{4,6},{5,7},{11,8},{10,9},{9,1... | collective-permute-start | bytes 27656 | tf_op jit(solution)/shard_map/ppermute | solution.py:466
  22.7 17.2 %copy-start.1 = (bf16[1,384,1152]{2,1,0:T(8,128)(2,1)S(1)}, bf16[1,384,1152]{2,1,0:T(8,128)(2,1)}, u32[]{:S(2)}) copy-start(bf16[1,384,1152]{2,1,0:T(8,128)(2,1)} %param.5) | copy-start | bytes 2654212
  28.7 5.9 %collective-permute-start.8 = (bf16[96,384]{1,0:T(8,128)(2,1)S(1)}, bf16[96,384]{1,0:T(8,128)(2,1)S(1)}, u32[]{:S(2)}, u32[]{:S(2)}) collective-permute-start(bf16[96,384]{1,0:T(8,128)(2,1)S(1)} %get-tuple-element.44), channel_id=1, source_target_pairs={{0,24},{4,28},{8,16},{12,20},{16,8},{20,12},{24,0},{28,4},{1,25},{... | collective-permute-start | bytes 221192 | tf_op jit(solution)/shard_map/ppermute | solution.py:466
  31.0 5.2 %collective-permute-start.9 = (bf16[96,384]{1,0:T(8,128)(2,1)S(1)}, bf16[96,384]{1,0:T(8,128)(2,1)S(1)}, u32[]{:S(2)}, u32[]{:S(2)}) collective-permute-start(bf16[96,384]{1,0:T(8,128)(2,1)S(1)} %get-tuple-element.45), channel_id=1, source_target_pairs={{0,28},{4,24},{8,20},{12,16},{16,12},{20,8},{24,4},{28,0},{1,29},{... | collective-permute-start | bytes 221192 | tf_op jit(solution)/shard_map/ppermute | solution.py:466
  31.2 6.0 %collective-permute-start.10 = (bf16[96,384]{1,0:T(8,128)(2,1)S(1)}, bf16[96,384]{1,0:T(8,128)(2,1)S(1)}, u32[]{:S(2)}, u32[]{:S(2)}) collective-permute-start(bf16[96,384]{1,0:T(8,128)(2,1)S(1)} %get-tuple-element.46), channel_id=1, source_target_pairs={{0,4},{4,0},{8,12},{12,8},{16,20},{20,16},{24,28},{28,24},{1,5},{5... | collective-permute-start | bytes 221192 | tf_op jit(solution)/shard_map/ppermute | solution.py:466
  31.8 5.7 %collective-permute-start.11 = (bf16[96,384]{1,0:T(8,128)(2,1)S(1)}, bf16[96,384]{1,0:T(8,128)(2,1)S(1)}, u32[]{:S(2)}, u32[]{:S(2)}) collective-permute-start(bf16[96,384]{1,0:T(8,128)(2,1)S(1)} %get-tuple-element.47), channel_id=1, source_target_pairs={{0,8},{4,12},{8,0},{12,4},{16,24},{20,28},{24,16},{28,20},{1,9},{5... | collective-permute-start | bytes 221192 | tf_op jit(solution)/shard_map/ppermute | solution.py:466
  33.8 4.4 %collective-permute-start.12 = (bf16[96,384]{1,0:T(8,128)(2,1)S(1)}, bf16[96,384]{1,0:T(8,128)(2,1)S(1)}, u32[]{:S(2)}, u32[]{:S(2)}) collective-permute-start(bf16[96,384]{1,0:T(8,128)(2,1)S(1)} %get-tuple-element.48), channel_id=1, source_target_pairs={{0,16},{4,20},{8,24},{12,28},{16,0},{20,4},{24,8},{28,12},{1,17},{... | collective-permute-start | bytes 221192 | tf_op jit(solution)/shard_map/ppermute | solution.py:466
  34.6 4.1 %collective-permute-start.13 = (bf16[96,384]{1,0:T(8,128)(2,1)S(1)}, bf16[96,384]{1,0:T(8,128)(2,1)S(1)}, u32[]{:S(2)}, u32[]{:S(2)}) collective-permute-start(bf16[96,384]{1,0:T(8,128)(2,1)S(1)} %get-tuple-element.49), channel_id=1, source_target_pairs={{0,12},{4,8},{8,4},{12,0},{16,28},{20,24},{24,20},{28,16},{1,13},{... | collective-permute-start | bytes 221192 | tf_op jit(solution)/shard_map/ppermute | solution.py:466
  36.2 3.8 %collective-permute-start.14 = (bf16[96,384]{1,0:T(8,128)(2,1)S(1)}, bf16[96,384]{1,0:T(8,128)(2,1)S(1)}, u32[]{:S(2)}, u32[]{:S(2)}) collective-permute-start(bf16[96,384]{1,0:T(8,128)(2,1)S(1)} %get-tuple-element.50), channel_id=1, source_target_pairs={{0,20},{4,16},{8,28},{12,24},{16,4},{20,0},{24,12},{28,8},{1,21},{... | collective-permute-start | bytes 221192 | tf_op jit(solution)/shard_map/ppermute | solution.py:466

commit v30 on v29

--- a/solution.py
+++ b/solution.py
@@ -18,7 +18,7 @@
 QUERY_AT = 2 * SIZE
 TEXT_ROWS = 16
 HIDDEN = -1e30
-ORDER = (6, 7, 1, 2, 4, 3, 5, 0)
+ORDER = (6, 7, 2, 4, 3, 5, 1, 0)
 EARLY = (6, 7, 1, 0)
 LATE = (2, 4, 3, 5)
 

time: 42.6 us -> 41.9 us (0.984)
  no operation moved by 1% of the time
where the time goes in v30:
time: 41.9 us; the launch traced here: 41.5 us
  starting transfers between devices  17.6 us (42%)
  Pallas kernels  14.5 us (35%)
  waiting for transfers between devices  8.75 us (21%)
  between operations  0.69 us (2%)
    ppermute x15, starting transfers between devices, moved(): return lax.ppermute(value, axis, pairs)  17.6 us
    ppermute x15, waiting for transfers between devices, moved(): return lax.ppermute(value, axis, pairs)  8.75 us
    pallas_call x1, Pallas kernels, local(): call(functools.partial(attend_kernel, images, piggy, halo), (shape((padde...  5.94 us
    pallas_call x1, Pallas kernels, local(): call(functools.partial(far_kernel, images, piggy), (shape((depth, count),...  2.8 us
    pallas_call x1, Pallas kernels, local(): call(functools.partial(finish_kernel, images), (shape((count, depth), bf1...  2.13 us
    pallas_call x1, Pallas kernels, local(): call(functools.partial(near_kernel, piggy), (block,) * 6, [], in_vmem(3),...  1.95 us
    pallas_call x1, Pallas kernels, local(): call(functools.partial(prepare_kernel, images, halo), (shape((len(EARLY)...  1.64 us
  transfers between devices with their start and end apart: 15, of which 9 were waited for; matrix products, arithmetic and copies ran while one was open for 0% of the time, Pallas kernels for 9%

profile of v30, /device:TPU:0, one launch (start us, length us, event | category | flops | bytes accessed | tf_op | source)
XLA Modules:
  0.0 41.5 jit_solution(8585440961463877493)
XLA Ops:
  0.6 0.0 copy-start
  0.6 2.8 %shard_map.68 = (bf16[1152,384]{1,0:T(8,128)(2,1)S(1)}, f32[8,1152]{1,0:T(8,128)S(1)}, bf16[224,384]{1,0:T(8,128)(2,1)S(1)}, bf16[224,384]{1,0:T(8,128)(2,1)S(1)}) custom-call(s32[1,3072]{1,0:T(1,128)} %ids_ref.5, bf16[384,1152]{1,0:T(8,128)(2,1)} %bitcast.6, bf16[1728,1152]{1,0:T(8,128)(2,1)} %bitcast.4), custom_call_target="tpu_custom_call" | custom-call | flops 382205952 | bytes 8388608 | tf_op jit(solution)/shard_map/pallas_call | solution.py:517
  3.4 4.0 %collective-permute-start = (bf16[224,384]{1,0:T(8,128)(2,1)S(1)}, bf16[224,384]{1,0:T(8,128)(2,1)S(1)}, u32[]{:S(2)}, u32[]{:S(2)}) collective-permute-start(bf16[224,384]{1,0:T(8,128)(2,1)S(1)} %get-tuple-element.28), channel_id=1, source_target_pairs={{0,24},{4,28},{8,16},{12,20},{16,8},{20,12},{24,0},{28,4},{1,25},{... | collective-permute-start | bytes 516104 | tf_op jit(solution)/shard_map/ppermute | solution.py:466
  7.4 0.0 collective-permute-start.1
  7.4 0.0 copy-done
  7.4 0.0 copy-start.3
  7.4 0.0 copy-start.2
  7.4 1.9 %shard_map.69 = (bf16[224,384]{1,0:T(8,128)(2,1)S(1)}, bf16[224,384]{1,0:T(8,128)(2,1)S(1)}, bf16[224,384]{1,0:T(8,128)(2,1)S(1)}, bf16[224,384]{1,0:T(8,128)(2,...) custom-call(bf16[1152,384]{1,0:T(8,128)(2,1)S(1)} %get-tuple-element.30.normed_ref, ...), custom_call_target="tpu_custom_call" | custom-call | flops 1146617856 | bytes 8388608 | tf_op jit(solution)/shard_map/pallas_call | solution.py:531
  9.4 0.2 collective-permute-start.2
  9.6 1.9 %collective-permute-start.3 = (bf16[224,384]{1,0:T(8,128)(2,1)S(1)}, bf16[224,384]{1,0:T(8,128)(2,1)S(1)}, u32[]{:S(2)}, u32[]{:S(2)}) collective-permute-start(bf16[224,384]{1,0:T(8,128)(2,1)S(1)} %get-tuple-element.39), channel_id=1, source_target_pairs={{0,8},{4,12},{8,0},{12,4},{16,24},{20,28},{24,16},{28,20},{1,9},{5... | collective-permute-start | bytes 516104 | tf_op jit(solution)/shard_map/ppermute | solution.py:466
  11.5 1.5 %collective-permute-start.4 = (bf16[224,384]{1,0:T(8,128)(2,1)S(1)}, bf16[224,384]{1,0:T(8,128)(2,1)S(1)}, u32[]{:S(2)}, u32[]{:S(2)}) collective-permute-start(bf16[224,384]{1,0:T(8,128)(2,1)S(1)} %get-tuple-element.40), channel_id=1, source_target_pairs={{0,16},{4,20},{8,24},{12,28},{16,0},{20,4},{24,8},{28,12},{1,17},{... | collective-permute-start | bytes 516104 | tf_op jit(solution)/shard_map/ppermute | solution.py:466
  13.0 0.0 collective-permute-done.rest_0_
  13.0 0.0 collective-permute-start.5
  13.0 2.9 %collective-permute-done.1.rest_1_ = bf16[224,384]{1,0:T(8,128)(2,1)S(1)} collective-permute-done((bf16[224,384]{1,0:T(8,128)(2,1)S(1)}, bf16[224,384]{1,0:T(8,128)(2,1)S(1)}, u32[]{:S(2)}, u32[]{:S(2)}) %collective-permute-start.1) | collective-permute-done | bytes 172064 | tf_op jit(solution)/shard_map/ppermute | solution.py:466
  15.9 1.9 %collective-permute-start.6 = (bf16[224,384]{1,0:T(8,128)(2,1)S(1)}, bf16[224,384]{1,0:T(8,128)(2,1)S(1)}, u32[]{:S(2)}, u32[]{:S(2)}) collective-permute-start(bf16[224,384]{1,0:T(8,128)(2,1)S(1)} %get-tuple-element.42), channel_id=1, source_target_pairs={{0,20},{4,16},{8,28},{12,24},{16,4},{20,0},{24,12},{28,8},{1,21},{... | collective-permute-start | bytes 516104 | tf_op jit(solution)/shard_map/ppermute | solution.py:466
  17.8 0.0 collective-permute-done.2.rest_2_
  17.8 0.0 copy-done.3
  17.8 1.6 %collective-permute-start.7 = (bf16[4,1152]{1,0:T(4,128)(2,1)S(1)}, bf16[4,1152]{1,0:T(4,128)(2,1)S(1)}, u32[]{:S(2)}, u32[]{:S(2)}) collective-permute-start(bf16[4,1152]{1,0:T(4,128)(2,1)S(1)} %copy-done.3), channel_id=1, source_target_pairs={{1,0},{0,1},{3,2},{2,3},{6,4},{7,5},{4,6},{5,7},{11,8},{10,9},{9,1... | collective-permute-start | bytes 27656 | tf_op jit(solution)/shard_map/ppermute | solution.py:466
  19.3 0.0 copy-done.2
  19.3 1.6 %shard_map.70 = (bf16[1536,128]{1,0:T(8,128)(2,1)S(1)}, f32[2,8,3072]{2,1,0:T(8,128)S(1)}, s32[8,128]{1,0:T(8,128)S(1)}, bf16[640,1152]{1,0:T(8,128)(2,1)S(1)}) custom-call(s32[1,3072]{1,0:T(1,128)S(1)} %copy-done.2, bf16[576,1152]{1,0:T(8,128)(2,1)} %out_weight_ref.1, bf16[224,384]{1,0:T(8,128)(2,1)S(1)} %collective-permute-done.rest_0_, ...), custom_call_target="tpu_custom_call" | custom-call | flops 1073741824 | bytes 8388608 | tf_op jit(solution)/shard_map/pallas_call | solution.py:572
  21.0 0.4 %collective-permute-done.7.rest_8_ = bf16[4,1152]{1,0:T(4,128)(2,1)S(1)} collective-permute-done((bf16[4,1152]{1,0:T(4,128)(2,1)S(1)}, bf16[4,1152]{1,0:T(4,128)(2,1)S(1)}, u32[]{:S(2)}, u32[]{:S(2)}) %collective-permute-start.7) | collective-permute-done | bytes 9248 | tf_op jit(solution)/shard_map/ppermute | solution.py:466
  21.4 0.0 collective-permute-done.3.rest_4_
  21.4 0.0 collective-permute-done.4.rest_5_
  21.4 0.7 %collective-permute-done.5.rest_6_ = bf16[224,384]{1,0:T(8,128)(2,1)S(1)} collective-permute-done((bf16[224,384]{1,0:T(8,128)(2,1)S(1)}, bf16[224,384]{1,0:T(8,128)(2,1)S(1)}, u32[]{:S(2)}, u32[]{:S(2)}) %collective-permute-start.5) | collective-permute-done | bytes 172064 | tf_op jit(solution)/shard_map/ppermute | solution.py:466
  22.1 0.6 %collective-permute-done.6.rest_7_ = bf16[224,384]{1,0:T(8,128)(2,1)S(1)} collective-permute-done((bf16[224,384]{1,0:T(8,128)(2,1)S(1)}, bf16[224,384]{1,0:T(8,128)(2,1)S(1)}, u32[]{:S(2)}, u32[]{:S(2)}) %collective-permute-start.6) | collective-permute-done | bytes 172064 | tf_op jit(solution)/shard_map/ppermute | solution.py:466
  22.7 0.0 copy-start.1
  22.7 5.9 %shard_map.71 = (bf16[96,384]{1,0:T(8,128)(2,1)S(1)}, bf16[96,384]{1,0:T(8,128)(2,1)S(1)}, bf16[96,384]{1,0:T(8,128)(2,1)S(1)}, bf16[96,384]{1,0:T(8,128)(2,1)S(...) custom-call(s32[1,3072]{1,0:T(1,128)S(1)} %copy-done.2, ...), custom_call_target="tpu_custom_call" | custom-call | flops 905969664 | bytes 8388608 | tf_op jit(solution)/shard_map/pallas_call | solution.py:585
  28.7 2.3 %collective-permute-start.8 = (bf16[96,384]{1,0:T(8,128)(2,1)S(1)}, bf16[96,384]{1,0:T(8,128)(2,1)S(1)}, u32[]{:S(2)}, u32[]{:S(2)}) collective-permute-start(bf16[96,384]{1,0:T(8,128)(2,1)S(1)} %get-tuple-element.44), channel_id=1, source_target_pairs={{0,24},{4,28},{8,16},{12,20},{16,8},{20,12},{24,0},{28,4},{1,25},{... | collective-permute-start | bytes 221192 | tf_op jit(solution)/shard_map/ppermute | solution.py:466
  31.0 0.2 collective-permute-start.9
  31.2 1.8 %collective-permute-start.10 = (bf16[96,384]{1,0:T(8,128)(2,1)S(1)}, bf16[96,384]{1,0:T(8,128)(2,1)S(1)}, u32[]{:S(2)}, u32[]{:S(2)}) collective-permute-start(bf16[96,384]{1,0:T(8,128)(2,1)S(1)} %get-tuple-element.46), channel_id=1, source_target_pairs={{0,8},{4,12},{8,0},{12,4},{16,24},{20,28},{24,16},{28,20},{1,9},{5... | collective-permute-start | bytes 221192 | tf_op jit(solution)/shard_map/ppermute | solution.py:466
  33.0 1.2 %collective-permute-start.11 = (bf16[96,384]{1,0:T(8,128)(2,1)S(1)}, bf16[96,384]{1,0:T(8,128)(2,1)S(1)}, u32[]{:S(2)}, u32[]{:S(2)}) collective-permute-start(bf16[96,384]{1,0:T(8,128)(2,1)S(1)} %get-tuple-element.47), channel_id=1, source_target_pairs={{0,16},{4,20},{8,24},{12,28},{16,0},{20,4},{24,8},{28,12},{1,17},{... | collective-permute-start | bytes 221192 | tf_op jit(solution)/shard_map/ppermute | solution.py:466
  34.1 0.0 collective-permute-start.12
  34.2 0.0 collective-permute-done.8.rest_0_
  34.2 0.8 %collective-permute-start.13 = (bf16[96,384]{1,0:T(8,128)(2,1)S(1)}, bf16[96,384]{1,0:T(8,128)(2,1)S(1)}, u32[]{:S(2)}, u32[]{:S(2)}) collective-permute-start(bf16[96,384]{1,0:T(8,128)(2,1)S(1)} %get-tuple-element.49), channel_id=1, source_target_pairs={{0,20},{4,16},{8,28},{12,24},{16,4},{20,0},{24,12},{28,8},{1,21},{... | collective-permute-start | bytes 221192 | tf_op jit(solution)/shard_map/ppermute | solution.py:466
  35.0 1.2 %collective-permute-done.9.rest_1_ = bf16[96,384]{1,0:T(8,128)(2,1)S(1)} collective-permute-done((bf16[96,384]{1,0:T(8,128)(2,1)S(1)}, bf16[96,384]{1,0:T(8,128)(2,1)S(1)}, u32[]{:S(2)}, u32[]{:S(2)}) %collective-permute-start.9) | collective-permute-done | bytes 73760 | tf_op jit(solution)/shard_map/ppermute | solution.py:466
  36.2 0.3 collective-permute-start.14
  36.5 1.0 %collective-permute-done.10.rest_2_ = bf16[96,384]{1,0:T(8,128)(2,1)S(1)} collective-permute-done((bf16[96,384]{1,0:T(8,128)(2,1)S(1)}, bf16[96,384]{1,0:T(8,128)(2,1)S(1)}, u32[]{:S(2)}, u32[]{:S(2)}) %collective-permute-start.10) | collective-permute-done | bytes 73760 | tf_op jit(solution)/shard_map/ppermute | solution.py:466
  37.5 0.7 %collective-permute-done.11.rest_3_ = bf16[96,384]{1,0:T(8,128)(2,1)S(1)} collective-permute-done((bf16[96,384]{1,0:T(8,128)(2,1)S(1)}, bf16[96,384]{1,0:T(8,128)(2,1)S(1)}, u32[]{:S(2)}, u32[]{:S(2)}) %collective-permute-start.11) | collective-permute-done | bytes 73760 | tf_op jit(solution)/shard_map/ppermute | solution.py:466
  38.2 1.1 %collective-permute-done.12.rest_4_ = bf16[96,384]{1,0:T(8,128)(2,1)S(1)} collective-permute-done((bf16[96,384]{1,0:T(8,128)(2,1)S(1)}, bf16[96,384]{1,0:T(8,128)(2,1)S(1)}, u32[]{:S(2)}, u32[]{:S(2)}) %collective-permute-start.12) | collective-permute-done | bytes 73760 | tf_op jit(solution)/shard_map/ppermute | solution.py:466
  39.2 0.2 collective-permute-done.13.rest_5_
  39.4 0.0 collective-permute-done.14.rest_6_
  39.4 0.0 copy-done.1
  39.4 2.1 %shard_map.72 = (bf16[384,1152]{1,0:T(8,128)(2,1)}, f32[1,4]{1,0:T(1,128)}) custom-call(bf16[384,1152]{1,0:T(8,128)(2,1)S(1)} %bitcast.7, bf16[640,1152]{1,0:T(8,128)(2,1)S(1)} %get-tuple-element.35.weight_ref, bf16[4,1152]{1,0:T(4,128)(2,1)S(1)} %copy-done.3, bf16[96,384]{1,0:T(8,128)(2,1)S(1)} %collective-permute-done.8.rest_0_, ...), custom_call_target="tpu_custom_call" | custom-call | flops 509607936 | bytes 8388608 | tf_op jit(solution)/shard_map/pallas_call | solution.py:614
Async XLA Ops:
  0.6 6.8 %copy-start = (bf16[1152,1728]{0,1:T(8,128)(2,1)S(1)}, bf16[1152,1728]{0,1:T(8,128)(2,1)}, u32[]{:S(2)}) copy-start(bf16[1152,1728]{0,1:T(8,128)(2,1)} %param.7) | copy-start | bytes 11943940
  3.4 9.6 %collective-permute-start = (bf16[224,384]{1,0:T(8,128)(2,1)S(1)}, bf16[224,384]{1,0:T(8,128)(2,1)S(1)}, u32[]{:S(2)}, u32[]{:S(2)}) collective-permute-start(bf16[224,384]{1,0:T(8,128)(2,1)S(1)} %get-tuple-element.28), channel_id=1, source_target_pairs={{0,24},{4,28},{8,16},{12,20},{16,8},{20,12},{24,0},{28,4},{1,25},{... | collective-permute-start | bytes 516104 | tf_op jit(solution)/shard_map/ppermute | solution.py:466
  7.4 8.5 %collective-permute-start.1 = (bf16[224,384]{1,0:T(8,128)(2,1)S(1)}, bf16[224,384]{1,0:T(8,128)(2,1)S(1)}, u32[]{:S(2)}, u32[]{:S(2)}) collective-permute-start(bf16[224,384]{1,0:T(8,128)(2,1)S(1)} %get-tuple-element.29), channel_id=1, source_target_pairs={{0,28},{4,24},{8,20},{12,16},{16,12},{20,8},{24,4},{28,0},{1,29},{... | collective-permute-start | bytes 516104 | tf_op jit(solution)/shard_map/ppermute | solution.py:466
  7.4 10.4 %copy-start.3 = (bf16[4,1152]{1,0:T(4,128)(2,1)S(1)}, bf16[4,1152]{1,0:T(4,128)(2,1)}, u32[]{:S(2)}) copy-start(bf16[4,1152]{1,0:T(4,128)(2,1)} %text_ref.1) | copy-start | bytes 27652
  7.4 11.9 %copy-start.2 = (s32[1,3072]{1,0:T(1,128)S(1)}, s32[1,3072]{1,0:T(1,128)}, u32[]{:S(2)}) copy-start(s32[1,3072]{1,0:T(1,128)} %ids_ref.5) | copy-start | bytes 36868
  9.4 8.4 %collective-permute-start.2 = (bf16[224,384]{1,0:T(8,128)(2,1)S(1)}, bf16[224,384]{1,0:T(8,128)(2,1)S(1)}, u32[]{:S(2)}, u32[]{:S(2)}) collective-permute-start(bf16[224,384]{1,0:T(8,128)(2,1)S(1)} %get-tuple-element.32), channel_id=1, source_target_pairs={{0,4},{4,0},{8,12},{12,8},{16,20},{20,16},{24,28},{28,24},{1,5},{5... | collective-permute-start | bytes 516104 | tf_op jit(solution)/shard_map/ppermute | solution.py:466
  9.6 11.8 %collective-permute-start.3 = (bf16[224,384]{1,0:T(8,128)(2,1)S(1)}, bf16[224,384]{1,0:T(8,128)(2,1)S(1)}, u32[]{:S(2)}, u32[]{:S(2)}) collective-permute-start(bf16[224,384]{1,0:T(8,128)(2,1)S(1)} %get-tuple-element.39), channel_id=1, source_target_pairs={{0,8},{4,12},{8,0},{12,4},{16,24},{20,28},{24,16},{28,20},{1,9},{5... | collective-permute-start | bytes 516104 | tf_op jit(solution)/shard_map/ppermute | solution.py:466
  11.5 9.9 %collective-permute-start.4 = (bf16[224,384]{1,0:T(8,128)(2,1)S(1)}, bf16[224,384]{1,0:T(8,128)(2,1)S(1)}, u32[]{:S(2)}, u32[]{:S(2)}) collective-permute-start(bf16[224,384]{1,0:T(8,128)(2,1)S(1)} %get-tuple-element.40), channel_id=1, source_target_pairs={{0,16},{4,20},{8,24},{12,28},{16,0},{20,4},{24,8},{28,12},{1,17},{... | collective-permute-start | bytes 516104 | tf_op jit(solution)/shard_map/ppermute | solution.py:466
  13.0 9.1 %collective-permute-start.5 = (bf16[224,384]{1,0:T(8,128)(2,1)S(1)}, bf16[224,384]{1,0:T(8,128)(2,1)S(1)}, u32[]{:S(2)}, u32[]{:S(2)}) collective-permute-start(bf16[224,384]{1,0:T(8,128)(2,1)S(1)} %get-tuple-element.41), channel_id=1, source_target_pairs={{0,12},{4,8},{8,4},{12,0},{16,28},{20,24},{24,20},{28,16},{1,13},{... | collective-permute-start | bytes 516104 | tf_op jit(solution)/shard_map/ppermute | solution.py:466
  15.9 6.9 %collective-permute-start.6 = (bf16[224,384]{1,0:T(8,128)(2,1)S(1)}, bf16[224,384]{1,0:T(8,128)(2,1)S(1)}, u32[]{:S(2)}, u32[]{:S(2)}) collective-permute-start(bf16[224,384]{1,0:T(8,128)(2,1)S(1)} %get-tuple-element.42), channel_id=1, source_target_pairs={{0,20},{4,16},{8,28},{12,24},{16,4},{20,0},{24,12},{28,8},{1,21},{... | collective-permute-start | bytes 516104 | tf_op jit(solution)/shard_map/ppermute | solution.py:466
  17.8 3.7 %collective-permute-start.7 = (bf16[4,1152]{1,0:T(4,128)(2,1)S(1)}, bf16[4,1152]{1,0:T(4,128)(2,1)S(1)}, u32[]{:S(2)}, u32[]{:S(2)}) collective-permute-start(bf16[4,1152]{1,0:T(4,128)(2,1)S(1)} %copy-done.3), channel_id=1, source_target_pairs={{1,0},{0,1},{3,2},{2,3},{6,4},{7,5},{4,6},{5,7},{11,8},{10,9},{9,1... | collective-permute-start | bytes 27656 | tf_op jit(solution)/shard_map/ppermute | solution.py:466
  22.7 16.7 %copy-start.1 = (bf16[1,384,1152]{2,1,0:T(8,128)(2,1)S(1)}, bf16[1,384,1152]{2,1,0:T(8,128)(2,1)}, u32[]{:S(2)}) copy-start(bf16[1,384,1152]{2,1,0:T(8,128)(2,1)} %param.5) | copy-start | bytes 2654212
  28.7 5.5 %collective-permute-start.8 = (bf16[96,384]{1,0:T(8,128)(2,1)S(1)}, bf16[96,384]{1,0:T(8,128)(2,1)S(1)}, u32[]{:S(2)}, u32[]{:S(2)}) collective-permute-start(bf16[96,384]{1,0:T(8,128)(2,1)S(1)} %get-tuple-element.44), channel_id=1, source_target_pairs={{0,24},{4,28},{8,16},{12,20},{16,8},{20,12},{24,0},{28,4},{1,25},{... | collective-permute-start | bytes 221192 | tf_op jit(solution)/shard_map/ppermute | solution.py:466
  31.0 5.2 %collective-permute-start.9 = (bf16[96,384]{1,0:T(8,128)(2,1)S(1)}, bf16[96,384]{1,0:T(8,128)(2,1)S(1)}, u32[]{:S(2)}, u32[]{:S(2)}) collective-permute-start(bf16[96,384]{1,0:T(8,128)(2,1)S(1)} %get-tuple-element.45), channel_id=1, source_target_pairs={{0,28},{4,24},{8,20},{12,16},{16,12},{20,8},{24,4},{28,0},{1,29},{... | collective-permute-start | bytes 221192 | tf_op jit(solution)/shard_map/ppermute | solution.py:466
  31.2 6.3 %collective-permute-start.10 = (bf16[96,384]{1,0:T(8,128)(2,1)S(1)}, bf16[96,384]{1,0:T(8,128)(2,1)S(1)}, u32[]{:S(2)}, u32[]{:S(2)}) collective-permute-start(bf16[96,384]{1,0:T(8,128)(2,1)S(1)} %get-tuple-element.46), channel_id=1, source_target_pairs={{0,8},{4,12},{8,0},{12,4},{16,24},{20,28},{24,16},{28,20},{1,9},{5... | collective-permute-start | bytes 221192 | tf_op jit(solution)/shard_map/ppermute | solution.py:466
  33.0 5.2 %collective-permute-start.11 = (bf16[96,384]{1,0:T(8,128)(2,1)S(1)}, bf16[96,384]{1,0:T(8,128)(2,1)S(1)}, u32[]{:S(2)}, u32[]{:S(2)}) collective-permute-start(bf16[96,384]{1,0:T(8,128)(2,1)S(1)} %get-tuple-element.47), channel_id=1, source_target_pairs={{0,16},{4,20},{8,24},{12,28},{16,0},{20,4},{24,8},{28,12},{1,17},{... | collective-permute-start | bytes 221192 | tf_op jit(solution)/shard_map/ppermute | solution.py:466
  34.1 5.1 %collective-permute-start.12 = (bf16[96,384]{1,0:T(8,128)(2,1)S(1)}, bf16[96,384]{1,0:T(8,128)(2,1)S(1)}, u32[]{:S(2)}, u32[]{:S(2)}) collective-permute-start(bf16[96,384]{1,0:T(8,128)(2,1)S(1)} %get-tuple-element.48), channel_id=1, source_target_pairs={{0,12},{4,8},{8,4},{12,0},{16,28},{20,24},{24,20},{28,16},{1,13},{... | collective-permute-start | bytes 221192 | tf_op jit(solution)/shard_map/ppermute | solution.py:466
  34.2 5.2 %collective-permute-start.13 = (bf16[96,384]{1,0:T(8,128)(2,1)S(1)}, bf16[96,384]{1,0:T(8,128)(2,1)S(1)}, u32[]{:S(2)}, u32[]{:S(2)}) collective-permute-start(bf16[96,384]{1,0:T(8,128)(2,1)S(1)} %get-tuple-element.49), channel_id=1, source_target_pairs={{0,20},{4,16},{8,28},{12,24},{16,4},{20,0},{24,12},{28,8},{1,21},{... | collective-permute-start | bytes 221192 | tf_op jit(solution)/shard_map/ppermute | solution.py:466
  36.2 3.2 %collective-permute-start.14 = (bf16[96,384]{1,0:T(8,128)(2,1)S(1)}, bf16[96,384]{1,0:T(8,128)(2,1)S(1)}, u32[]{:S(2)}, u32[]{:S(2)}) collective-permute-start(bf16[96,384]{1,0:T(8,128)(2,1)S(1)} %get-tuple-element.50), channel_id=1, source_target_pairs={{0,4},{4,0},{8,12},{12,8},{16,20},{20,16},{24,28},{28,24},{1,5},{5... | collective-permute-start | bytes 221192 | tf_op jit(solution)/shard_map/ppermute | solution.py:466

commit v31 on v22

--- a/solution.py
+++ b/solution.py
@@ -19,8 +19,8 @@
 TEXT_ROWS = 16
 HIDDEN = -1e30
 ORDER = (6, 7, 2, 4, 3, 5, 1, 0)
-EARLY = (6, 7, 1, 0)
-LATE = (2, 4, 3, 5)
+EARLY = (6, 7, 0)
+LATE = (2, 4, 3, 5, 1)
 
 logit_scale = 30.0
 logit_bias = -5.0

time: 42.1 us -> 43.2 us (1.026)
  starting transfers between devices: 17.6 us -> 18.3 us
  waiting for transfers between devices: 8.76 us -> 9.26 us
    ppermute x15, starting transfers between devices: 17.6 us -> 18.3 us  [moved(): return lax.ppermute(value, axis, pairs)]
    ppermute x15, waiting for transfers between devices: 8.76 us -> 9.26 us  [moved(): return lax.ppermute(value, axis, pairs)]
  transfers between devices with their start and end apart: 15 -> 15, of which waited for: 9 -> 9; matrix products, arithmetic and copies ran while one was open for 0% -> 0% of each run, Pallas kernels for 9% -> 8%
where the time goes in v31:
time: 43.2 us
  starting transfers between devices  18.3 us (42%)
  Pallas kernels  15 us (35%)
  waiting for transfers between devices  9.26 us (21%)
  between operations  0.7 us (2%)
    ppermute x15, starting transfers between devices, moved(): return lax.ppermute(value, axis, pairs)  18.3 us
    ppermute x15, waiting for transfers between devices, moved(): return lax.ppermute(value, axis, pairs)  9.26 us
    pallas_call x1, Pallas kernels, local(): call(functools.partial(attend_kernel, images, piggy, halo), (shape((padde...  6.52 us
    pallas_call x1, Pallas kernels, local(): call(functools.partial(far_kernel, images, piggy), (shape((depth, count),...  2.8 us
    pallas_call x1, Pallas kernels, local(): call(functools.partial(finish_kernel, images), (shape((count, depth), bf1...  2.13 us
    pallas_call x1, Pallas kernels, local(): call(functools.partial(near_kernel, piggy), (block,) * 6, [], in_vmem(3),...  1.95 us
    pallas_call x1, Pallas kernels, local(): call(functools.partial(prepare_kernel, images, halo), (shape((len(EARLY)...  1.6 us
  transfers between devices with their start and end apart: 15, of which 9 were waited for; matrix products, arithmetic and copies ran while one was open for 0% of the time, Pallas kernels for 8%

profile of v31, /device:TPU:0, one launch (start us, length us, event | category | flops | bytes accessed | tf_op | source)
XLA Modules:
  0.0 43.2 jit_solution(534746121837919152)
XLA Ops:
  0.6 0.0 copy-start
  0.6 2.8 %shard_map.68 = (bf16[1152,384]{1,0:T(8,128)(2,1)S(1)}, f32[8,1152]{1,0:T(8,128)S(1)}, bf16[224,384]{1,0:T(8,128)(2,1)S(1)}, bf16[224,384]{1,0:T(8,128)(2,1)S(1)}) custom-call(s32[1,3072]{1,0:T(1,128)} %ids_ref.5, bf16[384,1152]{1,0:T(8,128)(2,1)} %bitcast.6, bf16[1728,1152]{1,0:T(8,128)(2,1)} %bitcast.4), custom_call_target="tpu_custom_call" | custom-call | flops 382205952 | bytes 8388608 | tf_op jit(solution)/shard_map/pallas_call | solution.py:514
  3.4 4.0 %collective-permute-start = (bf16[224,384]{1,0:T(8,128)(2,1)S(1)}, bf16[224,384]{1,0:T(8,128)(2,1)S(1)}, u32[]{:S(2)}, u32[]{:S(2)}) collective-permute-start(bf16[224,384]{1,0:T(8,128)(2,1)S(1)} %get-tuple-element.28), channel_id=1, source_target_pairs={{0,24},{4,28},{8,16},{12,20},{16,8},{20,12},{24,0},{28,4},{1,25},{... | collective-permute-start | bytes 516104 | tf_op jit(solution)/shard_map/ppermute | solution.py:463
  7.4 0.0 collective-permute-start.1
  7.4 0.0 copy-done
  7.4 0.0 copy-start.3
  7.4 0.0 copy-start.2
  7.4 1.9 %shard_map.69 = (bf16[224,384]{1,0:T(8,128)(2,1)S(1)}, bf16[224,384]{1,0:T(8,128)(2,1)S(1)}, bf16[224,384]{1,0:T(8,128)(2,1)S(1)}, bf16[224,384]{1,0:T(8,128)(2,...) custom-call(bf16[1152,384]{1,0:T(8,128)(2,1)S(1)} %get-tuple-element.30.normed_ref, ...), custom_call_target="tpu_custom_call" | custom-call | flops 1146617856 | bytes 8388608 | tf_op jit(solution)/shard_map/pallas_call | solution.py:528
  9.4 0.0 copy-done.3
  9.4 1.6 %collective-permute-start.7 = (bf16[4,1152]{1,0:T(4,128)(2,1)S(1)}, bf16[4,1152]{1,0:T(4,128)(2,1)S(1)}, u32[]{:S(2)}, u32[]{:S(2)}) collective-permute-start(bf16[4,1152]{1,0:T(4,128)(2,1)S(1)} %copy-done.3), channel_id=1, source_target_pairs={{1,0},{0,1},{3,2},{2,3},{6,4},{7,5},{4,6},{5,7},{11,8},{10,9},{9,1... | collective-permute-start | bytes 27656 | tf_op jit(solution)/shard_map/ppermute | solution.py:463
  11.0 3.1 %collective-permute-start.2 = (bf16[224,384]{1,0:T(8,128)(2,1)S(1)}, bf16[224,384]{1,0:T(8,128)(2,1)S(1)}, u32[]{:S(2)}, u32[]{:S(2)}) collective-permute-start(bf16[224,384]{1,0:T(8,128)(2,1)S(1)} %get-tuple-element.38), channel_id=1, source_target_pairs={{0,8},{4,12},{8,0},{12,4},{16,24},{20,28},{24,16},{28,20},{1,9},{5... | collective-permute-start | bytes 516104 | tf_op jit(solution)/shard_map/ppermute | solution.py:463
  14.1 0.0 collective-permute-start.3
  14.1 0.0 collective-permute-done.7.rest_8_
  14.2 1.8 %collective-permute-start.4 = (bf16[224,384]{1,0:T(8,128)(2,1)S(1)}, bf16[224,384]{1,0:T(8,128)(2,1)S(1)}, u32[]{:S(2)}, u32[]{:S(2)}) collective-permute-start(bf16[224,384]{1,0:T(8,128)(2,1)S(1)} %get-tuple-element.40), channel_id=1, source_target_pairs={{0,12},{4,8},{8,4},{12,0},{16,28},{20,24},{24,20},{28,16},{1,13},{... | collective-permute-start | bytes 516104 | tf_op jit(solution)/shard_map/ppermute | solution.py:463
  15.9 0.0 collective-permute-done.rest_0_
  15.9 0.0 collective-permute-start.5
  16.0 0.0 collective-permute-done.1.rest_1_
  16.0 0.5 %collective-permute-start.6 = (bf16[224,384]{1,0:T(8,128)(2,1)S(1)}, bf16[224,384]{1,0:T(8,128)(2,1)S(1)}, u32[]{:S(2)}, u32[]{:S(2)}) collective-permute-start(bf16[224,384]{1,0:T(8,128)(2,1)S(1)} %get-tuple-element.42), channel_id=1, source_target_pairs={{0,4},{4,0},{8,12},{12,8},{16,20},{20,16},{24,28},{28,24},{1,5},{5... | collective-permute-start | bytes 516104 | tf_op jit(solution)/shard_map/ppermute | solution.py:463
  16.5 0.0 copy-done.2
  16.5 1.6 %shard_map.70 = (bf16[1152,128]{1,0:T(8,128)(2,1)S(1)}, f32[2,8,3072]{2,1,0:T(8,128)S(1)}, s32[8,128]{1,0:T(8,128)S(1)}, bf16[640,1152]{1,0:T(8,128)(2,1)S(1)}) custom-call(s32[1,3072]{1,0:T(1,128)S(1)} %copy-done.2, bf16[576,1152]{1,0:T(8,128)(2,1)} %out_weight_ref.1, bf16[224,384]{1,0:T(8,128)(2,1)S(1)} %collective-permute-done.rest_0_, ...), custom_call_target="tpu_custom_call" | custom-call | flops 1073741824 | bytes 8388608 | tf_op jit(solution)/shard_map/pallas_call | solution.py:569
  18.1 2.1 %collective-permute-done.2.rest_3_ = bf16[224,384]{1,0:T(8,128)(2,1)S(1)} collective-permute-done((bf16[224,384]{1,0:T(8,128)(2,1)S(1)}, bf16[224,384]{1,0:T(8,128)(2,1)S(1)}, u32[]{:S(2)}, u32[]{:S(2)}) %collective-permute-start.2) | collective-permute-done | bytes 172064 | tf_op jit(solution)/shard_map/ppermute | solution.py:463
  20.1 0.1 collective-permute-done.3.rest_4_
  20.2 2.2 %collective-permute-done.4.rest_5_ = bf16[224,384]{1,0:T(8,128)(2,1)S(1)} collective-permute-done((bf16[224,384]{1,0:T(8,128)(2,1)S(1)}, bf16[224,384]{1,0:T(8,128)(2,1)S(1)}, u32[]{:S(2)}, u32[]{:S(2)}) %collective-permute-start.4) | collective-permute-done | bytes 172064 | tf_op jit(solution)/shard_map/ppermute | solution.py:463
  22.4 0.3 collective-permute-done.5.rest_6_
  22.7 0.0 collective-permute-done.6.rest_7_
  22.7 0.0 copy-start.1
  22.7 6.5 %shard_map.71 = (bf16[96,384]{1,0:T(8,128)(2,1)S(1)}, bf16[96,384]{1,0:T(8,128)(2,1)S(1)}, bf16[96,384]{1,0:T(8,128)(2,1)S(1)}, bf16[96,384]{1,0:T(8,128)(2,1)S(...) custom-call(s32[1,3072]{1,0:T(1,128)S(1)} %copy-done.2, ...), custom_call_target="tpu_custom_call" | custom-call | flops 905969664 | bytes 8388608 | tf_op jit(solution)/shard_map/pallas_call | solution.py:582
  29.2 3.5 %collective-permute-start.8 = (bf16[96,384]{1,0:T(8,128)(2,1)S(1)}, bf16[96,384]{1,0:T(8,128)(2,1)S(1)}, u32[]{:S(2)}, u32[]{:S(2)}) collective-permute-start(bf16[96,384]{1,0:T(8,128)(2,1)S(1)} %get-tuple-element.44), channel_id=1, source_target_pairs={{0,24},{4,28},{8,16},{12,20},{16,8},{20,12},{24,0},{28,4},{1,25},{... | collective-permute-start | bytes 221192 | tf_op jit(solution)/shard_map/ppermute | solution.py:463
  32.7 0.0 collective-permute-start.9
  32.7 0.9 %collective-permute-start.10 = (bf16[96,384]{1,0:T(8,128)(2,1)S(1)}, bf16[96,384]{1,0:T(8,128)(2,1)S(1)}, u32[]{:S(2)}, u32[]{:S(2)}) collective-permute-start(bf16[96,384]{1,0:T(8,128)(2,1)S(1)} %get-tuple-element.46), channel_id=1, source_target_pairs={{0,8},{4,12},{8,0},{12,4},{16,24},{20,28},{24,16},{28,20},{1,9},{5... | collective-permute-start | bytes 221192 | tf_op jit(solution)/shard_map/ppermute | solution.py:463
  33.6 1.9 %collective-permute-start.11 = (bf16[96,384]{1,0:T(8,128)(2,1)S(1)}, bf16[96,384]{1,0:T(8,128)(2,1)S(1)}, u32[]{:S(2)}, u32[]{:S(2)}) collective-permute-start(bf16[96,384]{1,0:T(8,128)(2,1)S(1)} %get-tuple-element.47), channel_id=1, source_target_pairs={{0,16},{4,20},{8,24},{12,28},{16,0},{20,4},{24,8},{28,12},{1,17},{... | collective-permute-start | bytes 221192 | tf_op jit(solution)/shard_map/ppermute | solution.py:463
  35.4 0.4 collective-permute-start.12
  35.8 0.0 collective-permute-done.8.rest_0_
  35.8 0.7 %collective-permute-start.13 = (bf16[96,384]{1,0:T(8,128)(2,1)S(1)}, bf16[96,384]{1,0:T(8,128)(2,1)S(1)}, u32[]{:S(2)}, u32[]{:S(2)}) collective-permute-start(bf16[96,384]{1,0:T(8,128)(2,1)S(1)} %get-tuple-element.49), channel_id=1, source_target_pairs={{0,20},{4,16},{8,28},{12,24},{16,4},{20,0},{24,12},{28,8},{1,21},{... | collective-permute-start | bytes 221192 | tf_op jit(solution)/shard_map/ppermute | solution.py:463
  36.5 1.7 %collective-permute-done.9.rest_1_ = bf16[96,384]{1,0:T(8,128)(2,1)S(1)} collective-permute-done((bf16[96,384]{1,0:T(8,128)(2,1)S(1)}, bf16[96,384]{1,0:T(8,128)(2,1)S(1)}, u32[]{:S(2)}, u32[]{:S(2)}) %collective-permute-start.9) | collective-permute-done | bytes 73760 | tf_op jit(solution)/shard_map/ppermute | solution.py:463
  38.2 0.0 collective-permute-start.14
  38.2 0.7 %collective-permute-done.10.rest_2_ = bf16[96,384]{1,0:T(8,128)(2,1)S(1)} collective-permute-done((bf16[96,384]{1,0:T(8,128)(2,1)S(1)}, bf16[96,384]{1,0:T(8,128)(2,1)S(1)}, u32[]{:S(2)}, u32[]{:S(2)}) %collective-permute-start.10) | collective-permute-done | bytes 73760 | tf_op jit(solution)/shard_map/ppermute | solution.py:463
  38.9 0.7 %collective-permute-done.11.rest_3_ = bf16[96,384]{1,0:T(8,128)(2,1)S(1)} collective-permute-done((bf16[96,384]{1,0:T(8,128)(2,1)S(1)}, bf16[96,384]{1,0:T(8,128)(2,1)S(1)}, u32[]{:S(2)}, u32[]{:S(2)}) %collective-permute-start.11) | collective-permute-done | bytes 73760 | tf_op jit(solution)/shard_map/ppermute | solution.py:463
  39.6 0.4 collective-permute-done.12.rest_4_
  40.0 1.1 %collective-permute-done.13.rest_5_ = bf16[96,384]{1,0:T(8,128)(2,1)S(1)} collective-permute-done((bf16[96,384]{1,0:T(8,128)(2,1)S(1)}, bf16[96,384]{1,0:T(8,128)(2,1)S(1)}, u32[]{:S(2)}, u32[]{:S(2)}) %collective-permute-start.13) | collective-permute-done | bytes 73760 | tf_op jit(solution)/shard_map/ppermute | solution.py:463
  41.1 0.0 collective-permute-done.14.rest_6_
  41.1 0.0 copy-done.1
  41.1 2.1 %shard_map.72 = (bf16[384,1152]{1,0:T(8,128)(2,1)}, f32[1,4]{1,0:T(1,128)}) custom-call(bf16[384,1152]{1,0:T(8,128)(2,1)S(1)} %bitcast.7, bf16[640,1152]{1,0:T(8,128)(2,1)S(1)} %get-tuple-element.34.weight_ref, bf16[4,1152]{1,0:T(4,128)(2,1)S(1)} %copy-done.3, bf16[96,384]{1,0:T(8,128)(2,1)S(1)} %collective-permute-done.8.rest_0_, ...), custom_call_target="tpu_custom_call" | custom-call | flops 509607936 | bytes 8388608 | tf_op jit(solution)/shard_map/pallas_call | solution.py:610
Async XLA Ops:
  0.6 6.8 %copy-start = (bf16[1152,1728]{0,1:T(8,128)(2,1)S(1)}, bf16[1152,1728]{0,1:T(8,128)(2,1)}, u32[]{:S(2)}) copy-start(bf16[1152,1728]{0,1:T(8,128)(2,1)} %param.7) | copy-start | bytes 11943940
  3.4 12.5 %collective-permute-start = (bf16[224,384]{1,0:T(8,128)(2,1)S(1)}, bf16[224,384]{1,0:T(8,128)(2,1)S(1)}, u32[]{:S(2)}, u32[]{:S(2)}) collective-permute-start(bf16[224,384]{1,0:T(8,128)(2,1)S(1)} %get-tuple-element.28), channel_id=1, source_target_pairs={{0,24},{4,28},{8,16},{12,20},{16,8},{20,12},{24,0},{28,4},{1,25},{... | collective-permute-start | bytes 516104 | tf_op jit(solution)/shard_map/ppermute | solution.py:463
  7.4 8.6 %collective-permute-start.1 = (bf16[224,384]{1,0:T(8,128)(2,1)S(1)}, bf16[224,384]{1,0:T(8,128)(2,1)S(1)}, u32[]{:S(2)}, u32[]{:S(2)}) collective-permute-start(bf16[224,384]{1,0:T(8,128)(2,1)S(1)} %get-tuple-element.29), channel_id=1, source_target_pairs={{0,28},{4,24},{8,20},{12,16},{16,12},{20,8},{24,4},{28,0},{1,29},{... | collective-permute-start | bytes 516104 | tf_op jit(solution)/shard_map/ppermute | solution.py:463
  7.4 2.0 %copy-start.3 = (bf16[4,1152]{1,0:T(4,128)(2,1)S(1)}, bf16[4,1152]{1,0:T(4,128)(2,1)}, u32[]{:S(2)}) copy-start(bf16[4,1152]{1,0:T(4,128)(2,1)} %text_ref.1) | copy-start | bytes 27652
  7.4 9.0 %copy-start.2 = (s32[1,3072]{1,0:T(1,128)S(1)}, s32[1,3072]{1,0:T(1,128)}, u32[]{:S(2)}) copy-start(s32[1,3072]{1,0:T(1,128)} %ids_ref.5) | copy-start | bytes 36868
  9.4 4.8 %collective-permute-start.7 = (bf16[4,1152]{1,0:T(4,128)(2,1)S(1)}, bf16[4,1152]{1,0:T(4,128)(2,1)S(1)}, u32[]{:S(2)}, u32[]{:S(2)}) collective-permute-start(bf16[4,1152]{1,0:T(4,128)(2,1)S(1)} %copy-done.3), channel_id=1, source_target_pairs={{1,0},{0,1},{3,2},{2,3},{6,4},{7,5},{4,6},{5,7},{11,8},{10,9},{9,1... | collective-permute-start | bytes 27656 | tf_op jit(solution)/shard_map/ppermute | solution.py:463
  11.0 9.1 %collective-permute-start.2 = (bf16[224,384]{1,0:T(8,128)(2,1)S(1)}, bf16[224,384]{1,0:T(8,128)(2,1)S(1)}, u32[]{:S(2)}, u32[]{:S(2)}) collective-permute-start(bf16[224,384]{1,0:T(8,128)(2,1)S(1)} %get-tuple-element.38), channel_id=1, source_target_pairs={{0,8},{4,12},{8,0},{12,4},{16,24},{20,28},{24,16},{28,20},{1,9},{5... | collective-permute-start | bytes 516104 | tf_op jit(solution)/shard_map/ppermute | solution.py:463
  14.1 6.1 %collective-permute-start.3 = (bf16[224,384]{1,0:T(8,128)(2,1)S(1)}, bf16[224,384]{1,0:T(8,128)(2,1)S(1)}, u32[]{:S(2)}, u32[]{:S(2)}) collective-permute-start(bf16[224,384]{1,0:T(8,128)(2,1)S(1)} %get-tuple-element.39), channel_id=1, source_target_pairs={{0,16},{4,20},{8,24},{12,28},{16,0},{20,4},{24,8},{28,12},{1,17},{... | collective-permute-start | bytes 516104 | tf_op jit(solution)/shard_map/ppermute | solution.py:463
  14.2 8.2 %collective-permute-start.4 = (bf16[224,384]{1,0:T(8,128)(2,1)S(1)}, bf16[224,384]{1,0:T(8,128)(2,1)S(1)}, u32[]{:S(2)}, u32[]{:S(2)}) collective-permute-start(bf16[224,384]{1,0:T(8,128)(2,1)S(1)} %get-tuple-element.40), channel_id=1, source_target_pairs={{0,12},{4,8},{8,4},{12,0},{16,28},{20,24},{24,20},{28,16},{1,13},{... | collective-permute-start | bytes 516104 | tf_op jit(solution)/shard_map/ppermute | solution.py:463
  15.9 6.7 %collective-permute-start.5 = (bf16[224,384]{1,0:T(8,128)(2,1)S(1)}, bf16[224,384]{1,0:T(8,128)(2,1)S(1)}, u32[]{:S(2)}, u32[]{:S(2)}) collective-permute-start(bf16[224,384]{1,0:T(8,128)(2,1)S(1)} %get-tuple-element.41), channel_id=1, source_target_pairs={{0,20},{4,16},{8,28},{12,24},{16,4},{20,0},{24,12},{28,8},{1,21},{... | collective-permute-start | bytes 516104 | tf_op jit(solution)/shard_map/ppermute | solution.py:463
  16.0 6.7 %collective-permute-start.6 = (bf16[224,384]{1,0:T(8,128)(2,1)S(1)}, bf16[224,384]{1,0:T(8,128)(2,1)S(1)}, u32[]{:S(2)}, u32[]{:S(2)}) collective-permute-start(bf16[224,384]{1,0:T(8,128)(2,1)S(1)} %get-tuple-element.42), channel_id=1, source_target_pairs={{0,4},{4,0},{8,12},{12,8},{16,20},{20,16},{24,28},{28,24},{1,5},{5... | collective-permute-start | bytes 516104 | tf_op jit(solution)/shard_map/ppermute | solution.py:463
  22.7 18.4 %copy-start.1 = (bf16[1,384,1152]{2,1,0:T(8,128)(2,1)S(1)}, bf16[1,384,1152]{2,1,0:T(8,128)(2,1)}, u32[]{:S(2)}) copy-start(bf16[1,384,1152]{2,1,0:T(8,128)(2,1)} %param.5) | copy-start | bytes 2654212
  29.2 6.6 %collective-permute-start.8 = (bf16[96,384]{1,0:T(8,128)(2,1)S(1)}, bf16[96,384]{1,0:T(8,128)(2,1)S(1)}, u32[]{:S(2)}, u32[]{:S(2)}) collective-permute-start(bf16[96,384]{1,0:T(8,128)(2,1)S(1)} %get-tuple-element.44), channel_id=1, source_target_pairs={{0,24},{4,28},{8,16},{12,20},{16,8},{20,12},{24,0},{28,4},{1,25},{... | collective-permute-start | bytes 221192 | tf_op jit(solution)/shard_map/ppermute | solution.py:463
  32.7 5.5 %collective-permute-start.9 = (bf16[96,384]{1,0:T(8,128)(2,1)S(1)}, bf16[96,384]{1,0:T(8,128)(2,1)S(1)}, u32[]{:S(2)}, u32[]{:S(2)}) collective-permute-start(bf16[96,384]{1,0:T(8,128)(2,1)S(1)} %get-tuple-element.45), channel_id=1, source_target_pairs={{0,28},{4,24},{8,20},{12,16},{16,12},{20,8},{24,4},{28,0},{1,29},{... | collective-permute-start | bytes 221192 | tf_op jit(solution)/shard_map/ppermute | solution.py:463
  32.7 6.1 %collective-permute-start.10 = (bf16[96,384]{1,0:T(8,128)(2,1)S(1)}, bf16[96,384]{1,0:T(8,128)(2,1)S(1)}, u32[]{:S(2)}, u32[]{:S(2)}) collective-permute-start(bf16[96,384]{1,0:T(8,128)(2,1)S(1)} %get-tuple-element.46), channel_id=1, source_target_pairs={{0,8},{4,12},{8,0},{12,4},{16,24},{20,28},{24,16},{28,20},{1,9},{5... | collective-permute-start | bytes 221192 | tf_op jit(solution)/shard_map/ppermute | solution.py:463
  33.6 6.0 %collective-permute-start.11 = (bf16[96,384]{1,0:T(8,128)(2,1)S(1)}, bf16[96,384]{1,0:T(8,128)(2,1)S(1)}, u32[]{:S(2)}, u32[]{:S(2)}) collective-permute-start(bf16[96,384]{1,0:T(8,128)(2,1)S(1)} %get-tuple-element.47), channel_id=1, source_target_pairs={{0,16},{4,20},{8,24},{12,28},{16,0},{20,4},{24,8},{28,12},{1,17},{... | collective-permute-start | bytes 221192 | tf_op jit(solution)/shard_map/ppermute | solution.py:463
  35.4 4.6 %collective-permute-start.12 = (bf16[96,384]{1,0:T(8,128)(2,1)S(1)}, bf16[96,384]{1,0:T(8,128)(2,1)S(1)}, u32[]{:S(2)}, u32[]{:S(2)}) collective-permute-start(bf16[96,384]{1,0:T(8,128)(2,1)S(1)} %get-tuple-element.48), channel_id=1, source_target_pairs={{0,12},{4,8},{8,4},{12,0},{16,28},{20,24},{24,20},{28,16},{1,13},{... | collective-permute-start | bytes 221192 | tf_op jit(solution)/shard_map/ppermute | solution.py:463
  35.8 5.3 %collective-permute-start.13 = (bf16[96,384]{1,0:T(8,128)(2,1)S(1)}, bf16[96,384]{1,0:T(8,128)(2,1)S(1)}, u32[]{:S(2)}, u32[]{:S(2)}) collective-permute-start(bf16[96,384]{1,0:T(8,128)(2,1)S(1)} %get-tuple-element.49), channel_id=1, source_target_pairs={{0,20},{4,16},{8,28},{12,24},{16,4},{20,0},{24,12},{28,8},{1,21},{... | collective-permute-start | bytes 221192 | tf_op jit(solution)/shard_map/ppermute | solution.py:463
  38.2 2.9 %collective-permute-start.14 = (bf16[96,384]{1,0:T(8,128)(2,1)S(1)}, bf16[96,384]{1,0:T(8,128)(2,1)S(1)}, u32[]{:S(2)}, u32[]{:S(2)}) collective-permute-start(bf16[96,384]{1,0:T(8,128)(2,1)S(1)} %get-tuple-element.50), channel_id=1, source_target_pairs={{0,4},{4,0},{8,12},{12,8},{16,20},{20,16},{24,28},{28,24},{1,5},{5... | collective-permute-start | bytes 221192 | tf_op jit(solution)/shard_map/ppermute | solution.py:463

commit v32 on v22

--- a/solution.py
+++ b/solution.py
@@ -18,9 +18,9 @@
 QUERY_AT = 2 * SIZE
 TEXT_ROWS = 16
 HIDDEN = -1e30
-ORDER = (6, 7, 2, 4, 3, 5, 1, 0)
+ORDER = (6, 7, 4, 2, 5, 3, 1, 0)
 EARLY = (6, 7, 1, 0)
-LATE = (2, 4, 3, 5)
+LATE = (4, 2, 5, 3)
 
 logit_scale = 30.0
 logit_bias = -5.0

time: 42.1 us -> 41.6 us (0.988)
  transfers between devices with their start and end apart: 15 -> 15, of which waited for: 9 -> 6; matrix products, arithmetic and copies ran while one was open for 0% -> 0% of each run, Pallas kernels for 9% -> 9%
where the time goes in v32:
time: 41.6 us
  starting transfers between devices  17.6 us (42%)
  Pallas kernels  15 us (36%)
  waiting for transfers between devices  8.4 us (20%)
  between operations  0.69 us (2%)
    ppermute x15, starting transfers between devices, moved(): return lax.ppermute(value, axis, pairs)  17.6 us
    ppermute x15, waiting for transfers between devices, moved(): return lax.ppermute(value, axis, pairs)  8.4 us
    pallas_call x1, Pallas kernels, local(): call(functools.partial(attend_kernel, images, piggy, halo), (shape((padde...  6.44 us
    pallas_call x1, Pallas kernels, local(): call(functools.partial(far_kernel, images, piggy), (shape((depth, count),...  2.8 us
    pallas_call x1, Pallas kernels, local(): call(functools.partial(finish_kernel, images), (shape((count, depth), bf1...  2.14 us
    pallas_call x1, Pallas kernels, local(): call(functools.partial(near_kernel, piggy), (block,) * 6, [], in_vmem(3),...  1.95 us
    pallas_call x1, Pallas kernels, local(): call(functools.partial(prepare_kernel, images, halo), (shape((len(EARLY)...  1.64 us
  transfers between devices with their start and end apart: 15, of which 6 were waited for; matrix products, arithmetic and copies ran while one was open for 0% of the time, Pallas kernels for 9%

profile of v32, /device:TPU:0, one launch (start us, length us, event | category | flops | bytes accessed | tf_op | source)
XLA Modules:
  0.0 41.6 jit_solution(2164267181156800051)
XLA Ops:
  0.6 0.0 copy-start
  0.6 2.8 %shard_map.68 = (bf16[1152,384]{1,0:T(8,128)(2,1)S(1)}, f32[8,1152]{1,0:T(8,128)S(1)}, bf16[224,384]{1,0:T(8,128)(2,1)S(1)}, bf16[224,384]{1,0:T(8,128)(2,1)S(1)}) custom-call(s32[1,3072]{1,0:T(1,128)} %ids_ref.5, bf16[384,1152]{1,0:T(8,128)(2,1)} %bitcast.6, bf16[1728,1152]{1,0:T(8,128)(2,1)} %bitcast.4), custom_call_target="tpu_custom_call" | custom-call | flops 382205952 | bytes 8388608 | tf_op jit(solution)/shard_map/pallas_call | solution.py:514
  3.4 4.0 %collective-permute-start = (bf16[224,384]{1,0:T(8,128)(2,1)S(1)}, bf16[224,384]{1,0:T(8,128)(2,1)S(1)}, u32[]{:S(2)}, u32[]{:S(2)}) collective-permute-start(bf16[224,384]{1,0:T(8,128)(2,1)S(1)} %get-tuple-element.28), channel_id=1, source_target_pairs={{0,24},{4,28},{8,16},{12,20},{16,8},{20,12},{24,0},{28,4},{1,25},{... | collective-permute-start | bytes 516104 | tf_op jit(solution)/shard_map/ppermute | solution.py:463
  7.4 0.0 collective-permute-start.1
  7.4 0.0 copy-done
  7.4 0.0 copy-start.3
  7.4 0.0 copy-start.2
  7.4 1.9 %shard_map.69 = (bf16[224,384]{1,0:T(8,128)(2,1)S(1)}, bf16[224,384]{1,0:T(8,128)(2,1)S(1)}, bf16[224,384]{1,0:T(8,128)(2,1)S(1)}, bf16[224,384]{1,0:T(8,128)(2,...) custom-call(bf16[1152,384]{1,0:T(8,128)(2,1)S(1)} %get-tuple-element.30.normed_ref, ...), custom_call_target="tpu_custom_call" | custom-call | flops 1146617856 | bytes 8388608 | tf_op jit(solution)/shard_map/pallas_call | solution.py:528
  9.4 0.2 collective-permute-start.2
  9.6 1.9 %collective-permute-start.3 = (bf16[224,384]{1,0:T(8,128)(2,1)S(1)}, bf16[224,384]{1,0:T(8,128)(2,1)S(1)}, u32[]{:S(2)}, u32[]{:S(2)}) collective-permute-start(bf16[224,384]{1,0:T(8,128)(2,1)S(1)} %get-tuple-element.39), channel_id=1, source_target_pairs={{0,16},{4,20},{8,24},{12,28},{16,0},{20,4},{24,8},{28,12},{1,17},{... | collective-permute-start | bytes 516104 | tf_op jit(solution)/shard_map/ppermute | solution.py:463
  11.5 1.5 %collective-permute-start.4 = (bf16[224,384]{1,0:T(8,128)(2,1)S(1)}, bf16[224,384]{1,0:T(8,128)(2,1)S(1)}, u32[]{:S(2)}, u32[]{:S(2)}) collective-permute-start(bf16[224,384]{1,0:T(8,128)(2,1)S(1)} %get-tuple-element.40), channel_id=1, source_target_pairs={{0,8},{4,12},{8,0},{12,4},{16,24},{20,28},{24,16},{28,20},{1,9},{5... | collective-permute-start | bytes 516104 | tf_op jit(solution)/shard_map/ppermute | solution.py:463
  13.0 0.0 collective-permute-done.rest_0_
  13.0 0.0 collective-permute-start.5
  13.0 2.9 %collective-permute-done.1.rest_1_ = bf16[224,384]{1,0:T(8,128)(2,1)S(1)} collective-permute-done((bf16[224,384]{1,0:T(8,128)(2,1)S(1)}, bf16[224,384]{1,0:T(8,128)(2,1)S(1)}, u32[]{:S(2)}, u32[]{:S(2)}) %collective-permute-start.1) | collective-permute-done | bytes 172064 | tf_op jit(solution)/shard_map/ppermute | solution.py:463
  15.9 1.9 %collective-permute-start.6 = (bf16[224,384]{1,0:T(8,128)(2,1)S(1)}, bf16[224,384]{1,0:T(8,128)(2,1)S(1)}, u32[]{:S(2)}, u32[]{:S(2)}) collective-permute-start(bf16[224,384]{1,0:T(8,128)(2,1)S(1)} %get-tuple-element.42), channel_id=1, source_target_pairs={{0,12},{4,8},{8,4},{12,0},{16,28},{20,24},{24,20},{28,16},{1,13},{... | collective-permute-start | bytes 516104 | tf_op jit(solution)/shard_map/ppermute | solution.py:463
  17.8 0.0 collective-permute-done.2.rest_2_
  17.8 0.0 copy-done.3
  17.8 1.6 %collective-permute-start.7 = (bf16[4,1152]{1,0:T(4,128)(2,1)S(1)}, bf16[4,1152]{1,0:T(4,128)(2,1)S(1)}, u32[]{:S(2)}, u32[]{:S(2)}) collective-permute-start(bf16[4,1152]{1,0:T(4,128)(2,1)S(1)} %copy-done.3), channel_id=1, source_target_pairs={{1,0},{0,1},{3,2},{2,3},{6,4},{7,5},{4,6},{5,7},{11,8},{10,9},{9,1... | collective-permute-start | bytes 27656 | tf_op jit(solution)/shard_map/ppermute | solution.py:463
  19.4 0.0 copy-done.2
  19.4 1.6 %shard_map.70 = (bf16[1536,128]{1,0:T(8,128)(2,1)S(1)}, f32[2,8,3072]{2,1,0:T(8,128)S(1)}, s32[8,128]{1,0:T(8,128)S(1)}, bf16[640,1152]{1,0:T(8,128)(2,1)S(1)}) custom-call(s32[1,3072]{1,0:T(1,128)S(1)} %copy-done.2, bf16[576,1152]{1,0:T(8,128)(2,1)} %out_weight_ref.1, bf16[224,384]{1,0:T(8,128)(2,1)S(1)} %collective-permute-done.rest_0_, ...), custom_call_target="tpu_custom_call" | custom-call | flops 1073741824 | bytes 8388608 | tf_op jit(solution)/shard_map/pallas_call | solution.py:569
  21.0 0.4 %collective-permute-done.7.rest_8_ = bf16[4,1152]{1,0:T(4,128)(2,1)S(1)} collective-permute-done((bf16[4,1152]{1,0:T(4,128)(2,1)S(1)}, bf16[4,1152]{1,0:T(4,128)(2,1)S(1)}, u32[]{:S(2)}, u32[]{:S(2)}) %collective-permute-start.7) | collective-permute-done | bytes 9248 | tf_op jit(solution)/shard_map/ppermute | solution.py:463
  21.4 0.0 collective-permute-done.3.rest_4_
  21.4 0.0 collective-permute-done.4.rest_5_
  21.4 1.3 %collective-permute-done.5.rest_6_ = bf16[224,384]{1,0:T(8,128)(2,1)S(1)} collective-permute-done((bf16[224,384]{1,0:T(8,128)(2,1)S(1)}, bf16[224,384]{1,0:T(8,128)(2,1)S(1)}, u32[]{:S(2)}, u32[]{:S(2)}) %collective-permute-start.5) | collective-permute-done | bytes 172064 | tf_op jit(solution)/shard_map/ppermute | solution.py:463
  22.8 0.0 collective-permute-done.6.rest_7_
  22.8 0.0 copy-start.1
  22.8 6.4 %shard_map.71 = (bf16[96,384]{1,0:T(8,128)(2,1)S(1)}, bf16[96,384]{1,0:T(8,128)(2,1)S(1)}, bf16[96,384]{1,0:T(8,128)(2,1)S(1)}, bf16[96,384]{1,0:T(8,128)(2,1)S(...) custom-call(s32[1,3072]{1,0:T(1,128)S(1)} %copy-done.2, ...), custom_call_target="tpu_custom_call" | custom-call | flops 905969664 | bytes 8388608 | tf_op jit(solution)/shard_map/pallas_call | solution.py:582
  29.2 2.7 %collective-permute-start.8 = (bf16[96,384]{1,0:T(8,128)(2,1)S(1)}, bf16[96,384]{1,0:T(8,128)(2,1)S(1)}, u32[]{:S(2)}, u32[]{:S(2)}) collective-permute-start(bf16[96,384]{1,0:T(8,128)(2,1)S(1)} %get-tuple-element.44), channel_id=1, source_target_pairs={{0,24},{4,28},{8,16},{12,20},{16,8},{20,12},{24,0},{28,4},{1,25},{... | collective-permute-start | bytes 221192 | tf_op jit(solution)/shard_map/ppermute | solution.py:463
  31.9 0.0 collective-permute-start.9
  31.9 1.4 %collective-permute-start.10 = (bf16[96,384]{1,0:T(8,128)(2,1)S(1)}, bf16[96,384]{1,0:T(8,128)(2,1)S(1)}, u32[]{:S(2)}, u32[]{:S(2)}) collective-permute-start(bf16[96,384]{1,0:T(8,128)(2,1)S(1)} %get-tuple-element.46), channel_id=1, source_target_pairs={{0,16},{4,20},{8,24},{12,28},{16,0},{20,4},{24,8},{28,12},{1,17},{... | collective-permute-start | bytes 221192 | tf_op jit(solution)/shard_map/ppermute | solution.py:463
  33.4 1.5 %collective-permute-start.11 = (bf16[96,384]{1,0:T(8,128)(2,1)S(1)}, bf16[96,384]{1,0:T(8,128)(2,1)S(1)}, u32[]{:S(2)}, u32[]{:S(2)}) collective-permute-start(bf16[96,384]{1,0:T(8,128)(2,1)S(1)} %get-tuple-element.47), channel_id=1, source_target_pairs={{0,8},{4,12},{8,0},{12,4},{16,24},{20,28},{24,16},{28,20},{1,9},{5... | collective-permute-start | bytes 221192 | tf_op jit(solution)/shard_map/ppermute | solution.py:463
  34.9 0.2 collective-permute-start.12
  35.1 0.0 collective-permute-done.8.rest_0_
  35.1 0.6 %collective-permute-start.13 = (bf16[96,384]{1,0:T(8,128)(2,1)S(1)}, bf16[96,384]{1,0:T(8,128)(2,1)S(1)}, u32[]{:S(2)}, u32[]{:S(2)}) collective-permute-start(bf16[96,384]{1,0:T(8,128)(2,1)S(1)} %get-tuple-element.49), channel_id=1, source_target_pairs={{0,12},{4,8},{8,4},{12,0},{16,28},{20,24},{24,20},{28,16},{1,13},{... | collective-permute-start | bytes 221192 | tf_op jit(solution)/shard_map/ppermute | solution.py:463
  35.7 1.8 %collective-permute-done.9.rest_1_ = bf16[96,384]{1,0:T(8,128)(2,1)S(1)} collective-permute-done((bf16[96,384]{1,0:T(8,128)(2,1)S(1)}, bf16[96,384]{1,0:T(8,128)(2,1)S(1)}, u32[]{:S(2)}, u32[]{:S(2)}) %collective-permute-start.9) | collective-permute-done | bytes 73760 | tf_op jit(solution)/shard_map/ppermute | solution.py:463
  37.5 0.1 collective-permute-start.14
  37.5 0.8 %collective-permute-done.10.rest_2_ = bf16[96,384]{1,0:T(8,128)(2,1)S(1)} collective-permute-done((bf16[96,384]{1,0:T(8,128)(2,1)S(1)}, bf16[96,384]{1,0:T(8,128)(2,1)S(1)}, u32[]{:S(2)}, u32[]{:S(2)}) %collective-permute-start.10) | collective-permute-done | bytes 73760 | tf_op jit(solution)/shard_map/ppermute | solution.py:463
  38.3 0.0 collective-permute-done.11.rest_3_
  38.3 1.2 %collective-permute-done.12.rest_4_ = bf16[96,384]{1,0:T(8,128)(2,1)S(1)} collective-permute-done((bf16[96,384]{1,0:T(8,128)(2,1)S(1)}, bf16[96,384]{1,0:T(8,128)(2,1)S(1)}, u32[]{:S(2)}, u32[]{:S(2)}) %collective-permute-start.12) | collective-permute-done | bytes 73760 | tf_op jit(solution)/shard_map/ppermute | solution.py:463
  39.5 0.0 collective-permute-done.13.rest_5_
  39.5 0.0 collective-permute-done.14.rest_6_
  39.5 0.0 copy-done.1
  39.5 2.1 %shard_map.72 = (bf16[384,1152]{1,0:T(8,128)(2,1)}, f32[1,4]{1,0:T(1,128)}) custom-call(bf16[384,1152]{1,0:T(8,128)(2,1)S(1)} %bitcast.7, bf16[640,1152]{1,0:T(8,128)(2,1)S(1)} %get-tuple-element.35.weight_ref, bf16[4,1152]{1,0:T(4,128)(2,1)S(1)} %copy-done.3, bf16[96,384]{1,0:T(8,128)(2,1)S(1)} %collective-permute-done.8.rest_0_, ...), custom_call_target="tpu_custom_call" | custom-call | flops 509607936 | bytes 8388608 | tf_op jit(solution)/shard_map/pallas_call | solution.py:610
Async XLA Ops:
  0.6 6.8 %copy-start = (bf16[1152,1728]{0,1:T(8,128)(2,1)S(1)}, bf16[1152,1728]{0,1:T(8,128)(2,1)}, u32[]{:S(2)}) copy-start(bf16[1152,1728]{0,1:T(8,128)(2,1)} %param.7) | copy-start | bytes 11943940
  3.4 9.6 %collective-permute-start = (bf16[224,384]{1,0:T(8,128)(2,1)S(1)}, bf16[224,384]{1,0:T(8,128)(2,1)S(1)}, u32[]{:S(2)}, u32[]{:S(2)}) collective-permute-start(bf16[224,384]{1,0:T(8,128)(2,1)S(1)} %get-tuple-element.28), channel_id=1, source_target_pairs={{0,24},{4,28},{8,16},{12,20},{16,8},{20,12},{24,0},{28,4},{1,25},{... | collective-permute-start | bytes 516104 | tf_op jit(solution)/shard_map/ppermute | solution.py:463
  7.4 8.5 %collective-permute-start.1 = (bf16[224,384]{1,0:T(8,128)(2,1)S(1)}, bf16[224,384]{1,0:T(8,128)(2,1)S(1)}, u32[]{:S(2)}, u32[]{:S(2)}) collective-permute-start(bf16[224,384]{1,0:T(8,128)(2,1)S(1)} %get-tuple-element.29), channel_id=1, source_target_pairs={{0,28},{4,24},{8,20},{12,16},{16,12},{20,8},{24,4},{28,0},{1,29},{... | collective-permute-start | bytes 516104 | tf_op jit(solution)/shard_map/ppermute | solution.py:463
  7.4 10.4 %copy-start.3 = (bf16[4,1152]{1,0:T(4,128)(2,1)S(1)}, bf16[4,1152]{1,0:T(4,128)(2,1)}, u32[]{:S(2)}) copy-start(bf16[4,1152]{1,0:T(4,128)(2,1)} %text_ref.1) | copy-start | bytes 27652
  7.4 11.9 %copy-start.2 = (s32[1,3072]{1,0:T(1,128)S(1)}, s32[1,3072]{1,0:T(1,128)}, u32[]{:S(2)}) copy-start(s32[1,3072]{1,0:T(1,128)} %ids_ref.5) | copy-start | bytes 36868
  9.4 8.4 %collective-permute-start.2 = (bf16[224,384]{1,0:T(8,128)(2,1)S(1)}, bf16[224,384]{1,0:T(8,128)(2,1)S(1)}, u32[]{:S(2)}, u32[]{:S(2)}) collective-permute-start(bf16[224,384]{1,0:T(8,128)(2,1)S(1)} %get-tuple-element.32), channel_id=1, source_target_pairs={{0,4},{4,0},{8,12},{12,8},{16,20},{20,16},{24,28},{28,24},{1,5},{5... | collective-permute-start | bytes 516104 | tf_op jit(solution)/shard_map/ppermute | solution.py:463
  9.6 11.8 %collective-permute-start.3 = (bf16[224,384]{1,0:T(8,128)(2,1)S(1)}, bf16[224,384]{1,0:T(8,128)(2,1)S(1)}, u32[]{:S(2)}, u32[]{:S(2)}) collective-permute-start(bf16[224,384]{1,0:T(8,128)(2,1)S(1)} %get-tuple-element.39), channel_id=1, source_target_pairs={{0,16},{4,20},{8,24},{12,28},{16,0},{20,4},{24,8},{28,12},{1,17},{... | collective-permute-start | bytes 516104 | tf_op jit(solution)/shard_map/ppermute | solution.py:463
  11.5 9.9 %collective-permute-start.4 = (bf16[224,384]{1,0:T(8,128)(2,1)S(1)}, bf16[224,384]{1,0:T(8,128)(2,1)S(1)}, u32[]{:S(2)}, u32[]{:S(2)}) collective-permute-start(bf16[224,384]{1,0:T(8,128)(2,1)S(1)} %get-tuple-element.40), channel_id=1, source_target_pairs={{0,8},{4,12},{8,0},{12,4},{16,24},{20,28},{24,16},{28,20},{1,9},{5... | collective-permute-start | bytes 516104 | tf_op jit(solution)/shard_map/ppermute | solution.py:463
  13.0 9.8 %collective-permute-start.5 = (bf16[224,384]{1,0:T(8,128)(2,1)S(1)}, bf16[224,384]{1,0:T(8,128)(2,1)S(1)}, u32[]{:S(2)}, u32[]{:S(2)}) collective-permute-start(bf16[224,384]{1,0:T(8,128)(2,1)S(1)} %get-tuple-element.41), channel_id=1, source_target_pairs={{0,20},{4,16},{8,28},{12,24},{16,4},{20,0},{24,12},{28,8},{1,21},{... | collective-permute-start | bytes 516104 | tf_op jit(solution)/shard_map/ppermute | solution.py:463
  15.9 6.9 %collective-permute-start.6 = (bf16[224,384]{1,0:T(8,128)(2,1)S(1)}, bf16[224,384]{1,0:T(8,128)(2,1)S(1)}, u32[]{:S(2)}, u32[]{:S(2)}) collective-permute-start(bf16[224,384]{1,0:T(8,128)(2,1)S(1)} %get-tuple-element.42), channel_id=1, source_target_pairs={{0,12},{4,8},{8,4},{12,0},{16,28},{20,24},{24,20},{28,16},{1,13},{... | collective-permute-start | bytes 516104 | tf_op jit(solution)/shard_map/ppermute | solution.py:463
  17.8 3.7 %collective-permute-start.7 = (bf16[4,1152]{1,0:T(4,128)(2,1)S(1)}, bf16[4,1152]{1,0:T(4,128)(2,1)S(1)}, u32[]{:S(2)}, u32[]{:S(2)}) collective-permute-start(bf16[4,1152]{1,0:T(4,128)(2,1)S(1)} %copy-done.3), channel_id=1, source_target_pairs={{1,0},{0,1},{3,2},{2,3},{6,4},{7,5},{4,6},{5,7},{11,8},{10,9},{9,1... | collective-permute-start | bytes 27656 | tf_op jit(solution)/shard_map/ppermute | solution.py:463
  22.8 16.7 %copy-start.1 = (bf16[1,384,1152]{2,1,0:T(8,128)(2,1)S(1)}, bf16[1,384,1152]{2,1,0:T(8,128)(2,1)}, u32[]{:S(2)}) copy-start(bf16[1,384,1152]{2,1,0:T(8,128)(2,1)} %param.5) | copy-start | bytes 2654212
  29.2 5.8 %collective-permute-start.8 = (bf16[96,384]{1,0:T(8,128)(2,1)S(1)}, bf16[96,384]{1,0:T(8,128)(2,1)S(1)}, u32[]{:S(2)}, u32[]{:S(2)}) collective-permute-start(bf16[96,384]{1,0:T(8,128)(2,1)S(1)} %get-tuple-element.44), channel_id=1, source_target_pairs={{0,24},{4,28},{8,16},{12,20},{16,8},{20,12},{24,0},{28,4},{1,25},{... | collective-permute-start | bytes 221192 | tf_op jit(solution)/shard_map/ppermute | solution.py:463
  31.9 5.6 %collective-permute-start.9 = (bf16[96,384]{1,0:T(8,128)(2,1)S(1)}, bf16[96,384]{1,0:T(8,128)(2,1)S(1)}, u32[]{:S(2)}, u32[]{:S(2)}) collective-permute-start(bf16[96,384]{1,0:T(8,128)(2,1)S(1)} %get-tuple-element.45), channel_id=1, source_target_pairs={{0,28},{4,24},{8,20},{12,16},{16,12},{20,8},{24,4},{28,0},{1,29},{... | collective-permute-start | bytes 221192 | tf_op jit(solution)/shard_map/ppermute | solution.py:463
  31.9 6.4 %collective-permute-start.10 = (bf16[96,384]{1,0:T(8,128)(2,1)S(1)}, bf16[96,384]{1,0:T(8,128)(2,1)S(1)}, u32[]{:S(2)}, u32[]{:S(2)}) collective-permute-start(bf16[96,384]{1,0:T(8,128)(2,1)S(1)} %get-tuple-element.46), channel_id=1, source_target_pairs={{0,16},{4,20},{8,24},{12,28},{16,0},{20,4},{24,8},{28,12},{1,17},{... | collective-permute-start | bytes 221192 | tf_op jit(solution)/shard_map/ppermute | solution.py:463
  33.4 4.9 %collective-permute-start.11 = (bf16[96,384]{1,0:T(8,128)(2,1)S(1)}, bf16[96,384]{1,0:T(8,128)(2,1)S(1)}, u32[]{:S(2)}, u32[]{:S(2)}) collective-permute-start(bf16[96,384]{1,0:T(8,128)(2,1)S(1)} %get-tuple-element.47), channel_id=1, source_target_pairs={{0,8},{4,12},{8,0},{12,4},{16,24},{20,28},{24,16},{28,20},{1,9},{5... | collective-permute-start | bytes 221192 | tf_op jit(solution)/shard_map/ppermute | solution.py:463
  34.9 4.6 %collective-permute-start.12 = (bf16[96,384]{1,0:T(8,128)(2,1)S(1)}, bf16[96,384]{1,0:T(8,128)(2,1)S(1)}, u32[]{:S(2)}, u32[]{:S(2)}) collective-permute-start(bf16[96,384]{1,0:T(8,128)(2,1)S(1)} %get-tuple-element.48), channel_id=1, source_target_pairs={{0,20},{4,16},{8,28},{12,24},{16,4},{20,0},{24,12},{28,8},{1,21},{... | collective-permute-start | bytes 221192 | tf_op jit(solution)/shard_map/ppermute | solution.py:463
  35.1 4.4 %collective-permute-start.13 = (bf16[96,384]{1,0:T(8,128)(2,1)S(1)}, bf16[96,384]{1,0:T(8,128)(2,1)S(1)}, u32[]{:S(2)}, u32[]{:S(2)}) collective-permute-start(bf16[96,384]{1,0:T(8,128)(2,1)S(1)} %get-tuple-element.49), channel_id=1, source_target_pairs={{0,12},{4,8},{8,4},{12,0},{16,28},{20,24},{24,20},{28,16},{1,13},{... | collective-permute-start | bytes 221192 | tf_op jit(solution)/shard_map/ppermute | solution.py:463
  37.5 2.0 %collective-permute-start.14 = (bf16[96,384]{1,0:T(8,128)(2,1)S(1)}, bf16[96,384]{1,0:T(8,128)(2,1)S(1)}, u32[]{:S(2)}, u32[]{:S(2)}) collective-permute-start(bf16[96,384]{1,0:T(8,128)(2,1)S(1)} %get-tuple-element.50), channel_id=1, source_target_pairs={{0,4},{4,0},{8,12},{12,8},{16,20},{20,16},{24,28},{28,24},{1,5},{5... | collective-permute-start | bytes 221192 | tf_op jit(solution)/shard_map/ppermute | solution.py:463
